TPU v7x, 32 devices: a whole 2x2x4 slice. The times are simulated.
32 devices in a mesh: dp: 2 (over x), seq: 16 (over z, y, core).
Axes of the slice: x: 2, y: 2, z: 4, core: 2. Of those that a mesh axis runs over, the one named last changes fastest.
Arguments:
- signal: bfloat16 [2, 32768, 256], P('dp', 'seq'), may hold values from -6 to 6
- gating: bfloat16 [2, 32768, 256], P('dp', 'seq'), may hold values from -6 to 6
- upstream: bfloat16 [2, 32768, 256], P('dp', 'seq'), may hold values from -1.5 to 1.5
- left_factor: bfloat16 [64, 512, 512], P('seq'), may hold values from -0.25 to 0.25
- right_factor: bfloat16 [512, 64, 64], P('seq'), may hold values from -0.75 to 0.75
Outputs:
- output: bfloat16 [2, 32768, 256], P('dp', 'seq')
- grad_gating: bfloat16 [2, 32768, 256], P('dp', 'seq')
- grad_signal: bfloat16 [2, 32768, 256], P('dp', 'seq')
- grad_left: bfloat16 [64, 512, 512], P('seq')
- grad_right: bfloat16 [512, 64, 64], P('seq')
All inputs are finite; a program needn't handle non-finite values.
Results may differ from a plain program's by a relative error of at most 0.0075.
Values may be sent and summed in bfloat16 or wider, within the bound.
No kernel may reach another device: no remote copies, remote signals or barrier semaphores. Data moves between devices by JAX's collectives and lax.ppermute only.
A program may use at most 64 MiB of HBM per device.

v0:
```python
import jax
import jax.numpy as jnp
from jax import lax
from jax.sharding import PartitionSpec as P


def column_forward(right_factor, by_column):
    return jnp.einsum(
        "kmi,ikd->mkd", right_factor, by_column, preferred_element_type=jnp.float32
    ).astype(jnp.bfloat16)


def column_backward(right_factor, grad_column):
    return jnp.einsum(
        "kmi,mkd->ikd", right_factor, grad_column, preferred_element_type=jnp.float32
    ).astype(jnp.bfloat16)


def shards(signal, gating, upstream, left_factor, right_factor):
    block_count = left_factor.shape[0]
    block_len = left_factor.shape[1]
    channels = signal.shape[2]
    values = signal.reshape(block_count, block_len, channels)
    gate_rows = gating.reshape(block_count, block_len, channels)
    upstream_rows = upstream.reshape(block_count, block_len, channels)
    mixed_rows = jnp.einsum(
        "ikj,ijd->ikd", left_factor, values, preferred_element_type=jnp.float32
    ).astype(jnp.bfloat16)
    grad_rows = (upstream_rows.astype(jnp.float32) * gate_rows.astype(jnp.float32)).astype(
        jnp.bfloat16
    )
    by_column = lax.all_to_all(mixed_rows, "seq", split_axis=1, concat_axis=0, tiled=True)
    second = column_forward(right_factor, by_column)
    mixed_out = lax.all_to_all(second, "seq", split_axis=0, concat_axis=1, tiled=True)
    grad_column = lax.all_to_all(grad_rows, "seq", split_axis=1, concat_axis=0, tiled=True)
    grad_second = column_backward(right_factor, grad_column)
    grad_back = lax.all_to_all(grad_second, "seq", split_axis=0, concat_axis=1, tiled=True)
    mixed_wide = mixed_out.astype(jnp.float32)
    output = (gate_rows.astype(jnp.float32) * mixed_wide).astype(jnp.bfloat16).reshape(signal.shape)
    grad_gate = (
        (upstream_rows.astype(jnp.float32) * mixed_wide).astype(jnp.bfloat16).reshape(signal.shape)
    )
    grad_signal = (
        jnp.einsum("ikj,ikd->ijd", left_factor, grad_back, preferred_element_type=jnp.float32)
        .astype(jnp.bfloat16)
        .reshape(signal.shape)
    )
    left_term = jnp.einsum("ikd,ijd->ikj", grad_back, values, preferred_element_type=jnp.float32)
    right_term = jnp.einsum(
        "mkd,ikd->kmi", grad_column, by_column, preferred_element_type=jnp.float32
    )
    left_sum, right_sum = (
        lax.psum(left_term.astype(jnp.bfloat16), "dp").astype(jnp.float32),
        lax.psum(right_term.astype(jnp.bfloat16), "dp").astype(jnp.float32),
    )
    grad_left = left_sum.astype(jnp.bfloat16)
    grad_right = right_sum.astype(jnp.bfloat16)
    return (output, grad_gate, grad_signal, grad_left, grad_right)


def solution(mesh):
    in_specs = (
        P("dp", "seq", None),
        P("dp", "seq", None),
        P("dp", "seq", None),
        P("seq", None, None),
        P("seq", None, None),
    )
    out_specs = (
        P("dp", "seq", None),
        P("dp", "seq", None),
        P("dp", "seq", None),
        P("seq", None, None),
        P("seq", None, None),
    )
    return jax.shard_map(shards, mesh=mesh, in_specs=in_specs, out_specs=out_specs, check_vma=False)
```

profile of v0, /device:TPU:0, one launch (start us, length us, event | category | flops | bytes accessed | tf_op | source)
XLA Modules:
  0.0 238.7 jit_solution(12379009365001358727)
XLA Ops:
  7.2 0.0 copy-start
  7.2 1.6 copy-done
  8.8 1.9 convolution_convert_fusion.2
  10.7 0.8 copy.32
  11.5 32.0 %all_to_all.63 = bf16[4,512,256]{2,0,1:T(4,128)(2,1)S(1)} all-to-all(bf16[4,512,256]{2,0,1:T(4,128)(2,1)S(1)} %copy.32), channel_id=1, replica_groups=mesh['dp'=2,'seq'=16] {'seq'}, dimensions={1} | all-to-all | bytes 2097152 | tf_op jit(solution)/shard_map/all_to_all | solution.py:32
  43.6 1.5 copy.47
  45.1 1.3 all_to_all.49
  46.4 1.4 fusion.5
  47.9 0.6 copy.34
  48.5 29.7 %all_to_all.64 = bf16[64,32,256]{2,1,0:T(8,128)(2,1)S(1)} all-to-all(bf16[64,32,256]{2,1,0:T(8,128)(2,1)S(1)} %copy.34), channel_id=1, replica_groups=mesh['dp'=2,'seq'=16] {'seq'}, dimensions={0} | all-to-all | bytes 2097152 | tf_op jit(solution)/shard_map/all_to_all | solution.py:34
  78.1 0.0 copy-start.1
  78.1 0.0 copy-start.2
  78.1 0.2 copy.35
  78.4 1.0 copy-done.1
  79.3 0.3 copy-done.2
  79.7 1.9 fusion.1
  81.6 0.8 copy.36
  82.4 29.6 %all_to_all.65 = bf16[4,512,256]{2,0,1:T(4,128)(2,1)S(1)} all-to-all(bf16[4,512,256]{2,0,1:T(4,128)(2,1)S(1)} %copy.36), channel_id=1, replica_groups=mesh['dp'=2,'seq'=16] {'seq'}, dimensions={1} | all-to-all | bytes 2097152 | tf_op jit(solution)/shard_map/all_to_all | solution.py:35
  112.0 0.1 copy.37
  112.2 1.8 copy.38
  113.9 2.1 all_to_all.54
  116.1 1.8 fusion.4
  117.9 1.6 copy.40
  119.5 5.0 %all-to-all-start.3 = ((bf16[64,32,256]{2,1,0:T(8,128)(2,1)}), bf16[64,32,256]{2,1,0:T(8,128)(2,1)}, u32[]{:S(2)}, u32[]{:S(2)}) async-start(bf16[64,32,256]{2,1,0:T(8,128)(2,1)} %copy.40), calls=%async_computation.3 | async-start | bytes 2097152 | tf_op jit(solution)/shard_map/all_to_all | solution.py:37
  124.5 0.0 all-reduce.3.cloned.1.call-start
  124.6 2.4 %convolution_convert_fusion.5 = bf16[32,64,64]{2,1,0:T(8,128)(2,1)} fusion(bf16[64,32,256]{2,0,1:T(8,128)(2,1)} %all_to_all.54, bf16[64,32,256]{2,0,1:T(8,128)(2,1)S(1)} %all_to_all.49), kind=kOutput, calls=%fused_computation.14 | convolution fusion | flops 67239936 | bytes 2359296 | tf_op jit(solution)/shard_map/mkd,ikd->kmi/dot_general | solution.py:49
  127.0 20.5 %all-to-all-done.3 = bf16[64,32,256]{2,1,0:T(8,128)(2,1)} async-done(((bf16[64,32,256]{2,1,0:T(8,128)(2,1)}), bf16[64,32,256]{2,1,0:T(8,128)(2,1)}, u32[]{:S(2)}, u32[]{:S(2)}) %all-to-all-start.3) | async-done | bytes 1048608 | tf_op jit(solution)/shard_map/all_to_all | solution.py:37
  147.5 0.0 copy-start.3
  147.5 1.4 copy.41
  148.9 0.1 copy-done.3
  149.1 2.1 convolution_convert_fusion
  151.1 0.0 all-reduce.3.cloned.1.call-update
  151.2 1.8 fusion.3
  152.9 2.3 copy.43
  155.2 72.8 %all-reduce.3.cloned.1.call-done = (bf16[4,512,512]{2,1,0:T(8,128)(2,1)}, bf16[32,64,64]{2,1,0:T(8,128)(2,1)}) async-done(((bf16[4,512,512]{2,1,0:T(8,128)(2,1)}, bf16[32,64,64]{2,1,0:T(8,128)(2,1)}), (bf16[4,512,512]{2,1,0:T(8,128)(2,1)}, bf16[32,64,64]{2,1,0:T(8,128)(2,1)})) %all-reduce.3.cloned.1.call-update) | async-done | bytes 2359312 | tf_op jit(solution)/shard_map/psum | solution.py:53
  228.0 0.0 copy-start.4
  228.0 3.1 %copy.50 = bf16[4,512,512]{2,1,0:T(8,128)(2,1)} copy(bf16[4,512,512]{2,1,0:T(8,128)(2,1)} %get-tuple-element.13) | data formatting | bytes 4194304
  231.1 0.0 copy-done.4
  231.1 0.8 copy.51
Async XLA Ops:
  7.2 1.6 copy-start
  78.1 1.2 copy-start.1
  78.1 1.5 copy-start.2
  119.5 28.0 %all-to-all-start.3 = ((bf16[64,32,256]{2,1,0:T(8,128)(2,1)}), bf16[64,32,256]{2,1,0:T(8,128)(2,1)}, u32[]{:S(2)}, u32[]{:S(2)}) async-start(bf16[64,32,256]{2,1,0:T(8,128)(2,1)} %copy.40), calls=%async_computation.3 | async-start | bytes 2097152 | tf_op jit(solution)/shard_map/all_to_all | solution.py:37
  124.5 103.5 %all-reduce.3.cloned.1.call-start = ((), (), s32[]{:S(2)}) async-start(), calls=%async_computation.4 | async-start | bytes 5242880 | tf_op jit(solution)/shard_map/psum | solution.py:53
  147.5 1.5 copy-start.3
  228.0 3.1 %copy-start.4 = (bf16[32,64,64]{2,1,0:T(8,128)(2,1)S(1)}, bf16[32,64,64]{2,1,0:T(8,128)(2,1)}, u32[]{:S(2)}) copy-start(bf16[32,64,64]{2,1,0:T(8,128)(2,1)} %get-tuple-element.14) | copy-start | bytes 786436
Sparse Core Ops, SparseCore 0:
  151.3 76.6 all-reduce.2
where the time goes:
time: 239 us
  waiting for transfers between devices  93.4 us (39%)
  blocking collectives  91.3 us (38%)
  local copies, waits for them, and re-layouts  21.5 us (9%)
  between operations  14.1 us (6%)
  matrix products  11.5 us (5%)
  starting transfers between devices  5.08 us (2%)
    psum x1, waiting for transfers between devices, shards(): lax.psum(left_term.astype(jnp.bfloat16), 'dp').astype(jnp.float32)  72.8 us
    all_to_all x1, blocking collectives, shards(): lax.all_to_all(mixed_rows, 'seq', split_axis=1, concat_axis=0, tiled=True)  32 us
    all_to_all x1, blocking collectives, shards(): lax.all_to_all(second, 'seq', split_axis=0, concat_axis=1, tiled=True)  29.7 us
    all_to_all x1, blocking collectives, shards(): lax.all_to_all(grad_rows, 'seq', split_axis=1, concat_axis=0, tiled=True)  29.6 us
    all_to_all x1, waiting for transfers between devices, shards(): lax.all_to_all(grad_second, 'seq', split_axis=0, concat_axis=1, tiled=True)  20.5 us
    unnamed x12, local copies, waits for them, and re-layouts  6.91 us
    all_to_all x1, starting transfers between devices, shards(): lax.all_to_all(grad_second, 'seq', split_axis=0, concat_axis=1, tiled=True)  5.04 us
  transfers between devices with their start and end apart: 2, of which 2 were waited for; matrix products, arithmetic and copies ran while one was open for 3% of the time, Pallas kernels for 0%

commit v1 on v0

v1 whole, which is shorter than its diff:
```python
import jax
import jax.numpy as jnp
from jax import lax
from jax.sharding import PartitionSpec as P

BF16 = jnp.bfloat16
F32 = jnp.float32


def exchange(blocks):
    return lax.all_to_all(blocks, "seq", split_axis=0, concat_axis=0, tiled=True)


def swap_sequences(array):
    return lax.ppermute(array, "dp", [(0, 1), (1, 0)])


def shards(signal, gating, upstream, left_factor, right_factor):
    seq = lax.axis_size("seq")
    rows, block_len = left_factor.shape[:2]
    cols, block_count = right_factor.shape[:2]
    channels = signal.shape[2]
    values = signal.reshape(rows, block_len, channels)
    gate = gating.reshape(rows, block_len, channels)
    cotangent = upstream.reshape(rows, block_len, channels)

    def to_send(by_row):
        return by_row.reshape(rows, seq, cols, channels).transpose(1, 0, 2, 3)

    def from_received(blocks):
        return blocks.transpose(1, 0, 2, 3).reshape(rows, block_len, channels)

    def by_column(blocks):
        return blocks.reshape(block_count, cols, channels)

    grad_rows = (cotangent.astype(F32) * gate.astype(F32)).astype(BF16)
    grad_column = by_column(exchange(to_send(grad_rows)))
    other_values = swap_sequences(values)
    mixed_rows = jnp.einsum(
        "ikj,ijd->ikd", left_factor, values, preferred_element_type=F32
    ).astype(BF16)
    mixed_column = by_column(exchange(to_send(mixed_rows)))
    grad_second = jnp.einsum(
        "kmi,mkd->ikd", right_factor, grad_column, preferred_element_type=F32
    ).astype(BF16)
    grad_back = from_received(exchange(grad_second.reshape(seq, rows, cols, channels)))
    second = jnp.einsum(
        "kmi,ikd->mkd", right_factor, mixed_column, preferred_element_type=F32
    ).astype(BF16)
    second_rows = from_received(exchange(second.reshape(seq, rows, cols, channels)))
    right_part = jnp.einsum(
        "mkd,ikd->kmi", grad_column, mixed_column, preferred_element_type=F32
    ).astype(BF16)
    other_right = swap_sequences(right_part)
    other_grad_back = swap_sequences(grad_back)
    grad_signal = jnp.einsum(
        "ikj,ikd->ijd", left_factor, grad_back, preferred_element_type=F32
    ).astype(BF16)

    def left_term(grad, vals):
        return jnp.einsum("ikd,ijd->ikj", grad, vals, preferred_element_type=F32).astype(BF16)

    grad_left = left_term(grad_back, values).astype(F32) + left_term(
        other_grad_back, other_values
    ).astype(F32)
    grad_right = right_part.astype(F32) + other_right.astype(F32)
    wide = second_rows.astype(F32)
    output = (gate.astype(F32) * wide).astype(BF16)
    grad_gate = (cotangent.astype(F32) * wide).astype(BF16)
    return (
        output.reshape(signal.shape),
        grad_gate.reshape(signal.shape),
        grad_signal.reshape(signal.shape),
        grad_left.astype(BF16),
        grad_right.astype(BF16),
    )


def solution(mesh):
    by_position = P("dp", "seq", None)
    by_block = P("seq", None, None)
    return jax.shard_map(
        shards,
        mesh=mesh,
        in_specs=(by_position,) * 3 + (by_block,) * 2,
        out_specs=(by_position,) * 3 + (by_block,) * 2,
        check_vma=False,
    )
```

time: 239 us -> 184 us (0.77)
  waiting for transfers between devices: 93.4 us -> 46.4 us
  between operations: 14.1 us -> 0.72 us
  local copies, waits for them, and re-layouts: 21.5 us -> 16.4 us
  matrix products: 11.5 us -> 15.8 us
  starting transfers between devices: 5.08 us -> 8.62 us
  other arithmetic: 1.89 us -> 4.35 us
    psum x1 -> x0, waiting for transfers between devices: 72.8 us -> none  [shards(): lax.psum(left_term.astype(jnp.bfloat16), 'dp').astype(jnp.float32)]
    ppermute x0 -> x3, waiting for transfers between devices: none -> 28.3 us  [swap_sequences(): return lax.ppermute(array, 'dp', [(0, 1), (1, 0)])]
    reshape x0 -> x5, local copies, waits for them, and re-layouts: none -> 7.61 us  [the longest x2 3.83 us: shards(): second.reshape(seq, rows, cols, channels)]
    all_to_all x6 -> x2, local copies, waits for them, and re-layouts: 8.31 us -> 2.83 us  [exchange(): lax.all_to_all(blocks, 'seq', split_axis=0, concat_axis=0, tiled=True)]
    dot_general x5 -> x6, matrix products: 9.72 us -> 14.1 us  [the longest x2 5.58 us: left_term(): jnp.einsum('ikd,ijd->ikj', grad, vals, preferred_element_type=F32)]
    unnamed x12 -> x8, local copies, waits for them, and re-layouts: 6.91 us -> 2.85 us
    convert_element_type x5 -> x0, local copies, waits for them, and re-layouts: 4.02 us -> none  [the longest x1 1.56 us: column_backward(): return jnp.einsum('kmi,mkd->ikd', right_factor, grad_column, preferred_el...]
    ppermute x0 -> x3, starting transfers between devices: none -> 3.58 us  [swap_sequences(): return lax.ppermute(array, 'dp', [(0, 1), (1, 0)])]
  transfers between devices with their start and end apart: 2 -> 4, of which waited for: 2 -> 3; matrix products, arithmetic and copies ran while one was open for 3% -> 7% of each run, Pallas kernels for 0% -> 0%
where the time goes in v1:
time: 184 us
  blocking collectives  91.4 us (50%)
  waiting for transfers between devices  46.4 us (25%)
  local copies, waits for them, and re-layouts  16.4 us (9%)
  matrix products  15.8 us (9%)
  starting transfers between devices  8.62 us (5%)
  other arithmetic  4.35 us (2%)
    all_to_all x3, blocking collectives, exchange(): lax.all_to_all(blocks, 'seq', split_axis=0, concat_axis=0, tiled=True)  91.4 us
    ppermute x3, waiting for transfers between devices, swap_sequences(): return lax.ppermute(array, 'dp', [(0, 1), (1, 0)])  28.3 us
    all_to_all x1, waiting for transfers between devices, exchange(): lax.all_to_all(blocks, 'seq', split_axis=0, concat_axis=0, tiled=True)  18.1 us
    dot_general x2, matrix products, left_term(): jnp.einsum('ikd,ijd->ikj', grad, vals, preferred_element_type=F32)  5.58 us
    all_to_all x1, starting transfers between devices, exchange(): lax.all_to_all(blocks, 'seq', split_axis=0, concat_axis=0, tiled=True)  5.04 us
    reshape x2, local copies, waits for them, and re-layouts, shards(): second.reshape(seq, rows, cols, channels)  3.83 us
  transfers between devices with their start and end apart: 4, of which 3 were waited for; matrix products, arithmetic and copies ran while one was open for 7% of the time, Pallas kernels for 0%

profile of v1, /device:TPU:0, one launch (start us, length us, event | category | flops | bytes accessed | tf_op | source)
XLA Modules:
  0.0 183.8 jit_solution(3511967300880816572)
XLA Ops:
  0.6 0.0 copy-start
  0.6 1.6 copy-done
  2.2 1.9 %convolution_convert_fusion.1 = bf16[4,512,256]{2,1,0:T(8,128)(2,1)S(1)} fusion(bf16[4,512,512]{2,1,0:T(8,128)(2,1)S(1)} %copy-done, bf16[4,512,256]{2,1,0:T(8,128)(2,1)} %bitcast), kind=kOutput, calls=%fused_computation.8 | convolution fusion | flops 537395200 | bytes 4194304 | tf_op jit(solution)/shard_map/ikj,ijd->ikd/dot_general | solution.py:39
  4.2 0.0 copy-start.1
  4.2 0.1 copy.54
  4.3 32.2 %all_to_all.20 = bf16[16,4,32,256]{3,2,1,0:T(8,128)(2,1)S(1)} all-to-all(bf16[16,4,32,256]{3,2,1,0:T(8,128)(2,1)S(1)} %bitcast.47), channel_id=1, replica_groups=mesh['dp'=2,'seq'=16] {'seq'}, dimensions={0} | all-to-all | bytes 2097152 | tf_op jit(solution)/shard_map/all_to_all | solution.py:11
  36.4 0.0 copy-done.1
  36.4 1.9 %fusion.5 = bf16[64,32,256]{2,0,1:T(8,128)(2,1)} fusion(bf16[32,64,64]{2,1,0:T(8,128)(2,1)S(1)} %copy-done.1, bf16[64,32,256]{2,1,0:T(8,128)(2,1)S(1)} %bitcast.39), kind=kOutput, calls=%fused_computation.13 | convolution fusion | flops 67633152 | bytes 2359296 | tf_op jit(solution)/shard_map/kmi,ikd->mkd/dot_general | solution.py:47
  38.3 2.1 %reshape.62 = bf16[16,4,32,256]{3,1,0,2:T(4,128)(2,1)} reshape(bf16[64,32,256]{2,0,1:T(8,128)(2,1)} %fusion.5) | data formatting | bytes 2097152 | tf_op jit(solution)/shard_map/reshape | solution.py:50
  40.4 1.7 copy.35
  42.1 29.6 %all_to_all.21 = bf16[16,4,32,256]{3,1,2,0:T(4,128)(2,1)S(1)} all-to-all(bf16[16,4,32,256]{3,1,2,0:T(4,128)(2,1)S(1)} %copy.35), channel_id=1, replica_groups=mesh['dp'=2,'seq'=16] {'seq'}, dimensions={0} | all-to-all | bytes 2097152 | tf_op jit(solution)/shard_map/all_to_all | solution.py:11
  71.8 0.0 copy-start.2
  71.8 0.0 copy-start.3
  71.8 0.3 copy_convert_fusion
  72.1 0.9 copy-done.2
  73.0 0.3 copy-done.3
  73.3 1.9 %fusion.1 = (bf16[1,2048,256]{2,1,0:T(8,128)(2,1)}, bf16[1,2048,256]{2,1,0:T(8,128)(2,1)}, bf16[1,2048,256]{2,1,0:T(8,128)(2,1)S(1)}) fusion(f32[1,2048,256]{2,1,0:T(8,128)S(1)} %bitcast.44, bf16[1,2048,256]{2,1,0:T(8,128)(2,1)S(1)} %copy-done.2, bf16[1,2048,256]{2,1,0:T(8,128)(2,1)S(1)} %copy-done.3), kind=kLoop, calls=%fused_computation.5 | loop fusion | flops 4194304 | bytes 7340032 | tf_op jit(solution)/shard_map/convert_element_type | solution.py:69
  75.2 0.9 copy.37
  76.1 29.6 %all_to_all.22 = bf16[16,4,32,256]{3,1,2,0:T(4,128)(2,1)S(1)} all-to-all(bf16[16,4,32,256]{3,1,2,0:T(4,128)(2,1)S(1)} %copy.37), channel_id=1, replica_groups=mesh['dp'=2,'seq'=16] {'seq'}, dimensions={0} | all-to-all | bytes 2097152 | tf_op jit(solution)/shard_map/all_to_all | solution.py:11
  105.7 1.5 copy.38
  107.3 2.1 %reshape.63 = bf16[64,32,256]{2,0,1:T(8,128)(2,1)} reshape(bf16[16,4,32,256]{3,1,0,2:T(4,128)(2,1)} %copy.38) | data formatting | bytes 2097152 | tf_op jit(solution)/shard_map/reshape | solution.py:34
  109.4 1.8 %fusion.4 = bf16[64,32,256]{2,0,1:T(8,128)(2,1)S(1)} fusion(bf16[64,32,256]{2,0,1:T(8,128)(2,1)} %reshape.63, bf16[32,64,64]{2,1,0:T(8,128)(2,1)} %param.9), kind=kOutput, calls=%fused_computation.12 | convolution fusion | flops 67633152 | bytes 2359296 | tf_op jit(solution)/shard_map/kmi,mkd->ikd/dot_general | solution.py:43
  111.3 1.6 copy.47
  112.8 5.0 %all-to-all-start.3 = ((bf16[16,4,32,256]{3,2,1,0:T(8,128)(2,1)}), bf16[16,4,32,256]{3,2,1,0:T(8,128)(2,1)}, u32[]{:S(2)}, u32[]{:S(2)}) async-start(bf16[16,4,32,256]{3,2,1,0:T(8,128)(2,1)} %bitcast.46), calls=%async_computation.3 | async-start | bytes 2097152 | tf_op jit(solution)/shard_map/all_to_all | solution.py:11
  117.9 2.8 %convolution_convert_fusion.4 = bf16[32,64,64]{2,1,0:T(8,128)(2,1)} fusion(bf16[64,32,256]{2,0,1:T(8,128)(2,1)} %reshape.63, bf16[64,32,256]{2,1,0:T(8,128)(2,1)S(1)} %bitcast.40), kind=kOutput, calls=%fused_computation.14 | convolution fusion | flops 67239936 | bytes 2359296 | tf_op jit(solution)/shard_map/mkd,ikd->kmi/dot_general | solution.py:51
  120.7 1.5 collective-permute-start.2
  122.2 0.5 collective-permute-start.1
  122.7 18.1 %all-to-all-done.3 = bf16[16,4,32,256]{3,2,1,0:T(8,128)(2,1)} async-done(((bf16[16,4,32,256]{3,2,1,0:T(8,128)(2,1)}), bf16[16,4,32,256]{3,2,1,0:T(8,128)(2,1)}, u32[]{:S(2)}, u32[]{:S(2)}) %all-to-all-start.3) | async-done | bytes 1048608 | tf_op jit(solution)/shard_map/all_to_all | solution.py:11
  140.9 1.3 copy.41
  142.2 1.6 collective-permute-start
  143.7 0.0 collective-permute-done.2
  143.7 2.2 %add_convert_fusion.1 = bf16[32,64,64]{2,1,0:T(8,128)(2,1)} fusion(bf16[32,64,64]{2,1,0:T(8,128)(2,1)} %collective-permute-done.2, bf16[32,64,64]{2,1,0:T(8,128)(2,1)} %convolution_convert_fusion.4), kind=kLoop, calls=%fused_computation.17 | loop fusion | flops 524288 | bytes 786432 | tf_op jit(solution)/shard_map/convert_element_type | solution.py:75
  145.9 1.7 fusion.3
  147.6 2.3 %copy.43 = bf16[4,512,256]{2,1,0:T(8,128)(2,1)} copy(bf16[4,512,256]{1,2,0:T(8,128)(2,1)} %fusion.3) | data formatting | bytes 2097152 | tf_op jit(solution)/shard_map/convert_element_type | solution.py:58
  149.9 2.0 %fusion.8 = bf16[4,512,512]{2,1,0:T(8,128)(2,1)S(1)} fusion(bf16[4,512,256]{2,1,0:T(8,128)(2,1)S(1)} %bitcast.43, bf16[4,512,256]{2,1,0:T(8,128)(2,1)} %bitcast), kind=kOutput, calls=%fused_computation.20 | convolution fusion | flops 536870912 | bytes 4194304 | tf_op jit(solution)/shard_map/ikd,ijd->ikj/dot_general | solution.py:61
  151.9 6.4 %collective-permute-done.1 = bf16[4,512,256]{2,1,0:T(8,128)(2,1)} collective-permute-done((bf16[4,512,256]{2,1,0:T(8,128)(2,1)}, bf16[4,512,256]{2,1,0:T(8,128)(2,1)}, u32[]{:S(2)}, u32[]{:S(2)}) %collective-permute-start.1) | collective-permute-done | bytes 1048608 | tf_op jit(solution)/shard_map/ppermute | solution.py:15
  158.2 21.9 %collective-permute-done = bf16[4,512,256]{2,1,0:T(8,128)(2,1)} collective-permute-done((bf16[4,512,256]{2,1,0:T(8,128)(2,1)S(1)}, bf16[4,512,256]{2,1,0:T(8,128)(2,1)}, u32[]{:S(2)}, u32[]{:S(2)}) %collective-permute-start) | collective-permute-done | bytes 1048608 | tf_op jit(solution)/shard_map/ppermute | solution.py:15
  180.2 3.6 %add_convert_fusion = bf16[4,512,512]{2,1,0:T(8,128)(2,1)} fusion(bf16[4,512,512]{2,1,0:T(8,128)(2,1)S(1)} %fusion.8, bf16[4,512,256]{2,1,0:T(8,128)(2,1)} %collective-permute-done, bf16[4,512,256]{2,1,0:T(8,128)(2,1)} %collective-permute-done.1), kind=kOutput, calls=%fused_computation | convolution fusion | flops 542113792 | bytes 6291456 | tf_op jit(solution)/shard_map/ikd,ijd->ikj/dot_general | solution.py:61
Async XLA Ops:
  0.6 1.6 copy-start
  4.2 32.3 %copy-start.1 = (bf16[32,64,64]{2,1,0:T(8,128)(2,1)S(1)}, bf16[32,64,64]{2,1,0:T(8,128)(2,1)}, u32[]{:S(2)}) copy-start(bf16[32,64,64]{2,1,0:T(8,128)(2,1)} %param.9) | copy-start | bytes 786436
  71.8 1.2 copy-start.2
  71.8 1.5 copy-start.3
  112.8 28.0 %all-to-all-start.3 = ((bf16[16,4,32,256]{3,2,1,0:T(8,128)(2,1)}), bf16[16,4,32,256]{3,2,1,0:T(8,128)(2,1)}, u32[]{:S(2)}, u32[]{:S(2)}) async-start(bf16[16,4,32,256]{3,2,1,0:T(8,128)(2,1)} %bitcast.46), calls=%async_computation.3 | async-start | bytes 2097152 | tf_op jit(solution)/shard_map/all_to_all | solution.py:11
  120.7 23.0 %collective-permute-start.2 = (bf16[32,64,64]{2,1,0:T(8,128)(2,1)}, bf16[32,64,64]{2,1,0:T(8,128)(2,1)}, u32[]{:S(2)}, u32[]{:S(2)}) collective-permute-start(bf16[32,64,64]{2,1,0:T(8,128)(2,1)} %convolution_convert_fusion.4), channel_id=1, source_target_pairs={{0,16},{16,0},{1,17},{17,1},{2,18},{18,2},{3,19},{19,3},{4,20},{20... | collective-permute-start | bytes 786440 | tf_op jit(solution)/shard_map/ppermute | solution.py:15
  122.2 36.0 %collective-permute-start.1 = (bf16[4,512,256]{2,1,0:T(8,128)(2,1)}, bf16[4,512,256]{2,1,0:T(8,128)(2,1)}, u32[]{:S(2)}, u32[]{:S(2)}) collective-permute-start(bf16[4,512,256]{2,1,0:T(8,128)(2,1)} %bitcast), channel_id=1, source_target_pairs={{0,16},{16,0},{1,17},{17,1},{2,18},{18,2},{3,19},{19,3},{4,20},{20... | collective-permute-start | bytes 3145736 | tf_op jit(solution)/shard_map/ppermute | solution.py:15
  142.2 38.0 %collective-permute-start = (bf16[4,512,256]{2,1,0:T(8,128)(2,1)S(1)}, bf16[4,512,256]{2,1,0:T(8,128)(2,1)}, u32[]{:S(2)}, u32[]{:S(2)}) collective-permute-start(bf16[4,512,256]{2,1,0:T(8,128)(2,1)S(1)} %bitcast.41), channel_id=1, source_target_pairs={{0,16},{16,0},{1,17},{17,1},{2,18},{18,2},{3,19},{19,3},{4,20},{20... | collective-permute-start | bytes 3145736 | tf_op jit(solution)/shard_map/ppermute | solution.py:15

commit v2 on v1

v2 whole, which is shorter than its diff:
```python
import functools

import jax
import jax.numpy as jnp
from jax import lax
from jax.experimental import pallas as pl
from jax.experimental.pallas import tpu as pltpu
from jax.sharding import PartitionSpec as P

BF16 = jnp.bfloat16
F32 = jnp.float32
VMEM_LIMIT = 48 * 1024 * 1024


def partner_order(seq):
    return sorted(range(seq), key=lambda s: (-(s // (seq // 2)), s % (seq // 2), s))


def swap_sequences(array):
    return lax.ppermute(array, "dp", [(0, 1), (1, 0)])


def exchange(blocks):
    seq = len(blocks)
    received = list(blocks)
    for s in partner_order(seq):
        if s:
            received[s] = lax.ppermute(blocks[s], "seq", [(i, i ^ s) for i in range(seq)])
    return received


def call(kernel, me, inputs, out_shapes, scratch=(), flops=0):
    whole = pl.BlockSpec(memory_space=pltpu.VMEM)
    moved = sum(x.size * x.dtype.itemsize for x in (*inputs, *out_shapes))
    return pl.pallas_call(
        kernel,
        out_shape=out_shapes,
        in_specs=[pl.BlockSpec(memory_space=pltpu.SMEM)] + [whole] * len(inputs),
        out_specs=[whole] * len(out_shapes),
        scratch_shapes=scratch,
        compiler_params=pltpu.CompilerParams(vmem_limit_bytes=VMEM_LIMIT),
        cost_estimate=pl.CostEstimate(flops=flops, bytes_accessed=moved, transcendentals=0),
    )(me, *inputs)


def dot(a, b, contract):
    return lax.dot_general(a, b, (contract, ((), ())), preferred_element_type=F32)


def product_kernel(seq, me_ref, gate_ref, cotangent_ref, *out_refs):
    me = me_ref[0]
    for s in range(seq):
        c = me ^ s
        wide = gate_ref[:, c].astype(F32) * cotangent_ref[:, c].astype(F32)
        out_refs[s][...] = wide.astype(BF16)


def mix_kernel(seq, me_ref, left_ref, values_ref, *refs):
    out_refs, hold = refs[:seq], refs[seq]
    rows, _, cols, channels = hold.shape
    me = me_ref[0]
    for i in range(rows):
        mixed = dot(left_ref[i], values_ref[i], ((1,), (0,)))
        hold[i] = mixed.astype(BF16).reshape(seq, cols, channels)
    for s in range(seq):
        out_refs[s][...] = hold[:, me ^ s]


def load_columns(seq, me, in_refs, wide):
    rows, cols, channels = in_refs[0].shape
    size = rows * cols
    for s in range(seq):
        block = in_refs[s][...].reshape(size, channels).astype(F32)
        start = pl.multiple_of((me ^ s) * size, size)
        for h in range(channels // 128):
            wide[h, pl.ds(start, size), :] = block[:, h * 128 : (h + 1) * 128]


def column(wide, k, count, cols):
    halves = [wide[h, pl.ds(k, count, stride=cols), :] for h in range(wide.shape[0])]
    return jnp.concatenate(halves, axis=1).astype(BF16)


def store_column(wide, k, count, cols, value):
    for h in range(wide.shape[0]):
        wide[h, pl.ds(k, count, stride=cols), :] = value[:, h * 128 : (h + 1) * 128]


def send_columns(seq, me, wide, out_refs):
    rows, cols, channels = out_refs[0].shape
    size = rows * cols
    for s in range(seq):
        start = pl.multiple_of((me ^ s) * size, size)
        halves = [wide[h, pl.ds(start, size), :] for h in range(wide.shape[0])]
        block = jnp.concatenate(halves, axis=1).astype(BF16)
        out_refs[s][...] = block.reshape(rows, cols, channels)


def column_backward_kernel(seq, me_ref, right_ref, *refs):
    in_refs, out_refs = refs[:seq], refs[seq : 2 * seq]
    by_column_ref, wide, wide_out = refs[2 * seq :]
    cols, count, _ = right_ref.shape
    me = me_ref[0]
    load_columns(seq, me, in_refs, wide)
    for k in range(cols):
        grad = column(wide, k, count, cols)
        by_column_ref[k] = grad
        store_column(wide_out, k, count, cols, dot(right_ref[k], grad, ((0,), (0,))))
    send_columns(seq, me, wide_out, out_refs)


def column_forward_kernel(seq, me_ref, right_ref, grad_ref, *refs):
    in_refs, out_refs = refs[:seq], refs[seq : 2 * seq]
    right_part_ref, wide, wide_out = refs[2 * seq :]
    cols, count, _ = right_ref.shape
    me = me_ref[0]
    load_columns(seq, me, in_refs, wide)
    for k in range(cols):
        mixed = column(wide, k, count, cols)
        store_column(wide_out, k, count, cols, dot(right_ref[k], mixed, ((1,), (0,))))
        right_part_ref[k] = dot(grad_ref[k], mixed, ((1,), (1,))).astype(BF16)
    send_columns(seq, me, wide_out, out_refs)


def gather_kernel(seq, me_ref, *refs):
    in_refs, out_ref = refs[:seq], refs[seq]
    me = me_ref[0]
    for s in range(seq):
        out_ref[:, me ^ s] = in_refs[s][...]


def row_backward_kernel(me_ref, left_ref, values_ref, grad_ref, signal_ref, term_ref):
    for i in range(left_ref.shape[0]):
        grad = grad_ref[i]
        signal_ref[i] = dot(left_ref[i], grad, ((0,), (0,))).astype(BF16)
        term_ref[i] = dot(grad, values_ref[i], ((1,), (1,))).astype(BF16)


def left_sum_kernel(me_ref, term_ref, values_ref, grad_ref, out_ref):
    for i in range(term_ref.shape[0]):
        other = dot(grad_ref[i], values_ref[i], ((1,), (1,))).astype(BF16)
        out_ref[i] = (term_ref[i].astype(F32) + other.astype(F32)).astype(BF16)


def output_kernel(seq, me_ref, gate_ref, cotangent_ref, *refs):
    in_refs, (out_ref, grad_ref) = refs[:seq], refs[seq:]
    me = me_ref[0]
    for s in range(seq):
        c = me ^ s
        second = in_refs[s][...].astype(F32)
        out_ref[:, c] = (gate_ref[:, c].astype(F32) * second).astype(BF16)
        grad_ref[:, c] = (cotangent_ref[:, c].astype(F32) * second).astype(BF16)


def direct_shards(signal, gating, upstream, left_factor, right_factor):
    seq = lax.axis_size("seq")
    rows, block_len = left_factor.shape[:2]
    cols, count = right_factor.shape[:2]
    channels = signal.shape[2]
    me = lax.axis_index("seq").astype(jnp.int32).reshape(1)
    values = signal.reshape(rows, block_len, channels)
    gate = gating.reshape(rows, seq, cols, channels)
    cotangent = upstream.reshape(rows, seq, cols, channels)

    block = jax.ShapeDtypeStruct((rows, cols, channels), BF16)
    blocks = [block] * seq
    whole = jax.ShapeDtypeStruct((rows, seq, cols, channels), BF16)
    by_row = jax.ShapeDtypeStruct((rows, block_len, channels), BF16)
    left = jax.ShapeDtypeStruct(left_factor.shape, BF16)
    right = jax.ShapeDtypeStruct(right_factor.shape, BF16)
    by_column = jax.ShapeDtypeStruct((cols, count, channels), BF16)
    wide = pltpu.VMEM((channels // 128, count * cols, 128), F32)
    row_flops = 2 * rows * block_len * block_len * channels
    column_flops = 2 * cols * count * count * channels

    grad_rows = call(
        functools.partial(product_kernel, seq), me, [gate, cotangent], blocks
    )
    grad_blocks = exchange(grad_rows)
    other_values = swap_sequences(values)
    mixed_rows = call(
        functools.partial(mix_kernel, seq),
        me,
        [left_factor, values],
        blocks,
        [pltpu.VMEM(whole.shape, BF16)],
        row_flops,
    )
    mixed_blocks = exchange(mixed_rows)
    *grad_second, grad_column = call(
        functools.partial(column_backward_kernel, seq),
        me,
        [right_factor, *grad_blocks],
        blocks + [by_column],
        [wide, wide],
        column_flops,
    )
    back_blocks = exchange(grad_second)
    *second, right_part = call(
        functools.partial(column_forward_kernel, seq),
        me,
        [right_factor, grad_column, *mixed_blocks],
        blocks + [right],
        [wide, wide],
        2 * column_flops,
    )
    second_blocks = exchange(second)
    other_right = swap_sequences(right_part)
    (gathered,) = call(functools.partial(gather_kernel, seq), me, back_blocks, [whole])
    grad_back = gathered.reshape(rows, block_len, channels)
    other_grad_back = swap_sequences(grad_back)
    grad_signal, left_term = call(
        row_backward_kernel,
        me,
        [left_factor, values, grad_back],
        [by_row, left],
        flops=2 * row_flops,
    )
    (grad_left,) = call(
        left_sum_kernel,
        me,
        [left_term, other_values, other_grad_back],
        [left],
        flops=row_flops,
    )
    grad_right = (right_part.astype(F32) + other_right.astype(F32)).astype(BF16)
    output, grad_gate = call(
        functools.partial(output_kernel, seq),
        me,
        [gate, cotangent, *second_blocks],
        [whole, whole],
    )
    return (
        output.reshape(signal.shape),
        grad_gate.reshape(signal.shape),
        grad_signal.reshape(signal.shape),
        grad_left,
        grad_right,
    )


def plain_shards(signal, gating, upstream, left_factor, right_factor):
    seq = lax.axis_size("seq")
    rows, block_len = left_factor.shape[:2]
    cols, block_count = right_factor.shape[:2]
    channels = signal.shape[2]
    values = signal.reshape(rows, block_len, channels)
    gate = gating.reshape(rows, block_len, channels)
    cotangent = upstream.reshape(rows, block_len, channels)

    def einsum(spec, a, b):
        return jnp.einsum(spec, a, b, preferred_element_type=F32).astype(BF16)

    def all_to_all(blocks):
        return lax.all_to_all(blocks, "seq", split_axis=0, concat_axis=0, tiled=True)

    def to_columns(by_row):
        blocks = by_row.reshape(rows, seq, cols, channels).transpose(1, 0, 2, 3)
        return all_to_all(blocks).reshape(block_count, cols, channels)

    def to_rows(by_column):
        blocks = all_to_all(by_column.reshape(seq, rows, cols, channels))
        return blocks.transpose(1, 0, 2, 3).reshape(rows, block_len, channels)

    grad_rows = (cotangent.astype(F32) * gate.astype(F32)).astype(BF16)
    grad_column = to_columns(grad_rows)
    other_values = swap_sequences(values)
    mixed_column = to_columns(einsum("ikj,ijd->ikd", left_factor, values))
    grad_back = to_rows(einsum("kmi,mkd->ikd", right_factor, grad_column))
    second_rows = to_rows(einsum("kmi,ikd->mkd", right_factor, mixed_column))
    right_part = einsum("mkd,ikd->kmi", grad_column, mixed_column)
    other_right = swap_sequences(right_part)
    other_grad_back = swap_sequences(grad_back)
    grad_signal = einsum("ikj,ikd->ijd", left_factor, grad_back)
    left_term = einsum("ikd,ijd->ikj", grad_back, values)
    other_left = einsum("ikd,ijd->ikj", other_grad_back, other_values)
    grad_left = (left_term.astype(F32) + other_left.astype(F32)).astype(BF16)
    grad_right = (right_part.astype(F32) + other_right.astype(F32)).astype(BF16)
    wide = second_rows.astype(F32)
    output = (gate.astype(F32) * wide).astype(BF16)
    grad_gate = (cotangent.astype(F32) * wide).astype(BF16)
    return (
        output.reshape(signal.shape),
        grad_gate.reshape(signal.shape),
        grad_signal.reshape(signal.shape),
        grad_left,
        grad_right,
    )


def shards(signal, gating, upstream, left_factor, right_factor):
    seq = lax.axis_size("seq")
    cols = right_factor.shape[0]
    direct = seq <= 16 and seq & (seq - 1) == 0 and cols % 32 == 0
    run = direct_shards if direct else plain_shards
    return run(signal, gating, upstream, left_factor, right_factor)


def solution(mesh):
    by_position = P("dp", "seq", None)
    by_block = P("seq", None, None)
    return jax.shard_map(
        shards,
        mesh=mesh,
        in_specs=(by_position,) * 3 + (by_block,) * 2,
        out_specs=(by_position,) * 3 + (by_block,) * 2,
        check_vma=False,
    )
```

time: 184 us -> 159 us (0.86)
  starting transfers between devices: 8.62 us -> 104 us
  blocking collectives: 91.4 us -> 0 us
  matrix products: 15.8 us -> 0 us
  Pallas kernels: 0 us -> 14.9 us
  local copies, waits for them, and re-layouts: 16.4 us -> 3.66 us
  waiting for transfers between devices: 46.4 us -> 34.4 us
  other arithmetic: 4.35 us -> 0.98 us
    ppermute x0 -> x60, starting transfers between devices: none -> 99.8 us  [exchange(): lax.ppermute(blocks[s], 'seq', [(i, i ^ s) for i in range(seq)])]
    all_to_all x3 -> x0, blocking collectives: 91.4 us -> none  [exchange(): lax.all_to_all(blocks, 'seq', split_axis=0, concat_axis=0, tiled=True)]
    ppermute x0 -> x60, waiting for transfers between devices: none -> 34.4 us  [exchange(): lax.ppermute(blocks[s], 'seq', [(i, i ^ s) for i in range(seq)])]
    ppermute x3, waiting for transfers between devices: 28.3 us -> 0.01 us  [swap_sequences(): return lax.ppermute(array, 'dp', [(0, 1), (1, 0)])]
    all_to_all x1 -> x0, waiting for transfers between devices: 18.1 us -> none  [exchange(): lax.all_to_all(blocks, 'seq', split_axis=0, concat_axis=0, tiled=True)]
    dot_general x7 -> x0, matrix products: 15.8 us -> none  [the longest x2 5.58 us: left_term(): jnp.einsum('ikd,ijd->ikj', grad, vals, preferred_element_type=F32)]
    pallas_call x0 -> x8, Pallas kernels: none -> 14.9 us  [call(): pl.pallas_call(kernel, out_shape=out_shapes, in_specs=[pl.BlockSpec(memor...]
    reshape x5 -> x0, local copies, waits for them, and re-layouts: 7.61 us -> none  [the longest x2 3.83 us: shards(): second.reshape(seq, rows, cols, channels)]
  transfers between devices with their start and end apart: 4 -> 63, of which waited for: 3 -> 22; matrix products, arithmetic and copies ran while one was open for 7% -> 1% of each run, Pallas kernels for 0% -> 6%
where the time goes in v2:
time: 159 us
  starting transfers between devices  104 us (65%)
  waiting for transfers between devices  34.4 us (22%)
  Pallas kernels  14.9 us (9%)
  local copies, waits for them, and re-layouts  3.66 us (2%)
    ppermute x60, starting transfers between devices, exchange(): lax.ppermute(blocks[s], 'seq', [(i, i ^ s) for i in range(seq)])  99.8 us
    ppermute x60, waiting for transfers between devices, exchange(): lax.ppermute(blocks[s], 'seq', [(i, i ^ s) for i in range(seq)])  34.4 us
    pallas_call x8, Pallas kernels, call(): pl.pallas_call(kernel, out_shape=out_shapes, in_specs=[pl.BlockSpec(memor...  14.9 us
    ppermute x3, starting transfers between devices, swap_sequences(): return lax.ppermute(array, 'dp', [(0, 1), (1, 0)])  4.38 us
    unnamed x16, local copies, waits for them, and re-layouts  3.66 us
  transfers between devices with their start and end apart: 63, of which 22 were waited for; matrix products, arithmetic and copies ran while one was open for 1% of the time, Pallas kernels for 6%

profile of v2, /device:TPU:0, one launch (start us, length us, event | category | flops | bytes accessed | tf_op | source)
XLA Modules:
  0.0 158.8 jit_solution(16250907377008827673)
XLA Ops:
  4.0 2.6 %collective-permute-start.1 = (bf16[4,32,256]{2,1,0:T(8,128)(2,1)S(1)}, bf16[4,32,256]{2,1,0:T(8,128)(2,1)S(1)}, u32[]{:S(2)}, u32[]{:S(2)}) collective-permute-start(bf16[4,32,256]{2,1,0:T(8,128)(2,1)S(1)} %get-tuple-element.77), channel_id=1, source_target_pairs={{0,2},{1,3},{2,0},{3,1},{4,6},{5,7},{6,4},{7,5},{8,10},{9,11},{10,... | collective-permute-start | bytes 196616 | tf_op jit(solution)/shard_map/ppermute | solution.py:28
  6.6 2.3 %collective-permute-start.10 = (bf16[4,32,256]{2,1,0:T(8,128)(2,1)S(1)}, bf16[4,32,256]{2,1,0:T(8,128)(2,1)S(1)}, u32[]{:S(2)}, u32[]{:S(2)}) collective-permute-start(bf16[4,32,256]{2,1,0:T(8,128)(2,1)S(1)} %get-tuple-element.86), channel_id=1, source_target_pairs={{0,11},{1,10},{2,9},{3,8},{4,15},{5,14},{6,13},{7,12},{8,3},{9,2},... | collective-permute-start | bytes 196616 | tf_op jit(solution)/shard_map/ppermute | solution.py:28
  10.3 2.1 %collective-permute-start.12 = (bf16[4,32,256]{2,1,0:T(8,128)(2,1)S(1)}, bf16[4,32,256]{2,1,0:T(8,128)(2,1)S(1)}, u32[]{:S(2)}, u32[]{:S(2)}) collective-permute-start(bf16[4,32,256]{2,1,0:T(8,128)(2,1)S(1)} %get-tuple-element.88), channel_id=1, source_target_pairs={{0,13},{1,12},{2,15},{3,14},{4,9},{5,8},{6,11},{7,10},{8,5},{9,4},... | collective-permute-start | bytes 196616 | tf_op jit(solution)/shard_map/ppermute | solution.py:28
  12.4 2.3 %collective-permute-start.13 = (bf16[4,32,256]{2,1,0:T(8,128)(2,1)S(1)}, bf16[4,32,256]{2,1,0:T(8,128)(2,1)S(1)}, u32[]{:S(2)}, u32[]{:S(2)}) collective-permute-start(bf16[4,32,256]{2,1,0:T(8,128)(2,1)S(1)} %get-tuple-element.89), channel_id=1, source_target_pairs={{0,14},{1,15},{2,12},{3,13},{4,10},{5,11},{6,8},{7,9},{8,6},{9,7},... | collective-permute-start | bytes 196616 | tf_op jit(solution)/shard_map/ppermute | solution.py:28
  14.7 2.2 %collective-permute-start.14 = (bf16[4,32,256]{2,1,0:T(8,128)(2,1)S(1)}, bf16[4,32,256]{2,1,0:T(8,128)(2,1)S(1)}, u32[]{:S(2)}, u32[]{:S(2)}) collective-permute-start(bf16[4,32,256]{2,1,0:T(8,128)(2,1)S(1)} %get-tuple-element.90), channel_id=1, source_target_pairs={{0,15},{1,14},{2,13},{3,12},{4,11},{5,10},{6,9},{7,8},{8,7},{9,6},... | collective-permute-start | bytes 196616 | tf_op jit(solution)/shard_map/ppermute | solution.py:28
  18.4 2.6 %collective-permute-start.3 = (bf16[4,32,256]{2,1,0:T(8,128)(2,1)S(1)}, bf16[4,32,256]{2,1,0:T(8,128)(2,1)S(1)}, u32[]{:S(2)}, u32[]{:S(2)}) collective-permute-start(bf16[4,32,256]{2,1,0:T(8,128)(2,1)S(1)} %get-tuple-element.79), channel_id=1, source_target_pairs={{0,4},{1,5},{2,6},{3,7},{4,0},{5,1},{6,2},{7,3},{8,12},{9,13},{10,... | collective-permute-start | bytes 196616 | tf_op jit(solution)/shard_map/ppermute | solution.py:28
  22.0 2.8 %collective-permute-start.5 = (bf16[4,32,256]{2,1,0:T(8,128)(2,1)S(1)}, bf16[4,32,256]{2,1,0:T(8,128)(2,1)S(1)}, u32[]{:S(2)}, u32[]{:S(2)}) collective-permute-start(bf16[4,32,256]{2,1,0:T(8,128)(2,1)S(1)} %get-tuple-element.81), channel_id=1, source_target_pairs={{0,6},{1,7},{2,4},{3,5},{4,2},{5,3},{6,0},{7,1},{8,14},{9,15},{10,... | collective-permute-start | bytes 196616 | tf_op jit(solution)/shard_map/ppermute | solution.py:28
  25.8 3.2 %collective-permute-start.7 = (bf16[4,32,256]{2,1,0:T(8,128)(2,1)S(1)}, bf16[4,32,256]{2,1,0:T(8,128)(2,1)S(1)}, u32[]{:S(2)}, u32[]{:S(2)}) collective-permute-start(bf16[4,32,256]{2,1,0:T(8,128)(2,1)S(1)} %get-tuple-element.83), channel_id=1, source_target_pairs={{0,8},{1,9},{2,10},{3,11},{4,12},{5,13},{6,14},{7,15},{8,0},{9,1},... | collective-permute-start | bytes 196616 | tf_op jit(solution)/shard_map/ppermute | solution.py:28
  29.4 2.5 %collective-permute-start.9 = (bf16[4,32,256]{2,1,0:T(8,128)(2,1)S(1)}, bf16[4,32,256]{2,1,0:T(8,128)(2,1)S(1)}, u32[]{:S(2)}, u32[]{:S(2)}) collective-permute-start(bf16[4,32,256]{2,1,0:T(8,128)(2,1)S(1)} %get-tuple-element.85), channel_id=1, source_target_pairs={{0,10},{1,11},{2,8},{3,9},{4,14},{5,15},{6,12},{7,13},{8,2},{9,3},... | collective-permute-start | bytes 196616 | tf_op jit(solution)/shard_map/ppermute | solution.py:28
  32.2 5.3 %collective-permute-done.8.refs_9_ = bf16[4,32,256]{2,1,0:T(8,128)(2,1)S(1)} collective-permute-done((bf16[4,32,256]{2,1,0:T(8,128)(2,1)S(1)}, bf16[4,32,256]{2,1,0:T(8,128)(2,1)S(1)}, u32[]{:S(2)}, u32[]{:S(2)}) %collective-permute-start.8) | collective-permute-done | bytes 65568 | tf_op jit(solution)/shard_map/ppermute | solution.py:28
  37.5 2.1 %collective-permute-done.9.refs_10_ = bf16[4,32,256]{2,1,0:T(8,128)(2,1)S(1)} collective-permute-done((bf16[4,32,256]{2,1,0:T(8,128)(2,1)S(1)}, bf16[4,32,256]{2,1,0:T(8,128)(2,1)S(1)}, u32[]{:S(2)}, u32[]{:S(2)}) %collective-permute-start.9) | collective-permute-done | bytes 65568 | tf_op jit(solution)/shard_map/ppermute | solution.py:28
  40.7 3.0 %shard_map.93 = (bf16[4,32,256]{2,1,0:T(8,128)(2,1)S(1)}, bf16[4,32,256]{2,1,0:T(8,128)(2,1)S(1)}, bf16[4,32,256]{2,1,0:T(8,128)(2,1)S(1)}, bf16[4,32,256]{2,1,0...) custom-call(s32[1]{0:T(128)} %bitcast.me_ref, ...), custom_call_target="tpu_custom_call" | custom-call | flops 67108864 | bytes 3407872 | tf_op jit(solution)/shard_map/pallas_call | solution.py:35
  45.6 1.7 %collective-permute-start.49 = (bf16[4,32,256]{2,1,0:T(8,128)(2,1)S(1)}, bf16[4,32,256]{2,1,0:T(8,128)(2,1)S(1)}, u32[]{:S(2)}, u32[]{:S(2)}) collective-permute-start(bf16[4,32,256]{2,1,0:T(8,128)(2,1)S(1)} %get-tuple-element.131), channel_id=1, source_target_pairs={{0,5},{1,4},{2,7},{3,6},{4,1},{5,0},{6,3},{7,2},{8,13},{9,12},{10,... | collective-permute-start | bytes 196616 | tf_op jit(solution)/shard_map/ppermute | solution.py:28
  52.6 2.7 %collective-permute-start.54 = (bf16[4,32,256]{2,1,0:T(8,128)(2,1)S(1)}, bf16[4,32,256]{2,1,0:T(8,128)(2,1)S(1)}, u32[]{:S(2)}, u32[]{:S(2)}) collective-permute-start(bf16[4,32,256]{2,1,0:T(8,128)(2,1)S(1)} %get-tuple-element.136), channel_id=1, source_target_pairs={{0,10},{1,11},{2,8},{3,9},{4,14},{5,15},{6,12},{7,13},{8,2},{9,3},... | collective-permute-start | bytes 196616 | tf_op jit(solution)/shard_map/ppermute | solution.py:28
  56.2 2.8 %collective-permute-start.56 = (bf16[4,32,256]{2,1,0:T(8,128)(2,1)S(1)}, bf16[4,32,256]{2,1,0:T(8,128)(2,1)S(1)}, u32[]{:S(2)}, u32[]{:S(2)}) collective-permute-start(bf16[4,32,256]{2,1,0:T(8,128)(2,1)S(1)} %get-tuple-element.138), channel_id=1, source_target_pairs={{0,12},{1,13},{2,14},{3,15},{4,8},{5,9},{6,10},{7,11},{8,4},{9,5},... | collective-permute-start | bytes 196616 | tf_op jit(solution)/shard_map/ppermute | solution.py:28
  59.0 4.1 %collective-permute-start.57 = (bf16[4,32,256]{2,1,0:T(8,128)(2,1)S(1)}, bf16[4,32,256]{2,1,0:T(8,128)(2,1)S(1)}, u32[]{:S(2)}, u32[]{:S(2)}) collective-permute-start(bf16[4,32,256]{2,1,0:T(8,128)(2,1)S(1)} %get-tuple-element.139), channel_id=1, source_target_pairs={{0,13},{1,12},{2,15},{3,14},{4,9},{5,8},{6,11},{7,10},{8,5},{9,4},... | collective-permute-start | bytes 196616 | tf_op jit(solution)/shard_map/ppermute | solution.py:28
  63.4 2.5 %collective-permute-start.58 = (bf16[4,32,256]{2,1,0:T(8,128)(2,1)S(1)}, bf16[4,32,256]{2,1,0:T(8,128)(2,1)S(1)}, u32[]{:S(2)}, u32[]{:S(2)}) collective-permute-start(bf16[4,32,256]{2,1,0:T(8,128)(2,1)S(1)} %get-tuple-element.140), channel_id=1, source_target_pairs={{0,14},{1,15},{2,12},{3,13},{4,10},{5,11},{6,8},{7,9},{8,6},{9,7},... | collective-permute-start | bytes 196616 | tf_op jit(solution)/shard_map/ppermute | solution.py:28
  66.2 2.0 %collective-permute-start.59 = (bf16[4,32,256]{2,1,0:T(8,128)(2,1)S(1)}, bf16[4,32,256]{2,1,0:T(8,128)(2,1)S(1)}, u32[]{:S(2)}, u32[]{:S(2)}) collective-permute-start(bf16[4,32,256]{2,1,0:T(8,128)(2,1)S(1)} %get-tuple-element.141), channel_id=1, source_target_pairs={{0,15},{1,14},{2,13},{3,12},{4,11},{5,10},{6,9},{7,8},{8,7},{9,6},... | collective-permute-start | bytes 196616 | tf_op jit(solution)/shard_map/ppermute | solution.py:28
  69.8 1.7 %collective-permute-start.16 = (bf16[4,32,256]{2,1,0:T(8,128)(2,1)S(1)}, bf16[4,32,256]{2,1,0:T(8,128)(2,1)S(1)}, u32[]{:S(2)}, u32[]{:S(2)}) collective-permute-start(bf16[4,32,256]{2,1,0:T(8,128)(2,1)S(1)} %get-tuple-element.94), channel_id=1, source_target_pairs={{0,2},{1,3},{2,0},{3,1},{4,6},{5,7},{6,4},{7,5},{8,10},{9,11},{10,... | collective-permute-start | bytes 196616 | tf_op jit(solution)/shard_map/ppermute | solution.py:28
  74.6 4.1 %collective-permute-start.18 = (bf16[4,32,256]{2,1,0:T(8,128)(2,1)S(1)}, bf16[4,32,256]{2,1,0:T(8,128)(2,1)S(1)}, u32[]{:S(2)}, u32[]{:S(2)}) collective-permute-start(bf16[4,32,256]{2,1,0:T(8,128)(2,1)S(1)} %get-tuple-element.96), channel_id=1, source_target_pairs={{0,4},{1,5},{2,6},{3,7},{4,0},{5,1},{6,2},{7,3},{8,12},{9,13},{10,... | collective-permute-start | bytes 196616 | tf_op jit(solution)/shard_map/ppermute | solution.py:28
  78.8 1.7 %collective-permute-start.20 = (bf16[4,32,256]{2,1,0:T(8,128)(2,1)S(1)}, bf16[4,32,256]{2,1,0:T(8,128)(2,1)S(1)}, u32[]{:S(2)}, u32[]{:S(2)}) collective-permute-start(bf16[4,32,256]{2,1,0:T(8,128)(2,1)S(1)} %get-tuple-element.98), channel_id=1, source_target_pairs={{0,6},{1,7},{2,4},{3,5},{4,2},{5,3},{6,0},{7,1},{8,14},{9,15},{10,... | collective-permute-start | bytes 196616 | tf_op jit(solution)/shard_map/ppermute | solution.py:28
  84.7 1.7 %collective-permute-start.23 = (bf16[4,32,256]{2,1,0:T(8,128)(2,1)S(1)}, bf16[4,32,256]{2,1,0:T(8,128)(2,1)S(1)}, u32[]{:S(2)}, u32[]{:S(2)}) collective-permute-start(bf16[4,32,256]{2,1,0:T(8,128)(2,1)S(1)} %get-tuple-element.101), channel_id=1, source_target_pairs={{0,9},{1,8},{2,11},{3,10},{4,13},{5,12},{6,15},{7,14},{8,1},{9,0},... | collective-permute-start | bytes 196616 | tf_op jit(solution)/shard_map/ppermute | solution.py:28
  86.4 3.6 %collective-permute-start.24 = (bf16[4,32,256]{2,1,0:T(8,128)(2,1)S(1)}, bf16[4,32,256]{2,1,0:T(8,128)(2,1)S(1)}, u32[]{:S(2)}, u32[]{:S(2)}) collective-permute-start(bf16[4,32,256]{2,1,0:T(8,128)(2,1)S(1)} %get-tuple-element.102), channel_id=1, source_target_pairs={{0,10},{1,11},{2,8},{3,9},{4,14},{5,15},{6,12},{7,13},{8,2},{9,3},... | collective-permute-start | bytes 196616 | tf_op jit(solution)/shard_map/ppermute | solution.py:28
  90.0 2.0 %collective-permute-done.22.refs_8_ = bf16[4,32,256]{2,1,0:T(8,128)(2,1)S(1)} collective-permute-done((bf16[4,32,256]{2,1,0:T(8,128)(2,1)S(1)}, bf16[4,32,256]{2,1,0:T(8,128)(2,1)S(1)}, u32[]{:S(2)}, u32[]{:S(2)}) %collective-permute-start.22) | collective-permute-done | bytes 65568 | tf_op jit(solution)/shard_map/ppermute | solution.py:28
  92.1 2.1 %collective-permute-done.23.refs_9_ = bf16[4,32,256]{2,1,0:T(8,128)(2,1)S(1)} collective-permute-done((bf16[4,32,256]{2,1,0:T(8,128)(2,1)S(1)}, bf16[4,32,256]{2,1,0:T(8,128)(2,1)S(1)}, u32[]{:S(2)}, u32[]{:S(2)}) %collective-permute-start.23) | collective-permute-done | bytes 65568 | tf_op jit(solution)/shard_map/ppermute | solution.py:28
  94.2 2.3 %collective-permute-start.26 = (bf16[4,32,256]{2,1,0:T(8,128)(2,1)S(1)}, bf16[4,32,256]{2,1,0:T(8,128)(2,1)S(1)}, u32[]{:S(2)}, u32[]{:S(2)}) collective-permute-start(bf16[4,32,256]{2,1,0:T(8,128)(2,1)S(1)} %get-tuple-element.104), channel_id=1, source_target_pairs={{0,12},{1,13},{2,14},{3,15},{4,8},{5,9},{6,10},{7,11},{8,4},{9,5},... | collective-permute-start | bytes 196616 | tf_op jit(solution)/shard_map/ppermute | solution.py:28
  96.9 1.8 %collective-permute-start.27 = (bf16[4,32,256]{2,1,0:T(8,128)(2,1)S(1)}, bf16[4,32,256]{2,1,0:T(8,128)(2,1)S(1)}, u32[]{:S(2)}, u32[]{:S(2)}) collective-permute-start(bf16[4,32,256]{2,1,0:T(8,128)(2,1)S(1)} %get-tuple-element.105), channel_id=1, source_target_pairs={{0,13},{1,12},{2,15},{3,14},{4,9},{5,8},{6,11},{7,10},{8,5},{9,4},... | collective-permute-start | bytes 196616 | tf_op jit(solution)/shard_map/ppermute | solution.py:28
  98.8 2.8 %collective-permute-start.28 = (bf16[4,32,256]{2,1,0:T(8,128)(2,1)S(1)}, bf16[4,32,256]{2,1,0:T(8,128)(2,1)S(1)}, u32[]{:S(2)}, u32[]{:S(2)}) collective-permute-start(bf16[4,32,256]{2,1,0:T(8,128)(2,1)S(1)} %get-tuple-element.106), channel_id=1, source_target_pairs={{0,14},{1,15},{2,12},{3,13},{4,10},{5,11},{6,8},{7,9},{8,6},{9,7},... | collective-permute-start | bytes 196616 | tf_op jit(solution)/shard_map/ppermute | solution.py:28
  101.7 2.7 %collective-permute-start.29 = (bf16[4,32,256]{2,1,0:T(8,128)(2,1)S(1)}, bf16[4,32,256]{2,1,0:T(8,128)(2,1)S(1)}, u32[]{:S(2)}, u32[]{:S(2)}) collective-permute-start(bf16[4,32,256]{2,1,0:T(8,128)(2,1)S(1)} %get-tuple-element.107), channel_id=1, source_target_pairs={{0,15},{1,14},{2,13},{3,12},{4,11},{5,10},{6,9},{7,8},{8,7},{9,6},... | collective-permute-start | bytes 196616 | tf_op jit(solution)/shard_map/ppermute | solution.py:28
  104.3 1.8 %collective-permute-done.28.refs_14_ = bf16[4,32,256]{2,1,0:T(8,128)(2,1)S(1)} collective-permute-done((bf16[4,32,256]{2,1,0:T(8,128)(2,1)S(1)}, bf16[4,32,256]{2,1,0:T(8,128)(2,1)S(1)}, u32[]{:S(2)}, u32[]{:S(2)}) %collective-permute-start.28) | collective-permute-done | bytes 65568 | tf_op jit(solution)/shard_map/ppermute | solution.py:28
  106.2 2.4 %collective-permute-done.29.refs_15_ = bf16[4,32,256]{2,1,0:T(8,128)(2,1)S(1)} collective-permute-done((bf16[4,32,256]{2,1,0:T(8,128)(2,1)S(1)}, bf16[4,32,256]{2,1,0:T(8,128)(2,1)S(1)}, u32[]{:S(2)}, u32[]{:S(2)}) %collective-permute-start.29) | collective-permute-done | bytes 65568 | tf_op jit(solution)/shard_map/ppermute | solution.py:28
  108.6 3.1 %shard_map.95 = (bf16[4,32,256]{2,1,0:T(8,128)(2,1)S(1)}, bf16[4,32,256]{2,1,0:T(8,128)(2,1)S(1)}, bf16[4,32,256]{2,1,0:T(8,128)(2,1)S(1)}, bf16[4,32,256]{2,1,0...) custom-call(s32[1]{0:T(128)} %bitcast.me_ref, ...), custom_call_target="tpu_custom_call" | custom-call | flops 134217728 | bytes 3670016 | tf_op jit(solution)/shard_map/pallas_call | solution.py:35
  113.6 2.0 %collective-permute-start.33 = (bf16[4,32,256]{2,1,0:T(8,128)(2,1)S(1)}, bf16[4,32,256]{2,1,0:T(8,128)(2,1)S(1)}, u32[]{:S(2)}, u32[]{:S(2)}) collective-permute-start(bf16[4,32,256]{2,1,0:T(8,128)(2,1)S(1)} %get-tuple-element.112), channel_id=1, source_target_pairs={{0,4},{1,5},{2,6},{3,7},{4,0},{5,1},{6,2},{7,3},{8,12},{9,13},{10,... | collective-permute-start | bytes 196616 | tf_op jit(solution)/shard_map/ppermute | solution.py:28
  117.5 2.3 %collective-permute-start.35 = (bf16[4,32,256]{2,1,0:T(8,128)(2,1)S(1)}, bf16[4,32,256]{2,1,0:T(8,128)(2,1)S(1)}, u32[]{:S(2)}, u32[]{:S(2)}) collective-permute-start(bf16[4,32,256]{2,1,0:T(8,128)(2,1)S(1)} %get-tuple-element.114), channel_id=1, source_target_pairs={{0,6},{1,7},{2,4},{3,5},{4,2},{5,3},{6,0},{7,1},{8,14},{9,15},{10,... | collective-permute-start | bytes 196616 | tf_op jit(solution)/shard_map/ppermute | solution.py:28
  121.1 2.3 %collective-permute-start.37 = (bf16[4,32,256]{2,1,0:T(8,128)(2,1)S(1)}, bf16[4,32,256]{2,1,0:T(8,128)(2,1)S(1)}, u32[]{:S(2)}, u32[]{:S(2)}) collective-permute-start(bf16[4,32,256]{2,1,0:T(8,128)(2,1)S(1)} %get-tuple-element.116), channel_id=1, source_target_pairs={{0,8},{1,9},{2,10},{3,11},{4,12},{5,13},{6,14},{7,15},{8,0},{9,1},... | collective-permute-start | bytes 196616 | tf_op jit(solution)/shard_map/ppermute | solution.py:28
  123.5 1.6 %collective-permute-start.38 = (bf16[4,32,256]{2,1,0:T(8,128)(2,1)S(1)}, bf16[4,32,256]{2,1,0:T(8,128)(2,1)S(1)}, u32[]{:S(2)}, u32[]{:S(2)}) collective-permute-start(bf16[4,32,256]{2,1,0:T(8,128)(2,1)S(1)} %get-tuple-element.117), channel_id=1, source_target_pairs={{0,9},{1,8},{2,11},{3,10},{4,13},{5,12},{6,15},{7,14},{8,1},{9,0},... | collective-permute-start | bytes 196616 | tf_op jit(solution)/shard_map/ppermute | solution.py:28
  125.1 1.6 %collective-permute-start.39 = (bf16[4,32,256]{2,1,0:T(8,128)(2,1)S(1)}, bf16[4,32,256]{2,1,0:T(8,128)(2,1)S(1)}, u32[]{:S(2)}, u32[]{:S(2)}) collective-permute-start(bf16[4,32,256]{2,1,0:T(8,128)(2,1)S(1)} %get-tuple-element.118), channel_id=1, source_target_pairs={{0,10},{1,11},{2,8},{3,9},{4,14},{5,15},{6,12},{7,13},{8,2},{9,3},... | collective-permute-start | bytes 196616 | tf_op jit(solution)/shard_map/ppermute | solution.py:28
  127.6 1.6 %collective-permute-start.40 = (bf16[4,32,256]{2,1,0:T(8,128)(2,1)S(1)}, bf16[4,32,256]{2,1,0:T(8,128)(2,1)S(1)}, u32[]{:S(2)}, u32[]{:S(2)}) collective-permute-start(bf16[4,32,256]{2,1,0:T(8,128)(2,1)S(1)} %get-tuple-element.119), channel_id=1, source_target_pairs={{0,11},{1,10},{2,9},{3,8},{4,15},{5,14},{6,13},{7,12},{8,3},{9,2},... | collective-permute-start | bytes 196616 | tf_op jit(solution)/shard_map/ppermute | solution.py:28
  129.2 2.5 %collective-permute-done.38.refs_9_ = bf16[4,32,256]{2,1,0:T(8,128)(2,1)S(1)} collective-permute-done((bf16[4,32,256]{2,1,0:T(8,128)(2,1)S(1)}, bf16[4,32,256]{2,1,0:T(8,128)(2,1)S(1)}, u32[]{:S(2)}, u32[]{:S(2)}) %collective-permute-start.38) | collective-permute-done | bytes 65568 | tf_op jit(solution)/shard_map/ppermute | solution.py:28
  133.1 2.1 %collective-permute-done.39.refs_10_ = bf16[4,32,256]{2,1,0:T(8,128)(2,1)S(1)} collective-permute-done((bf16[4,32,256]{2,1,0:T(8,128)(2,1)S(1)}, bf16[4,32,256]{2,1,0:T(8,128)(2,1)S(1)}, u32[]{:S(2)}, u32[]{:S(2)}) %collective-permute-start.39) | collective-permute-done | bytes 65568 | tf_op jit(solution)/shard_map/ppermute | solution.py:28
  135.2 2.2 %collective-permute-start.41 = (bf16[4,32,256]{2,1,0:T(8,128)(2,1)S(1)}, bf16[4,32,256]{2,1,0:T(8,128)(2,1)S(1)}, u32[]{:S(2)}, u32[]{:S(2)}) collective-permute-start(bf16[4,32,256]{2,1,0:T(8,128)(2,1)S(1)} %get-tuple-element.120), channel_id=1, source_target_pairs={{0,12},{1,13},{2,14},{3,15},{4,8},{5,9},{6,10},{7,11},{8,4},{9,5},... | collective-permute-start | bytes 196616 | tf_op jit(solution)/shard_map/ppermute | solution.py:28
  138.4 2.9 %collective-permute-done.41.refs_12_ = bf16[4,32,256]{2,1,0:T(8,128)(2,1)S(1)} collective-permute-done((bf16[4,32,256]{2,1,0:T(8,128)(2,1)S(1)}, bf16[4,32,256]{2,1,0:T(8,128)(2,1)S(1)}, u32[]{:S(2)}, u32[]{:S(2)}) %collective-permute-start.41) | collective-permute-done | bytes 65568 | tf_op jit(solution)/shard_map/ppermute | solution.py:28
  141.3 2.5 %collective-permute-start.43 = (bf16[4,32,256]{2,1,0:T(8,128)(2,1)S(1)}, bf16[4,32,256]{2,1,0:T(8,128)(2,1)S(1)}, u32[]{:S(2)}, u32[]{:S(2)}) collective-permute-start(bf16[4,32,256]{2,1,0:T(8,128)(2,1)S(1)} %get-tuple-element.122), channel_id=1, source_target_pairs={{0,14},{1,15},{2,12},{3,13},{4,10},{5,11},{6,8},{7,9},{8,6},{9,7},... | collective-permute-start | bytes 196616 | tf_op jit(solution)/shard_map/ppermute | solution.py:28
  145.2 3.1 %collective-permute-done.43.refs_14_ = bf16[4,32,256]{2,1,0:T(8,128)(2,1)S(1)} collective-permute-done((bf16[4,32,256]{2,1,0:T(8,128)(2,1)S(1)}, bf16[4,32,256]{2,1,0:T(8,128)(2,1)S(1)}, u32[]{:S(2)}, u32[]{:S(2)}) %collective-permute-start.43) | collective-permute-done | bytes 65568 | tf_op jit(solution)/shard_map/ppermute | solution.py:28
  148.2 1.9 %collective-permute-done.44.refs_15_ = bf16[4,32,256]{2,1,0:T(8,128)(2,1)S(1)} collective-permute-done((bf16[4,32,256]{2,1,0:T(8,128)(2,1)S(1)}, bf16[4,32,256]{2,1,0:T(8,128)(2,1)S(1)}, u32[]{:S(2)}, u32[]{:S(2)}) %collective-permute-start.44) | collective-permute-done | bytes 65568 | tf_op jit(solution)/shard_map/ppermute | solution.py:28
  150.2 1.8 %shard_map.96 = (bf16[4,16,32,256]{3,2,1,0:T(8,128)(2,1)}, bf16[4,16,32,256]{3,2,1,0:T(8,128)(2,1)}) custom-call(s32[1]{0:T(128)} %bitcast.me_ref, bf16[4,16,32,256]{3,2,1,0:T(8,128)(2,1)S(1)} %bitcast.14, bf16[4,16,32,256]{3,2,1,0:T(8,128)(2,1)S(1)} %bitcast.16, bf16[4,32,256]{2,1,0:T(8,128)(2,1)S(1)} %get-tuple-element.108.refs_0_, ...), custom_call_target="tpu_custom_call" | custom-call | bytes 5242880 | tf_op jit(solution)/shard_map/pallas_call | solution.py:35
  151.9 3.8 %shard_map.98 = (bf16[4,512,256]{2,1,0:T(8,128)(2,1)}, bf16[4,512,512]{2,1,0:T(8,128)(2,1)S(1)}) custom-call(s32[1]{0:T(128)} %bitcast.me_ref, bf16[4,512,512]{2,1,0:T(8,128)(2,1)} %left_ref.3, bf16[4,512,256]{2,1,0:T(8,128)(2,1)S(1)} %bitcast.12, bf16[4,512,256]{2,1,0:T(8,128)(2,1)S(1)} %bitcast.9), custom_call_target="tpu_custom_call" | custom-call | flops 1073741824 | bytes 7340032 | tf_op jit(solution)/shard_map/pallas_call | solution.py:35
  156.8 2.1 %shard_map.99 = bf16[4,512,512]{2,1,0:T(8,128)(2,1)} custom-call(s32[1]{0:T(128)} %bitcast.me_ref, bf16[4,512,512]{2,1,0:T(8,128)(2,1)S(1)} %get-tuple-element.143.term_ref, bf16[4,512,256]{2,1,0:T(8,128)(2,1)S(1)} %collective-permute-done.60.values_ref, bf16[4,512,256]{2,1,0:T(8,128)(2,1)S(1)} %collective-permute-done.61.grad_ref), custom_call_target="tpu_custom_call" | custom-call | flops 536870912 | bytes 6291456 | tf_op jit(solution)/shard_map/pallas_call | solution.py:35
  (103 shorter events, 38.9 us)
Async XLA Ops:
  3.5 8.9 %collective-permute-start = (bf16[4,32,256]{2,1,0:T(8,128)(2,1)S(1)}, bf16[4,32,256]{2,1,0:T(8,128)(2,1)S(1)}, u32[]{:S(2)}, u32[]{:S(2)}) collective-permute-start(bf16[4,32,256]{2,1,0:T(8,128)(2,1)S(1)} %get-tuple-element.76), channel_id=1, source_target_pairs={{0,1},{1,0},{2,3},{3,2},{4,5},{5,4},{6,7},{7,6},{8,9},{9,8},{10,11... | collective-permute-start | bytes 196616 | tf_op jit(solution)/shard_map/ppermute | solution.py:28
  4.0 10.7 %collective-permute-start.1 = (bf16[4,32,256]{2,1,0:T(8,128)(2,1)S(1)}, bf16[4,32,256]{2,1,0:T(8,128)(2,1)S(1)}, u32[]{:S(2)}, u32[]{:S(2)}) collective-permute-start(bf16[4,32,256]{2,1,0:T(8,128)(2,1)S(1)} %get-tuple-element.77), channel_id=1, source_target_pairs={{0,2},{1,3},{2,0},{3,1},{4,6},{5,7},{6,4},{7,5},{8,10},{9,11},{10,... | collective-permute-start | bytes 196616 | tf_op jit(solution)/shard_map/ppermute | solution.py:28
  6.6 10.3 %collective-permute-start.10 = (bf16[4,32,256]{2,1,0:T(8,128)(2,1)S(1)}, bf16[4,32,256]{2,1,0:T(8,128)(2,1)S(1)}, u32[]{:S(2)}, u32[]{:S(2)}) collective-permute-start(bf16[4,32,256]{2,1,0:T(8,128)(2,1)S(1)} %get-tuple-element.86), channel_id=1, source_target_pairs={{0,11},{1,10},{2,9},{3,8},{4,15},{5,14},{6,13},{7,12},{8,3},{9,2},... | collective-permute-start | bytes 196616 | tf_op jit(solution)/shard_map/ppermute | solution.py:28
  8.9 9.5 %collective-permute-start.11 = (bf16[4,32,256]{2,1,0:T(8,128)(2,1)S(1)}, bf16[4,32,256]{2,1,0:T(8,128)(2,1)S(1)}, u32[]{:S(2)}, u32[]{:S(2)}) collective-permute-start(bf16[4,32,256]{2,1,0:T(8,128)(2,1)S(1)} %get-tuple-element.87), channel_id=1, source_target_pairs={{0,12},{1,13},{2,14},{3,15},{4,8},{5,9},{6,10},{7,11},{8,4},{9,5},... | collective-permute-start | bytes 196616 | tf_op jit(solution)/shard_map/ppermute | solution.py:28
  10.3 10.7 %collective-permute-start.12 = (bf16[4,32,256]{2,1,0:T(8,128)(2,1)S(1)}, bf16[4,32,256]{2,1,0:T(8,128)(2,1)S(1)}, u32[]{:S(2)}, u32[]{:S(2)}) collective-permute-start(bf16[4,32,256]{2,1,0:T(8,128)(2,1)S(1)} %get-tuple-element.88), channel_id=1, source_target_pairs={{0,13},{1,12},{2,15},{3,14},{4,9},{5,8},{6,11},{7,10},{8,5},{9,4},... | collective-permute-start | bytes 196616 | tf_op jit(solution)/shard_map/ppermute | solution.py:28
  12.4 9.6 %collective-permute-start.13 = (bf16[4,32,256]{2,1,0:T(8,128)(2,1)S(1)}, bf16[4,32,256]{2,1,0:T(8,128)(2,1)S(1)}, u32[]{:S(2)}, u32[]{:S(2)}) collective-permute-start(bf16[4,32,256]{2,1,0:T(8,128)(2,1)S(1)} %get-tuple-element.89), channel_id=1, source_target_pairs={{0,14},{1,15},{2,12},{3,13},{4,10},{5,11},{6,8},{7,9},{8,6},{9,7},... | collective-permute-start | bytes 196616 | tf_op jit(solution)/shard_map/ppermute | solution.py:28
  14.7 10.1 %collective-permute-start.14 = (bf16[4,32,256]{2,1,0:T(8,128)(2,1)S(1)}, bf16[4,32,256]{2,1,0:T(8,128)(2,1)S(1)}, u32[]{:S(2)}, u32[]{:S(2)}) collective-permute-start(bf16[4,32,256]{2,1,0:T(8,128)(2,1)S(1)} %get-tuple-element.90), channel_id=1, source_target_pairs={{0,15},{1,14},{2,13},{3,12},{4,11},{5,10},{6,9},{7,8},{8,7},{9,6},... | collective-permute-start | bytes 196616 | tf_op jit(solution)/shard_map/ppermute | solution.py:28
  16.9 8.9 %collective-permute-start.2 = (bf16[4,32,256]{2,1,0:T(8,128)(2,1)S(1)}, bf16[4,32,256]{2,1,0:T(8,128)(2,1)S(1)}, u32[]{:S(2)}, u32[]{:S(2)}) collective-permute-start(bf16[4,32,256]{2,1,0:T(8,128)(2,1)S(1)} %get-tuple-element.78), channel_id=1, source_target_pairs={{0,3},{1,2},{2,1},{3,0},{4,7},{5,6},{6,5},{7,4},{8,11},{9,10},{10,... | collective-permute-start | bytes 196616 | tf_op jit(solution)/shard_map/ppermute | solution.py:28
  18.4 10.6 %collective-permute-start.3 = (bf16[4,32,256]{2,1,0:T(8,128)(2,1)S(1)}, bf16[4,32,256]{2,1,0:T(8,128)(2,1)S(1)}, u32[]{:S(2)}, u32[]{:S(2)}) collective-permute-start(bf16[4,32,256]{2,1,0:T(8,128)(2,1)S(1)} %get-tuple-element.79), channel_id=1, source_target_pairs={{0,4},{1,5},{2,6},{3,7},{4,0},{5,1},{6,2},{7,3},{8,12},{9,13},{10,... | collective-permute-start | bytes 196616 | tf_op jit(solution)/shard_map/ppermute | solution.py:28
  21.0 8.4 %collective-permute-start.4 = (bf16[4,32,256]{2,1,0:T(8,128)(2,1)S(1)}, bf16[4,32,256]{2,1,0:T(8,128)(2,1)S(1)}, u32[]{:S(2)}, u32[]{:S(2)}) collective-permute-start(bf16[4,32,256]{2,1,0:T(8,128)(2,1)S(1)} %get-tuple-element.80), channel_id=1, source_target_pairs={{0,5},{1,4},{2,7},{3,6},{4,1},{5,0},{6,3},{7,2},{8,13},{9,12},{10,... | collective-permute-start | bytes 196616 | tf_op jit(solution)/shard_map/ppermute | solution.py:28
  22.0 9.9 %collective-permute-start.5 = (bf16[4,32,256]{2,1,0:T(8,128)(2,1)S(1)}, bf16[4,32,256]{2,1,0:T(8,128)(2,1)S(1)}, u32[]{:S(2)}, u32[]{:S(2)}) collective-permute-start(bf16[4,32,256]{2,1,0:T(8,128)(2,1)S(1)} %get-tuple-element.81), channel_id=1, source_target_pairs={{0,6},{1,7},{2,4},{3,5},{4,2},{5,3},{6,0},{7,1},{8,14},{9,15},{10,... | collective-permute-start | bytes 196616 | tf_op jit(solution)/shard_map/ppermute | solution.py:28
  24.8 7.1 %collective-permute-start.6 = (bf16[4,32,256]{2,1,0:T(8,128)(2,1)S(1)}, bf16[4,32,256]{2,1,0:T(8,128)(2,1)S(1)}, u32[]{:S(2)}, u32[]{:S(2)}) collective-permute-start(bf16[4,32,256]{2,1,0:T(8,128)(2,1)S(1)} %get-tuple-element.82), channel_id=1, source_target_pairs={{0,7},{1,6},{2,5},{3,4},{4,3},{5,2},{6,1},{7,0},{8,15},{9,14},{10,... | collective-permute-start | bytes 196616 | tf_op jit(solution)/shard_map/ppermute | solution.py:28
  25.8 6.4 %collective-permute-start.7 = (bf16[4,32,256]{2,1,0:T(8,128)(2,1)S(1)}, bf16[4,32,256]{2,1,0:T(8,128)(2,1)S(1)}, u32[]{:S(2)}, u32[]{:S(2)}) collective-permute-start(bf16[4,32,256]{2,1,0:T(8,128)(2,1)S(1)} %get-tuple-element.83), channel_id=1, source_target_pairs={{0,8},{1,9},{2,10},{3,11},{4,12},{5,13},{6,14},{7,15},{8,0},{9,1},... | collective-permute-start | bytes 196616 | tf_op jit(solution)/shard_map/ppermute | solution.py:28
  29.0 8.5 %collective-permute-start.8 = (bf16[4,32,256]{2,1,0:T(8,128)(2,1)S(1)}, bf16[4,32,256]{2,1,0:T(8,128)(2,1)S(1)}, u32[]{:S(2)}, u32[]{:S(2)}) collective-permute-start(bf16[4,32,256]{2,1,0:T(8,128)(2,1)S(1)} %get-tuple-element.84), channel_id=1, source_target_pairs={{0,9},{1,8},{2,11},{3,10},{4,13},{5,12},{6,15},{7,14},{8,1},{9,0},... | collective-permute-start | bytes 196616 | tf_op jit(solution)/shard_map/ppermute | solution.py:28
  29.4 10.3 %collective-permute-start.9 = (bf16[4,32,256]{2,1,0:T(8,128)(2,1)S(1)}, bf16[4,32,256]{2,1,0:T(8,128)(2,1)S(1)}, u32[]{:S(2)}, u32[]{:S(2)}) collective-permute-start(bf16[4,32,256]{2,1,0:T(8,128)(2,1)S(1)} %get-tuple-element.85), channel_id=1, source_target_pairs={{0,10},{1,11},{2,8},{3,9},{4,14},{5,15},{6,12},{7,13},{8,2},{9,3},... | collective-permute-start | bytes 196616 | tf_op jit(solution)/shard_map/ppermute | solution.py:28
  45.6 7.0 %collective-permute-start.49 = (bf16[4,32,256]{2,1,0:T(8,128)(2,1)S(1)}, bf16[4,32,256]{2,1,0:T(8,128)(2,1)S(1)}, u32[]{:S(2)}, u32[]{:S(2)}) collective-permute-start(bf16[4,32,256]{2,1,0:T(8,128)(2,1)S(1)} %get-tuple-element.131), channel_id=1, source_target_pairs={{0,5},{1,4},{2,7},{3,6},{4,1},{5,0},{6,3},{7,2},{8,13},{9,12},{10,... | collective-permute-start | bytes 196616 | tf_op jit(solution)/shard_map/ppermute | solution.py:28
  47.3 8.0 %collective-permute-start.50 = (bf16[4,32,256]{2,1,0:T(8,128)(2,1)S(1)}, bf16[4,32,256]{2,1,0:T(8,128)(2,1)S(1)}, u32[]{:S(2)}, u32[]{:S(2)}) collective-permute-start(bf16[4,32,256]{2,1,0:T(8,128)(2,1)S(1)} %get-tuple-element.132), channel_id=1, source_target_pairs={{0,6},{1,7},{2,4},{3,5},{4,2},{5,3},{6,0},{7,1},{8,14},{9,15},{10,... | collective-permute-start | bytes 196616 | tf_op jit(solution)/shard_map/ppermute | solution.py:28
  48.7 7.5 %collective-permute-start.51 = (bf16[4,32,256]{2,1,0:T(8,128)(2,1)S(1)}, bf16[4,32,256]{2,1,0:T(8,128)(2,1)S(1)}, u32[]{:S(2)}, u32[]{:S(2)}) collective-permute-start(bf16[4,32,256]{2,1,0:T(8,128)(2,1)S(1)} %get-tuple-element.133), channel_id=1, source_target_pairs={{0,7},{1,6},{2,5},{3,4},{4,3},{5,2},{6,1},{7,0},{8,15},{9,14},{10,... | collective-permute-start | bytes 196616 | tf_op jit(solution)/shard_map/ppermute | solution.py:28
  50.0 9.0 %collective-permute-start.52 = (bf16[4,32,256]{2,1,0:T(8,128)(2,1)S(1)}, bf16[4,32,256]{2,1,0:T(8,128)(2,1)S(1)}, u32[]{:S(2)}, u32[]{:S(2)}) collective-permute-start(bf16[4,32,256]{2,1,0:T(8,128)(2,1)S(1)} %get-tuple-element.134), channel_id=1, source_target_pairs={{0,8},{1,9},{2,10},{3,11},{4,12},{5,13},{6,14},{7,15},{8,0},{9,1},... | collective-permute-start | bytes 196616 | tf_op jit(solution)/shard_map/ppermute | solution.py:28
  51.4 12.0 %collective-permute-start.53 = (bf16[4,32,256]{2,1,0:T(8,128)(2,1)S(1)}, bf16[4,32,256]{2,1,0:T(8,128)(2,1)S(1)}, u32[]{:S(2)}, u32[]{:S(2)}) collective-permute-start(bf16[4,32,256]{2,1,0:T(8,128)(2,1)S(1)} %get-tuple-element.135), channel_id=1, source_target_pairs={{0,9},{1,8},{2,11},{3,10},{4,13},{5,12},{6,15},{7,14},{8,1},{9,0},... | collective-permute-start | bytes 196616 | tf_op jit(solution)/shard_map/ppermute | solution.py:28
  52.6 13.6 %collective-permute-start.54 = (bf16[4,32,256]{2,1,0:T(8,128)(2,1)S(1)}, bf16[4,32,256]{2,1,0:T(8,128)(2,1)S(1)}, u32[]{:S(2)}, u32[]{:S(2)}) collective-permute-start(bf16[4,32,256]{2,1,0:T(8,128)(2,1)S(1)} %get-tuple-element.136), channel_id=1, source_target_pairs={{0,10},{1,11},{2,8},{3,9},{4,14},{5,15},{6,12},{7,13},{8,2},{9,3},... | collective-permute-start | bytes 196616 | tf_op jit(solution)/shard_map/ppermute | solution.py:28
  55.3 13.7 %collective-permute-start.55 = (bf16[4,32,256]{2,1,0:T(8,128)(2,1)S(1)}, bf16[4,32,256]{2,1,0:T(8,128)(2,1)S(1)}, u32[]{:S(2)}, u32[]{:S(2)}) collective-permute-start(bf16[4,32,256]{2,1,0:T(8,128)(2,1)S(1)} %get-tuple-element.137), channel_id=1, source_target_pairs={{0,11},{1,10},{2,9},{3,8},{4,15},{5,14},{6,13},{7,12},{8,3},{9,2},... | collective-permute-start | bytes 196616 | tf_op jit(solution)/shard_map/ppermute | solution.py:28
  56.2 13.6 %collective-permute-start.56 = (bf16[4,32,256]{2,1,0:T(8,128)(2,1)S(1)}, bf16[4,32,256]{2,1,0:T(8,128)(2,1)S(1)}, u32[]{:S(2)}, u32[]{:S(2)}) collective-permute-start(bf16[4,32,256]{2,1,0:T(8,128)(2,1)S(1)} %get-tuple-element.138), channel_id=1, source_target_pairs={{0,12},{1,13},{2,14},{3,15},{4,8},{5,9},{6,10},{7,11},{8,4},{9,5},... | collective-permute-start | bytes 196616 | tf_op jit(solution)/shard_map/ppermute | solution.py:28
  59.0 12.5 %collective-permute-start.57 = (bf16[4,32,256]{2,1,0:T(8,128)(2,1)S(1)}, bf16[4,32,256]{2,1,0:T(8,128)(2,1)S(1)}, u32[]{:S(2)}, u32[]{:S(2)}) collective-permute-start(bf16[4,32,256]{2,1,0:T(8,128)(2,1)S(1)} %get-tuple-element.139), channel_id=1, source_target_pairs={{0,13},{1,12},{2,15},{3,14},{4,9},{5,8},{6,11},{7,10},{8,5},{9,4},... | collective-permute-start | bytes 196616 | tf_op jit(solution)/shard_map/ppermute | solution.py:28
  63.4 8.2 %collective-permute-start.58 = (bf16[4,32,256]{2,1,0:T(8,128)(2,1)S(1)}, bf16[4,32,256]{2,1,0:T(8,128)(2,1)S(1)}, u32[]{:S(2)}, u32[]{:S(2)}) collective-permute-start(bf16[4,32,256]{2,1,0:T(8,128)(2,1)S(1)} %get-tuple-element.140), channel_id=1, source_target_pairs={{0,14},{1,15},{2,12},{3,13},{4,10},{5,11},{6,8},{7,9},{8,6},{9,7},... | collective-permute-start | bytes 196616 | tf_op jit(solution)/shard_map/ppermute | solution.py:28
  66.2 6.9 %collective-permute-start.59 = (bf16[4,32,256]{2,1,0:T(8,128)(2,1)S(1)}, bf16[4,32,256]{2,1,0:T(8,128)(2,1)S(1)}, u32[]{:S(2)}, u32[]{:S(2)}) collective-permute-start(bf16[4,32,256]{2,1,0:T(8,128)(2,1)S(1)} %get-tuple-element.141), channel_id=1, source_target_pairs={{0,15},{1,14},{2,13},{3,12},{4,11},{5,10},{6,9},{7,8},{8,7},{9,6},... | collective-permute-start | bytes 196616 | tf_op jit(solution)/shard_map/ppermute | solution.py:28
  69.8 8.9 %collective-permute-start.16 = (bf16[4,32,256]{2,1,0:T(8,128)(2,1)S(1)}, bf16[4,32,256]{2,1,0:T(8,128)(2,1)S(1)}, u32[]{:S(2)}, u32[]{:S(2)}) collective-permute-start(bf16[4,32,256]{2,1,0:T(8,128)(2,1)S(1)} %get-tuple-element.94), channel_id=1, source_target_pairs={{0,2},{1,3},{2,0},{3,1},{4,6},{5,7},{6,4},{7,5},{8,10},{9,11},{10,... | collective-permute-start | bytes 196616 | tf_op jit(solution)/shard_map/ppermute | solution.py:28
  71.6 7.2 %collective-permute-start.17 = (bf16[4,32,256]{2,1,0:T(8,128)(2,1)S(1)}, bf16[4,32,256]{2,1,0:T(8,128)(2,1)S(1)}, u32[]{:S(2)}, u32[]{:S(2)}) collective-permute-start(bf16[4,32,256]{2,1,0:T(8,128)(2,1)S(1)} %get-tuple-element.95), channel_id=1, source_target_pairs={{0,3},{1,2},{2,1},{3,0},{4,7},{5,6},{6,5},{7,4},{8,11},{9,10},{10,... | collective-permute-start | bytes 196616 | tf_op jit(solution)/shard_map/ppermute | solution.py:28
  71.6 85.2 %collective-permute-start.60 = (bf16[4,512,256]{2,1,0:T(8,128)(2,1)S(1)}, bf16[4,512,256]{2,1,0:T(8,128)(2,1)S(1)}, u32[]{:S(2)}, u32[]{:S(2)}) collective-permute-start(bf16[4,512,256]{2,1,0:T(8,128)(2,1)S(1)} %bitcast.11), channel_id=1, source_target_pairs={{0,16},{16,0},{1,17},{17,1},{2,18},{18,2},{3,19},{19,3},{4,20},{20... | collective-permute-start | bytes 3145736 | tf_op jit(solution)/shard_map/ppermute | solution.py:20
  73.2 83.6 %collective-permute-start.61 = (bf16[4,512,256]{2,1,0:T(8,128)(2,1)S(1)}, bf16[4,512,256]{2,1,0:T(8,128)(2,1)S(1)}, u32[]{:S(2)}, u32[]{:S(2)}) collective-permute-start(bf16[4,512,256]{2,1,0:T(8,128)(2,1)S(1)} %bitcast.8), channel_id=1, source_target_pairs={{0,16},{16,0},{1,17},{17,1},{2,18},{18,2},{3,19},{19,3},{4,20},{20... | collective-permute-start | bytes 3145736 | tf_op jit(solution)/shard_map/ppermute | solution.py:20
  74.6 6.4 %collective-permute-start.18 = (bf16[4,32,256]{2,1,0:T(8,128)(2,1)S(1)}, bf16[4,32,256]{2,1,0:T(8,128)(2,1)S(1)}, u32[]{:S(2)}, u32[]{:S(2)}) collective-permute-start(bf16[4,32,256]{2,1,0:T(8,128)(2,1)S(1)} %get-tuple-element.96), channel_id=1, source_target_pairs={{0,4},{1,5},{2,6},{3,7},{4,0},{5,1},{6,2},{7,3},{8,12},{9,13},{10,... | collective-permute-start | bytes 196616 | tf_op jit(solution)/shard_map/ppermute | solution.py:28
  82.8 9.2 %collective-permute-start.22 = (bf16[4,32,256]{2,1,0:T(8,128)(2,1)S(1)}, bf16[4,32,256]{2,1,0:T(8,128)(2,1)S(1)}, u32[]{:S(2)}, u32[]{:S(2)}) collective-permute-start(bf16[4,32,256]{2,1,0:T(8,128)(2,1)S(1)} %get-tuple-element.100), channel_id=1, source_target_pairs={{0,8},{1,9},{2,10},{3,11},{4,12},{5,13},{6,14},{7,15},{8,0},{9,1},... | collective-permute-start | bytes 196616 | tf_op jit(solution)/shard_map/ppermute | solution.py:28
  84.7 9.5 %collective-permute-start.23 = (bf16[4,32,256]{2,1,0:T(8,128)(2,1)S(1)}, bf16[4,32,256]{2,1,0:T(8,128)(2,1)S(1)}, u32[]{:S(2)}, u32[]{:S(2)}) collective-permute-start(bf16[4,32,256]{2,1,0:T(8,128)(2,1)S(1)} %get-tuple-element.101), channel_id=1, source_target_pairs={{0,9},{1,8},{2,11},{3,10},{4,13},{5,12},{6,15},{7,14},{8,1},{9,0},... | collective-permute-start | bytes 196616 | tf_op jit(solution)/shard_map/ppermute | solution.py:28
  86.4 10.5 %collective-permute-start.24 = (bf16[4,32,256]{2,1,0:T(8,128)(2,1)S(1)}, bf16[4,32,256]{2,1,0:T(8,128)(2,1)S(1)}, u32[]{:S(2)}, u32[]{:S(2)}) collective-permute-start(bf16[4,32,256]{2,1,0:T(8,128)(2,1)S(1)} %get-tuple-element.102), channel_id=1, source_target_pairs={{0,10},{1,11},{2,8},{3,9},{4,14},{5,15},{6,12},{7,13},{8,2},{9,3},... | collective-permute-start | bytes 196616 | tf_op jit(solution)/shard_map/ppermute | solution.py:28
  92.1 6.8 %collective-permute-start.25 = (bf16[4,32,256]{2,1,0:T(8,128)(2,1)S(1)}, bf16[4,32,256]{2,1,0:T(8,128)(2,1)S(1)}, u32[]{:S(2)}, u32[]{:S(2)}) collective-permute-start(bf16[4,32,256]{2,1,0:T(8,128)(2,1)S(1)} %get-tuple-element.103), channel_id=1, source_target_pairs={{0,11},{1,10},{2,9},{3,8},{4,15},{5,14},{6,13},{7,12},{8,3},{9,2},... | collective-permute-start | bytes 196616 | tf_op jit(solution)/shard_map/ppermute | solution.py:28
  94.2 7.5 %collective-permute-start.26 = (bf16[4,32,256]{2,1,0:T(8,128)(2,1)S(1)}, bf16[4,32,256]{2,1,0:T(8,128)(2,1)S(1)}, u32[]{:S(2)}, u32[]{:S(2)}) collective-permute-start(bf16[4,32,256]{2,1,0:T(8,128)(2,1)S(1)} %get-tuple-element.104), channel_id=1, source_target_pairs={{0,12},{1,13},{2,14},{3,15},{4,8},{5,9},{6,10},{7,11},{8,4},{9,5},... | collective-permute-start | bytes 196616 | tf_op jit(solution)/shard_map/ppermute | solution.py:28
  96.9 7.5 %collective-permute-start.27 = (bf16[4,32,256]{2,1,0:T(8,128)(2,1)S(1)}, bf16[4,32,256]{2,1,0:T(8,128)(2,1)S(1)}, u32[]{:S(2)}, u32[]{:S(2)}) collective-permute-start(bf16[4,32,256]{2,1,0:T(8,128)(2,1)S(1)} %get-tuple-element.105), channel_id=1, source_target_pairs={{0,13},{1,12},{2,15},{3,14},{4,9},{5,8},{6,11},{7,10},{8,5},{9,4},... | collective-permute-start | bytes 196616 | tf_op jit(solution)/shard_map/ppermute | solution.py:28
  98.8 7.4 %collective-permute-start.28 = (bf16[4,32,256]{2,1,0:T(8,128)(2,1)S(1)}, bf16[4,32,256]{2,1,0:T(8,128)(2,1)S(1)}, u32[]{:S(2)}, u32[]{:S(2)}) collective-permute-start(bf16[4,32,256]{2,1,0:T(8,128)(2,1)S(1)} %get-tuple-element.106), channel_id=1, source_target_pairs={{0,14},{1,15},{2,12},{3,13},{4,10},{5,11},{6,8},{7,9},{8,6},{9,7},... | collective-permute-start | bytes 196616 | tf_op jit(solution)/shard_map/ppermute | solution.py:28
  101.7 6.9 %collective-permute-start.29 = (bf16[4,32,256]{2,1,0:T(8,128)(2,1)S(1)}, bf16[4,32,256]{2,1,0:T(8,128)(2,1)S(1)}, u32[]{:S(2)}, u32[]{:S(2)}) collective-permute-start(bf16[4,32,256]{2,1,0:T(8,128)(2,1)S(1)} %get-tuple-element.107), channel_id=1, source_target_pairs={{0,15},{1,14},{2,13},{3,12},{4,11},{5,10},{6,9},{7,8},{8,7},{9,6},... | collective-permute-start | bytes 196616 | tf_op jit(solution)/shard_map/ppermute | solution.py:28
  113.6 6.2 %collective-permute-start.33 = (bf16[4,32,256]{2,1,0:T(8,128)(2,1)S(1)}, bf16[4,32,256]{2,1,0:T(8,128)(2,1)S(1)}, u32[]{:S(2)}, u32[]{:S(2)}) collective-permute-start(bf16[4,32,256]{2,1,0:T(8,128)(2,1)S(1)} %get-tuple-element.112), channel_id=1, source_target_pairs={{0,4},{1,5},{2,6},{3,7},{4,0},{5,1},{6,2},{7,3},{8,12},{9,13},{10,... | collective-permute-start | bytes 196616 | tf_op jit(solution)/shard_map/ppermute | solution.py:28
  121.1 6.5 %collective-permute-start.37 = (bf16[4,32,256]{2,1,0:T(8,128)(2,1)S(1)}, bf16[4,32,256]{2,1,0:T(8,128)(2,1)S(1)}, u32[]{:S(2)}, u32[]{:S(2)}) collective-permute-start(bf16[4,32,256]{2,1,0:T(8,128)(2,1)S(1)} %get-tuple-element.116), channel_id=1, source_target_pairs={{0,8},{1,9},{2,10},{3,11},{4,12},{5,13},{6,14},{7,15},{8,0},{9,1},... | collective-permute-start | bytes 196616 | tf_op jit(solution)/shard_map/ppermute | solution.py:28
  123.5 8.2 %collective-permute-start.38 = (bf16[4,32,256]{2,1,0:T(8,128)(2,1)S(1)}, bf16[4,32,256]{2,1,0:T(8,128)(2,1)S(1)}, u32[]{:S(2)}, u32[]{:S(2)}) collective-permute-start(bf16[4,32,256]{2,1,0:T(8,128)(2,1)S(1)} %get-tuple-element.117), channel_id=1, source_target_pairs={{0,9},{1,8},{2,11},{3,10},{4,13},{5,12},{6,15},{7,14},{8,1},{9,0},... | collective-permute-start | bytes 196616 | tf_op jit(solution)/shard_map/ppermute | solution.py:28
  125.1 10.1 %collective-permute-start.39 = (bf16[4,32,256]{2,1,0:T(8,128)(2,1)S(1)}, bf16[4,32,256]{2,1,0:T(8,128)(2,1)S(1)}, u32[]{:S(2)}, u32[]{:S(2)}) collective-permute-start(bf16[4,32,256]{2,1,0:T(8,128)(2,1)S(1)} %get-tuple-element.118), channel_id=1, source_target_pairs={{0,10},{1,11},{2,8},{3,9},{4,14},{5,15},{6,12},{7,13},{8,2},{9,3},... | collective-permute-start | bytes 196616 | tf_op jit(solution)/shard_map/ppermute | solution.py:28
  127.6 9.8 %collective-permute-start.40 = (bf16[4,32,256]{2,1,0:T(8,128)(2,1)S(1)}, bf16[4,32,256]{2,1,0:T(8,128)(2,1)S(1)}, u32[]{:S(2)}, u32[]{:S(2)}) collective-permute-start(bf16[4,32,256]{2,1,0:T(8,128)(2,1)S(1)} %get-tuple-element.119), channel_id=1, source_target_pairs={{0,11},{1,10},{2,9},{3,8},{4,15},{5,14},{6,13},{7,12},{8,3},{9,2},... | collective-permute-start | bytes 196616 | tf_op jit(solution)/shard_map/ppermute | solution.py:28
  131.7 24.1 %collective-permute-start.62 = (bf16[32,64,64]{2,1,0:T(8,128)(2,1)S(1)}, bf16[32,64,64]{2,1,0:T(8,128)(2,1)S(1)}, u32[]{:S(2)}, u32[]{:S(2)}) collective-permute-start(bf16[32,64,64]{2,1,0:T(8,128)(2,1)S(1)} %get-tuple-element.144), channel_id=1, source_target_pairs={{0,16},{16,0},{1,17},{17,1},{2,18},{18,2},{3,19},{19,3},{4,20},{20... | collective-permute-start | bytes 786440 | tf_op jit(solution)/shard_map/ppermute | solution.py:20
  137.4 6.3 %collective-permute-start.42 = (bf16[4,32,256]{2,1,0:T(8,128)(2,1)S(1)}, bf16[4,32,256]{2,1,0:T(8,128)(2,1)S(1)}, u32[]{:S(2)}, u32[]{:S(2)}) collective-permute-start(bf16[4,32,256]{2,1,0:T(8,128)(2,1)S(1)} %get-tuple-element.121), channel_id=1, source_target_pairs={{0,13},{1,12},{2,15},{3,14},{4,9},{5,8},{6,11},{7,10},{8,5},{9,4},... | collective-permute-start | bytes 196616 | tf_op jit(solution)/shard_map/ppermute | solution.py:28
  141.3 7.0 %collective-permute-start.43 = (bf16[4,32,256]{2,1,0:T(8,128)(2,1)S(1)}, bf16[4,32,256]{2,1,0:T(8,128)(2,1)S(1)}, u32[]{:S(2)}, u32[]{:S(2)}) collective-permute-start(bf16[4,32,256]{2,1,0:T(8,128)(2,1)S(1)} %get-tuple-element.122), channel_id=1, source_target_pairs={{0,14},{1,15},{2,12},{3,13},{4,10},{5,11},{6,8},{7,9},{8,6},{9,7},... | collective-permute-start | bytes 196616 | tf_op jit(solution)/shard_map/ppermute | solution.py:28
  143.8 6.4 %collective-permute-start.44 = (bf16[4,32,256]{2,1,0:T(8,128)(2,1)S(1)}, bf16[4,32,256]{2,1,0:T(8,128)(2,1)S(1)}, u32[]{:S(2)}, u32[]{:S(2)}) collective-permute-start(bf16[4,32,256]{2,1,0:T(8,128)(2,1)S(1)} %get-tuple-element.123), channel_id=1, source_target_pairs={{0,15},{1,14},{2,13},{3,12},{4,11},{5,10},{6,9},{7,8},{8,7},{9,6},... | collective-permute-start | bytes 196616 | tf_op jit(solution)/shard_map/ppermute | solution.py:28
  (23 other events, 407.1 us)

commit v3 on v2

v3 whole, which is shorter than its diff:
```python
import jax
import jax.numpy as jnp
from jax import lax
from jax.experimental import pallas as pl
from jax.experimental.pallas import tpu as pltpu
from jax.sharding import PartitionSpec as P

BF16 = jnp.bfloat16
F32 = jnp.float32
VMEM_LIMIT = 48 * 1024 * 1024


def swap_sequences(array):
    return lax.ppermute(array, "dp", [(0, 1), (1, 0)])


def exchange(blocks):
    return lax.all_to_all(blocks, "seq", split_axis=0, concat_axis=0, tiled=True)


def call(kernel, inputs, out_shapes, scratch=(), flops=0):
    whole = pl.BlockSpec(memory_space=pltpu.VMEM)
    moved = sum(x.size * x.dtype.itemsize for x in (*inputs, *out_shapes))
    return pl.pallas_call(
        kernel,
        out_shape=out_shapes,
        in_specs=[whole] * len(inputs),
        out_specs=[whole] * len(out_shapes),
        scratch_shapes=scratch,
        compiler_params=pltpu.CompilerParams(vmem_limit_bytes=VMEM_LIMIT),
        cost_estimate=pl.CostEstimate(flops=flops, bytes_accessed=moved, transcendentals=0),
    )(*inputs)


def dot(a, b, contract):
    return lax.dot_general(a, b, (contract, ((), ())), preferred_element_type=F32)


def product_kernel(gate_ref, cotangent_ref, out_ref):
    for i in range(gate_ref.shape[0]):
        wide = gate_ref[i].astype(F32) * cotangent_ref[i].astype(F32)
        out_ref[:, i] = wide.astype(BF16)


def mix_kernel(left_ref, values_ref, out_ref):
    seq, rows, cols, channels = out_ref.shape
    for i in range(rows):
        mixed = dot(left_ref[i], values_ref[i], ((1,), (0,)))
        out_ref[:, i] = mixed.astype(BF16).reshape(seq, cols, channels)


def load_columns(in_ref, wide):
    for p in range(in_ref.shape[0]):
        rows, cols, channels = in_ref.shape[1:]
        size = rows * cols
        block = in_ref[p].reshape(size, channels).astype(F32)
        for h in range(channels // 128):
            wide[h, p * size : (p + 1) * size, :] = block[:, h * 128 : (h + 1) * 128]


def column(wide, k, count, cols):
    halves = [wide[h, pl.ds(k, count, stride=cols), :] for h in range(wide.shape[0])]
    return jnp.concatenate(halves, axis=1).astype(BF16)


def store_column(wide, k, count, cols, value):
    for h in range(wide.shape[0]):
        wide[h, pl.ds(k, count, stride=cols), :] = value[:, h * 128 : (h + 1) * 128]


def store_blocks(wide, out_ref):
    seq, rows, cols, channels = out_ref.shape
    size = rows * cols
    for p in range(seq):
        halves = [wide[h, p * size : (p + 1) * size, :] for h in range(wide.shape[0])]
        block = jnp.concatenate(halves, axis=1).astype(BF16)
        out_ref[p] = block.reshape(rows, cols, channels)


def column_backward_kernel(right_ref, in_ref, out_ref, by_column_ref, wide, wide_out):
    cols, count, _ = right_ref.shape
    load_columns(in_ref, wide)
    for k in range(cols):
        grad = column(wide, k, count, cols)
        by_column_ref[k] = grad
        store_column(wide_out, k, count, cols, dot(right_ref[k], grad, ((0,), (0,))))
    store_blocks(wide_out, out_ref)


def column_forward_kernel(right_ref, grad_ref, in_ref, out_ref, part_ref, wide, wide_out):
    cols, count, _ = right_ref.shape
    load_columns(in_ref, wide)
    for k in range(cols):
        mixed = column(wide, k, count, cols)
        store_column(wide_out, k, count, cols, dot(right_ref[k], mixed, ((1,), (0,))))
        part_ref[k] = dot(grad_ref[k], mixed, ((1,), (1,))).astype(BF16)
    store_blocks(wide_out, out_ref)


def gather_kernel(in_ref, out_ref):
    for i in range(out_ref.shape[0]):
        out_ref[i] = in_ref[:, i]


def row_backward_kernel(left_ref, values_ref, grad_ref, signal_ref, term_ref):
    for i in range(left_ref.shape[0]):
        grad = grad_ref[i]
        signal_ref[i] = dot(left_ref[i], grad, ((0,), (0,))).astype(BF16)
        term_ref[i] = dot(grad, values_ref[i], ((1,), (1,))).astype(BF16)


def left_sum_kernel(term_ref, values_ref, grad_ref, out_ref):
    for i in range(term_ref.shape[0]):
        other = dot(grad_ref[i], values_ref[i], ((1,), (1,))).astype(BF16)
        out_ref[i] = (term_ref[i].astype(F32) + other.astype(F32)).astype(BF16)


def output_kernel(gate_ref, cotangent_ref, in_ref, out_ref, grad_ref):
    for i in range(gate_ref.shape[0]):
        second = in_ref[:, i].astype(F32)
        out_ref[i] = (gate_ref[i].astype(F32) * second).astype(BF16)
        grad_ref[i] = (cotangent_ref[i].astype(F32) * second).astype(BF16)


def direct_shards(signal, gating, upstream, left_factor, right_factor):
    seq = lax.axis_size("seq")
    rows, block_len = left_factor.shape[:2]
    cols, count = right_factor.shape[:2]
    channels = signal.shape[2]
    values = signal.reshape(rows, block_len, channels)
    gate = gating.reshape(rows, seq, cols, channels)
    cotangent = upstream.reshape(rows, seq, cols, channels)

    blocks = jax.ShapeDtypeStruct((seq, rows, cols, channels), BF16)
    whole = jax.ShapeDtypeStruct((rows, seq, cols, channels), BF16)
    by_row = jax.ShapeDtypeStruct((rows, block_len, channels), BF16)
    left = jax.ShapeDtypeStruct(left_factor.shape, BF16)
    right = jax.ShapeDtypeStruct(right_factor.shape, BF16)
    by_column = jax.ShapeDtypeStruct((cols, count, channels), BF16)
    wide = pltpu.VMEM((channels // 128, count * cols, 128), F32)
    row_flops = 2 * rows * block_len * block_len * channels
    column_flops = 2 * cols * count * count * channels

    (grad_rows,) = call(product_kernel, [gate, cotangent], [blocks])
    grad_blocks = exchange(grad_rows)
    other_values = swap_sequences(values)
    (mixed_rows,) = call(mix_kernel, [left_factor, values], [blocks], flops=row_flops)
    mixed_blocks = exchange(mixed_rows)
    grad_second, grad_column = call(
        column_backward_kernel,
        [right_factor, grad_blocks],
        [blocks, by_column],
        [wide, wide],
        column_flops,
    )
    back_blocks = exchange(grad_second)
    second, right_part = call(
        column_forward_kernel,
        [right_factor, grad_column, mixed_blocks],
        [blocks, right],
        [wide, wide],
        2 * column_flops,
    )
    second_blocks = exchange(second)
    other_right = swap_sequences(right_part)
    (gathered,) = call(gather_kernel, [back_blocks], [whole])
    grad_back = gathered.reshape(rows, block_len, channels)
    other_grad_back = swap_sequences(grad_back)
    grad_signal, left_term = call(
        row_backward_kernel, [left_factor, values, grad_back], [by_row, left], flops=2 * row_flops
    )
    (grad_left,) = call(
        left_sum_kernel, [left_term, other_values, other_grad_back], [left], flops=row_flops
    )
    grad_right = (right_part.astype(F32) + other_right.astype(F32)).astype(BF16)
    output, grad_gate = call(output_kernel, [gate, cotangent, second_blocks], [whole, whole])
    return (
        output.reshape(signal.shape),
        grad_gate.reshape(signal.shape),
        grad_signal.reshape(signal.shape),
        grad_left,
        grad_right,
    )


def plain_shards(signal, gating, upstream, left_factor, right_factor):
    seq = lax.axis_size("seq")
    rows, block_len = left_factor.shape[:2]
    cols, block_count = right_factor.shape[:2]
    channels = signal.shape[2]
    values = signal.reshape(rows, block_len, channels)
    gate = gating.reshape(rows, block_len, channels)
    cotangent = upstream.reshape(rows, block_len, channels)

    def einsum(spec, a, b):
        return jnp.einsum(spec, a, b, preferred_element_type=F32).astype(BF16)

    def all_to_all(blocks):
        return lax.all_to_all(blocks, "seq", split_axis=0, concat_axis=0, tiled=True)

    def to_columns(by_row):
        blocks = by_row.reshape(rows, seq, cols, channels).transpose(1, 0, 2, 3)
        return all_to_all(blocks).reshape(block_count, cols, channels)

    def to_rows(by_column):
        blocks = all_to_all(by_column.reshape(seq, rows, cols, channels))
        return blocks.transpose(1, 0, 2, 3).reshape(rows, block_len, channels)

    grad_rows = (cotangent.astype(F32) * gate.astype(F32)).astype(BF16)
    grad_column = to_columns(grad_rows)
    other_values = swap_sequences(values)
    mixed_column = to_columns(einsum("ikj,ijd->ikd", left_factor, values))
    grad_back = to_rows(einsum("kmi,mkd->ikd", right_factor, grad_column))
    second_rows = to_rows(einsum("kmi,ikd->mkd", right_factor, mixed_column))
    right_part = einsum("mkd,ikd->kmi", grad_column, mixed_column)
    other_right = swap_sequences(right_part)
    other_grad_back = swap_sequences(grad_back)
    grad_signal = einsum("ikj,ikd->ijd", left_factor, grad_back)
    left_term = einsum("ikd,ijd->ikj", grad_back, values)
    other_left = einsum("ikd,ijd->ikj", other_grad_back, other_values)
    grad_left = (left_term.astype(F32) + other_left.astype(F32)).astype(BF16)
    grad_right = (right_part.astype(F32) + other_right.astype(F32)).astype(BF16)
    wide = second_rows.astype(F32)
    output = (gate.astype(F32) * wide).astype(BF16)
    grad_gate = (cotangent.astype(F32) * wide).astype(BF16)
    return (
        output.reshape(signal.shape),
        grad_gate.reshape(signal.shape),
        grad_signal.reshape(signal.shape),
        grad_left,
        grad_right,
    )


def shards(signal, gating, upstream, left_factor, right_factor):
    seq = lax.axis_size("seq")
    cols = right_factor.shape[0]
    direct = seq <= 16 and seq & (seq - 1) == 0 and cols % 32 == 0
    run = direct_shards if direct else plain_shards
    return run(signal, gating, upstream, left_factor, right_factor)


def solution(mesh):
    by_position = P("dp", "seq", None)
    by_block = P("seq", None, None)
    return jax.shard_map(
        shards,
        mesh=mesh,
        in_specs=(by_position,) * 3 + (by_block,) * 2,
        out_specs=(by_position,) * 3 + (by_block,) * 2,
        check_vma=False,
    )
```

time: 159 us -> 174 us (1.094)
  waiting for transfers between devices: 34.4 us -> 108 us
  starting transfers between devices: 104 us -> 31.6 us
  local copies, waits for them, and re-layouts: 3.66 us -> 11.8 us
  Pallas kernels: 14.9 us -> 18.9 us
    ppermute x60 -> x0, starting transfers between devices: 99.8 us -> none  [exchange(): lax.ppermute(blocks[s], 'seq', [(i, i ^ s) for i in range(seq)])]
    all_to_all x0 -> x4, waiting for transfers between devices: none -> 54.4 us  [exchange(): lax.all_to_all(blocks, 'seq', split_axis=0, concat_axis=0, tiled=True)]
    ppermute x3, waiting for transfers between devices: 0.01 us -> 53.6 us  [swap_sequences(): return lax.ppermute(array, 'dp', [(0, 1), (1, 0)])]
    ppermute x60 -> x0, waiting for transfers between devices: 34.4 us -> none  [exchange(): lax.ppermute(blocks[s], 'seq', [(i, i ^ s) for i in range(seq)])]
    all_to_all x0 -> x4, starting transfers between devices: none -> 28 us  [exchange(): lax.all_to_all(blocks, 'seq', split_axis=0, concat_axis=0, tiled=True)]
    unnamed x16 -> x34, local copies, waits for them, and re-layouts: 3.66 us -> 11.8 us
    pallas_call x8, Pallas kernels: 14.9 us -> 18.9 us  [call(): pl.pallas_call(kernel, out_shape=out_shapes, in_specs=[whole] * len(input...]
  transfers between devices with their start and end apart: 63 -> 7, of which waited for: 22 -> 4; matrix products, arithmetic and copies ran while one was open for 1% -> 1% of each run, Pallas kernels for 6% -> 8%
where the time goes in v3:
time: 174 us; the launch traced here: 173 us
  waiting for transfers between devices  108 us (62%)
  starting transfers between devices  31.6 us (18%)
  Pallas kernels  18.9 us (11%)
  local copies, waits for them, and re-layouts  11.8 us (7%)
  other arithmetic  2.02 us (1%)
    all_to_all x4, waiting for transfers between devices, exchange(): lax.all_to_all(blocks, 'seq', split_axis=0, concat_axis=0, tiled=True)  54.4 us
    ppermute x3, waiting for transfers between devices, swap_sequences(): return lax.ppermute(array, 'dp', [(0, 1), (1, 0)])  53.6 us
    all_to_all x4, starting transfers between devices, exchange(): lax.all_to_all(blocks, 'seq', split_axis=0, concat_axis=0, tiled=True)  28 us
    pallas_call x8, Pallas kernels, call(): pl.pallas_call(kernel, out_shape=out_shapes, in_specs=[whole] * len(input...  18.9 us
    unnamed x34, local copies, waits for them, and re-layouts  11.8 us
    ppermute x3, starting transfers between devices, swap_sequences(): return lax.ppermute(array, 'dp', [(0, 1), (1, 0)])  3.58 us
  transfers between devices with their start and end apart: 7, of which 4 were waited for; matrix products, arithmetic and copies ran while one was open for 1% of the time, Pallas kernels for 8%

profile of v3, /device:TPU:0, one launch (start us, length us, event | category | flops | bytes accessed | tf_op | source)
XLA Modules:
  0.0 173.1 jit_solution(9620826010480029181)
XLA Ops:
  0.6 0.0 copy-start.1
  0.6 1.2 copy-done.1
  1.9 1.2 copy-done.3
  3.1 1.2 shard_map.92
  4.3 7.4 %all-to-all-start = ((bf16[16,4,32,256]{3,2,1,0:T(8,128)(2,1)}), bf16[16,4,32,256]{3,2,1,0:T(8,128)(2,1)S(1)}, u32[]{:S(2)}, u32[]{:S(2)}) async-start(bf16[16,4,32,256]{3,2,1,0:T(8,128)(2,1)} %shard_map.92), calls=%async_computation | async-start | bytes 2097152 | tf_op jit(solution)/shard_map/all_to_all | solution.py:18
  11.7 0.0 copy-done
  11.7 0.0 copy-start.8
  11.7 1.2 copy-done.8
  12.9 0.7 shard_map.94
  13.6 0.0 copy-start.7
  13.7 1.0 copy-done.7
  14.6 20.0 %all-to-all-done.in_ref = bf16[16,4,32,256]{3,2,1,0:T(8,128)(2,1)S(1)} async-done(((bf16[16,4,32,256]{3,2,1,0:T(8,128)(2,1)}), bf16[16,4,32,256]{3,2,1,0:T(8,128)(2,1)S(1)}, u32[]{:S(2)}, u32[]{:S(2)}) %all-to-all-start) | async-done | bytes 1048608 | tf_op jit(solution)/shard_map/all_to_all | solution.py:18
  34.6 6.9 %all-to-all-start.1 = ((bf16[16,4,32,256]{3,2,1,0:T(8,128)(2,1)}), bf16[16,4,32,256]{3,2,1,0:T(8,128)(2,1)S(1)}, u32[]{:S(2)}, u32[]{:S(2)}) async-start(bf16[16,4,32,256]{3,2,1,0:T(8,128)(2,1)} %copy-done.7), calls=%async_computation.1 | async-start | bytes 2097152 | tf_op jit(solution)/shard_map/all_to_all | solution.py:18
  41.5 0.0 copy-done.10
  41.5 3.1 %shard_map.93 = (bf16[16,4,32,256]{3,2,1,0:T(8,128)(2,1)S(1)}, bf16[32,64,256]{2,1,0:T(8,128)(2,1)S(1)}) custom-call(bf16[32,64,64]{2,1,0:T(8,128)(2,1)S(1)} %copy-done.10, bf16[16,4,32,256]{3,2,1,0:T(8,128)(2,1)S(1)} %all-to-all-done.in_ref), custom_call_target="tpu_custom_call" | custom-call | flops 67108864 | bytes 3407872 | tf_op jit(solution)/shard_map/pallas_call | solution.py:24
  44.6 0.0 copy-start.13
  44.6 1.0 copy-done.13
  45.6 1.0 copy-done.15
  46.6 17.9 %all-to-all-done.1.in_ref = bf16[16,4,32,256]{3,2,1,0:T(8,128)(2,1)S(1)} async-done(((bf16[16,4,32,256]{3,2,1,0:T(8,128)(2,1)}), bf16[16,4,32,256]{3,2,1,0:T(8,128)(2,1)S(1)}, u32[]{:S(2)}, u32[]{:S(2)}) %all-to-all-start.1) | async-done | bytes 1048608 | tf_op jit(solution)/shard_map/all_to_all | solution.py:18
  64.4 6.9 %all-to-all-start.3 = ((bf16[16,4,32,256]{3,2,1,0:T(8,128)(2,1)}), bf16[16,4,32,256]{3,2,1,0:T(8,128)(2,1)S(1)}, u32[]{:S(2)}, u32[]{:S(2)}) async-start(bf16[16,4,32,256]{3,2,1,0:T(8,128)(2,1)} %copy-done.15), calls=%async_computation.3 | async-start | bytes 2097152 | tf_op jit(solution)/shard_map/all_to_all | solution.py:18
  71.3 0.0 copy-done.11
  71.3 0.0 copy-start.14
  71.3 1.2 copy-done.14
  72.6 3.4 %shard_map.95 = (bf16[16,4,32,256]{3,2,1,0:T(8,128)(2,1)S(1)}, bf16[32,64,64]{2,1,0:T(8,128)(2,1)S(1)}) custom-call(bf16[32,64,64]{2,1,0:T(8,128)(2,1)S(1)} %copy-done.11, bf16[32,64,256]{2,1,0:T(8,128)(2,1)S(1)} %copy-done.14, bf16[16,4,32,256]{3,2,1,0:T(8,128)(2,1)S(1)} %all-to-all-done.1.in_ref), custom_call_target="tpu_custom_call" | custom-call | flops 134217728 | bytes 3670016 | tf_op jit(solution)/shard_map/pallas_call | solution.py:24
  76.0 0.0 copy-start.12
  76.0 1.0 copy-done.12
  76.9 0.8 copy-done.16
  77.7 16.5 %all-to-all-done.3.in_ref = bf16[16,4,32,256]{3,2,1,0:T(8,128)(2,1)S(1)} async-done(((bf16[16,4,32,256]{3,2,1,0:T(8,128)(2,1)}), bf16[16,4,32,256]{3,2,1,0:T(8,128)(2,1)S(1)}, u32[]{:S(2)}, u32[]{:S(2)}) %all-to-all-start.3) | async-done | bytes 1048608 | tf_op jit(solution)/shard_map/all_to_all | solution.py:18
  94.3 1.0 copy-done.5
  95.2 6.9 %all-to-all-start.2 = ((bf16[16,4,32,256]{3,2,1,0:T(8,128)(2,1)}), bf16[16,4,32,256]{3,2,1,0:T(8,128)(2,1)S(1)}, u32[]{:S(2)}, u32[]{:S(2)}) async-start(bf16[16,4,32,256]{3,2,1,0:T(8,128)(2,1)} %copy-done.12), calls=%async_computation.2 | async-start | bytes 2097152 | tf_op jit(solution)/shard_map/all_to_all | solution.py:18
  102.1 0.0 copy-start.2
  102.1 0.0 copy-start.4
  102.1 1.6 collective-permute-start
  103.7 1.2 copy-done.6
  104.9 1.0 shard_map.97
  105.9 0.6 collective-permute-start.1
  106.5 1.5 collective-permute-start.2
  108.0 53.6 %collective-permute-done.2 = bf16[32,64,64]{2,1,0:T(8,128)(2,1)S(1)} collective-permute-done((bf16[32,64,64]{2,1,0:T(8,128)(2,1)}, bf16[32,64,64]{2,1,0:T(8,128)(2,1)S(1)}, u32[]{:S(2)}, u32[]{:S(2)}) %collective-permute-start.2) | collective-permute-done | bytes 262176 | tf_op jit(solution)/shard_map/ppermute | solution.py:14
  161.6 2.0 %add_convert_fusion = bf16[32,64,64]{2,1,0:T(8,128)(2,1)} fusion(bf16[32,64,64]{2,1,0:T(8,128)(2,1)S(1)} %collective-permute-done.2, bf16[32,64,64]{2,1,0:T(8,128)(2,1)} %copy-done.16), kind=kLoop, calls=%fused_computation | loop fusion | flops 524288 | bytes 786432 | tf_op jit(solution)/shard_map/convert_element_type | solution.py:175
  163.6 0.0 all-to-all-done.2.in_ref
  163.6 0.0 copy-done.2
  163.6 0.0 copy-done.4
  163.6 0.0 copy-start.9
  163.7 1.7 %shard_map.96 = (bf16[4,16,32,256]{3,2,1,0:T(8,128)(2,1)}, bf16[4,16,32,256]{3,2,1,0:T(8,128)(2,1)}) custom-call(bf16[4,16,32,256]{3,2,1,0:T(8,128)(2,1)S(1)} %bitcast.8, bf16[4,16,32,256]{3,2,1,0:T(8,128)(2,1)S(1)} %bitcast.10, bf16[16,4,32,256]{3,2,1,0:T(8,128)(2,1)S(1)} %all-to-all-done.2.in_ref), custom_call_target="tpu_custom_call" | custom-call | bytes 5242880 | tf_op jit(solution)/shard_map/pallas_call | solution.py:24
  165.4 4.1 %shard_map.98 = (bf16[4,512,256]{2,1,0:T(8,128)(2,1)}, bf16[4,512,512]{2,1,0:T(8,128)(2,1)S(1)}) custom-call(bf16[4,512,512]{2,1,0:T(8,128)(2,1)} %left_ref.3, bf16[4,512,256]{2,1,0:T(8,128)(2,1)S(1)} %bitcast.13, bf16[4,512,256]{2,1,0:T(8,128)(2,1)} %bitcast.5.grad_ref), custom_call_target="tpu_custom_call" | custom-call | flops 1073741824 | bytes 7340032 | tf_op jit(solution)/shard_map/pallas_call | solution.py:24
  169.5 0.0 collective-permute-done.values_ref
  169.5 0.0 collective-permute-done.1.grad_ref
  169.5 3.6 %shard_map.99 = bf16[4,512,512]{2,1,0:T(8,128)(2,1)} custom-call(bf16[4,512,512]{2,1,0:T(8,128)(2,1)S(1)} %get-tuple-element.19.term_ref, bf16[4,512,256]{2,1,0:T(8,128)(2,1)} %collective-permute-done.values_ref, bf16[4,512,256]{2,1,0:T(8,128)(2,1)} %collective-permute-done.1.grad_ref), custom_call_target="tpu_custom_call" | custom-call | flops 536870912 | bytes 6291456 | tf_op jit(solution)/shard_map/pallas_call | solution.py:24
  (9 shorter events, 0.0 us)
Async XLA Ops:
  0.6 1.2 copy-start.1
  1.9 1.2 copy-start.3
  3.1 8.6 %copy-start = (bf16[4,512,512]{2,1,0:T(8,128)(2,1)S(1)}, bf16[4,512,512]{2,1,0:T(8,128)(2,1)}, u32[]{:S(2)}) copy-start(bf16[4,512,512]{2,1,0:T(8,128)(2,1)} %left_ref.3) | copy-start | bytes 6291460
  4.3 30.3 %all-to-all-start = ((bf16[16,4,32,256]{3,2,1,0:T(8,128)(2,1)}), bf16[16,4,32,256]{3,2,1,0:T(8,128)(2,1)S(1)}, u32[]{:S(2)}, u32[]{:S(2)}) async-start(bf16[16,4,32,256]{3,2,1,0:T(8,128)(2,1)} %shard_map.92), calls=%async_computation | async-start | bytes 2097152 | tf_op jit(solution)/shard_map/all_to_all | solution.py:18
  11.7 1.2 copy-start.8
  13.6 1.0 copy-start.7
  14.6 26.9 %copy-start.10 = (bf16[32,64,64]{2,1,0:T(8,128)(2,1)S(1)}, bf16[32,64,64]{2,1,0:T(8,128)(2,1)}, u32[]{:S(2)}) copy-start(bf16[32,64,64]{2,1,0:T(8,128)(2,1)} %right_ref.3) | copy-start | bytes 786436
  34.6 29.8 %all-to-all-start.1 = ((bf16[16,4,32,256]{3,2,1,0:T(8,128)(2,1)}), bf16[16,4,32,256]{3,2,1,0:T(8,128)(2,1)S(1)}, u32[]{:S(2)}, u32[]{:S(2)}) async-start(bf16[16,4,32,256]{3,2,1,0:T(8,128)(2,1)} %copy-done.7), calls=%async_computation.1 | async-start | bytes 2097152 | tf_op jit(solution)/shard_map/all_to_all | solution.py:18
  44.6 1.0 copy-start.13
  45.6 1.0 copy-start.15
  46.6 24.7 %copy-start.11 = (bf16[32,64,64]{2,1,0:T(8,128)(2,1)S(1)}, bf16[32,64,64]{2,1,0:T(8,128)(2,1)}, u32[]{:S(2)}) copy-start(bf16[32,64,64]{2,1,0:T(8,128)(2,1)} %right_ref.3) | copy-start | bytes 786436
  64.4 29.8 %all-to-all-start.3 = ((bf16[16,4,32,256]{3,2,1,0:T(8,128)(2,1)}), bf16[16,4,32,256]{3,2,1,0:T(8,128)(2,1)S(1)}, u32[]{:S(2)}, u32[]{:S(2)}) async-start(bf16[16,4,32,256]{3,2,1,0:T(8,128)(2,1)} %copy-done.15), calls=%async_computation.3 | async-start | bytes 2097152 | tf_op jit(solution)/shard_map/all_to_all | solution.py:18
  71.3 1.2 copy-start.14
  76.0 1.0 copy-start.12
  76.9 0.8 copy-start.16
  94.3 1.0 copy-start.5
  95.2 68.4 %all-to-all-start.2 = ((bf16[16,4,32,256]{3,2,1,0:T(8,128)(2,1)}), bf16[16,4,32,256]{3,2,1,0:T(8,128)(2,1)S(1)}, u32[]{:S(2)}, u32[]{:S(2)}) async-start(bf16[16,4,32,256]{3,2,1,0:T(8,128)(2,1)} %copy-done.12), calls=%async_computation.2 | async-start | bytes 2097152 | tf_op jit(solution)/shard_map/all_to_all | solution.py:18
  102.1 61.5 %copy-start.2 = (bf16[1,2048,256]{2,1,0:T(8,128)(2,1)S(1)}, bf16[1,2048,256]{2,1,0:T(8,128)(2,1)}, u32[]{:S(2)}) copy-start(bf16[1,2048,256]{2,1,0:T(8,128)(2,1)} %param.6) | copy-start | bytes 3145732
  102.1 61.5 %copy-start.4 = (bf16[1,2048,256]{2,1,0:T(8,128)(2,1)S(1)}, bf16[1,2048,256]{2,1,0:T(8,128)(2,1)}, u32[]{:S(2)}) copy-start(bf16[1,2048,256]{2,1,0:T(8,128)(2,1)} %param.7) | copy-start | bytes 3145732
  102.1 67.4 %collective-permute-start = (bf16[4,512,256]{2,1,0:T(8,128)(2,1)}, bf16[4,512,256]{2,1,0:T(8,128)(2,1)}, u32[]{:S(2)}, u32[]{:S(2)}) collective-permute-start(bf16[4,512,256]{2,1,0:T(8,128)(2,1)} %bitcast.11), channel_id=1, source_target_pairs={{0,16},{16,0},{1,17},{17,1},{2,18},{18,2},{3,19},{19,3},{4,20},{20... | collective-permute-start | bytes 3145736 | tf_op jit(solution)/shard_map/ppermute | solution.py:14
  103.7 1.2 copy-start.6
  105.9 63.5 %collective-permute-start.1 = (bf16[4,512,256]{2,1,0:T(8,128)(2,1)}, bf16[4,512,256]{2,1,0:T(8,128)(2,1)}, u32[]{:S(2)}, u32[]{:S(2)}) collective-permute-start(bf16[4,512,256]{2,1,0:T(8,128)(2,1)} %bitcast.5.grad_ref), channel_id=1, source_target_pairs={{0,16},{16,0},{1,17},{17,1},{2,18},{18,2},{3,19},{19,3},{4,20},{20... | collective-permute-start | bytes 3145736 | tf_op jit(solution)/shard_map/ppermute | solution.py:14
  106.5 55.1 %collective-permute-start.2 = (bf16[32,64,64]{2,1,0:T(8,128)(2,1)}, bf16[32,64,64]{2,1,0:T(8,128)(2,1)S(1)}, u32[]{:S(2)}, u32[]{:S(2)}) collective-permute-start(bf16[32,64,64]{2,1,0:T(8,128)(2,1)} %copy-done.16), channel_id=1, source_target_pairs={{0,16},{16,0},{1,17},{17,1},{2,18},{18,2},{3,19},{19,3},{4,20},{20... | collective-permute-start | bytes 786440 | tf_op jit(solution)/shard_map/ppermute | solution.py:14
  163.6 1.7 %copy-start.9 = (bf16[1,2048,256]{2,1,0:T(8,128)(2,1)S(1)}, bf16[1,2048,256]{2,1,0:T(8,128)(2,1)}, u32[]{:S(2)}) copy-start(bf16[1,2048,256]{2,1,0:T(8,128)(2,1)} %param.5) | copy-start | bytes 3145732

commit v4 on v2

--- a/solution.py
+++ b/solution.py
@@ -13,7 +13,20 @@
 
 
 def partner_order(seq):
-    return sorted(range(seq), key=lambda s: (-(s // (seq // 2)), s % (seq // 2), s))
+    half = seq // 2
+    near = sorted(range(1, half), key=lambda s: (s % max(half // 2, 1), s))
+    order = []
+    for n in range(half):
+        order += [half + n] + near[n : n + 1]
+    return order
+
+
+def sorted_partners(seq):
+    listed = [0] * seq
+    names = sorted(range(seq - 1), key=lambda n: str(n) if n else "")
+    for name, s in zip(names, partner_order(seq)):
+        listed[name + 1] = s
+    return listed
 
 
 def swap_sequences(array):
@@ -24,18 +37,23 @@
     seq = len(blocks)
     received = list(blocks)
     for s in partner_order(seq):
-        if s:
-            received[s] = lax.ppermute(blocks[s], "seq", [(i, i ^ s) for i in range(seq)])
+        received[s] = lax.ppermute(blocks[s], "seq", [(i, i ^ s) for i in range(seq)])
     return received
 
 
-def call(kernel, me, inputs, out_shapes, scratch=(), flops=0):
+def after(array, earlier):
+    return lax.optimization_barrier((array, earlier))[0]
+
+
+def call(kernel, me, inputs, out_shapes, scratch=(), flops=0, unread=None):
     whole = pl.BlockSpec(memory_space=pltpu.VMEM)
     moved = sum(x.size * x.dtype.itemsize for x in (*inputs, *out_shapes))
     return pl.pallas_call(
         kernel,
         out_shape=out_shapes,
-        in_specs=[pl.BlockSpec(memory_space=pltpu.SMEM)] + [whole] * len(inputs),
+        in_specs=[pl.BlockSpec(memory_space=pltpu.SMEM)] + [
+            pl.BlockSpec(memory_space=pl.ANY) if n == unread else whole for n in range(len(inputs))
+        ],
         out_specs=[whole] * len(out_shapes),
         scratch_shapes=scratch,
         compiler_params=pltpu.CompilerParams(vmem_limit_bytes=VMEM_LIMIT),
@@ -47,15 +65,7 @@
     return lax.dot_general(a, b, (contract, ((), ())), preferred_element_type=F32)
 
 
-def product_kernel(seq, me_ref, gate_ref, cotangent_ref, *out_refs):
-    me = me_ref[0]
-    for s in range(seq):
-        c = me ^ s
-        wide = gate_ref[:, c].astype(F32) * cotangent_ref[:, c].astype(F32)
-        out_refs[s][...] = wide.astype(BF16)
-
-
-def mix_kernel(seq, me_ref, left_ref, values_ref, *refs):
+def send_kernel(seq, me_ref, gate_ref, cotangent_ref, left_ref, values_ref, *refs):
     out_refs, hold = refs[:seq], refs[seq]
     rows, _, cols, channels = hold.shape
     me = me_ref[0]
@@ -63,14 +73,17 @@
         mixed = dot(left_ref[i], values_ref[i], ((1,), (0,)))
         hold[i] = mixed.astype(BF16).reshape(seq, cols, channels)
     for s in range(seq):
-        out_refs[s][...] = hold[:, me ^ s]
-
-
-def load_columns(seq, me, in_refs, wide):
-    rows, cols, channels = in_refs[0].shape
+        c = me ^ s
+        wide = gate_ref[:, c].astype(F32) * cotangent_ref[:, c].astype(F32)
+        out_refs[s][0] = wide.astype(BF16)
+        out_refs[s][1] = hold[:, c]
+
+
+def load_columns(seq, me, in_refs, which, wide):
+    rows, cols, channels = in_refs[0].shape[1:]
     size = rows * cols
-    for s in range(seq):
-        block = in_refs[s][...].reshape(size, channels).astype(F32)
+    for s, in_ref in zip(sorted_partners(seq), in_refs):
+        block = in_ref[which].reshape(size, channels).astype(F32)
         start = pl.multiple_of((me ^ s) * size, size)
         for h in range(channels // 128):
             wide[h, pl.ds(start, size), :] = block[:, h * 128 : (h + 1) * 128]
@@ -101,7 +114,7 @@
     by_column_ref, wide, wide_out = refs[2 * seq :]
     cols, count, _ = right_ref.shape
     me = me_ref[0]
-    load_columns(seq, me, in_refs, wide)
+    load_columns(seq, me, in_refs, 0, wide)
     for k in range(cols):
         grad = column(wide, k, count, cols)
         by_column_ref[k] = grad
@@ -109,12 +122,12 @@
     send_columns(seq, me, wide_out, out_refs)
 
 
-def column_forward_kernel(seq, me_ref, right_ref, grad_ref, *refs):
+def column_forward_kernel(seq, me_ref, right_ref, grad_ref, after_ref, *refs):
     in_refs, out_refs = refs[:seq], refs[seq : 2 * seq]
     right_part_ref, wide, wide_out = refs[2 * seq :]
     cols, count, _ = right_ref.shape
     me = me_ref[0]
-    load_columns(seq, me, in_refs, wide)
+    load_columns(seq, me, in_refs, 1, wide)
     for k in range(cols):
         mixed = column(wide, k, count, cols)
         store_column(wide_out, k, count, cols, dot(right_ref[k], mixed, ((1,), (0,))))
@@ -125,8 +138,8 @@
 def gather_kernel(seq, me_ref, *refs):
     in_refs, out_ref = refs[:seq], refs[seq]
     me = me_ref[0]
-    for s in range(seq):
-        out_ref[:, me ^ s] = in_refs[s][...]
+    for s, in_ref in zip([0] + partner_order(seq), in_refs):
+        out_ref[:, me ^ s] = in_ref[...]
 
 
 def row_backward_kernel(me_ref, left_ref, values_ref, grad_ref, signal_ref, term_ref):
@@ -136,18 +149,21 @@
         term_ref[i] = dot(grad, values_ref[i], ((1,), (1,))).astype(BF16)
 
 
-def left_sum_kernel(me_ref, term_ref, values_ref, grad_ref, out_ref):
+def factor_sum_kernel(
+    me_ref, term_ref, values_ref, grad_ref, right_ref, other_ref, left_out_ref, right_out_ref
+):
     for i in range(term_ref.shape[0]):
         other = dot(grad_ref[i], values_ref[i], ((1,), (1,))).astype(BF16)
-        out_ref[i] = (term_ref[i].astype(F32) + other.astype(F32)).astype(BF16)
+        left_out_ref[i] = (term_ref[i].astype(F32) + other.astype(F32)).astype(BF16)
+    right_out_ref[...] = (right_ref[...].astype(F32) + other_ref[...].astype(F32)).astype(BF16)
 
 
 def output_kernel(seq, me_ref, gate_ref, cotangent_ref, *refs):
     in_refs, (out_ref, grad_ref) = refs[:seq], refs[seq:]
     me = me_ref[0]
-    for s in range(seq):
+    for s, in_ref in zip([0] + partner_order(seq), in_refs):
         c = me ^ s
-        second = in_refs[s][...].astype(F32)
+        second = in_ref[...].astype(F32)
         out_ref[:, c] = (gate_ref[:, c].astype(F32) * second).astype(BF16)
         grad_ref[:, c] = (cotangent_ref[:, c].astype(F32) * second).astype(BF16)
 
@@ -173,38 +189,42 @@
     row_flops = 2 * rows * block_len * block_len * channels
     column_flops = 2 * cols * count * count * channels
 
-    grad_rows = call(
-        functools.partial(product_kernel, seq), me, [gate, cotangent], blocks
-    )
-    grad_blocks = exchange(grad_rows)
-    other_values = swap_sequences(values)
-    mixed_rows = call(
-        functools.partial(mix_kernel, seq),
-        me,
-        [left_factor, values],
-        blocks,
+    pair = jax.ShapeDtypeStruct((2, rows, cols, channels), BF16)
+    sent = call(
+        functools.partial(send_kernel, seq),
+        me,
+        [gate, cotangent, left_factor, values],
+        [pair] * seq,
         [pltpu.VMEM(whole.shape, BF16)],
         row_flops,
     )
-    mixed_blocks = exchange(mixed_rows)
+    received = exchange(sent)
+    columns = [received[s] for s in sorted_partners(seq)]
+    other_values = swap_sequences(values)
     *grad_second, grad_column = call(
         functools.partial(column_backward_kernel, seq),
         me,
-        [right_factor, *grad_blocks],
+        [right_factor, *columns],
         blocks + [by_column],
         [wide, wide],
         column_flops,
     )
-    back_blocks = exchange(grad_second)
     *second, right_part = call(
         functools.partial(column_forward_kernel, seq),
         me,
-        [right_factor, grad_column, *mixed_blocks],
+        [right_factor, grad_column, other_values, *columns],
         blocks + [right],
         [wide, wide],
         2 * column_flops,
-    )
+        unread=2,
+    )
+    order = partner_order(seq)
+    for s in order[seq // 2 :]:
+        grad_second[s] = after(grad_second[s], right_part)
+    back_blocks = exchange(grad_second)
+    back_blocks = [back_blocks[s] for s in [0] + order]
     second_blocks = exchange(second)
+    second_blocks = [second_blocks[s] for s in [0] + order]
     other_right = swap_sequences(right_part)
     (gathered,) = call(functools.partial(gather_kernel, seq), me, back_blocks, [whole])
     grad_back = gathered.reshape(rows, block_len, channels)
@@ -216,14 +236,13 @@
         [by_row, left],
         flops=2 * row_flops,
     )
-    (grad_left,) = call(
-        left_sum_kernel,
-        me,
-        [left_term, other_values, other_grad_back],
-        [left],
+    grad_left, grad_right = call(
+        factor_sum_kernel,
+        me,
+        [left_term, other_values, other_grad_back, right_part, other_right],
+        [left, right],
         flops=row_flops,
     )
-    grad_right = (right_part.astype(F32) + other_right.astype(F32)).astype(BF16)
     output, grad_gate = call(
         functools.partial(output_kernel, seq),
         me,

time: 159 us -> 133 us (0.84)
  starting transfers between devices: 104 us -> 82.5 us
  waiting for transfers between devices: 34.4 us -> 29.5 us
  Pallas kernels: 14.9 us -> 16.7 us
    ppermute x60 -> x45, starting transfers between devices: 99.8 us -> 77.4 us  [exchange(): lax.ppermute(blocks[s], 'seq', [(i, i ^ s) for i in range(seq)])]
    ppermute x60 -> x45, waiting for transfers between devices: 34.4 us -> 29.5 us  [exchange(): lax.ppermute(blocks[s], 'seq', [(i, i ^ s) for i in range(seq)])]
    pallas_call x8 -> x7, Pallas kernels: 14.9 us -> 16.7 us  [call(): pl.pallas_call(kernel, out_shape=out_shapes, in_specs=[pl.BlockSpec(memor...]
    unnamed x16 -> x18, local copies, waits for them, and re-layouts: 3.66 us -> 3.74 us
  transfers between devices with their start and end apart: 63 -> 48, of which waited for: 22 -> 15; matrix products, arithmetic and copies ran while one was open for 1% -> 0% of each run, Pallas kernels for 6% -> 11%
where the time goes in v4:
time: 133 us
  starting transfers between devices  82.5 us (62%)
  waiting for transfers between devices  29.5 us (22%)
  Pallas kernels  16.7 us (13%)
  local copies, waits for them, and re-layouts  3.74 us (3%)
    ppermute x45, starting transfers between devices, exchange(): lax.ppermute(blocks[s], 'seq', [(i, i ^ s) for i in range(seq)])  77.4 us
    ppermute x45, waiting for transfers between devices, exchange(): lax.ppermute(blocks[s], 'seq', [(i, i ^ s) for i in range(seq)])  29.5 us
    pallas_call x7, Pallas kernels, call(): pl.pallas_call(kernel, out_shape=out_shapes, in_specs=[pl.BlockSpec(memor...  16.7 us
    ppermute x3, starting transfers between devices, swap_sequences(): return lax.ppermute(array, 'dp', [(0, 1), (1, 0)])  5.1 us
    unnamed x18, local copies, waits for them, and re-layouts  3.74 us
  transfers between devices with their start and end apart: 48, of which 15 were waited for; matrix products, arithmetic and copies ran while one was open for 0% of the time, Pallas kernels for 11%

profile of v4, /device:TPU:0, one launch (start us, length us, event | category | flops | bytes accessed | tf_op | source)
XLA Modules:
  0.0 133.1 jit_solution(11127979230194097667)
XLA Ops:
  0.6 3.0 %collective-permute-start.15 = (bf16[4,512,256]{2,1,0:T(8,128)(2,1)}, bf16[4,512,256]{2,1,0:T(8,128)(2,1)S(1)}, u32[]{:S(2)}, u32[]{:S(2)}) collective-permute-start(bf16[4,512,256]{2,1,0:T(8,128)(2,1)} %bitcast.10), channel_id=1, source_target_pairs={{0,16},{16,0},{1,17},{17,1},{2,18},{18,2},{3,19},{19,3},{4,20},{20... | collective-permute-start | bytes 3145736 | tf_op jit(solution)/shard_map/ppermute | solution.py:33
  3.6 1.3 copy-done
  4.9 1.2 copy-done.4
  6.1 1.2 copy-done.6
  7.3 2.5 %shard_map.92 = (bf16[2,4,32,256]{3,2,1,0:T(8,128)(2,1)S(1)}, bf16[2,4,32,256]{3,2,1,0:T(8,128)(2,1)S(1)}, bf16[2,4,32,256]{3,2,1,0:T(8,128)(2,1)S(1)}, bf16[2,4...) custom-call(s32[1]{0:T(128)} %bitcast.me_ref, ...), custom_call_target="tpu_custom_call" | custom-call | flops 536870912 | bytes 7340032 | tf_op jit(solution)/shard_map/pallas_call | solution.py:51
  9.9 2.7 %collective-permute-start = (bf16[2,4,32,256]{3,2,1,0:T(8,128)(2,1)S(1)}, bf16[2,4,32,256]{3,2,1,0:T(8,128)(2,1)S(1)}, u32[]{:S(2)}, u32[]{:S(2)}) collective-permute-start(bf16[2,4,32,256]{3,2,1,0:T(8,128)(2,1)S(1)} %get-tuple-element.69), channel_id=1, source_target_pairs={{0,8},{1,9},{2,10},{3,11},{4,12},{5,13},{6,14},{7,15},{8,0},{9,1},... | collective-permute-start | bytes 393224 | tf_op jit(solution)/shard_map/ppermute | solution.py:40
  12.5 1.6 %collective-permute-start.1 = (bf16[2,4,32,256]{3,2,1,0:T(8,128)(2,1)S(1)}, bf16[2,4,32,256]{3,2,1,0:T(8,128)(2,1)S(1)}, u32[]{:S(2)}, u32[]{:S(2)}) collective-permute-start(bf16[2,4,32,256]{3,2,1,0:T(8,128)(2,1)S(1)} %get-tuple-element.70), channel_id=1, source_target_pairs={{0,4},{1,5},{2,6},{3,7},{4,0},{5,1},{6,2},{7,3},{8,12},{9,13},{10,... | collective-permute-start | bytes 393224 | tf_op jit(solution)/shard_map/ppermute | solution.py:40
  14.6 5.2 %collective-permute-done.refs_1_ = bf16[2,4,32,256]{3,2,1,0:T(8,128)(2,1)S(1)} collective-permute-done((bf16[2,4,32,256]{3,2,1,0:T(8,128)(2,1)S(1)}, bf16[2,4,32,256]{3,2,1,0:T(8,128)(2,1)S(1)}, u32[]{:S(2)}, u32[]{:S(2)}) %collective-permute-start) | collective-permute-done | bytes 131104 | tf_op jit(solution)/shard_map/ppermute | solution.py:40
  19.8 1.0 collective-permute-start.12
  20.8 3.5 %collective-permute-start.13 = (bf16[2,4,32,256]{3,2,1,0:T(8,128)(2,1)S(1)}, bf16[2,4,32,256]{3,2,1,0:T(8,128)(2,1)S(1)}, u32[]{:S(2)}, u32[]{:S(2)}) collective-permute-start(bf16[2,4,32,256]{3,2,1,0:T(8,128)(2,1)S(1)} %get-tuple-element.82), channel_id=1, source_target_pairs={{0,5},{1,4},{2,7},{3,6},{4,1},{5,0},{6,3},{7,2},{8,13},{9,12},{10,... | collective-permute-start | bytes 393224 | tf_op jit(solution)/shard_map/ppermute | solution.py:40
  24.3 4.8 %collective-permute-start.14 = (bf16[2,4,32,256]{3,2,1,0:T(8,128)(2,1)S(1)}, bf16[2,4,32,256]{3,2,1,0:T(8,128)(2,1)S(1)}, u32[]{:S(2)}, u32[]{:S(2)}) collective-permute-start(bf16[2,4,32,256]{3,2,1,0:T(8,128)(2,1)S(1)} %get-tuple-element.83), channel_id=1, source_target_pairs={{0,11},{1,10},{2,9},{3,8},{4,15},{5,14},{6,13},{7,12},{8,3},{9,2},... | collective-permute-start | bytes 393224 | tf_op jit(solution)/shard_map/ppermute | solution.py:40
  29.7 5.2 %collective-permute-start.3 = (bf16[2,4,32,256]{3,2,1,0:T(8,128)(2,1)S(1)}, bf16[2,4,32,256]{3,2,1,0:T(8,128)(2,1)S(1)}, u32[]{:S(2)}, u32[]{:S(2)}) collective-permute-start(bf16[2,4,32,256]{3,2,1,0:T(8,128)(2,1)S(1)} %get-tuple-element.72), channel_id=1, source_target_pairs={{0,12},{1,13},{2,14},{3,15},{4,8},{5,9},{6,10},{7,11},{8,4},{9,5},... | collective-permute-start | bytes 393224 | tf_op jit(solution)/shard_map/ppermute | solution.py:40
  34.9 8.1 %collective-permute-start.5 = (bf16[2,4,32,256]{3,2,1,0:T(8,128)(2,1)S(1)}, bf16[2,4,32,256]{3,2,1,0:T(8,128)(2,1)S(1)}, u32[]{:S(2)}, u32[]{:S(2)}) collective-permute-start(bf16[2,4,32,256]{3,2,1,0:T(8,128)(2,1)S(1)} %get-tuple-element.74), channel_id=1, source_target_pairs={{0,13},{1,12},{2,15},{3,14},{4,9},{5,8},{6,11},{7,10},{8,5},{9,4},... | collective-permute-start | bytes 393224 | tf_op jit(solution)/shard_map/ppermute | solution.py:40
  43.0 1.6 %collective-permute-start.6 = (bf16[2,4,32,256]{3,2,1,0:T(8,128)(2,1)S(1)}, bf16[2,4,32,256]{3,2,1,0:T(8,128)(2,1)S(1)}, u32[]{:S(2)}, u32[]{:S(2)}) collective-permute-start(bf16[2,4,32,256]{3,2,1,0:T(8,128)(2,1)S(1)} %get-tuple-element.75), channel_id=1, source_target_pairs={{0,3},{1,2},{2,1},{3,0},{4,7},{5,6},{6,5},{7,4},{8,11},{9,10},{10,... | collective-permute-start | bytes 393224 | tf_op jit(solution)/shard_map/ppermute | solution.py:40
  44.8 1.3 collective-permute-start.8
  46.6 5.2 %collective-permute-start.9 = (bf16[2,4,32,256]{3,2,1,0:T(8,128)(2,1)S(1)}, bf16[2,4,32,256]{3,2,1,0:T(8,128)(2,1)S(1)}, u32[]{:S(2)}, u32[]{:S(2)}) collective-permute-start(bf16[2,4,32,256]{3,2,1,0:T(8,128)(2,1)S(1)} %get-tuple-element.78), channel_id=1, source_target_pairs={{0,15},{1,14},{2,13},{3,12},{4,11},{5,10},{6,9},{7,8},{8,7},{9,6},... | collective-permute-start | bytes 393224 | tf_op jit(solution)/shard_map/ppermute | solution.py:40
  51.8 1.8 %collective-permute-done.7.refs_8_ = bf16[2,4,32,256]{3,2,1,0:T(8,128)(2,1)S(1)} collective-permute-done((bf16[2,4,32,256]{3,2,1,0:T(8,128)(2,1)S(1)}, bf16[2,4,32,256]{3,2,1,0:T(8,128)(2,1)S(1)}, u32[]{:S(2)}, u32[]{:S(2)}) %collective-permute-start.7) | collective-permute-done | bytes 131104 | tf_op jit(solution)/shard_map/ppermute | solution.py:40
  53.7 4.0 %collective-permute-done.9.refs_10_ = bf16[2,4,32,256]{3,2,1,0:T(8,128)(2,1)S(1)} collective-permute-done((bf16[2,4,32,256]{3,2,1,0:T(8,128)(2,1)S(1)}, bf16[2,4,32,256]{3,2,1,0:T(8,128)(2,1)S(1)}, u32[]{:S(2)}, u32[]{:S(2)}) %collective-permute-start.9) | collective-permute-done | bytes 131104 | tf_op jit(solution)/shard_map/ppermute | solution.py:40
  57.7 3.0 %shard_map.93 = (bf16[4,32,256]{2,1,0:T(8,128)(2,1)S(1)}, bf16[4,32,256]{2,1,0:T(8,128)(2,1)S(1)}, bf16[4,32,256]{2,1,0:T(8,128)(2,1)S(1)}, bf16[4,32,256]{2,1,0...) custom-call(s32[1]{0:T(128)} %bitcast.me_ref, ...), custom_call_target="tpu_custom_call" | custom-call | flops 67108864 | bytes 4456448 | tf_op jit(solution)/shard_map/pallas_call | solution.py:51
  60.6 5.6 %collective-permute-start.31 = (bf16[4,32,256]{2,1,0:T(8,128)(2,1)S(1)}, bf16[4,32,256]{2,1,0:T(8,128)(2,1)S(1)}, u32[]{:S(2)}, u32[]{:S(2)}) collective-permute-start(bf16[4,32,256]{2,1,0:T(8,128)(2,1)S(1)} %get-tuple-element.104), channel_id=1, source_target_pairs={{0,8},{1,9},{2,10},{3,11},{4,12},{5,13},{6,14},{7,15},{8,0},{9,1},... | collective-permute-start | bytes 196616 | tf_op jit(solution)/shard_map/ppermute | solution.py:40
  66.3 1.0 collective-permute-start.34
  67.3 2.7 %collective-permute-start.35 = (bf16[4,32,256]{2,1,0:T(8,128)(2,1)S(1)}, bf16[4,32,256]{2,1,0:T(8,128)(2,1)S(1)}, u32[]{:S(2)}, u32[]{:S(2)}) collective-permute-start(bf16[4,32,256]{2,1,0:T(8,128)(2,1)S(1)} %get-tuple-element.108), channel_id=1, source_target_pairs={{0,10},{1,11},{2,8},{3,9},{4,14},{5,15},{6,12},{7,13},{8,2},{9,3},... | collective-permute-start | bytes 196616 | tf_op jit(solution)/shard_map/ppermute | solution.py:40
  70.0 3.1 %shard_map.94 = (bf16[4,32,256]{2,1,0:T(8,128)(2,1)S(1)}, bf16[4,32,256]{2,1,0:T(8,128)(2,1)S(1)}, bf16[4,32,256]{2,1,0:T(8,128)(2,1)S(1)}, bf16[4,32,256]{2,1,0...) custom-call(s32[1]{0:T(128)} %bitcast.me_ref, ...), custom_call_target="tpu_custom_call" | custom-call | flops 134217728 | bytes 5767168 | tf_op jit(solution)/shard_map/pallas_call | solution.py:51
  73.2 1.5 %collective-permute-start.36 = (bf16[4,32,256]{2,1,0:T(8,128)(2,1)S(1)}, bf16[4,32,256]{2,1,0:T(8,128)(2,1)S(1)}, u32[]{:S(2)}, u32[]{:S(2)}) collective-permute-start(bf16[4,32,256]{2,1,0:T(8,128)(2,1)S(1)} %get-tuple-element.109), channel_id=1, source_target_pairs={{0,5},{1,4},{2,7},{3,6},{4,1},{5,0},{6,3},{7,2},{8,13},{9,12},{10,... | collective-permute-start | bytes 196616 | tf_op jit(solution)/shard_map/ppermute | solution.py:40
  74.7 1.3 collective-permute-start.37
  76.7 2.1 %collective-permute-start.45 = (bf16[4,32,256]{2,1,0:T(8,128)(2,1)S(1)}, bf16[4,32,256]{2,1,0:T(8,128)(2,1)S(1)}, u32[]{:S(2)}, u32[]{:S(2)}) collective-permute-start(bf16[4,32,256]{2,1,0:T(8,128)(2,1)S(1)} %get-tuple-element.126), channel_id=1, source_target_pairs={{0,15},{1,14},{2,13},{3,12},{4,11},{5,10},{6,9},{7,8},{8,7},{9,6},... | collective-permute-start | bytes 196616 | tf_op jit(solution)/shard_map/ppermute | solution.py:40
  78.8 1.8 %collective-permute-start.44 = (bf16[4,32,256]{2,1,0:T(8,128)(2,1)S(1)}, bf16[4,32,256]{2,1,0:T(8,128)(2,1)S(1)}, u32[]{:S(2)}, u32[]{:S(2)}) collective-permute-start(bf16[4,32,256]{2,1,0:T(8,128)(2,1)S(1)} %get-tuple-element.124), channel_id=1, source_target_pairs={{0,7},{1,6},{2,5},{3,4},{4,3},{5,2},{6,1},{7,0},{8,15},{9,14},{10,... | collective-permute-start | bytes 196616 | tf_op jit(solution)/shard_map/ppermute | solution.py:40
  82.6 2.9 %collective-permute-start.41 = (bf16[4,32,256]{2,1,0:T(8,128)(2,1)S(1)}, bf16[4,32,256]{2,1,0:T(8,128)(2,1)S(1)}, u32[]{:S(2)}, u32[]{:S(2)}) collective-permute-start(bf16[4,32,256]{2,1,0:T(8,128)(2,1)S(1)} %get-tuple-element.118), channel_id=1, source_target_pairs={{0,13},{1,12},{2,15},{3,14},{4,9},{5,8},{6,11},{7,10},{8,5},{9,4},... | collective-permute-start | bytes 196616 | tf_op jit(solution)/shard_map/ppermute | solution.py:40
  85.9 2.1 %collective-permute-start.39 = (bf16[4,32,256]{2,1,0:T(8,128)(2,1)S(1)}, bf16[4,32,256]{2,1,0:T(8,128)(2,1)S(1)}, u32[]{:S(2)}, u32[]{:S(2)}) collective-permute-start(bf16[4,32,256]{2,1,0:T(8,128)(2,1)S(1)} %get-tuple-element.114), channel_id=1, source_target_pairs={{0,12},{1,13},{2,14},{3,15},{4,8},{5,9},{6,10},{7,11},{8,4},{9,5},... | collective-permute-start | bytes 196616 | tf_op jit(solution)/shard_map/ppermute | solution.py:40
  88.2 3.0 %collective-permute-done.40.refs_10_ = bf16[4,32,256]{2,1,0:T(8,128)(2,1)S(1)} collective-permute-done((bf16[4,32,256]{2,1,0:T(8,128)(2,1)S(1)}, bf16[4,32,256]{2,1,0:T(8,128)(2,1)S(1)}, u32[]{:S(2)}, u32[]{:S(2)}) %collective-permute-start.40) | collective-permute-done | bytes 65568 | tf_op jit(solution)/shard_map/ppermute | solution.py:40
  92.8 1.7 %collective-permute-start.16 = (bf16[4,32,256]{2,1,0:T(8,128)(2,1)S(1)}, bf16[4,32,256]{2,1,0:T(8,128)(2,1)S(1)}, u32[]{:S(2)}, u32[]{:S(2)}) collective-permute-start(bf16[4,32,256]{2,1,0:T(8,128)(2,1)S(1)} %get-tuple-element.86), channel_id=1, source_target_pairs={{0,8},{1,9},{2,10},{3,11},{4,12},{5,13},{6,14},{7,15},{8,0},{9,1},... | collective-permute-start | bytes 196616 | tf_op jit(solution)/shard_map/ppermute | solution.py:40
  94.5 1.2 collective-permute-start.17
  95.7 1.6 %collective-permute-start.19 = (bf16[4,32,256]{2,1,0:T(8,128)(2,1)S(1)}, bf16[4,32,256]{2,1,0:T(8,128)(2,1)S(1)}, u32[]{:S(2)}, u32[]{:S(2)}) collective-permute-start(bf16[4,32,256]{2,1,0:T(8,128)(2,1)S(1)} %get-tuple-element.89), channel_id=1, source_target_pairs={{0,1},{1,0},{2,3},{3,2},{4,5},{5,4},{6,7},{7,6},{8,9},{9,8},{10,11... | collective-permute-start | bytes 196616 | tf_op jit(solution)/shard_map/ppermute | solution.py:40
  98.1 2.4 %collective-permute-start.20 = (bf16[4,32,256]{2,1,0:T(8,128)(2,1)S(1)}, bf16[4,32,256]{2,1,0:T(8,128)(2,1)S(1)}, u32[]{:S(2)}, u32[]{:S(2)}) collective-permute-start(bf16[4,32,256]{2,1,0:T(8,128)(2,1)S(1)} %get-tuple-element.90), channel_id=1, source_target_pairs={{0,10},{1,11},{2,8},{3,9},{4,14},{5,15},{6,12},{7,13},{8,2},{9,3},... | collective-permute-start | bytes 196616 | tf_op jit(solution)/shard_map/ppermute | solution.py:40
  100.5 1.2 collective-permute-done.18.refs_3_
  101.7 1.3 collective-permute-start.22
  103.0 1.4 %collective-permute-start.23 = (bf16[4,32,256]{2,1,0:T(8,128)(2,1)S(1)}, bf16[4,32,256]{2,1,0:T(8,128)(2,1)S(1)}, u32[]{:S(2)}, u32[]{:S(2)}) collective-permute-start(bf16[4,32,256]{2,1,0:T(8,128)(2,1)S(1)} %get-tuple-element.93), channel_id=1, source_target_pairs={{0,2},{1,3},{2,0},{3,1},{4,6},{5,7},{6,4},{7,5},{8,10},{9,11},{10,... | collective-permute-start | bytes 196616 | tf_op jit(solution)/shard_map/ppermute | solution.py:40
  104.4 1.2 collective-permute-done.20.refs_5_
  105.6 2.2 %collective-permute-start.24 = (bf16[4,32,256]{2,1,0:T(8,128)(2,1)S(1)}, bf16[4,32,256]{2,1,0:T(8,128)(2,1)S(1)}, u32[]{:S(2)}, u32[]{:S(2)}) collective-permute-start(bf16[4,32,256]{2,1,0:T(8,128)(2,1)S(1)} %get-tuple-element.94), channel_id=1, source_target_pairs={{0,12},{1,13},{2,14},{3,15},{4,8},{5,9},{6,10},{7,11},{8,4},{9,5},... | collective-permute-start | bytes 196616 | tf_op jit(solution)/shard_map/ppermute | solution.py:40
  107.9 1.5 %collective-permute-start.47 = (bf16[32,64,64]{2,1,0:T(8,128)(2,1)S(1)}, bf16[32,64,64]{2,1,0:T(8,128)(2,1)S(1)}, u32[]{:S(2)}, u32[]{:S(2)}) collective-permute-start(bf16[32,64,64]{2,1,0:T(8,128)(2,1)S(1)} %get-tuple-element.113.right_ref), channel_id=1, source_target_pairs={{0,16},{16,0},{1,17},{17,1},{2,18},{18,2},{3,19},{19,3},{4,20},{20... | collective-permute-start | bytes 786440 | tf_op jit(solution)/shard_map/ppermute | solution.py:33
  109.7 2.0 %collective-permute-start.26 = (bf16[4,32,256]{2,1,0:T(8,128)(2,1)S(1)}, bf16[4,32,256]{2,1,0:T(8,128)(2,1)S(1)}, u32[]{:S(2)}, u32[]{:S(2)}) collective-permute-start(bf16[4,32,256]{2,1,0:T(8,128)(2,1)S(1)} %get-tuple-element.96), channel_id=1, source_target_pairs={{0,13},{1,12},{2,15},{3,14},{4,9},{5,8},{6,11},{7,10},{8,5},{9,4},... | collective-permute-start | bytes 196616 | tf_op jit(solution)/shard_map/ppermute | solution.py:40
  112.2 4.1 %collective-permute-done.25.refs_10_ = bf16[4,32,256]{2,1,0:T(8,128)(2,1)S(1)} collective-permute-done((bf16[4,32,256]{2,1,0:T(8,128)(2,1)S(1)}, bf16[4,32,256]{2,1,0:T(8,128)(2,1)S(1)}, u32[]{:S(2)}, u32[]{:S(2)}) %collective-permute-start.25) | collective-permute-done | bytes 65568 | tf_op jit(solution)/shard_map/ppermute | solution.py:40
  117.9 2.0 %collective-permute-start.30 = (bf16[4,32,256]{2,1,0:T(8,128)(2,1)S(1)}, bf16[4,32,256]{2,1,0:T(8,128)(2,1)S(1)}, u32[]{:S(2)}, u32[]{:S(2)}) collective-permute-start(bf16[4,32,256]{2,1,0:T(8,128)(2,1)S(1)} %get-tuple-element.100), channel_id=1, source_target_pairs={{0,15},{1,14},{2,13},{3,12},{4,11},{5,10},{6,9},{7,8},{8,7},{9,6},... | collective-permute-start | bytes 196616 | tf_op jit(solution)/shard_map/ppermute | solution.py:40
  119.9 3.4 %collective-permute-done.28.refs_13_ = bf16[4,32,256]{2,1,0:T(8,128)(2,1)S(1)} collective-permute-done((bf16[4,32,256]{2,1,0:T(8,128)(2,1)S(1)}, bf16[4,32,256]{2,1,0:T(8,128)(2,1)S(1)}, u32[]{:S(2)}, u32[]{:S(2)}) %collective-permute-start.28) | collective-permute-done | bytes 65568 | tf_op jit(solution)/shard_map/ppermute | solution.py:40
  123.3 1.8 %collective-permute-done.30.refs_15_ = bf16[4,32,256]{2,1,0:T(8,128)(2,1)S(1)} collective-permute-done((bf16[4,32,256]{2,1,0:T(8,128)(2,1)S(1)}, bf16[4,32,256]{2,1,0:T(8,128)(2,1)S(1)}, u32[]{:S(2)}, u32[]{:S(2)}) %collective-permute-start.30) | collective-permute-done | bytes 65568 | tf_op jit(solution)/shard_map/ppermute | solution.py:40
  125.1 1.8 %shard_map.95 = (bf16[4,16,32,256]{3,2,1,0:T(8,128)(2,1)}, bf16[4,16,32,256]{3,2,1,0:T(8,128)(2,1)}) custom-call(s32[1]{0:T(128)} %bitcast.me_ref, bf16[4,16,32,256]{3,2,1,0:T(8,128)(2,1)S(1)} %bitcast.14, bf16[4,16,32,256]{3,2,1,0:T(8,128)(2,1)S(1)} %bitcast.16, bf16[4,32,256]{2,1,0:T(8,128)(2,1)S(1)} %get-tuple-element.85.refs_0_, ...), custom_call_target="tpu_custom_call" | custom-call | bytes 5242880 | tf_op jit(solution)/shard_map/pallas_call | solution.py:51
  126.9 3.9 %shard_map.97 = (bf16[4,512,256]{2,1,0:T(8,128)(2,1)}, bf16[4,512,512]{2,1,0:T(8,128)(2,1)S(1)}) custom-call(s32[1]{0:T(128)} %bitcast.me_ref, bf16[4,512,512]{2,1,0:T(8,128)(2,1)} %left_ref.3, bf16[4,512,256]{2,1,0:T(8,128)(2,1)S(1)} %bitcast.12, bf16[4,512,256]{2,1,0:T(8,128)(2,1)S(1)} %bitcast.9), custom_call_target="tpu_custom_call" | custom-call | flops 1073741824 | bytes 7340032 | tf_op jit(solution)/shard_map/pallas_call | solution.py:51
  130.8 2.3 %shard_map.98 = (bf16[4,512,512]{2,1,0:T(8,128)(2,1)}, bf16[32,64,64]{2,1,0:T(8,128)(2,1)}) custom-call(s32[1]{0:T(128)} %bitcast.me_ref, bf16[4,512,512]{2,1,0:T(8,128)(2,1)S(1)} %get-tuple-element.128.term_ref, bf16[4,512,256]{2,1,0:T(8,128)(2,1)S(1)} %copy-done.3, bf16[4,512,256]{2,1,0:T(8,128)(2,1)S(1)} %collective-permute-done.46.grad_ref, ...), custom_call_target="tpu_custom_call" | custom-call | flops 536870912 | bytes 7077888 | tf_op jit(solution)/shard_map/pallas_call | solution.py:51
  (73 shorter events, 10.1 us)
Async XLA Ops:
  0.6 66.7 %collective-permute-start.15 = (bf16[4,512,256]{2,1,0:T(8,128)(2,1)}, bf16[4,512,256]{2,1,0:T(8,128)(2,1)S(1)}, u32[]{:S(2)}, u32[]{:S(2)}) collective-permute-start(bf16[4,512,256]{2,1,0:T(8,128)(2,1)} %bitcast.10), channel_id=1, source_target_pairs={{0,16},{16,0},{1,17},{17,1},{2,18},{18,2},{3,19},{19,3},{4,20},{20... | collective-permute-start | bytes 3145736 | tf_op jit(solution)/shard_map/ppermute | solution.py:33
  9.9 9.9 %collective-permute-start = (bf16[2,4,32,256]{3,2,1,0:T(8,128)(2,1)S(1)}, bf16[2,4,32,256]{3,2,1,0:T(8,128)(2,1)S(1)}, u32[]{:S(2)}, u32[]{:S(2)}) collective-permute-start(bf16[2,4,32,256]{3,2,1,0:T(8,128)(2,1)S(1)} %get-tuple-element.69), channel_id=1, source_target_pairs={{0,8},{1,9},{2,10},{3,11},{4,12},{5,13},{6,14},{7,15},{8,0},{9,1},... | collective-permute-start | bytes 393224 | tf_op jit(solution)/shard_map/ppermute | solution.py:40
  12.5 8.3 %collective-permute-start.1 = (bf16[2,4,32,256]{3,2,1,0:T(8,128)(2,1)S(1)}, bf16[2,4,32,256]{3,2,1,0:T(8,128)(2,1)S(1)}, u32[]{:S(2)}, u32[]{:S(2)}) collective-permute-start(bf16[2,4,32,256]{3,2,1,0:T(8,128)(2,1)S(1)} %get-tuple-element.70), channel_id=1, source_target_pairs={{0,4},{1,5},{2,6},{3,7},{4,0},{5,1},{6,2},{7,3},{8,12},{9,13},{10,... | collective-permute-start | bytes 393224 | tf_op jit(solution)/shard_map/ppermute | solution.py:40
  14.1 10.2 %collective-permute-start.10 = (bf16[2,4,32,256]{3,2,1,0:T(8,128)(2,1)S(1)}, bf16[2,4,32,256]{3,2,1,0:T(8,128)(2,1)S(1)}, u32[]{:S(2)}, u32[]{:S(2)}) collective-permute-start(bf16[2,4,32,256]{3,2,1,0:T(8,128)(2,1)S(1)} %get-tuple-element.79), channel_id=1, source_target_pairs={{0,9},{1,8},{2,11},{3,10},{4,13},{5,12},{6,15},{7,14},{8,1},{9,0},... | collective-permute-start | bytes 393224 | tf_op jit(solution)/shard_map/ppermute | solution.py:40
  14.1 15.0 %collective-permute-start.11 = (bf16[2,4,32,256]{3,2,1,0:T(8,128)(2,1)S(1)}, bf16[2,4,32,256]{3,2,1,0:T(8,128)(2,1)S(1)}, u32[]{:S(2)}, u32[]{:S(2)}) collective-permute-start(bf16[2,4,32,256]{3,2,1,0:T(8,128)(2,1)S(1)} %get-tuple-element.80), channel_id=1, source_target_pairs={{0,1},{1,0},{2,3},{3,2},{4,5},{5,4},{6,7},{7,6},{8,9},{9,8},{10,11... | collective-permute-start | bytes 393224 | tf_op jit(solution)/shard_map/ppermute | solution.py:40
  19.8 9.9 %collective-permute-start.12 = (bf16[2,4,32,256]{3,2,1,0:T(8,128)(2,1)S(1)}, bf16[2,4,32,256]{3,2,1,0:T(8,128)(2,1)S(1)}, u32[]{:S(2)}, u32[]{:S(2)}) collective-permute-start(bf16[2,4,32,256]{3,2,1,0:T(8,128)(2,1)S(1)} %get-tuple-element.81), channel_id=1, source_target_pairs={{0,10},{1,11},{2,8},{3,9},{4,14},{5,15},{6,12},{7,13},{8,2},{9,3},... | collective-permute-start | bytes 393224 | tf_op jit(solution)/shard_map/ppermute | solution.py:40
  20.8 14.1 %collective-permute-start.13 = (bf16[2,4,32,256]{3,2,1,0:T(8,128)(2,1)S(1)}, bf16[2,4,32,256]{3,2,1,0:T(8,128)(2,1)S(1)}, u32[]{:S(2)}, u32[]{:S(2)}) collective-permute-start(bf16[2,4,32,256]{3,2,1,0:T(8,128)(2,1)S(1)} %get-tuple-element.82), channel_id=1, source_target_pairs={{0,5},{1,4},{2,7},{3,6},{4,1},{5,0},{6,3},{7,2},{8,13},{9,12},{10,... | collective-permute-start | bytes 393224 | tf_op jit(solution)/shard_map/ppermute | solution.py:40
  24.3 10.6 %collective-permute-start.14 = (bf16[2,4,32,256]{3,2,1,0:T(8,128)(2,1)S(1)}, bf16[2,4,32,256]{3,2,1,0:T(8,128)(2,1)S(1)}, u32[]{:S(2)}, u32[]{:S(2)}) collective-permute-start(bf16[2,4,32,256]{3,2,1,0:T(8,128)(2,1)S(1)} %get-tuple-element.83), channel_id=1, source_target_pairs={{0,11},{1,10},{2,9},{3,8},{4,15},{5,14},{6,13},{7,12},{8,3},{9,2},... | collective-permute-start | bytes 393224 | tf_op jit(solution)/shard_map/ppermute | solution.py:40
  29.1 13.8 %collective-permute-start.2 = (bf16[2,4,32,256]{3,2,1,0:T(8,128)(2,1)S(1)}, bf16[2,4,32,256]{3,2,1,0:T(8,128)(2,1)S(1)}, u32[]{:S(2)}, u32[]{:S(2)}) collective-permute-start(bf16[2,4,32,256]{3,2,1,0:T(8,128)(2,1)S(1)} %get-tuple-element.71), channel_id=1, source_target_pairs={{0,2},{1,3},{2,0},{3,1},{4,6},{5,7},{6,4},{7,5},{8,10},{9,11},{10,... | collective-permute-start | bytes 393224 | tf_op jit(solution)/shard_map/ppermute | solution.py:40
  29.7 14.9 %collective-permute-start.3 = (bf16[2,4,32,256]{3,2,1,0:T(8,128)(2,1)S(1)}, bf16[2,4,32,256]{3,2,1,0:T(8,128)(2,1)S(1)}, u32[]{:S(2)}, u32[]{:S(2)}) collective-permute-start(bf16[2,4,32,256]{3,2,1,0:T(8,128)(2,1)S(1)} %get-tuple-element.72), channel_id=1, source_target_pairs={{0,12},{1,13},{2,14},{3,15},{4,8},{5,9},{6,10},{7,11},{8,4},{9,5},... | collective-permute-start | bytes 393224 | tf_op jit(solution)/shard_map/ppermute | solution.py:40
  34.9 9.9 %collective-permute-start.4 = (bf16[2,4,32,256]{3,2,1,0:T(8,128)(2,1)S(1)}, bf16[2,4,32,256]{3,2,1,0:T(8,128)(2,1)S(1)}, u32[]{:S(2)}, u32[]{:S(2)}) collective-permute-start(bf16[2,4,32,256]{3,2,1,0:T(8,128)(2,1)S(1)} %get-tuple-element.73), channel_id=1, source_target_pairs={{0,6},{1,7},{2,4},{3,5},{4,2},{5,3},{6,0},{7,1},{8,14},{9,15},{10,... | collective-permute-start | bytes 393224 | tf_op jit(solution)/shard_map/ppermute | solution.py:40
  34.9 11.8 %collective-permute-start.5 = (bf16[2,4,32,256]{3,2,1,0:T(8,128)(2,1)S(1)}, bf16[2,4,32,256]{3,2,1,0:T(8,128)(2,1)S(1)}, u32[]{:S(2)}, u32[]{:S(2)}) collective-permute-start(bf16[2,4,32,256]{3,2,1,0:T(8,128)(2,1)S(1)} %get-tuple-element.74), channel_id=1, source_target_pairs={{0,13},{1,12},{2,15},{3,14},{4,9},{5,8},{6,11},{7,10},{8,5},{9,4},... | collective-permute-start | bytes 393224 | tf_op jit(solution)/shard_map/ppermute | solution.py:40
  43.0 8.9 %collective-permute-start.6 = (bf16[2,4,32,256]{3,2,1,0:T(8,128)(2,1)S(1)}, bf16[2,4,32,256]{3,2,1,0:T(8,128)(2,1)S(1)}, u32[]{:S(2)}, u32[]{:S(2)}) collective-permute-start(bf16[2,4,32,256]{3,2,1,0:T(8,128)(2,1)S(1)} %get-tuple-element.75), channel_id=1, source_target_pairs={{0,3},{1,2},{2,1},{3,0},{4,7},{5,6},{6,5},{7,4},{8,11},{9,10},{10,... | collective-permute-start | bytes 393224 | tf_op jit(solution)/shard_map/ppermute | solution.py:40
  44.5 9.1 %collective-permute-start.7 = (bf16[2,4,32,256]{3,2,1,0:T(8,128)(2,1)S(1)}, bf16[2,4,32,256]{3,2,1,0:T(8,128)(2,1)S(1)}, u32[]{:S(2)}, u32[]{:S(2)}) collective-permute-start(bf16[2,4,32,256]{3,2,1,0:T(8,128)(2,1)S(1)} %get-tuple-element.76), channel_id=1, source_target_pairs={{0,14},{1,15},{2,12},{3,13},{4,10},{5,11},{6,8},{7,9},{8,6},{9,7},... | collective-permute-start | bytes 393224 | tf_op jit(solution)/shard_map/ppermute | solution.py:40
  44.8 8.9 %collective-permute-start.8 = (bf16[2,4,32,256]{3,2,1,0:T(8,128)(2,1)S(1)}, bf16[2,4,32,256]{3,2,1,0:T(8,128)(2,1)S(1)}, u32[]{:S(2)}, u32[]{:S(2)}) collective-permute-start(bf16[2,4,32,256]{3,2,1,0:T(8,128)(2,1)S(1)} %get-tuple-element.77), channel_id=1, source_target_pairs={{0,7},{1,6},{2,5},{3,4},{4,3},{5,2},{6,1},{7,0},{8,15},{9,14},{10,... | collective-permute-start | bytes 393224 | tf_op jit(solution)/shard_map/ppermute | solution.py:40
  46.6 11.0 %collective-permute-start.9 = (bf16[2,4,32,256]{3,2,1,0:T(8,128)(2,1)S(1)}, bf16[2,4,32,256]{3,2,1,0:T(8,128)(2,1)S(1)}, u32[]{:S(2)}, u32[]{:S(2)}) collective-permute-start(bf16[2,4,32,256]{3,2,1,0:T(8,128)(2,1)S(1)} %get-tuple-element.78), channel_id=1, source_target_pairs={{0,15},{1,14},{2,13},{3,12},{4,11},{5,10},{6,9},{7,8},{8,7},{9,6},... | collective-permute-start | bytes 393224 | tf_op jit(solution)/shard_map/ppermute | solution.py:40
  60.6 12.5 %collective-permute-start.31 = (bf16[4,32,256]{2,1,0:T(8,128)(2,1)S(1)}, bf16[4,32,256]{2,1,0:T(8,128)(2,1)S(1)}, u32[]{:S(2)}, u32[]{:S(2)}) collective-permute-start(bf16[4,32,256]{2,1,0:T(8,128)(2,1)S(1)} %get-tuple-element.104), channel_id=1, source_target_pairs={{0,8},{1,9},{2,10},{3,11},{4,12},{5,13},{6,14},{7,15},{8,0},{9,1},... | collective-permute-start | bytes 196616 | tf_op jit(solution)/shard_map/ppermute | solution.py:40
  66.2 8.4 %collective-permute-start.32 = (bf16[4,32,256]{2,1,0:T(8,128)(2,1)S(1)}, bf16[4,32,256]{2,1,0:T(8,128)(2,1)S(1)}, u32[]{:S(2)}, u32[]{:S(2)}) collective-permute-start(bf16[4,32,256]{2,1,0:T(8,128)(2,1)S(1)} %get-tuple-element.105), channel_id=1, source_target_pairs={{0,4},{1,5},{2,6},{3,7},{4,0},{5,1},{6,2},{7,3},{8,12},{9,13},{10,... | collective-permute-start | bytes 196616 | tf_op jit(solution)/shard_map/ppermute | solution.py:40
  66.2 9.7 %collective-permute-start.33 = (bf16[4,32,256]{2,1,0:T(8,128)(2,1)S(1)}, bf16[4,32,256]{2,1,0:T(8,128)(2,1)S(1)}, u32[]{:S(2)}, u32[]{:S(2)}) collective-permute-start(bf16[4,32,256]{2,1,0:T(8,128)(2,1)S(1)} %get-tuple-element.106), channel_id=1, source_target_pairs={{0,9},{1,8},{2,11},{3,10},{4,13},{5,12},{6,15},{7,14},{8,1},{9,0},... | collective-permute-start | bytes 196616 | tf_op jit(solution)/shard_map/ppermute | solution.py:40
  66.3 10.4 %collective-permute-start.34 = (bf16[4,32,256]{2,1,0:T(8,128)(2,1)S(1)}, bf16[4,32,256]{2,1,0:T(8,128)(2,1)S(1)}, u32[]{:S(2)}, u32[]{:S(2)}) collective-permute-start(bf16[4,32,256]{2,1,0:T(8,128)(2,1)S(1)} %get-tuple-element.107), channel_id=1, source_target_pairs={{0,1},{1,0},{2,3},{3,2},{4,5},{5,4},{6,7},{7,6},{8,9},{9,8},{10,11... | collective-permute-start | bytes 196616 | tf_op jit(solution)/shard_map/ppermute | solution.py:40
  67.3 11.5 %collective-permute-start.35 = (bf16[4,32,256]{2,1,0:T(8,128)(2,1)S(1)}, bf16[4,32,256]{2,1,0:T(8,128)(2,1)S(1)}, u32[]{:S(2)}, u32[]{:S(2)}) collective-permute-start(bf16[4,32,256]{2,1,0:T(8,128)(2,1)S(1)} %get-tuple-element.108), channel_id=1, source_target_pairs={{0,10},{1,11},{2,8},{3,9},{4,14},{5,15},{6,12},{7,13},{8,2},{9,3},... | collective-permute-start | bytes 196616 | tf_op jit(solution)/shard_map/ppermute | solution.py:40
  73.2 7.4 %collective-permute-start.36 = (bf16[4,32,256]{2,1,0:T(8,128)(2,1)S(1)}, bf16[4,32,256]{2,1,0:T(8,128)(2,1)S(1)}, u32[]{:S(2)}, u32[]{:S(2)}) collective-permute-start(bf16[4,32,256]{2,1,0:T(8,128)(2,1)S(1)} %get-tuple-element.109), channel_id=1, source_target_pairs={{0,5},{1,4},{2,7},{3,6},{4,1},{5,0},{6,3},{7,2},{8,13},{9,12},{10,... | collective-permute-start | bytes 196616 | tf_op jit(solution)/shard_map/ppermute | solution.py:40
  74.7 7.4 %collective-permute-start.37 = (bf16[4,32,256]{2,1,0:T(8,128)(2,1)S(1)}, bf16[4,32,256]{2,1,0:T(8,128)(2,1)S(1)}, u32[]{:S(2)}, u32[]{:S(2)}) collective-permute-start(bf16[4,32,256]{2,1,0:T(8,128)(2,1)S(1)} %get-tuple-element.110), channel_id=1, source_target_pairs={{0,11},{1,10},{2,9},{3,8},{4,15},{5,14},{6,13},{7,12},{8,3},{9,2},... | collective-permute-start | bytes 196616 | tf_op jit(solution)/shard_map/ppermute | solution.py:40
  76.0 6.7 %collective-permute-start.38 = (bf16[4,32,256]{2,1,0:T(8,128)(2,1)S(1)}, bf16[4,32,256]{2,1,0:T(8,128)(2,1)S(1)}, u32[]{:S(2)}, u32[]{:S(2)}) collective-permute-start(bf16[4,32,256]{2,1,0:T(8,128)(2,1)S(1)} %get-tuple-element.111), channel_id=1, source_target_pairs={{0,2},{1,3},{2,0},{3,1},{4,6},{5,7},{6,4},{7,5},{8,10},{9,11},{10,... | collective-permute-start | bytes 196616 | tf_op jit(solution)/shard_map/ppermute | solution.py:40
  76.7 8.9 %collective-permute-start.45 = (bf16[4,32,256]{2,1,0:T(8,128)(2,1)S(1)}, bf16[4,32,256]{2,1,0:T(8,128)(2,1)S(1)}, u32[]{:S(2)}, u32[]{:S(2)}) collective-permute-start(bf16[4,32,256]{2,1,0:T(8,128)(2,1)S(1)} %get-tuple-element.126), channel_id=1, source_target_pairs={{0,15},{1,14},{2,13},{3,12},{4,11},{5,10},{6,9},{7,8},{8,7},{9,6},... | collective-permute-start | bytes 196616 | tf_op jit(solution)/shard_map/ppermute | solution.py:40
  78.8 7.2 %collective-permute-start.44 = (bf16[4,32,256]{2,1,0:T(8,128)(2,1)S(1)}, bf16[4,32,256]{2,1,0:T(8,128)(2,1)S(1)}, u32[]{:S(2)}, u32[]{:S(2)}) collective-permute-start(bf16[4,32,256]{2,1,0:T(8,128)(2,1)S(1)} %get-tuple-element.124), channel_id=1, source_target_pairs={{0,7},{1,6},{2,5},{3,4},{4,3},{5,2},{6,1},{7,0},{8,15},{9,14},{10,... | collective-permute-start | bytes 196616 | tf_op jit(solution)/shard_map/ppermute | solution.py:40
  80.6 7.4 %collective-permute-start.43 = (bf16[4,32,256]{2,1,0:T(8,128)(2,1)S(1)}, bf16[4,32,256]{2,1,0:T(8,128)(2,1)S(1)}, u32[]{:S(2)}, u32[]{:S(2)}) collective-permute-start(bf16[4,32,256]{2,1,0:T(8,128)(2,1)S(1)} %get-tuple-element.122), channel_id=1, source_target_pairs={{0,14},{1,15},{2,12},{3,13},{4,10},{5,11},{6,8},{7,9},{8,6},{9,7},... | collective-permute-start | bytes 196616 | tf_op jit(solution)/shard_map/ppermute | solution.py:40
  82.0 6.0 %collective-permute-start.42 = (bf16[4,32,256]{2,1,0:T(8,128)(2,1)S(1)}, bf16[4,32,256]{2,1,0:T(8,128)(2,1)S(1)}, u32[]{:S(2)}, u32[]{:S(2)}) collective-permute-start(bf16[4,32,256]{2,1,0:T(8,128)(2,1)S(1)} %get-tuple-element.120), channel_id=1, source_target_pairs={{0,3},{1,2},{2,1},{3,0},{4,7},{5,6},{6,5},{7,4},{8,11},{9,10},{10,... | collective-permute-start | bytes 196616 | tf_op jit(solution)/shard_map/ppermute | solution.py:40
  82.6 5.6 %collective-permute-start.41 = (bf16[4,32,256]{2,1,0:T(8,128)(2,1)S(1)}, bf16[4,32,256]{2,1,0:T(8,128)(2,1)S(1)}, u32[]{:S(2)}, u32[]{:S(2)}) collective-permute-start(bf16[4,32,256]{2,1,0:T(8,128)(2,1)S(1)} %get-tuple-element.118), channel_id=1, source_target_pairs={{0,13},{1,12},{2,15},{3,14},{4,9},{5,8},{6,11},{7,10},{8,5},{9,4},... | collective-permute-start | bytes 196616 | tf_op jit(solution)/shard_map/ppermute | solution.py:40
  85.6 5.6 %collective-permute-start.40 = (bf16[4,32,256]{2,1,0:T(8,128)(2,1)S(1)}, bf16[4,32,256]{2,1,0:T(8,128)(2,1)S(1)}, u32[]{:S(2)}, u32[]{:S(2)}) collective-permute-start(bf16[4,32,256]{2,1,0:T(8,128)(2,1)S(1)} %get-tuple-element.116), channel_id=1, source_target_pairs={{0,6},{1,7},{2,4},{3,5},{4,2},{5,3},{6,0},{7,1},{8,14},{9,15},{10,... | collective-permute-start | bytes 196616 | tf_op jit(solution)/shard_map/ppermute | solution.py:40
  85.9 6.2 %collective-permute-start.39 = (bf16[4,32,256]{2,1,0:T(8,128)(2,1)S(1)}, bf16[4,32,256]{2,1,0:T(8,128)(2,1)S(1)}, u32[]{:S(2)}, u32[]{:S(2)}) collective-permute-start(bf16[4,32,256]{2,1,0:T(8,128)(2,1)S(1)} %get-tuple-element.114), channel_id=1, source_target_pairs={{0,12},{1,13},{2,14},{3,15},{4,8},{5,9},{6,10},{7,11},{8,4},{9,5},... | collective-permute-start | bytes 196616 | tf_op jit(solution)/shard_map/ppermute | solution.py:40
  92.2 38.6 %collective-permute-start.46 = (bf16[4,512,256]{2,1,0:T(8,128)(2,1)S(1)}, bf16[4,512,256]{2,1,0:T(8,128)(2,1)S(1)}, u32[]{:S(2)}, u32[]{:S(2)}) collective-permute-start(bf16[4,512,256]{2,1,0:T(8,128)(2,1)S(1)} %bitcast.8), channel_id=1, source_target_pairs={{0,16},{16,0},{1,17},{17,1},{2,18},{18,2},{3,19},{19,3},{4,20},{20... | collective-permute-start | bytes 3145736 | tf_op jit(solution)/shard_map/ppermute | solution.py:33
  92.8 5.3 %collective-permute-start.16 = (bf16[4,32,256]{2,1,0:T(8,128)(2,1)S(1)}, bf16[4,32,256]{2,1,0:T(8,128)(2,1)S(1)}, u32[]{:S(2)}, u32[]{:S(2)}) collective-permute-start(bf16[4,32,256]{2,1,0:T(8,128)(2,1)S(1)} %get-tuple-element.86), channel_id=1, source_target_pairs={{0,8},{1,9},{2,10},{3,11},{4,12},{5,13},{6,14},{7,15},{8,0},{9,1},... | collective-permute-start | bytes 196616 | tf_op jit(solution)/shard_map/ppermute | solution.py:40
  94.5 6.0 %collective-permute-start.17 = (bf16[4,32,256]{2,1,0:T(8,128)(2,1)S(1)}, bf16[4,32,256]{2,1,0:T(8,128)(2,1)S(1)}, u32[]{:S(2)}, u32[]{:S(2)}) collective-permute-start(bf16[4,32,256]{2,1,0:T(8,128)(2,1)S(1)} %get-tuple-element.87), channel_id=1, source_target_pairs={{0,4},{1,5},{2,6},{3,7},{4,0},{5,1},{6,2},{7,3},{8,12},{9,13},{10,... | collective-permute-start | bytes 196616 | tf_op jit(solution)/shard_map/ppermute | solution.py:40
  95.7 5.9 %collective-permute-start.18 = (bf16[4,32,256]{2,1,0:T(8,128)(2,1)S(1)}, bf16[4,32,256]{2,1,0:T(8,128)(2,1)S(1)}, u32[]{:S(2)}, u32[]{:S(2)}) collective-permute-start(bf16[4,32,256]{2,1,0:T(8,128)(2,1)S(1)} %get-tuple-element.88), channel_id=1, source_target_pairs={{0,9},{1,8},{2,11},{3,10},{4,13},{5,12},{6,15},{7,14},{8,1},{9,0},... | collective-permute-start | bytes 196616 | tf_op jit(solution)/shard_map/ppermute | solution.py:40
  95.7 7.2 %collective-permute-start.19 = (bf16[4,32,256]{2,1,0:T(8,128)(2,1)S(1)}, bf16[4,32,256]{2,1,0:T(8,128)(2,1)S(1)}, u32[]{:S(2)}, u32[]{:S(2)}) collective-permute-start(bf16[4,32,256]{2,1,0:T(8,128)(2,1)S(1)} %get-tuple-element.89), channel_id=1, source_target_pairs={{0,1},{1,0},{2,3},{3,2},{4,5},{5,4},{6,7},{7,6},{8,9},{9,8},{10,11... | collective-permute-start | bytes 196616 | tf_op jit(solution)/shard_map/ppermute | solution.py:40
  98.1 7.5 %collective-permute-start.20 = (bf16[4,32,256]{2,1,0:T(8,128)(2,1)S(1)}, bf16[4,32,256]{2,1,0:T(8,128)(2,1)S(1)}, u32[]{:S(2)}, u32[]{:S(2)}) collective-permute-start(bf16[4,32,256]{2,1,0:T(8,128)(2,1)S(1)} %get-tuple-element.90), channel_id=1, source_target_pairs={{0,10},{1,11},{2,8},{3,9},{4,14},{5,15},{6,12},{7,13},{8,2},{9,3},... | collective-permute-start | bytes 196616 | tf_op jit(solution)/shard_map/ppermute | solution.py:40
  100.5 7.4 %collective-permute-start.21 = (bf16[4,32,256]{2,1,0:T(8,128)(2,1)S(1)}, bf16[4,32,256]{2,1,0:T(8,128)(2,1)S(1)}, u32[]{:S(2)}, u32[]{:S(2)}) collective-permute-start(bf16[4,32,256]{2,1,0:T(8,128)(2,1)S(1)} %get-tuple-element.91), channel_id=1, source_target_pairs={{0,5},{1,4},{2,7},{3,6},{4,1},{5,0},{6,3},{7,2},{8,13},{9,12},{10,... | collective-permute-start | bytes 196616 | tf_op jit(solution)/shard_map/ppermute | solution.py:40
  101.7 8.1 %collective-permute-start.22 = (bf16[4,32,256]{2,1,0:T(8,128)(2,1)S(1)}, bf16[4,32,256]{2,1,0:T(8,128)(2,1)S(1)}, u32[]{:S(2)}, u32[]{:S(2)}) collective-permute-start(bf16[4,32,256]{2,1,0:T(8,128)(2,1)S(1)} %get-tuple-element.92), channel_id=1, source_target_pairs={{0,11},{1,10},{2,9},{3,8},{4,15},{5,14},{6,13},{7,12},{8,3},{9,2},... | collective-permute-start | bytes 196616 | tf_op jit(solution)/shard_map/ppermute | solution.py:40
  103.0 6.7 %collective-permute-start.23 = (bf16[4,32,256]{2,1,0:T(8,128)(2,1)S(1)}, bf16[4,32,256]{2,1,0:T(8,128)(2,1)S(1)}, u32[]{:S(2)}, u32[]{:S(2)}) collective-permute-start(bf16[4,32,256]{2,1,0:T(8,128)(2,1)S(1)} %get-tuple-element.93), channel_id=1, source_target_pairs={{0,2},{1,3},{2,0},{3,1},{4,6},{5,7},{6,4},{7,5},{8,10},{9,11},{10,... | collective-permute-start | bytes 196616 | tf_op jit(solution)/shard_map/ppermute | solution.py:40
  105.6 6.2 %collective-permute-start.24 = (bf16[4,32,256]{2,1,0:T(8,128)(2,1)S(1)}, bf16[4,32,256]{2,1,0:T(8,128)(2,1)S(1)}, u32[]{:S(2)}, u32[]{:S(2)}) collective-permute-start(bf16[4,32,256]{2,1,0:T(8,128)(2,1)S(1)} %get-tuple-element.94), channel_id=1, source_target_pairs={{0,12},{1,13},{2,14},{3,15},{4,8},{5,9},{6,10},{7,11},{8,4},{9,5},... | collective-permute-start | bytes 196616 | tf_op jit(solution)/shard_map/ppermute | solution.py:40
  107.9 22.9 %collective-permute-start.47 = (bf16[32,64,64]{2,1,0:T(8,128)(2,1)S(1)}, bf16[32,64,64]{2,1,0:T(8,128)(2,1)S(1)}, u32[]{:S(2)}, u32[]{:S(2)}) collective-permute-start(bf16[32,64,64]{2,1,0:T(8,128)(2,1)S(1)} %get-tuple-element.113.right_ref), channel_id=1, source_target_pairs={{0,16},{16,0},{1,17},{17,1},{2,18},{18,2},{3,19},{19,3},{4,20},{20... | collective-permute-start | bytes 786440 | tf_op jit(solution)/shard_map/ppermute | solution.py:33
  109.7 6.6 %collective-permute-start.25 = (bf16[4,32,256]{2,1,0:T(8,128)(2,1)S(1)}, bf16[4,32,256]{2,1,0:T(8,128)(2,1)S(1)}, u32[]{:S(2)}, u32[]{:S(2)}) collective-permute-start(bf16[4,32,256]{2,1,0:T(8,128)(2,1)S(1)} %get-tuple-element.95), channel_id=1, source_target_pairs={{0,6},{1,7},{2,4},{3,5},{4,2},{5,3},{6,0},{7,1},{8,14},{9,15},{10,... | collective-permute-start | bytes 196616 | tf_op jit(solution)/shard_map/ppermute | solution.py:40
  109.7 7.3 %collective-permute-start.26 = (bf16[4,32,256]{2,1,0:T(8,128)(2,1)S(1)}, bf16[4,32,256]{2,1,0:T(8,128)(2,1)S(1)}, u32[]{:S(2)}, u32[]{:S(2)}) collective-permute-start(bf16[4,32,256]{2,1,0:T(8,128)(2,1)S(1)} %get-tuple-element.96), channel_id=1, source_target_pairs={{0,13},{1,12},{2,15},{3,14},{4,9},{5,8},{6,11},{7,10},{8,5},{9,4},... | collective-permute-start | bytes 196616 | tf_op jit(solution)/shard_map/ppermute | solution.py:40
  111.8 6.1 %collective-permute-start.27 = (bf16[4,32,256]{2,1,0:T(8,128)(2,1)S(1)}, bf16[4,32,256]{2,1,0:T(8,128)(2,1)S(1)}, u32[]{:S(2)}, u32[]{:S(2)}) collective-permute-start(bf16[4,32,256]{2,1,0:T(8,128)(2,1)S(1)} %get-tuple-element.97), channel_id=1, source_target_pairs={{0,3},{1,2},{2,1},{3,0},{4,7},{5,6},{6,5},{7,4},{8,11},{9,10},{10,... | collective-permute-start | bytes 196616 | tf_op jit(solution)/shard_map/ppermute | solution.py:40
  116.3 7.0 %collective-permute-start.28 = (bf16[4,32,256]{2,1,0:T(8,128)(2,1)S(1)}, bf16[4,32,256]{2,1,0:T(8,128)(2,1)S(1)}, u32[]{:S(2)}, u32[]{:S(2)}) collective-permute-start(bf16[4,32,256]{2,1,0:T(8,128)(2,1)S(1)} %get-tuple-element.98), channel_id=1, source_target_pairs={{0,14},{1,15},{2,12},{3,13},{4,10},{5,11},{6,8},{7,9},{8,6},{9,7},... | collective-permute-start | bytes 196616 | tf_op jit(solution)/shard_map/ppermute | solution.py:40
  117.0 6.3 %collective-permute-start.29 = (bf16[4,32,256]{2,1,0:T(8,128)(2,1)S(1)}, bf16[4,32,256]{2,1,0:T(8,128)(2,1)S(1)}, u32[]{:S(2)}, u32[]{:S(2)}) collective-permute-start(bf16[4,32,256]{2,1,0:T(8,128)(2,1)S(1)} %get-tuple-element.99), channel_id=1, source_target_pairs={{0,7},{1,6},{2,5},{3,4},{4,3},{5,2},{6,1},{7,0},{8,15},{9,14},{10,... | collective-permute-start | bytes 196616 | tf_op jit(solution)/shard_map/ppermute | solution.py:40
  117.9 7.2 %collective-permute-start.30 = (bf16[4,32,256]{2,1,0:T(8,128)(2,1)S(1)}, bf16[4,32,256]{2,1,0:T(8,128)(2,1)S(1)}, u32[]{:S(2)}, u32[]{:S(2)}) collective-permute-start(bf16[4,32,256]{2,1,0:T(8,128)(2,1)S(1)} %get-tuple-element.100), channel_id=1, source_target_pairs={{0,15},{1,14},{2,13},{3,12},{4,11},{5,10},{6,9},{7,8},{8,7},{9,6},... | collective-permute-start | bytes 196616 | tf_op jit(solution)/shard_map/ppermute | solution.py:40
  (9 other events, 199.2 us)

commit v5 on v4

v5 whole, which is shorter than its diff:
```python
import functools

import jax
import jax.numpy as jnp
from jax import lax
from jax.experimental import pallas as pl
from jax.experimental.pallas import tpu as pltpu
from jax.sharding import PartitionSpec as P

BF16 = jnp.bfloat16
F32 = jnp.float32
MIB = 1024 * 1024


def swap_sequences(array):
    return lax.ppermute(array, "dp", [(0, 1), (1, 0)])


def after(array, earlier):
    return lax.optimization_barrier((array, earlier))[0]


def exchange(near, far):
    half = len(far)
    seq = 2 * half
    groups = [list(range(half)), list(range(half, seq))]
    near = lax.all_to_all(
        near, "seq", split_axis=0, concat_axis=0, axis_index_groups=groups, tiled=True
    )
    far = [
        lax.ppermute(block, "seq", [(i, i ^ (half + t)) for i in range(seq)])
        for t, block in enumerate(far)
    ]
    return near, far


def call(kernel, me, inputs, out_shapes, scratch=(), flops=0, unblocked=(), vmem=40):
    whole = pl.BlockSpec(memory_space=pltpu.VMEM)
    moved = sum(x.size * x.dtype.itemsize for x in (*inputs, *out_shapes))
    in_specs = [
        pl.BlockSpec(memory_space=pl.ANY) if n in unblocked else whole for n in range(len(inputs))
    ]
    return pl.pallas_call(
        kernel,
        out_shape=out_shapes,
        in_specs=[pl.BlockSpec(memory_space=pltpu.SMEM)] + in_specs,
        out_specs=[whole] * len(out_shapes),
        scratch_shapes=scratch,
        compiler_params=pltpu.CompilerParams(vmem_limit_bytes=vmem * MIB),
        cost_estimate=pl.CostEstimate(flops=flops, bytes_accessed=moved, transcendentals=0),
    )(me, *inputs)


def dot(a, b, contract):
    return lax.dot_general(a, b, (contract, ((), ())), preferred_element_type=F32)


def block_views(half, me, near_ref, far_refs):
    base = me // half * half
    near = [(base + p, near_ref.at[p]) for p in range(half)]
    return near + [(me ^ (half + t), far_refs[t]) for t in range(half)]


def send_kernel(half, me_ref, gate_hbm, cotangent_hbm, left_hbm, values_hbm, *refs):
    near_ref, far_refs = refs[0], refs[1 : half + 1]
    gate, cotangent, left, values, hold, sems = refs[half + 1 :]
    rows, seq, cols, channels = hold.shape
    me = me_ref[0]
    loads = []
    for i in range(rows):
        for n, (source, target) in enumerate(((left_hbm, left), (values_hbm, values))):
            loads.append(pltpu.make_async_copy(source.at[i], target.at[i], sems.at[n, i]))
    loads.append(pltpu.make_async_copy(gate_hbm, gate, sems.at[2, 0]))
    loads.append(pltpu.make_async_copy(cotangent_hbm, cotangent, sems.at[2, 1]))
    for load in loads:
        load.start()
    for i in range(rows):
        loads[2 * i].wait()
        loads[2 * i + 1].wait()
        mixed = dot(left[i], values[i], ((1,), (0,)))
        hold[i] = mixed.astype(BF16).reshape(seq, cols, channels)
    loads[-2].wait()
    loads[-1].wait()
    for c, ref in block_views(half, me, near_ref, far_refs):
        wide = gate[:, c].astype(F32) * cotangent[:, c].astype(F32)
        ref[0] = wide.astype(BF16)
        ref[1] = hold[:, c]


def load_columns(half, me, near_ref, far_refs, which, wide):
    rows, cols, channels = far_refs[0].shape[1:]
    size = rows * cols
    for c, ref in block_views(half, me, near_ref, far_refs):
        block = ref[which].reshape(size, channels).astype(F32)
        start = pl.multiple_of(c * size, size)
        for h in range(channels // 128):
            wide[h, pl.ds(start, size), :] = block[:, h * 128 : (h + 1) * 128]


def column(wide, k, count, cols):
    halves = [wide[h, pl.ds(k, count, stride=cols), :] for h in range(wide.shape[0])]
    return jnp.concatenate(halves, axis=1).astype(BF16)


def store_column(wide, k, count, cols, value):
    for h in range(wide.shape[0]):
        wide[h, pl.ds(k, count, stride=cols), :] = value[:, h * 128 : (h + 1) * 128]


def send_columns(half, me, wide, near_ref, far_refs):
    rows, cols, channels = far_refs[0].shape
    size = rows * cols
    for c, ref in block_views(half, me, near_ref, far_refs):
        start = pl.multiple_of(c * size, size)
        halves = [wide[h, pl.ds(start, size), :] for h in range(wide.shape[0])]
        block = jnp.concatenate(halves, axis=1).astype(BF16)
        ref[...] = block.reshape(rows, cols, channels)


def column_backward_kernel(half, me_ref, right_ref, near_ref, *refs):
    far_refs, near_out, far_out = refs[:half], refs[half], refs[half + 1 : 2 * half + 1]
    by_column_ref, wide, wide_out = refs[2 * half + 1 :]
    cols, count, _ = right_ref.shape
    me = me_ref[0]
    load_columns(half, me, near_ref, far_refs, 0, wide)
    for k in range(cols):
        grad = column(wide, k, count, cols)
        by_column_ref[k] = grad
        store_column(wide_out, k, count, cols, dot(right_ref[k], grad, ((0,), (0,))))
    send_columns(half, me, wide_out, near_out, far_out)


def column_forward_kernel(half, me_ref, right_ref, grad_ref, after_ref, near_ref, *refs):
    far_refs, near_out, far_out = refs[:half], refs[half], refs[half + 1 : 2 * half + 1]
    right_part_ref, wide, wide_out = refs[2 * half + 1 :]
    cols, count, _ = right_ref.shape
    me = me_ref[0]
    load_columns(half, me, near_ref, far_refs, 1, wide)
    for k in range(cols):
        mixed = column(wide, k, count, cols)
        store_column(wide_out, k, count, cols, dot(right_ref[k], mixed, ((1,), (0,))))
        right_part_ref[k] = dot(grad_ref[k], mixed, ((1,), (1,))).astype(BF16)
    send_columns(half, me, wide_out, near_out, far_out)


def gather_kernel(half, me_ref, near_ref, *refs):
    for c, ref in block_views(half, me_ref[0], near_ref, refs[:half]):
        refs[half][:, c] = ref[...]


def row_backward_kernel(me_ref, left_ref, values_ref, grad_ref, signal_ref, term_ref):
    for i in range(left_ref.shape[0]):
        grad = grad_ref[i]
        signal_ref[i] = dot(left_ref[i], grad, ((0,), (0,))).astype(BF16)
        term_ref[i] = dot(grad, values_ref[i], ((1,), (1,))).astype(BF16)


def factor_sum_kernel(
    me_ref, term_ref, values_ref, grad_ref, right_ref, other_ref, left_out_ref, right_out_ref
):
    for i in range(term_ref.shape[0]):
        other = dot(grad_ref[i], values_ref[i], ((1,), (1,))).astype(BF16)
        left_out_ref[i] = (term_ref[i].astype(F32) + other.astype(F32)).astype(BF16)
    right_out_ref[...] = (right_ref[...].astype(F32) + other_ref[...].astype(F32)).astype(BF16)


def output_kernel(half, me_ref, gate_ref, cotangent_ref, near_ref, *refs):
    far_refs, (out_ref, grad_ref) = refs[:half], refs[half:]
    for c, ref in block_views(half, me_ref[0], near_ref, far_refs):
        second = ref[...].astype(F32)
        out_ref[:, c] = (gate_ref[:, c].astype(F32) * second).astype(BF16)
        grad_ref[:, c] = (cotangent_ref[:, c].astype(F32) * second).astype(BF16)


def direct_shards(signal, gating, upstream, left_factor, right_factor):
    seq = lax.axis_size("seq")
    half = seq // 2
    rows, block_len = left_factor.shape[:2]
    cols, count = right_factor.shape[:2]
    channels = signal.shape[2]
    me = lax.axis_index("seq").astype(jnp.int32).reshape(1)
    values = signal.reshape(rows, block_len, channels)
    gate = gating.reshape(rows, seq, cols, channels)
    cotangent = upstream.reshape(rows, seq, cols, channels)

    def shape(*dims):
        return jax.ShapeDtypeStruct(dims, BF16)

    def with_half(kernel):
        return functools.partial(kernel, half)

    block = (rows, cols, channels)
    pairs = [shape(half, 2, *block)] + [shape(2, *block)] * half
    blocks = [shape(half, *block)] + [shape(*block)] * half
    whole = shape(rows, seq, cols, channels)
    by_row = shape(rows, block_len, channels)
    left = shape(*left_factor.shape)
    right = shape(*right_factor.shape)
    wide = pltpu.VMEM((channels // 128, count * cols, 128), F32)
    row_flops = 2 * rows * block_len * block_len * channels
    column_flops = 2 * cols * count * count * channels

    near, *far = call(
        with_half(send_kernel),
        me,
        [gate, cotangent, left_factor, values],
        pairs,
        [pltpu.VMEM(x.shape, BF16) for x in (gate, cotangent, left_factor, values, whole)]
        + [pltpu.SemaphoreType.DMA((3, max(rows, 2)))],
        row_flops,
        unblocked=range(4),
        vmem=60,
    )
    other_values = swap_sequences(after(values, near))
    near, far = exchange(near, far)
    *second_in, grad_column = call(
        with_half(column_backward_kernel),
        me,
        [right_factor, near, *far],
        blocks + [shape(cols, count, channels)],
        [wide, wide],
        column_flops,
    )
    back_near, *back_far = second_in
    second_near, *second_far, right_part = call(
        with_half(column_forward_kernel),
        me,
        [right_factor, grad_column, other_values, near, *far],
        blocks + [right],
        [wide, wide],
        2 * column_flops,
        unblocked=[2],
    )
    other_right = swap_sequences(right_part)
    back_far[half // 2 :] = [after(x, right_part) for x in back_far[half // 2 :]]
    back_near, back_far = exchange(back_near, back_far)
    (gathered,) = call(with_half(gather_kernel), me, [back_near, *back_far], [whole])
    grad_back = gathered.reshape(rows, block_len, channels)
    other_grad_back = swap_sequences(grad_back)
    grad_signal, left_term = call(
        row_backward_kernel,
        me,
        [left_factor, values, grad_back],
        [by_row, left],
        flops=2 * row_flops,
    )
    second_far[half // 2 :] = [after(x, left_term) for x in second_far[half // 2 :]]
    second_near, second_far = exchange(second_near, second_far)
    grad_left, grad_right = call(
        factor_sum_kernel,
        me,
        [left_term, other_values, other_grad_back, right_part, other_right],
        [left, right],
        flops=row_flops,
    )
    output, grad_gate = call(
        with_half(output_kernel), me, [gate, cotangent, second_near, *second_far], [whole, whole]
    )
    return (
        output.reshape(signal.shape),
        grad_gate.reshape(signal.shape),
        grad_signal.reshape(signal.shape),
        grad_left,
        grad_right,
    )


def plain_shards(signal, gating, upstream, left_factor, right_factor):
    seq = lax.axis_size("seq")
    rows, block_len = left_factor.shape[:2]
    cols, block_count = right_factor.shape[:2]
    channels = signal.shape[2]
    values = signal.reshape(rows, block_len, channels)
    gate = gating.reshape(rows, block_len, channels)
    cotangent = upstream.reshape(rows, block_len, channels)

    def einsum(spec, a, b):
        return jnp.einsum(spec, a, b, preferred_element_type=F32).astype(BF16)

    def all_to_all(blocks):
        return lax.all_to_all(blocks, "seq", split_axis=0, concat_axis=0, tiled=True)

    def to_columns(by_row):
        blocks = by_row.reshape(rows, seq, cols, channels).transpose(1, 0, 2, 3)
        return all_to_all(blocks).reshape(block_count, cols, channels)

    def to_rows(by_column):
        blocks = all_to_all(by_column.reshape(seq, rows, cols, channels))
        return blocks.transpose(1, 0, 2, 3).reshape(rows, block_len, channels)

    grad_rows = (cotangent.astype(F32) * gate.astype(F32)).astype(BF16)
    grad_column = to_columns(grad_rows)
    other_values = swap_sequences(values)
    mixed_column = to_columns(einsum("ikj,ijd->ikd", left_factor, values))
    grad_back = to_rows(einsum("kmi,mkd->ikd", right_factor, grad_column))
    second_rows = to_rows(einsum("kmi,ikd->mkd", right_factor, mixed_column))
    right_part = einsum("mkd,ikd->kmi", grad_column, mixed_column)
    other_right = swap_sequences(right_part)
    other_grad_back = swap_sequences(grad_back)
    grad_signal = einsum("ikj,ikd->ijd", left_factor, grad_back)
    left_term = einsum("ikd,ijd->ikj", grad_back, values)
    other_left = einsum("ikd,ijd->ikj", other_grad_back, other_values)
    grad_left = (left_term.astype(F32) + other_left.astype(F32)).astype(BF16)
    grad_right = (right_part.astype(F32) + other_right.astype(F32)).astype(BF16)
    wide = second_rows.astype(F32)
    output = (gate.astype(F32) * wide).astype(BF16)
    grad_gate = (cotangent.astype(F32) * wide).astype(BF16)
    return (
        output.reshape(signal.shape),
        grad_gate.reshape(signal.shape),
        grad_signal.reshape(signal.shape),
        grad_left,
        grad_right,
    )


def shards(signal, gating, upstream, left_factor, right_factor):
    seq = lax.axis_size("seq")
    cols = right_factor.shape[0]
    direct = seq <= 16 and seq & (seq - 1) == 0 and cols % 32 == 0
    run = direct_shards if direct else plain_shards
    return run(signal, gating, upstream, left_factor, right_factor)


def solution(mesh):
    by_position = P("dp", "seq", None)
    by_block = P("seq", None, None)
    return jax.shard_map(
        shards,
        mesh=mesh,
        in_specs=(by_position,) * 3 + (by_block,) * 2,
        out_specs=(by_position,) * 3 + (by_block,) * 2,
        check_vma=False,
    )
```

time: 133 us -> 174 us (1.31); the launches traced: 133 us -> 172 us
  local copies, waits for them, and re-layouts: 3.74 us -> 39.3 us
  waiting for transfers between devices: 29.5 us -> 19.9 us
  starting transfers between devices: 82.5 us -> 90.6 us
  Pallas kernels: 16.7 us -> 21 us
    unnamed x18 -> x126, local copies, waits for them, and re-layouts: 3.74 us -> 39.3 us
    all_to_all x0 -> x3, starting transfers between devices: none -> 17.5 us  [exchange(): lax.all_to_all(near, 'seq', split_axis=0, concat_axis=0, axis_index_group...]
    ppermute x45 -> x24, waiting for transfers between devices: 29.5 us -> 19.9 us  [exchange(): lax.ppermute(block, 'seq', [(i, i ^ half + t) for i in range(seq)])]
    ppermute x45 -> x24, starting transfers between devices: 77.4 us -> 69.3 us  [exchange(): lax.ppermute(block, 'seq', [(i, i ^ half + t) for i in range(seq)])]
    pallas_call x7, Pallas kernels: 16.7 us -> 21 us  [call(): pl.pallas_call(kernel, out_shape=out_shapes, in_specs=[pl.BlockSpec(memor...]
  transfers between devices with their start and end apart: 48 -> 30, of which waited for: 15 -> 9; matrix products, arithmetic and copies ran while one was open for 0% -> 0% of each run, Pallas kernels for 11% -> 7%
where the time goes in v5:
time: 174 us; the launch traced here: 172 us
  starting transfers between devices  90.6 us (52%)
  local copies, waits for them, and re-layouts  39.3 us (23%)
  Pallas kernels  21 us (12%)
  waiting for transfers between devices  19.9 us (11%)
    ppermute x24, starting transfers between devices, exchange(): lax.ppermute(block, 'seq', [(i, i ^ half + t) for i in range(seq)])  69.3 us
    unnamed x126, local copies, waits for them, and re-layouts  39.3 us
    pallas_call x7, Pallas kernels, call(): pl.pallas_call(kernel, out_shape=out_shapes, in_specs=[pl.BlockSpec(memor...  21 us
    ppermute x24, waiting for transfers between devices, exchange(): lax.ppermute(block, 'seq', [(i, i ^ half + t) for i in range(seq)])  19.9 us
    all_to_all x3, starting transfers between devices, exchange(): lax.all_to_all(near, 'seq', split_axis=0, concat_axis=0, axis_index_group...  17.5 us
    ppermute x3, starting transfers between devices, swap_sequences(): return lax.ppermute(array, 'dp', [(0, 1), (1, 0)])  3.71 us
  transfers between devices with their start and end apart: 30, of which 9 were waited for; matrix products, arithmetic and copies ran while one was open for 0% of the time, Pallas kernels for 7%

profile of v5, /device:TPU:0, one launch (start us, length us, event | category | flops | bytes accessed | tf_op | source)
XLA Modules:
  0.0 171.6 jit_solution(15005094254268616208)
XLA Ops:
  0.6 4.3 %shard_map.92 = (bf16[8,2,4,32,256]{4,3,2,1,0:T(8,128)(2,1)}, bf16[2,4,32,256]{3,2,1,0:T(8,128)(2,1)}, bf16[2,4,32,256]{3,2,1,0:T(8,128)(2,1)}, bf16[2,4,32,256]...) custom-call(s32[1]{0:T(128)} %bitcast.me_ref, ...), custom_call_target="tpu_custom_call" | custom-call | flops 536870912 | bytes 7340032 | tf_op jit(solution)/shard_map/pallas_call | solution.py:43
  5.0 5.4 %all-to-all-start = ((bf16[8,2,4,32,256]{4,3,2,1,0:T(8,128)(2,1)}), bf16[8,2,4,32,256]{4,3,2,1,0:T(8,128)(2,1)S(1)}, u32[]{:S(2)}, u32[]{:S(2)}) async-start(bf16[8,2,4,32,256]{4,3,2,1,0:T(8,128)(2,1)} %get-tuple-element.49), calls=%async_computation | async-start | bytes 2097152 | tf_op jit(solution)/shard_map/all_to_all | solution.py:27
  10.4 1.6 collective-permute-start.8
  12.0 2.6 %collective-permute-start = (bf16[2,4,32,256]{3,2,1,0:T(8,128)(2,1)}, bf16[2,4,32,256]{3,2,1,0:T(8,128)(2,1)S(1)}, u32[]{:S(2)}, u32[]{:S(2)}) collective-permute-start(bf16[2,4,32,256]{3,2,1,0:T(8,128)(2,1)} %get-tuple-element.50), channel_id=1, source_target_pairs={{0,8},{1,9},{2,10},{3,11},{4,12},{5,13},{6,14},{7,15},{8,0},{9,1},... | collective-permute-start | bytes 393224 | tf_op jit(solution)/shard_map/ppermute | solution.py:31
  14.5 3.5 %collective-permute-start.2 = (bf16[2,4,32,256]{3,2,1,0:T(8,128)(2,1)}, bf16[2,4,32,256]{3,2,1,0:T(8,128)(2,1)S(1)}, u32[]{:S(2)}, u32[]{:S(2)}) collective-permute-start(bf16[2,4,32,256]{3,2,1,0:T(8,128)(2,1)} %get-tuple-element.52), channel_id=1, source_target_pairs={{0,10},{1,11},{2,8},{3,9},{4,14},{5,15},{6,12},{7,13},{8,2},{9,3},... | collective-permute-start | bytes 393224 | tf_op jit(solution)/shard_map/ppermute | solution.py:31
  18.6 7.3 %collective-permute-done.refs_0_ = bf16[2,4,32,256]{3,2,1,0:T(8,128)(2,1)S(1)} collective-permute-done((bf16[2,4,32,256]{3,2,1,0:T(8,128)(2,1)}, bf16[2,4,32,256]{3,2,1,0:T(8,128)(2,1)S(1)}, u32[]{:S(2)}, u32[]{:S(2)}) %collective-permute-start) | collective-permute-done | bytes 131104 | tf_op jit(solution)/shard_map/ppermute | solution.py:31
  25.9 3.9 %collective-permute-start.4 = (bf16[2,4,32,256]{3,2,1,0:T(8,128)(2,1)}, bf16[2,4,32,256]{3,2,1,0:T(8,128)(2,1)S(1)}, u32[]{:S(2)}, u32[]{:S(2)}) collective-permute-start(bf16[2,4,32,256]{3,2,1,0:T(8,128)(2,1)} %get-tuple-element.54), channel_id=1, source_target_pairs={{0,12},{1,13},{2,14},{3,15},{4,8},{5,9},{6,10},{7,11},{8,4},{9,5},... | collective-permute-start | bytes 393224 | tf_op jit(solution)/shard_map/ppermute | solution.py:31
  29.9 1.6 collective-permute-start.5
  31.5 16.7 %collective-permute-start.6 = (bf16[2,4,32,256]{3,2,1,0:T(8,128)(2,1)}, bf16[2,4,32,256]{3,2,1,0:T(8,128)(2,1)S(1)}, u32[]{:S(2)}, u32[]{:S(2)}) collective-permute-start(bf16[2,4,32,256]{3,2,1,0:T(8,128)(2,1)} %get-tuple-element.56), channel_id=1, source_target_pairs={{0,14},{1,15},{2,12},{3,13},{4,10},{5,11},{6,8},{7,9},{8,6},{9,7},... | collective-permute-start | bytes 393224 | tf_op jit(solution)/shard_map/ppermute | solution.py:31
  48.9 2.2 %collective-permute-start.7 = (bf16[2,4,32,256]{3,2,1,0:T(8,128)(2,1)}, bf16[2,4,32,256]{3,2,1,0:T(8,128)(2,1)S(1)}, u32[]{:S(2)}, u32[]{:S(2)}) collective-permute-start(bf16[2,4,32,256]{3,2,1,0:T(8,128)(2,1)} %get-tuple-element.57), channel_id=1, source_target_pairs={{0,15},{1,14},{2,13},{3,12},{4,11},{5,10},{6,9},{7,8},{8,7},{9,6},... | collective-permute-start | bytes 393224 | tf_op jit(solution)/shard_map/ppermute | solution.py:31
  53.1 3.1 %collective-permute-done.7.refs_7_ = bf16[2,4,32,256]{3,2,1,0:T(8,128)(2,1)S(1)} collective-permute-done((bf16[2,4,32,256]{3,2,1,0:T(8,128)(2,1)}, bf16[2,4,32,256]{3,2,1,0:T(8,128)(2,1)S(1)}, u32[]{:S(2)}, u32[]{:S(2)}) %collective-permute-start.7) | collective-permute-done | bytes 131104 | tf_op jit(solution)/shard_map/ppermute | solution.py:31
  56.8 1.0 copy-done.9
  57.9 0.9 copy-done.14
  58.8 0.9 copy-done.17
  59.7 0.9 copy-done.20
  60.6 0.9 copy-done.23
  62.4 2.9 %shard_map.93 = (bf16[8,4,32,256]{3,2,1,0:T(8,128)(2,1)S(1)}, bf16[4,32,256]{2,1,0:T(8,128)(2,1)S(1)}, bf16[4,32,256]{2,1,0:T(8,128)(2,1)S(1)}, bf16[4,32,256]{2...) custom-call(s32[1]{0:T(128)} %bitcast.me_ref, ...), custom_call_target="tpu_custom_call" | custom-call | flops 67108864 | bytes 4456448 | tf_op jit(solution)/shard_map/pallas_call | solution.py:43
  65.3 1.0 copy-done.11
  72.0 7.8 %all-to-all-start.2 = ((bf16[8,4,32,256]{3,2,1,0:T(8,128)(2,1)}), bf16[8,4,32,256]{3,2,1,0:T(8,128)(2,1)}, u32[]{:S(2)}, u32[]{:S(2)}) async-start(bf16[8,4,32,256]{3,2,1,0:T(8,128)(2,1)} %copy-done.29), calls=%async_computation.2 | async-start | bytes 1048576 | tf_op jit(solution)/shard_map/all_to_all | solution.py:27
  79.8 1.4 copy-done.10
  81.3 1.2 copy-done.12
  86.1 0.9 copy-done.27
  87.1 3.8 %shard_map.94 = (bf16[8,4,32,256]{3,2,1,0:T(8,128)(2,1)S(1)}, bf16[4,32,256]{2,1,0:T(8,128)(2,1)S(1)}, bf16[4,32,256]{2,1,0:T(8,128)(2,1)S(1)}, bf16[4,32,256]{2...) custom-call(s32[1]{0:T(128)} %bitcast.me_ref, ...), custom_call_target="tpu_custom_call" | custom-call | flops 134217728 | bytes 5767168 | tf_op jit(solution)/shard_map/pallas_call | solution.py:43
  95.6 5.0 %collective-permute-start.17 = (bf16[4,32,256]{2,1,0:T(8,128)(2,1)S(1)}, bf16[4,32,256]{2,1,0:T(8,128)(2,1)S(1)}, u32[]{:S(2)}, u32[]{:S(2)}) collective-permute-start(bf16[4,32,256]{2,1,0:T(8,128)(2,1)S(1)} %copy-done.62), channel_id=1, source_target_pairs={{0,12},{1,13},{2,14},{3,15},{4,8},{5,9},{6,10},{7,11},{8,4},{9,5},... | collective-permute-start | bytes 196616 | tf_op jit(solution)/shard_map/ppermute | solution.py:31
  100.5 4.2 %collective-permute-start.19 = (bf16[4,32,256]{2,1,0:T(8,128)(2,1)S(1)}, bf16[4,32,256]{2,1,0:T(8,128)(2,1)S(1)}, u32[]{:S(2)}, u32[]{:S(2)}) collective-permute-start(bf16[4,32,256]{2,1,0:T(8,128)(2,1)S(1)} %copy-done.58), channel_id=1, source_target_pairs={{0,14},{1,15},{2,12},{3,13},{4,10},{5,11},{6,8},{7,9},{8,6},{9,7},... | collective-permute-start | bytes 196616 | tf_op jit(solution)/shard_map/ppermute | solution.py:31
  105.1 2.6 %collective-permute-start.14 = (bf16[4,32,256]{2,1,0:T(8,128)(2,1)S(1)}, bf16[4,32,256]{2,1,0:T(8,128)(2,1)S(1)}, u32[]{:S(2)}, u32[]{:S(2)}) collective-permute-start(bf16[4,32,256]{2,1,0:T(8,128)(2,1)S(1)} %copy-done.52), channel_id=1, source_target_pairs={{0,9},{1,8},{2,11},{3,10},{4,13},{5,12},{6,15},{7,14},{8,1},{9,0},... | collective-permute-start | bytes 196616 | tf_op jit(solution)/shard_map/ppermute | solution.py:31
  107.7 1.3 collective-permute-start.15
  109.1 7.3 %collective-permute-start.16 = (bf16[4,32,256]{2,1,0:T(8,128)(2,1)S(1)}, bf16[4,32,256]{2,1,0:T(8,128)(2,1)S(1)}, u32[]{:S(2)}, u32[]{:S(2)}) collective-permute-start(bf16[4,32,256]{2,1,0:T(8,128)(2,1)S(1)} %copy-done.48), channel_id=1, source_target_pairs={{0,11},{1,10},{2,9},{3,8},{4,15},{5,14},{6,13},{7,12},{8,3},{9,2},... | collective-permute-start | bytes 196616 | tf_op jit(solution)/shard_map/ppermute | solution.py:31
  118.1 4.8 %collective-permute-done.15.refs_2_ = bf16[4,32,256]{2,1,0:T(8,128)(2,1)S(1)} collective-permute-done((bf16[4,32,256]{2,1,0:T(8,128)(2,1)S(1)}, bf16[4,32,256]{2,1,0:T(8,128)(2,1)S(1)}, u32[]{:S(2)}, u32[]{:S(2)}) %collective-permute-start.15) | collective-permute-done | bytes 65568 | tf_op jit(solution)/shard_map/ppermute | solution.py:31
  125.9 1.1 shard_map.95
  127.6 4.3 %all-to-all-start.1 = ((bf16[8,4,32,256]{3,2,1,0:T(8,128)(2,1)}), bf16[8,4,32,256]{3,2,1,0:T(8,128)(2,1)}, u32[]{:S(2)}, u32[]{:S(2)}) async-start(bf16[8,4,32,256]{3,2,1,0:T(8,128)(2,1)} %copy-done.28), calls=%async_computation.1 | async-start | bytes 1048576 | tf_op jit(solution)/shard_map/all_to_all | solution.py:27
  132.0 1.6 collective-permute-start.26
  134.1 1.5 collective-permute-start.10
  135.6 2.1 %collective-permute-start.11 = (bf16[4,32,256]{2,1,0:T(8,128)(2,1)}, bf16[4,32,256]{2,1,0:T(8,128)(2,1)S(1)}, u32[]{:S(2)}, u32[]{:S(2)}) collective-permute-start(bf16[4,32,256]{2,1,0:T(8,128)(2,1)} %copy-done.44), channel_id=1, source_target_pairs={{0,10},{1,11},{2,8},{3,9},{4,14},{5,15},{6,12},{7,13},{8,2},{9,3},... | collective-permute-start | bytes 196616 | tf_op jit(solution)/shard_map/ppermute | solution.py:31
  137.7 1.2 copy-done.2
  138.9 2.2 %shard_map.96 = (bf16[4,512,256]{2,1,0:T(8,128)(2,1)}, bf16[4,512,512]{2,1,0:T(8,128)(2,1)S(1)}) custom-call(s32[1]{0:T(128)} %bitcast.me_ref, bf16[4,512,512]{2,1,0:T(8,128)(2,1)S(1)} %copy-done, bf16[4,512,256]{2,1,0:T(8,128)(2,1)S(1)} %bitcast.12, bf16[4,512,256]{2,1,0:T(8,128)(2,1)S(1)} %bitcast.9), custom_call_target="tpu_custom_call" | custom-call | flops 1073741824 | bytes 7340032 | tf_op jit(solution)/shard_map/pallas_call | solution.py:43
  141.2 1.3 copy-done.7
  142.5 2.1 %collective-permute-start.12 = (bf16[4,32,256]{2,1,0:T(8,128)(2,1)S(1)}, bf16[4,32,256]{2,1,0:T(8,128)(2,1)S(1)}, u32[]{:S(2)}, u32[]{:S(2)}) collective-permute-start(bf16[4,32,256]{2,1,0:T(8,128)(2,1)S(1)} %copy-done.43), channel_id=1, source_target_pairs={{0,11},{1,10},{2,9},{3,8},{4,15},{5,14},{6,13},{7,12},{8,3},{9,2},... | collective-permute-start | bytes 196616 | tf_op jit(solution)/shard_map/ppermute | solution.py:31
  144.6 2.9 %collective-permute-start.21 = (bf16[4,32,256]{2,1,0:T(8,128)(2,1)S(1)}, bf16[4,32,256]{2,1,0:T(8,128)(2,1)S(1)}, u32[]{:S(2)}, u32[]{:S(2)}) collective-permute-start(bf16[4,32,256]{2,1,0:T(8,128)(2,1)S(1)} %copy-done.41), channel_id=1, source_target_pairs={{0,12},{1,13},{2,14},{3,15},{4,8},{5,9},{6,10},{7,11},{8,4},{9,5},... | collective-permute-start | bytes 196616 | tf_op jit(solution)/shard_map/ppermute | solution.py:31
  147.5 1.4 collective-permute-start.22
  148.8 3.8 %collective-permute-start.23 = (bf16[4,32,256]{2,1,0:T(8,128)(2,1)}, bf16[4,32,256]{2,1,0:T(8,128)(2,1)S(1)}, u32[]{:S(2)}, u32[]{:S(2)}) collective-permute-start(bf16[4,32,256]{2,1,0:T(8,128)(2,1)} %get-tuple-element.85), channel_id=1, source_target_pairs={{0,14},{1,15},{2,12},{3,13},{4,10},{5,11},{6,8},{7,9},{8,6},{9,7},... | collective-permute-start | bytes 196616 | tf_op jit(solution)/shard_map/ppermute | solution.py:31
  152.6 3.2 %collective-permute-start.24 = (bf16[4,32,256]{2,1,0:T(8,128)(2,1)}, bf16[4,32,256]{2,1,0:T(8,128)(2,1)S(1)}, u32[]{:S(2)}, u32[]{:S(2)}) collective-permute-start(bf16[4,32,256]{2,1,0:T(8,128)(2,1)} %get-tuple-element.87), channel_id=1, source_target_pairs={{0,15},{1,14},{2,13},{3,12},{4,11},{5,10},{6,9},{7,8},{8,7},{9,6},... | collective-permute-start | bytes 196616 | tf_op jit(solution)/shard_map/ppermute | solution.py:31
  156.7 2.5 %collective-permute-done.24.refs_7_ = bf16[4,32,256]{2,1,0:T(8,128)(2,1)S(1)} collective-permute-done((bf16[4,32,256]{2,1,0:T(8,128)(2,1)}, bf16[4,32,256]{2,1,0:T(8,128)(2,1)S(1)}, u32[]{:S(2)}, u32[]{:S(2)}) %collective-permute-start.24) | collective-permute-done | bytes 65568 | tf_op jit(solution)/shard_map/ppermute | solution.py:31
  159.9 1.2 copy-done.5
  161.1 1.2 copy-done.6
  164.0 2.9 %shard_map.97 = (bf16[4,16,32,256]{3,2,1,0:T(8,128)(2,1)}, bf16[4,16,32,256]{3,2,1,0:T(8,128)(2,1)}) custom-call(s32[1]{0:T(128)} %bitcast.me_ref, bf16[4,16,32,256]{3,2,1,0:T(8,128)(2,1)S(1)} %bitcast.14, bf16[4,16,32,256]{3,2,1,0:T(8,128)(2,1)S(1)} %bitcast.16, bf16[8,4,32,256]{3,2,1,0:T(8,128)(2,1)} %all-to-all-done.1.near_ref, ...), custom_call_target="tpu_custom_call" | custom-call | bytes 5242880 | tf_op jit(solution)/shard_map/pallas_call | solution.py:43
  167.0 1.0 copy-done.31
  168.0 3.6 %shard_map.98 = (bf16[4,512,512]{2,1,0:T(8,128)(2,1)}, bf16[32,64,64]{2,1,0:T(8,128)(2,1)}) custom-call(s32[1]{0:T(128)} %bitcast.me_ref, bf16[4,512,512]{2,1,0:T(8,128)(2,1)S(1)} %copy-done.8, bf16[4,512,256]{2,1,0:T(8,128)(2,1)S(1)} %copy-done.4, bf16[4,512,256]{2,1,0:T(8,128)(2,1)} %collective-permute-done.25.grad_ref, ...), custom_call_target="tpu_custom_call" | custom-call | flops 536870912 | bytes 7077888 | tf_op jit(solution)/shard_map/pallas_call | solution.py:43
  (145 shorter events, 28.5 us)
Async XLA Ops:
  5.0 5.4 %copy-start.1 = (bf16[1,2048,256]{2,1,0:T(8,128)(2,1)S(1)}, bf16[1,2048,256]{2,1,0:T(8,128)(2,1)}, u32[]{:S(2)}) copy-start(bf16[1,2048,256]{2,1,0:T(8,128)(2,1)} %param.5) | copy-start | bytes 3145732
  5.0 51.8 %all-to-all-start = ((bf16[8,2,4,32,256]{4,3,2,1,0:T(8,128)(2,1)}), bf16[8,2,4,32,256]{4,3,2,1,0:T(8,128)(2,1)S(1)}, u32[]{:S(2)}, u32[]{:S(2)}) async-start(bf16[8,2,4,32,256]{4,3,2,1,0:T(8,128)(2,1)} %get-tuple-element.49), calls=%async_computation | async-start | bytes 2097152 | tf_op jit(solution)/shard_map/all_to_all | solution.py:27
  10.4 69.4 %collective-permute-start.8 = (bf16[4,512,256]{2,1,0:T(8,128)(2,1)S(1)}, bf16[4,512,256]{2,1,0:T(8,128)(2,1)S(1)}, u32[]{:S(2)}, u32[]{:S(2)}) collective-permute-start(bf16[4,512,256]{2,1,0:T(8,128)(2,1)S(1)} %bitcast.11), channel_id=1, source_target_pairs={{0,16},{16,0},{1,17},{17,1},{2,18},{18,2},{3,19},{19,3},{4,20},{20... | collective-permute-start | bytes 3145736 | tf_op jit(solution)/shard_map/ppermute | solution.py:16
  12.0 14.0 %collective-permute-start = (bf16[2,4,32,256]{3,2,1,0:T(8,128)(2,1)}, bf16[2,4,32,256]{3,2,1,0:T(8,128)(2,1)S(1)}, u32[]{:S(2)}, u32[]{:S(2)}) collective-permute-start(bf16[2,4,32,256]{3,2,1,0:T(8,128)(2,1)} %get-tuple-element.50), channel_id=1, source_target_pairs={{0,8},{1,9},{2,10},{3,11},{4,12},{5,13},{6,14},{7,15},{8,0},{9,1},... | collective-permute-start | bytes 393224 | tf_op jit(solution)/shard_map/ppermute | solution.py:31
  14.5 15.3 %collective-permute-start.1 = (bf16[2,4,32,256]{3,2,1,0:T(8,128)(2,1)}, bf16[2,4,32,256]{3,2,1,0:T(8,128)(2,1)S(1)}, u32[]{:S(2)}, u32[]{:S(2)}) collective-permute-start(bf16[2,4,32,256]{3,2,1,0:T(8,128)(2,1)} %get-tuple-element.51), channel_id=1, source_target_pairs={{0,9},{1,8},{2,11},{3,10},{4,13},{5,12},{6,15},{7,14},{8,1},{9,0},... | collective-permute-start | bytes 393224 | tf_op jit(solution)/shard_map/ppermute | solution.py:31
  14.5 17.0 %collective-permute-start.2 = (bf16[2,4,32,256]{3,2,1,0:T(8,128)(2,1)}, bf16[2,4,32,256]{3,2,1,0:T(8,128)(2,1)S(1)}, u32[]{:S(2)}, u32[]{:S(2)}) collective-permute-start(bf16[2,4,32,256]{3,2,1,0:T(8,128)(2,1)} %get-tuple-element.52), channel_id=1, source_target_pairs={{0,10},{1,11},{2,8},{3,9},{4,14},{5,15},{6,12},{7,13},{8,2},{9,3},... | collective-permute-start | bytes 393224 | tf_op jit(solution)/shard_map/ppermute | solution.py:31
  18.1 30.1 %collective-permute-start.3 = (bf16[2,4,32,256]{3,2,1,0:T(8,128)(2,1)}, bf16[2,4,32,256]{3,2,1,0:T(8,128)(2,1)S(1)}, u32[]{:S(2)}, u32[]{:S(2)}) collective-permute-start(bf16[2,4,32,256]{3,2,1,0:T(8,128)(2,1)} %get-tuple-element.53), channel_id=1, source_target_pairs={{0,11},{1,10},{2,9},{3,8},{4,15},{5,14},{6,13},{7,12},{8,3},{9,2},... | collective-permute-start | bytes 393224 | tf_op jit(solution)/shard_map/ppermute | solution.py:31
  25.9 25.2 %collective-permute-start.4 = (bf16[2,4,32,256]{3,2,1,0:T(8,128)(2,1)}, bf16[2,4,32,256]{3,2,1,0:T(8,128)(2,1)S(1)}, u32[]{:S(2)}, u32[]{:S(2)}) collective-permute-start(bf16[2,4,32,256]{3,2,1,0:T(8,128)(2,1)} %get-tuple-element.54), channel_id=1, source_target_pairs={{0,12},{1,13},{2,14},{3,15},{4,8},{5,9},{6,10},{7,11},{8,4},{9,5},... | collective-permute-start | bytes 393224 | tf_op jit(solution)/shard_map/ppermute | solution.py:31
  29.9 21.9 %collective-permute-start.5 = (bf16[2,4,32,256]{3,2,1,0:T(8,128)(2,1)}, bf16[2,4,32,256]{3,2,1,0:T(8,128)(2,1)S(1)}, u32[]{:S(2)}, u32[]{:S(2)}) collective-permute-start(bf16[2,4,32,256]{3,2,1,0:T(8,128)(2,1)} %get-tuple-element.55), channel_id=1, source_target_pairs={{0,13},{1,12},{2,15},{3,14},{4,9},{5,8},{6,11},{7,10},{8,5},{9,4},... | collective-permute-start | bytes 393224 | tf_op jit(solution)/shard_map/ppermute | solution.py:31
  31.5 20.9 %collective-permute-start.6 = (bf16[2,4,32,256]{3,2,1,0:T(8,128)(2,1)}, bf16[2,4,32,256]{3,2,1,0:T(8,128)(2,1)S(1)}, u32[]{:S(2)}, u32[]{:S(2)}) collective-permute-start(bf16[2,4,32,256]{3,2,1,0:T(8,128)(2,1)} %get-tuple-element.56), channel_id=1, source_target_pairs={{0,14},{1,15},{2,12},{3,13},{4,10},{5,11},{6,8},{7,9},{8,6},{9,7},... | collective-permute-start | bytes 393224 | tf_op jit(solution)/shard_map/ppermute | solution.py:31
  48.9 7.3 %collective-permute-start.7 = (bf16[2,4,32,256]{3,2,1,0:T(8,128)(2,1)}, bf16[2,4,32,256]{3,2,1,0:T(8,128)(2,1)S(1)}, u32[]{:S(2)}, u32[]{:S(2)}) collective-permute-start(bf16[2,4,32,256]{3,2,1,0:T(8,128)(2,1)} %get-tuple-element.57), channel_id=1, source_target_pairs={{0,15},{1,14},{2,13},{3,12},{4,11},{5,10},{6,9},{7,8},{8,7},{9,6},... | collective-permute-start | bytes 393224 | tf_op jit(solution)/shard_map/ppermute | solution.py:31
  72.0 52.2 %all-to-all-start.2 = ((bf16[8,4,32,256]{3,2,1,0:T(8,128)(2,1)}), bf16[8,4,32,256]{3,2,1,0:T(8,128)(2,1)}, u32[]{:S(2)}, u32[]{:S(2)}) async-start(bf16[8,4,32,256]{3,2,1,0:T(8,128)(2,1)} %copy-done.29), calls=%async_computation.2 | async-start | bytes 1048576 | tf_op jit(solution)/shard_map/all_to_all | solution.py:27
  79.8 11.0 %copy-start.3 = (bf16[4,512,256]{2,1,0:T(8,128)(2,1)}, bf16[4,512,256]{2,1,0:T(8,128)(2,1)S(1)}, u32[]{:S(2)}) copy-start(bf16[4,512,256]{2,1,0:T(8,128)(2,1)S(1)} %collective-permute-done.8.after_ref.values_ref) | copy-start | bytes 3145732
  79.8 1.4 copy-start.10
  87.0 8.6 %copy-start.62 = (bf16[4,32,256]{2,1,0:T(8,128)(2,1)S(1)}, bf16[4,32,256]{2,1,0:T(8,128)(2,1)}, u32[]{:S(2)}) copy-start(bf16[4,32,256]{2,1,0:T(8,128)(2,1)} %copy-done.61) | copy-start | bytes 196612
  87.0 13.5 %copy-start.60 = (bf16[4,32,256]{2,1,0:T(8,128)(2,1)S(1)}, bf16[4,32,256]{2,1,0:T(8,128)(2,1)}, u32[]{:S(2)}) copy-start(bf16[4,32,256]{2,1,0:T(8,128)(2,1)} %copy-done.59) | copy-start | bytes 196612
  87.0 13.5 %copy-start.58 = (bf16[4,32,256]{2,1,0:T(8,128)(2,1)S(1)}, bf16[4,32,256]{2,1,0:T(8,128)(2,1)}, u32[]{:S(2)}) copy-start(bf16[4,32,256]{2,1,0:T(8,128)(2,1)} %copy-done.57) | copy-start | bytes 196612
  87.0 17.7 %copy-start.56 = (bf16[4,32,256]{2,1,0:T(8,128)(2,1)S(1)}, bf16[4,32,256]{2,1,0:T(8,128)(2,1)}, u32[]{:S(2)}) copy-start(bf16[4,32,256]{2,1,0:T(8,128)(2,1)} %copy-done.55) | copy-start | bytes 196612
  87.0 18.0 %copy-start.54 = (bf16[4,32,256]{2,1,0:T(8,128)(2,1)S(1)}, bf16[4,32,256]{2,1,0:T(8,128)(2,1)}, u32[]{:S(2)}) copy-start(bf16[4,32,256]{2,1,0:T(8,128)(2,1)} %copy-done.53) | copy-start | bytes 196612
  87.0 18.0 %copy-start.52 = (bf16[4,32,256]{2,1,0:T(8,128)(2,1)S(1)}, bf16[4,32,256]{2,1,0:T(8,128)(2,1)}, u32[]{:S(2)}) copy-start(bf16[4,32,256]{2,1,0:T(8,128)(2,1)} %copy-done.51) | copy-start | bytes 196612
  87.0 20.7 %copy-start.50 = (bf16[4,32,256]{2,1,0:T(8,128)(2,1)S(1)}, bf16[4,32,256]{2,1,0:T(8,128)(2,1)}, u32[]{:S(2)}) copy-start(bf16[4,32,256]{2,1,0:T(8,128)(2,1)} %copy-done.49) | copy-start | bytes 196612
  87.1 22.1 %copy-start.48 = (bf16[4,32,256]{2,1,0:T(8,128)(2,1)S(1)}, bf16[4,32,256]{2,1,0:T(8,128)(2,1)}, u32[]{:S(2)}) copy-start(bf16[4,32,256]{2,1,0:T(8,128)(2,1)} %copy-done.47) | copy-start | bytes 196612
  95.6 42.1 %copy-start = (bf16[4,512,512]{2,1,0:T(8,128)(2,1)S(1)}, bf16[4,512,512]{2,1,0:T(8,128)(2,1)}, u32[]{:S(2)}) copy-start(bf16[4,512,512]{2,1,0:T(8,128)(2,1)} %left_ref.1) | copy-start | bytes 6291460
  95.6 9.5 %collective-permute-start.17 = (bf16[4,32,256]{2,1,0:T(8,128)(2,1)S(1)}, bf16[4,32,256]{2,1,0:T(8,128)(2,1)S(1)}, u32[]{:S(2)}, u32[]{:S(2)}) collective-permute-start(bf16[4,32,256]{2,1,0:T(8,128)(2,1)S(1)} %copy-done.62), channel_id=1, source_target_pairs={{0,12},{1,13},{2,14},{3,15},{4,8},{5,9},{6,10},{7,11},{8,4},{9,5},... | collective-permute-start | bytes 196616 | tf_op jit(solution)/shard_map/ppermute | solution.py:31
  100.5 7.2 %collective-permute-start.18 = (bf16[4,32,256]{2,1,0:T(8,128)(2,1)S(1)}, bf16[4,32,256]{2,1,0:T(8,128)(2,1)S(1)}, u32[]{:S(2)}, u32[]{:S(2)}) collective-permute-start(bf16[4,32,256]{2,1,0:T(8,128)(2,1)S(1)} %copy-done.60), channel_id=1, source_target_pairs={{0,13},{1,12},{2,15},{3,14},{4,9},{5,8},{6,11},{7,10},{8,5},{9,4},... | collective-permute-start | bytes 196616 | tf_op jit(solution)/shard_map/ppermute | solution.py:31
  100.5 8.6 %collective-permute-start.19 = (bf16[4,32,256]{2,1,0:T(8,128)(2,1)S(1)}, bf16[4,32,256]{2,1,0:T(8,128)(2,1)S(1)}, u32[]{:S(2)}, u32[]{:S(2)}) collective-permute-start(bf16[4,32,256]{2,1,0:T(8,128)(2,1)S(1)} %copy-done.58), channel_id=1, source_target_pairs={{0,14},{1,15},{2,12},{3,13},{4,10},{5,11},{6,8},{7,9},{8,6},{9,7},... | collective-permute-start | bytes 196616 | tf_op jit(solution)/shard_map/ppermute | solution.py:31
  104.7 11.7 %collective-permute-start.20 = (bf16[4,32,256]{2,1,0:T(8,128)(2,1)S(1)}, bf16[4,32,256]{2,1,0:T(8,128)(2,1)S(1)}, u32[]{:S(2)}, u32[]{:S(2)}) collective-permute-start(bf16[4,32,256]{2,1,0:T(8,128)(2,1)S(1)} %copy-done.56), channel_id=1, source_target_pairs={{0,15},{1,14},{2,13},{3,12},{4,11},{5,10},{6,9},{7,8},{8,7},{9,6},... | collective-permute-start | bytes 196616 | tf_op jit(solution)/shard_map/ppermute | solution.py:31
  105.1 12.3 %collective-permute-start.13 = (bf16[4,32,256]{2,1,0:T(8,128)(2,1)S(1)}, bf16[4,32,256]{2,1,0:T(8,128)(2,1)S(1)}, u32[]{:S(2)}, u32[]{:S(2)}) collective-permute-start(bf16[4,32,256]{2,1,0:T(8,128)(2,1)S(1)} %copy-done.54), channel_id=1, source_target_pairs={{0,8},{1,9},{2,10},{3,11},{4,12},{5,13},{6,14},{7,15},{8,0},{9,1},... | collective-permute-start | bytes 196616 | tf_op jit(solution)/shard_map/ppermute | solution.py:31
  105.1 13.0 %collective-permute-start.14 = (bf16[4,32,256]{2,1,0:T(8,128)(2,1)S(1)}, bf16[4,32,256]{2,1,0:T(8,128)(2,1)S(1)}, u32[]{:S(2)}, u32[]{:S(2)}) collective-permute-start(bf16[4,32,256]{2,1,0:T(8,128)(2,1)S(1)} %copy-done.52), channel_id=1, source_target_pairs={{0,9},{1,8},{2,11},{3,10},{4,13},{5,12},{6,15},{7,14},{8,1},{9,0},... | collective-permute-start | bytes 196616 | tf_op jit(solution)/shard_map/ppermute | solution.py:31
  107.7 15.2 %collective-permute-start.15 = (bf16[4,32,256]{2,1,0:T(8,128)(2,1)S(1)}, bf16[4,32,256]{2,1,0:T(8,128)(2,1)S(1)}, u32[]{:S(2)}, u32[]{:S(2)}) collective-permute-start(bf16[4,32,256]{2,1,0:T(8,128)(2,1)S(1)} %copy-done.50), channel_id=1, source_target_pairs={{0,10},{1,11},{2,8},{3,9},{4,14},{5,15},{6,12},{7,13},{8,2},{9,3},... | collective-permute-start | bytes 196616 | tf_op jit(solution)/shard_map/ppermute | solution.py:31
  109.1 14.5 %collective-permute-start.16 = (bf16[4,32,256]{2,1,0:T(8,128)(2,1)S(1)}, bf16[4,32,256]{2,1,0:T(8,128)(2,1)S(1)}, u32[]{:S(2)}, u32[]{:S(2)}) collective-permute-start(bf16[4,32,256]{2,1,0:T(8,128)(2,1)S(1)} %copy-done.48), channel_id=1, source_target_pairs={{0,11},{1,10},{2,9},{3,8},{4,15},{5,14},{6,13},{7,12},{8,3},{9,2},... | collective-permute-start | bytes 196616 | tf_op jit(solution)/shard_map/ppermute | solution.py:31
  127.0 39.9 %collective-permute-start.25 = (bf16[4,512,256]{2,1,0:T(8,128)(2,1)S(1)}, bf16[4,512,256]{2,1,0:T(8,128)(2,1)}, u32[]{:S(2)}, u32[]{:S(2)}) collective-permute-start(bf16[4,512,256]{2,1,0:T(8,128)(2,1)S(1)} %bitcast.8), channel_id=1, source_target_pairs={{0,16},{16,0},{1,17},{17,1},{2,18},{18,2},{3,19},{19,3},{4,20},{20... | collective-permute-start | bytes 3145736 | tf_op jit(solution)/shard_map/ppermute | solution.py:16
  127.6 28.2 %all-to-all-start.1 = ((bf16[8,4,32,256]{3,2,1,0:T(8,128)(2,1)}), bf16[8,4,32,256]{3,2,1,0:T(8,128)(2,1)}, u32[]{:S(2)}, u32[]{:S(2)}) async-start(bf16[8,4,32,256]{3,2,1,0:T(8,128)(2,1)} %copy-done.28), calls=%async_computation.1 | async-start | bytes 1048576 | tf_op jit(solution)/shard_map/all_to_all | solution.py:27
  132.0 35.0 %collective-permute-start.26 = (bf16[32,64,64]{2,1,0:T(8,128)(2,1)}, bf16[32,64,64]{2,1,0:T(8,128)(2,1)}, u32[]{:S(2)}, u32[]{:S(2)}) collective-permute-start(bf16[32,64,64]{2,1,0:T(8,128)(2,1)} %copy-done.30), channel_id=1, source_target_pairs={{0,16},{16,0},{1,17},{17,1},{2,18},{18,2},{3,19},{19,3},{4,20},{20... | collective-permute-start | bytes 786440 | tf_op jit(solution)/shard_map/ppermute | solution.py:16
  133.5 9.0 %collective-permute-start.9 = (bf16[4,32,256]{2,1,0:T(8,128)(2,1)}, bf16[4,32,256]{2,1,0:T(8,128)(2,1)S(1)}, u32[]{:S(2)}, u32[]{:S(2)}) collective-permute-start(bf16[4,32,256]{2,1,0:T(8,128)(2,1)} %copy-done.46), channel_id=1, source_target_pairs={{0,8},{1,9},{2,10},{3,11},{4,12},{5,13},{6,14},{7,15},{8,0},{9,1},... | collective-permute-start | bytes 196616 | tf_op jit(solution)/shard_map/ppermute | solution.py:31
  134.1 10.4 %collective-permute-start.10 = (bf16[4,32,256]{2,1,0:T(8,128)(2,1)}, bf16[4,32,256]{2,1,0:T(8,128)(2,1)S(1)}, u32[]{:S(2)}, u32[]{:S(2)}) collective-permute-start(bf16[4,32,256]{2,1,0:T(8,128)(2,1)} %copy-done.45), channel_id=1, source_target_pairs={{0,9},{1,8},{2,11},{3,10},{4,13},{5,12},{6,15},{7,14},{8,1},{9,0},... | collective-permute-start | bytes 196616 | tf_op jit(solution)/shard_map/ppermute | solution.py:31
  135.6 11.9 %collective-permute-start.11 = (bf16[4,32,256]{2,1,0:T(8,128)(2,1)}, bf16[4,32,256]{2,1,0:T(8,128)(2,1)S(1)}, u32[]{:S(2)}, u32[]{:S(2)}) collective-permute-start(bf16[4,32,256]{2,1,0:T(8,128)(2,1)} %copy-done.44), channel_id=1, source_target_pairs={{0,10},{1,11},{2,8},{3,9},{4,14},{5,15},{6,12},{7,13},{8,2},{9,3},... | collective-permute-start | bytes 196616 | tf_op jit(solution)/shard_map/ppermute | solution.py:31
  137.7 1.2 copy-start.2
  138.9 3.6 %copy-start.43 = (bf16[4,32,256]{2,1,0:T(8,128)(2,1)S(1)}, bf16[4,32,256]{2,1,0:T(8,128)(2,1)}, u32[]{:S(2)}) copy-start(bf16[4,32,256]{2,1,0:T(8,128)(2,1)} %copy-done.42) | copy-start | bytes 196612
  138.9 5.6 %copy-start.41 = (bf16[4,32,256]{2,1,0:T(8,128)(2,1)S(1)}, bf16[4,32,256]{2,1,0:T(8,128)(2,1)}, u32[]{:S(2)}) copy-start(bf16[4,32,256]{2,1,0:T(8,128)(2,1)} %copy-done.40) | copy-start | bytes 196612
  141.2 1.3 copy-start.7
  142.5 24.4 %copy-start.4 = (bf16[4,512,256]{2,1,0:T(8,128)(2,1)S(1)}, bf16[4,512,256]{2,1,0:T(8,128)(2,1)}, u32[]{:S(2)}) copy-start(bf16[4,512,256]{2,1,0:T(8,128)(2,1)} %copy-done.3) | copy-start | bytes 3145732
  142.5 6.3 %collective-permute-start.12 = (bf16[4,32,256]{2,1,0:T(8,128)(2,1)S(1)}, bf16[4,32,256]{2,1,0:T(8,128)(2,1)S(1)}, u32[]{:S(2)}, u32[]{:S(2)}) collective-permute-start(bf16[4,32,256]{2,1,0:T(8,128)(2,1)S(1)} %copy-done.43), channel_id=1, source_target_pairs={{0,11},{1,10},{2,9},{3,8},{4,15},{5,14},{6,13},{7,12},{8,3},{9,2},... | collective-permute-start | bytes 196616 | tf_op jit(solution)/shard_map/ppermute | solution.py:31
  144.6 8.0 %collective-permute-start.21 = (bf16[4,32,256]{2,1,0:T(8,128)(2,1)S(1)}, bf16[4,32,256]{2,1,0:T(8,128)(2,1)S(1)}, u32[]{:S(2)}, u32[]{:S(2)}) collective-permute-start(bf16[4,32,256]{2,1,0:T(8,128)(2,1)S(1)} %copy-done.41), channel_id=1, source_target_pairs={{0,12},{1,13},{2,14},{3,15},{4,8},{5,9},{6,10},{7,11},{8,4},{9,5},... | collective-permute-start | bytes 196616 | tf_op jit(solution)/shard_map/ppermute | solution.py:31
  147.5 8.4 %collective-permute-start.22 = (bf16[4,32,256]{2,1,0:T(8,128)(2,1)}, bf16[4,32,256]{2,1,0:T(8,128)(2,1)S(1)}, u32[]{:S(2)}, u32[]{:S(2)}) collective-permute-start(bf16[4,32,256]{2,1,0:T(8,128)(2,1)} %get-tuple-element.83), channel_id=1, source_target_pairs={{0,13},{1,12},{2,15},{3,14},{4,9},{5,8},{6,11},{7,10},{8,5},{9,4},... | collective-permute-start | bytes 196616 | tf_op jit(solution)/shard_map/ppermute | solution.py:31
  148.8 7.3 %collective-permute-start.23 = (bf16[4,32,256]{2,1,0:T(8,128)(2,1)}, bf16[4,32,256]{2,1,0:T(8,128)(2,1)S(1)}, u32[]{:S(2)}, u32[]{:S(2)}) collective-permute-start(bf16[4,32,256]{2,1,0:T(8,128)(2,1)} %get-tuple-element.85), channel_id=1, source_target_pairs={{0,14},{1,15},{2,12},{3,13},{4,10},{5,11},{6,8},{7,9},{8,6},{9,7},... | collective-permute-start | bytes 196616 | tf_op jit(solution)/shard_map/ppermute | solution.py:31
  152.6 6.6 %collective-permute-start.24 = (bf16[4,32,256]{2,1,0:T(8,128)(2,1)}, bf16[4,32,256]{2,1,0:T(8,128)(2,1)S(1)}, u32[]{:S(2)}, u32[]{:S(2)}) collective-permute-start(bf16[4,32,256]{2,1,0:T(8,128)(2,1)} %get-tuple-element.87), channel_id=1, source_target_pairs={{0,15},{1,14},{2,13},{3,12},{4,11},{5,10},{6,9},{7,8},{8,7},{9,6},... | collective-permute-start | bytes 196616 | tf_op jit(solution)/shard_map/ppermute | solution.py:31
  164.0 3.0 %copy-start.8 = (bf16[4,512,512]{2,1,0:T(8,128)(2,1)S(1)}, bf16[4,512,512]{2,1,0:T(8,128)(2,1)}, u32[]{:S(2)}) copy-start(bf16[4,512,512]{2,1,0:T(8,128)(2,1)} %copy-done.7) | copy-start | bytes 6291460
  (45 other events, 35.4 us)

commit v6 on v5

v6 whole, which is shorter than its diff:
```python
import functools
import math

import jax
import jax.numpy as jnp
from jax import lax
from jax.experimental import pallas as pl
from jax.experimental.pallas import tpu as pltpu
from jax.sharding import PartitionSpec as P

BF16 = jnp.bfloat16
F32 = jnp.float32
MIB = 1024 * 1024


def swap_sequences(array):
    return lax.ppermute(array, "dp", [(0, 1), (1, 0)])


def after(array, earlier):
    return lax.optimization_barrier((array, earlier))[0]


def far_first(count):
    return sorted(range(1, count), key=lambda t: -(t // (count // 2)))


def step(messages, stride):
    seq = lax.axis_size("seq")
    received = list(messages)
    for t in far_first(len(messages)):
        pairs = [(i, i ^ (t * stride)) for i in range(seq)]
        received[t] = lax.ppermute(messages[t], "seq", pairs)
    return received


def call(kernel, me, inputs, out_shapes, scratch=(), flops=0, unblocked=(), vmem=32):
    whole = pl.BlockSpec(memory_space=pltpu.VMEM)
    moved = sum(x.size * x.dtype.itemsize for x in (*inputs, *out_shapes))
    in_specs = [
        pl.BlockSpec(memory_space=pl.ANY) if n in unblocked else whole for n in range(len(inputs))
    ]
    return pl.pallas_call(
        kernel,
        out_shape=out_shapes,
        in_specs=[pl.BlockSpec(memory_space=pltpu.SMEM)] + in_specs,
        out_specs=[whole] * len(out_shapes),
        scratch_shapes=scratch,
        compiler_params=pltpu.CompilerParams(vmem_limit_bytes=vmem * MIB),
        name=getattr(kernel, "func", kernel).__name__,
        cost_estimate=pl.CostEstimate(flops=flops, bytes_accessed=moved, transcendentals=0),
    )(me, *inputs)


def dot(a, b, contract):
    return lax.dot_general(a, b, (contract, ((), ())), preferred_element_type=F32)


def by_outer(outer, inner, me, refs):
    return [(me ^ (t * inner + r), refs[t].at[r]) for t in range(outer) for r in range(inner)]


def by_inner(outer, inner, me, refs):
    return [(me ^ (t * inner + r), refs[r].at[t]) for t in range(outer) for r in range(inner)]


def product_kernel(outer, inner, me_ref, gate_hbm, cotangent_hbm, *refs):
    out_refs, (gate, cotangent, sems) = refs[:outer], refs[outer:]
    rows = gate.shape[0]
    loads = [
        [
            pltpu.make_async_copy(source.at[i], target.at[i], sems.at[n, i])
            for n, (source, target) in enumerate(((gate_hbm, gate), (cotangent_hbm, cotangent)))
        ]
        for i in range(rows)
    ]
    for pair in loads:
        for load in pair:
            load.start()
    blocks = by_outer(outer, inner, me_ref[0], out_refs)
    for i in range(rows):
        for load in loads[i]:
            load.wait()
        for c, ref in blocks:
            ref[i] = (gate[i, c].astype(F32) * cotangent[i, c].astype(F32)).astype(BF16)


def mix_kernel(outer, inner, me_ref, left_ref, values_ref, *refs):
    out_refs, hold = refs[:outer], refs[outer]
    rows, seq, cols, channels = hold.shape
    for i in range(rows):
        mixed = dot(left_ref[i], values_ref[i], ((1,), (0,)))
        hold[i] = mixed.astype(BF16).reshape(seq, cols, channels)
    for c, ref in by_outer(outer, inner, me_ref[0], out_refs):
        ref[...] = hold[:, c]


def turn_kernel(count, me_ref, *refs):
    in_refs, out_refs = refs[:count], refs[count:]
    for t, in_ref in enumerate(in_refs):
        for r, out_ref in enumerate(out_refs):
            out_ref[t] = in_ref[r]


def load_columns(blocks, wide):
    rows, cols, channels = blocks[0][1].shape
    size = rows * cols
    for c, ref in blocks:
        block = ref[...].reshape(size, channels).astype(F32)
        start = pl.multiple_of(c * size, size)
        for h in range(channels // 128):
            wide[h, pl.ds(start, size), :] = block[:, h * 128 : (h + 1) * 128]


def column(wide, k, count, cols):
    halves = [wide[h, pl.ds(k, count, stride=cols), :] for h in range(wide.shape[0])]
    return jnp.concatenate(halves, axis=1).astype(BF16)


def store_column(wide, k, count, cols, value):
    for h in range(wide.shape[0]):
        wide[h, pl.ds(k, count, stride=cols), :] = value[:, h * 128 : (h + 1) * 128]


def send_columns(wide, blocks):
    rows, cols, channels = blocks[0][1].shape
    size = rows * cols
    for c, ref in blocks:
        start = pl.multiple_of(c * size, size)
        halves = [wide[h, pl.ds(start, size), :] for h in range(wide.shape[0])]
        block = jnp.concatenate(halves, axis=1).astype(BF16)
        ref[...] = block.reshape(rows, cols, channels)


def column_backward_kernel(outer, inner, me_ref, right_ref, *refs):
    in_refs, out_refs = refs[:inner], refs[inner : 2 * inner]
    by_column_ref, wide, wide_out = refs[2 * inner :]
    cols, count, _ = right_ref.shape
    me = me_ref[0]
    load_columns(by_inner(outer, inner, me, in_refs), wide)
    for k in range(cols):
        grad = column(wide, k, count, cols)
        by_column_ref[k] = grad
        store_column(wide_out, k, count, cols, dot(right_ref[k], grad, ((0,), (0,))))
    send_columns(wide_out, by_inner(outer, inner, me, out_refs))


def column_forward_kernel(outer, inner, me_ref, right_ref, grad_ref, after_ref, *refs):
    in_refs, out_refs = refs[:inner], refs[inner : 2 * inner]
    right_part_ref, wide, wide_out = refs[2 * inner :]
    cols, count, _ = right_ref.shape
    me = me_ref[0]
    load_columns(by_inner(outer, inner, me, in_refs), wide)
    for k in range(cols):
        mixed = column(wide, k, count, cols)
        store_column(wide_out, k, count, cols, dot(right_ref[k], mixed, ((1,), (0,))))
        right_part_ref[k] = dot(grad_ref[k], mixed, ((1,), (1,))).astype(BF16)
    send_columns(wide_out, by_inner(outer, inner, me, out_refs))


def gather_kernel(outer, inner, me_ref, *refs):
    for c, ref in by_outer(outer, inner, me_ref[0], refs[:outer]):
        refs[outer][:, c] = ref[...]


def row_backward_kernel(me_ref, left_ref, values_ref, grad_ref, signal_ref, term_ref):
    for i in range(left_ref.shape[0]):
        grad = grad_ref[i]
        signal_ref[i] = dot(left_ref[i], grad, ((0,), (0,))).astype(BF16)
        term_ref[i] = dot(grad, values_ref[i], ((1,), (1,))).astype(BF16)


def factor_sum_kernel(
    me_ref, term_ref, values_ref, grad_ref, right_ref, other_ref, left_out_ref, right_out_ref
):
    for i in range(term_ref.shape[0]):
        other = dot(grad_ref[i], values_ref[i], ((1,), (1,))).astype(BF16)
        left_out_ref[i] = (term_ref[i].astype(F32) + other.astype(F32)).astype(BF16)
    right_out_ref[...] = (right_ref[...].astype(F32) + other_ref[...].astype(F32)).astype(BF16)


def output_kernel(outer, inner, me_ref, gate_ref, cotangent_ref, *refs):
    out_ref, grad_ref = refs[outer:]
    for c, ref in by_outer(outer, inner, me_ref[0], refs[:outer]):
        second = ref[...].astype(F32)
        out_ref[:, c] = (gate_ref[:, c].astype(F32) * second).astype(BF16)
        grad_ref[:, c] = (cotangent_ref[:, c].astype(F32) * second).astype(BF16)


def direct_shards(signal, gating, upstream, left_factor, right_factor):
    seq = lax.axis_size("seq")
    side = math.isqrt(seq)
    rows, block_len = left_factor.shape[:2]
    cols, count = right_factor.shape[:2]
    channels = signal.shape[2]
    me = lax.axis_index("seq").astype(jnp.int32).reshape(1)
    values = signal.reshape(rows, block_len, channels)
    gate = gating.reshape(rows, seq, cols, channels)
    cotangent = upstream.reshape(rows, seq, cols, channels)

    def shape(*dims):
        return jax.ShapeDtypeStruct(dims, BF16)

    def grouped(kernel):
        return functools.partial(kernel, side, side)

    messages = [shape(side, rows, cols, channels)] * side
    whole = shape(rows, seq, cols, channels)
    by_row = shape(rows, block_len, channels)
    left = shape(*left_factor.shape)
    right = shape(*right_factor.shape)
    wide = pltpu.VMEM((channels // 128, count * cols, 128), F32)
    row_flops = 2 * rows * block_len * block_len * channels
    column_flops = 2 * cols * count * count * channels

    def turn(received):
        return call(functools.partial(turn_kernel, side), me, received, messages)

    grad_rows = call(
        grouped(product_kernel),
        me,
        [gate, cotangent],
        messages,
        [pltpu.VMEM(whole.shape, BF16)] * 2 + [pltpu.SemaphoreType.DMA((2, rows))],
        unblocked=range(2),
        vmem=60,
    )
    mixed_rows = call(
        grouped(mix_kernel),
        me,
        [left_factor, values],
        messages,
        [pltpu.VMEM(whole.shape, BF16)],
        row_flops,
    )
    grad_received = step(grad_rows, side)
    grad_received[0] = after(grad_received[0], mixed_rows[0])
    mixed_received = step(mixed_rows, side)
    grad_columns = step(turn(grad_received), 1)
    other_values = swap_sequences(after(values, grad_rows[0]))
    *grad_second, grad_column = call(
        grouped(column_backward_kernel),
        me,
        [right_factor, *grad_columns],
        messages + [shape(cols, count, channels)],
        [wide, wide],
        column_flops,
    )
    mixed_columns = step(turn(mixed_received), 1)
    back_received = step(grad_second, 1)
    back_received[0] = after(back_received[0], mixed_received[-1])
    back_turned = list(turn(back_received))
    *second, right_part = call(
        grouped(column_forward_kernel),
        me,
        [right_factor, grad_column, other_values, *mixed_columns],
        messages + [right],
        [wide, wide],
        2 * column_flops,
        unblocked=[2],
    )
    back_turned[1] = after(back_turned[1], right_part)
    back_blocks = step(back_turned, side)
    other_right = swap_sequences(right_part)
    second_turned = list(turn(step(second, 1)))
    back_blocks[0] = after(back_blocks[0], second_turned[0])
    (gathered,) = call(grouped(gather_kernel), me, back_blocks, [whole])
    grad_back = gathered.reshape(rows, block_len, channels)
    other_grad_back = swap_sequences(grad_back)
    grad_signal, left_term = call(
        row_backward_kernel,
        me,
        [left_factor, values, grad_back],
        [by_row, left],
        flops=2 * row_flops,
    )
    second_turned[1] = after(second_turned[1], left_term)
    second_blocks = step(second_turned, side)
    grad_left, grad_right = call(
        factor_sum_kernel,
        me,
        [left_term, other_values, other_grad_back, right_part, other_right],
        [left, right],
        flops=row_flops,
    )
    output, grad_gate = call(
        grouped(output_kernel), me, [gate, cotangent, *second_blocks], [whole, whole]
    )
    return (
        output.reshape(signal.shape),
        grad_gate.reshape(signal.shape),
        grad_signal.reshape(signal.shape),
        grad_left,
        grad_right,
    )


def plain_shards(signal, gating, upstream, left_factor, right_factor):
    seq = lax.axis_size("seq")
    rows, block_len = left_factor.shape[:2]
    cols, block_count = right_factor.shape[:2]
    channels = signal.shape[2]
    values = signal.reshape(rows, block_len, channels)
    gate = gating.reshape(rows, block_len, channels)
    cotangent = upstream.reshape(rows, block_len, channels)

    def einsum(spec, a, b):
        return jnp.einsum(spec, a, b, preferred_element_type=F32).astype(BF16)

    def all_to_all(blocks):
        return lax.all_to_all(blocks, "seq", split_axis=0, concat_axis=0, tiled=True)

    def to_columns(by_row):
        blocks = by_row.reshape(rows, seq, cols, channels).transpose(1, 0, 2, 3)
        return all_to_all(blocks).reshape(block_count, cols, channels)

    def to_rows(by_column):
        blocks = all_to_all(by_column.reshape(seq, rows, cols, channels))
        return blocks.transpose(1, 0, 2, 3).reshape(rows, block_len, channels)

    grad_rows = (cotangent.astype(F32) * gate.astype(F32)).astype(BF16)
    grad_column = to_columns(grad_rows)
    other_values = swap_sequences(values)
    mixed_column = to_columns(einsum("ikj,ijd->ikd", left_factor, values))
    grad_back = to_rows(einsum("kmi,mkd->ikd", right_factor, grad_column))
    second_rows = to_rows(einsum("kmi,ikd->mkd", right_factor, mixed_column))
    right_part = einsum("mkd,ikd->kmi", grad_column, mixed_column)
    other_right = swap_sequences(right_part)
    other_grad_back = swap_sequences(grad_back)
    grad_signal = einsum("ikj,ikd->ijd", left_factor, grad_back)
    left_term = einsum("ikd,ijd->ikj", grad_back, values)
    other_left = einsum("ikd,ijd->ikj", other_grad_back, other_values)
    grad_left = (left_term.astype(F32) + other_left.astype(F32)).astype(BF16)
    grad_right = (right_part.astype(F32) + other_right.astype(F32)).astype(BF16)
    wide = second_rows.astype(F32)
    output = (gate.astype(F32) * wide).astype(BF16)
    grad_gate = (cotangent.astype(F32) * wide).astype(BF16)
    return (
        output.reshape(signal.shape),
        grad_gate.reshape(signal.shape),
        grad_signal.reshape(signal.shape),
        grad_left,
        grad_right,
    )


def shards(signal, gating, upstream, left_factor, right_factor):
    seq = lax.axis_size("seq")
    cols = right_factor.shape[0]
    direct = seq in (4, 16) and cols % 32 == 0
    run = direct_shards if direct else plain_shards
    return run(signal, gating, upstream, left_factor, right_factor)


def solution(mesh):
    by_position = P("dp", "seq", None)
    by_block = P("seq", None, None)
    return jax.shard_map(
        shards,
        mesh=mesh,
        in_specs=(by_position,) * 3 + (by_block,) * 2,
        out_specs=(by_position,) * 3 + (by_block,) * 2,
        check_vma=False,
    )
```

time: 174 us -> 146 us (0.84); the launches traced: 172 us -> 145 us
  waiting for transfers between devices: 19.9 us -> 95.3 us
  starting transfers between devices: 90.6 us -> 31.9 us
  local copies, waits for them, and re-layouts: 39.3 us -> 1.25 us
  Pallas kernels: 21 us -> 16.2 us
    ppermute x24, waiting for transfers between devices: 19.9 us -> 86.5 us  [step(): received[t] = lax.ppermute(messages[t], 'seq', pairs)]
    ppermute x24, starting transfers between devices: 69.3 us -> 26.8 us  [step(): received[t] = lax.ppermute(messages[t], 'seq', pairs)]
    unnamed x126 -> x14, local copies, waits for them, and re-layouts: 39.3 us -> 1.25 us
    all_to_all x3 -> x0, starting transfers between devices: 17.5 us -> none  [exchange(): lax.all_to_all(near, 'seq', split_axis=0, concat_axis=0, axis_index_group...]
    ppermute x3, waiting for transfers between devices: 0.01 us -> 8.78 us  [swap_sequences(): return lax.ppermute(array, 'dp', [(0, 1), (1, 0)])]
    pallas_call x7 -> x12, Pallas kernels: 21 us -> 16.2 us  [call(): pl.pallas_call(kernel, out_shape=out_shapes, in_specs=[pl.BlockSpec(memor...]
  transfers between devices with their start and end apart: 30 -> 27, of which waited for: 9 -> 15; matrix products, arithmetic and copies ran while one was open for 0% -> 0% of each run, Pallas kernels for 7% -> 8%
where the time goes in v6:
time: 146 us; the launch traced here: 145 us
  waiting for transfers between devices  95.3 us (65%)
  starting transfers between devices  31.9 us (22%)
  Pallas kernels  16.2 us (11%)
    ppermute x24, waiting for transfers between devices, step(): received[t] = lax.ppermute(messages[t], 'seq', pairs)  86.5 us
    ppermute x24, starting transfers between devices, step(): received[t] = lax.ppermute(messages[t], 'seq', pairs)  26.8 us
    pallas_call x12, Pallas kernels, call(): pl.pallas_call(kernel, out_shape=out_shapes, in_specs=[pl.BlockSpec(memor...  16.2 us
    ppermute x3, waiting for transfers between devices, swap_sequences(): return lax.ppermute(array, 'dp', [(0, 1), (1, 0)])  8.78 us
    ppermute x3, starting transfers between devices, swap_sequences(): return lax.ppermute(array, 'dp', [(0, 1), (1, 0)])  5.09 us
  transfers between devices with their start and end apart: 27, of which 15 were waited for; matrix products, arithmetic and copies ran while one was open for 0% of the time, Pallas kernels for 8%

profile of v6, /device:TPU:0, one launch (start us, length us, event | category | flops | bytes accessed | tf_op | source)
XLA Modules:
  0.0 145.4 jit_solution(11617745802709573559)
XLA Ops:
  0.6 2.7 %product_kernel.1 = (bf16[4,4,32,256]{3,2,1,0:T(8,128)(2,1)}, bf16[4,4,32,256]{3,2,1,0:T(8,128)(2,1)}, bf16[4,4,32,256]{3,2,1,0:T(8,128)(2,1)}, bf16[4,4,32,256]{3,2,1,0:T(8,128)(2,1)}) custom-call(s32[1]{0:T(128)} %bitcast.me_ref, bf16[4,16,32,256]{3,2,1,0:T(8,128)(2,1)} %bitcast.13, bf16[4,16,32,256]{3,2,1,0:T(8,128)(2,1)} %bitcast.15), custom_call_target="tpu_custom_call" | custom-call | bytes 3145728 | tf_op jit(solution)/shard_map/product_kernel/pallas_call | solution.py:43
  3.4 3.0 %collective-permute-start.6 = (bf16[4,512,256]{2,1,0:T(8,128)(2,1)}, bf16[4,512,256]{2,1,0:T(8,128)(2,1)S(1)}, u32[]{:S(2)}, u32[]{:S(2)}) collective-permute-start(bf16[4,512,256]{2,1,0:T(8,128)(2,1)} %bitcast.10), channel_id=1, source_target_pairs={{0,16},{16,0},{1,17},{17,1},{2,18},{18,2},{3,19},{19,3},{4,20},{20... | collective-permute-start | bytes 3145736 | tf_op jit(solution)/shard_map/ppermute | solution.py:17
  6.4 1.6 %collective-permute-start = (bf16[4,4,32,256]{3,2,1,0:T(8,128)(2,1)}, bf16[4,4,32,256]{3,2,1,0:T(8,128)(2,1)S(1)}, u32[]{:S(2)}, u32[]{:S(2)}) collective-permute-start(bf16[4,4,32,256]{3,2,1,0:T(8,128)(2,1)} %get-tuple-element.54), channel_id=1, source_target_pairs={{0,4},{1,5},{2,6},{3,7},{4,0},{5,1},{6,2},{7,3},{8,12},{9,13},{10,... | collective-permute-start | bytes 786440 | tf_op jit(solution)/shard_map/ppermute | solution.py:33
  7.9 2.6 %collective-permute-start.1 = (bf16[4,4,32,256]{3,2,1,0:T(8,128)(2,1)}, bf16[4,4,32,256]{3,2,1,0:T(8,128)(2,1)S(1)}, u32[]{:S(2)}, u32[]{:S(2)}) collective-permute-start(bf16[4,4,32,256]{3,2,1,0:T(8,128)(2,1)} %get-tuple-element.55), channel_id=1, source_target_pairs={{0,8},{1,9},{2,10},{3,11},{4,12},{5,13},{6,14},{7,15},{8,0},{9,1},... | collective-permute-start | bytes 786440 | tf_op jit(solution)/shard_map/ppermute | solution.py:33
  10.5 0.2 collective-permute-start.2
  10.8 1.2 copy-done.1
  12.0 0.8 mix_kernel.1
  12.8 0.7 collective-permute-start.7
  13.5 7.0 %collective-permute-done.refs_1_ = bf16[4,4,32,256]{3,2,1,0:T(8,128)(2,1)S(1)} collective-permute-done((bf16[4,4,32,256]{3,2,1,0:T(8,128)(2,1)}, bf16[4,4,32,256]{3,2,1,0:T(8,128)(2,1)S(1)}, u32[]{:S(2)}, u32[]{:S(2)}) %collective-permute-start) | collective-permute-done | bytes 262176 | tf_op jit(solution)/shard_map/ppermute | solution.py:33
  20.5 1.8 %collective-permute-start.8 = (bf16[4,4,32,256]{3,2,1,0:T(8,128)(2,1)S(1)}, bf16[4,4,32,256]{3,2,1,0:T(8,128)(2,1)S(1)}, u32[]{:S(2)}, u32[]{:S(2)}) collective-permute-start(bf16[4,4,32,256]{3,2,1,0:T(8,128)(2,1)S(1)} %get-tuple-element.64), channel_id=1, source_target_pairs={{0,8},{1,9},{2,10},{3,11},{4,12},{5,13},{6,14},{7,15},{8,0},{9,1},... | collective-permute-start | bytes 786440 | tf_op jit(solution)/shard_map/ppermute | solution.py:33
  22.3 7.3 %collective-permute-done.1.refs_2_ = bf16[4,4,32,256]{3,2,1,0:T(8,128)(2,1)S(1)} collective-permute-done((bf16[4,4,32,256]{3,2,1,0:T(8,128)(2,1)}, bf16[4,4,32,256]{3,2,1,0:T(8,128)(2,1)S(1)}, u32[]{:S(2)}, u32[]{:S(2)}) %collective-permute-start.1) | collective-permute-done | bytes 262176 | tf_op jit(solution)/shard_map/ppermute | solution.py:33
  29.6 2.5 %collective-permute-start.9 = (bf16[4,4,32,256]{3,2,1,0:T(8,128)(2,1)S(1)}, bf16[4,4,32,256]{3,2,1,0:T(8,128)(2,1)S(1)}, u32[]{:S(2)}, u32[]{:S(2)}) collective-permute-start(bf16[4,4,32,256]{3,2,1,0:T(8,128)(2,1)S(1)} %get-tuple-element.65), channel_id=1, source_target_pairs={{0,12},{1,13},{2,14},{3,15},{4,8},{5,9},{6,10},{7,11},{8,4},{9,5},... | collective-permute-start | bytes 786440 | tf_op jit(solution)/shard_map/ppermute | solution.py:33
  32.1 0.1 collective-permute-start.3
  32.2 1.6 %collective-permute-start.4 = (bf16[4,4,32,256]{3,2,1,0:T(8,128)(2,1)S(1)}, bf16[4,4,32,256]{3,2,1,0:T(8,128)(2,1)S(1)}, u32[]{:S(2)}, u32[]{:S(2)}) collective-permute-start(bf16[4,4,32,256]{3,2,1,0:T(8,128)(2,1)S(1)} %get-tuple-element.59), channel_id=1, source_target_pairs={{0,2},{1,3},{2,0},{3,1},{4,6},{5,7},{6,4},{7,5},{8,10},{9,11},{10,... | collective-permute-start | bytes 786440 | tf_op jit(solution)/shard_map/ppermute | solution.py:33
  33.8 18.2 %collective-permute-done.8.refs_2_ = bf16[4,4,32,256]{3,2,1,0:T(8,128)(2,1)S(1)} collective-permute-done((bf16[4,4,32,256]{3,2,1,0:T(8,128)(2,1)S(1)}, bf16[4,4,32,256]{3,2,1,0:T(8,128)(2,1)S(1)}, u32[]{:S(2)}, u32[]{:S(2)}) %collective-permute-start.8) | collective-permute-done | bytes 262176 | tf_op jit(solution)/shard_map/ppermute | solution.py:33
  52.1 1.7 %collective-permute-start.10 = (bf16[4,4,32,256]{3,2,1,0:T(8,128)(2,1)S(1)}, bf16[4,4,32,256]{3,2,1,0:T(8,128)(2,1)S(1)}, u32[]{:S(2)}, u32[]{:S(2)}) collective-permute-start(bf16[4,4,32,256]{3,2,1,0:T(8,128)(2,1)S(1)} %get-tuple-element.67), channel_id=1, source_target_pairs={{0,1},{1,0},{2,3},{3,2},{4,5},{5,4},{6,7},{7,6},{8,9},{9,8},{10,11... | collective-permute-start | bytes 786440 | tf_op jit(solution)/shard_map/ppermute | solution.py:33
  53.8 0.5 collective-permute-start.11
  54.3 0.9 collective-permute-start.12
  55.3 5.3 %collective-permute-done.5.refs_3_ = bf16[4,4,32,256]{3,2,1,0:T(8,128)(2,1)S(1)} collective-permute-done((bf16[4,4,32,256]{3,2,1,0:T(8,128)(2,1)S(1)}, bf16[4,4,32,256]{3,2,1,0:T(8,128)(2,1)S(1)}, u32[]{:S(2)}, u32[]{:S(2)}) %collective-permute-start.5) | collective-permute-done | bytes 262176 | tf_op jit(solution)/shard_map/ppermute | solution.py:33
  60.6 3.0 %column_backward_kernel.1 = (bf16[4,4,32,256]{3,2,1,0:T(8,128)(2,1)S(1)}, bf16[4,4,32,256]{3,2,1,0:T(8,128)(2,1)S(1)}, bf16[4,4,32,256]{3,2,1,0:T(8,128)(2,1)S(1...) custom-call(s32[1]{0:T(128)} %bitcast.me_ref, bf16[32,64,64]{2,1,0:T(8,128)(2,1)S(1)} %copy-done.5, ...), custom_call_target="tpu_custom_call" | custom-call | flops 67108864 | bytes 3407872 | tf_op jit(solution)/shard_map/column_backward_kernel/pallas_call | solution.py:43
  63.5 0.2 collective-permute-start.16
  63.7 1.6 %collective-permute-start.17 = (bf16[4,4,32,256]{3,2,1,0:T(8,128)(2,1)S(1)}, bf16[4,4,32,256]{3,2,1,0:T(8,128)(2,1)S(1)}, u32[]{:S(2)}, u32[]{:S(2)}) collective-permute-start(bf16[4,4,32,256]{3,2,1,0:T(8,128)(2,1)S(1)} %get-tuple-element.79), channel_id=1, source_target_pairs={{0,2},{1,3},{2,0},{3,1},{4,6},{5,7},{6,4},{7,5},{8,10},{9,11},{10,... | collective-permute-start | bytes 786440 | tf_op jit(solution)/shard_map/ppermute | solution.py:33
  65.3 1.1 collective-permute-done.11.refs_2_
  66.3 0.9 collective-permute-start.18
  67.2 4.6 %collective-permute-done.12.refs_3_ = bf16[4,4,32,256]{3,2,1,0:T(8,128)(2,1)S(1)} collective-permute-done((bf16[4,4,32,256]{3,2,1,0:T(8,128)(2,1)S(1)}, bf16[4,4,32,256]{3,2,1,0:T(8,128)(2,1)S(1)}, u32[]{:S(2)}, u32[]{:S(2)}) %collective-permute-start.12) | collective-permute-done | bytes 262176 | tf_op jit(solution)/shard_map/ppermute | solution.py:33
  71.8 3.1 %column_forward_kernel.1 = (bf16[4,4,32,256]{3,2,1,0:T(8,128)(2,1)S(1)}, bf16[4,4,32,256]{3,2,1,0:T(8,128)(2,1)S(1)}, bf16[4,4,32,256]{3,2,1,0:T(8,128)(2,1)S(1)...) custom-call(s32[1]{0:T(128)} %bitcast.me_ref, bf16[32,64,64]{2,1,0:T(8,128)(2,1)S(1)} %copy-done.5, ...), custom_call_target="tpu_custom_call" | custom-call | flops 134217728 | bytes 4718592 | tf_op jit(solution)/shard_map/column_forward_kernel/pallas_call | solution.py:43
  74.9 0.2 collective-permute-start.13
  75.1 2.4 %collective-permute-done.17.refs_2_ = bf16[4,4,32,256]{3,2,1,0:T(8,128)(2,1)S(1)} collective-permute-done((bf16[4,4,32,256]{3,2,1,0:T(8,128)(2,1)S(1)}, bf16[4,4,32,256]{3,2,1,0:T(8,128)(2,1)S(1)}, u32[]{:S(2)}, u32[]{:S(2)}) %collective-permute-start.17) | collective-permute-done | bytes 262176 | tf_op jit(solution)/shard_map/ppermute | solution.py:33
  77.6 5.5 %collective-permute-done.18.refs_3_ = bf16[4,4,32,256]{3,2,1,0:T(8,128)(2,1)S(1)} collective-permute-done((bf16[4,4,32,256]{3,2,1,0:T(8,128)(2,1)S(1)}, bf16[4,4,32,256]{3,2,1,0:T(8,128)(2,1)S(1)}, u32[]{:S(2)}, u32[]{:S(2)}) %collective-permute-start.18) | collective-permute-done | bytes 262176 | tf_op jit(solution)/shard_map/ppermute | solution.py:33
  83.1 1.5 %collective-permute-start.20 = (bf16[4,4,32,256]{3,2,1,0:T(8,128)(2,1)S(1)}, bf16[4,4,32,256]{3,2,1,0:T(8,128)(2,1)S(1)}, u32[]{:S(2)}, u32[]{:S(2)}) collective-permute-start(bf16[4,4,32,256]{3,2,1,0:T(8,128)(2,1)S(1)} %get-tuple-element.86), channel_id=1, source_target_pairs={{0,8},{1,9},{2,10},{3,11},{4,12},{5,13},{6,14},{7,15},{8,0},{9,1},... | collective-permute-start | bytes 786440 | tf_op jit(solution)/shard_map/ppermute | solution.py:33
  84.6 1.5 %collective-permute-start.14 = (bf16[4,4,32,256]{3,2,1,0:T(8,128)(2,1)S(1)}, bf16[4,4,32,256]{3,2,1,0:T(8,128)(2,1)S(1)}, u32[]{:S(2)}, u32[]{:S(2)}) collective-permute-start(bf16[4,4,32,256]{3,2,1,0:T(8,128)(2,1)S(1)} %get-tuple-element.72), channel_id=1, source_target_pairs={{0,2},{1,3},{2,0},{3,1},{4,6},{5,7},{6,4},{7,5},{8,10},{9,11},{10,... | collective-permute-start | bytes 786440 | tf_op jit(solution)/shard_map/ppermute | solution.py:33
  86.2 1.3 collective-permute-start.21
  87.5 0.3 collective-permute-start.19
  87.9 6.0 %collective-permute-done.14.refs_2_ = bf16[4,4,32,256]{3,2,1,0:T(8,128)(2,1)S(1)} collective-permute-done((bf16[4,4,32,256]{3,2,1,0:T(8,128)(2,1)S(1)}, bf16[4,4,32,256]{3,2,1,0:T(8,128)(2,1)S(1)}, u32[]{:S(2)}, u32[]{:S(2)}) %collective-permute-start.14) | collective-permute-done | bytes 262176 | tf_op jit(solution)/shard_map/ppermute | solution.py:33
  93.8 3.7 %collective-permute-done.15.refs_3_ = bf16[4,4,32,256]{3,2,1,0:T(8,128)(2,1)S(1)} collective-permute-done((bf16[4,4,32,256]{3,2,1,0:T(8,128)(2,1)S(1)}, bf16[4,4,32,256]{3,2,1,0:T(8,128)(2,1)S(1)}, u32[]{:S(2)}, u32[]{:S(2)}) %collective-permute-start.15) | collective-permute-done | bytes 262176 | tf_op jit(solution)/shard_map/ppermute | solution.py:33
  97.6 6.2 %collective-permute-done.20.refs_2_ = bf16[4,4,32,256]{3,2,1,0:T(8,128)(2,1)S(1)} collective-permute-done((bf16[4,4,32,256]{3,2,1,0:T(8,128)(2,1)S(1)}, bf16[4,4,32,256]{3,2,1,0:T(8,128)(2,1)S(1)}, u32[]{:S(2)}, u32[]{:S(2)}) %collective-permute-start.20) | collective-permute-done | bytes 262176 | tf_op jit(solution)/shard_map/ppermute | solution.py:33
  103.8 3.3 %collective-permute-done.19.refs_1_ = bf16[4,4,32,256]{3,2,1,0:T(8,128)(2,1)S(1)} collective-permute-done((bf16[4,4,32,256]{3,2,1,0:T(8,128)(2,1)S(1)}, bf16[4,4,32,256]{3,2,1,0:T(8,128)(2,1)S(1)}, u32[]{:S(2)}, u32[]{:S(2)}) %collective-permute-start.19) | collective-permute-done | bytes 262176 | tf_op jit(solution)/shard_map/ppermute | solution.py:33
  107.1 0.1 gather_kernel.1
  107.2 0.6 collective-permute-start.25
  107.8 3.7 %collective-permute-start.23 = (bf16[4,4,32,256]{3,2,1,0:T(8,128)(2,1)S(1)}, bf16[4,4,32,256]{3,2,1,0:T(8,128)(2,1)S(1)}, u32[]{:S(2)}, u32[]{:S(2)}) collective-permute-start(bf16[4,4,32,256]{3,2,1,0:T(8,128)(2,1)S(1)} %get-tuple-element.90), channel_id=1, source_target_pairs={{0,8},{1,9},{2,10},{3,11},{4,12},{5,13},{6,14},{7,15},{8,0},{9,1},... | collective-permute-start | bytes 786440 | tf_op jit(solution)/shard_map/ppermute | solution.py:33
  111.6 1.3 collective-permute-start.24
  112.9 2.2 %row_backward_kernel.1 = (bf16[4,512,256]{2,1,0:T(8,128)(2,1)}, bf16[4,512,512]{2,1,0:T(8,128)(2,1)S(1)}) custom-call(s32[1]{0:T(128)} %bitcast.me_ref, bf16[4,512,512]{2,1,0:T(8,128)(2,1)S(1)} %copy-done, bf16[4,512,256]{2,1,0:T(8,128)(2,1)S(1)} %bitcast.12, bf16[4,512,256]{2,1,0:T(8,128)(2,1)S(1)} %bitcast.9), custom_call_target="tpu_custom_call" | custom-call | flops 1073741824 | bytes 7340032 | tf_op jit(solution)/shard_map/row_backward_kernel/pallas_call | solution.py:43
  115.2 1.5 %collective-permute-start.26 = (bf16[32,64,64]{2,1,0:T(8,128)(2,1)S(1)}, bf16[32,64,64]{2,1,0:T(8,128)(2,1)S(1)}, u32[]{:S(2)}, u32[]{:S(2)}) collective-permute-start(bf16[32,64,64]{2,1,0:T(8,128)(2,1)S(1)} %get-tuple-element.84.right_ref), channel_id=1, source_target_pairs={{0,16},{16,0},{1,17},{17,1},{2,18},{18,2},{3,19},{19,3},{4,20},{20... | collective-permute-start | bytes 786440 | tf_op jit(solution)/shard_map/ppermute | solution.py:17
  116.6 13.3 %collective-permute-done.23.refs_2_ = bf16[4,4,32,256]{3,2,1,0:T(8,128)(2,1)S(1)} collective-permute-done((bf16[4,4,32,256]{3,2,1,0:T(8,128)(2,1)S(1)}, bf16[4,4,32,256]{3,2,1,0:T(8,128)(2,1)S(1)}, u32[]{:S(2)}, u32[]{:S(2)}) %collective-permute-start.23) | collective-permute-done | bytes 262176 | tf_op jit(solution)/shard_map/ppermute | solution.py:33
  130.0 2.6 %collective-permute-done.22.refs_1_ = bf16[4,4,32,256]{3,2,1,0:T(8,128)(2,1)S(1)} collective-permute-done((bf16[4,4,32,256]{3,2,1,0:T(8,128)(2,1)S(1)}, bf16[4,4,32,256]{3,2,1,0:T(8,128)(2,1)S(1)}, u32[]{:S(2)}, u32[]{:S(2)}) %collective-permute-start.22) | collective-permute-done | bytes 262176 | tf_op jit(solution)/shard_map/ppermute | solution.py:33
  132.6 1.8 %output_kernel.1 = (bf16[4,16,32,256]{3,2,1,0:T(8,128)(2,1)}, bf16[4,16,32,256]{3,2,1,0:T(8,128)(2,1)}) custom-call(s32[1]{0:T(128)} %bitcast.me_ref, bf16[4,16,32,256]{3,2,1,0:T(8,128)(2,1)S(1)} %bitcast.14, bf16[4,16,32,256]{3,2,1,0:T(8,128)(2,1)S(1)} %bitcast.16, bf16[4,4,32,256]{3,2,1,0:T(8,128)(2,1)S(1)} %get-tuple-element.74.refs_0_, ...), custom_call_target="tpu_custom_call" | custom-call | bytes 5242880 | tf_op jit(solution)/shard_map/output_kernel/pallas_call | solution.py:43
  134.3 8.8 %collective-permute-done.26.other_ref = bf16[32,64,64]{2,1,0:T(8,128)(2,1)S(1)} collective-permute-done((bf16[32,64,64]{2,1,0:T(8,128)(2,1)S(1)}, bf16[32,64,64]{2,1,0:T(8,128)(2,1)S(1)}, u32[]{:S(2)}, u32[]{:S(2)}) %collective-permute-start.26) | collective-permute-done | bytes 262176 | tf_op jit(solution)/shard_map/ppermute | solution.py:17
  143.1 2.3 %factor_sum_kernel.1 = (bf16[4,512,512]{2,1,0:T(8,128)(2,1)}, bf16[32,64,64]{2,1,0:T(8,128)(2,1)}) custom-call(s32[1]{0:T(128)} %bitcast.me_ref, bf16[4,512,512]{2,1,0:T(8,128)(2,1)S(1)} %get-tuple-element.88.term_ref, bf16[4,512,256]{2,1,0:T(8,128)(2,1)S(1)} %collective-permute-done.6.after_ref.values_ref, ...), custom_call_target="tpu_custom_call" | custom-call | flops 536870912 | bytes 7077888 | tf_op jit(solution)/shard_map/factor_sum_kernel/pallas_call | solution.py:43
  (32 shorter events, 0.3 us)
Async XLA Ops:
  0.6 10.1 %copy-start = (bf16[4,512,512]{2,1,0:T(8,128)(2,1)S(1)}, bf16[4,512,512]{2,1,0:T(8,128)(2,1)}, u32[]{:S(2)}) copy-start(bf16[4,512,512]{2,1,0:T(8,128)(2,1)} %left_ref.3) | copy-start | bytes 6291460
  3.4 68.5 %collective-permute-start.6 = (bf16[4,512,256]{2,1,0:T(8,128)(2,1)}, bf16[4,512,256]{2,1,0:T(8,128)(2,1)S(1)}, u32[]{:S(2)}, u32[]{:S(2)}) collective-permute-start(bf16[4,512,256]{2,1,0:T(8,128)(2,1)} %bitcast.10), channel_id=1, source_target_pairs={{0,16},{16,0},{1,17},{17,1},{2,18},{18,2},{3,19},{19,3},{4,20},{20... | collective-permute-start | bytes 3145736 | tf_op jit(solution)/shard_map/ppermute | solution.py:17
  6.4 14.1 %collective-permute-start = (bf16[4,4,32,256]{3,2,1,0:T(8,128)(2,1)}, bf16[4,4,32,256]{3,2,1,0:T(8,128)(2,1)S(1)}, u32[]{:S(2)}, u32[]{:S(2)}) collective-permute-start(bf16[4,4,32,256]{3,2,1,0:T(8,128)(2,1)} %get-tuple-element.54), channel_id=1, source_target_pairs={{0,4},{1,5},{2,6},{3,7},{4,0},{5,1},{6,2},{7,3},{8,12},{9,13},{10,... | collective-permute-start | bytes 786440 | tf_op jit(solution)/shard_map/ppermute | solution.py:33
  7.9 21.6 %collective-permute-start.1 = (bf16[4,4,32,256]{3,2,1,0:T(8,128)(2,1)}, bf16[4,4,32,256]{3,2,1,0:T(8,128)(2,1)S(1)}, u32[]{:S(2)}, u32[]{:S(2)}) collective-permute-start(bf16[4,4,32,256]{3,2,1,0:T(8,128)(2,1)} %get-tuple-element.55), channel_id=1, source_target_pairs={{0,8},{1,9},{2,10},{3,11},{4,12},{5,13},{6,14},{7,15},{8,0},{9,1},... | collective-permute-start | bytes 786440 | tf_op jit(solution)/shard_map/ppermute | solution.py:33
  10.5 21.5 %collective-permute-start.2 = (bf16[4,4,32,256]{3,2,1,0:T(8,128)(2,1)}, bf16[4,4,32,256]{3,2,1,0:T(8,128)(2,1)S(1)}, u32[]{:S(2)}, u32[]{:S(2)}) collective-permute-start(bf16[4,4,32,256]{3,2,1,0:T(8,128)(2,1)} %get-tuple-element.56), channel_id=1, source_target_pairs={{0,12},{1,13},{2,14},{3,15},{4,8},{5,9},{6,10},{7,11},{8,4},{9,5},... | collective-permute-start | bytes 786440 | tf_op jit(solution)/shard_map/ppermute | solution.py:33
  10.7 1.2 copy-start.1
  12.0 20.1 %copy-start.6 = (bf16[4,4,32,256]{3,2,1,0:T(8,128)(2,1)S(1)}, bf16[4,4,32,256]{3,2,1,0:T(8,128)(2,1)}, u32[]{:S(2)}) copy-start(bf16[4,4,32,256]{3,2,1,0:T(8,128)(2,1)} %get-tuple-element.53.refs_0_) | copy-start | bytes 786436
  12.0 48.6 %copy-start.5 = (bf16[32,64,64]{2,1,0:T(8,128)(2,1)S(1)}, bf16[32,64,64]{2,1,0:T(8,128)(2,1)}, u32[]{:S(2)}) copy-start(bf16[32,64,64]{2,1,0:T(8,128)(2,1)} %right_ref.3) | copy-start | bytes 786436
  12.8 19.4 %collective-permute-start.7 = (bf16[4,4,32,256]{3,2,1,0:T(8,128)(2,1)S(1)}, bf16[4,4,32,256]{3,2,1,0:T(8,128)(2,1)S(1)}, u32[]{:S(2)}, u32[]{:S(2)}) collective-permute-start(bf16[4,4,32,256]{3,2,1,0:T(8,128)(2,1)S(1)} %get-tuple-element.63), channel_id=1, source_target_pairs={{0,4},{1,5},{2,6},{3,7},{4,0},{5,1},{6,2},{7,3},{8,12},{9,13},{10,... | collective-permute-start | bytes 786440 | tf_op jit(solution)/shard_map/ppermute | solution.py:33
  20.5 31.5 %collective-permute-start.8 = (bf16[4,4,32,256]{3,2,1,0:T(8,128)(2,1)S(1)}, bf16[4,4,32,256]{3,2,1,0:T(8,128)(2,1)S(1)}, u32[]{:S(2)}, u32[]{:S(2)}) collective-permute-start(bf16[4,4,32,256]{3,2,1,0:T(8,128)(2,1)S(1)} %get-tuple-element.64), channel_id=1, source_target_pairs={{0,8},{1,9},{2,10},{3,11},{4,12},{5,13},{6,14},{7,15},{8,0},{9,1},... | collective-permute-start | bytes 786440 | tf_op jit(solution)/shard_map/ppermute | solution.py:33
  29.6 22.5 %collective-permute-start.9 = (bf16[4,4,32,256]{3,2,1,0:T(8,128)(2,1)S(1)}, bf16[4,4,32,256]{3,2,1,0:T(8,128)(2,1)S(1)}, u32[]{:S(2)}, u32[]{:S(2)}) collective-permute-start(bf16[4,4,32,256]{3,2,1,0:T(8,128)(2,1)S(1)} %get-tuple-element.65), channel_id=1, source_target_pairs={{0,12},{1,13},{2,14},{3,15},{4,8},{5,9},{6,10},{7,11},{8,4},{9,5},... | collective-permute-start | bytes 786440 | tf_op jit(solution)/shard_map/ppermute | solution.py:33
  32.1 21.7 %collective-permute-start.3 = (bf16[4,4,32,256]{3,2,1,0:T(8,128)(2,1)S(1)}, bf16[4,4,32,256]{3,2,1,0:T(8,128)(2,1)S(1)}, u32[]{:S(2)}, u32[]{:S(2)}) collective-permute-start(bf16[4,4,32,256]{3,2,1,0:T(8,128)(2,1)S(1)} %get-tuple-element.58), channel_id=1, source_target_pairs={{0,1},{1,0},{2,3},{3,2},{4,5},{5,4},{6,7},{7,6},{8,9},{9,8},{10,11... | collective-permute-start | bytes 786440 | tf_op jit(solution)/shard_map/ppermute | solution.py:33
  32.2 22.1 %collective-permute-start.4 = (bf16[4,4,32,256]{3,2,1,0:T(8,128)(2,1)S(1)}, bf16[4,4,32,256]{3,2,1,0:T(8,128)(2,1)S(1)}, u32[]{:S(2)}, u32[]{:S(2)}) collective-permute-start(bf16[4,4,32,256]{3,2,1,0:T(8,128)(2,1)S(1)} %get-tuple-element.59), channel_id=1, source_target_pairs={{0,2},{1,3},{2,0},{3,1},{4,6},{5,7},{6,4},{7,5},{8,10},{9,11},{10,... | collective-permute-start | bytes 786440 | tf_op jit(solution)/shard_map/ppermute | solution.py:33
  52.0 8.5 %collective-permute-start.5 = (bf16[4,4,32,256]{3,2,1,0:T(8,128)(2,1)S(1)}, bf16[4,4,32,256]{3,2,1,0:T(8,128)(2,1)S(1)}, u32[]{:S(2)}, u32[]{:S(2)}) collective-permute-start(bf16[4,4,32,256]{3,2,1,0:T(8,128)(2,1)S(1)} %get-tuple-element.60), channel_id=1, source_target_pairs={{0,3},{1,2},{2,1},{3,0},{4,7},{5,6},{6,5},{7,4},{8,11},{9,10},{10,... | collective-permute-start | bytes 786440 | tf_op jit(solution)/shard_map/ppermute | solution.py:33
  52.1 11.6 %collective-permute-start.10 = (bf16[4,4,32,256]{3,2,1,0:T(8,128)(2,1)S(1)}, bf16[4,4,32,256]{3,2,1,0:T(8,128)(2,1)S(1)}, u32[]{:S(2)}, u32[]{:S(2)}) collective-permute-start(bf16[4,4,32,256]{3,2,1,0:T(8,128)(2,1)S(1)} %get-tuple-element.67), channel_id=1, source_target_pairs={{0,1},{1,0},{2,3},{3,2},{4,5},{5,4},{6,7},{7,6},{8,9},{9,8},{10,11... | collective-permute-start | bytes 786440 | tf_op jit(solution)/shard_map/ppermute | solution.py:33
  53.8 12.5 %collective-permute-start.11 = (bf16[4,4,32,256]{3,2,1,0:T(8,128)(2,1)S(1)}, bf16[4,4,32,256]{3,2,1,0:T(8,128)(2,1)S(1)}, u32[]{:S(2)}, u32[]{:S(2)}) collective-permute-start(bf16[4,4,32,256]{3,2,1,0:T(8,128)(2,1)S(1)} %get-tuple-element.68), channel_id=1, source_target_pairs={{0,2},{1,3},{2,0},{3,1},{4,6},{5,7},{6,4},{7,5},{8,10},{9,11},{10,... | collective-permute-start | bytes 786440 | tf_op jit(solution)/shard_map/ppermute | solution.py:33
  54.3 17.5 %collective-permute-start.12 = (bf16[4,4,32,256]{3,2,1,0:T(8,128)(2,1)S(1)}, bf16[4,4,32,256]{3,2,1,0:T(8,128)(2,1)S(1)}, u32[]{:S(2)}, u32[]{:S(2)}) collective-permute-start(bf16[4,4,32,256]{3,2,1,0:T(8,128)(2,1)S(1)} %get-tuple-element.69), channel_id=1, source_target_pairs={{0,3},{1,2},{2,1},{3,0},{4,7},{5,6},{6,5},{7,4},{8,11},{9,10},{10,... | collective-permute-start | bytes 786440 | tf_op jit(solution)/shard_map/ppermute | solution.py:33
  63.5 11.6 %collective-permute-start.16 = (bf16[4,4,32,256]{3,2,1,0:T(8,128)(2,1)S(1)}, bf16[4,4,32,256]{3,2,1,0:T(8,128)(2,1)S(1)}, u32[]{:S(2)}, u32[]{:S(2)}) collective-permute-start(bf16[4,4,32,256]{3,2,1,0:T(8,128)(2,1)S(1)} %get-tuple-element.78), channel_id=1, source_target_pairs={{0,1},{1,0},{2,3},{3,2},{4,5},{5,4},{6,7},{7,6},{8,9},{9,8},{10,11... | collective-permute-start | bytes 786440 | tf_op jit(solution)/shard_map/ppermute | solution.py:33
  63.7 13.9 %collective-permute-start.17 = (bf16[4,4,32,256]{3,2,1,0:T(8,128)(2,1)S(1)}, bf16[4,4,32,256]{3,2,1,0:T(8,128)(2,1)S(1)}, u32[]{:S(2)}, u32[]{:S(2)}) collective-permute-start(bf16[4,4,32,256]{3,2,1,0:T(8,128)(2,1)S(1)} %get-tuple-element.79), channel_id=1, source_target_pairs={{0,2},{1,3},{2,0},{3,1},{4,6},{5,7},{6,4},{7,5},{8,10},{9,11},{10,... | collective-permute-start | bytes 786440 | tf_op jit(solution)/shard_map/ppermute | solution.py:33
  66.3 16.7 %collective-permute-start.18 = (bf16[4,4,32,256]{3,2,1,0:T(8,128)(2,1)S(1)}, bf16[4,4,32,256]{3,2,1,0:T(8,128)(2,1)S(1)}, u32[]{:S(2)}, u32[]{:S(2)}) collective-permute-start(bf16[4,4,32,256]{3,2,1,0:T(8,128)(2,1)S(1)} %get-tuple-element.80), channel_id=1, source_target_pairs={{0,3},{1,2},{2,1},{3,0},{4,7},{5,6},{6,5},{7,4},{8,11},{9,10},{10,... | collective-permute-start | bytes 786440 | tf_op jit(solution)/shard_map/ppermute | solution.py:33
  74.9 12.6 %collective-permute-start.13 = (bf16[4,4,32,256]{3,2,1,0:T(8,128)(2,1)S(1)}, bf16[4,4,32,256]{3,2,1,0:T(8,128)(2,1)S(1)}, u32[]{:S(2)}, u32[]{:S(2)}) collective-permute-start(bf16[4,4,32,256]{3,2,1,0:T(8,128)(2,1)S(1)} %get-tuple-element.71), channel_id=1, source_target_pairs={{0,1},{1,0},{2,3},{3,2},{4,5},{5,4},{6,7},{7,6},{8,9},{9,8},{10,11... | collective-permute-start | bytes 786440 | tf_op jit(solution)/shard_map/ppermute | solution.py:33
  75.1 37.8 %copy-start.2 = (bf16[1,2048,256]{2,1,0:T(8,128)(2,1)S(1)}, bf16[1,2048,256]{2,1,0:T(8,128)(2,1)}, u32[]{:S(2)}) copy-start(bf16[1,2048,256]{2,1,0:T(8,128)(2,1)} %param.5) | copy-start | bytes 3145732
  83.1 20.7 %collective-permute-start.20 = (bf16[4,4,32,256]{3,2,1,0:T(8,128)(2,1)S(1)}, bf16[4,4,32,256]{3,2,1,0:T(8,128)(2,1)S(1)}, u32[]{:S(2)}, u32[]{:S(2)}) collective-permute-start(bf16[4,4,32,256]{3,2,1,0:T(8,128)(2,1)S(1)} %get-tuple-element.86), channel_id=1, source_target_pairs={{0,8},{1,9},{2,10},{3,11},{4,12},{5,13},{6,14},{7,15},{8,0},{9,1},... | collective-permute-start | bytes 786440 | tf_op jit(solution)/shard_map/ppermute | solution.py:33
  84.6 9.2 %collective-permute-start.14 = (bf16[4,4,32,256]{3,2,1,0:T(8,128)(2,1)S(1)}, bf16[4,4,32,256]{3,2,1,0:T(8,128)(2,1)S(1)}, u32[]{:S(2)}, u32[]{:S(2)}) collective-permute-start(bf16[4,4,32,256]{3,2,1,0:T(8,128)(2,1)S(1)} %get-tuple-element.72), channel_id=1, source_target_pairs={{0,2},{1,3},{2,0},{3,1},{4,6},{5,7},{6,4},{7,5},{8,10},{9,11},{10,... | collective-permute-start | bytes 786440 | tf_op jit(solution)/shard_map/ppermute | solution.py:33
  86.2 11.4 %collective-permute-start.15 = (bf16[4,4,32,256]{3,2,1,0:T(8,128)(2,1)S(1)}, bf16[4,4,32,256]{3,2,1,0:T(8,128)(2,1)S(1)}, u32[]{:S(2)}, u32[]{:S(2)}) collective-permute-start(bf16[4,4,32,256]{3,2,1,0:T(8,128)(2,1)S(1)} %get-tuple-element.73), channel_id=1, source_target_pairs={{0,3},{1,2},{2,1},{3,0},{4,7},{5,6},{6,5},{7,4},{8,11},{9,10},{10,... | collective-permute-start | bytes 786440 | tf_op jit(solution)/shard_map/ppermute | solution.py:33
  86.2 17.7 %collective-permute-start.21 = (bf16[4,4,32,256]{3,2,1,0:T(8,128)(2,1)S(1)}, bf16[4,4,32,256]{3,2,1,0:T(8,128)(2,1)S(1)}, u32[]{:S(2)}, u32[]{:S(2)}) collective-permute-start(bf16[4,4,32,256]{3,2,1,0:T(8,128)(2,1)S(1)} %get-tuple-element.87), channel_id=1, source_target_pairs={{0,12},{1,13},{2,14},{3,15},{4,8},{5,9},{6,10},{7,11},{8,4},{9,5},... | collective-permute-start | bytes 786440 | tf_op jit(solution)/shard_map/ppermute | solution.py:33
  87.5 19.6 %collective-permute-start.19 = (bf16[4,4,32,256]{3,2,1,0:T(8,128)(2,1)S(1)}, bf16[4,4,32,256]{3,2,1,0:T(8,128)(2,1)S(1)}, u32[]{:S(2)}, u32[]{:S(2)}) collective-permute-start(bf16[4,4,32,256]{3,2,1,0:T(8,128)(2,1)S(1)} %get-tuple-element.85), channel_id=1, source_target_pairs={{0,4},{1,5},{2,6},{3,7},{4,0},{5,1},{6,2},{7,3},{8,12},{9,13},{10,... | collective-permute-start | bytes 786440 | tf_op jit(solution)/shard_map/ppermute | solution.py:33
  107.2 35.9 %collective-permute-start.25 = (bf16[4,512,256]{2,1,0:T(8,128)(2,1)S(1)}, bf16[4,512,256]{2,1,0:T(8,128)(2,1)S(1)}, u32[]{:S(2)}, u32[]{:S(2)}) collective-permute-start(bf16[4,512,256]{2,1,0:T(8,128)(2,1)S(1)} %bitcast.8), channel_id=1, source_target_pairs={{0,16},{16,0},{1,17},{17,1},{2,18},{18,2},{3,19},{19,3},{4,20},{20... | collective-permute-start | bytes 3145736 | tf_op jit(solution)/shard_map/ppermute | solution.py:17
  107.8 22.2 %collective-permute-start.23 = (bf16[4,4,32,256]{3,2,1,0:T(8,128)(2,1)S(1)}, bf16[4,4,32,256]{3,2,1,0:T(8,128)(2,1)S(1)}, u32[]{:S(2)}, u32[]{:S(2)}) collective-permute-start(bf16[4,4,32,256]{3,2,1,0:T(8,128)(2,1)S(1)} %get-tuple-element.90), channel_id=1, source_target_pairs={{0,8},{1,9},{2,10},{3,11},{4,12},{5,13},{6,14},{7,15},{8,0},{9,1},... | collective-permute-start | bytes 786440 | tf_op jit(solution)/shard_map/ppermute | solution.py:33
  111.6 21.0 %copy-start.3 = (bf16[1,2048,256]{2,1,0:T(8,128)(2,1)S(1)}, bf16[1,2048,256]{2,1,0:T(8,128)(2,1)}, u32[]{:S(2)}) copy-start(bf16[1,2048,256]{2,1,0:T(8,128)(2,1)} %param.6) | copy-start | bytes 3145732
  111.6 21.0 %copy-start.4 = (bf16[1,2048,256]{2,1,0:T(8,128)(2,1)S(1)}, bf16[1,2048,256]{2,1,0:T(8,128)(2,1)}, u32[]{:S(2)}) copy-start(bf16[1,2048,256]{2,1,0:T(8,128)(2,1)} %param.7) | copy-start | bytes 3145732
  111.6 18.4 %collective-permute-start.24 = (bf16[4,4,32,256]{3,2,1,0:T(8,128)(2,1)S(1)}, bf16[4,4,32,256]{3,2,1,0:T(8,128)(2,1)S(1)}, u32[]{:S(2)}, u32[]{:S(2)}) collective-permute-start(bf16[4,4,32,256]{3,2,1,0:T(8,128)(2,1)S(1)} %get-tuple-element.91), channel_id=1, source_target_pairs={{0,12},{1,13},{2,14},{3,15},{4,8},{5,9},{6,10},{7,11},{8,4},{9,5},... | collective-permute-start | bytes 786440 | tf_op jit(solution)/shard_map/ppermute | solution.py:33
  115.2 17.4 %collective-permute-start.22 = (bf16[4,4,32,256]{3,2,1,0:T(8,128)(2,1)S(1)}, bf16[4,4,32,256]{3,2,1,0:T(8,128)(2,1)S(1)}, u32[]{:S(2)}, u32[]{:S(2)}) collective-permute-start(bf16[4,4,32,256]{3,2,1,0:T(8,128)(2,1)S(1)} %get-tuple-element.89), channel_id=1, source_target_pairs={{0,4},{1,5},{2,6},{3,7},{4,0},{5,1},{6,2},{7,3},{8,12},{9,13},{10,... | collective-permute-start | bytes 786440 | tf_op jit(solution)/shard_map/ppermute | solution.py:33
  115.2 28.0 %collective-permute-start.26 = (bf16[32,64,64]{2,1,0:T(8,128)(2,1)S(1)}, bf16[32,64,64]{2,1,0:T(8,128)(2,1)S(1)}, u32[]{:S(2)}, u32[]{:S(2)}) collective-permute-start(bf16[32,64,64]{2,1,0:T(8,128)(2,1)S(1)} %get-tuple-element.84.right_ref), channel_id=1, source_target_pairs={{0,16},{16,0},{1,17},{17,1},{2,18},{18,2},{3,19},{19,3},{4,20},{20... | collective-permute-start | bytes 786440 | tf_op jit(solution)/shard_map/ppermute | solution.py:17

commit v7 on v5

--- a/solution.py
+++ b/solution.py
@@ -20,21 +20,26 @@
     return lax.optimization_barrier((array, earlier))[0]
 
 
-def exchange(near, far):
-    half = len(far)
-    seq = 2 * half
-    groups = [list(range(half)), list(range(half, seq))]
-    near = lax.all_to_all(
-        near, "seq", split_axis=0, concat_axis=0, axis_index_groups=groups, tiled=True
-    )
-    far = [
-        lax.ppermute(block, "seq", [(i, i ^ (half + t)) for i in range(seq)])
-        for t, block in enumerate(far)
-    ]
-    return near, far
-
-
-def call(kernel, me, inputs, out_shapes, scratch=(), flops=0, unblocked=(), vmem=40):
+def far_first(count):
+    half = count // 2
+    far = [t for pair in zip(range(half, half + half // 2), range(half + half // 2, count)) for t in pair]
+    return far + list(range(half - 1, 0, -1))
+
+
+def permute(array, offset):
+    seq = lax.axis_size("seq")
+    return lax.ppermute(array, "seq", [(i, i ^ offset) for i in range(seq)])
+
+
+def exchange(messages):
+    return [messages[0]] + [permute(message, 2 * t) for t, message in list(enumerate(messages))[1:]]
+
+
+def listed(messages):
+    return [messages[t] for t in [0] + far_first(len(messages))]
+
+
+def call(kernel, me, inputs, out_shapes, scratch=(), flops=0, unblocked=(), vmem=32):
     whole = pl.BlockSpec(memory_space=pltpu.VMEM)
     moved = sum(x.size * x.dtype.itemsize for x in (*inputs, *out_shapes))
     in_specs = [
@@ -47,6 +52,7 @@
         out_specs=[whole] * len(out_shapes),
         scratch_shapes=scratch,
         compiler_params=pltpu.CompilerParams(vmem_limit_bytes=vmem * MIB),
+        name=getattr(kernel, "func", kernel).__name__,
         cost_estimate=pl.CostEstimate(flops=flops, bytes_accessed=moved, transcendentals=0),
     )(me, *inputs)
 
@@ -55,15 +61,18 @@
     return lax.dot_general(a, b, (contract, ((), ())), preferred_element_type=F32)
 
 
-def block_views(half, me, near_ref, far_refs):
-    base = me // half * half
-    near = [(base + p, near_ref.at[p]) for p in range(half)]
-    return near + [(me ^ (half + t), far_refs[t]) for t in range(half)]
-
-
-def send_kernel(half, me_ref, gate_hbm, cotangent_hbm, left_hbm, values_hbm, *refs):
-    near_ref, far_refs = refs[0], refs[1 : half + 1]
-    gate, cotangent, left, values, hold, sems = refs[half + 1 :]
+def block_views(me, refs):
+    return [(me ^ (2 * t + e), ref.at[t]) for e, ref in enumerate(refs) for t in range(ref.shape[0])]
+
+
+def received_views(me, refs):
+    order = [0] + far_first(len(refs))
+    return [(me ^ (2 * t + e), ref.at[e]) for t, ref in zip(order, refs) for e in range(2)]
+
+
+def send_kernel(me_ref, gate_hbm, cotangent_hbm, left_hbm, values_hbm, *refs):
+    out_refs = refs[:2]
+    gate, cotangent, left, values, hold, sems = refs[2:]
     rows, seq, cols, channels = hold.shape
     me = me_ref[0]
     loads = []
@@ -81,17 +90,23 @@
         hold[i] = mixed.astype(BF16).reshape(seq, cols, channels)
     loads[-2].wait()
     loads[-1].wait()
-    for c, ref in block_views(half, me, near_ref, far_refs):
+    for c, ref in block_views(me, out_refs):
         wide = gate[:, c].astype(F32) * cotangent[:, c].astype(F32)
         ref[0] = wide.astype(BF16)
         ref[1] = hold[:, c]
 
 
-def load_columns(half, me, near_ref, far_refs, which, wide):
-    rows, cols, channels = far_refs[0].shape[1:]
+def pack_kernel(me_ref, own_ref, other_ref, *out_refs):
+    for t, out_ref in enumerate(out_refs):
+        out_ref[0] = own_ref[t]
+        out_ref[1] = other_ref[t]
+
+
+def load_columns(blocks, wide):
+    rows, cols, channels = blocks[0][1].shape
     size = rows * cols
-    for c, ref in block_views(half, me, near_ref, far_refs):
-        block = ref[which].reshape(size, channels).astype(F32)
+    for c, ref in blocks:
+        block = ref[...].reshape(size, channels).astype(F32)
         start = pl.multiple_of(c * size, size)
         for h in range(channels // 128):
             wide[h, pl.ds(start, size), :] = block[:, h * 128 : (h + 1) * 128]
@@ -107,45 +122,45 @@
         wide[h, pl.ds(k, count, stride=cols), :] = value[:, h * 128 : (h + 1) * 128]
 
 
-def send_columns(half, me, wide, near_ref, far_refs):
-    rows, cols, channels = far_refs[0].shape
+def send_columns(wide, blocks):
+    rows, cols, channels = blocks[0][1].shape
     size = rows * cols
-    for c, ref in block_views(half, me, near_ref, far_refs):
+    for c, ref in blocks:
         start = pl.multiple_of(c * size, size)
         halves = [wide[h, pl.ds(start, size), :] for h in range(wide.shape[0])]
         block = jnp.concatenate(halves, axis=1).astype(BF16)
         ref[...] = block.reshape(rows, cols, channels)
 
 
-def column_backward_kernel(half, me_ref, right_ref, near_ref, *refs):
-    far_refs, near_out, far_out = refs[:half], refs[half], refs[half + 1 : 2 * half + 1]
-    by_column_ref, wide, wide_out = refs[2 * half + 1 :]
+def column_backward_kernel(chips, me_ref, right_ref, *refs):
+    in_refs, out_refs = refs[:chips], refs[chips : chips + 2]
+    by_column_ref, wide, wide_out = refs[chips + 2 :]
     cols, count, _ = right_ref.shape
     me = me_ref[0]
-    load_columns(half, me, near_ref, far_refs, 0, wide)
+    load_columns([(c, ref.at[0]) for c, ref in received_views(me, in_refs)], wide)
     for k in range(cols):
         grad = column(wide, k, count, cols)
         by_column_ref[k] = grad
         store_column(wide_out, k, count, cols, dot(right_ref[k], grad, ((0,), (0,))))
-    send_columns(half, me, wide_out, near_out, far_out)
-
-
-def column_forward_kernel(half, me_ref, right_ref, grad_ref, after_ref, near_ref, *refs):
-    far_refs, near_out, far_out = refs[:half], refs[half], refs[half + 1 : 2 * half + 1]
-    right_part_ref, wide, wide_out = refs[2 * half + 1 :]
+    send_columns(wide_out, block_views(me, out_refs))
+
+
+def column_forward_kernel(chips, me_ref, right_ref, grad_ref, after_ref, *refs):
+    in_refs, out_refs = refs[:chips], refs[chips : chips + 2]
+    right_part_ref, wide, wide_out = refs[chips + 2 :]
     cols, count, _ = right_ref.shape
     me = me_ref[0]
-    load_columns(half, me, near_ref, far_refs, 1, wide)
+    load_columns([(c, ref.at[1]) for c, ref in received_views(me, in_refs)], wide)
     for k in range(cols):
         mixed = column(wide, k, count, cols)
         store_column(wide_out, k, count, cols, dot(right_ref[k], mixed, ((1,), (0,))))
         right_part_ref[k] = dot(grad_ref[k], mixed, ((1,), (1,))).astype(BF16)
-    send_columns(half, me, wide_out, near_out, far_out)
-
-
-def gather_kernel(half, me_ref, near_ref, *refs):
-    for c, ref in block_views(half, me_ref[0], near_ref, refs[:half]):
-        refs[half][:, c] = ref[...]
+    send_columns(wide_out, block_views(me, out_refs))
+
+
+def gather_kernel(chips, me_ref, *refs):
+    for c, ref in received_views(me_ref[0], refs[:chips]):
+        refs[chips][:, c] = ref[...]
 
 
 def row_backward_kernel(me_ref, left_ref, values_ref, grad_ref, signal_ref, term_ref):
@@ -164,9 +179,9 @@
     right_out_ref[...] = (right_ref[...].astype(F32) + other_ref[...].astype(F32)).astype(BF16)
 
 
-def output_kernel(half, me_ref, gate_ref, cotangent_ref, near_ref, *refs):
-    far_refs, (out_ref, grad_ref) = refs[:half], refs[half:]
-    for c, ref in block_views(half, me_ref[0], near_ref, far_refs):
+def output_kernel(chips, me_ref, gate_ref, cotangent_ref, *refs):
+    out_ref, grad_ref = refs[chips:]
+    for c, ref in received_views(me_ref[0], refs[:chips]):
         second = ref[...].astype(F32)
         out_ref[:, c] = (gate_ref[:, c].astype(F32) * second).astype(BF16)
         grad_ref[:, c] = (cotangent_ref[:, c].astype(F32) * second).astype(BF16)
@@ -174,7 +189,7 @@
 
 def direct_shards(signal, gating, upstream, left_factor, right_factor):
     seq = lax.axis_size("seq")
-    half = seq // 2
+    chips = seq // 2
     rows, block_len = left_factor.shape[:2]
     cols, count = right_factor.shape[:2]
     channels = signal.shape[2]
@@ -186,12 +201,10 @@
     def shape(*dims):
         return jax.ShapeDtypeStruct(dims, BF16)
 
-    def with_half(kernel):
-        return functools.partial(kernel, half)
+    def on_chips(kernel):
+        return functools.partial(kernel, chips)
 
     block = (rows, cols, channels)
-    pairs = [shape(half, 2, *block)] + [shape(2, *block)] * half
-    blocks = [shape(half, *block)] + [shape(*block)] * half
     whole = shape(rows, seq, cols, channels)
     by_row = shape(rows, block_len, channels)
     left = shape(*left_factor.shape)
@@ -200,41 +213,49 @@
     row_flops = 2 * rows * block_len * block_len * channels
     column_flops = 2 * cols * count * count * channels
 
-    near, *far = call(
-        with_half(send_kernel),
+    def pack(own, other):
+        message = shape(2, *own.shape[1:])
+        return list(call(pack_kernel, me, [own, permute(other, 1)], [message] * chips))
+
+    own, other = call(
+        send_kernel,
         me,
         [gate, cotangent, left_factor, values],
-        pairs,
+        [shape(chips, 2, *block)] * 2,
         [pltpu.VMEM(x.shape, BF16) for x in (gate, cotangent, left_factor, values, whole)]
         + [pltpu.SemaphoreType.DMA((3, max(rows, 2)))],
         row_flops,
         unblocked=range(4),
         vmem=60,
     )
-    other_values = swap_sequences(after(values, near))
-    near, far = exchange(near, far)
-    *second_in, grad_column = call(
-        with_half(column_backward_kernel),
-        me,
-        [right_factor, near, *far],
-        blocks + [shape(cols, count, channels)],
+    messages = pack(own, other)
+    other_values = swap_sequences(after(values, messages[0]))
+    columns = listed(exchange(messages))
+    own, other, grad_column = call(
+        on_chips(column_backward_kernel),
+        me,
+        [right_factor, *columns],
+        [shape(chips, *block)] * 2 + [shape(cols, count, channels)],
         [wide, wide],
         column_flops,
     )
-    back_near, *back_far = second_in
-    second_near, *second_far, right_part = call(
-        with_half(column_forward_kernel),
-        me,
-        [right_factor, grad_column, other_values, near, *far],
-        blocks + [right],
+    messages = pack(own, other)
+    own, other, right_part = call(
+        on_chips(column_forward_kernel),
+        me,
+        [right_factor, grad_column, other_values, *columns],
+        [shape(chips, *block)] * 2 + [right],
         [wide, wide],
         2 * column_flops,
         unblocked=[2],
     )
+    second_messages = pack(own, other)
+    for t in range(1, chips // 2):
+        messages[t] = after(messages[t], second_messages[0])
+    back = listed(exchange(messages))
     other_right = swap_sequences(right_part)
-    back_far[half // 2 :] = [after(x, right_part) for x in back_far[half // 2 :]]
-    back_near, back_far = exchange(back_near, back_far)
-    (gathered,) = call(with_half(gather_kernel), me, [back_near, *back_far], [whole])
+    back[0] = after(back[0], other_right)
+    (gathered,) = call(on_chips(gather_kernel), me, back, [whole])
     grad_back = gathered.reshape(rows, block_len, channels)
     other_grad_back = swap_sequences(grad_back)
     grad_signal, left_term = call(
@@ -244,8 +265,9 @@
         [by_row, left],
         flops=2 * row_flops,
     )
-    second_far[half // 2 :] = [after(x, left_term) for x in second_far[half // 2 :]]
-    second_near, second_far = exchange(second_near, second_far)
+    for t in range(1, chips // 2):
+        second_messages[t] = after(second_messages[t], left_term)
+    second = listed(exchange(second_messages))
     grad_left, grad_right = call(
         factor_sum_kernel,
         me,
@@ -254,7 +276,7 @@
         flops=row_flops,
     )
     output, grad_gate = call(
-        with_half(output_kernel), me, [gate, cotangent, second_near, *second_far], [whole, whole]
+        on_chips(output_kernel), me, [gate, cotangent, *second], [whole, whole]
     )
     return (
         output.reshape(signal.shape),
@@ -317,7 +339,7 @@
 def shards(signal, gating, upstream, left_factor, right_factor):
     seq = lax.axis_size("seq")
     cols = right_factor.shape[0]
-    direct = seq <= 16 and seq & (seq - 1) == 0 and cols % 32 == 0
+    direct = seq in (8, 16) and cols % 32 == 0
     run = direct_shards if direct else plain_shards
     return run(signal, gating, upstream, left_factor, right_factor)
 

time: 174 us -> 136 us (0.78); the launches traced: 172 us -> 136 us
  waiting for transfers between devices: 19.9 us -> 73.7 us
  starting transfers between devices: 90.6 us -> 43.5 us
  local copies, waits for them, and re-layouts: 39.3 us -> 1.25 us
  Pallas kernels: 21 us -> 17.2 us
    ppermute x24, waiting for transfers between devices: 19.9 us -> 73.7 us  [permute(): return lax.ppermute(array, 'seq', [(i, i ^ offset) for i in range(seq)])]
    unnamed x126 -> x12, local copies, waits for them, and re-layouts: 39.3 us -> 1.25 us
    ppermute x24, starting transfers between devices: 69.3 us -> 38.4 us  [permute(): return lax.ppermute(array, 'seq', [(i, i ^ offset) for i in range(seq)])]
    all_to_all x3 -> x0, starting transfers between devices: 17.5 us -> none  [exchange(): lax.all_to_all(near, 'seq', split_axis=0, concat_axis=0, axis_index_group...]
    pallas_call x7 -> x10, Pallas kernels: 21 us -> 17.2 us  [call(): pl.pallas_call(kernel, out_shape=out_shapes, in_specs=[pl.BlockSpec(memor...]
  transfers between devices with their start and end apart: 30 -> 27, of which waited for: 9 -> 16; matrix products, arithmetic and copies ran while one was open for 0% -> 0% of each run, Pallas kernels for 7% -> 8%
where the time goes in v7:
time: 136 us
  waiting for transfers between devices  73.7 us (54%)
  starting transfers between devices  43.5 us (32%)
  Pallas kernels  17.2 us (13%)
    ppermute x24, waiting for transfers between devices, permute(): return lax.ppermute(array, 'seq', [(i, i ^ offset) for i in range(seq)])  73.7 us
    ppermute x24, starting transfers between devices, permute(): return lax.ppermute(array, 'seq', [(i, i ^ offset) for i in range(seq)])  38.4 us
    pallas_call x10, Pallas kernels, call(): pl.pallas_call(kernel, out_shape=out_shapes, in_specs=[pl.BlockSpec(memor...  17.2 us
    ppermute x3, starting transfers between devices, swap_sequences(): return lax.ppermute(array, 'dp', [(0, 1), (1, 0)])  5.05 us
  transfers between devices with their start and end apart: 27, of which 16 were waited for; matrix products, arithmetic and copies ran while one was open for 0% of the time, Pallas kernels for 8%

profile of v7, /device:TPU:0, one launch (start us, length us, event | category | flops | bytes accessed | tf_op | source)
XLA Modules:
  0.0 136.3 jit_solution(17885793559796011356)
XLA Ops:
  0.6 4.4 %send_kernel.1 = (bf16[8,2,4,32,256]{4,3,2,1,0:T(8,128)(2,1)}, bf16[8,2,4,32,256]{4,3,2,1,0:T(8,128)(2,1)}) custom-call(s32[1]{0:T(128)} %bitcast.me_ref, bf16[4,16,32,256]{3,2,1,0:T(8,128)(2,1)} %bitcast.13, bf16[4,16,32,256]{3,2,1,0:T(8,128)(2,1)} %bitcast.15, bf16[4,512,512]{2,1,0:T(8,128)(2,1)} %left_ref.1, bf16[4,512,256]{2,1,0:T(8,128)(2,1)} %bitcast.10), custom_call_target="tpu_custom_call" | custom-call | flops 536870912 | bytes 7340032 | tf_op jit(solution)/shard_map/send_kernel/pallas_call | solution.py:48
  5.1 0.5 collective-permute-start
  5.6 2.5 %collective-permute-done.other_ref = bf16[8,2,4,32,256]{4,3,2,1,0:T(8,128)(2,1)S(1)} collective-permute-done((bf16[8,2,4,32,256]{4,3,2,1,0:T(8,128)(2,1)}, bf16[8,2,4,32,256]{4,3,2,1,0:T(8,128)(2,1)S(1)}, u32[]{:S(2)}, u32[]{:S(2)}) %collective-permute-start) | collective-permute-done | bytes 1048608 | tf_op jit(solution)/shard_map/ppermute | solution.py:31
  8.1 1.2 copy-done.5
  9.5 2.9 %collective-permute-start.8 = (bf16[4,512,256]{2,1,0:T(8,128)(2,1)S(1)}, bf16[4,512,256]{2,1,0:T(8,128)(2,1)S(1)}, u32[]{:S(2)}, u32[]{:S(2)}) collective-permute-start(bf16[4,512,256]{2,1,0:T(8,128)(2,1)S(1)} %bitcast.11), channel_id=1, source_target_pairs={{0,16},{16,0},{1,17},{17,1},{2,18},{18,2},{3,19},{19,3},{4,20},{20... | collective-permute-start | bytes 3145736 | tf_op jit(solution)/shard_map/ppermute | solution.py:16
  12.4 2.6 %collective-permute-start.1 = (bf16[2,2,4,32,256]{4,3,2,1,0:T(8,128)(2,1)S(1)}, bf16[2,2,4,32,256]{4,3,2,1,0:T(8,128)(2,1)S(1)}, u32[]{:S(2)}, u32[]{:S(2)}) collective-permute-start(bf16[2,2,4,32,256]{4,3,2,1,0:T(8,128)(2,1)S(1)} %get-tuple-element.54), channel_id=1, source_target_pairs={{0,8},{1,9},{2,10},{3,11},{4,12},{5,13},{6,14},{7,15},{8,0},{9,1},... | collective-permute-start | bytes 786440 | tf_op jit(solution)/shard_map/ppermute | solution.py:31
  15.0 1.3 collective-permute-start.2
  16.3 2.6 %collective-permute-start.3 = (bf16[2,2,4,32,256]{4,3,2,1,0:T(8,128)(2,1)S(1)}, bf16[2,2,4,32,256]{4,3,2,1,0:T(8,128)(2,1)S(1)}, u32[]{:S(2)}, u32[]{:S(2)}) collective-permute-start(bf16[2,2,4,32,256]{4,3,2,1,0:T(8,128)(2,1)S(1)} %get-tuple-element.56), channel_id=1, source_target_pairs={{0,10},{1,11},{2,8},{3,9},{4,14},{5,15},{6,12},{7,13},{8,2},{9,3},... | collective-permute-start | bytes 786440 | tf_op jit(solution)/shard_map/ppermute | solution.py:31
  19.0 0.8 collective-permute-start.4
  19.8 25.1 %collective-permute-done.1.refs_1_ = bf16[2,2,4,32,256]{4,3,2,1,0:T(8,128)(2,1)S(1)} collective-permute-done((bf16[2,2,4,32,256]{4,3,2,1,0:T(8,128)(2,1)S(1)}, bf16[2,2,4,32,256]{4,3,2,1,0:T(8,128)(2,1)S(1)}, u32[]{:S(2)}, u32[]{:S(2)}) %collective-permute-start.1) | collective-permute-done | bytes 262176 | tf_op jit(solution)/shard_map/ppermute | solution.py:31
  44.9 0.6 collective-permute-start.5
  45.5 5.6 %collective-permute-start.6 = (bf16[2,2,4,32,256]{4,3,2,1,0:T(8,128)(2,1)S(1)}, bf16[2,2,4,32,256]{4,3,2,1,0:T(8,128)(2,1)S(1)}, u32[]{:S(2)}, u32[]{:S(2)}) collective-permute-start(bf16[2,2,4,32,256]{4,3,2,1,0:T(8,128)(2,1)S(1)} %get-tuple-element.59), channel_id=1, source_target_pairs={{0,4},{1,5},{2,6},{3,7},{4,0},{5,1},{6,2},{7,3},{8,12},{9,13},{10,... | collective-permute-start | bytes 786440 | tf_op jit(solution)/shard_map/ppermute | solution.py:31
  51.1 6.1 %collective-permute-done.3.refs_3_ = bf16[2,2,4,32,256]{4,3,2,1,0:T(8,128)(2,1)S(1)} collective-permute-done((bf16[2,2,4,32,256]{4,3,2,1,0:T(8,128)(2,1)S(1)}, bf16[2,2,4,32,256]{4,3,2,1,0:T(8,128)(2,1)S(1)}, u32[]{:S(2)}, u32[]{:S(2)}) %collective-permute-start.3) | collective-permute-done | bytes 262176 | tf_op jit(solution)/shard_map/ppermute | solution.py:31
  57.2 0.5 collective-permute-start.7
  57.7 1.7 %collective-permute-done.5.refs_5_ = bf16[2,2,4,32,256]{4,3,2,1,0:T(8,128)(2,1)S(1)} collective-permute-done((bf16[2,2,4,32,256]{4,3,2,1,0:T(8,128)(2,1)S(1)}, bf16[2,2,4,32,256]{4,3,2,1,0:T(8,128)(2,1)S(1)}, u32[]{:S(2)}, u32[]{:S(2)}) %collective-permute-start.5) | collective-permute-done | bytes 262176 | tf_op jit(solution)/shard_map/ppermute | solution.py:31
  59.3 3.9 %collective-permute-done.6.refs_6_ = bf16[2,2,4,32,256]{4,3,2,1,0:T(8,128)(2,1)S(1)} collective-permute-done((bf16[2,2,4,32,256]{4,3,2,1,0:T(8,128)(2,1)S(1)}, bf16[2,2,4,32,256]{4,3,2,1,0:T(8,128)(2,1)S(1)}, u32[]{:S(2)}, u32[]{:S(2)}) %collective-permute-start.6) | collective-permute-done | bytes 262176 | tf_op jit(solution)/shard_map/ppermute | solution.py:31
  63.2 0.9 collective-permute-done.7.refs_7_
  64.1 3.0 %column_backward_kernel.1 = (bf16[8,4,32,256]{3,2,1,0:T(8,128)(2,1)S(1)}, bf16[8,4,32,256]{3,2,1,0:T(8,128)(2,1)S(1)}, bf16[32,64,256]{2,1,0:T(8,128)(2,1)S(1)}) custom-call(s32[1]{0:T(128)} %bitcast.me_ref, bf16[32,64,64]{2,1,0:T(8,128)(2,1)S(1)} %copy-done.4, bf16[2,2,4,32,256]{4,3,2,1,0:T(8,128)(2,1)S(1)} %get-tuple-element.53.refs_0_, ...), custom_call_target="tpu_custom_call" | custom-call | flops 67108864 | bytes 4456448 | tf_op jit(solution)/shard_map/column_backward_kernel/pallas_call | solution.py:48
  67.2 3.1 %column_forward_kernel.1 = (bf16[8,4,32,256]{3,2,1,0:T(8,128)(2,1)S(1)}, bf16[8,4,32,256]{3,2,1,0:T(8,128)(2,1)S(1)}, bf16[32,64,64]{2,1,0:T(8,128)(2,1)S(1)}) custom-call(s32[1]{0:T(128)} %bitcast.me_ref, bf16[32,64,64]{2,1,0:T(8,128)(2,1)S(1)} %copy-done.4, bf16[32,64,256]{2,1,0:T(8,128)(2,1)S(1)} %get-tuple-element.61.grad_ref, ...), custom_call_target="tpu_custom_call" | custom-call | flops 134217728 | bytes 5767168 | tf_op jit(solution)/shard_map/column_forward_kernel/pallas_call | solution.py:48
  70.3 0.5 collective-permute-start.9
  70.9 0.6 collective-permute-start.15
  71.5 3.6 %collective-permute-start.16 = (bf16[2,4,32,256]{3,2,1,0:T(8,128)(2,1)S(1)}, bf16[2,4,32,256]{3,2,1,0:T(8,128)(2,1)S(1)}, u32[]{:S(2)}, u32[]{:S(2)}) collective-permute-start(bf16[2,4,32,256]{3,2,1,0:T(8,128)(2,1)S(1)} %get-tuple-element.76), channel_id=1, source_target_pairs={{0,8},{1,9},{2,10},{3,11},{4,12},{5,13},{6,14},{7,15},{8,0},{9,1},... | collective-permute-start | bytes 393224 | tf_op jit(solution)/shard_map/ppermute | solution.py:31
  75.1 2.5 %collective-permute-start.17 = (bf16[2,4,32,256]{3,2,1,0:T(8,128)(2,1)S(1)}, bf16[2,4,32,256]{3,2,1,0:T(8,128)(2,1)S(1)}, u32[]{:S(2)}, u32[]{:S(2)}) collective-permute-start(bf16[2,4,32,256]{3,2,1,0:T(8,128)(2,1)S(1)} %get-tuple-element.77), channel_id=1, source_target_pairs={{0,12},{1,13},{2,14},{3,15},{4,8},{5,9},{6,10},{7,11},{8,4},{9,5},... | collective-permute-start | bytes 393224 | tf_op jit(solution)/shard_map/ppermute | solution.py:31
  77.6 0.5 collective-permute-start.18
  78.1 1.5 %collective-permute-start.19 = (bf16[2,4,32,256]{3,2,1,0:T(8,128)(2,1)S(1)}, bf16[2,4,32,256]{3,2,1,0:T(8,128)(2,1)S(1)}, u32[]{:S(2)}, u32[]{:S(2)}) collective-permute-start(bf16[2,4,32,256]{3,2,1,0:T(8,128)(2,1)S(1)} %get-tuple-element.79), channel_id=1, source_target_pairs={{0,14},{1,15},{2,12},{3,13},{4,10},{5,11},{6,8},{7,9},{8,6},{9,7},... | collective-permute-start | bytes 393224 | tf_op jit(solution)/shard_map/ppermute | solution.py:31
  79.7 10.9 %collective-permute-done.16.refs_1_ = bf16[2,4,32,256]{3,2,1,0:T(8,128)(2,1)S(1)} collective-permute-done((bf16[2,4,32,256]{3,2,1,0:T(8,128)(2,1)S(1)}, bf16[2,4,32,256]{3,2,1,0:T(8,128)(2,1)S(1)}, u32[]{:S(2)}, u32[]{:S(2)}) %collective-permute-start.16) | collective-permute-done | bytes 131104 | tf_op jit(solution)/shard_map/ppermute | solution.py:31
  90.7 1.3 collective-permute-start.22
  92.0 2.1 %collective-permute-start.21 = (bf16[2,4,32,256]{3,2,1,0:T(8,128)(2,1)S(1)}, bf16[2,4,32,256]{3,2,1,0:T(8,128)(2,1)S(1)}, u32[]{:S(2)}, u32[]{:S(2)}) collective-permute-start(bf16[2,4,32,256]{3,2,1,0:T(8,128)(2,1)S(1)} %get-tuple-element.83), channel_id=1, source_target_pairs={{0,4},{1,5},{2,6},{3,7},{4,0},{5,1},{6,2},{7,3},{8,12},{9,13},{10,... | collective-permute-start | bytes 393224 | tf_op jit(solution)/shard_map/ppermute | solution.py:31
  94.0 0.7 collective-permute-start.20
  94.8 2.3 %collective-permute-done.18.refs_3_ = bf16[2,4,32,256]{3,2,1,0:T(8,128)(2,1)S(1)} collective-permute-done((bf16[2,4,32,256]{3,2,1,0:T(8,128)(2,1)S(1)}, bf16[2,4,32,256]{3,2,1,0:T(8,128)(2,1)S(1)}, u32[]{:S(2)}, u32[]{:S(2)}) %collective-permute-start.18) | collective-permute-done | bytes 131104 | tf_op jit(solution)/shard_map/ppermute | solution.py:31
  97.1 0.5 collective-permute-done.22.refs_7_
  97.6 1.3 collective-permute-done.21.refs_6_
  98.8 2.8 %collective-permute-done.20.refs_5_ = bf16[2,4,32,256]{3,2,1,0:T(8,128)(2,1)S(1)} collective-permute-done((bf16[2,4,32,256]{3,2,1,0:T(8,128)(2,1)S(1)}, bf16[2,4,32,256]{3,2,1,0:T(8,128)(2,1)S(1)}, u32[]{:S(2)}, u32[]{:S(2)}) %collective-permute-start.20) | collective-permute-done | bytes 131104 | tf_op jit(solution)/shard_map/ppermute | solution.py:31
  101.7 1.6 %collective-permute-start.26 = (bf16[4,512,256]{2,1,0:T(8,128)(2,1)S(1)}, bf16[4,512,256]{2,1,0:T(8,128)(2,1)S(1)}, u32[]{:S(2)}, u32[]{:S(2)}) collective-permute-start(bf16[4,512,256]{2,1,0:T(8,128)(2,1)S(1)} %bitcast.8), channel_id=1, source_target_pairs={{0,16},{16,0},{1,17},{17,1},{2,18},{18,2},{3,19},{19,3},{4,20},{20... | collective-permute-start | bytes 3145736 | tf_op jit(solution)/shard_map/ppermute | solution.py:16
  103.3 2.0 %collective-permute-start.10 = (bf16[2,4,32,256]{3,2,1,0:T(8,128)(2,1)S(1)}, bf16[2,4,32,256]{3,2,1,0:T(8,128)(2,1)S(1)}, u32[]{:S(2)}, u32[]{:S(2)}) collective-permute-start(bf16[2,4,32,256]{3,2,1,0:T(8,128)(2,1)S(1)} %get-tuple-element.66), channel_id=1, source_target_pairs={{0,8},{1,9},{2,10},{3,11},{4,12},{5,13},{6,14},{7,15},{8,0},{9,1},... | collective-permute-start | bytes 393224 | tf_op jit(solution)/shard_map/ppermute | solution.py:31
  105.3 1.0 collective-permute-start.11
  106.3 2.5 %collective-permute-start.12 = (bf16[2,4,32,256]{3,2,1,0:T(8,128)(2,1)S(1)}, bf16[2,4,32,256]{3,2,1,0:T(8,128)(2,1)S(1)}, u32[]{:S(2)}, u32[]{:S(2)}) collective-permute-start(bf16[2,4,32,256]{3,2,1,0:T(8,128)(2,1)S(1)} %get-tuple-element.68), channel_id=1, source_target_pairs={{0,10},{1,11},{2,8},{3,9},{4,14},{5,15},{6,12},{7,13},{8,2},{9,3},... | collective-permute-start | bytes 393224 | tf_op jit(solution)/shard_map/ppermute | solution.py:31
  108.8 1.3 collective-permute-start.13
  110.2 2.2 %row_backward_kernel.1 = (bf16[4,512,256]{2,1,0:T(8,128)(2,1)}, bf16[4,512,512]{2,1,0:T(8,128)(2,1)S(1)}) custom-call(s32[1]{0:T(128)} %bitcast.me_ref, bf16[4,512,512]{2,1,0:T(8,128)(2,1)S(1)} %copy-done, bf16[4,512,256]{2,1,0:T(8,128)(2,1)S(1)} %bitcast.12, bf16[4,512,256]{2,1,0:T(8,128)(2,1)S(1)} %bitcast.9), custom_call_target="tpu_custom_call" | custom-call | flops 1073741824 | bytes 7340032 | tf_op jit(solution)/shard_map/row_backward_kernel/pallas_call | solution.py:48
  112.4 8.4 %collective-permute-done.10.refs_1_ = bf16[2,4,32,256]{3,2,1,0:T(8,128)(2,1)S(1)} collective-permute-done((bf16[2,4,32,256]{3,2,1,0:T(8,128)(2,1)S(1)}, bf16[2,4,32,256]{3,2,1,0:T(8,128)(2,1)S(1)}, u32[]{:S(2)}, u32[]{:S(2)}) %collective-permute-start.10) | collective-permute-done | bytes 131104 | tf_op jit(solution)/shard_map/ppermute | solution.py:31
  120.9 3.2 %collective-permute-start.24 = (bf16[2,4,32,256]{3,2,1,0:T(8,128)(2,1)S(1)}, bf16[2,4,32,256]{3,2,1,0:T(8,128)(2,1)S(1)}, u32[]{:S(2)}, u32[]{:S(2)}) collective-permute-start(bf16[2,4,32,256]{3,2,1,0:T(8,128)(2,1)S(1)} %get-tuple-element.89), channel_id=1, source_target_pairs={{0,4},{1,5},{2,6},{3,7},{4,0},{5,1},{6,2},{7,3},{8,12},{9,13},{10,... | collective-permute-start | bytes 393224 | tf_op jit(solution)/shard_map/ppermute | solution.py:31
  124.1 3.1 %collective-permute-done.12.refs_3_ = bf16[2,4,32,256]{3,2,1,0:T(8,128)(2,1)S(1)} collective-permute-done((bf16[2,4,32,256]{3,2,1,0:T(8,128)(2,1)S(1)}, bf16[2,4,32,256]{3,2,1,0:T(8,128)(2,1)S(1)}, u32[]{:S(2)}, u32[]{:S(2)}) %collective-permute-start.12) | collective-permute-done | bytes 131104 | tf_op jit(solution)/shard_map/ppermute | solution.py:31
  127.2 0.7 collective-permute-start.25
  127.9 1.2 collective-permute-done.23.refs_5_
  129.1 0.9 collective-permute-done.24.refs_6_
  130.0 2.2 %collective-permute-done.25.refs_7_ = bf16[2,4,32,256]{3,2,1,0:T(8,128)(2,1)S(1)} collective-permute-done((bf16[2,4,32,256]{3,2,1,0:T(8,128)(2,1)S(1)}, bf16[2,4,32,256]{3,2,1,0:T(8,128)(2,1)S(1)}, u32[]{:S(2)}, u32[]{:S(2)}) %collective-permute-start.25) | collective-permute-done | bytes 131104 | tf_op jit(solution)/shard_map/ppermute | solution.py:31
  132.2 1.8 %output_kernel.1 = (bf16[4,16,32,256]{3,2,1,0:T(8,128)(2,1)}, bf16[4,16,32,256]{3,2,1,0:T(8,128)(2,1)}) custom-call(s32[1]{0:T(128)} %bitcast.me_ref, bf16[4,16,32,256]{3,2,1,0:T(8,128)(2,1)S(1)} %bitcast.14, bf16[4,16,32,256]{3,2,1,0:T(8,128)(2,1)S(1)} %bitcast.16, bf16[2,4,32,256]{3,2,1,0:T(8,128)(2,1)S(1)} %get-tuple-element.65.refs_0_, ...), custom_call_target="tpu_custom_call" | custom-call | bytes 5242880 | tf_op jit(solution)/shard_map/output_kernel/pallas_call | solution.py:48
  134.0 2.3 %factor_sum_kernel.1 = (bf16[4,512,512]{2,1,0:T(8,128)(2,1)}, bf16[32,64,64]{2,1,0:T(8,128)(2,1)}) custom-call(s32[1]{0:T(128)} %bitcast.me_ref, bf16[4,512,512]{2,1,0:T(8,128)(2,1)S(1)} %get-tuple-element.86.term_ref, bf16[4,512,256]{2,1,0:T(8,128)(2,1)S(1)} %collective-permute-done.8.after_ref.values_ref, ...), custom_call_target="tpu_custom_call" | custom-call | flops 536870912 | bytes 7077888 | tf_op jit(solution)/shard_map/factor_sum_kernel/pallas_call | solution.py:48
  (28 shorter events, 0.6 us)
Async XLA Ops:
  5.0 4.4 %copy-start.1 = (bf16[1,2048,256]{2,1,0:T(8,128)(2,1)S(1)}, bf16[1,2048,256]{2,1,0:T(8,128)(2,1)}, u32[]{:S(2)}) copy-start(bf16[1,2048,256]{2,1,0:T(8,128)(2,1)} %param.5) | copy-start | bytes 3145732
  5.1 59.1 %copy-start.4 = (bf16[32,64,64]{2,1,0:T(8,128)(2,1)S(1)}, bf16[32,64,64]{2,1,0:T(8,128)(2,1)}, u32[]{:S(2)}) copy-start(bf16[32,64,64]{2,1,0:T(8,128)(2,1)} %right_ref.3) | copy-start | bytes 786436
  5.1 3.0 %collective-permute-start = (bf16[8,2,4,32,256]{4,3,2,1,0:T(8,128)(2,1)}, bf16[8,2,4,32,256]{4,3,2,1,0:T(8,128)(2,1)S(1)}, u32[]{:S(2)}, u32[]{:S(2)}) collective-permute-start(bf16[8,2,4,32,256]{4,3,2,1,0:T(8,128)(2,1)} %get-tuple-element.52), channel_id=1, source_target_pairs={{0,1},{1,0},{2,3},{3,2},{4,5},{5,4},{6,7},{7,6},{8,9},{9,8},{10,11... | collective-permute-start | bytes 3145736 | tf_op jit(solution)/shard_map/ppermute | solution.py:31
  8.1 1.2 copy-start.5
  9.5 57.7 %collective-permute-start.8 = (bf16[4,512,256]{2,1,0:T(8,128)(2,1)S(1)}, bf16[4,512,256]{2,1,0:T(8,128)(2,1)S(1)}, u32[]{:S(2)}, u32[]{:S(2)}) collective-permute-start(bf16[4,512,256]{2,1,0:T(8,128)(2,1)S(1)} %bitcast.11), channel_id=1, source_target_pairs={{0,16},{16,0},{1,17},{17,1},{2,18},{18,2},{3,19},{19,3},{4,20},{20... | collective-permute-start | bytes 3145736 | tf_op jit(solution)/shard_map/ppermute | solution.py:16
  12.4 32.6 %collective-permute-start.1 = (bf16[2,2,4,32,256]{4,3,2,1,0:T(8,128)(2,1)S(1)}, bf16[2,2,4,32,256]{4,3,2,1,0:T(8,128)(2,1)S(1)}, u32[]{:S(2)}, u32[]{:S(2)}) collective-permute-start(bf16[2,2,4,32,256]{4,3,2,1,0:T(8,128)(2,1)S(1)} %get-tuple-element.54), channel_id=1, source_target_pairs={{0,8},{1,9},{2,10},{3,11},{4,12},{5,13},{6,14},{7,15},{8,0},{9,1},... | collective-permute-start | bytes 786440 | tf_op jit(solution)/shard_map/ppermute | solution.py:31
  15.0 30.6 %collective-permute-start.2 = (bf16[2,2,4,32,256]{4,3,2,1,0:T(8,128)(2,1)S(1)}, bf16[2,2,4,32,256]{4,3,2,1,0:T(8,128)(2,1)S(1)}, u32[]{:S(2)}, u32[]{:S(2)}) collective-permute-start(bf16[2,2,4,32,256]{4,3,2,1,0:T(8,128)(2,1)S(1)} %get-tuple-element.55), channel_id=1, source_target_pairs={{0,12},{1,13},{2,14},{3,15},{4,8},{5,9},{6,10},{7,11},{8,4},{9,5},... | collective-permute-start | bytes 786440 | tf_op jit(solution)/shard_map/ppermute | solution.py:31
  16.3 40.8 %collective-permute-start.3 = (bf16[2,2,4,32,256]{4,3,2,1,0:T(8,128)(2,1)S(1)}, bf16[2,2,4,32,256]{4,3,2,1,0:T(8,128)(2,1)S(1)}, u32[]{:S(2)}, u32[]{:S(2)}) collective-permute-start(bf16[2,2,4,32,256]{4,3,2,1,0:T(8,128)(2,1)S(1)} %get-tuple-element.56), channel_id=1, source_target_pairs={{0,10},{1,11},{2,8},{3,9},{4,14},{5,15},{6,12},{7,13},{8,2},{9,3},... | collective-permute-start | bytes 786440 | tf_op jit(solution)/shard_map/ppermute | solution.py:31
  19.0 38.7 %collective-permute-start.4 = (bf16[2,2,4,32,256]{4,3,2,1,0:T(8,128)(2,1)S(1)}, bf16[2,2,4,32,256]{4,3,2,1,0:T(8,128)(2,1)S(1)}, u32[]{:S(2)}, u32[]{:S(2)}) collective-permute-start(bf16[2,2,4,32,256]{4,3,2,1,0:T(8,128)(2,1)S(1)} %get-tuple-element.57), channel_id=1, source_target_pairs={{0,14},{1,15},{2,12},{3,13},{4,10},{5,11},{6,8},{7,9},{8,6},{9,7},... | collective-permute-start | bytes 786440 | tf_op jit(solution)/shard_map/ppermute | solution.py:31
  44.9 14.4 %collective-permute-start.5 = (bf16[2,2,4,32,256]{4,3,2,1,0:T(8,128)(2,1)S(1)}, bf16[2,2,4,32,256]{4,3,2,1,0:T(8,128)(2,1)S(1)}, u32[]{:S(2)}, u32[]{:S(2)}) collective-permute-start(bf16[2,2,4,32,256]{4,3,2,1,0:T(8,128)(2,1)S(1)} %get-tuple-element.58), channel_id=1, source_target_pairs={{0,6},{1,7},{2,4},{3,5},{4,2},{5,3},{6,0},{7,1},{8,14},{9,15},{10,... | collective-permute-start | bytes 786440 | tf_op jit(solution)/shard_map/ppermute | solution.py:31
  45.5 17.7 %collective-permute-start.6 = (bf16[2,2,4,32,256]{4,3,2,1,0:T(8,128)(2,1)S(1)}, bf16[2,2,4,32,256]{4,3,2,1,0:T(8,128)(2,1)S(1)}, u32[]{:S(2)}, u32[]{:S(2)}) collective-permute-start(bf16[2,2,4,32,256]{4,3,2,1,0:T(8,128)(2,1)S(1)} %get-tuple-element.59), channel_id=1, source_target_pairs={{0,4},{1,5},{2,6},{3,7},{4,0},{5,1},{6,2},{7,3},{8,12},{9,13},{10,... | collective-permute-start | bytes 786440 | tf_op jit(solution)/shard_map/ppermute | solution.py:31
  57.2 6.9 %collective-permute-start.7 = (bf16[2,2,4,32,256]{4,3,2,1,0:T(8,128)(2,1)S(1)}, bf16[2,2,4,32,256]{4,3,2,1,0:T(8,128)(2,1)S(1)}, u32[]{:S(2)}, u32[]{:S(2)}) collective-permute-start(bf16[2,2,4,32,256]{4,3,2,1,0:T(8,128)(2,1)S(1)} %get-tuple-element.60), channel_id=1, source_target_pairs={{0,2},{1,3},{2,0},{3,1},{4,6},{5,7},{6,4},{7,5},{8,10},{9,11},{10,... | collective-permute-start | bytes 786440 | tf_op jit(solution)/shard_map/ppermute | solution.py:31
  67.1 4.4 %collective-permute-start.14 = (bf16[8,4,32,256]{3,2,1,0:T(8,128)(2,1)S(1)}, bf16[8,4,32,256]{3,2,1,0:T(8,128)(2,1)S(1)}, u32[]{:S(2)}, u32[]{:S(2)}) collective-permute-start(bf16[8,4,32,256]{3,2,1,0:T(8,128)(2,1)S(1)} %get-tuple-element.72), channel_id=1, source_target_pairs={{0,1},{1,0},{2,3},{3,2},{4,5},{5,4},{6,7},{7,6},{8,9},{9,8},{10,11... | collective-permute-start | bytes 1572872 | tf_op jit(solution)/shard_map/ppermute | solution.py:31
  70.3 7.8 %collective-permute-start.9 = (bf16[8,4,32,256]{3,2,1,0:T(8,128)(2,1)S(1)}, bf16[8,4,32,256]{3,2,1,0:T(8,128)(2,1)S(1)}, u32[]{:S(2)}, u32[]{:S(2)}) collective-permute-start(bf16[8,4,32,256]{3,2,1,0:T(8,128)(2,1)S(1)} %get-tuple-element.64), channel_id=1, source_target_pairs={{0,1},{1,0},{2,3},{3,2},{4,5},{5,4},{6,7},{7,6},{8,9},{9,8},{10,11... | collective-permute-start | bytes 1572872 | tf_op jit(solution)/shard_map/ppermute | solution.py:31
  70.9 23.2 %collective-permute-start.15 = (bf16[32,64,64]{2,1,0:T(8,128)(2,1)S(1)}, bf16[32,64,64]{2,1,0:T(8,128)(2,1)S(1)}, u32[]{:S(2)}, u32[]{:S(2)}) collective-permute-start(bf16[32,64,64]{2,1,0:T(8,128)(2,1)S(1)} %get-tuple-element.74.right_ref), channel_id=1, source_target_pairs={{0,16},{16,0},{1,17},{17,1},{2,18},{18,2},{3,19},{19,3},{4,20},{20... | collective-permute-start | bytes 786440 | tf_op jit(solution)/shard_map/ppermute | solution.py:16
  71.4 38.7 %copy-start = (bf16[4,512,512]{2,1,0:T(8,128)(2,1)S(1)}, bf16[4,512,512]{2,1,0:T(8,128)(2,1)}, u32[]{:S(2)}) copy-start(bf16[4,512,512]{2,1,0:T(8,128)(2,1)} %left_ref.1) | copy-start | bytes 6291460
  71.5 19.2 %collective-permute-start.16 = (bf16[2,4,32,256]{3,2,1,0:T(8,128)(2,1)S(1)}, bf16[2,4,32,256]{3,2,1,0:T(8,128)(2,1)S(1)}, u32[]{:S(2)}, u32[]{:S(2)}) collective-permute-start(bf16[2,4,32,256]{3,2,1,0:T(8,128)(2,1)S(1)} %get-tuple-element.76), channel_id=1, source_target_pairs={{0,8},{1,9},{2,10},{3,11},{4,12},{5,13},{6,14},{7,15},{8,0},{9,1},... | collective-permute-start | bytes 393224 | tf_op jit(solution)/shard_map/ppermute | solution.py:31
  75.1 16.8 %collective-permute-start.17 = (bf16[2,4,32,256]{3,2,1,0:T(8,128)(2,1)S(1)}, bf16[2,4,32,256]{3,2,1,0:T(8,128)(2,1)S(1)}, u32[]{:S(2)}, u32[]{:S(2)}) collective-permute-start(bf16[2,4,32,256]{3,2,1,0:T(8,128)(2,1)S(1)} %get-tuple-element.77), channel_id=1, source_target_pairs={{0,12},{1,13},{2,14},{3,15},{4,8},{5,9},{6,10},{7,11},{8,4},{9,5},... | collective-permute-start | bytes 393224 | tf_op jit(solution)/shard_map/ppermute | solution.py:31
  77.6 19.4 %collective-permute-start.18 = (bf16[2,4,32,256]{3,2,1,0:T(8,128)(2,1)S(1)}, bf16[2,4,32,256]{3,2,1,0:T(8,128)(2,1)S(1)}, u32[]{:S(2)}, u32[]{:S(2)}) collective-permute-start(bf16[2,4,32,256]{3,2,1,0:T(8,128)(2,1)S(1)} %get-tuple-element.78), channel_id=1, source_target_pairs={{0,10},{1,11},{2,8},{3,9},{4,14},{5,15},{6,12},{7,13},{8,2},{9,3},... | collective-permute-start | bytes 393224 | tf_op jit(solution)/shard_map/ppermute | solution.py:31
  78.1 18.9 %collective-permute-start.19 = (bf16[2,4,32,256]{3,2,1,0:T(8,128)(2,1)S(1)}, bf16[2,4,32,256]{3,2,1,0:T(8,128)(2,1)S(1)}, u32[]{:S(2)}, u32[]{:S(2)}) collective-permute-start(bf16[2,4,32,256]{3,2,1,0:T(8,128)(2,1)S(1)} %get-tuple-element.79), channel_id=1, source_target_pairs={{0,14},{1,15},{2,12},{3,13},{4,10},{5,11},{6,8},{7,9},{8,6},{9,7},... | collective-permute-start | bytes 393224 | tf_op jit(solution)/shard_map/ppermute | solution.py:31
  90.7 6.9 %collective-permute-start.22 = (bf16[2,4,32,256]{3,2,1,0:T(8,128)(2,1)S(1)}, bf16[2,4,32,256]{3,2,1,0:T(8,128)(2,1)S(1)}, u32[]{:S(2)}, u32[]{:S(2)}) collective-permute-start(bf16[2,4,32,256]{3,2,1,0:T(8,128)(2,1)S(1)} %get-tuple-element.85), channel_id=1, source_target_pairs={{0,2},{1,3},{2,0},{3,1},{4,6},{5,7},{6,4},{7,5},{8,10},{9,11},{10,... | collective-permute-start | bytes 393224 | tf_op jit(solution)/shard_map/ppermute | solution.py:31
  92.0 6.8 %collective-permute-start.21 = (bf16[2,4,32,256]{3,2,1,0:T(8,128)(2,1)S(1)}, bf16[2,4,32,256]{3,2,1,0:T(8,128)(2,1)S(1)}, u32[]{:S(2)}, u32[]{:S(2)}) collective-permute-start(bf16[2,4,32,256]{3,2,1,0:T(8,128)(2,1)S(1)} %get-tuple-element.83), channel_id=1, source_target_pairs={{0,4},{1,5},{2,6},{3,7},{4,0},{5,1},{6,2},{7,3},{8,12},{9,13},{10,... | collective-permute-start | bytes 393224 | tf_op jit(solution)/shard_map/ppermute | solution.py:31
  94.0 7.6 %collective-permute-start.20 = (bf16[2,4,32,256]{3,2,1,0:T(8,128)(2,1)S(1)}, bf16[2,4,32,256]{3,2,1,0:T(8,128)(2,1)S(1)}, u32[]{:S(2)}, u32[]{:S(2)}) collective-permute-start(bf16[2,4,32,256]{3,2,1,0:T(8,128)(2,1)S(1)} %get-tuple-element.81), channel_id=1, source_target_pairs={{0,6},{1,7},{2,4},{3,5},{4,2},{5,3},{6,0},{7,1},{8,14},{9,15},{10,... | collective-permute-start | bytes 393224 | tf_op jit(solution)/shard_map/ppermute | solution.py:31
  101.7 32.2 %collective-permute-start.26 = (bf16[4,512,256]{2,1,0:T(8,128)(2,1)S(1)}, bf16[4,512,256]{2,1,0:T(8,128)(2,1)S(1)}, u32[]{:S(2)}, u32[]{:S(2)}) collective-permute-start(bf16[4,512,256]{2,1,0:T(8,128)(2,1)S(1)} %bitcast.8), channel_id=1, source_target_pairs={{0,16},{16,0},{1,17},{17,1},{2,18},{18,2},{3,19},{19,3},{4,20},{20... | collective-permute-start | bytes 3145736 | tf_op jit(solution)/shard_map/ppermute | solution.py:16
  103.3 17.4 %collective-permute-start.10 = (bf16[2,4,32,256]{3,2,1,0:T(8,128)(2,1)S(1)}, bf16[2,4,32,256]{3,2,1,0:T(8,128)(2,1)S(1)}, u32[]{:S(2)}, u32[]{:S(2)}) collective-permute-start(bf16[2,4,32,256]{3,2,1,0:T(8,128)(2,1)S(1)} %get-tuple-element.66), channel_id=1, source_target_pairs={{0,8},{1,9},{2,10},{3,11},{4,12},{5,13},{6,14},{7,15},{8,0},{9,1},... | collective-permute-start | bytes 393224 | tf_op jit(solution)/shard_map/ppermute | solution.py:31
  105.3 15.6 %collective-permute-start.11 = (bf16[2,4,32,256]{3,2,1,0:T(8,128)(2,1)S(1)}, bf16[2,4,32,256]{3,2,1,0:T(8,128)(2,1)S(1)}, u32[]{:S(2)}, u32[]{:S(2)}) collective-permute-start(bf16[2,4,32,256]{3,2,1,0:T(8,128)(2,1)S(1)} %get-tuple-element.67), channel_id=1, source_target_pairs={{0,12},{1,13},{2,14},{3,15},{4,8},{5,9},{6,10},{7,11},{8,4},{9,5},... | collective-permute-start | bytes 393224 | tf_op jit(solution)/shard_map/ppermute | solution.py:31
  106.3 20.9 %collective-permute-start.12 = (bf16[2,4,32,256]{3,2,1,0:T(8,128)(2,1)S(1)}, bf16[2,4,32,256]{3,2,1,0:T(8,128)(2,1)S(1)}, u32[]{:S(2)}, u32[]{:S(2)}) collective-permute-start(bf16[2,4,32,256]{3,2,1,0:T(8,128)(2,1)S(1)} %get-tuple-element.68), channel_id=1, source_target_pairs={{0,10},{1,11},{2,8},{3,9},{4,14},{5,15},{6,12},{7,13},{8,2},{9,3},... | collective-permute-start | bytes 393224 | tf_op jit(solution)/shard_map/ppermute | solution.py:31
  108.8 23.4 %copy-start.2 = (bf16[1,2048,256]{2,1,0:T(8,128)(2,1)S(1)}, bf16[1,2048,256]{2,1,0:T(8,128)(2,1)}, u32[]{:S(2)}) copy-start(bf16[1,2048,256]{2,1,0:T(8,128)(2,1)} %param.6) | copy-start | bytes 3145732
  108.8 23.4 %copy-start.3 = (bf16[1,2048,256]{2,1,0:T(8,128)(2,1)S(1)}, bf16[1,2048,256]{2,1,0:T(8,128)(2,1)}, u32[]{:S(2)}) copy-start(bf16[1,2048,256]{2,1,0:T(8,128)(2,1)} %param.7) | copy-start | bytes 3145732
  108.8 19.0 %collective-permute-start.13 = (bf16[2,4,32,256]{3,2,1,0:T(8,128)(2,1)S(1)}, bf16[2,4,32,256]{3,2,1,0:T(8,128)(2,1)S(1)}, u32[]{:S(2)}, u32[]{:S(2)}) collective-permute-start(bf16[2,4,32,256]{3,2,1,0:T(8,128)(2,1)S(1)} %get-tuple-element.69), channel_id=1, source_target_pairs={{0,14},{1,15},{2,12},{3,13},{4,10},{5,11},{6,8},{7,9},{8,6},{9,7},... | collective-permute-start | bytes 393224 | tf_op jit(solution)/shard_map/ppermute | solution.py:31
  120.7 8.3 %collective-permute-start.23 = (bf16[2,4,32,256]{3,2,1,0:T(8,128)(2,1)S(1)}, bf16[2,4,32,256]{3,2,1,0:T(8,128)(2,1)S(1)}, u32[]{:S(2)}, u32[]{:S(2)}) collective-permute-start(bf16[2,4,32,256]{3,2,1,0:T(8,128)(2,1)S(1)} %get-tuple-element.87), channel_id=1, source_target_pairs={{0,6},{1,7},{2,4},{3,5},{4,2},{5,3},{6,0},{7,1},{8,14},{9,15},{10,... | collective-permute-start | bytes 393224 | tf_op jit(solution)/shard_map/ppermute | solution.py:31
  120.9 9.1 %collective-permute-start.24 = (bf16[2,4,32,256]{3,2,1,0:T(8,128)(2,1)S(1)}, bf16[2,4,32,256]{3,2,1,0:T(8,128)(2,1)S(1)}, u32[]{:S(2)}, u32[]{:S(2)}) collective-permute-start(bf16[2,4,32,256]{3,2,1,0:T(8,128)(2,1)S(1)} %get-tuple-element.89), channel_id=1, source_target_pairs={{0,4},{1,5},{2,6},{3,7},{4,0},{5,1},{6,2},{7,3},{8,12},{9,13},{10,... | collective-permute-start | bytes 393224 | tf_op jit(solution)/shard_map/ppermute | solution.py:31
  127.2 5.0 %collective-permute-start.25 = (bf16[2,4,32,256]{3,2,1,0:T(8,128)(2,1)S(1)}, bf16[2,4,32,256]{3,2,1,0:T(8,128)(2,1)S(1)}, u32[]{:S(2)}, u32[]{:S(2)}) collective-permute-start(bf16[2,4,32,256]{3,2,1,0:T(8,128)(2,1)S(1)} %get-tuple-element.91), channel_id=1, source_target_pairs={{0,2},{1,3},{2,0},{3,1},{4,6},{5,7},{6,4},{7,5},{8,10},{9,11},{10,... | collective-permute-start | bytes 393224 | tf_op jit(solution)/shard_map/ppermute | solution.py:31

commit v8 on v7

--- a/solution.py
+++ b/solution.py
@@ -20,10 +20,10 @@
     return lax.optimization_barrier((array, earlier))[0]
 
 
-def far_first(count):
-    half = count // 2
-    far = [t for pair in zip(range(half, half + half // 2), range(half + half // 2, count)) for t in pair]
-    return far + list(range(half - 1, 0, -1))
+def partner_order(chips):
+    half = chips // 2
+    far = list(range(half, chips, 2)) + list(range(half + 1, chips, 2))
+    return far[:-1] + list(range(1, half)) + far[-1:]
 
 
 def permute(array, offset):
@@ -31,12 +31,15 @@
     return lax.ppermute(array, "seq", [(i, i ^ offset) for i in range(seq)])
 
 
-def exchange(messages):
-    return [messages[0]] + [permute(message, 2 * t) for t, message in list(enumerate(messages))[1:]]
+def exchange(messages, sent=0, received=None):
+    result = [permute(message, 2 * t) if t else message for t, message in enumerate(messages)]
+    if received is not None:
+        result[sent] = received
+    return result
 
 
 def listed(messages):
-    return [messages[t] for t in [0] + far_first(len(messages))]
+    return [messages[t] for t in [0] + partner_order(len(messages))]
 
 
 def call(kernel, me, inputs, out_shapes, scratch=(), flops=0, unblocked=(), vmem=32):
@@ -66,34 +69,39 @@
 
 
 def received_views(me, refs):
-    order = [0] + far_first(len(refs))
+    order = [0] + partner_order(len(refs))
     return [(me ^ (2 * t + e), ref.at[e]) for t, ref in zip(order, refs) for e in range(2)]
 
 
-def send_kernel(me_ref, gate_hbm, cotangent_hbm, left_hbm, values_hbm, *refs):
-    out_refs = refs[:2]
-    gate, cotangent, left, values, hold, sems = refs[2:]
+def product_kernel(me_ref, gate_hbm, cotangent_hbm, *refs):
+    out_refs, (gate, cotangent, sems) = refs[:2], refs[2:]
+    rows = gate.shape[0]
+    loads = [
+        [
+            pltpu.make_async_copy(source.at[i], target.at[i], sems.at[n, i])
+            for n, (source, target) in enumerate(((gate_hbm, gate), (cotangent_hbm, cotangent)))
+        ]
+        for i in range(rows)
+    ]
+    for pair in loads:
+        for load in pair:
+            load.start()
+    blocks = block_views(me_ref[0], out_refs)
+    for i in range(rows):
+        for load in loads[i]:
+            load.wait()
+        for c, ref in blocks:
+            ref[i] = (gate[i, c].astype(F32) * cotangent[i, c].astype(F32)).astype(BF16)
+
+
+def mix_kernel(me_ref, left_ref, values_ref, *refs):
+    out_refs, hold = refs[:2], refs[2]
     rows, seq, cols, channels = hold.shape
-    me = me_ref[0]
-    loads = []
     for i in range(rows):
-        for n, (source, target) in enumerate(((left_hbm, left), (values_hbm, values))):
-            loads.append(pltpu.make_async_copy(source.at[i], target.at[i], sems.at[n, i]))
-    loads.append(pltpu.make_async_copy(gate_hbm, gate, sems.at[2, 0]))
-    loads.append(pltpu.make_async_copy(cotangent_hbm, cotangent, sems.at[2, 1]))
-    for load in loads:
-        load.start()
-    for i in range(rows):
-        loads[2 * i].wait()
-        loads[2 * i + 1].wait()
-        mixed = dot(left[i], values[i], ((1,), (0,)))
+        mixed = dot(left_ref[i], values_ref[i], ((1,), (0,)))
         hold[i] = mixed.astype(BF16).reshape(seq, cols, channels)
-    loads[-2].wait()
-    loads[-1].wait()
-    for c, ref in block_views(me, out_refs):
-        wide = gate[:, c].astype(F32) * cotangent[:, c].astype(F32)
-        ref[0] = wide.astype(BF16)
-        ref[1] = hold[:, c]
+    for c, ref in block_views(me_ref[0], out_refs):
+        ref[...] = hold[:, c]
 
 
 def pack_kernel(me_ref, own_ref, other_ref, *out_refs):
@@ -137,7 +145,7 @@
     by_column_ref, wide, wide_out = refs[chips + 2 :]
     cols, count, _ = right_ref.shape
     me = me_ref[0]
-    load_columns([(c, ref.at[0]) for c, ref in received_views(me, in_refs)], wide)
+    load_columns(received_views(me, in_refs), wide)
     for k in range(cols):
         grad = column(wide, k, count, cols)
         by_column_ref[k] = grad
@@ -150,7 +158,7 @@
     right_part_ref, wide, wide_out = refs[chips + 2 :]
     cols, count, _ = right_ref.shape
     me = me_ref[0]
-    load_columns([(c, ref.at[1]) for c, ref in received_views(me, in_refs)], wide)
+    load_columns(received_views(me, in_refs), wide)
     for k in range(cols):
         mixed = column(wide, k, count, cols)
         store_column(wide_out, k, count, cols, dot(right_ref[k], mixed, ((1,), (0,))))
@@ -158,25 +166,54 @@
     send_columns(wide_out, block_views(me, out_refs))
 
 
-def gather_kernel(chips, me_ref, *refs):
-    for c, ref in received_views(me_ref[0], refs[:chips]):
-        refs[chips][:, c] = ref[...]
-
-
-def row_backward_kernel(me_ref, left_ref, values_ref, grad_ref, signal_ref, term_ref):
+def gather_kernel(me_ref, *refs):
+    out_ref = refs[-1]
+    for t, ref in enumerate(refs[:-1]):
+        for e in range(2):
+            out_ref[2 * t + e] = ref[e]
+
+
+def load_rows(me, parts, hold):
+    half = parts[0].shape[0]
+    order = [0] + partner_order(half)
+    for n, t in enumerate(order):
+        for e in range(2):
+            j = 2 * n + e
+            hold[:, me ^ (2 * t + e)] = parts[j // half][j % half]
+
+
+def row_of(hold, i):
+    seq, cols, channels = hold.shape[1:]
+    return hold[i].reshape(seq * cols, channels)
+
+
+def row_backward_kernel(
+    me_ref, left_ref, values_ref, first_ref, second_ref, signal_ref, term_ref, hold
+):
+    load_rows(me_ref[0], (first_ref, second_ref), hold)
     for i in range(left_ref.shape[0]):
-        grad = grad_ref[i]
+        grad = row_of(hold, i)
         signal_ref[i] = dot(left_ref[i], grad, ((0,), (0,))).astype(BF16)
         term_ref[i] = dot(grad, values_ref[i], ((1,), (1,))).astype(BF16)
 
 
 def factor_sum_kernel(
-    me_ref, term_ref, values_ref, grad_ref, right_ref, other_ref, left_out_ref, right_out_ref
+    me_ref,
+    term_ref,
+    values_ref,
+    first_ref,
+    second_ref,
+    right_ref,
+    other_ref,
+    left_out_ref,
+    right_out_ref,
+    hold,
 ):
+    right_out_ref[...] = (right_ref[...].astype(F32) + other_ref[...].astype(F32)).astype(BF16)
+    load_rows(me_ref[0], (first_ref, second_ref), hold)
     for i in range(term_ref.shape[0]):
-        other = dot(grad_ref[i], values_ref[i], ((1,), (1,))).astype(BF16)
+        other = dot(row_of(hold, i), values_ref[i], ((1,), (1,))).astype(BF16)
         left_out_ref[i] = (term_ref[i].astype(F32) + other.astype(F32)).astype(BF16)
-    right_out_ref[...] = (right_ref[...].astype(F32) + other_ref[...].astype(F32)).astype(BF16)
 
 
 def output_kernel(chips, me_ref, gate_ref, cotangent_ref, *refs):
@@ -217,63 +254,83 @@
         message = shape(2, *own.shape[1:])
         return list(call(pack_kernel, me, [own, permute(other, 1)], [message] * chips))
 
-    own, other = call(
-        send_kernel,
+    def pin(messages, t, earlier):
+        messages[t] = after(messages[t], earlier)
+
+    last, early = chips - 1, chips // 2
+    halves = [shape(chips, *block)] * 2
+    hold = pltpu.VMEM(whole.shape, BF16)
+
+    grad_rows = call(
+        product_kernel,
         me,
-        [gate, cotangent, left_factor, values],
-        [shape(chips, 2, *block)] * 2,
-        [pltpu.VMEM(x.shape, BF16) for x in (gate, cotangent, left_factor, values, whole)]
-        + [pltpu.SemaphoreType.DMA((3, max(rows, 2)))],
-        row_flops,
-        unblocked=range(4),
+        [gate, cotangent],
+        halves,
+        [hold, hold, pltpu.SemaphoreType.DMA((2, rows))],
+        unblocked=range(2),
         vmem=60,
     )
-    messages = pack(own, other)
-    other_values = swap_sequences(after(values, messages[0]))
-    columns = listed(exchange(messages))
-    own, other, grad_column = call(
+    out_grad = pack(*grad_rows)
+    other_values = swap_sequences(after(values, out_grad[0]))
+    mixed_rows = call(
+        mix_kernel, me, [left_factor, after(values, out_grad[0])], halves, [hold], row_flops
+    )
+    out_mixed = pack(*mixed_rows)
+    pin(out_grad, last, out_mixed[0])
+    grad_columns = exchange(out_grad)
+    first_mixed = permute(out_mixed[early], 2 * early)
+    pin(grad_columns, 0, first_mixed)
+    *grad_second, grad_column = call(
         on_chips(column_backward_kernel),
         me,
-        [right_factor, *columns],
-        [shape(chips, *block)] * 2 + [shape(cols, count, channels)],
+        [right_factor, *listed(grad_columns)],
+        halves + [shape(cols, count, channels)],
         [wide, wide],
         column_flops,
     )
-    messages = pack(own, other)
-    own, other, right_part = call(
+    back = pack(*grad_second)
+    pin(out_mixed, last, back[0])
+    mixed_columns = exchange(out_mixed, early, first_mixed)
+    first_back = permute(back[early], 2 * early)
+    pin(mixed_columns, 0, first_back)
+    *second, right_part = call(
         on_chips(column_forward_kernel),
         me,
-        [right_factor, grad_column, other_values, *columns],
-        [shape(chips, *block)] * 2 + [right],
+        [right_factor, grad_column, other_values, *listed(mixed_columns)],
+        halves + [right],
         [wide, wide],
         2 * column_flops,
         unblocked=[2],
     )
-    second_messages = pack(own, other)
-    for t in range(1, chips // 2):
-        messages[t] = after(messages[t], second_messages[0])
-    back = listed(exchange(messages))
+    second = pack(*second)
+    pin(back, last, second[0])
     other_right = swap_sequences(right_part)
-    back[0] = after(back[0], other_right)
-    (gathered,) = call(on_chips(gather_kernel), me, back, [whole])
-    grad_back = gathered.reshape(rows, block_len, channels)
-    other_grad_back = swap_sequences(grad_back)
+    back = exchange(back, early, first_back)
+    first_second = permute(second[early], 2 * early)
+    pin(back, last, (first_second, other_right))
+    back = listed(back)
+    half_rows = shape(seq // 2, *block)
+    (first_half,) = call(gather_kernel, me, back[:early], [half_rows])
+    (second_half,) = call(gather_kernel, me, back[early:], [half_rows])
+    other_first = swap_sequences(first_half)
+    other_second = swap_sequences(second_half)
     grad_signal, left_term = call(
         row_backward_kernel,
         me,
-        [left_factor, values, grad_back],
+        [left_factor, values, first_half, second_half],
         [by_row, left],
-        flops=2 * row_flops,
-    )
-    for t in range(1, chips // 2):
-        second_messages[t] = after(second_messages[t], left_term)
-    second = listed(exchange(second_messages))
+        [hold],
+        2 * row_flops,
+    )
+    pin(second, last, left_term)
+    second = listed(exchange(second, early, first_second))
     grad_left, grad_right = call(
         factor_sum_kernel,
         me,
-        [left_term, other_values, other_grad_back, right_part, other_right],
+        [left_term, other_values, other_first, other_second, right_part, other_right],
         [left, right],
-        flops=row_flops,
+        [hold],
+        row_flops,
     )
     output, grad_gate = call(
         on_chips(output_kernel), me, [gate, cotangent, *second], [whole, whole]

time: 136 us -> 137 us (level)
  starting transfers between devices: 43.5 us -> 69 us
  waiting for transfers between devices: 73.7 us -> 49.8 us
    ppermute x24 -> x32, starting transfers between devices: 38.4 us -> 64.7 us  [permute(): return lax.ppermute(array, 'seq', [(i, i ^ offset) for i in range(seq)])]
    ppermute x24 -> x32, waiting for transfers between devices: 73.7 us -> 49.8 us  [permute(): return lax.ppermute(array, 'seq', [(i, i ^ offset) for i in range(seq)])]
    pallas_call x10 -> x13, Pallas kernels: 17.2 us -> 16.3 us  [call(): pl.pallas_call(kernel, out_shape=out_shapes, in_specs=[pl.BlockSpec(memor...]
    ppermute x3 -> x4, starting transfers between devices: 5.05 us -> 4.24 us  [swap_sequences(): return lax.ppermute(array, 'dp', [(0, 1), (1, 0)])]
  transfers between devices with their start and end apart: 27 -> 36, of which waited for: 16 -> 18; matrix products, arithmetic and copies ran while one was open for 0% -> 0% of each run, Pallas kernels for 8% -> 5%
where the time goes in v8:
time: 137 us
  starting transfers between devices  69 us (50%)
  waiting for transfers between devices  49.8 us (36%)
  Pallas kernels  16.3 us (12%)
    ppermute x32, starting transfers between devices, permute(): return lax.ppermute(array, 'seq', [(i, i ^ offset) for i in range(seq)])  64.7 us
    ppermute x32, waiting for transfers between devices, permute(): return lax.ppermute(array, 'seq', [(i, i ^ offset) for i in range(seq)])  49.8 us
    pallas_call x13, Pallas kernels, call(): pl.pallas_call(kernel, out_shape=out_shapes, in_specs=[pl.BlockSpec(memor...  16.3 us
    ppermute x4, starting transfers between devices, swap_sequences(): return lax.ppermute(array, 'dp', [(0, 1), (1, 0)])  4.24 us
  transfers between devices with their start and end apart: 36, of which 18 were waited for; matrix products, arithmetic and copies ran while one was open for 0% of the time, Pallas kernels for 5%

profile of v8, /device:TPU:0, one launch (start us, length us, event | category | flops | bytes accessed | tf_op | source)
XLA Modules:
  0.0 136.9 jit_solution(2618017179870068121)
XLA Ops:
  0.7 2.7 %product_kernel.1 = (bf16[8,4,32,256]{3,2,1,0:T(8,128)(2,1)}, bf16[8,4,32,256]{3,2,1,0:T(8,128)(2,1)}) custom-call(s32[1]{0:T(128)} %bitcast.me_ref, bf16[4,16,32,256]{3,2,1,0:T(8,128)(2,1)} %bitcast.10, bf16[4,16,32,256]{3,2,1,0:T(8,128)(2,1)} %bitcast.12), custom_call_target="tpu_custom_call" | custom-call | bytes 3145728 | tf_op jit(solution)/shard_map/product_kernel/pallas_call | solution.py:51
  3.9 1.7 %collective-permute-done.other_ref = bf16[8,4,32,256]{3,2,1,0:T(8,128)(2,1)S(1)} collective-permute-done((bf16[8,4,32,256]{3,2,1,0:T(8,128)(2,1)}, bf16[8,4,32,256]{3,2,1,0:T(8,128)(2,1)S(1)}, u32[]{:S(2)}, u32[]{:S(2)}) %collective-permute-start) | collective-permute-done | bytes 524320 | tf_op jit(solution)/shard_map/ppermute | solution.py:31
  5.7 1.0 copy-done.5
  6.8 0.8 mix_kernel.1
  8.0 3.7 %collective-permute-start.3 = (bf16[2,4,32,256]{3,2,1,0:T(8,128)(2,1)S(1)}, bf16[2,4,32,256]{3,2,1,0:T(8,128)(2,1)S(1)}, u32[]{:S(2)}, u32[]{:S(2)}) collective-permute-start(bf16[2,4,32,256]{3,2,1,0:T(8,128)(2,1)S(1)} %get-tuple-element.69), channel_id=1, source_target_pairs={{0,8},{1,9},{2,10},{3,11},{4,12},{5,13},{6,14},{7,15},{8,0},{9,1},... | collective-permute-start | bytes 393224 | tf_op jit(solution)/shard_map/ppermute | solution.py:31
  11.8 1.3 collective-permute-start.4
  13.1 2.6 %collective-permute-start.5 = (bf16[2,4,32,256]{3,2,1,0:T(8,128)(2,1)S(1)}, bf16[2,4,32,256]{3,2,1,0:T(8,128)(2,1)S(1)}, u32[]{:S(2)}, u32[]{:S(2)}) collective-permute-start(bf16[2,4,32,256]{3,2,1,0:T(8,128)(2,1)S(1)} %get-tuple-element.71), channel_id=1, source_target_pairs={{0,10},{1,11},{2,8},{3,9},{4,14},{5,15},{6,12},{7,13},{8,2},{9,3},... | collective-permute-start | bytes 393224 | tf_op jit(solution)/shard_map/ppermute | solution.py:31
  15.8 1.3 collective-permute-start.2
  17.1 1.5 %collective-permute-start.10 = (bf16[4,512,256]{2,1,0:T(8,128)(2,1)S(1)}, bf16[4,512,256]{2,1,0:T(8,128)(2,1)S(1)}, u32[]{:S(2)}, u32[]{:S(2)}) collective-permute-start(bf16[4,512,256]{2,1,0:T(8,128)(2,1)S(1)} %bitcast.8), channel_id=1, source_target_pairs={{0,16},{16,0},{1,17},{17,1},{2,18},{18,2},{3,19},{19,3},{4,20},{20... | collective-permute-start | bytes 3145736 | tf_op jit(solution)/shard_map/ppermute | solution.py:16
  18.6 8.7 %collective-permute-done.3.refs_1_ = bf16[2,4,32,256]{3,2,1,0:T(8,128)(2,1)S(1)} collective-permute-done((bf16[2,4,32,256]{3,2,1,0:T(8,128)(2,1)S(1)}, bf16[2,4,32,256]{3,2,1,0:T(8,128)(2,1)S(1)}, u32[]{:S(2)}, u32[]{:S(2)}) %collective-permute-start.3) | collective-permute-done | bytes 131104 | tf_op jit(solution)/shard_map/ppermute | solution.py:31
  27.3 1.8 %collective-permute-start.6 = (bf16[2,4,32,256]{3,2,1,0:T(8,128)(2,1)S(1)}, bf16[2,4,32,256]{3,2,1,0:T(8,128)(2,1)S(1)}, u32[]{:S(2)}, u32[]{:S(2)}) collective-permute-start(bf16[2,4,32,256]{3,2,1,0:T(8,128)(2,1)S(1)} %get-tuple-element.72), channel_id=1, source_target_pairs={{0,2},{1,3},{2,0},{3,1},{4,6},{5,7},{6,4},{7,5},{8,10},{9,11},{10,... | collective-permute-start | bytes 393224 | tf_op jit(solution)/shard_map/ppermute | solution.py:31
  29.1 1.6 %collective-permute-start.7 = (bf16[2,4,32,256]{3,2,1,0:T(8,128)(2,1)S(1)}, bf16[2,4,32,256]{3,2,1,0:T(8,128)(2,1)S(1)}, u32[]{:S(2)}, u32[]{:S(2)}) collective-permute-start(bf16[2,4,32,256]{3,2,1,0:T(8,128)(2,1)S(1)} %get-tuple-element.73), channel_id=1, source_target_pairs={{0,4},{1,5},{2,6},{3,7},{4,0},{5,1},{6,2},{7,3},{8,12},{9,13},{10,... | collective-permute-start | bytes 393224 | tf_op jit(solution)/shard_map/ppermute | solution.py:31
  30.7 3.6 %collective-permute-done.5.refs_3_ = bf16[2,4,32,256]{3,2,1,0:T(8,128)(2,1)S(1)} collective-permute-done((bf16[2,4,32,256]{3,2,1,0:T(8,128)(2,1)S(1)}, bf16[2,4,32,256]{3,2,1,0:T(8,128)(2,1)S(1)}, u32[]{:S(2)}, u32[]{:S(2)}) %collective-permute-start.5) | collective-permute-done | bytes 131104 | tf_op jit(solution)/shard_map/ppermute | solution.py:31
  34.4 1.2 collective-permute-done.2.refs_1_
  35.6 4.5 %collective-permute-start.9 = (bf16[2,4,32,256]{3,2,1,0:T(8,128)(2,1)S(1)}, bf16[2,4,32,256]{3,2,1,0:T(8,128)(2,1)S(1)}, u32[]{:S(2)}, u32[]{:S(2)}) collective-permute-start(bf16[2,4,32,256]{3,2,1,0:T(8,128)(2,1)S(1)} %get-tuple-element.77), channel_id=1, source_target_pairs={{0,14},{1,15},{2,12},{3,13},{4,10},{5,11},{6,8},{7,9},{8,6},{9,7},... | collective-permute-start | bytes 393224 | tf_op jit(solution)/shard_map/ppermute | solution.py:31
  40.1 4.8 %collective-permute-done.8.refs_6_ = bf16[2,4,32,256]{3,2,1,0:T(8,128)(2,1)S(1)} collective-permute-done((bf16[2,4,32,256]{3,2,1,0:T(8,128)(2,1)S(1)}, bf16[2,4,32,256]{3,2,1,0:T(8,128)(2,1)S(1)}, u32[]{:S(2)}, u32[]{:S(2)}) %collective-permute-start.8) | collective-permute-done | bytes 131104 | tf_op jit(solution)/shard_map/ppermute | solution.py:31
  44.9 3.0 %column_backward_kernel.1 = (bf16[8,4,32,256]{3,2,1,0:T(8,128)(2,1)S(1)}, bf16[8,4,32,256]{3,2,1,0:T(8,128)(2,1)S(1)}, bf16[32,64,256]{2,1,0:T(8,128)(2,1)S(1)}) custom-call(s32[1]{0:T(128)} %bitcast.me_ref, bf16[32,64,64]{2,1,0:T(8,128)(2,1)S(1)} %copy-done.4, bf16[2,4,32,256]{3,2,1,0:T(8,128)(2,1)S(1)} %get-tuple-element.68.refs_0_, ...), custom_call_target="tpu_custom_call" | custom-call | flops 67108864 | bytes 3407872 | tf_op jit(solution)/shard_map/column_backward_kernel/pallas_call | solution.py:51
  48.0 3.5 %collective-permute-start.13 = (bf16[2,4,32,256]{3,2,1,0:T(8,128)(2,1)S(1)}, bf16[2,4,32,256]{3,2,1,0:T(8,128)(2,1)S(1)}, u32[]{:S(2)}, u32[]{:S(2)}) collective-permute-start(bf16[2,4,32,256]{3,2,1,0:T(8,128)(2,1)S(1)} %get-tuple-element.83), channel_id=1, source_target_pairs={{0,12},{1,13},{2,14},{3,15},{4,8},{5,9},{6,10},{7,11},{8,4},{9,5},... | collective-permute-start | bytes 393224 | tf_op jit(solution)/shard_map/ppermute | solution.py:31
  51.6 2.9 %collective-permute-start.12 = (bf16[2,4,32,256]{3,2,1,0:T(8,128)(2,1)S(1)}, bf16[2,4,32,256]{3,2,1,0:T(8,128)(2,1)S(1)}, u32[]{:S(2)}, u32[]{:S(2)}) collective-permute-start(bf16[2,4,32,256]{3,2,1,0:T(8,128)(2,1)S(1)} %get-tuple-element.81), channel_id=1, source_target_pairs={{0,8},{1,9},{2,10},{3,11},{4,12},{5,13},{6,14},{7,15},{8,0},{9,1},... | collective-permute-start | bytes 393224 | tf_op jit(solution)/shard_map/ppermute | solution.py:31
  54.5 1.5 %collective-permute-start.15 = (bf16[2,4,32,256]{3,2,1,0:T(8,128)(2,1)S(1)}, bf16[2,4,32,256]{3,2,1,0:T(8,128)(2,1)S(1)}, u32[]{:S(2)}, u32[]{:S(2)}) collective-permute-start(bf16[2,4,32,256]{3,2,1,0:T(8,128)(2,1)S(1)} %get-tuple-element.85), channel_id=1, source_target_pairs={{0,2},{1,3},{2,0},{3,1},{4,6},{5,7},{6,4},{7,5},{8,10},{9,11},{10,... | collective-permute-start | bytes 393224 | tf_op jit(solution)/shard_map/ppermute | solution.py:31
  56.2 7.5 %collective-permute-start.16 = (bf16[2,4,32,256]{3,2,1,0:T(8,128)(2,1)S(1)}, bf16[2,4,32,256]{3,2,1,0:T(8,128)(2,1)S(1)}, u32[]{:S(2)}, u32[]{:S(2)}) collective-permute-start(bf16[2,4,32,256]{3,2,1,0:T(8,128)(2,1)S(1)} %get-tuple-element.86), channel_id=1, source_target_pairs={{0,4},{1,5},{2,6},{3,7},{4,0},{5,1},{6,2},{7,3},{8,12},{9,13},{10,... | collective-permute-start | bytes 393224 | tf_op jit(solution)/shard_map/ppermute | solution.py:31
  63.7 3.0 %collective-permute-done.14.refs_3_ = bf16[2,4,32,256]{3,2,1,0:T(8,128)(2,1)S(1)} collective-permute-done((bf16[2,4,32,256]{3,2,1,0:T(8,128)(2,1)S(1)}, bf16[2,4,32,256]{3,2,1,0:T(8,128)(2,1)S(1)}, u32[]{:S(2)}, u32[]{:S(2)}) %collective-permute-start.14) | collective-permute-done | bytes 131104 | tf_op jit(solution)/shard_map/ppermute | solution.py:31
  66.7 1.9 %collective-permute-done.12.refs_1_ = bf16[2,4,32,256]{3,2,1,0:T(8,128)(2,1)S(1)} collective-permute-done((bf16[2,4,32,256]{3,2,1,0:T(8,128)(2,1)S(1)}, bf16[2,4,32,256]{3,2,1,0:T(8,128)(2,1)S(1)}, u32[]{:S(2)}, u32[]{:S(2)}) %collective-permute-start.12) | collective-permute-done | bytes 131104 | tf_op jit(solution)/shard_map/ppermute | solution.py:31
  68.6 3.3 %collective-permute-start.18 = (bf16[2,4,32,256]{3,2,1,0:T(8,128)(2,1)S(1)}, bf16[2,4,32,256]{3,2,1,0:T(8,128)(2,1)S(1)}, u32[]{:S(2)}, u32[]{:S(2)}) collective-permute-start(bf16[2,4,32,256]{3,2,1,0:T(8,128)(2,1)S(1)} %get-tuple-element.90), channel_id=1, source_target_pairs={{0,14},{1,15},{2,12},{3,13},{4,10},{5,11},{6,8},{7,9},{8,6},{9,7},... | collective-permute-start | bytes 393224 | tf_op jit(solution)/shard_map/ppermute | solution.py:31
  71.9 5.7 %collective-permute-done.17.refs_6_ = bf16[2,4,32,256]{3,2,1,0:T(8,128)(2,1)S(1)} collective-permute-done((bf16[2,4,32,256]{3,2,1,0:T(8,128)(2,1)S(1)}, bf16[2,4,32,256]{3,2,1,0:T(8,128)(2,1)S(1)}, u32[]{:S(2)}, u32[]{:S(2)}) %collective-permute-start.17) | collective-permute-done | bytes 131104 | tf_op jit(solution)/shard_map/ppermute | solution.py:31
  77.6 3.1 %column_forward_kernel.1 = (bf16[8,4,32,256]{3,2,1,0:T(8,128)(2,1)S(1)}, bf16[8,4,32,256]{3,2,1,0:T(8,128)(2,1)S(1)}, bf16[32,64,64]{2,1,0:T(8,128)(2,1)S(1)}) custom-call(s32[1]{0:T(128)} %bitcast.me_ref, bf16[32,64,64]{2,1,0:T(8,128)(2,1)S(1)} %copy-done.4, bf16[32,64,256]{2,1,0:T(8,128)(2,1)S(1)} %get-tuple-element.78.grad_ref, ...), custom_call_target="tpu_custom_call" | custom-call | flops 134217728 | bytes 4718592 | tf_op jit(solution)/shard_map/column_forward_kernel/pallas_call | solution.py:51
  80.8 1.6 %collective-permute-start.32 = (bf16[32,64,64]{2,1,0:T(8,128)(2,1)S(1)}, bf16[32,64,64]{2,1,0:T(8,128)(2,1)S(1)}, u32[]{:S(2)}, u32[]{:S(2)}) collective-permute-start(bf16[32,64,64]{2,1,0:T(8,128)(2,1)S(1)} %get-tuple-element.108.right_ref), channel_id=1, source_target_pairs={{0,16},{16,0},{1,17},{17,1},{2,18},{18,2},{3,19},{19,3},{4,20},{20... | collective-permute-start | bytes 786440 | tf_op jit(solution)/shard_map/ppermute | solution.py:16
  82.3 2.7 %collective-permute-start.26 = (bf16[2,4,32,256]{3,2,1,0:T(8,128)(2,1)S(1)}, bf16[2,4,32,256]{3,2,1,0:T(8,128)(2,1)S(1)}, u32[]{:S(2)}, u32[]{:S(2)}) collective-permute-start(bf16[2,4,32,256]{3,2,1,0:T(8,128)(2,1)S(1)} %get-tuple-element.101), channel_id=1, source_target_pairs={{0,12},{1,13},{2,14},{3,15},{4,8},{5,9},{6,10},{7,11},{8,4},{9,5},... | collective-permute-start | bytes 393224 | tf_op jit(solution)/shard_map/ppermute | solution.py:31
  85.0 0.8 collective-permute-start.28
  85.9 3.1 %collective-permute-start.31 = (bf16[2,4,32,256]{3,2,1,0:T(8,128)(2,1)S(1)}, bf16[2,4,32,256]{3,2,1,0:T(8,128)(2,1)S(1)}, u32[]{:S(2)}, u32[]{:S(2)}) collective-permute-start(bf16[2,4,32,256]{3,2,1,0:T(8,128)(2,1)S(1)} %get-tuple-element.107), channel_id=1, source_target_pairs={{0,14},{1,15},{2,12},{3,13},{4,10},{5,11},{6,8},{7,9},{8,6},{9,7},... | collective-permute-start | bytes 393224 | tf_op jit(solution)/shard_map/ppermute | solution.py:31
  89.0 1.6 %collective-permute-done.26.refs_2_ = bf16[2,4,32,256]{3,2,1,0:T(8,128)(2,1)S(1)} collective-permute-done((bf16[2,4,32,256]{3,2,1,0:T(8,128)(2,1)S(1)}, bf16[2,4,32,256]{3,2,1,0:T(8,128)(2,1)S(1)}, u32[]{:S(2)}, u32[]{:S(2)}) %collective-permute-start.26) | collective-permute-done | bytes 131104 | tf_op jit(solution)/shard_map/ppermute | solution.py:31
  90.6 9.2 %collective-permute-start.20 = (bf16[2,4,32,256]{3,2,1,0:T(8,128)(2,1)S(1)}, bf16[2,4,32,256]{3,2,1,0:T(8,128)(2,1)S(1)}, u32[]{:S(2)}, u32[]{:S(2)}) collective-permute-start(bf16[2,4,32,256]{3,2,1,0:T(8,128)(2,1)S(1)} %get-tuple-element.94), channel_id=1, source_target_pairs={{0,8},{1,9},{2,10},{3,11},{4,12},{5,13},{6,14},{7,15},{8,0},{9,1},... | collective-permute-start | bytes 393224 | tf_op jit(solution)/shard_map/ppermute | solution.py:31
  99.8 1.7 %collective-permute-done.27.refs_3_ = bf16[2,4,32,256]{3,2,1,0:T(8,128)(2,1)S(1)} collective-permute-done((bf16[2,4,32,256]{3,2,1,0:T(8,128)(2,1)S(1)}, bf16[2,4,32,256]{3,2,1,0:T(8,128)(2,1)S(1)}, u32[]{:S(2)}, u32[]{:S(2)}) %collective-permute-start.27) | collective-permute-done | bytes 131104 | tf_op jit(solution)/shard_map/ppermute | solution.py:31
  101.5 2.3 %collective-permute-start.30 = (bf16[2,4,32,256]{3,2,1,0:T(8,128)(2,1)S(1)}, bf16[2,4,32,256]{3,2,1,0:T(8,128)(2,1)S(1)}, u32[]{:S(2)}, u32[]{:S(2)}) collective-permute-start(bf16[2,4,32,256]{3,2,1,0:T(8,128)(2,1)S(1)} %get-tuple-element.105), channel_id=1, source_target_pairs={{0,6},{1,7},{2,4},{3,5},{4,2},{5,3},{6,0},{7,1},{8,14},{9,15},{10,... | collective-permute-start | bytes 393224 | tf_op jit(solution)/shard_map/ppermute | solution.py:31
  103.8 0.6 collective-permute-start.34
  104.4 3.0 %collective-permute-done.20.refs_1_ = bf16[2,4,32,256]{3,2,1,0:T(8,128)(2,1)S(1)} collective-permute-done((bf16[2,4,32,256]{3,2,1,0:T(8,128)(2,1)S(1)}, bf16[2,4,32,256]{3,2,1,0:T(8,128)(2,1)S(1)}, u32[]{:S(2)}, u32[]{:S(2)}) %collective-permute-start.20) | collective-permute-done | bytes 131104 | tf_op jit(solution)/shard_map/ppermute | solution.py:31
  107.4 1.3 collective-permute-done.29.refs_1_
  108.7 1.8 %collective-permute-done.30.refs_2_ = bf16[2,4,32,256]{3,2,1,0:T(8,128)(2,1)S(1)} collective-permute-done((bf16[2,4,32,256]{3,2,1,0:T(8,128)(2,1)S(1)}, bf16[2,4,32,256]{3,2,1,0:T(8,128)(2,1)S(1)}, u32[]{:S(2)}, u32[]{:S(2)}) %collective-permute-start.30) | collective-permute-done | bytes 131104 | tf_op jit(solution)/shard_map/ppermute | solution.py:31
  111.2 3.8 %collective-permute-start.21 = (bf16[2,4,32,256]{3,2,1,0:T(8,128)(2,1)S(1)}, bf16[2,4,32,256]{3,2,1,0:T(8,128)(2,1)S(1)}, u32[]{:S(2)}, u32[]{:S(2)}) collective-permute-start(bf16[2,4,32,256]{3,2,1,0:T(8,128)(2,1)S(1)} %get-tuple-element.95), channel_id=1, source_target_pairs={{0,12},{1,13},{2,14},{3,15},{4,8},{5,9},{6,10},{7,11},{8,4},{9,5},... | collective-permute-start | bytes 393224 | tf_op jit(solution)/shard_map/ppermute | solution.py:31
  115.0 2.3 %row_backward_kernel.1 = (bf16[4,512,256]{2,1,0:T(8,128)(2,1)}, bf16[4,512,512]{2,1,0:T(8,128)(2,1)S(1)}) custom-call(s32[1]{0:T(128)} %bitcast.me_ref, bf16[4,512,512]{2,1,0:T(8,128)(2,1)S(1)} %copy-done, bf16[4,512,256]{2,1,0:T(8,128)(2,1)S(1)} %bitcast.9, bf16[8,4,32,256]{3,2,1,0:T(8,128)(2,1)S(1)} %gather_kernel.2.first_ref, ...), custom_call_target="tpu_custom_call" | custom-call | flops 1073741824 | bytes 7340032 | tf_op jit(solution)/shard_map/row_backward_kernel/pallas_call | solution.py:51
  117.4 0.9 collective-permute-done.21.refs_2_
  118.2 3.8 %collective-permute-start.24 = (bf16[2,4,32,256]{3,2,1,0:T(8,128)(2,1)S(1)}, bf16[2,4,32,256]{3,2,1,0:T(8,128)(2,1)S(1)}, u32[]{:S(2)}, u32[]{:S(2)}) collective-permute-start(bf16[2,4,32,256]{3,2,1,0:T(8,128)(2,1)S(1)} %get-tuple-element.98), channel_id=1, source_target_pairs={{0,4},{1,5},{2,6},{3,7},{4,0},{5,1},{6,2},{7,3},{8,12},{9,13},{10,... | collective-permute-start | bytes 393224 | tf_op jit(solution)/shard_map/ppermute | solution.py:31
  122.0 1.5 %collective-permute-done.22.refs_3_ = bf16[2,4,32,256]{3,2,1,0:T(8,128)(2,1)S(1)} collective-permute-done((bf16[2,4,32,256]{3,2,1,0:T(8,128)(2,1)S(1)}, bf16[2,4,32,256]{3,2,1,0:T(8,128)(2,1)S(1)}, u32[]{:S(2)}, u32[]{:S(2)}) %collective-permute-start.22) | collective-permute-done | bytes 131104 | tf_op jit(solution)/shard_map/ppermute | solution.py:31
  123.5 2.2 %collective-permute-start.33 = (bf16[2,4,32,256]{3,2,1,0:T(8,128)(2,1)S(1)}, bf16[2,4,32,256]{3,2,1,0:T(8,128)(2,1)S(1)}, u32[]{:S(2)}, u32[]{:S(2)}) collective-permute-start(bf16[2,4,32,256]{3,2,1,0:T(8,128)(2,1)S(1)} %get-tuple-element.111), channel_id=1, source_target_pairs={{0,14},{1,15},{2,12},{3,13},{4,10},{5,11},{6,8},{7,9},{8,6},{9,7},... | collective-permute-start | bytes 393224 | tf_op jit(solution)/shard_map/ppermute | solution.py:31
  125.7 4.8 %collective-permute-done.25.refs_6_ = bf16[2,4,32,256]{3,2,1,0:T(8,128)(2,1)S(1)} collective-permute-done((bf16[2,4,32,256]{3,2,1,0:T(8,128)(2,1)S(1)}, bf16[2,4,32,256]{3,2,1,0:T(8,128)(2,1)S(1)}, u32[]{:S(2)}, u32[]{:S(2)}) %collective-permute-start.25) | collective-permute-done | bytes 131104 | tf_op jit(solution)/shard_map/ppermute | solution.py:31
  130.5 2.3 %collective-permute-done.33.refs_7_ = bf16[2,4,32,256]{3,2,1,0:T(8,128)(2,1)S(1)} collective-permute-done((bf16[2,4,32,256]{3,2,1,0:T(8,128)(2,1)S(1)}, bf16[2,4,32,256]{3,2,1,0:T(8,128)(2,1)S(1)}, u32[]{:S(2)}, u32[]{:S(2)}) %collective-permute-start.33) | collective-permute-done | bytes 131104 | tf_op jit(solution)/shard_map/ppermute | solution.py:31
  132.8 1.8 %output_kernel.1 = (bf16[4,16,32,256]{3,2,1,0:T(8,128)(2,1)}, bf16[4,16,32,256]{3,2,1,0:T(8,128)(2,1)}) custom-call(s32[1]{0:T(128)} %bitcast.me_ref, bf16[4,16,32,256]{3,2,1,0:T(8,128)(2,1)S(1)} %bitcast.11, bf16[4,16,32,256]{3,2,1,0:T(8,128)(2,1)S(1)} %bitcast.13, bf16[2,4,32,256]{3,2,1,0:T(8,128)(2,1)S(1)} %get-tuple-element.93.refs_0_, ...), custom_call_target="tpu_custom_call" | custom-call | bytes 5242880 | tf_op jit(solution)/shard_map/output_kernel/pallas_call | solution.py:51
  134.6 2.3 %factor_sum_kernel.1 = (bf16[4,512,512]{2,1,0:T(8,128)(2,1)}, bf16[32,64,64]{2,1,0:T(8,128)(2,1)}) custom-call(s32[1]{0:T(128)} %bitcast.me_ref, bf16[4,512,512]{2,1,0:T(8,128)(2,1)S(1)} %get-tuple-element.110.term_ref, bf16[4,512,256]{2,1,0:T(8,128)(2,1)S(1)} %collective-permute-done.10.after_ref.values_ref, ...), custom_call_target="tpu_custom_call" | custom-call | flops 536870912 | bytes 7077888 | tf_op jit(solution)/shard_map/factor_sum_kernel/pallas_call | solution.py:51
  (49 shorter events, 2.4 us)
Async XLA Ops:
  0.6 6.1 %copy-start.1 = (bf16[1,2048,256]{2,1,0:T(8,128)(2,1)S(1)}, bf16[1,2048,256]{2,1,0:T(8,128)(2,1)}, u32[]{:S(2)}) copy-start(bf16[1,2048,256]{2,1,0:T(8,128)(2,1)} %param.5) | copy-start | bytes 3145732
  0.6 6.1 %copy-start = (bf16[4,512,512]{2,1,0:T(8,128)(2,1)S(1)}, bf16[4,512,512]{2,1,0:T(8,128)(2,1)}, u32[]{:S(2)}) copy-start(bf16[4,512,512]{2,1,0:T(8,128)(2,1)} %left_ref.3) | copy-start | bytes 6291460
  3.4 2.3 %collective-permute-start = (bf16[8,4,32,256]{3,2,1,0:T(8,128)(2,1)}, bf16[8,4,32,256]{3,2,1,0:T(8,128)(2,1)S(1)}, u32[]{:S(2)}, u32[]{:S(2)}) collective-permute-start(bf16[8,4,32,256]{3,2,1,0:T(8,128)(2,1)} %get-tuple-element.62), channel_id=1, source_target_pairs={{0,1},{1,0},{2,3},{3,2},{4,5},{5,4},{6,7},{7,6},{8,9},{9,8},{10,11... | collective-permute-start | bytes 1572872 | tf_op jit(solution)/shard_map/ppermute | solution.py:31
  5.7 1.0 copy-start.5
  6.8 38.1 %copy-start.4 = (bf16[32,64,64]{2,1,0:T(8,128)(2,1)S(1)}, bf16[32,64,64]{2,1,0:T(8,128)(2,1)}, u32[]{:S(2)}) copy-start(bf16[32,64,64]{2,1,0:T(8,128)(2,1)} %right_ref.3) | copy-start | bytes 786436
  7.6 8.2 %collective-permute-start.1 = (bf16[8,4,32,256]{3,2,1,0:T(8,128)(2,1)S(1)}, bf16[8,4,32,256]{3,2,1,0:T(8,128)(2,1)S(1)}, u32[]{:S(2)}, u32[]{:S(2)}) collective-permute-start(bf16[8,4,32,256]{3,2,1,0:T(8,128)(2,1)S(1)} %get-tuple-element.66), channel_id=1, source_target_pairs={{0,1},{1,0},{2,3},{3,2},{4,5},{5,4},{6,7},{7,6},{8,9},{9,8},{10,11... | collective-permute-start | bytes 1572872 | tf_op jit(solution)/shard_map/ppermute | solution.py:31
  8.0 19.3 %collective-permute-start.3 = (bf16[2,4,32,256]{3,2,1,0:T(8,128)(2,1)S(1)}, bf16[2,4,32,256]{3,2,1,0:T(8,128)(2,1)S(1)}, u32[]{:S(2)}, u32[]{:S(2)}) collective-permute-start(bf16[2,4,32,256]{3,2,1,0:T(8,128)(2,1)S(1)} %get-tuple-element.69), channel_id=1, source_target_pairs={{0,8},{1,9},{2,10},{3,11},{4,12},{5,13},{6,14},{7,15},{8,0},{9,1},... | collective-permute-start | bytes 393224 | tf_op jit(solution)/shard_map/ppermute | solution.py:31
  11.8 17.4 %collective-permute-start.4 = (bf16[2,4,32,256]{3,2,1,0:T(8,128)(2,1)S(1)}, bf16[2,4,32,256]{3,2,1,0:T(8,128)(2,1)S(1)}, u32[]{:S(2)}, u32[]{:S(2)}) collective-permute-start(bf16[2,4,32,256]{3,2,1,0:T(8,128)(2,1)S(1)} %get-tuple-element.70), channel_id=1, source_target_pairs={{0,12},{1,13},{2,14},{3,15},{4,8},{5,9},{6,10},{7,11},{8,4},{9,5},... | collective-permute-start | bytes 393224 | tf_op jit(solution)/shard_map/ppermute | solution.py:31
  13.1 21.2 %collective-permute-start.5 = (bf16[2,4,32,256]{3,2,1,0:T(8,128)(2,1)S(1)}, bf16[2,4,32,256]{3,2,1,0:T(8,128)(2,1)S(1)}, u32[]{:S(2)}, u32[]{:S(2)}) collective-permute-start(bf16[2,4,32,256]{3,2,1,0:T(8,128)(2,1)S(1)} %get-tuple-element.71), channel_id=1, source_target_pairs={{0,10},{1,11},{2,8},{3,9},{4,14},{5,15},{6,12},{7,13},{8,2},{9,3},... | collective-permute-start | bytes 393224 | tf_op jit(solution)/shard_map/ppermute | solution.py:31
  15.8 19.8 %collective-permute-start.2 = (bf16[2,4,32,256]{3,2,1,0:T(8,128)(2,1)S(1)}, bf16[2,4,32,256]{3,2,1,0:T(8,128)(2,1)S(1)}, u32[]{:S(2)}, u32[]{:S(2)}) collective-permute-start(bf16[2,4,32,256]{3,2,1,0:T(8,128)(2,1)S(1)} %get-tuple-element.67), channel_id=1, source_target_pairs={{0,8},{1,9},{2,10},{3,11},{4,12},{5,13},{6,14},{7,15},{8,0},{9,1},... | collective-permute-start | bytes 393224 | tf_op jit(solution)/shard_map/ppermute | solution.py:31
  17.1 60.4 %collective-permute-start.10 = (bf16[4,512,256]{2,1,0:T(8,128)(2,1)S(1)}, bf16[4,512,256]{2,1,0:T(8,128)(2,1)S(1)}, u32[]{:S(2)}, u32[]{:S(2)}) collective-permute-start(bf16[4,512,256]{2,1,0:T(8,128)(2,1)S(1)} %bitcast.8), channel_id=1, source_target_pairs={{0,16},{16,0},{1,17},{17,1},{2,18},{18,2},{3,19},{19,3},{4,20},{20... | collective-permute-start | bytes 3145736 | tf_op jit(solution)/shard_map/ppermute | solution.py:16
  27.3 12.8 %collective-permute-start.6 = (bf16[2,4,32,256]{3,2,1,0:T(8,128)(2,1)S(1)}, bf16[2,4,32,256]{3,2,1,0:T(8,128)(2,1)S(1)}, u32[]{:S(2)}, u32[]{:S(2)}) collective-permute-start(bf16[2,4,32,256]{3,2,1,0:T(8,128)(2,1)S(1)} %get-tuple-element.72), channel_id=1, source_target_pairs={{0,2},{1,3},{2,0},{3,1},{4,6},{5,7},{6,4},{7,5},{8,10},{9,11},{10,... | collective-permute-start | bytes 393224 | tf_op jit(solution)/shard_map/ppermute | solution.py:31
  29.1 10.9 %collective-permute-start.7 = (bf16[2,4,32,256]{3,2,1,0:T(8,128)(2,1)S(1)}, bf16[2,4,32,256]{3,2,1,0:T(8,128)(2,1)S(1)}, u32[]{:S(2)}, u32[]{:S(2)}) collective-permute-start(bf16[2,4,32,256]{3,2,1,0:T(8,128)(2,1)S(1)} %get-tuple-element.73), channel_id=1, source_target_pairs={{0,4},{1,5},{2,6},{3,7},{4,0},{5,1},{6,2},{7,3},{8,12},{9,13},{10,... | collective-permute-start | bytes 393224 | tf_op jit(solution)/shard_map/ppermute | solution.py:31
  34.3 10.6 %collective-permute-start.8 = (bf16[2,4,32,256]{3,2,1,0:T(8,128)(2,1)S(1)}, bf16[2,4,32,256]{3,2,1,0:T(8,128)(2,1)S(1)}, u32[]{:S(2)}, u32[]{:S(2)}) collective-permute-start(bf16[2,4,32,256]{3,2,1,0:T(8,128)(2,1)S(1)} %get-tuple-element.74), channel_id=1, source_target_pairs={{0,6},{1,7},{2,4},{3,5},{4,2},{5,3},{6,0},{7,1},{8,14},{9,15},{10,... | collective-permute-start | bytes 393224 | tf_op jit(solution)/shard_map/ppermute | solution.py:31
  35.6 9.3 %collective-permute-start.9 = (bf16[2,4,32,256]{3,2,1,0:T(8,128)(2,1)S(1)}, bf16[2,4,32,256]{3,2,1,0:T(8,128)(2,1)S(1)}, u32[]{:S(2)}, u32[]{:S(2)}) collective-permute-start(bf16[2,4,32,256]{3,2,1,0:T(8,128)(2,1)S(1)} %get-tuple-element.77), channel_id=1, source_target_pairs={{0,14},{1,15},{2,12},{3,13},{4,10},{5,11},{6,8},{7,9},{8,6},{9,7},... | collective-permute-start | bytes 393224 | tf_op jit(solution)/shard_map/ppermute | solution.py:31
  47.9 3.6 %collective-permute-start.11 = (bf16[8,4,32,256]{3,2,1,0:T(8,128)(2,1)S(1)}, bf16[8,4,32,256]{3,2,1,0:T(8,128)(2,1)S(1)}, u32[]{:S(2)}, u32[]{:S(2)}) collective-permute-start(bf16[8,4,32,256]{3,2,1,0:T(8,128)(2,1)S(1)} %get-tuple-element.80), channel_id=1, source_target_pairs={{0,1},{1,0},{2,3},{3,2},{4,5},{5,4},{6,7},{7,6},{8,9},{9,8},{10,11... | collective-permute-start | bytes 1572872 | tf_op jit(solution)/shard_map/ppermute | solution.py:31
  48.0 8.3 %collective-permute-start.13 = (bf16[2,4,32,256]{3,2,1,0:T(8,128)(2,1)S(1)}, bf16[2,4,32,256]{3,2,1,0:T(8,128)(2,1)S(1)}, u32[]{:S(2)}, u32[]{:S(2)}) collective-permute-start(bf16[2,4,32,256]{3,2,1,0:T(8,128)(2,1)S(1)} %get-tuple-element.83), channel_id=1, source_target_pairs={{0,12},{1,13},{2,14},{3,15},{4,8},{5,9},{6,10},{7,11},{8,4},{9,5},... | collective-permute-start | bytes 393224 | tf_op jit(solution)/shard_map/ppermute | solution.py:31
  51.5 15.2 %collective-permute-start.14 = (bf16[2,4,32,256]{3,2,1,0:T(8,128)(2,1)S(1)}, bf16[2,4,32,256]{3,2,1,0:T(8,128)(2,1)S(1)}, u32[]{:S(2)}, u32[]{:S(2)}) collective-permute-start(bf16[2,4,32,256]{3,2,1,0:T(8,128)(2,1)S(1)} %get-tuple-element.84), channel_id=1, source_target_pairs={{0,10},{1,11},{2,8},{3,9},{4,14},{5,15},{6,12},{7,13},{8,2},{9,3},... | collective-permute-start | bytes 393224 | tf_op jit(solution)/shard_map/ppermute | solution.py:31
  51.6 17.0 %collective-permute-start.12 = (bf16[2,4,32,256]{3,2,1,0:T(8,128)(2,1)S(1)}, bf16[2,4,32,256]{3,2,1,0:T(8,128)(2,1)S(1)}, u32[]{:S(2)}, u32[]{:S(2)}) collective-permute-start(bf16[2,4,32,256]{3,2,1,0:T(8,128)(2,1)S(1)} %get-tuple-element.81), channel_id=1, source_target_pairs={{0,8},{1,9},{2,10},{3,11},{4,12},{5,13},{6,14},{7,15},{8,0},{9,1},... | collective-permute-start | bytes 393224 | tf_op jit(solution)/shard_map/ppermute | solution.py:31
  54.5 17.4 %collective-permute-start.15 = (bf16[2,4,32,256]{3,2,1,0:T(8,128)(2,1)S(1)}, bf16[2,4,32,256]{3,2,1,0:T(8,128)(2,1)S(1)}, u32[]{:S(2)}, u32[]{:S(2)}) collective-permute-start(bf16[2,4,32,256]{3,2,1,0:T(8,128)(2,1)S(1)} %get-tuple-element.85), channel_id=1, source_target_pairs={{0,2},{1,3},{2,0},{3,1},{4,6},{5,7},{6,4},{7,5},{8,10},{9,11},{10,... | collective-permute-start | bytes 393224 | tf_op jit(solution)/shard_map/ppermute | solution.py:31
  56.2 15.7 %collective-permute-start.16 = (bf16[2,4,32,256]{3,2,1,0:T(8,128)(2,1)S(1)}, bf16[2,4,32,256]{3,2,1,0:T(8,128)(2,1)S(1)}, u32[]{:S(2)}, u32[]{:S(2)}) collective-permute-start(bf16[2,4,32,256]{3,2,1,0:T(8,128)(2,1)S(1)} %get-tuple-element.86), channel_id=1, source_target_pairs={{0,4},{1,5},{2,6},{3,7},{4,0},{5,1},{6,2},{7,3},{8,12},{9,13},{10,... | collective-permute-start | bytes 393224 | tf_op jit(solution)/shard_map/ppermute | solution.py:31
  66.7 10.9 %collective-permute-start.17 = (bf16[2,4,32,256]{3,2,1,0:T(8,128)(2,1)S(1)}, bf16[2,4,32,256]{3,2,1,0:T(8,128)(2,1)S(1)}, u32[]{:S(2)}, u32[]{:S(2)}) collective-permute-start(bf16[2,4,32,256]{3,2,1,0:T(8,128)(2,1)S(1)} %get-tuple-element.87), channel_id=1, source_target_pairs={{0,6},{1,7},{2,4},{3,5},{4,2},{5,3},{6,0},{7,1},{8,14},{9,15},{10,... | collective-permute-start | bytes 393224 | tf_op jit(solution)/shard_map/ppermute | solution.py:31
  68.6 9.0 %collective-permute-start.18 = (bf16[2,4,32,256]{3,2,1,0:T(8,128)(2,1)S(1)}, bf16[2,4,32,256]{3,2,1,0:T(8,128)(2,1)S(1)}, u32[]{:S(2)}, u32[]{:S(2)}) collective-permute-start(bf16[2,4,32,256]{3,2,1,0:T(8,128)(2,1)S(1)} %get-tuple-element.90), channel_id=1, source_target_pairs={{0,14},{1,15},{2,12},{3,13},{4,10},{5,11},{6,8},{7,9},{8,6},{9,7},... | collective-permute-start | bytes 393224 | tf_op jit(solution)/shard_map/ppermute | solution.py:31
  80.7 5.1 %collective-permute-start.19 = (bf16[8,4,32,256]{3,2,1,0:T(8,128)(2,1)S(1)}, bf16[8,4,32,256]{3,2,1,0:T(8,128)(2,1)S(1)}, u32[]{:S(2)}, u32[]{:S(2)}) collective-permute-start(bf16[8,4,32,256]{3,2,1,0:T(8,128)(2,1)S(1)} %get-tuple-element.92), channel_id=1, source_target_pairs={{0,1},{1,0},{2,3},{3,2},{4,5},{5,4},{6,7},{7,6},{8,9},{9,8},{10,11... | collective-permute-start | bytes 1572872 | tf_op jit(solution)/shard_map/ppermute | solution.py:31
  80.8 20.7 %collective-permute-start.32 = (bf16[32,64,64]{2,1,0:T(8,128)(2,1)S(1)}, bf16[32,64,64]{2,1,0:T(8,128)(2,1)S(1)}, u32[]{:S(2)}, u32[]{:S(2)}) collective-permute-start(bf16[32,64,64]{2,1,0:T(8,128)(2,1)S(1)} %get-tuple-element.108.right_ref), channel_id=1, source_target_pairs={{0,16},{16,0},{1,17},{17,1},{2,18},{18,2},{3,19},{19,3},{4,20},{20... | collective-permute-start | bytes 786440 | tf_op jit(solution)/shard_map/ppermute | solution.py:16
  82.3 8.2 %collective-permute-start.26 = (bf16[2,4,32,256]{3,2,1,0:T(8,128)(2,1)S(1)}, bf16[2,4,32,256]{3,2,1,0:T(8,128)(2,1)S(1)}, u32[]{:S(2)}, u32[]{:S(2)}) collective-permute-start(bf16[2,4,32,256]{3,2,1,0:T(8,128)(2,1)S(1)} %get-tuple-element.101), channel_id=1, source_target_pairs={{0,12},{1,13},{2,14},{3,15},{4,8},{5,9},{6,10},{7,11},{8,4},{9,5},... | collective-permute-start | bytes 393224 | tf_op jit(solution)/shard_map/ppermute | solution.py:31
  85.0 16.5 %collective-permute-start.27 = (bf16[2,4,32,256]{3,2,1,0:T(8,128)(2,1)S(1)}, bf16[2,4,32,256]{3,2,1,0:T(8,128)(2,1)S(1)}, u32[]{:S(2)}, u32[]{:S(2)}) collective-permute-start(bf16[2,4,32,256]{3,2,1,0:T(8,128)(2,1)S(1)} %get-tuple-element.102), channel_id=1, source_target_pairs={{0,10},{1,11},{2,8},{3,9},{4,14},{5,15},{6,12},{7,13},{8,2},{9,3},... | collective-permute-start | bytes 393224 | tf_op jit(solution)/shard_map/ppermute | solution.py:31
  85.0 22.4 %collective-permute-start.28 = (bf16[2,4,32,256]{3,2,1,0:T(8,128)(2,1)S(1)}, bf16[2,4,32,256]{3,2,1,0:T(8,128)(2,1)S(1)}, u32[]{:S(2)}, u32[]{:S(2)}) collective-permute-start(bf16[2,4,32,256]{3,2,1,0:T(8,128)(2,1)S(1)} %get-tuple-element.103), channel_id=1, source_target_pairs={{0,2},{1,3},{2,0},{3,1},{4,6},{5,7},{6,4},{7,5},{8,10},{9,11},{10,... | collective-permute-start | bytes 393224 | tf_op jit(solution)/shard_map/ppermute | solution.py:31
  85.9 17.9 %collective-permute-start.31 = (bf16[2,4,32,256]{3,2,1,0:T(8,128)(2,1)S(1)}, bf16[2,4,32,256]{3,2,1,0:T(8,128)(2,1)S(1)}, u32[]{:S(2)}, u32[]{:S(2)}) collective-permute-start(bf16[2,4,32,256]{3,2,1,0:T(8,128)(2,1)S(1)} %get-tuple-element.107), channel_id=1, source_target_pairs={{0,14},{1,15},{2,12},{3,13},{4,10},{5,11},{6,8},{7,9},{8,6},{9,7},... | collective-permute-start | bytes 393224 | tf_op jit(solution)/shard_map/ppermute | solution.py:31
  90.6 16.8 %collective-permute-start.20 = (bf16[2,4,32,256]{3,2,1,0:T(8,128)(2,1)S(1)}, bf16[2,4,32,256]{3,2,1,0:T(8,128)(2,1)S(1)}, u32[]{:S(2)}, u32[]{:S(2)}) collective-permute-start(bf16[2,4,32,256]{3,2,1,0:T(8,128)(2,1)S(1)} %get-tuple-element.94), channel_id=1, source_target_pairs={{0,8},{1,9},{2,10},{3,11},{4,12},{5,13},{6,14},{7,15},{8,0},{9,1},... | collective-permute-start | bytes 393224 | tf_op jit(solution)/shard_map/ppermute | solution.py:31
  101.5 7.2 %collective-permute-start.29 = (bf16[2,4,32,256]{3,2,1,0:T(8,128)(2,1)S(1)}, bf16[2,4,32,256]{3,2,1,0:T(8,128)(2,1)S(1)}, u32[]{:S(2)}, u32[]{:S(2)}) collective-permute-start(bf16[2,4,32,256]{3,2,1,0:T(8,128)(2,1)S(1)} %get-tuple-element.104), channel_id=1, source_target_pairs={{0,4},{1,5},{2,6},{3,7},{4,0},{5,1},{6,2},{7,3},{8,12},{9,13},{10,... | collective-permute-start | bytes 393224 | tf_op jit(solution)/shard_map/ppermute | solution.py:31
  101.5 9.1 %collective-permute-start.30 = (bf16[2,4,32,256]{3,2,1,0:T(8,128)(2,1)S(1)}, bf16[2,4,32,256]{3,2,1,0:T(8,128)(2,1)S(1)}, u32[]{:S(2)}, u32[]{:S(2)}) collective-permute-start(bf16[2,4,32,256]{3,2,1,0:T(8,128)(2,1)S(1)} %get-tuple-element.105), channel_id=1, source_target_pairs={{0,6},{1,7},{2,4},{3,5},{4,2},{5,3},{6,0},{7,1},{8,14},{9,15},{10,... | collective-permute-start | bytes 393224 | tf_op jit(solution)/shard_map/ppermute | solution.py:31
  103.8 30.8 %collective-permute-start.34 = (bf16[8,4,32,256]{3,2,1,0:T(8,128)(2,1)S(1)}, bf16[8,4,32,256]{3,2,1,0:T(8,128)(2,1)S(1)}, u32[]{:S(2)}, u32[]{:S(2)}) collective-permute-start(bf16[8,4,32,256]{3,2,1,0:T(8,128)(2,1)S(1)} %gather_kernel.2.first_ref), channel_id=1, source_target_pairs={{0,16},{16,0},{1,17},{17,1},{2,18},{18,2},{3,19},{19,3},{4,20},{20... | collective-permute-start | bytes 1572872 | tf_op jit(solution)/shard_map/ppermute | solution.py:16
  110.6 24.0 %collective-permute-start.35 = (bf16[8,4,32,256]{3,2,1,0:T(8,128)(2,1)S(1)}, bf16[8,4,32,256]{3,2,1,0:T(8,128)(2,1)S(1)}, u32[]{:S(2)}, u32[]{:S(2)}) collective-permute-start(bf16[8,4,32,256]{3,2,1,0:T(8,128)(2,1)S(1)} %gather_kernel.3.second_ref), channel_id=1, source_target_pairs={{0,16},{16,0},{1,17},{17,1},{2,18},{18,2},{3,19},{19,3},{4,20},{20... | collective-permute-start | bytes 1572872 | tf_op jit(solution)/shard_map/ppermute | solution.py:16
  111.2 7.0 %collective-permute-start.21 = (bf16[2,4,32,256]{3,2,1,0:T(8,128)(2,1)S(1)}, bf16[2,4,32,256]{3,2,1,0:T(8,128)(2,1)S(1)}, u32[]{:S(2)}, u32[]{:S(2)}) collective-permute-start(bf16[2,4,32,256]{3,2,1,0:T(8,128)(2,1)S(1)} %get-tuple-element.95), channel_id=1, source_target_pairs={{0,12},{1,13},{2,14},{3,15},{4,8},{5,9},{6,10},{7,11},{8,4},{9,5},... | collective-permute-start | bytes 393224 | tf_op jit(solution)/shard_map/ppermute | solution.py:31
  115.0 8.5 %collective-permute-start.22 = (bf16[2,4,32,256]{3,2,1,0:T(8,128)(2,1)S(1)}, bf16[2,4,32,256]{3,2,1,0:T(8,128)(2,1)S(1)}, u32[]{:S(2)}, u32[]{:S(2)}) collective-permute-start(bf16[2,4,32,256]{3,2,1,0:T(8,128)(2,1)S(1)} %get-tuple-element.96), channel_id=1, source_target_pairs={{0,10},{1,11},{2,8},{3,9},{4,14},{5,15},{6,12},{7,13},{8,2},{9,3},... | collective-permute-start | bytes 393224 | tf_op jit(solution)/shard_map/ppermute | solution.py:31
  115.0 17.8 %copy-start.2 = (bf16[1,2048,256]{2,1,0:T(8,128)(2,1)S(1)}, bf16[1,2048,256]{2,1,0:T(8,128)(2,1)}, u32[]{:S(2)}) copy-start(bf16[1,2048,256]{2,1,0:T(8,128)(2,1)} %param.6) | copy-start | bytes 3145732
  115.0 17.8 %copy-start.3 = (bf16[1,2048,256]{2,1,0:T(8,128)(2,1)S(1)}, bf16[1,2048,256]{2,1,0:T(8,128)(2,1)}, u32[]{:S(2)}) copy-start(bf16[1,2048,256]{2,1,0:T(8,128)(2,1)} %param.7) | copy-start | bytes 3145732
  115.0 8.5 %collective-permute-start.23 = (bf16[2,4,32,256]{3,2,1,0:T(8,128)(2,1)S(1)}, bf16[2,4,32,256]{3,2,1,0:T(8,128)(2,1)S(1)}, u32[]{:S(2)}, u32[]{:S(2)}) collective-permute-start(bf16[2,4,32,256]{3,2,1,0:T(8,128)(2,1)S(1)} %get-tuple-element.97), channel_id=1, source_target_pairs={{0,2},{1,3},{2,0},{3,1},{4,6},{5,7},{6,4},{7,5},{8,10},{9,11},{10,... | collective-permute-start | bytes 393224 | tf_op jit(solution)/shard_map/ppermute | solution.py:31
  118.2 7.5 %collective-permute-start.24 = (bf16[2,4,32,256]{3,2,1,0:T(8,128)(2,1)S(1)}, bf16[2,4,32,256]{3,2,1,0:T(8,128)(2,1)S(1)}, u32[]{:S(2)}, u32[]{:S(2)}) collective-permute-start(bf16[2,4,32,256]{3,2,1,0:T(8,128)(2,1)S(1)} %get-tuple-element.98), channel_id=1, source_target_pairs={{0,4},{1,5},{2,6},{3,7},{4,0},{5,1},{6,2},{7,3},{8,12},{9,13},{10,... | collective-permute-start | bytes 393224 | tf_op jit(solution)/shard_map/ppermute | solution.py:31
  123.5 6.9 %collective-permute-start.25 = (bf16[2,4,32,256]{3,2,1,0:T(8,128)(2,1)S(1)}, bf16[2,4,32,256]{3,2,1,0:T(8,128)(2,1)S(1)}, u32[]{:S(2)}, u32[]{:S(2)}) collective-permute-start(bf16[2,4,32,256]{3,2,1,0:T(8,128)(2,1)S(1)} %get-tuple-element.99), channel_id=1, source_target_pairs={{0,6},{1,7},{2,4},{3,5},{4,2},{5,3},{6,0},{7,1},{8,14},{9,15},{10,... | collective-permute-start | bytes 393224 | tf_op jit(solution)/shard_map/ppermute | solution.py:31
  123.5 9.3 %collective-permute-start.33 = (bf16[2,4,32,256]{3,2,1,0:T(8,128)(2,1)S(1)}, bf16[2,4,32,256]{3,2,1,0:T(8,128)(2,1)S(1)}, u32[]{:S(2)}, u32[]{:S(2)}) collective-permute-start(bf16[2,4,32,256]{3,2,1,0:T(8,128)(2,1)S(1)} %get-tuple-element.111), channel_id=1, source_target_pairs={{0,14},{1,15},{2,12},{3,13},{4,10},{5,11},{6,8},{7,9},{8,6},{9,7},... | collective-permute-start | bytes 393224 | tf_op jit(solution)/shard_map/ppermute | solution.py:31

commit v9 on v3

--- a/solution.py
+++ b/solution.py
@@ -7,7 +7,7 @@
 
 BF16 = jnp.bfloat16
 F32 = jnp.float32
-VMEM_LIMIT = 48 * 1024 * 1024
+MIB = 1024 * 1024
 
 
 def swap_sequences(array):
@@ -18,16 +18,24 @@
     return lax.all_to_all(blocks, "seq", split_axis=0, concat_axis=0, tiled=True)
 
 
-def call(kernel, inputs, out_shapes, scratch=(), flops=0):
+def after(array, earlier):
+    return lax.optimization_barrier((array, earlier))[0]
+
+
+def call(kernel, inputs, out_shapes, scratch=(), flops=0, unblocked=(), vmem=48):
     whole = pl.BlockSpec(memory_space=pltpu.VMEM)
     moved = sum(x.size * x.dtype.itemsize for x in (*inputs, *out_shapes))
     return pl.pallas_call(
         kernel,
         out_shape=out_shapes,
-        in_specs=[whole] * len(inputs),
+        in_specs=[
+            pl.BlockSpec(memory_space=pl.ANY) if n in unblocked else whole
+            for n in range(len(inputs))
+        ],
         out_specs=[whole] * len(out_shapes),
         scratch_shapes=scratch,
-        compiler_params=pltpu.CompilerParams(vmem_limit_bytes=VMEM_LIMIT),
+        compiler_params=pltpu.CompilerParams(vmem_limit_bytes=vmem * MIB),
+        name=kernel.__name__,
         cost_estimate=pl.CostEstimate(flops=flops, bytes_accessed=moved, transcendentals=0),
     )(*inputs)
 
@@ -36,24 +44,33 @@
     return lax.dot_general(a, b, (contract, ((), ())), preferred_element_type=F32)
 
 
-def product_kernel(gate_ref, cotangent_ref, out_ref):
-    for i in range(gate_ref.shape[0]):
-        wide = gate_ref[i].astype(F32) * cotangent_ref[i].astype(F32)
-        out_ref[:, i] = wide.astype(BF16)
-
-
-def mix_kernel(left_ref, values_ref, out_ref):
-    seq, rows, cols, channels = out_ref.shape
+def send_kernel(gate_hbm, cotangent_hbm, left_hbm, values_hbm, out_ref, gate, cotangent, left, values, sems):
+    seq, _, rows, cols, channels = out_ref.shape
+    pairs = [(gate_hbm, gate), (cotangent_hbm, cotangent), (left_hbm, left), (values_hbm, values)]
+    loads = [
+        [
+            pltpu.make_async_copy(source.at[i], target.at[i], sems.at[n, i])
+            for n, (source, target) in enumerate(pairs)
+        ]
+        for i in range(rows)
+    ]
+    for row in loads:
+        for load in row:
+            load.start()
     for i in range(rows):
-        mixed = dot(left_ref[i], values_ref[i], ((1,), (0,)))
-        out_ref[:, i] = mixed.astype(BF16).reshape(seq, cols, channels)
-
-
-def load_columns(in_ref, wide):
+        for load in loads[i]:
+            load.wait()
+        mixed = dot(left[i], values[i], ((1,), (0,)))
+        out_ref[:, 1, i] = mixed.astype(BF16).reshape(seq, cols, channels)
+        wide = gate[i].astype(F32) * cotangent[i].astype(F32)
+        out_ref[:, 0, i] = wide.astype(BF16)
+
+
+def load_columns(in_ref, which, wide):
     for p in range(in_ref.shape[0]):
-        rows, cols, channels = in_ref.shape[1:]
+        rows, cols, channels = in_ref.shape[2:]
         size = rows * cols
-        block = in_ref[p].reshape(size, channels).astype(F32)
+        block = in_ref[p, which].reshape(size, channels).astype(F32)
         for h in range(channels // 128):
             wide[h, p * size : (p + 1) * size, :] = block[:, h * 128 : (h + 1) * 128]
 
@@ -77,9 +94,9 @@
         out_ref[p] = block.reshape(rows, cols, channels)
 
 
-def column_backward_kernel(right_ref, in_ref, out_ref, by_column_ref, wide, wide_out):
+def column_backward_kernel(right_ref, after_ref, in_ref, out_ref, by_column_ref, wide, wide_out):
     cols, count, _ = right_ref.shape
-    load_columns(in_ref, wide)
+    load_columns(in_ref, 0, wide)
     for k in range(cols):
         grad = column(wide, k, count, cols)
         by_column_ref[k] = grad
@@ -89,7 +106,7 @@
 
 def column_forward_kernel(right_ref, grad_ref, in_ref, out_ref, part_ref, wide, wide_out):
     cols, count, _ = right_ref.shape
-    load_columns(in_ref, wide)
+    load_columns(in_ref, 1, wide)
     for k in range(cols):
         mixed = column(wide, k, count, cols)
         store_column(wide_out, k, count, cols, dot(right_ref[k], mixed, ((1,), (0,))))
@@ -109,10 +126,13 @@
         term_ref[i] = dot(grad, values_ref[i], ((1,), (1,))).astype(BF16)
 
 
-def left_sum_kernel(term_ref, values_ref, grad_ref, out_ref):
+def factor_sum_kernel(
+    term_ref, values_ref, grad_ref, right_ref, other_ref, left_out_ref, right_out_ref
+):
     for i in range(term_ref.shape[0]):
         other = dot(grad_ref[i], values_ref[i], ((1,), (1,))).astype(BF16)
-        out_ref[i] = (term_ref[i].astype(F32) + other.astype(F32)).astype(BF16)
+        left_out_ref[i] = (term_ref[i].astype(F32) + other.astype(F32)).astype(BF16)
+    right_out_ref[...] = (right_ref[...].astype(F32) + other_ref[...].astype(F32)).astype(BF16)
 
 
 def output_kernel(gate_ref, cotangent_ref, in_ref, out_ref, grad_ref):
@@ -141,39 +161,52 @@
     row_flops = 2 * rows * block_len * block_len * channels
     column_flops = 2 * cols * count * count * channels
 
-    (grad_rows,) = call(product_kernel, [gate, cotangent], [blocks])
-    grad_blocks = exchange(grad_rows)
-    other_values = swap_sequences(values)
-    (mixed_rows,) = call(mix_kernel, [left_factor, values], [blocks], flops=row_flops)
-    mixed_blocks = exchange(mixed_rows)
+    pairs = jax.ShapeDtypeStruct((seq, 2, rows, cols, channels), BF16)
+    loaded = (gate, cotangent, left_factor, values)
+    (sent,) = call(
+        send_kernel,
+        loaded,
+        [pairs],
+        [pltpu.VMEM(x.shape, BF16) for x in loaded] + [pltpu.SemaphoreType.DMA((4, rows))],
+        row_flops,
+        unblocked=range(4),
+        vmem=60,
+    )
+    received = exchange(sent)
+    other_values = swap_sequences(after(values, sent))
     grad_second, grad_column = call(
         column_backward_kernel,
-        [right_factor, grad_blocks],
+        [right_factor, other_values, received],
         [blocks, by_column],
         [wide, wide],
         column_flops,
+        unblocked=[1],
     )
     back_blocks = exchange(grad_second)
     second, right_part = call(
         column_forward_kernel,
-        [right_factor, grad_column, mixed_blocks],
+        [right_factor, grad_column, received],
         [blocks, right],
         [wide, wide],
         2 * column_flops,
     )
-    second_blocks = exchange(second)
     other_right = swap_sequences(right_part)
+    second_blocks = exchange(after(second, other_right))
     (gathered,) = call(gather_kernel, [back_blocks], [whole])
     grad_back = gathered.reshape(rows, block_len, channels)
     other_grad_back = swap_sequences(grad_back)
     grad_signal, left_term = call(
         row_backward_kernel, [left_factor, values, grad_back], [by_row, left], flops=2 * row_flops
     )
-    (grad_left,) = call(
-        left_sum_kernel, [left_term, other_values, other_grad_back], [left], flops=row_flops
-    )
-    grad_right = (right_part.astype(F32) + other_right.astype(F32)).astype(BF16)
-    output, grad_gate = call(output_kernel, [gate, cotangent, second_blocks], [whole, whole])
+    grad_left, grad_right = call(
+        factor_sum_kernel,
+        [left_term, other_values, other_grad_back, right_part, other_right],
+        [left, right],
+        flops=row_flops,
+    )
+    output, grad_gate = call(
+        output_kernel, [after(gate, left_term), cotangent, second_blocks], [whole, whole]
+    )
     return (
         output.reshape(signal.shape),
         grad_gate.reshape(signal.shape),

time: 174 us -> 133 us (0.76)
  waiting for transfers between devices: 108 us -> 67.2 us
  Pallas kernels: 18.9 us -> 24.2 us
  other arithmetic: 2.02 us -> 0 us
    all_to_all x4 -> x3, waiting for transfers between devices: 54.4 us -> 29.3 us  [exchange(): lax.all_to_all(blocks, 'seq', split_axis=0, concat_axis=0, tiled=True)]
    ppermute x3, waiting for transfers between devices: 53.6 us -> 37.9 us  [swap_sequences(): return lax.ppermute(array, 'dp', [(0, 1), (1, 0)])]
    pallas_call x8 -> x7, Pallas kernels: 18.9 us -> 24.2 us  [call(): pl.pallas_call(kernel, out_shape=out_shapes, in_specs=[pl.BlockSpec(memor...]
    all_to_all x4 -> x3, starting transfers between devices: 28 us -> 25.6 us  [exchange(): lax.all_to_all(blocks, 'seq', split_axis=0, concat_axis=0, tiled=True)]
    convert_element_type x1 -> x0, other arithmetic: 2.02 us -> none  [direct_shards(): grad_right = (right_part.astype(F32) + other_right.astype(F32)).astype(BF16)]
    unnamed x34 -> x30, local copies, waits for them, and re-layouts: 11.8 us -> 10.4 us
  transfers between devices with their start and end apart: 7 -> 6, of which waited for: 4 -> 6; matrix products, arithmetic and copies ran while one was open for 1% -> 0% of each run, Pallas kernels for 8% -> 10%
where the time goes in v9:
time: 133 us
  waiting for transfers between devices  67.2 us (51%)
  starting transfers between devices  30.1 us (23%)
  Pallas kernels  24.2 us (18%)
  local copies, waits for them, and re-layouts  10.4 us (8%)
    ppermute x3, waiting for transfers between devices, swap_sequences(): return lax.ppermute(array, 'dp', [(0, 1), (1, 0)])  37.9 us
    all_to_all x3, waiting for transfers between devices, exchange(): lax.all_to_all(blocks, 'seq', split_axis=0, concat_axis=0, tiled=True)  29.3 us
    all_to_all x3, starting transfers between devices, exchange(): lax.all_to_all(blocks, 'seq', split_axis=0, concat_axis=0, tiled=True)  25.6 us
    pallas_call x7, Pallas kernels, call(): pl.pallas_call(kernel, out_shape=out_shapes, in_specs=[pl.BlockSpec(memor...  24.2 us
    unnamed x30, local copies, waits for them, and re-layouts  10.4 us
    ppermute x3, starting transfers between devices, swap_sequences(): return lax.ppermute(array, 'dp', [(0, 1), (1, 0)])  4.56 us
  transfers between devices with their start and end apart: 6, of which 6 were waited for; matrix products, arithmetic and copies ran while one was open for 0% of the time, Pallas kernels for 10%

profile of v9, /device:TPU:0, one launch (start us, length us, event | category | flops | bytes accessed | tf_op | source)
XLA Modules:
  0.0 132.7 jit_solution(13490472853253800391)
XLA Ops:
  0.6 4.7 %send_kernel.1 = bf16[16,2,4,32,256]{4,3,2,1,0:T(8,128)(2,1)} custom-call(bf16[4,16,32,256]{3,2,1,0:T(8,128)(2,1)} %bitcast.7, bf16[4,16,32,256]{3,2,1,0:T(8,128)(2,1)} %bitcast.9, bf16[4,512,512]{2,1,0:T(8,128)(2,1)} %left_ref.1, bf16[4,512,256]{2,1,0:T(8,128)(2,1)} %bitcast.11), custom_call_target="tpu_custom_call" | custom-call | flops 536870912 | bytes 7340032 | tf_op jit(solution)/shard_map/send_kernel/pallas_call | solution.py:28
  5.3 7.4 %all-to-all-start = ((bf16[16,2,4,32,256]{4,3,2,1,0:T(8,128)(2,1)}), bf16[16,2,4,32,256]{4,3,2,1,0:T(8,128)(2,1)S(1)}, u32[]{:S(2)}, u32[]{:S(2)}) async-start(bf16[16,2,4,32,256]{4,3,2,1,0:T(8,128)(2,1)} %send_kernel.1), calls=%async_computation | async-start | bytes 4194304 | tf_op jit(solution)/shard_map/all_to_all | solution.py:18
  12.7 1.6 %collective-permute-start = (bf16[4,512,256]{2,1,0:T(8,128)(2,1)}, bf16[4,512,256]{2,1,0:T(8,128)(2,1)S(1)}, u32[]{:S(2)}, u32[]{:S(2)}) collective-permute-start(bf16[4,512,256]{2,1,0:T(8,128)(2,1)} %bitcast.12), channel_id=1, source_target_pairs={{0,16},{16,0},{1,17},{17,1},{2,18},{18,2},{3,19},{19,3},{4,20},{20... | collective-permute-start | bytes 3145736 | tf_op jit(solution)/shard_map/ppermute | solution.py:14
  14.3 24.1 %collective-permute-done.after_ref.values_ref = bf16[4,512,256]{2,1,0:T(8,128)(2,1)S(1)} collective-permute-done((bf16[4,512,256]{2,1,0:T(8,128)(2,1)}, bf16[4,512,256]{2,1,0:T(8,128)(2,1)S(1)}, u32[]{:S(2)}, u32[]{:S(2)}) %collective-permute-start) | collective-permute-done | bytes 1048608 | tf_op jit(solution)/shard_map/ppermute | solution.py:14
  38.4 15.4 %all-to-all-done.in_ref = bf16[16,2,4,32,256]{4,3,2,1,0:T(8,128)(2,1)S(1)} async-done(((bf16[16,2,4,32,256]{4,3,2,1,0:T(8,128)(2,1)}), bf16[16,2,4,32,256]{4,3,2,1,0:T(8,128)(2,1)S(1)}, u32[]{:S(2)}, u32[]{:S(2)}) %all-to-all-start) | async-done | bytes 2097184 | tf_op jit(solution)/shard_map/all_to_all | solution.py:18
  53.8 0.0 copy-start.3
  53.8 1.0 copy-done.3
  54.9 3.1 %column_backward_kernel.1 = (bf16[16,4,32,256]{3,2,1,0:T(8,128)(2,1)S(1)}, bf16[32,64,256]{2,1,0:T(8,128)(2,1)S(1)}) custom-call(bf16[32,64,64]{2,1,0:T(8,128)(2,1)S(1)} %copy-done.3, bf16[4,512,256]{2,1,0:T(8,128)(2,1)S(1)} %collective-permute-done.after_ref.values_ref, bf16[16,2,4,32,256]{4,3,2,1,0:T(8,128)(2,1)S(1)} %all-to-all-done.in_ref), custom_call_target="tpu_custom_call" | custom-call | flops 67108864 | bytes 5505024 | tf_op jit(solution)/shard_map/column_backward_kernel/pallas_call | solution.py:28
  58.0 0.0 copy-start.7
  58.0 1.0 copy-done.7
  59.0 0.0 copy-start.10
  59.0 1.0 copy-done.10
  59.9 11.3 %all-to-all-start.1 = ((bf16[16,4,32,256]{3,2,1,0:T(8,128)(2,1)}), bf16[16,4,32,256]{3,2,1,0:T(8,128)(2,1)}, u32[]{:S(2)}, u32[]{:S(2)}) async-start(bf16[16,4,32,256]{3,2,1,0:T(8,128)(2,1)} %copy-done.10), calls=%async_computation.1 | async-start | bytes 2097152 | tf_op jit(solution)/shard_map/all_to_all | solution.py:18
  71.2 0.0 copy-start.4
  71.2 1.0 copy-done.4
  72.3 0.0 copy-start.8
  72.3 1.2 copy-done.8
  73.5 3.4 %column_forward_kernel.1 = (bf16[16,4,32,256]{3,2,1,0:T(8,128)(2,1)S(1)}, bf16[32,64,64]{2,1,0:T(8,128)(2,1)S(1)}) custom-call(bf16[32,64,64]{2,1,0:T(8,128)(2,1)S(1)} %copy-done.4, bf16[32,64,256]{2,1,0:T(8,128)(2,1)S(1)} %copy-done.8, bf16[16,2,4,32,256]{4,3,2,1,0:T(8,128)(2,1)S(1)} %all-to-all-done.in_ref), custom_call_target="tpu_custom_call" | custom-call | flops 134217728 | bytes 4718592 | tf_op jit(solution)/shard_map/column_forward_kernel/pallas_call | solution.py:28
  76.9 0.0 copy-start.9
  76.9 1.0 copy-done.9
  77.9 1.5 %collective-permute-start.1 = (bf16[32,64,64]{2,1,0:T(8,128)(2,1)S(1)}, bf16[32,64,64]{2,1,0:T(8,128)(2,1)S(1)}, u32[]{:S(2)}, u32[]{:S(2)}) collective-permute-start(bf16[32,64,64]{2,1,0:T(8,128)(2,1)S(1)} %get-tuple-element.24.right_ref), channel_id=1, source_target_pairs={{0,16},{16,0},{1,17},{17,1},{2,18},{18,2},{3,19},{19,3},{4,20},{20... | collective-permute-start | bytes 786440 | tf_op jit(solution)/shard_map/ppermute | solution.py:14
  79.4 0.0 copy-start.11
  79.4 0.8 copy-done.11
  80.2 11.9 %collective-permute-done.1.other_ref = bf16[32,64,64]{2,1,0:T(8,128)(2,1)S(1)} collective-permute-done((bf16[32,64,64]{2,1,0:T(8,128)(2,1)S(1)}, bf16[32,64,64]{2,1,0:T(8,128)(2,1)S(1)}, u32[]{:S(2)}, u32[]{:S(2)}) %collective-permute-start.1) | collective-permute-done | bytes 262176 | tf_op jit(solution)/shard_map/ppermute | solution.py:14
  92.1 0.0 copy-start.13
  92.1 0.8 copy-done.13
  92.9 1.3 %all-to-all-done.1.in_ref = bf16[16,4,32,256]{3,2,1,0:T(8,128)(2,1)} async-done(((bf16[16,4,32,256]{3,2,1,0:T(8,128)(2,1)}), bf16[16,4,32,256]{3,2,1,0:T(8,128)(2,1)}, u32[]{:S(2)}, u32[]{:S(2)}) %all-to-all-start.1) | async-done | bytes 1048608 | tf_op jit(solution)/shard_map/all_to_all | solution.py:18
  94.2 6.9 %all-to-all-start.2 = ((bf16[16,4,32,256]{3,2,1,0:T(8,128)(2,1)}), bf16[16,4,32,256]{3,2,1,0:T(8,128)(2,1)}, u32[]{:S(2)}, u32[]{:S(2)}) async-start(bf16[16,4,32,256]{3,2,1,0:T(8,128)(2,1)} %copy-done.9), calls=%async_computation.2 | async-start | bytes 2097152 | tf_op jit(solution)/shard_map/all_to_all | solution.py:18
  101.1 2.3 %gather_kernel.1 = bf16[4,16,32,256]{3,2,1,0:T(8,128)(2,1)} custom-call(bf16[16,4,32,256]{3,2,1,0:T(8,128)(2,1)} %all-to-all-done.1.in_ref), custom_call_target="tpu_custom_call" | custom-call | bytes 2097152 | tf_op jit(solution)/shard_map/gather_kernel/pallas_call | solution.py:28
  103.4 0.0 copy-start
  103.4 0.0 copy-start.1
  103.4 1.5 %collective-permute-start.2 = (bf16[4,512,256]{2,1,0:T(8,128)(2,1)}, bf16[4,512,256]{2,1,0:T(8,128)(2,1)}, u32[]{:S(2)}, u32[]{:S(2)}) collective-permute-start(bf16[4,512,256]{2,1,0:T(8,128)(2,1)} %bitcast.3.grad_ref), channel_id=1, source_target_pairs={{0,16},{16,0},{1,17},{17,1},{2,18},{18,2},{3,19},{19,3},{4,20},{20... | collective-permute-start | bytes 3145736 | tf_op jit(solution)/shard_map/ppermute | solution.py:14
  104.9 0.0 copy-start.2
  104.9 1.2 copy-done.2
  106.2 4.1 %row_backward_kernel.1 = (bf16[4,512,256]{2,1,0:T(8,128)(2,1)}, bf16[4,512,512]{2,1,0:T(8,128)(2,1)S(1)}) custom-call(bf16[4,512,512]{2,1,0:T(8,128)(2,1)} %left_ref.1, bf16[4,512,256]{2,1,0:T(8,128)(2,1)S(1)} %bitcast.13, bf16[4,512,256]{2,1,0:T(8,128)(2,1)} %bitcast.3.grad_ref), custom_call_target="tpu_custom_call" | custom-call | flops 1073741824 | bytes 7340032 | tf_op jit(solution)/shard_map/row_backward_kernel/pallas_call | solution.py:28
  110.3 0.0 copy-start.5
  110.3 1.3 copy-done.5
  111.6 12.6 %all-to-all-done.2.in_ref = bf16[16,4,32,256]{3,2,1,0:T(8,128)(2,1)} async-done(((bf16[16,4,32,256]{3,2,1,0:T(8,128)(2,1)}), bf16[16,4,32,256]{3,2,1,0:T(8,128)(2,1)}, u32[]{:S(2)}, u32[]{:S(2)}) %all-to-all-start.2) | async-done | bytes 1048608 | tf_op jit(solution)/shard_map/all_to_all | solution.py:18
  124.1 0.0 copy-done
  124.1 0.0 copy-done.1
  124.1 0.0 copy-start.6
  124.2 0.0 copy-start.14
  124.2 3.1 %output_kernel.1 = (bf16[4,16,32,256]{3,2,1,0:T(8,128)(2,1)}, bf16[4,16,32,256]{3,2,1,0:T(8,128)(2,1)}) custom-call(bf16[4,16,32,256]{3,2,1,0:T(8,128)(2,1)S(1)} %bitcast.8, bf16[4,16,32,256]{3,2,1,0:T(8,128)(2,1)S(1)} %bitcast.10, bf16[16,4,32,256]{3,2,1,0:T(8,128)(2,1)} %all-to-all-done.2.in_ref), custom_call_target="tpu_custom_call" | custom-call | bytes 5242880 | tf_op jit(solution)/shard_map/output_kernel/pallas_call | solution.py:28
  127.3 1.9 %collective-permute-done.2.grad_ref = bf16[4,512,256]{2,1,0:T(8,128)(2,1)} collective-permute-done((bf16[4,512,256]{2,1,0:T(8,128)(2,1)}, bf16[4,512,256]{2,1,0:T(8,128)(2,1)}, u32[]{:S(2)}, u32[]{:S(2)}) %collective-permute-start.2) | collective-permute-done | bytes 1048608 | tf_op jit(solution)/shard_map/ppermute | solution.py:14
  129.2 0.0 copy-done.6
  129.2 0.0 copy-done.12
  129.2 0.0 copy-done.14
  129.2 3.5 %factor_sum_kernel.1 = (bf16[4,512,512]{2,1,0:T(8,128)(2,1)}, bf16[32,64,64]{2,1,0:T(8,128)(2,1)}) custom-call(bf16[4,512,512]{2,1,0:T(8,128)(2,1)S(1)} %copy-done.6, bf16[4,512,256]{2,1,0:T(8,128)(2,1)S(1)} %collective-permute-done.after_ref.values_ref, bf16[4,512,256]{2,1,0:T(8,128)(2,1)} %collective-permute-done.2.grad_ref, ...), custom_call_target="tpu_custom_call" | custom-call | flops 536870912 | bytes 7077888 | tf_op jit(solution)/shard_map/factor_sum_kernel/pallas_call | solution.py:28
  (1 shorter events, 0.0 us)
Async XLA Ops:
  5.3 48.5 %all-to-all-start = ((bf16[16,2,4,32,256]{4,3,2,1,0:T(8,128)(2,1)}), bf16[16,2,4,32,256]{4,3,2,1,0:T(8,128)(2,1)S(1)}, u32[]{:S(2)}, u32[]{:S(2)}) async-start(bf16[16,2,4,32,256]{4,3,2,1,0:T(8,128)(2,1)} %send_kernel.1), calls=%async_computation | async-start | bytes 4194304 | tf_op jit(solution)/shard_map/all_to_all | solution.py:18
  12.7 25.7 %collective-permute-start = (bf16[4,512,256]{2,1,0:T(8,128)(2,1)}, bf16[4,512,256]{2,1,0:T(8,128)(2,1)S(1)}, u32[]{:S(2)}, u32[]{:S(2)}) collective-permute-start(bf16[4,512,256]{2,1,0:T(8,128)(2,1)} %bitcast.12), channel_id=1, source_target_pairs={{0,16},{16,0},{1,17},{17,1},{2,18},{18,2},{3,19},{19,3},{4,20},{20... | collective-permute-start | bytes 3145736 | tf_op jit(solution)/shard_map/ppermute | solution.py:14
  53.8 1.0 copy-start.3
  58.0 1.0 copy-start.7
  59.0 1.0 copy-start.10
  59.9 34.3 %all-to-all-start.1 = ((bf16[16,4,32,256]{3,2,1,0:T(8,128)(2,1)}), bf16[16,4,32,256]{3,2,1,0:T(8,128)(2,1)}, u32[]{:S(2)}, u32[]{:S(2)}) async-start(bf16[16,4,32,256]{3,2,1,0:T(8,128)(2,1)} %copy-done.10), calls=%async_computation.1 | async-start | bytes 2097152 | tf_op jit(solution)/shard_map/all_to_all | solution.py:18
  71.2 1.0 copy-start.4
  72.3 1.2 copy-start.8
  76.9 1.0 copy-start.9
  77.9 14.2 %collective-permute-start.1 = (bf16[32,64,64]{2,1,0:T(8,128)(2,1)S(1)}, bf16[32,64,64]{2,1,0:T(8,128)(2,1)S(1)}, u32[]{:S(2)}, u32[]{:S(2)}) collective-permute-start(bf16[32,64,64]{2,1,0:T(8,128)(2,1)S(1)} %get-tuple-element.24.right_ref), channel_id=1, source_target_pairs={{0,16},{16,0},{1,17},{17,1},{2,18},{18,2},{3,19},{19,3},{4,20},{20... | collective-permute-start | bytes 786440 | tf_op jit(solution)/shard_map/ppermute | solution.py:14
  79.4 0.8 copy-start.11
  92.1 0.8 copy-start.13
  94.2 29.9 %all-to-all-start.2 = ((bf16[16,4,32,256]{3,2,1,0:T(8,128)(2,1)}), bf16[16,4,32,256]{3,2,1,0:T(8,128)(2,1)}, u32[]{:S(2)}, u32[]{:S(2)}) async-start(bf16[16,4,32,256]{3,2,1,0:T(8,128)(2,1)} %copy-done.9), calls=%async_computation.2 | async-start | bytes 2097152 | tf_op jit(solution)/shard_map/all_to_all | solution.py:18
  103.4 20.7 %copy-start = (bf16[1,2048,256]{2,1,0:T(8,128)(2,1)S(1)}, bf16[1,2048,256]{2,1,0:T(8,128)(2,1)}, u32[]{:S(2)}) copy-start(bf16[1,2048,256]{2,1,0:T(8,128)(2,1)} %param.6) | copy-start | bytes 3145732
  103.4 20.7 %copy-start.1 = (bf16[1,2048,256]{2,1,0:T(8,128)(2,1)S(1)}, bf16[1,2048,256]{2,1,0:T(8,128)(2,1)}, u32[]{:S(2)}) copy-start(bf16[1,2048,256]{2,1,0:T(8,128)(2,1)} %param.7) | copy-start | bytes 3145732
  103.4 25.7 %collective-permute-start.2 = (bf16[4,512,256]{2,1,0:T(8,128)(2,1)}, bf16[4,512,256]{2,1,0:T(8,128)(2,1)}, u32[]{:S(2)}, u32[]{:S(2)}) collective-permute-start(bf16[4,512,256]{2,1,0:T(8,128)(2,1)} %bitcast.3.grad_ref), channel_id=1, source_target_pairs={{0,16},{16,0},{1,17},{17,1},{2,18},{18,2},{3,19},{19,3},{4,20},{20... | collective-permute-start | bytes 3145736 | tf_op jit(solution)/shard_map/ppermute | solution.py:14
  104.9 1.2 copy-start.2
  110.3 1.3 copy-start.5
  124.1 5.0 %copy-start.6 = (bf16[4,512,512]{2,1,0:T(8,128)(2,1)S(1)}, bf16[4,512,512]{2,1,0:T(8,128)(2,1)}, u32[]{:S(2)}) copy-start(bf16[4,512,512]{2,1,0:T(8,128)(2,1)} %copy-done.5) | copy-start | bytes 6291460
  124.1 5.0 %copy-start.12 = (bf16[32,64,64]{2,1,0:T(8,128)(2,1)S(1)}, bf16[32,64,64]{2,1,0:T(8,128)(2,1)}, u32[]{:S(2)}) copy-start(bf16[32,64,64]{2,1,0:T(8,128)(2,1)} %copy-done.11) | copy-start | bytes 786436
  124.2 5.0 %copy-start.14 = (bf16[32,64,64]{2,1,0:T(8,128)(2,1)S(1)}, bf16[32,64,64]{2,1,0:T(8,128)(2,1)}, u32[]{:S(2)}) copy-start(bf16[32,64,64]{2,1,0:T(8,128)(2,1)} %copy-done.13) | copy-start | bytes 786436

commit v10 on v7

--- a/solution.py
+++ b/solution.py
@@ -20,10 +20,12 @@
     return lax.optimization_barrier((array, earlier))[0]
 
 
-def far_first(count):
-    half = count // 2
-    far = [t for pair in zip(range(half, half + half // 2), range(half + half // 2, count)) for t in pair]
-    return far + list(range(half - 1, 0, -1))
+def orders(chips):
+    half = chips // 2
+    near = list(range(1, half))
+    far = list(range(half, chips, 2)) + list(range(half + 1, chips, 2))
+    in_turns = [t for pair in zip(near, far) for t in pair]
+    return [0] + in_turns + far[half - 1 :], [0] + far[:-1] + near + far[-1:]
 
 
 def permute(array, offset):
@@ -31,12 +33,15 @@
     return lax.ppermute(array, "seq", [(i, i ^ offset) for i in range(seq)])
 
 
-def exchange(messages):
-    return [messages[0]] + [permute(message, 2 * t) for t, message in list(enumerate(messages))[1:]]
-
-
-def listed(messages):
-    return [messages[t] for t in [0] + far_first(len(messages))]
+def exchange(messages, sent=0, received=None):
+    result = [permute(message, 2 * t) if t else message for t, message in enumerate(messages)]
+    if received is not None:
+        result[sent] = received
+    return result
+
+
+def listed(messages, order):
+    return [messages[t] for t in order]
 
 
 def call(kernel, me, inputs, out_shapes, scratch=(), flops=0, unblocked=(), vmem=32):
@@ -65,8 +70,7 @@
     return [(me ^ (2 * t + e), ref.at[t]) for e, ref in enumerate(refs) for t in range(ref.shape[0])]
 
 
-def received_views(me, refs):
-    order = [0] + far_first(len(refs))
+def received_views(me, refs, order):
     return [(me ^ (2 * t + e), ref.at[e]) for t, ref in zip(order, refs) for e in range(2)]
 
 
@@ -132,12 +136,13 @@
         ref[...] = block.reshape(rows, cols, channels)
 
 
-def column_backward_kernel(chips, me_ref, right_ref, *refs):
+def column_backward_kernel(order, me_ref, right_ref, *refs):
+    chips = len(order)
     in_refs, out_refs = refs[:chips], refs[chips : chips + 2]
     by_column_ref, wide, wide_out = refs[chips + 2 :]
     cols, count, _ = right_ref.shape
     me = me_ref[0]
-    load_columns([(c, ref.at[0]) for c, ref in received_views(me, in_refs)], wide)
+    load_columns([(c, ref.at[0]) for c, ref in received_views(me, in_refs, order)], wide)
     for k in range(cols):
         grad = column(wide, k, count, cols)
         by_column_ref[k] = grad
@@ -145,12 +150,13 @@
     send_columns(wide_out, block_views(me, out_refs))
 
 
-def column_forward_kernel(chips, me_ref, right_ref, grad_ref, after_ref, *refs):
+def column_forward_kernel(order, me_ref, right_ref, grad_ref, after_ref, *refs):
+    chips = len(order)
     in_refs, out_refs = refs[:chips], refs[chips : chips + 2]
     right_part_ref, wide, wide_out = refs[chips + 2 :]
     cols, count, _ = right_ref.shape
     me = me_ref[0]
-    load_columns([(c, ref.at[1]) for c, ref in received_views(me, in_refs)], wide)
+    load_columns([(c, ref.at[1]) for c, ref in received_views(me, in_refs, order)], wide)
     for k in range(cols):
         mixed = column(wide, k, count, cols)
         store_column(wide_out, k, count, cols, dot(right_ref[k], mixed, ((1,), (0,))))
@@ -158,30 +164,60 @@
     send_columns(wide_out, block_views(me, out_refs))
 
 
-def gather_kernel(chips, me_ref, *refs):
-    for c, ref in received_views(me_ref[0], refs[:chips]):
-        refs[chips][:, c] = ref[...]
-
-
-def row_backward_kernel(me_ref, left_ref, values_ref, grad_ref, signal_ref, term_ref):
+def gather_kernel(me_ref, *refs):
+    out_ref = refs[-1]
+    for t, ref in enumerate(refs[:-1]):
+        for e in range(2):
+            out_ref[2 * t + e] = ref[e]
+
+
+def load_rows(order, me, parts, hold):
+    half = parts[0].shape[0]
+    for n, t in enumerate(order):
+        for e in range(2):
+            j = 2 * n + e
+            hold[:, me ^ (2 * t + e)] = parts[j // half][j % half]
+
+
+def row_of(hold, i):
+    seq, cols, channels = hold.shape[1:]
+    return hold[i].reshape(seq * cols, channels)
+
+
+def row_backward_kernel(
+    order, me_ref, left_ref, values_ref, first_ref, second_ref, signal_ref, term_ref, hold
+):
+    load_rows(order, me_ref[0], (first_ref, second_ref), hold)
     for i in range(left_ref.shape[0]):
-        grad = grad_ref[i]
+        grad = row_of(hold, i)
         signal_ref[i] = dot(left_ref[i], grad, ((0,), (0,))).astype(BF16)
         term_ref[i] = dot(grad, values_ref[i], ((1,), (1,))).astype(BF16)
 
 
 def factor_sum_kernel(
-    me_ref, term_ref, values_ref, grad_ref, right_ref, other_ref, left_out_ref, right_out_ref
+    order,
+    me_ref,
+    term_ref,
+    values_ref,
+    first_ref,
+    second_ref,
+    right_ref,
+    other_ref,
+    left_out_ref,
+    right_out_ref,
+    hold,
 ):
+    right_out_ref[...] = (right_ref[...].astype(F32) + other_ref[...].astype(F32)).astype(BF16)
+    load_rows(order, me_ref[0], (first_ref, second_ref), hold)
     for i in range(term_ref.shape[0]):
-        other = dot(grad_ref[i], values_ref[i], ((1,), (1,))).astype(BF16)
+        other = dot(row_of(hold, i), values_ref[i], ((1,), (1,))).astype(BF16)
         left_out_ref[i] = (term_ref[i].astype(F32) + other.astype(F32)).astype(BF16)
-    right_out_ref[...] = (right_ref[...].astype(F32) + other_ref[...].astype(F32)).astype(BF16)
-
-
-def output_kernel(chips, me_ref, gate_ref, cotangent_ref, *refs):
+
+
+def output_kernel(order, me_ref, gate_ref, cotangent_ref, *refs):
+    chips = len(order)
     out_ref, grad_ref = refs[chips:]
-    for c, ref in received_views(me_ref[0], refs[:chips]):
+    for c, ref in received_views(me_ref[0], refs[:chips], order):
         second = ref[...].astype(F32)
         out_ref[:, c] = (gate_ref[:, c].astype(F32) * second).astype(BF16)
         grad_ref[:, c] = (cotangent_ref[:, c].astype(F32) * second).astype(BF16)
@@ -201,8 +237,10 @@
     def shape(*dims):
         return jax.ShapeDtypeStruct(dims, BF16)
 
-    def on_chips(kernel):
-        return functools.partial(kernel, chips)
+    in_turns, far_first = orders(chips)
+
+    def ordered(kernel, order=in_turns):
+        return functools.partial(kernel, order)
 
     block = (rows, cols, channels)
     whole = shape(rows, seq, cols, channels)
@@ -213,9 +251,10 @@
     row_flops = 2 * rows * block_len * block_len * channels
     column_flops = 2 * cols * count * count * channels
 
-    def pack(own, other):
+    def pack(own, other, earlier=()):
         message = shape(2, *own.shape[1:])
-        return list(call(pack_kernel, me, [own, permute(other, 1)], [message] * chips))
+        swapped = permute(after(other, earlier), 1)
+        return list(call(pack_kernel, me, [own, swapped], [message] * chips))
 
     own, other = call(
         send_kernel,
@@ -230,18 +269,18 @@
     )
     messages = pack(own, other)
     other_values = swap_sequences(after(values, messages[0]))
-    columns = listed(exchange(messages))
+    columns = listed(exchange(messages), in_turns)
     own, other, grad_column = call(
-        on_chips(column_backward_kernel),
+        ordered(column_backward_kernel),
         me,
         [right_factor, *columns],
         [shape(chips, *block)] * 2 + [shape(cols, count, channels)],
         [wide, wide],
         column_flops,
     )
-    messages = pack(own, other)
+    back = pack(own, other)
     own, other, right_part = call(
-        on_chips(column_forward_kernel),
+        ordered(column_forward_kernel),
         me,
         [right_factor, grad_column, other_values, *columns],
         [shape(chips, *block)] * 2 + [right],
@@ -249,34 +288,40 @@
         2 * column_flops,
         unblocked=[2],
     )
-    second_messages = pack(own, other)
-    for t in range(1, chips // 2):
-        messages[t] = after(messages[t], second_messages[0])
-    back = listed(exchange(messages))
+    first = far_first[1]
+    first_back = permute(back[first], 2 * first)
+    second = pack(own, other, first_back)
+    back[far_first[-1]] = after(back[far_first[-1]], second[0])
     other_right = swap_sequences(right_part)
-    back[0] = after(back[0], other_right)
-    (gathered,) = call(on_chips(gather_kernel), me, back, [whole])
-    grad_back = gathered.reshape(rows, block_len, channels)
-    other_grad_back = swap_sequences(grad_back)
+    back = listed(exchange(back, first, first_back), far_first)
+    first_second = permute(second[first], 2 * first)
+    back[-1] = after(back[-1], (first_second, other_right))
+    half_rows = shape(seq // 2, *block)
+    hold = pltpu.VMEM(whole.shape, BF16)
+    (first_half,) = call(gather_kernel, me, back[: chips // 2], [half_rows])
+    (second_half,) = call(gather_kernel, me, back[chips // 2 :], [half_rows])
+    other_first = swap_sequences(first_half)
+    other_second = swap_sequences(second_half)
     grad_signal, left_term = call(
-        row_backward_kernel,
+        ordered(row_backward_kernel, far_first),
         me,
-        [left_factor, values, grad_back],
+        [left_factor, values, first_half, second_half],
         [by_row, left],
-        flops=2 * row_flops,
-    )
-    for t in range(1, chips // 2):
-        second_messages[t] = after(second_messages[t], left_term)
-    second = listed(exchange(second_messages))
+        [hold],
+        2 * row_flops,
+    )
+    second[far_first[-1]] = after(second[far_first[-1]], left_term)
+    second = listed(exchange(second, first, first_second), far_first)
     grad_left, grad_right = call(
-        factor_sum_kernel,
+        ordered(factor_sum_kernel, far_first),
         me,
-        [left_term, other_values, other_grad_back, right_part, other_right],
+        [left_term, other_values, other_first, other_second, right_part, other_right],
         [left, right],
-        flops=row_flops,
+        [hold],
+        row_flops,
     )
     output, grad_gate = call(
-        on_chips(output_kernel), me, [gate, cotangent, *second], [whole, whole]
+        ordered(output_kernel, far_first), me, [gate, cotangent, *second], [whole, whole]
     )
     return (
         output.reshape(signal.shape),

time: 136 us -> 133 us (0.978)
  starting transfers between devices: 43.5 us -> 38.7 us
    ppermute x24, starting transfers between devices: 38.4 us -> 34.5 us  [permute(): return lax.ppermute(array, 'seq', [(i, i ^ offset) for i in range(seq)])]
    ppermute x3 -> x4, starting transfers between devices: 5.05 us -> 4.18 us  [swap_sequences(): return lax.ppermute(array, 'dp', [(0, 1), (1, 0)])]
    pallas_call x10 -> x11, Pallas kernels: 17.2 us -> 17.2 us  [call(): pl.pallas_call(kernel, out_shape=out_shapes, in_specs=[pl.BlockSpec(memor...]
  transfers between devices with their start and end apart: 27 -> 28, of which waited for: 16 -> 18; matrix products, arithmetic and copies ran while one was open for 0% -> 0% of each run, Pallas kernels for 8% -> 8%
where the time goes in v10:
time: 133 us; the launch traced here: 132 us
  waiting for transfers between devices  74.6 us (56%)
  starting transfers between devices  38.7 us (29%)
  Pallas kernels  17.2 us (13%)
    ppermute x24, waiting for transfers between devices, permute(): return lax.ppermute(array, 'seq', [(i, i ^ offset) for i in range(seq)])  74.6 us
    ppermute x24, starting transfers between devices, permute(): return lax.ppermute(array, 'seq', [(i, i ^ offset) for i in range(seq)])  34.5 us
    pallas_call x11, Pallas kernels, call(): pl.pallas_call(kernel, out_shape=out_shapes, in_specs=[pl.BlockSpec(memor...  17.2 us
    ppermute x4, starting transfers between devices, swap_sequences(): return lax.ppermute(array, 'dp', [(0, 1), (1, 0)])  4.18 us
  transfers between devices with their start and end apart: 28, of which 18 were waited for; matrix products, arithmetic and copies ran while one was open for 0% of the time, Pallas kernels for 8%

profile of v10, /device:TPU:0, one launch (start us, length us, event | category | flops | bytes accessed | tf_op | source)
XLA Modules:
  0.0 132.5 jit_solution(13484764870766231240)
XLA Ops:
  0.6 4.4 %send_kernel.1 = (bf16[8,2,4,32,256]{4,3,2,1,0:T(8,128)(2,1)}, bf16[8,2,4,32,256]{4,3,2,1,0:T(8,128)(2,1)}) custom-call(s32[1]{0:T(128)} %bitcast.me_ref, bf16[4,16,32,256]{3,2,1,0:T(8,128)(2,1)} %bitcast.10, bf16[4,16,32,256]{3,2,1,0:T(8,128)(2,1)} %bitcast.12, bf16[4,512,512]{2,1,0:T(8,128)(2,1)} %left_ref.1, bf16[4,512,256]{2,1,0:T(8,128)(2,1)} %bitcast.7), custom_call_target="tpu_custom_call" | custom-call | flops 536870912 | bytes 7340032 | tf_op jit(solution)/shard_map/send_kernel/pallas_call | solution.py:53
  5.1 0.5 collective-permute-start
  5.6 2.5 %collective-permute-done.other_ref = bf16[8,2,4,32,256]{4,3,2,1,0:T(8,128)(2,1)S(1)} collective-permute-done((bf16[8,2,4,32,256]{4,3,2,1,0:T(8,128)(2,1)}, bf16[8,2,4,32,256]{4,3,2,1,0:T(8,128)(2,1)S(1)}, u32[]{:S(2)}, u32[]{:S(2)}) %collective-permute-start) | collective-permute-done | bytes 1048608 | tf_op jit(solution)/shard_map/ppermute | solution.py:33
  8.1 1.2 copy-done.5
  9.3 0.1 pack_kernel.3
  9.4 3.0 %collective-permute-start.1 = (bf16[2,2,4,32,256]{4,3,2,1,0:T(8,128)(2,1)S(1)}, bf16[2,2,4,32,256]{4,3,2,1,0:T(8,128)(2,1)S(1)}, u32[]{:S(2)}, u32[]{:S(2)}) collective-permute-start(bf16[2,2,4,32,256]{4,3,2,1,0:T(8,128)(2,1)S(1)} %get-tuple-element.51), channel_id=1, source_target_pairs={{0,2},{1,3},{2,0},{3,1},{4,6},{5,7},{6,4},{7,5},{8,10},{9,11},{10,... | collective-permute-start | bytes 786440 | tf_op jit(solution)/shard_map/ppermute | solution.py:33
  12.4 2.6 %collective-permute-start.2 = (bf16[2,2,4,32,256]{4,3,2,1,0:T(8,128)(2,1)S(1)}, bf16[2,2,4,32,256]{4,3,2,1,0:T(8,128)(2,1)S(1)}, u32[]{:S(2)}, u32[]{:S(2)}) collective-permute-start(bf16[2,2,4,32,256]{4,3,2,1,0:T(8,128)(2,1)S(1)} %get-tuple-element.52), channel_id=1, source_target_pairs={{0,8},{1,9},{2,10},{3,11},{4,12},{5,13},{6,14},{7,15},{8,0},{9,1},... | collective-permute-start | bytes 786440 | tf_op jit(solution)/shard_map/ppermute | solution.py:33
  15.0 1.6 %collective-permute-start.3 = (bf16[2,2,4,32,256]{4,3,2,1,0:T(8,128)(2,1)S(1)}, bf16[2,2,4,32,256]{4,3,2,1,0:T(8,128)(2,1)S(1)}, u32[]{:S(2)}, u32[]{:S(2)}) collective-permute-start(bf16[2,2,4,32,256]{4,3,2,1,0:T(8,128)(2,1)S(1)} %get-tuple-element.53), channel_id=1, source_target_pairs={{0,4},{1,5},{2,6},{3,7},{4,0},{5,1},{6,2},{7,3},{8,12},{9,13},{10,... | collective-permute-start | bytes 786440 | tf_op jit(solution)/shard_map/ppermute | solution.py:33
  16.6 1.5 %collective-permute-start.8 = (bf16[4,512,256]{2,1,0:T(8,128)(2,1)S(1)}, bf16[4,512,256]{2,1,0:T(8,128)(2,1)S(1)}, u32[]{:S(2)}, u32[]{:S(2)}) collective-permute-start(bf16[4,512,256]{2,1,0:T(8,128)(2,1)S(1)} %bitcast.8), channel_id=1, source_target_pairs={{0,16},{16,0},{1,17},{17,1},{2,18},{18,2},{3,19},{19,3},{4,20},{20... | collective-permute-start | bytes 3145736 | tf_op jit(solution)/shard_map/ppermute | solution.py:16
  18.1 0.2 collective-permute-start.4
  18.3 0.7 collective-permute-done.1.refs_1_
  19.0 2.8 %collective-permute-start.5 = (bf16[2,2,4,32,256]{4,3,2,1,0:T(8,128)(2,1)S(1)}, bf16[2,2,4,32,256]{4,3,2,1,0:T(8,128)(2,1)S(1)}, u32[]{:S(2)}, u32[]{:S(2)}) collective-permute-start(bf16[2,2,4,32,256]{4,3,2,1,0:T(8,128)(2,1)S(1)} %get-tuple-element.55), channel_id=1, source_target_pairs={{0,6},{1,7},{2,4},{3,5},{4,2},{5,3},{6,0},{7,1},{8,14},{9,15},{10,... | collective-permute-start | bytes 786440 | tf_op jit(solution)/shard_map/ppermute | solution.py:33
  21.8 7.5 %collective-permute-done.2.refs_2_ = bf16[2,2,4,32,256]{4,3,2,1,0:T(8,128)(2,1)S(1)} collective-permute-done((bf16[2,2,4,32,256]{4,3,2,1,0:T(8,128)(2,1)S(1)}, bf16[2,2,4,32,256]{4,3,2,1,0:T(8,128)(2,1)S(1)}, u32[]{:S(2)}, u32[]{:S(2)}) %collective-permute-start.2) | collective-permute-done | bytes 262176 | tf_op jit(solution)/shard_map/ppermute | solution.py:33
  29.2 3.7 %collective-permute-done.3.refs_3_ = bf16[2,2,4,32,256]{4,3,2,1,0:T(8,128)(2,1)S(1)} collective-permute-done((bf16[2,2,4,32,256]{4,3,2,1,0:T(8,128)(2,1)S(1)}, bf16[2,2,4,32,256]{4,3,2,1,0:T(8,128)(2,1)S(1)}, u32[]{:S(2)}, u32[]{:S(2)}) %collective-permute-start.3) | collective-permute-done | bytes 262176 | tf_op jit(solution)/shard_map/ppermute | solution.py:33
  32.9 1.9 %collective-permute-done.4.refs_4_ = bf16[2,2,4,32,256]{4,3,2,1,0:T(8,128)(2,1)S(1)} collective-permute-done((bf16[2,2,4,32,256]{4,3,2,1,0:T(8,128)(2,1)S(1)}, bf16[2,2,4,32,256]{4,3,2,1,0:T(8,128)(2,1)S(1)}, u32[]{:S(2)}, u32[]{:S(2)}) %collective-permute-start.4) | collective-permute-done | bytes 262176 | tf_op jit(solution)/shard_map/ppermute | solution.py:33
  34.8 4.3 %collective-permute-done.5.refs_5_ = bf16[2,2,4,32,256]{4,3,2,1,0:T(8,128)(2,1)S(1)} collective-permute-done((bf16[2,2,4,32,256]{4,3,2,1,0:T(8,128)(2,1)S(1)}, bf16[2,2,4,32,256]{4,3,2,1,0:T(8,128)(2,1)S(1)}, u32[]{:S(2)}, u32[]{:S(2)}) %collective-permute-start.5) | collective-permute-done | bytes 262176 | tf_op jit(solution)/shard_map/ppermute | solution.py:33
  39.0 16.8 %collective-permute-done.6.refs_6_ = bf16[2,2,4,32,256]{4,3,2,1,0:T(8,128)(2,1)S(1)} collective-permute-done((bf16[2,2,4,32,256]{4,3,2,1,0:T(8,128)(2,1)S(1)}, bf16[2,2,4,32,256]{4,3,2,1,0:T(8,128)(2,1)S(1)}, u32[]{:S(2)}, u32[]{:S(2)}) %collective-permute-start.6) | collective-permute-done | bytes 262176 | tf_op jit(solution)/shard_map/ppermute | solution.py:33
  55.8 3.0 %column_backward_kernel.1 = (bf16[8,4,32,256]{3,2,1,0:T(8,128)(2,1)S(1)}, bf16[8,4,32,256]{3,2,1,0:T(8,128)(2,1)S(1)}, bf16[32,64,256]{2,1,0:T(8,128)(2,1)S(1)}) custom-call(s32[1]{0:T(128)} %bitcast.me_ref, bf16[32,64,64]{2,1,0:T(8,128)(2,1)S(1)} %copy-done.4, bf16[2,2,4,32,256]{4,3,2,1,0:T(8,128)(2,1)S(1)} %get-tuple-element.50.refs_0_, ...), custom_call_target="tpu_custom_call" | custom-call | flops 67108864 | bytes 4456448 | tf_op jit(solution)/shard_map/column_backward_kernel/pallas_call | solution.py:53
  58.8 0.1 collective-permute-start.9
  58.9 1.9 %collective-permute-done.9.other_ref = bf16[8,4,32,256]{3,2,1,0:T(8,128)(2,1)S(1)} collective-permute-done((bf16[8,4,32,256]{3,2,1,0:T(8,128)(2,1)S(1)}, bf16[8,4,32,256]{3,2,1,0:T(8,128)(2,1)S(1)}, u32[]{:S(2)}, u32[]{:S(2)}) %collective-permute-start.9) | collective-permute-done | bytes 524320 | tf_op jit(solution)/shard_map/ppermute | solution.py:33
  60.8 0.1 pack_kernel.4
  60.8 7.5 %collective-permute-start.10 = (bf16[2,4,32,256]{3,2,1,0:T(8,128)(2,1)S(1)}, bf16[2,4,32,256]{3,2,1,0:T(8,128)(2,1)S(1)}, u32[]{:S(2)}, u32[]{:S(2)}) collective-permute-start(bf16[2,4,32,256]{3,2,1,0:T(8,128)(2,1)S(1)} %get-tuple-element.64), channel_id=1, source_target_pairs={{0,8},{1,9},{2,10},{3,11},{4,12},{5,13},{6,14},{7,15},{8,0},{9,1},... | collective-permute-start | bytes 393224 | tf_op jit(solution)/shard_map/ppermute | solution.py:33
  68.3 3.1 %column_forward_kernel.1 = (bf16[8,4,32,256]{3,2,1,0:T(8,128)(2,1)S(1)}, bf16[8,4,32,256]{3,2,1,0:T(8,128)(2,1)S(1)}, bf16[32,64,64]{2,1,0:T(8,128)(2,1)S(1)}) custom-call(s32[1]{0:T(128)} %bitcast.me_ref, bf16[32,64,64]{2,1,0:T(8,128)(2,1)S(1)} %copy-done.4, bf16[32,64,256]{2,1,0:T(8,128)(2,1)S(1)} %get-tuple-element.58.grad_ref, ...), custom_call_target="tpu_custom_call" | custom-call | flops 134217728 | bytes 5767168 | tf_op jit(solution)/shard_map/column_forward_kernel/pallas_call | solution.py:53
  71.5 3.5 %collective-permute-done.10.refs_1_ = bf16[2,4,32,256]{3,2,1,0:T(8,128)(2,1)S(1)} collective-permute-done((bf16[2,4,32,256]{3,2,1,0:T(8,128)(2,1)S(1)}, bf16[2,4,32,256]{3,2,1,0:T(8,128)(2,1)S(1)}, u32[]{:S(2)}, u32[]{:S(2)}) %collective-permute-start.10) | collective-permute-done | bytes 131104 | tf_op jit(solution)/shard_map/ppermute | solution.py:33
  74.9 1.5 %collective-permute-start.24 = (bf16[32,64,64]{2,1,0:T(8,128)(2,1)S(1)}, bf16[32,64,64]{2,1,0:T(8,128)(2,1)S(1)}, u32[]{:S(2)}, u32[]{:S(2)}) collective-permute-start(bf16[32,64,64]{2,1,0:T(8,128)(2,1)S(1)} %get-tuple-element.82.right_ref), channel_id=1, source_target_pairs={{0,16},{16,0},{1,17},{17,1},{2,18},{18,2},{3,19},{19,3},{4,20},{20... | collective-permute-start | bytes 786440 | tf_op jit(solution)/shard_map/ppermute | solution.py:16
  76.4 0.8 collective-permute-start.19
  77.2 0.7 collective-permute-start.20
  78.0 0.1 pack_kernel.5
  78.0 3.8 %collective-permute-start.23 = (bf16[2,4,32,256]{3,2,1,0:T(8,128)(2,1)S(1)}, bf16[2,4,32,256]{3,2,1,0:T(8,128)(2,1)S(1)}, u32[]{:S(2)}, u32[]{:S(2)}) collective-permute-start(bf16[2,4,32,256]{3,2,1,0:T(8,128)(2,1)S(1)} %get-tuple-element.81), channel_id=1, source_target_pairs={{0,14},{1,15},{2,12},{3,13},{4,10},{5,11},{6,8},{7,9},{8,6},{9,7},... | collective-permute-start | bytes 393224 | tf_op jit(solution)/shard_map/ppermute | solution.py:33
  81.9 2.8 %collective-permute-done.18.refs_2_ = bf16[2,4,32,256]{3,2,1,0:T(8,128)(2,1)S(1)} collective-permute-done((bf16[2,4,32,256]{3,2,1,0:T(8,128)(2,1)S(1)}, bf16[2,4,32,256]{3,2,1,0:T(8,128)(2,1)S(1)}, u32[]{:S(2)}, u32[]{:S(2)}) %collective-permute-start.18) | collective-permute-done | bytes 131104 | tf_op jit(solution)/shard_map/ppermute | solution.py:33
  84.7 6.4 %collective-permute-start.12 = (bf16[2,4,32,256]{3,2,1,0:T(8,128)(2,1)S(1)}, bf16[2,4,32,256]{3,2,1,0:T(8,128)(2,1)S(1)}, u32[]{:S(2)}, u32[]{:S(2)}) collective-permute-start(bf16[2,4,32,256]{3,2,1,0:T(8,128)(2,1)S(1)} %get-tuple-element.67), channel_id=1, source_target_pairs={{0,8},{1,9},{2,10},{3,11},{4,12},{5,13},{6,14},{7,15},{8,0},{9,1},... | collective-permute-start | bytes 393224 | tf_op jit(solution)/shard_map/ppermute | solution.py:33
  91.0 4.8 %collective-permute-done.19.refs_3_ = bf16[2,4,32,256]{3,2,1,0:T(8,128)(2,1)S(1)} collective-permute-done((bf16[2,4,32,256]{3,2,1,0:T(8,128)(2,1)S(1)}, bf16[2,4,32,256]{3,2,1,0:T(8,128)(2,1)S(1)}, u32[]{:S(2)}, u32[]{:S(2)}) %collective-permute-start.19) | collective-permute-done | bytes 131104 | tf_op jit(solution)/shard_map/ppermute | solution.py:33
  95.8 2.3 %collective-permute-start.22 = (bf16[2,4,32,256]{3,2,1,0:T(8,128)(2,1)S(1)}, bf16[2,4,32,256]{3,2,1,0:T(8,128)(2,1)S(1)}, u32[]{:S(2)}, u32[]{:S(2)}) collective-permute-start(bf16[2,4,32,256]{3,2,1,0:T(8,128)(2,1)S(1)} %get-tuple-element.79), channel_id=1, source_target_pairs={{0,6},{1,7},{2,4},{3,5},{4,2},{5,3},{6,0},{7,1},{8,14},{9,15},{10,... | collective-permute-start | bytes 393224 | tf_op jit(solution)/shard_map/ppermute | solution.py:33
  98.1 0.6 collective-permute-start.26
  98.7 2.1 %collective-permute-done.12.refs_1_ = bf16[2,4,32,256]{3,2,1,0:T(8,128)(2,1)S(1)} collective-permute-done((bf16[2,4,32,256]{3,2,1,0:T(8,128)(2,1)S(1)}, bf16[2,4,32,256]{3,2,1,0:T(8,128)(2,1)S(1)}, u32[]{:S(2)}, u32[]{:S(2)}) %collective-permute-start.12) | collective-permute-done | bytes 131104 | tf_op jit(solution)/shard_map/ppermute | solution.py:33
  100.8 2.7 %collective-permute-done.21.refs_1_ = bf16[2,4,32,256]{3,2,1,0:T(8,128)(2,1)S(1)} collective-permute-done((bf16[2,4,32,256]{3,2,1,0:T(8,128)(2,1)S(1)}, bf16[2,4,32,256]{3,2,1,0:T(8,128)(2,1)S(1)}, u32[]{:S(2)}, u32[]{:S(2)}) %collective-permute-start.21) | collective-permute-done | bytes 131104 | tf_op jit(solution)/shard_map/ppermute | solution.py:33
  103.5 2.9 %collective-permute-done.22.refs_2_ = bf16[2,4,32,256]{3,2,1,0:T(8,128)(2,1)S(1)} collective-permute-done((bf16[2,4,32,256]{3,2,1,0:T(8,128)(2,1)S(1)}, bf16[2,4,32,256]{3,2,1,0:T(8,128)(2,1)S(1)}, u32[]{:S(2)}, u32[]{:S(2)}) %collective-permute-start.22) | collective-permute-done | bytes 131104 | tf_op jit(solution)/shard_map/ppermute | solution.py:33
  106.4 0.6 collective-permute-start.27
  107.0 1.0 collective-permute-start.14
  108.0 0.1 collective-permute-start.15
  108.1 2.3 %row_backward_kernel.1 = (bf16[4,512,256]{2,1,0:T(8,128)(2,1)}, bf16[4,512,512]{2,1,0:T(8,128)(2,1)S(1)}) custom-call(s32[1]{0:T(128)} %bitcast.me_ref, bf16[4,512,512]{2,1,0:T(8,128)(2,1)S(1)} %copy-done, bf16[4,512,256]{2,1,0:T(8,128)(2,1)S(1)} %bitcast.9, bf16[8,4,32,256]{3,2,1,0:T(8,128)(2,1)S(1)} %gather_kernel.2.first_ref, ...), custom_call_target="tpu_custom_call" | custom-call | flops 1073741824 | bytes 7340032 | tf_op jit(solution)/shard_map/row_backward_kernel/pallas_call | solution.py:53
  110.4 4.9 %collective-permute-done.13.refs_2_ = bf16[2,4,32,256]{3,2,1,0:T(8,128)(2,1)S(1)} collective-permute-done((bf16[2,4,32,256]{3,2,1,0:T(8,128)(2,1)S(1)}, bf16[2,4,32,256]{3,2,1,0:T(8,128)(2,1)S(1)}, u32[]{:S(2)}, u32[]{:S(2)}) %collective-permute-start.13) | collective-permute-done | bytes 131104 | tf_op jit(solution)/shard_map/ppermute | solution.py:33
  115.3 4.4 %collective-permute-done.14.refs_3_ = bf16[2,4,32,256]{3,2,1,0:T(8,128)(2,1)S(1)} collective-permute-done((bf16[2,4,32,256]{3,2,1,0:T(8,128)(2,1)S(1)}, bf16[2,4,32,256]{3,2,1,0:T(8,128)(2,1)S(1)}, u32[]{:S(2)}, u32[]{:S(2)}) %collective-permute-start.14) | collective-permute-done | bytes 131104 | tf_op jit(solution)/shard_map/ppermute | solution.py:33
  119.7 1.2 collective-permute-start.25
  120.9 0.7 collective-permute-done.16.refs_5_
  121.5 6.8 %collective-permute-done.17.refs_6_ = bf16[2,4,32,256]{3,2,1,0:T(8,128)(2,1)S(1)} collective-permute-done((bf16[2,4,32,256]{3,2,1,0:T(8,128)(2,1)S(1)}, bf16[2,4,32,256]{3,2,1,0:T(8,128)(2,1)S(1)}, u32[]{:S(2)}, u32[]{:S(2)}) %collective-permute-start.17) | collective-permute-done | bytes 131104 | tf_op jit(solution)/shard_map/ppermute | solution.py:33
  128.4 1.8 %output_kernel.1 = (bf16[4,16,32,256]{3,2,1,0:T(8,128)(2,1)}, bf16[4,16,32,256]{3,2,1,0:T(8,128)(2,1)}) custom-call(s32[1]{0:T(128)} %bitcast.me_ref, bf16[4,16,32,256]{3,2,1,0:T(8,128)(2,1)S(1)} %bitcast.11, bf16[4,16,32,256]{3,2,1,0:T(8,128)(2,1)S(1)} %bitcast.13, bf16[2,4,32,256]{3,2,1,0:T(8,128)(2,1)S(1)} %get-tuple-element.66.refs_0_, ...), custom_call_target="tpu_custom_call" | custom-call | bytes 5242880 | tf_op jit(solution)/shard_map/output_kernel/pallas_call | solution.py:53
  130.2 2.3 %factor_sum_kernel.1 = (bf16[4,512,512]{2,1,0:T(8,128)(2,1)}, bf16[32,64,64]{2,1,0:T(8,128)(2,1)}) custom-call(s32[1]{0:T(128)} %bitcast.me_ref, bf16[4,512,512]{2,1,0:T(8,128)(2,1)S(1)} %get-tuple-element.84.term_ref, bf16[4,512,256]{2,1,0:T(8,128)(2,1)S(1)} %collective-permute-done.8.after_ref.values_ref, ...), custom_call_target="tpu_custom_call" | custom-call | flops 536870912 | bytes 7077888 | tf_op jit(solution)/shard_map/factor_sum_kernel/pallas_call | solution.py:53
  (31 shorter events, 0.1 us)
Async XLA Ops:
  5.0 11.5 %copy-start.1 = (bf16[1,2048,256]{2,1,0:T(8,128)(2,1)S(1)}, bf16[1,2048,256]{2,1,0:T(8,128)(2,1)}, u32[]{:S(2)}) copy-start(bf16[1,2048,256]{2,1,0:T(8,128)(2,1)} %param.5) | copy-start | bytes 3145732
  5.1 50.8 %copy-start.4 = (bf16[32,64,64]{2,1,0:T(8,128)(2,1)S(1)}, bf16[32,64,64]{2,1,0:T(8,128)(2,1)}, u32[]{:S(2)}) copy-start(bf16[32,64,64]{2,1,0:T(8,128)(2,1)} %right_ref.3) | copy-start | bytes 786436
  5.1 3.0 %collective-permute-start = (bf16[8,2,4,32,256]{4,3,2,1,0:T(8,128)(2,1)}, bf16[8,2,4,32,256]{4,3,2,1,0:T(8,128)(2,1)S(1)}, u32[]{:S(2)}, u32[]{:S(2)}) collective-permute-start(bf16[8,2,4,32,256]{4,3,2,1,0:T(8,128)(2,1)} %get-tuple-element.49), channel_id=1, source_target_pairs={{0,1},{1,0},{2,3},{3,2},{4,5},{5,4},{6,7},{7,6},{8,9},{9,8},{10,11... | collective-permute-start | bytes 3145736 | tf_op jit(solution)/shard_map/ppermute | solution.py:33
  8.1 1.2 copy-start.5
  9.4 9.6 %collective-permute-start.1 = (bf16[2,2,4,32,256]{4,3,2,1,0:T(8,128)(2,1)S(1)}, bf16[2,2,4,32,256]{4,3,2,1,0:T(8,128)(2,1)S(1)}, u32[]{:S(2)}, u32[]{:S(2)}) collective-permute-start(bf16[2,2,4,32,256]{4,3,2,1,0:T(8,128)(2,1)S(1)} %get-tuple-element.51), channel_id=1, source_target_pairs={{0,2},{1,3},{2,0},{3,1},{4,6},{5,7},{6,4},{7,5},{8,10},{9,11},{10,... | collective-permute-start | bytes 786440 | tf_op jit(solution)/shard_map/ppermute | solution.py:33
  12.4 16.8 %collective-permute-start.2 = (bf16[2,2,4,32,256]{4,3,2,1,0:T(8,128)(2,1)S(1)}, bf16[2,2,4,32,256]{4,3,2,1,0:T(8,128)(2,1)S(1)}, u32[]{:S(2)}, u32[]{:S(2)}) collective-permute-start(bf16[2,2,4,32,256]{4,3,2,1,0:T(8,128)(2,1)S(1)} %get-tuple-element.52), channel_id=1, source_target_pairs={{0,8},{1,9},{2,10},{3,11},{4,12},{5,13},{6,14},{7,15},{8,0},{9,1},... | collective-permute-start | bytes 786440 | tf_op jit(solution)/shard_map/ppermute | solution.py:33
  15.0 17.9 %collective-permute-start.3 = (bf16[2,2,4,32,256]{4,3,2,1,0:T(8,128)(2,1)S(1)}, bf16[2,2,4,32,256]{4,3,2,1,0:T(8,128)(2,1)S(1)}, u32[]{:S(2)}, u32[]{:S(2)}) collective-permute-start(bf16[2,2,4,32,256]{4,3,2,1,0:T(8,128)(2,1)S(1)} %get-tuple-element.53), channel_id=1, source_target_pairs={{0,4},{1,5},{2,6},{3,7},{4,0},{5,1},{6,2},{7,3},{8,12},{9,13},{10,... | collective-permute-start | bytes 786440 | tf_op jit(solution)/shard_map/ppermute | solution.py:33
  16.6 51.8 %collective-permute-start.8 = (bf16[4,512,256]{2,1,0:T(8,128)(2,1)S(1)}, bf16[4,512,256]{2,1,0:T(8,128)(2,1)S(1)}, u32[]{:S(2)}, u32[]{:S(2)}) collective-permute-start(bf16[4,512,256]{2,1,0:T(8,128)(2,1)S(1)} %bitcast.8), channel_id=1, source_target_pairs={{0,16},{16,0},{1,17},{17,1},{2,18},{18,2},{3,19},{19,3},{4,20},{20... | collective-permute-start | bytes 3145736 | tf_op jit(solution)/shard_map/ppermute | solution.py:16
  18.1 16.7 %collective-permute-start.4 = (bf16[2,2,4,32,256]{4,3,2,1,0:T(8,128)(2,1)S(1)}, bf16[2,2,4,32,256]{4,3,2,1,0:T(8,128)(2,1)S(1)}, u32[]{:S(2)}, u32[]{:S(2)}) collective-permute-start(bf16[2,2,4,32,256]{4,3,2,1,0:T(8,128)(2,1)S(1)} %get-tuple-element.54), channel_id=1, source_target_pairs={{0,12},{1,13},{2,14},{3,15},{4,8},{5,9},{6,10},{7,11},{8,4},{9,5},... | collective-permute-start | bytes 786440 | tf_op jit(solution)/shard_map/ppermute | solution.py:33
  19.0 20.0 %collective-permute-start.5 = (bf16[2,2,4,32,256]{4,3,2,1,0:T(8,128)(2,1)S(1)}, bf16[2,2,4,32,256]{4,3,2,1,0:T(8,128)(2,1)S(1)}, u32[]{:S(2)}, u32[]{:S(2)}) collective-permute-start(bf16[2,2,4,32,256]{4,3,2,1,0:T(8,128)(2,1)S(1)} %get-tuple-element.55), channel_id=1, source_target_pairs={{0,6},{1,7},{2,4},{3,5},{4,2},{5,3},{6,0},{7,1},{8,14},{9,15},{10,... | collective-permute-start | bytes 786440 | tf_op jit(solution)/shard_map/ppermute | solution.py:33
  29.2 26.6 %collective-permute-start.6 = (bf16[2,2,4,32,256]{4,3,2,1,0:T(8,128)(2,1)S(1)}, bf16[2,2,4,32,256]{4,3,2,1,0:T(8,128)(2,1)S(1)}, u32[]{:S(2)}, u32[]{:S(2)}) collective-permute-start(bf16[2,2,4,32,256]{4,3,2,1,0:T(8,128)(2,1)S(1)} %get-tuple-element.56), channel_id=1, source_target_pairs={{0,10},{1,11},{2,8},{3,9},{4,14},{5,15},{6,12},{7,13},{8,2},{9,3},... | collective-permute-start | bytes 786440 | tf_op jit(solution)/shard_map/ppermute | solution.py:33
  32.9 22.9 %collective-permute-start.7 = (bf16[2,2,4,32,256]{4,3,2,1,0:T(8,128)(2,1)S(1)}, bf16[2,2,4,32,256]{4,3,2,1,0:T(8,128)(2,1)S(1)}, u32[]{:S(2)}, u32[]{:S(2)}) collective-permute-start(bf16[2,2,4,32,256]{4,3,2,1,0:T(8,128)(2,1)S(1)} %get-tuple-element.57), channel_id=1, source_target_pairs={{0,14},{1,15},{2,12},{3,13},{4,10},{5,11},{6,8},{7,9},{8,6},{9,7},... | collective-permute-start | bytes 786440 | tf_op jit(solution)/shard_map/ppermute | solution.py:33
  58.8 2.0 %collective-permute-start.9 = (bf16[8,4,32,256]{3,2,1,0:T(8,128)(2,1)S(1)}, bf16[8,4,32,256]{3,2,1,0:T(8,128)(2,1)S(1)}, u32[]{:S(2)}, u32[]{:S(2)}) collective-permute-start(bf16[8,4,32,256]{3,2,1,0:T(8,128)(2,1)S(1)} %get-tuple-element.63), channel_id=1, source_target_pairs={{0,1},{1,0},{2,3},{3,2},{4,5},{5,4},{6,7},{7,6},{8,9},{9,8},{10,11... | collective-permute-start | bytes 1572872 | tf_op jit(solution)/shard_map/ppermute | solution.py:33
  60.8 14.1 %collective-permute-start.10 = (bf16[2,4,32,256]{3,2,1,0:T(8,128)(2,1)S(1)}, bf16[2,4,32,256]{3,2,1,0:T(8,128)(2,1)S(1)}, u32[]{:S(2)}, u32[]{:S(2)}) collective-permute-start(bf16[2,4,32,256]{3,2,1,0:T(8,128)(2,1)S(1)} %get-tuple-element.64), channel_id=1, source_target_pairs={{0,8},{1,9},{2,10},{3,11},{4,12},{5,13},{6,14},{7,15},{8,0},{9,1},... | collective-permute-start | bytes 393224 | tf_op jit(solution)/shard_map/ppermute | solution.py:33
  71.5 36.6 %copy-start = (bf16[4,512,512]{2,1,0:T(8,128)(2,1)S(1)}, bf16[4,512,512]{2,1,0:T(8,128)(2,1)}, u32[]{:S(2)}) copy-start(bf16[4,512,512]{2,1,0:T(8,128)(2,1)} %left_ref.1) | copy-start | bytes 6291460
  74.9 3.0 %collective-permute-start.11 = (bf16[8,4,32,256]{3,2,1,0:T(8,128)(2,1)S(1)}, bf16[8,4,32,256]{3,2,1,0:T(8,128)(2,1)S(1)}, u32[]{:S(2)}, u32[]{:S(2)}) collective-permute-start(bf16[8,4,32,256]{3,2,1,0:T(8,128)(2,1)S(1)} %get-tuple-element.65), channel_id=1, source_target_pairs={{0,1},{1,0},{2,3},{3,2},{4,5},{5,4},{6,7},{7,6},{8,9},{9,8},{10,11... | collective-permute-start | bytes 1572872 | tf_op jit(solution)/shard_map/ppermute | solution.py:33
  74.9 20.9 %collective-permute-start.24 = (bf16[32,64,64]{2,1,0:T(8,128)(2,1)S(1)}, bf16[32,64,64]{2,1,0:T(8,128)(2,1)S(1)}, u32[]{:S(2)}, u32[]{:S(2)}) collective-permute-start(bf16[32,64,64]{2,1,0:T(8,128)(2,1)S(1)} %get-tuple-element.82.right_ref), channel_id=1, source_target_pairs={{0,16},{16,0},{1,17},{17,1},{2,18},{18,2},{3,19},{19,3},{4,20},{20... | collective-permute-start | bytes 786440 | tf_op jit(solution)/shard_map/ppermute | solution.py:16
  76.4 8.2 %collective-permute-start.18 = (bf16[2,4,32,256]{3,2,1,0:T(8,128)(2,1)S(1)}, bf16[2,4,32,256]{3,2,1,0:T(8,128)(2,1)S(1)}, u32[]{:S(2)}, u32[]{:S(2)}) collective-permute-start(bf16[2,4,32,256]{3,2,1,0:T(8,128)(2,1)S(1)} %get-tuple-element.75), channel_id=1, source_target_pairs={{0,12},{1,13},{2,14},{3,15},{4,8},{5,9},{6,10},{7,11},{8,4},{9,5},... | collective-permute-start | bytes 393224 | tf_op jit(solution)/shard_map/ppermute | solution.py:33
  76.4 19.4 %collective-permute-start.19 = (bf16[2,4,32,256]{3,2,1,0:T(8,128)(2,1)S(1)}, bf16[2,4,32,256]{3,2,1,0:T(8,128)(2,1)S(1)}, u32[]{:S(2)}, u32[]{:S(2)}) collective-permute-start(bf16[2,4,32,256]{3,2,1,0:T(8,128)(2,1)S(1)} %get-tuple-element.76), channel_id=1, source_target_pairs={{0,10},{1,11},{2,8},{3,9},{4,14},{5,15},{6,12},{7,13},{8,2},{9,3},... | collective-permute-start | bytes 393224 | tf_op jit(solution)/shard_map/ppermute | solution.py:33
  77.2 23.6 %collective-permute-start.20 = (bf16[2,4,32,256]{3,2,1,0:T(8,128)(2,1)S(1)}, bf16[2,4,32,256]{3,2,1,0:T(8,128)(2,1)S(1)}, u32[]{:S(2)}, u32[]{:S(2)}) collective-permute-start(bf16[2,4,32,256]{3,2,1,0:T(8,128)(2,1)S(1)} %get-tuple-element.77), channel_id=1, source_target_pairs={{0,2},{1,3},{2,0},{3,1},{4,6},{5,7},{6,4},{7,5},{8,10},{9,11},{10,... | collective-permute-start | bytes 393224 | tf_op jit(solution)/shard_map/ppermute | solution.py:33
  78.0 20.1 %collective-permute-start.23 = (bf16[2,4,32,256]{3,2,1,0:T(8,128)(2,1)S(1)}, bf16[2,4,32,256]{3,2,1,0:T(8,128)(2,1)S(1)}, u32[]{:S(2)}, u32[]{:S(2)}) collective-permute-start(bf16[2,4,32,256]{3,2,1,0:T(8,128)(2,1)S(1)} %get-tuple-element.81), channel_id=1, source_target_pairs={{0,14},{1,15},{2,12},{3,13},{4,10},{5,11},{6,8},{7,9},{8,6},{9,7},... | collective-permute-start | bytes 393224 | tf_op jit(solution)/shard_map/ppermute | solution.py:33
  84.7 16.2 %collective-permute-start.12 = (bf16[2,4,32,256]{3,2,1,0:T(8,128)(2,1)S(1)}, bf16[2,4,32,256]{3,2,1,0:T(8,128)(2,1)S(1)}, u32[]{:S(2)}, u32[]{:S(2)}) collective-permute-start(bf16[2,4,32,256]{3,2,1,0:T(8,128)(2,1)S(1)} %get-tuple-element.67), channel_id=1, source_target_pairs={{0,8},{1,9},{2,10},{3,11},{4,12},{5,13},{6,14},{7,15},{8,0},{9,1},... | collective-permute-start | bytes 393224 | tf_op jit(solution)/shard_map/ppermute | solution.py:33
  95.8 7.7 %collective-permute-start.21 = (bf16[2,4,32,256]{3,2,1,0:T(8,128)(2,1)S(1)}, bf16[2,4,32,256]{3,2,1,0:T(8,128)(2,1)S(1)}, u32[]{:S(2)}, u32[]{:S(2)}) collective-permute-start(bf16[2,4,32,256]{3,2,1,0:T(8,128)(2,1)S(1)} %get-tuple-element.78), channel_id=1, source_target_pairs={{0,4},{1,5},{2,6},{3,7},{4,0},{5,1},{6,2},{7,3},{8,12},{9,13},{10,... | collective-permute-start | bytes 393224 | tf_op jit(solution)/shard_map/ppermute | solution.py:33
  95.8 10.6 %collective-permute-start.22 = (bf16[2,4,32,256]{3,2,1,0:T(8,128)(2,1)S(1)}, bf16[2,4,32,256]{3,2,1,0:T(8,128)(2,1)S(1)}, u32[]{:S(2)}, u32[]{:S(2)}) collective-permute-start(bf16[2,4,32,256]{3,2,1,0:T(8,128)(2,1)S(1)} %get-tuple-element.79), channel_id=1, source_target_pairs={{0,6},{1,7},{2,4},{3,5},{4,2},{5,3},{6,0},{7,1},{8,14},{9,15},{10,... | collective-permute-start | bytes 393224 | tf_op jit(solution)/shard_map/ppermute | solution.py:33
  98.1 32.0 %collective-permute-start.26 = (bf16[8,4,32,256]{3,2,1,0:T(8,128)(2,1)S(1)}, bf16[8,4,32,256]{3,2,1,0:T(8,128)(2,1)S(1)}, u32[]{:S(2)}, u32[]{:S(2)}) collective-permute-start(bf16[8,4,32,256]{3,2,1,0:T(8,128)(2,1)S(1)} %gather_kernel.2.first_ref), channel_id=1, source_target_pairs={{0,16},{16,0},{1,17},{17,1},{2,18},{18,2},{3,19},{19,3},{4,20},{20... | collective-permute-start | bytes 1572872 | tf_op jit(solution)/shard_map/ppermute | solution.py:16
  106.4 23.7 %collective-permute-start.27 = (bf16[8,4,32,256]{3,2,1,0:T(8,128)(2,1)S(1)}, bf16[8,4,32,256]{3,2,1,0:T(8,128)(2,1)S(1)}, u32[]{:S(2)}, u32[]{:S(2)}) collective-permute-start(bf16[8,4,32,256]{3,2,1,0:T(8,128)(2,1)S(1)} %gather_kernel.3.second_ref), channel_id=1, source_target_pairs={{0,16},{16,0},{1,17},{17,1},{2,18},{18,2},{3,19},{19,3},{4,20},{20... | collective-permute-start | bytes 1572872 | tf_op jit(solution)/shard_map/ppermute | solution.py:16
  107.0 8.3 %collective-permute-start.13 = (bf16[2,4,32,256]{3,2,1,0:T(8,128)(2,1)S(1)}, bf16[2,4,32,256]{3,2,1,0:T(8,128)(2,1)S(1)}, u32[]{:S(2)}, u32[]{:S(2)}) collective-permute-start(bf16[2,4,32,256]{3,2,1,0:T(8,128)(2,1)S(1)} %get-tuple-element.68), channel_id=1, source_target_pairs={{0,12},{1,13},{2,14},{3,15},{4,8},{5,9},{6,10},{7,11},{8,4},{9,5},... | collective-permute-start | bytes 393224 | tf_op jit(solution)/shard_map/ppermute | solution.py:33
  107.0 12.6 %collective-permute-start.14 = (bf16[2,4,32,256]{3,2,1,0:T(8,128)(2,1)S(1)}, bf16[2,4,32,256]{3,2,1,0:T(8,128)(2,1)S(1)}, u32[]{:S(2)}, u32[]{:S(2)}) collective-permute-start(bf16[2,4,32,256]{3,2,1,0:T(8,128)(2,1)S(1)} %get-tuple-element.69), channel_id=1, source_target_pairs={{0,10},{1,11},{2,8},{3,9},{4,14},{5,15},{6,12},{7,13},{8,2},{9,3},... | collective-permute-start | bytes 393224 | tf_op jit(solution)/shard_map/ppermute | solution.py:33
  108.0 20.3 %copy-start.2 = (bf16[1,2048,256]{2,1,0:T(8,128)(2,1)S(1)}, bf16[1,2048,256]{2,1,0:T(8,128)(2,1)}, u32[]{:S(2)}) copy-start(bf16[1,2048,256]{2,1,0:T(8,128)(2,1)} %param.6) | copy-start | bytes 3145732
  108.0 20.3 %copy-start.3 = (bf16[1,2048,256]{2,1,0:T(8,128)(2,1)S(1)}, bf16[1,2048,256]{2,1,0:T(8,128)(2,1)}, u32[]{:S(2)}) copy-start(bf16[1,2048,256]{2,1,0:T(8,128)(2,1)} %param.7) | copy-start | bytes 3145732
  108.0 11.6 %collective-permute-start.15 = (bf16[2,4,32,256]{3,2,1,0:T(8,128)(2,1)S(1)}, bf16[2,4,32,256]{3,2,1,0:T(8,128)(2,1)S(1)}, u32[]{:S(2)}, u32[]{:S(2)}) collective-permute-start(bf16[2,4,32,256]{3,2,1,0:T(8,128)(2,1)S(1)} %get-tuple-element.70), channel_id=1, source_target_pairs={{0,2},{1,3},{2,0},{3,1},{4,6},{5,7},{6,4},{7,5},{8,10},{9,11},{10,... | collective-permute-start | bytes 393224 | tf_op jit(solution)/shard_map/ppermute | solution.py:33
  115.3 6.2 %collective-permute-start.16 = (bf16[2,4,32,256]{3,2,1,0:T(8,128)(2,1)S(1)}, bf16[2,4,32,256]{3,2,1,0:T(8,128)(2,1)S(1)}, u32[]{:S(2)}, u32[]{:S(2)}) collective-permute-start(bf16[2,4,32,256]{3,2,1,0:T(8,128)(2,1)S(1)} %get-tuple-element.71), channel_id=1, source_target_pairs={{0,4},{1,5},{2,6},{3,7},{4,0},{5,1},{6,2},{7,3},{8,12},{9,13},{10,... | collective-permute-start | bytes 393224 | tf_op jit(solution)/shard_map/ppermute | solution.py:33
  119.7 8.7 %collective-permute-start.17 = (bf16[2,4,32,256]{3,2,1,0:T(8,128)(2,1)S(1)}, bf16[2,4,32,256]{3,2,1,0:T(8,128)(2,1)S(1)}, u32[]{:S(2)}, u32[]{:S(2)}) collective-permute-start(bf16[2,4,32,256]{3,2,1,0:T(8,128)(2,1)S(1)} %get-tuple-element.72), channel_id=1, source_target_pairs={{0,6},{1,7},{2,4},{3,5},{4,2},{5,3},{6,0},{7,1},{8,14},{9,15},{10,... | collective-permute-start | bytes 393224 | tf_op jit(solution)/shard_map/ppermute | solution.py:33
  119.7 8.7 %collective-permute-start.25 = (bf16[2,4,32,256]{3,2,1,0:T(8,128)(2,1)S(1)}, bf16[2,4,32,256]{3,2,1,0:T(8,128)(2,1)S(1)}, u32[]{:S(2)}, u32[]{:S(2)}) collective-permute-start(bf16[2,4,32,256]{3,2,1,0:T(8,128)(2,1)S(1)} %get-tuple-element.85), channel_id=1, source_target_pairs={{0,14},{1,15},{2,12},{3,13},{4,10},{5,11},{6,8},{7,9},{8,6},{9,7},... | collective-permute-start | bytes 393224 | tf_op jit(solution)/shard_map/ppermute | solution.py:33

commit v11 on v10

--- a/solution.py
+++ b/solution.py
@@ -1,4 +1,5 @@
 import functools
+import math
 
 import jax
 import jax.numpy as jnp
@@ -24,8 +25,8 @@
     half = chips // 2
     near = list(range(1, half))
     far = list(range(half, chips, 2)) + list(range(half + 1, chips, 2))
-    in_turns = [t for pair in zip(near, far) for t in pair]
-    return [0] + in_turns + far[half - 1 :], [0] + far[:-1] + near + far[-1:]
+    in_turns = [t for pair in zip(far, near) for t in pair]
+    return [0] + in_turns + far[half - 1 :], [0] + far[:2] + near + far[2:], [0] + far + near
 
 
 def permute(array, offset):
@@ -153,26 +154,40 @@
 def column_forward_kernel(order, me_ref, right_ref, grad_ref, after_ref, *refs):
     chips = len(order)
     in_refs, out_refs = refs[:chips], refs[chips : chips + 2]
-    right_part_ref, wide, wide_out = refs[chips + 2 :]
+    packed_ref, wide, wide_out = refs[chips + 2 :]
     cols, count, _ = right_ref.shape
+    channels = packed_ref.shape[1]
+    terms = []
     me = me_ref[0]
     load_columns([(c, ref.at[1]) for c, ref in received_views(me, in_refs, order)], wide)
     for k in range(cols):
         mixed = column(wide, k, count, cols)
         store_column(wide_out, k, count, cols, dot(right_ref[k], mixed, ((1,), (0,))))
-        right_part_ref[k] = dot(grad_ref[k], mixed, ((1,), (1,))).astype(BF16)
+        terms.append(dot(grad_ref[k], mixed, ((1,), (1,))))
+        if len(terms) == channels // count:
+            row = k * count // channels * count
+            packed_ref[row : row + count] = jnp.concatenate(terms, axis=1).astype(BF16)
+            terms = []
     send_columns(wide_out, block_views(me, out_refs))
 
 
 def gather_kernel(me_ref, *refs):
-    out_ref = refs[-1]
-    for t, ref in enumerate(refs[:-1]):
-        for e in range(2):
-            out_ref[2 * t + e] = ref[e]
+    out_ref, n = refs[-1], 0
+    _, rows, cols, channels = out_ref.shape
+    size = rows * cols
+    for ref in refs[:-1]:
+        if ref.ndim == 2:
+            for start in range(0, ref.shape[0], size):
+                out_ref[n] = ref[start : start + size].reshape(rows, cols, channels)
+                n += 1
+            continue
+        for e in range(ref.shape[0]):
+            out_ref[n] = ref[e]
+            n += 1
 
 
 def load_rows(order, me, parts, hold):
-    half = parts[0].shape[0]
+    half = len(order)
     for n, t in enumerate(order):
         for e in range(2):
             j = 2 * n + e
@@ -201,17 +216,25 @@
     values_ref,
     first_ref,
     second_ref,
-    right_ref,
-    other_ref,
+    packed_ref,
     left_out_ref,
     right_out_ref,
     hold,
 ):
-    right_out_ref[...] = (right_ref[...].astype(F32) + other_ref[...].astype(F32)).astype(BF16)
     load_rows(order, me_ref[0], (first_ref, second_ref), hold)
     for i in range(term_ref.shape[0]):
         other = dot(row_of(hold, i), values_ref[i], ((1,), (1,))).astype(BF16)
         left_out_ref[i] = (term_ref[i].astype(F32) + other.astype(F32)).astype(BF16)
+    cols, count, _ = right_out_ref.shape
+    height, channels = packed_ref.shape
+    size = height // (first_ref.shape[0] - len(order))
+    share = channels // count
+    for n in range(height // count):
+        block, row = len(order) + n * count // size, n * count % size
+        other = first_ref[block].reshape(size, channels)[row : row + count]
+        total = packed_ref[n * count : (n + 1) * count].astype(F32) + other.astype(F32)
+        for q in range(share):
+            right_out_ref[n * share + q] = total[:, q * count : (q + 1) * count].astype(BF16)
 
 
 def output_kernel(order, me_ref, gate_ref, cotangent_ref, *refs):
@@ -237,9 +260,9 @@
     def shape(*dims):
         return jax.ShapeDtypeStruct(dims, BF16)
 
-    in_turns, far_first = orders(chips)
-
-    def ordered(kernel, order=in_turns):
+    in_turns, two_far, all_far = orders(chips)
+
+    def ordered(kernel, order):
         return functools.partial(kernel, order)
 
     block = (rows, cols, channels)
@@ -271,57 +294,59 @@
     other_values = swap_sequences(after(values, messages[0]))
     columns = listed(exchange(messages), in_turns)
     own, other, grad_column = call(
-        ordered(column_backward_kernel),
+        ordered(column_backward_kernel, in_turns),
         me,
         [right_factor, *columns],
         [shape(chips, *block)] * 2 + [shape(cols, count, channels)],
         [wide, wide],
         column_flops,
     )
-    back = pack(own, other)
+    back = exchange(pack(own, other))
+    packed_right = shape(cols * count * count // channels, channels)
     own, other, right_part = call(
-        ordered(column_forward_kernel),
+        ordered(column_forward_kernel, in_turns),
         me,
         [right_factor, grad_column, other_values, *columns],
-        [shape(chips, *block)] * 2 + [right],
+        [shape(chips, *block)] * 2 + [packed_right],
         [wide, wide],
         2 * column_flops,
         unblocked=[2],
     )
-    first = far_first[1]
-    first_back = permute(back[first], 2 * first)
-    second = pack(own, other, first_back)
-    back[far_first[-1]] = after(back[far_first[-1]], second[0])
-    other_right = swap_sequences(right_part)
-    back = listed(exchange(back, first, first_back), far_first)
-    first_second = permute(second[first], 2 * first)
-    back[-1] = after(back[-1], (first_second, other_right))
-    half_rows = shape(seq // 2, *block)
-    hold = pltpu.VMEM(whole.shape, BF16)
-    (first_half,) = call(gather_kernel, me, back[: chips // 2], [half_rows])
+    back = listed(back, two_far)
+    messages = pack(own, other, back[1 : chips - 2])
+    first = all_far[1]
+    first_second = permute(messages[first], 2 * first)
+    back[-1] = after(back[-1], first_second)
+    half_rows = shape(chips, *block)
+    extra = packed_right.size // math.prod(block)
+    (first_half,) = call(
+        gather_kernel, me, [*back[: chips // 2], right_part], [shape(chips + extra, *block)]
+    )
     (second_half,) = call(gather_kernel, me, back[chips // 2 :], [half_rows])
     other_first = swap_sequences(first_half)
     other_second = swap_sequences(second_half)
+    hold = pltpu.VMEM(whole.shape, BF16)
     grad_signal, left_term = call(
-        ordered(row_backward_kernel, far_first),
+        ordered(row_backward_kernel, two_far),
         me,
         [left_factor, values, first_half, second_half],
         [by_row, left],
         [hold],
         2 * row_flops,
     )
-    second[far_first[-1]] = after(second[far_first[-1]], left_term)
-    second = listed(exchange(second, first, first_second), far_first)
     grad_left, grad_right = call(
-        ordered(factor_sum_kernel, far_first),
+        ordered(factor_sum_kernel, two_far),
         me,
-        [left_term, other_values, other_first, other_second, right_part, other_right],
+        [left_term, other_values, other_first, other_second, right_part],
         [left, right],
         [hold],
         row_flops,
     )
+    last = all_far[-1]
+    messages[last] = after(messages[last], grad_left)
+    second = listed(exchange(messages, first, first_second), all_far)
     output, grad_gate = call(
-        ordered(output_kernel, far_first), me, [gate, cotangent, *second], [whole, whole]
+        ordered(output_kernel, all_far), me, [gate, cotangent, *second], [whole, whole]
     )
     return (
         output.reshape(signal.shape),

time: 133 us -> 128 us (0.962)
  waiting for transfers between devices: 74.6 us -> 66.6 us
  starting transfers between devices: 38.7 us -> 41.8 us
    ppermute x24, waiting for transfers between devices: 74.6 us -> 61.1 us  [permute(): return lax.ppermute(array, 'seq', [(i, i ^ offset) for i in range(seq)])]
    ppermute x4 -> x3, waiting for transfers between devices: 0.01 us -> 5.5 us  [swap_sequences(): return lax.ppermute(array, 'dp', [(0, 1), (1, 0)])]
    ppermute x24, starting transfers between devices: 34.5 us -> 38.1 us  [permute(): return lax.ppermute(array, 'seq', [(i, i ^ offset) for i in range(seq)])]
    ppermute x4 -> x3, starting transfers between devices: 4.18 us -> 3.64 us  [swap_sequences(): return lax.ppermute(array, 'dp', [(0, 1), (1, 0)])]
  transfers between devices with their start and end apart: 28 -> 27, of which waited for: 18 -> 13; matrix products, arithmetic and copies ran while one was open for 0% -> 0% of each run, Pallas kernels for 8% -> 9%
where the time goes in v11:
time: 128 us
  waiting for transfers between devices  66.6 us (52%)
  starting transfers between devices  41.8 us (33%)
  Pallas kernels  17.5 us (14%)
    ppermute x24, waiting for transfers between devices, permute(): return lax.ppermute(array, 'seq', [(i, i ^ offset) for i in range(seq)])  61.1 us
    ppermute x24, starting transfers between devices, permute(): return lax.ppermute(array, 'seq', [(i, i ^ offset) for i in range(seq)])  38.1 us
    pallas_call x11, Pallas kernels, call(): pl.pallas_call(kernel, out_shape=out_shapes, in_specs=[pl.BlockSpec(memor...  17.5 us
    ppermute x3, waiting for transfers between devices, swap_sequences(): return lax.ppermute(array, 'dp', [(0, 1), (1, 0)])  5.5 us
    ppermute x3, starting transfers between devices, swap_sequences(): return lax.ppermute(array, 'dp', [(0, 1), (1, 0)])  3.64 us
  transfers between devices with their start and end apart: 27, of which 13 were waited for; matrix products, arithmetic and copies ran while one was open for 0% of the time, Pallas kernels for 9%

profile of v11, /device:TPU:0, one launch (start us, length us, event | category | flops | bytes accessed | tf_op | source)
XLA Modules:
  0.0 127.9 jit_solution(14879743347095753925)
XLA Ops:
  0.6 4.4 %send_kernel.1 = (bf16[8,2,4,32,256]{4,3,2,1,0:T(8,128)(2,1)}, bf16[8,2,4,32,256]{4,3,2,1,0:T(8,128)(2,1)}) custom-call(s32[1]{0:T(128)} %bitcast.me_ref, bf16[4,16,32,256]{3,2,1,0:T(8,128)(2,1)} %bitcast.10, bf16[4,16,32,256]{3,2,1,0:T(8,128)(2,1)} %bitcast.12, bf16[4,512,512]{2,1,0:T(8,128)(2,1)} %left_ref.1, bf16[4,512,256]{2,1,0:T(8,128)(2,1)} %bitcast.7), custom_call_target="tpu_custom_call" | custom-call | flops 536870912 | bytes 7340032 | tf_op jit(solution)/shard_map/send_kernel/pallas_call | solution.py:54
  5.1 0.5 collective-permute-start
  5.6 2.5 %collective-permute-done.other_ref = bf16[8,2,4,32,256]{4,3,2,1,0:T(8,128)(2,1)S(1)} collective-permute-done((bf16[8,2,4,32,256]{4,3,2,1,0:T(8,128)(2,1)}, bf16[8,2,4,32,256]{4,3,2,1,0:T(8,128)(2,1)S(1)}, u32[]{:S(2)}, u32[]{:S(2)}) %collective-permute-start) | collective-permute-done | bytes 1048608 | tf_op jit(solution)/shard_map/ppermute | solution.py:34
  8.1 1.2 copy-done.5
  9.3 0.1 pack_kernel.3
  9.4 4.0 %collective-permute-start.1 = (bf16[2,2,4,32,256]{4,3,2,1,0:T(8,128)(2,1)S(1)}, bf16[2,2,4,32,256]{4,3,2,1,0:T(8,128)(2,1)S(1)}, u32[]{:S(2)}, u32[]{:S(2)}) collective-permute-start(bf16[2,2,4,32,256]{4,3,2,1,0:T(8,128)(2,1)S(1)} %get-tuple-element.50), channel_id=1, source_target_pairs={{0,8},{1,9},{2,10},{3,11},{4,12},{5,13},{6,14},{7,15},{8,0},{9,1},... | collective-permute-start | bytes 786440 | tf_op jit(solution)/shard_map/ppermute | solution.py:34
  13.5 1.5 %collective-permute-start.2 = (bf16[2,2,4,32,256]{4,3,2,1,0:T(8,128)(2,1)S(1)}, bf16[2,2,4,32,256]{4,3,2,1,0:T(8,128)(2,1)S(1)}, u32[]{:S(2)}, u32[]{:S(2)}) collective-permute-start(bf16[2,2,4,32,256]{4,3,2,1,0:T(8,128)(2,1)S(1)} %get-tuple-element.51), channel_id=1, source_target_pairs={{0,2},{1,3},{2,0},{3,1},{4,6},{5,7},{6,4},{7,5},{8,10},{9,11},{10,... | collective-permute-start | bytes 786440 | tf_op jit(solution)/shard_map/ppermute | solution.py:34
  15.0 1.3 %collective-permute-start.3 = (bf16[2,2,4,32,256]{4,3,2,1,0:T(8,128)(2,1)S(1)}, bf16[2,2,4,32,256]{4,3,2,1,0:T(8,128)(2,1)S(1)}, u32[]{:S(2)}, u32[]{:S(2)}) collective-permute-start(bf16[2,2,4,32,256]{4,3,2,1,0:T(8,128)(2,1)S(1)} %get-tuple-element.52), channel_id=1, source_target_pairs={{0,12},{1,13},{2,14},{3,15},{4,8},{5,9},{6,10},{7,11},{8,4},{9,5},... | collective-permute-start | bytes 786440 | tf_op jit(solution)/shard_map/ppermute | solution.py:34
  16.3 1.5 %collective-permute-start.8 = (bf16[4,512,256]{2,1,0:T(8,128)(2,1)S(1)}, bf16[4,512,256]{2,1,0:T(8,128)(2,1)S(1)}, u32[]{:S(2)}, u32[]{:S(2)}) collective-permute-start(bf16[4,512,256]{2,1,0:T(8,128)(2,1)S(1)} %bitcast.8), channel_id=1, source_target_pairs={{0,16},{16,0},{1,17},{17,1},{2,18},{18,2},{3,19},{19,3},{4,20},{20... | collective-permute-start | bytes 3145736 | tf_op jit(solution)/shard_map/ppermute | solution.py:17
  17.8 0.2 collective-permute-start.4
  18.1 13.8 %collective-permute-done.1.refs_1_ = bf16[2,2,4,32,256]{4,3,2,1,0:T(8,128)(2,1)S(1)} collective-permute-done((bf16[2,2,4,32,256]{4,3,2,1,0:T(8,128)(2,1)S(1)}, bf16[2,2,4,32,256]{4,3,2,1,0:T(8,128)(2,1)S(1)}, u32[]{:S(2)}, u32[]{:S(2)}) %collective-permute-start.1) | collective-permute-done | bytes 262176 | tf_op jit(solution)/shard_map/ppermute | solution.py:34
  31.8 0.9 collective-permute-start.5
  32.7 3.7 %collective-permute-start.6 = (bf16[2,2,4,32,256]{4,3,2,1,0:T(8,128)(2,1)S(1)}, bf16[2,2,4,32,256]{4,3,2,1,0:T(8,128)(2,1)S(1)}, u32[]{:S(2)}, u32[]{:S(2)}) collective-permute-start(bf16[2,2,4,32,256]{4,3,2,1,0:T(8,128)(2,1)S(1)} %get-tuple-element.55), channel_id=1, source_target_pairs={{0,6},{1,7},{2,4},{3,5},{4,2},{5,3},{6,0},{7,1},{8,14},{9,15},{10,... | collective-permute-start | bytes 786440 | tf_op jit(solution)/shard_map/ppermute | solution.py:34
  36.4 2.0 %collective-permute-start.7 = (bf16[2,2,4,32,256]{4,3,2,1,0:T(8,128)(2,1)S(1)}, bf16[2,2,4,32,256]{4,3,2,1,0:T(8,128)(2,1)S(1)}, u32[]{:S(2)}, u32[]{:S(2)}) collective-permute-start(bf16[2,2,4,32,256]{4,3,2,1,0:T(8,128)(2,1)S(1)} %get-tuple-element.56), channel_id=1, source_target_pairs={{0,14},{1,15},{2,12},{3,13},{4,10},{5,11},{6,8},{7,9},{8,6},{9,7},... | collective-permute-start | bytes 786440 | tf_op jit(solution)/shard_map/ppermute | solution.py:34
  38.5 17.2 %collective-permute-done.5.refs_5_ = bf16[2,2,4,32,256]{4,3,2,1,0:T(8,128)(2,1)S(1)} collective-permute-done((bf16[2,2,4,32,256]{4,3,2,1,0:T(8,128)(2,1)S(1)}, bf16[2,2,4,32,256]{4,3,2,1,0:T(8,128)(2,1)S(1)}, u32[]{:S(2)}, u32[]{:S(2)}) %collective-permute-start.5) | collective-permute-done | bytes 262176 | tf_op jit(solution)/shard_map/ppermute | solution.py:34
  55.6 3.0 %column_backward_kernel.1 = (bf16[8,4,32,256]{3,2,1,0:T(8,128)(2,1)S(1)}, bf16[8,4,32,256]{3,2,1,0:T(8,128)(2,1)S(1)}, bf16[32,64,256]{2,1,0:T(8,128)(2,1)S(1)}) custom-call(s32[1]{0:T(128)} %bitcast.me_ref, bf16[32,64,64]{2,1,0:T(8,128)(2,1)S(1)} %copy-done.4, bf16[2,2,4,32,256]{4,3,2,1,0:T(8,128)(2,1)S(1)} %get-tuple-element.49.refs_0_, ...), custom_call_target="tpu_custom_call" | custom-call | flops 67108864 | bytes 4456448 | tf_op jit(solution)/shard_map/column_backward_kernel/pallas_call | solution.py:54
  58.6 0.1 collective-permute-start.9
  58.7 1.9 %collective-permute-done.9.other_ref = bf16[8,4,32,256]{3,2,1,0:T(8,128)(2,1)S(1)} collective-permute-done((bf16[8,4,32,256]{3,2,1,0:T(8,128)(2,1)S(1)}, bf16[8,4,32,256]{3,2,1,0:T(8,128)(2,1)S(1)}, u32[]{:S(2)}, u32[]{:S(2)}) %collective-permute-start.9) | collective-permute-done | bytes 524320 | tf_op jit(solution)/shard_map/ppermute | solution.py:34
  60.6 0.1 pack_kernel.4
  60.7 7.5 %collective-permute-start.10 = (bf16[2,4,32,256]{3,2,1,0:T(8,128)(2,1)S(1)}, bf16[2,4,32,256]{3,2,1,0:T(8,128)(2,1)S(1)}, u32[]{:S(2)}, u32[]{:S(2)}) collective-permute-start(bf16[2,4,32,256]{3,2,1,0:T(8,128)(2,1)S(1)} %get-tuple-element.63), channel_id=1, source_target_pairs={{0,8},{1,9},{2,10},{3,11},{4,12},{5,13},{6,14},{7,15},{8,0},{9,1},... | collective-permute-start | bytes 393224 | tf_op jit(solution)/shard_map/ppermute | solution.py:34
  68.1 0.3 collective-permute-start.11
  68.5 0.7 collective-permute-start.12
  69.1 0.1 collective-permute-start.13
  69.3 2.7 %collective-permute-start.14 = (bf16[2,4,32,256]{3,2,1,0:T(8,128)(2,1)S(1)}, bf16[2,4,32,256]{3,2,1,0:T(8,128)(2,1)S(1)}, u32[]{:S(2)}, u32[]{:S(2)}) collective-permute-start(bf16[2,4,32,256]{3,2,1,0:T(8,128)(2,1)S(1)} %get-tuple-element.67), channel_id=1, source_target_pairs={{0,6},{1,7},{2,4},{3,5},{4,2},{5,3},{6,0},{7,1},{8,14},{9,15},{10,... | collective-permute-start | bytes 393224 | tf_op jit(solution)/shard_map/ppermute | solution.py:34
  71.9 3.3 %column_forward_kernel.1 = (bf16[8,4,32,256]{3,2,1,0:T(8,128)(2,1)S(1)}, bf16[8,4,32,256]{3,2,1,0:T(8,128)(2,1)S(1)}, bf16[512,256]{1,0:T(8,128)(2,1)S(1)}) custom-call(s32[1]{0:T(128)} %bitcast.me_ref, bf16[32,64,64]{2,1,0:T(8,128)(2,1)S(1)} %copy-done.4, bf16[32,64,256]{2,1,0:T(8,128)(2,1)S(1)} %get-tuple-element.57.grad_ref, ...), custom_call_target="tpu_custom_call" | custom-call | flops 134217728 | bytes 5767168 | tf_op jit(solution)/shard_map/column_forward_kernel/pallas_call | solution.py:54
  75.3 2.4 %collective-permute-done.10.refs_1_ = bf16[2,4,32,256]{3,2,1,0:T(8,128)(2,1)S(1)} collective-permute-done((bf16[2,4,32,256]{3,2,1,0:T(8,128)(2,1)S(1)}, bf16[2,4,32,256]{3,2,1,0:T(8,128)(2,1)S(1)}, u32[]{:S(2)}, u32[]{:S(2)}) %collective-permute-start.10) | collective-permute-done | bytes 131104 | tf_op jit(solution)/shard_map/ppermute | solution.py:34
  77.7 2.8 %collective-permute-done.13.refs_0_ = bf16[2,4,32,256]{3,2,1,0:T(8,128)(2,1)S(1)} collective-permute-done((bf16[2,4,32,256]{3,2,1,0:T(8,128)(2,1)S(1)}, bf16[2,4,32,256]{3,2,1,0:T(8,128)(2,1)S(1)}, u32[]{:S(2)}, u32[]{:S(2)}) %collective-permute-start.13) | collective-permute-done | bytes 131104 | tf_op jit(solution)/shard_map/ppermute | solution.py:34
  80.5 2.2 %collective-permute-done.14.refs_1_ = bf16[2,4,32,256]{3,2,1,0:T(8,128)(2,1)S(1)} collective-permute-done((bf16[2,4,32,256]{3,2,1,0:T(8,128)(2,1)S(1)}, bf16[2,4,32,256]{3,2,1,0:T(8,128)(2,1)S(1)}, u32[]{:S(2)}, u32[]{:S(2)}) %collective-permute-start.14) | collective-permute-done | bytes 131104 | tf_op jit(solution)/shard_map/ppermute | solution.py:34
  82.7 0.1 gather_kernel.2.first_ref
  82.8 1.5 %collective-permute-start.24 = (bf16[12,4,32,256]{3,2,1,0:T(8,128)(2,1)S(1)}, bf16[12,4,32,256]{3,2,1,0:T(8,128)(2,1)S(1)}, u32[]{:S(2)}, u32[]{:S(2)}) collective-permute-start(bf16[12,4,32,256]{3,2,1,0:T(8,128)(2,1)S(1)} %gather_kernel.2.first_ref), channel_id=1, source_target_pairs={{0,16},{16,0},{1,17},{17,1},{2,18},{18,2},{3,19},{19,3},{4,20},{20... | collective-permute-start | bytes 2359304 | tf_op jit(solution)/shard_map/ppermute | solution.py:17
  84.3 0.9 collective-permute-start.23
  85.3 0.1 pack_kernel.5
  85.4 0.9 collective-permute-start.16
  86.2 2.8 %collective-permute-start.22 = (bf16[2,4,32,256]{3,2,1,0:T(8,128)(2,1)S(1)}, bf16[2,4,32,256]{3,2,1,0:T(8,128)(2,1)S(1)}, u32[]{:S(2)}, u32[]{:S(2)}) collective-permute-start(bf16[2,4,32,256]{3,2,1,0:T(8,128)(2,1)S(1)} %get-tuple-element.79), channel_id=1, source_target_pairs={{0,10},{1,11},{2,8},{3,9},{4,14},{5,15},{6,12},{7,13},{8,2},{9,3},... | collective-permute-start | bytes 393224 | tf_op jit(solution)/shard_map/ppermute | solution.py:34
  89.1 4.4 %collective-permute-done.23.refs_3_ = bf16[2,4,32,256]{3,2,1,0:T(8,128)(2,1)S(1)} collective-permute-done((bf16[2,4,32,256]{3,2,1,0:T(8,128)(2,1)S(1)}, bf16[2,4,32,256]{3,2,1,0:T(8,128)(2,1)S(1)}, u32[]{:S(2)}, u32[]{:S(2)}) %collective-permute-start.23) | collective-permute-done | bytes 131104 | tf_op jit(solution)/shard_map/ppermute | solution.py:34
  93.5 8.2 %collective-permute-done.16.refs_1_ = bf16[2,4,32,256]{3,2,1,0:T(8,128)(2,1)S(1)} collective-permute-done((bf16[2,4,32,256]{3,2,1,0:T(8,128)(2,1)S(1)}, bf16[2,4,32,256]{3,2,1,0:T(8,128)(2,1)S(1)}, u32[]{:S(2)}, u32[]{:S(2)}) %collective-permute-start.16) | collective-permute-done | bytes 131104 | tf_op jit(solution)/shard_map/ppermute | solution.py:34
  101.6 2.0 %collective-permute-done.22.refs_2_ = bf16[2,4,32,256]{3,2,1,0:T(8,128)(2,1)S(1)} collective-permute-done((bf16[2,4,32,256]{3,2,1,0:T(8,128)(2,1)S(1)}, bf16[2,4,32,256]{3,2,1,0:T(8,128)(2,1)S(1)}, u32[]{:S(2)}, u32[]{:S(2)}) %collective-permute-start.22) | collective-permute-done | bytes 131104 | tf_op jit(solution)/shard_map/ppermute | solution.py:34
  103.7 0.6 collective-permute-start.25
  104.3 1.2 collective-permute-start.17
  105.6 3.5 %collective-permute-start.19 = (bf16[2,4,32,256]{3,2,1,0:T(8,128)(2,1)S(1)}, bf16[2,4,32,256]{3,2,1,0:T(8,128)(2,1)S(1)}, u32[]{:S(2)}, u32[]{:S(2)}) collective-permute-start(bf16[2,4,32,256]{3,2,1,0:T(8,128)(2,1)S(1)} %get-tuple-element.73), channel_id=1, source_target_pairs={{0,14},{1,15},{2,12},{3,13},{4,10},{5,11},{6,8},{7,9},{8,6},{9,7},... | collective-permute-start | bytes 393224 | tf_op jit(solution)/shard_map/ppermute | solution.py:34
  109.1 2.3 %row_backward_kernel.1 = (bf16[4,512,256]{2,1,0:T(8,128)(2,1)}, bf16[4,512,512]{2,1,0:T(8,128)(2,1)S(1)}) custom-call(s32[1]{0:T(128)} %bitcast.me_ref, bf16[4,512,512]{2,1,0:T(8,128)(2,1)S(1)} %copy-done, bf16[4,512,256]{2,1,0:T(8,128)(2,1)S(1)} %bitcast.9, bf16[12,4,32,256]{3,2,1,0:T(8,128)(2,1)S(1)} %gather_kernel.2.first_ref, ...), custom_call_target="tpu_custom_call" | custom-call | flops 1073741824 | bytes 7602176 | tf_op jit(solution)/shard_map/row_backward_kernel/pallas_call | solution.py:54
  111.4 0.5 collective-permute-start.20
  111.9 5.5 %collective-permute-done.25.second_ref = bf16[8,4,32,256]{3,2,1,0:T(8,128)(2,1)S(1)} collective-permute-done((bf16[8,4,32,256]{3,2,1,0:T(8,128)(2,1)S(1)}, bf16[8,4,32,256]{3,2,1,0:T(8,128)(2,1)S(1)}, u32[]{:S(2)}, u32[]{:S(2)}) %collective-permute-start.25) | collective-permute-done | bytes 524320 | tf_op jit(solution)/shard_map/ppermute | solution.py:17
  117.4 2.4 %factor_sum_kernel.1 = (bf16[4,512,512]{2,1,0:T(8,128)(2,1)}, bf16[32,64,64]{2,1,0:T(8,128)(2,1)}) custom-call(s32[1]{0:T(128)} %bitcast.me_ref, bf16[4,512,512]{2,1,0:T(8,128)(2,1)S(1)} %get-tuple-element.82.term_ref, bf16[4,512,256]{2,1,0:T(8,128)(2,1)S(1)} %collective-permute-done.8.after_ref.values_ref, ...), custom_call_target="tpu_custom_call" | custom-call | flops 536870912 | bytes 7077888 | tf_op jit(solution)/shard_map/factor_sum_kernel/pallas_call | solution.py:54
  119.8 2.6 %collective-permute-start.26 = (bf16[2,4,32,256]{3,2,1,0:T(8,128)(2,1)S(1)}, bf16[2,4,32,256]{3,2,1,0:T(8,128)(2,1)S(1)}, u32[]{:S(2)}, u32[]{:S(2)}) collective-permute-start(bf16[2,4,32,256]{3,2,1,0:T(8,128)(2,1)S(1)} %get-tuple-element.84), channel_id=1, source_target_pairs={{0,6},{1,7},{2,4},{3,5},{4,2},{5,3},{6,0},{7,1},{8,14},{9,15},{10,... | collective-permute-start | bytes 393224 | tf_op jit(solution)/shard_map/ppermute | solution.py:34
  122.4 1.0 collective-permute-done.21.refs_6_
  123.4 2.7 %collective-permute-done.26.refs_7_ = bf16[2,4,32,256]{3,2,1,0:T(8,128)(2,1)S(1)} collective-permute-done((bf16[2,4,32,256]{3,2,1,0:T(8,128)(2,1)S(1)}, bf16[2,4,32,256]{3,2,1,0:T(8,128)(2,1)S(1)}, u32[]{:S(2)}, u32[]{:S(2)}) %collective-permute-start.26) | collective-permute-done | bytes 131104 | tf_op jit(solution)/shard_map/ppermute | solution.py:34
  126.1 1.8 %output_kernel.1 = (bf16[4,16,32,256]{3,2,1,0:T(8,128)(2,1)}, bf16[4,16,32,256]{3,2,1,0:T(8,128)(2,1)}) custom-call(s32[1]{0:T(128)} %bitcast.me_ref, bf16[4,16,32,256]{3,2,1,0:T(8,128)(2,1)S(1)} %bitcast.11, bf16[4,16,32,256]{3,2,1,0:T(8,128)(2,1)S(1)} %bitcast.13, bf16[2,4,32,256]{3,2,1,0:T(8,128)(2,1)S(1)} %get-tuple-element.69.refs_0_, ...), custom_call_target="tpu_custom_call" | custom-call | bytes 5242880 | tf_op jit(solution)/shard_map/output_kernel/pallas_call | solution.py:54
  (29 shorter events, 0.1 us)
Async XLA Ops:
  5.0 11.3 %copy-start.1 = (bf16[1,2048,256]{2,1,0:T(8,128)(2,1)S(1)}, bf16[1,2048,256]{2,1,0:T(8,128)(2,1)}, u32[]{:S(2)}) copy-start(bf16[1,2048,256]{2,1,0:T(8,128)(2,1)} %param.5) | copy-start | bytes 3145732
  5.1 50.6 %copy-start.4 = (bf16[32,64,64]{2,1,0:T(8,128)(2,1)S(1)}, bf16[32,64,64]{2,1,0:T(8,128)(2,1)}, u32[]{:S(2)}) copy-start(bf16[32,64,64]{2,1,0:T(8,128)(2,1)} %right_ref.3) | copy-start | bytes 786436
  5.1 3.0 %collective-permute-start = (bf16[8,2,4,32,256]{4,3,2,1,0:T(8,128)(2,1)}, bf16[8,2,4,32,256]{4,3,2,1,0:T(8,128)(2,1)S(1)}, u32[]{:S(2)}, u32[]{:S(2)}) collective-permute-start(bf16[8,2,4,32,256]{4,3,2,1,0:T(8,128)(2,1)} %get-tuple-element.48), channel_id=1, source_target_pairs={{0,1},{1,0},{2,3},{3,2},{4,5},{5,4},{6,7},{7,6},{8,9},{9,8},{10,11... | collective-permute-start | bytes 3145736 | tf_op jit(solution)/shard_map/ppermute | solution.py:34
  8.1 1.2 copy-start.5
  9.4 22.4 %collective-permute-start.1 = (bf16[2,2,4,32,256]{4,3,2,1,0:T(8,128)(2,1)S(1)}, bf16[2,2,4,32,256]{4,3,2,1,0:T(8,128)(2,1)S(1)}, u32[]{:S(2)}, u32[]{:S(2)}) collective-permute-start(bf16[2,2,4,32,256]{4,3,2,1,0:T(8,128)(2,1)S(1)} %get-tuple-element.50), channel_id=1, source_target_pairs={{0,8},{1,9},{2,10},{3,11},{4,12},{5,13},{6,14},{7,15},{8,0},{9,1},... | collective-permute-start | bytes 786440 | tf_op jit(solution)/shard_map/ppermute | solution.py:34
  13.5 19.2 %collective-permute-start.2 = (bf16[2,2,4,32,256]{4,3,2,1,0:T(8,128)(2,1)S(1)}, bf16[2,2,4,32,256]{4,3,2,1,0:T(8,128)(2,1)S(1)}, u32[]{:S(2)}, u32[]{:S(2)}) collective-permute-start(bf16[2,2,4,32,256]{4,3,2,1,0:T(8,128)(2,1)S(1)} %get-tuple-element.51), channel_id=1, source_target_pairs={{0,2},{1,3},{2,0},{3,1},{4,6},{5,7},{6,4},{7,5},{8,10},{9,11},{10,... | collective-permute-start | bytes 786440 | tf_op jit(solution)/shard_map/ppermute | solution.py:34
  15.0 21.5 %collective-permute-start.3 = (bf16[2,2,4,32,256]{4,3,2,1,0:T(8,128)(2,1)S(1)}, bf16[2,2,4,32,256]{4,3,2,1,0:T(8,128)(2,1)S(1)}, u32[]{:S(2)}, u32[]{:S(2)}) collective-permute-start(bf16[2,2,4,32,256]{4,3,2,1,0:T(8,128)(2,1)S(1)} %get-tuple-element.52), channel_id=1, source_target_pairs={{0,12},{1,13},{2,14},{3,15},{4,8},{5,9},{6,10},{7,11},{8,4},{9,5},... | collective-permute-start | bytes 786440 | tf_op jit(solution)/shard_map/ppermute | solution.py:34
  16.3 52.9 %collective-permute-start.8 = (bf16[4,512,256]{2,1,0:T(8,128)(2,1)S(1)}, bf16[4,512,256]{2,1,0:T(8,128)(2,1)S(1)}, u32[]{:S(2)}, u32[]{:S(2)}) collective-permute-start(bf16[4,512,256]{2,1,0:T(8,128)(2,1)S(1)} %bitcast.8), channel_id=1, source_target_pairs={{0,16},{16,0},{1,17},{17,1},{2,18},{18,2},{3,19},{19,3},{4,20},{20... | collective-permute-start | bytes 3145736 | tf_op jit(solution)/shard_map/ppermute | solution.py:17
  17.8 20.6 %collective-permute-start.4 = (bf16[2,2,4,32,256]{4,3,2,1,0:T(8,128)(2,1)S(1)}, bf16[2,2,4,32,256]{4,3,2,1,0:T(8,128)(2,1)S(1)}, u32[]{:S(2)}, u32[]{:S(2)}) collective-permute-start(bf16[2,2,4,32,256]{4,3,2,1,0:T(8,128)(2,1)S(1)} %get-tuple-element.53), channel_id=1, source_target_pairs={{0,4},{1,5},{2,6},{3,7},{4,0},{5,1},{6,2},{7,3},{8,12},{9,13},{10,... | collective-permute-start | bytes 786440 | tf_op jit(solution)/shard_map/ppermute | solution.py:34
  31.8 23.8 %collective-permute-start.5 = (bf16[2,2,4,32,256]{4,3,2,1,0:T(8,128)(2,1)S(1)}, bf16[2,2,4,32,256]{4,3,2,1,0:T(8,128)(2,1)S(1)}, u32[]{:S(2)}, u32[]{:S(2)}) collective-permute-start(bf16[2,2,4,32,256]{4,3,2,1,0:T(8,128)(2,1)S(1)} %get-tuple-element.54), channel_id=1, source_target_pairs={{0,10},{1,11},{2,8},{3,9},{4,14},{5,15},{6,12},{7,13},{8,2},{9,3},... | collective-permute-start | bytes 786440 | tf_op jit(solution)/shard_map/ppermute | solution.py:34
  32.7 22.9 %collective-permute-start.6 = (bf16[2,2,4,32,256]{4,3,2,1,0:T(8,128)(2,1)S(1)}, bf16[2,2,4,32,256]{4,3,2,1,0:T(8,128)(2,1)S(1)}, u32[]{:S(2)}, u32[]{:S(2)}) collective-permute-start(bf16[2,2,4,32,256]{4,3,2,1,0:T(8,128)(2,1)S(1)} %get-tuple-element.55), channel_id=1, source_target_pairs={{0,6},{1,7},{2,4},{3,5},{4,2},{5,3},{6,0},{7,1},{8,14},{9,15},{10,... | collective-permute-start | bytes 786440 | tf_op jit(solution)/shard_map/ppermute | solution.py:34
  36.4 19.2 %collective-permute-start.7 = (bf16[2,2,4,32,256]{4,3,2,1,0:T(8,128)(2,1)S(1)}, bf16[2,2,4,32,256]{4,3,2,1,0:T(8,128)(2,1)S(1)}, u32[]{:S(2)}, u32[]{:S(2)}) collective-permute-start(bf16[2,2,4,32,256]{4,3,2,1,0:T(8,128)(2,1)S(1)} %get-tuple-element.56), channel_id=1, source_target_pairs={{0,14},{1,15},{2,12},{3,13},{4,10},{5,11},{6,8},{7,9},{8,6},{9,7},... | collective-permute-start | bytes 786440 | tf_op jit(solution)/shard_map/ppermute | solution.py:34
  58.6 2.0 %collective-permute-start.9 = (bf16[8,4,32,256]{3,2,1,0:T(8,128)(2,1)S(1)}, bf16[8,4,32,256]{3,2,1,0:T(8,128)(2,1)S(1)}, u32[]{:S(2)}, u32[]{:S(2)}) collective-permute-start(bf16[8,4,32,256]{3,2,1,0:T(8,128)(2,1)S(1)} %get-tuple-element.62), channel_id=1, source_target_pairs={{0,1},{1,0},{2,3},{3,2},{4,5},{5,4},{6,7},{7,6},{8,9},{9,8},{10,11... | collective-permute-start | bytes 1572872 | tf_op jit(solution)/shard_map/ppermute | solution.py:34
  60.7 17.1 %collective-permute-start.10 = (bf16[2,4,32,256]{3,2,1,0:T(8,128)(2,1)S(1)}, bf16[2,4,32,256]{3,2,1,0:T(8,128)(2,1)S(1)}, u32[]{:S(2)}, u32[]{:S(2)}) collective-permute-start(bf16[2,4,32,256]{3,2,1,0:T(8,128)(2,1)S(1)} %get-tuple-element.63), channel_id=1, source_target_pairs={{0,8},{1,9},{2,10},{3,11},{4,12},{5,13},{6,14},{7,15},{8,0},{9,1},... | collective-permute-start | bytes 393224 | tf_op jit(solution)/shard_map/ppermute | solution.py:34
  68.1 9.6 %collective-permute-start.11 = (bf16[2,4,32,256]{3,2,1,0:T(8,128)(2,1)S(1)}, bf16[2,4,32,256]{3,2,1,0:T(8,128)(2,1)S(1)}, u32[]{:S(2)}, u32[]{:S(2)}) collective-permute-start(bf16[2,4,32,256]{3,2,1,0:T(8,128)(2,1)S(1)} %get-tuple-element.64), channel_id=1, source_target_pairs={{0,12},{1,13},{2,14},{3,15},{4,8},{5,9},{6,10},{7,11},{8,4},{9,5},... | collective-permute-start | bytes 393224 | tf_op jit(solution)/shard_map/ppermute | solution.py:34
  68.5 9.3 %collective-permute-start.12 = (bf16[2,4,32,256]{3,2,1,0:T(8,128)(2,1)S(1)}, bf16[2,4,32,256]{3,2,1,0:T(8,128)(2,1)S(1)}, u32[]{:S(2)}, u32[]{:S(2)}) collective-permute-start(bf16[2,4,32,256]{3,2,1,0:T(8,128)(2,1)S(1)} %get-tuple-element.65), channel_id=1, source_target_pairs={{0,2},{1,3},{2,0},{3,1},{4,6},{5,7},{6,4},{7,5},{8,10},{9,11},{10,... | collective-permute-start | bytes 393224 | tf_op jit(solution)/shard_map/ppermute | solution.py:34
  69.1 11.4 %collective-permute-start.13 = (bf16[2,4,32,256]{3,2,1,0:T(8,128)(2,1)S(1)}, bf16[2,4,32,256]{3,2,1,0:T(8,128)(2,1)S(1)}, u32[]{:S(2)}, u32[]{:S(2)}) collective-permute-start(bf16[2,4,32,256]{3,2,1,0:T(8,128)(2,1)S(1)} %get-tuple-element.66), channel_id=1, source_target_pairs={{0,4},{1,5},{2,6},{3,7},{4,0},{5,1},{6,2},{7,3},{8,12},{9,13},{10,... | collective-permute-start | bytes 393224 | tf_op jit(solution)/shard_map/ppermute | solution.py:34
  69.3 13.5 %collective-permute-start.14 = (bf16[2,4,32,256]{3,2,1,0:T(8,128)(2,1)S(1)}, bf16[2,4,32,256]{3,2,1,0:T(8,128)(2,1)S(1)}, u32[]{:S(2)}, u32[]{:S(2)}) collective-permute-start(bf16[2,4,32,256]{3,2,1,0:T(8,128)(2,1)S(1)} %get-tuple-element.67), channel_id=1, source_target_pairs={{0,6},{1,7},{2,4},{3,5},{4,2},{5,3},{6,0},{7,1},{8,14},{9,15},{10,... | collective-permute-start | bytes 393224 | tf_op jit(solution)/shard_map/ppermute | solution.py:34
  75.3 33.8 %copy-start = (bf16[4,512,512]{2,1,0:T(8,128)(2,1)S(1)}, bf16[4,512,512]{2,1,0:T(8,128)(2,1)}, u32[]{:S(2)}) copy-start(bf16[4,512,512]{2,1,0:T(8,128)(2,1)} %left_ref.1) | copy-start | bytes 6291460
  82.7 2.6 %collective-permute-start.15 = (bf16[8,4,32,256]{3,2,1,0:T(8,128)(2,1)S(1)}, bf16[8,4,32,256]{3,2,1,0:T(8,128)(2,1)S(1)}, u32[]{:S(2)}, u32[]{:S(2)}) collective-permute-start(bf16[8,4,32,256]{3,2,1,0:T(8,128)(2,1)S(1)} %get-tuple-element.68), channel_id=1, source_target_pairs={{0,1},{1,0},{2,3},{3,2},{4,5},{5,4},{6,7},{7,6},{8,9},{9,8},{10,11... | collective-permute-start | bytes 1572872 | tf_op jit(solution)/shard_map/ppermute | solution.py:34
  82.8 28.6 %collective-permute-start.24 = (bf16[12,4,32,256]{3,2,1,0:T(8,128)(2,1)S(1)}, bf16[12,4,32,256]{3,2,1,0:T(8,128)(2,1)S(1)}, u32[]{:S(2)}, u32[]{:S(2)}) collective-permute-start(bf16[12,4,32,256]{3,2,1,0:T(8,128)(2,1)S(1)} %gather_kernel.2.first_ref), channel_id=1, source_target_pairs={{0,16},{16,0},{1,17},{17,1},{2,18},{18,2},{3,19},{19,3},{4,20},{20... | collective-permute-start | bytes 2359304 | tf_op jit(solution)/shard_map/ppermute | solution.py:17
  84.3 9.1 %collective-permute-start.23 = (bf16[2,4,32,256]{3,2,1,0:T(8,128)(2,1)S(1)}, bf16[2,4,32,256]{3,2,1,0:T(8,128)(2,1)S(1)}, u32[]{:S(2)}, u32[]{:S(2)}) collective-permute-start(bf16[2,4,32,256]{3,2,1,0:T(8,128)(2,1)S(1)} %get-tuple-element.80), channel_id=1, source_target_pairs={{0,14},{1,15},{2,12},{3,13},{4,10},{5,11},{6,8},{7,9},{8,6},{9,7},... | collective-permute-start | bytes 393224 | tf_op jit(solution)/shard_map/ppermute | solution.py:34
  85.4 16.3 %collective-permute-start.16 = (bf16[2,4,32,256]{3,2,1,0:T(8,128)(2,1)S(1)}, bf16[2,4,32,256]{3,2,1,0:T(8,128)(2,1)S(1)}, u32[]{:S(2)}, u32[]{:S(2)}) collective-permute-start(bf16[2,4,32,256]{3,2,1,0:T(8,128)(2,1)S(1)} %get-tuple-element.70), channel_id=1, source_target_pairs={{0,8},{1,9},{2,10},{3,11},{4,12},{5,13},{6,14},{7,15},{8,0},{9,1},... | collective-permute-start | bytes 393224 | tf_op jit(solution)/shard_map/ppermute | solution.py:34
  86.2 17.4 %collective-permute-start.22 = (bf16[2,4,32,256]{3,2,1,0:T(8,128)(2,1)S(1)}, bf16[2,4,32,256]{3,2,1,0:T(8,128)(2,1)S(1)}, u32[]{:S(2)}, u32[]{:S(2)}) collective-permute-start(bf16[2,4,32,256]{3,2,1,0:T(8,128)(2,1)S(1)} %get-tuple-element.79), channel_id=1, source_target_pairs={{0,10},{1,11},{2,8},{3,9},{4,14},{5,15},{6,12},{7,13},{8,2},{9,3},... | collective-permute-start | bytes 393224 | tf_op jit(solution)/shard_map/ppermute | solution.py:34
  103.7 13.7 %collective-permute-start.25 = (bf16[8,4,32,256]{3,2,1,0:T(8,128)(2,1)S(1)}, bf16[8,4,32,256]{3,2,1,0:T(8,128)(2,1)S(1)}, u32[]{:S(2)}, u32[]{:S(2)}) collective-permute-start(bf16[8,4,32,256]{3,2,1,0:T(8,128)(2,1)S(1)} %gather_kernel.3.second_ref), channel_id=1, source_target_pairs={{0,16},{16,0},{1,17},{17,1},{2,18},{18,2},{3,19},{19,3},{4,20},{20... | collective-permute-start | bytes 1572872 | tf_op jit(solution)/shard_map/ppermute | solution.py:17
  104.3 15.5 %collective-permute-start.17 = (bf16[2,4,32,256]{3,2,1,0:T(8,128)(2,1)S(1)}, bf16[2,4,32,256]{3,2,1,0:T(8,128)(2,1)S(1)}, u32[]{:S(2)}, u32[]{:S(2)}) collective-permute-start(bf16[2,4,32,256]{3,2,1,0:T(8,128)(2,1)S(1)} %get-tuple-element.71), channel_id=1, source_target_pairs={{0,12},{1,13},{2,14},{3,15},{4,8},{5,9},{6,10},{7,11},{8,4},{9,5},... | collective-permute-start | bytes 393224 | tf_op jit(solution)/shard_map/ppermute | solution.py:34
  105.6 16.8 %collective-permute-start.18 = (bf16[2,4,32,256]{3,2,1,0:T(8,128)(2,1)S(1)}, bf16[2,4,32,256]{3,2,1,0:T(8,128)(2,1)S(1)}, u32[]{:S(2)}, u32[]{:S(2)}) collective-permute-start(bf16[2,4,32,256]{3,2,1,0:T(8,128)(2,1)S(1)} %get-tuple-element.72), channel_id=1, source_target_pairs={{0,10},{1,11},{2,8},{3,9},{4,14},{5,15},{6,12},{7,13},{8,2},{9,3},... | collective-permute-start | bytes 393224 | tf_op jit(solution)/shard_map/ppermute | solution.py:34
  105.6 16.8 %collective-permute-start.19 = (bf16[2,4,32,256]{3,2,1,0:T(8,128)(2,1)S(1)}, bf16[2,4,32,256]{3,2,1,0:T(8,128)(2,1)S(1)}, u32[]{:S(2)}, u32[]{:S(2)}) collective-permute-start(bf16[2,4,32,256]{3,2,1,0:T(8,128)(2,1)S(1)} %get-tuple-element.73), channel_id=1, source_target_pairs={{0,14},{1,15},{2,12},{3,13},{4,10},{5,11},{6,8},{7,9},{8,6},{9,7},... | collective-permute-start | bytes 393224 | tf_op jit(solution)/shard_map/ppermute | solution.py:34
  111.4 11.0 %collective-permute-start.20 = (bf16[2,4,32,256]{3,2,1,0:T(8,128)(2,1)S(1)}, bf16[2,4,32,256]{3,2,1,0:T(8,128)(2,1)S(1)}, u32[]{:S(2)}, u32[]{:S(2)}) collective-permute-start(bf16[2,4,32,256]{3,2,1,0:T(8,128)(2,1)S(1)} %get-tuple-element.74), channel_id=1, source_target_pairs={{0,2},{1,3},{2,0},{3,1},{4,6},{5,7},{6,4},{7,5},{8,10},{9,11},{10,... | collective-permute-start | bytes 393224 | tf_op jit(solution)/shard_map/ppermute | solution.py:34
  117.4 6.0 %collective-permute-start.21 = (bf16[2,4,32,256]{3,2,1,0:T(8,128)(2,1)S(1)}, bf16[2,4,32,256]{3,2,1,0:T(8,128)(2,1)S(1)}, u32[]{:S(2)}, u32[]{:S(2)}) collective-permute-start(bf16[2,4,32,256]{3,2,1,0:T(8,128)(2,1)S(1)} %get-tuple-element.75), channel_id=1, source_target_pairs={{0,4},{1,5},{2,6},{3,7},{4,0},{5,1},{6,2},{7,3},{8,12},{9,13},{10,... | collective-permute-start | bytes 393224 | tf_op jit(solution)/shard_map/ppermute | solution.py:34
  117.4 8.7 %copy-start.2 = (bf16[1,2048,256]{2,1,0:T(8,128)(2,1)S(1)}, bf16[1,2048,256]{2,1,0:T(8,128)(2,1)}, u32[]{:S(2)}) copy-start(bf16[1,2048,256]{2,1,0:T(8,128)(2,1)} %param.6) | copy-start | bytes 3145732
  117.4 8.7 %copy-start.3 = (bf16[1,2048,256]{2,1,0:T(8,128)(2,1)S(1)}, bf16[1,2048,256]{2,1,0:T(8,128)(2,1)}, u32[]{:S(2)}) copy-start(bf16[1,2048,256]{2,1,0:T(8,128)(2,1)} %param.7) | copy-start | bytes 3145732
  119.8 6.3 %collective-permute-start.26 = (bf16[2,4,32,256]{3,2,1,0:T(8,128)(2,1)S(1)}, bf16[2,4,32,256]{3,2,1,0:T(8,128)(2,1)S(1)}, u32[]{:S(2)}, u32[]{:S(2)}) collective-permute-start(bf16[2,4,32,256]{3,2,1,0:T(8,128)(2,1)S(1)} %get-tuple-element.84), channel_id=1, source_target_pairs={{0,6},{1,7},{2,4},{3,5},{4,2},{5,3},{6,0},{7,1},{8,14},{9,15},{10,... | collective-permute-start | bytes 393224 | tf_op jit(solution)/shard_map/ppermute | solution.py:34

commit v12 on v11

--- a/solution.py
+++ b/solution.py
@@ -34,11 +34,12 @@
     return lax.ppermute(array, "seq", [(i, i ^ offset) for i in range(seq)])
 
 
-def exchange(messages, sent=0, received=None):
-    result = [permute(message, 2 * t) if t else message for t, message in enumerate(messages)]
-    if received is not None:
-        result[sent] = received
-    return result
+def exchange(messages, done=()):
+    done = dict(done)
+    return [
+        done[t] if t in done else permute(message, 2 * t) if t else message
+        for t, message in enumerate(messages)
+    ]
 
 
 def listed(messages, order):
@@ -75,36 +76,55 @@
     return [(me ^ (2 * t + e), ref.at[e]) for t, ref in zip(order, refs) for e in range(2)]
 
 
-def send_kernel(me_ref, gate_hbm, cotangent_hbm, left_hbm, values_hbm, *refs):
-    out_refs = refs[:2]
-    gate, cotangent, left, values, hold, sems = refs[2:]
+def product_kernel(me_ref, gate_hbm, cotangent_hbm, *refs):
+    out_refs, (gate, cotangent, sems) = refs[:2], refs[2:]
+    rows = gate.shape[0]
+    loads = [
+        [
+            pltpu.make_async_copy(source.at[i], target.at[i], sems.at[n, i])
+            for n, (source, target) in enumerate(((gate_hbm, gate), (cotangent_hbm, cotangent)))
+        ]
+        for i in range(rows)
+    ]
+    for pair in loads:
+        for load in pair:
+            load.start()
+    blocks = block_views(me_ref[0], out_refs)
+    for i in range(rows):
+        for load in loads[i]:
+            load.wait()
+        for c, ref in blocks:
+            ref[i] = (gate[i, c].astype(F32) * cotangent[i, c].astype(F32)).astype(BF16)
+
+
+def mix_kernel(me_ref, left_ref, values_ref, *refs):
+    out_refs, hold = refs[:2], refs[2]
     rows, seq, cols, channels = hold.shape
-    me = me_ref[0]
-    loads = []
     for i in range(rows):
-        for n, (source, target) in enumerate(((left_hbm, left), (values_hbm, values))):
-            loads.append(pltpu.make_async_copy(source.at[i], target.at[i], sems.at[n, i]))
-    loads.append(pltpu.make_async_copy(gate_hbm, gate, sems.at[2, 0]))
-    loads.append(pltpu.make_async_copy(cotangent_hbm, cotangent, sems.at[2, 1]))
-    for load in loads:
-        load.start()
-    for i in range(rows):
-        loads[2 * i].wait()
-        loads[2 * i + 1].wait()
-        mixed = dot(left[i], values[i], ((1,), (0,)))
+        mixed = dot(left_ref[i], values_ref[i], ((1,), (0,)))
         hold[i] = mixed.astype(BF16).reshape(seq, cols, channels)
-    loads[-2].wait()
-    loads[-1].wait()
-    for c, ref in block_views(me, out_refs):
-        wide = gate[:, c].astype(F32) * cotangent[:, c].astype(F32)
-        ref[0] = wide.astype(BF16)
-        ref[1] = hold[:, c]
+    for c, ref in block_views(me_ref[0], out_refs):
+        ref[...] = hold[:, c]
 
 
 def pack_kernel(me_ref, own_ref, other_ref, *out_refs):
     for t, out_ref in enumerate(out_refs):
         out_ref[0] = own_ref[t]
         out_ref[1] = other_ref[t]
+
+
+def pack_pairs_kernel(me_ref, *refs):
+    pairs, out_refs = (refs[0:2], refs[2:4]), refs[4:]
+    last = len(out_refs) - 2
+    for which, pair in enumerate(pairs):
+        for e, ref in enumerate(pair):
+            for t in range(last):
+                out_refs[t][e, which] = ref[t]
+            out_refs[last + which][e] = ref[last]
+
+
+def of_pair(views, which):
+    return [(c, ref.at[which] if len(ref.shape) == 4 else ref) for c, ref in views]
 
 
 def load_columns(blocks, wide):
@@ -143,7 +163,7 @@
     by_column_ref, wide, wide_out = refs[chips + 2 :]
     cols, count, _ = right_ref.shape
     me = me_ref[0]
-    load_columns([(c, ref.at[0]) for c, ref in received_views(me, in_refs, order)], wide)
+    load_columns(of_pair(received_views(me, in_refs, order), 0), wide)
     for k in range(cols):
         grad = column(wide, k, count, cols)
         by_column_ref[k] = grad
@@ -159,7 +179,7 @@
     channels = packed_ref.shape[1]
     terms = []
     me = me_ref[0]
-    load_columns([(c, ref.at[1]) for c, ref in received_views(me, in_refs, order)], wide)
+    load_columns(of_pair(received_views(me, in_refs, order), 1), wide)
     for k in range(cols):
         mixed = column(wide, k, count, cols)
         store_column(wide_out, k, count, cols, dot(right_ref[k], mixed, ((1,), (0,))))
@@ -187,11 +207,11 @@
 
 
 def load_rows(order, me, parts, hold):
-    half = len(order)
+    left = 2 * len(order) - parts[1].shape[0]
     for n, t in enumerate(order):
         for e in range(2):
             j = 2 * n + e
-            hold[:, me ^ (2 * t + e)] = parts[j // half][j % half]
+            hold[:, me ^ (2 * t + e)] = parts[0][j] if j < left else parts[1][j - left]
 
 
 def row_of(hold, i):
@@ -227,10 +247,11 @@
         left_out_ref[i] = (term_ref[i].astype(F32) + other.astype(F32)).astype(BF16)
     cols, count, _ = right_out_ref.shape
     height, channels = packed_ref.shape
-    size = height // (first_ref.shape[0] - len(order))
+    blocks = 2 * len(order) - second_ref.shape[0]
+    size = height // (first_ref.shape[0] - blocks)
     share = channels // count
     for n in range(height // count):
-        block, row = len(order) + n * count // size, n * count % size
+        block, row = blocks + n * count // size, n * count % size
         other = first_ref[block].reshape(size, channels)[row : row + count]
         total = packed_ref[n * count : (n + 1) * count].astype(F32) + other.astype(F32)
         for q in range(share):
@@ -274,25 +295,33 @@
     row_flops = 2 * rows * block_len * block_len * channels
     column_flops = 2 * cols * count * count * channels
 
-    def pack(own, other, earlier=()):
-        message = shape(2, *own.shape[1:])
-        swapped = permute(after(other, earlier), 1)
-        return list(call(pack_kernel, me, [own, swapped], [message] * chips))
-
+    def pack(own, swapped):
+        return list(call(pack_kernel, me, [own, swapped], [shape(2, *own.shape[1:])] * chips))
+
+    hold = pltpu.VMEM(whole.shape, BF16)
+    halves = [shape(chips, *block)] * 2
+    last = in_turns[-1]
     own, other = call(
-        send_kernel,
-        me,
-        [gate, cotangent, left_factor, values],
-        [shape(chips, 2, *block)] * 2,
-        [pltpu.VMEM(x.shape, BF16) for x in (gate, cotangent, left_factor, values, whole)]
-        + [pltpu.SemaphoreType.DMA((3, max(rows, 2)))],
-        row_flops,
-        unblocked=range(4),
+        product_kernel,
+        me,
+        [gate, cotangent],
+        halves,
+        [hold, hold, pltpu.SemaphoreType.DMA((2, rows))],
+        unblocked=range(2),
         vmem=60,
     )
-    messages = pack(own, other)
+    own_mixed, other_mixed = call(
+        mix_kernel, me, [left_factor, after(values, own)], halves, [hold], row_flops
+    )
+    *messages, mixed_last = call(
+        pack_pairs_kernel,
+        me,
+        [own, permute(other, 1), own_mixed, permute(other_mixed, 1)],
+        [shape(2, 2, *block)] * last + [shape(2, *block)] * 2,
+    )
     other_values = swap_sequences(after(values, messages[0]))
     columns = listed(exchange(messages), in_turns)
+    mixed_last = permute(after(mixed_last, columns[1:]), 2 * last)
     own, other, grad_column = call(
         ordered(column_backward_kernel, in_turns),
         me,
@@ -301,7 +330,8 @@
         [wide, wide],
         column_flops,
     )
-    back = exchange(pack(own, other))
+    back = exchange(pack(own, permute(after(other, mixed_last), 1)))
+    columns[-1] = mixed_last
     packed_right = shape(cols * count * count // channels, channels)
     own, other, right_part = call(
         ordered(column_forward_kernel, in_turns),
@@ -313,23 +343,20 @@
         unblocked=[2],
     )
     back = listed(back, two_far)
-    messages = pack(own, other, back[1 : chips - 2])
-    first = all_far[1]
-    first_second = permute(messages[first], 2 * first)
-    back[-1] = after(back[-1], first_second)
-    half_rows = shape(chips, *block)
+    messages = pack(own, permute(after(other, back[1 : chips - 2]), 1))
+    done = [(t, permute(messages[t], 2 * t)) for t in all_far[1:3]]
+    back[-1] = after(back[-1], [block for _, block in done])
     extra = packed_right.size // math.prod(block)
-    (first_half,) = call(
-        gather_kernel, me, [*back[: chips // 2], right_part], [shape(chips + extra, *block)]
-    )
-    (second_half,) = call(gather_kernel, me, back[chips // 2 :], [half_rows])
-    other_first = swap_sequences(first_half)
-    other_second = swap_sequences(second_half)
-    hold = pltpu.VMEM(whole.shape, BF16)
+    (first_part,) = call(
+        gather_kernel, me, [*back[:-2], right_part], [shape(2 * chips - 4 + extra, *block)]
+    )
+    (second_part,) = call(gather_kernel, me, back[-2:], [shape(4, *block)])
+    other_first = swap_sequences(first_part)
+    other_second = swap_sequences(second_part)
     grad_signal, left_term = call(
         ordered(row_backward_kernel, two_far),
         me,
-        [left_factor, values, first_half, second_half],
+        [left_factor, values, first_part, second_part],
         [by_row, left],
         [hold],
         2 * row_flops,
@@ -344,7 +371,7 @@
     )
     last = all_far[-1]
     messages[last] = after(messages[last], grad_left)
-    second = listed(exchange(messages, first, first_second), all_far)
+    second = listed(exchange(messages, done), all_far)
     output, grad_gate = call(
         ordered(output_kernel, all_far), me, [gate, cotangent, *second], [whole, whole]
     )

time: 128 us -> 131 us (1.023)
  starting transfers between devices: 41.8 us -> 53.1 us
  waiting for transfers between devices: 66.6 us -> 59 us
    ppermute x24 -> x26, starting transfers between devices: 38.1 us -> 49.6 us  [permute(): return lax.ppermute(array, 'seq', [(i, i ^ offset) for i in range(seq)])]
    ppermute x24 -> x26, waiting for transfers between devices: 61.1 us -> 56 us  [permute(): return lax.ppermute(array, 'seq', [(i, i ^ offset) for i in range(seq)])]
    ppermute x3, waiting for transfers between devices: 5.5 us -> 2.98 us  [swap_sequences(): return lax.ppermute(array, 'dp', [(0, 1), (1, 0)])]
    pallas_call x11 -> x12, Pallas kernels: 17.5 us -> 16.6 us  [call(): pl.pallas_call(kernel, out_shape=out_shapes, in_specs=[pl.BlockSpec(memor...]
  transfers between devices with their start and end apart: 27 -> 29, of which waited for: 13 -> 18; matrix products, arithmetic and copies ran while one was open for 0% -> 0% of each run, Pallas kernels for 9% -> 9%
where the time goes in v12:
time: 131 us
  waiting for transfers between devices  59 us (45%)
  starting transfers between devices  53.1 us (41%)
  Pallas kernels  16.6 us (13%)
    ppermute x26, waiting for transfers between devices, permute(): return lax.ppermute(array, 'seq', [(i, i ^ offset) for i in range(seq)])  56 us
    ppermute x26, starting transfers between devices, permute(): return lax.ppermute(array, 'seq', [(i, i ^ offset) for i in range(seq)])  49.6 us
    pallas_call x12, Pallas kernels, call(): pl.pallas_call(kernel, out_shape=out_shapes, in_specs=[pl.BlockSpec(memor...  16.6 us
    ppermute x3, starting transfers between devices, swap_sequences(): return lax.ppermute(array, 'dp', [(0, 1), (1, 0)])  3.54 us
    ppermute x3, waiting for transfers between devices, swap_sequences(): return lax.ppermute(array, 'dp', [(0, 1), (1, 0)])  2.98 us
  transfers between devices with their start and end apart: 29, of which 18 were waited for; matrix products, arithmetic and copies ran while one was open for 0% of the time, Pallas kernels for 9%

profile of v12, /device:TPU:0, one launch (start us, length us, event | category | flops | bytes accessed | tf_op | source)
XLA Modules:
  0.0 130.7 jit_solution(16052441940747127470)
XLA Ops:
  0.6 2.7 %product_kernel.1 = (bf16[8,4,32,256]{3,2,1,0:T(8,128)(2,1)}, bf16[8,4,32,256]{3,2,1,0:T(8,128)(2,1)}) custom-call(s32[1]{0:T(128)} %bitcast.me_ref, bf16[4,16,32,256]{3,2,1,0:T(8,128)(2,1)} %bitcast.10, bf16[4,16,32,256]{3,2,1,0:T(8,128)(2,1)} %bitcast.12), custom_call_target="tpu_custom_call" | custom-call | bytes 3145728 | tf_op jit(solution)/shard_map/product_kernel/pallas_call | solution.py:55
  3.4 0.5 collective-permute-start
  3.9 1.2 copy-done.1
  5.1 0.8 mix_kernel.1
  6.0 1.9 %collective-permute-done.1.refs_3_ = bf16[8,4,32,256]{3,2,1,0:T(8,128)(2,1)S(1)} collective-permute-done((bf16[8,4,32,256]{3,2,1,0:T(8,128)(2,1)S(1)}, bf16[8,4,32,256]{3,2,1,0:T(8,128)(2,1)S(1)}, u32[]{:S(2)}, u32[]{:S(2)}) %collective-permute-start.1) | collective-permute-done | bytes 524320 | tf_op jit(solution)/shard_map/ppermute | solution.py:34
  8.0 3.8 %collective-permute-start.2 = (bf16[2,2,4,32,256]{4,3,2,1,0:T(8,128)(2,1)S(1)}, bf16[2,2,4,32,256]{4,3,2,1,0:T(8,128)(2,1)S(1)}, u32[]{:S(2)}, u32[]{:S(2)}) collective-permute-start(bf16[2,2,4,32,256]{4,3,2,1,0:T(8,128)(2,1)S(1)} %get-tuple-element.59), channel_id=1, source_target_pairs={{0,8},{1,9},{2,10},{3,11},{4,12},{5,13},{6,14},{7,15},{8,0},{9,1},... | collective-permute-start | bytes 786440 | tf_op jit(solution)/shard_map/ppermute | solution.py:34
  11.8 1.5 %collective-permute-start.3 = (bf16[2,2,4,32,256]{4,3,2,1,0:T(8,128)(2,1)S(1)}, bf16[2,2,4,32,256]{4,3,2,1,0:T(8,128)(2,1)S(1)}, u32[]{:S(2)}, u32[]{:S(2)}) collective-permute-start(bf16[2,2,4,32,256]{4,3,2,1,0:T(8,128)(2,1)S(1)} %get-tuple-element.60), channel_id=1, source_target_pairs={{0,2},{1,3},{2,0},{3,1},{4,6},{5,7},{6,4},{7,5},{8,10},{9,11},{10,... | collective-permute-start | bytes 786440 | tf_op jit(solution)/shard_map/ppermute | solution.py:34
  13.3 1.3 collective-permute-start.8
  14.6 1.5 %collective-permute-start.9 = (bf16[4,512,256]{2,1,0:T(8,128)(2,1)S(1)}, bf16[4,512,256]{2,1,0:T(8,128)(2,1)S(1)}, u32[]{:S(2)}, u32[]{:S(2)}) collective-permute-start(bf16[4,512,256]{2,1,0:T(8,128)(2,1)S(1)} %bitcast.8), channel_id=1, source_target_pairs={{0,16},{16,0},{1,17},{17,1},{2,18},{18,2},{3,19},{19,3},{4,20},{20... | collective-permute-start | bytes 3145736 | tf_op jit(solution)/shard_map/ppermute | solution.py:17
  16.1 2.5 %collective-permute-start.4 = (bf16[2,2,4,32,256]{4,3,2,1,0:T(8,128)(2,1)S(1)}, bf16[2,2,4,32,256]{4,3,2,1,0:T(8,128)(2,1)S(1)}, u32[]{:S(2)}, u32[]{:S(2)}) collective-permute-start(bf16[2,2,4,32,256]{4,3,2,1,0:T(8,128)(2,1)S(1)} %get-tuple-element.61), channel_id=1, source_target_pairs={{0,12},{1,13},{2,14},{3,15},{4,8},{5,9},{6,10},{7,11},{8,4},{9,5},... | collective-permute-start | bytes 786440 | tf_op jit(solution)/shard_map/ppermute | solution.py:34
  18.6 5.5 %collective-permute-done.8.refs_7_ = bf16[2,4,32,256]{3,2,1,0:T(8,128)(2,1)S(1)} collective-permute-done((bf16[2,4,32,256]{3,2,1,0:T(8,128)(2,1)S(1)}, bf16[2,4,32,256]{3,2,1,0:T(8,128)(2,1)S(1)}, u32[]{:S(2)}, u32[]{:S(2)}) %collective-permute-start.8) | collective-permute-done | bytes 131104 | tf_op jit(solution)/shard_map/ppermute | solution.py:34
  24.1 13.5 %collective-permute-start.5 = (bf16[2,2,4,32,256]{4,3,2,1,0:T(8,128)(2,1)S(1)}, bf16[2,2,4,32,256]{4,3,2,1,0:T(8,128)(2,1)S(1)}, u32[]{:S(2)}, u32[]{:S(2)}) collective-permute-start(bf16[2,2,4,32,256]{4,3,2,1,0:T(8,128)(2,1)S(1)} %get-tuple-element.62), channel_id=1, source_target_pairs={{0,4},{1,5},{2,6},{3,7},{4,0},{5,1},{6,2},{7,3},{8,12},{9,13},{10,... | collective-permute-start | bytes 786440 | tf_op jit(solution)/shard_map/ppermute | solution.py:34
  37.6 1.5 %collective-permute-start.6 = (bf16[2,2,4,32,256]{4,3,2,1,0:T(8,128)(2,1)S(1)}, bf16[2,2,4,32,256]{4,3,2,1,0:T(8,128)(2,1)S(1)}, u32[]{:S(2)}, u32[]{:S(2)}) collective-permute-start(bf16[2,2,4,32,256]{4,3,2,1,0:T(8,128)(2,1)S(1)} %get-tuple-element.63), channel_id=1, source_target_pairs={{0,10},{1,11},{2,8},{3,9},{4,14},{5,15},{6,12},{7,13},{8,2},{9,3},... | collective-permute-start | bytes 786440 | tf_op jit(solution)/shard_map/ppermute | solution.py:34
  39.1 3.0 %collective-permute-start.7 = (bf16[2,2,4,32,256]{4,3,2,1,0:T(8,128)(2,1)S(1)}, bf16[2,2,4,32,256]{4,3,2,1,0:T(8,128)(2,1)S(1)}, u32[]{:S(2)}, u32[]{:S(2)}) collective-permute-start(bf16[2,2,4,32,256]{4,3,2,1,0:T(8,128)(2,1)S(1)} %get-tuple-element.64), channel_id=1, source_target_pairs={{0,6},{1,7},{2,4},{3,5},{4,2},{5,3},{6,0},{7,1},{8,14},{9,15},{10,... | collective-permute-start | bytes 786440 | tf_op jit(solution)/shard_map/ppermute | solution.py:34
  42.1 8.4 %collective-permute-done.5.refs_4_ = bf16[2,2,4,32,256]{4,3,2,1,0:T(8,128)(2,1)S(1)} collective-permute-done((bf16[2,2,4,32,256]{4,3,2,1,0:T(8,128)(2,1)S(1)}, bf16[2,2,4,32,256]{4,3,2,1,0:T(8,128)(2,1)S(1)}, u32[]{:S(2)}, u32[]{:S(2)}) %collective-permute-start.5) | collective-permute-done | bytes 262176 | tf_op jit(solution)/shard_map/ppermute | solution.py:34
  50.5 2.8 %collective-permute-done.6.refs_5_ = bf16[2,2,4,32,256]{4,3,2,1,0:T(8,128)(2,1)S(1)} collective-permute-done((bf16[2,2,4,32,256]{4,3,2,1,0:T(8,128)(2,1)S(1)}, bf16[2,2,4,32,256]{4,3,2,1,0:T(8,128)(2,1)S(1)}, u32[]{:S(2)}, u32[]{:S(2)}) %collective-permute-start.6) | collective-permute-done | bytes 262176 | tf_op jit(solution)/shard_map/ppermute | solution.py:34
  53.3 2.8 %collective-permute-done.7.refs_6_ = bf16[2,2,4,32,256]{4,3,2,1,0:T(8,128)(2,1)S(1)} collective-permute-done((bf16[2,2,4,32,256]{4,3,2,1,0:T(8,128)(2,1)S(1)}, bf16[2,2,4,32,256]{4,3,2,1,0:T(8,128)(2,1)S(1)}, u32[]{:S(2)}, u32[]{:S(2)}) %collective-permute-start.7) | collective-permute-done | bytes 262176 | tf_op jit(solution)/shard_map/ppermute | solution.py:34
  56.1 3.2 %collective-permute-start.10 = (bf16[2,4,32,256]{3,2,1,0:T(8,128)(2,1)S(1)}, bf16[2,4,32,256]{3,2,1,0:T(8,128)(2,1)S(1)}, u32[]{:S(2)}, u32[]{:S(2)}) collective-permute-start(bf16[2,4,32,256]{3,2,1,0:T(8,128)(2,1)S(1)} %get-tuple-element.69), channel_id=1, source_target_pairs={{0,14},{1,15},{2,12},{3,13},{4,10},{5,11},{6,8},{7,9},{8,6},{9,7},... | collective-permute-start | bytes 393224 | tf_op jit(solution)/shard_map/ppermute | solution.py:34
  59.2 3.0 %column_backward_kernel.1 = (bf16[8,4,32,256]{3,2,1,0:T(8,128)(2,1)S(1)}, bf16[8,4,32,256]{3,2,1,0:T(8,128)(2,1)S(1)}, bf16[32,64,256]{2,1,0:T(8,128)(2,1)S(1)}) custom-call(s32[1]{0:T(128)} %bitcast.me_ref, bf16[32,64,64]{2,1,0:T(8,128)(2,1)S(1)} %copy-done.5, bf16[2,2,4,32,256]{4,3,2,1,0:T(8,128)(2,1)S(1)} %get-tuple-element.58.refs_0_, ...), custom_call_target="tpu_custom_call" | custom-call | flops 67108864 | bytes 4325376 | tf_op jit(solution)/shard_map/column_backward_kernel/pallas_call | solution.py:55
  62.2 1.6 %collective-permute-done.10.refs_7_ = bf16[2,4,32,256]{3,2,1,0:T(8,128)(2,1)S(1)} collective-permute-done((bf16[2,4,32,256]{3,2,1,0:T(8,128)(2,1)S(1)}, bf16[2,4,32,256]{3,2,1,0:T(8,128)(2,1)S(1)}, u32[]{:S(2)}, u32[]{:S(2)}) %collective-permute-start.10) | collective-permute-done | bytes 131104 | tf_op jit(solution)/shard_map/ppermute | solution.py:34
  63.8 1.9 %collective-permute-done.11.other_ref = bf16[8,4,32,256]{3,2,1,0:T(8,128)(2,1)S(1)} collective-permute-done((bf16[8,4,32,256]{3,2,1,0:T(8,128)(2,1)S(1)}, bf16[8,4,32,256]{3,2,1,0:T(8,128)(2,1)S(1)}, u32[]{:S(2)}, u32[]{:S(2)}) %collective-permute-start.11) | collective-permute-done | bytes 524320 | tf_op jit(solution)/shard_map/ppermute | solution.py:34
  65.8 3.1 %collective-permute-start.12 = (bf16[2,4,32,256]{3,2,1,0:T(8,128)(2,1)S(1)}, bf16[2,4,32,256]{3,2,1,0:T(8,128)(2,1)S(1)}, u32[]{:S(2)}, u32[]{:S(2)}) collective-permute-start(bf16[2,4,32,256]{3,2,1,0:T(8,128)(2,1)S(1)} %get-tuple-element.75), channel_id=1, source_target_pairs={{0,8},{1,9},{2,10},{3,11},{4,12},{5,13},{6,14},{7,15},{8,0},{9,1},... | collective-permute-start | bytes 393224 | tf_op jit(solution)/shard_map/ppermute | solution.py:34
  68.9 1.3 %collective-permute-start.13 = (bf16[2,4,32,256]{3,2,1,0:T(8,128)(2,1)S(1)}, bf16[2,4,32,256]{3,2,1,0:T(8,128)(2,1)S(1)}, u32[]{:S(2)}, u32[]{:S(2)}) collective-permute-start(bf16[2,4,32,256]{3,2,1,0:T(8,128)(2,1)S(1)} %get-tuple-element.76), channel_id=1, source_target_pairs={{0,12},{1,13},{2,14},{3,15},{4,8},{5,9},{6,10},{7,11},{8,4},{9,5},... | collective-permute-start | bytes 393224 | tf_op jit(solution)/shard_map/ppermute | solution.py:34
  70.2 1.1 collective-permute-start.14
  71.4 0.4 collective-permute-start.15
  71.8 1.9 %collective-permute-start.16 = (bf16[2,4,32,256]{3,2,1,0:T(8,128)(2,1)S(1)}, bf16[2,4,32,256]{3,2,1,0:T(8,128)(2,1)S(1)}, u32[]{:S(2)}, u32[]{:S(2)}) collective-permute-start(bf16[2,4,32,256]{3,2,1,0:T(8,128)(2,1)S(1)} %get-tuple-element.79), channel_id=1, source_target_pairs={{0,6},{1,7},{2,4},{3,5},{4,2},{5,3},{6,0},{7,1},{8,14},{9,15},{10,... | collective-permute-start | bytes 393224 | tf_op jit(solution)/shard_map/ppermute | solution.py:34
  73.7 3.3 %column_forward_kernel.1 = (bf16[8,4,32,256]{3,2,1,0:T(8,128)(2,1)S(1)}, bf16[8,4,32,256]{3,2,1,0:T(8,128)(2,1)S(1)}, bf16[512,256]{1,0:T(8,128)(2,1)S(1)}) custom-call(s32[1]{0:T(128)} %bitcast.me_ref, bf16[32,64,64]{2,1,0:T(8,128)(2,1)S(1)} %copy-done.5, bf16[32,64,256]{2,1,0:T(8,128)(2,1)S(1)} %get-tuple-element.66.grad_ref, ...), custom_call_target="tpu_custom_call" | custom-call | flops 134217728 | bytes 5636096 | tf_op jit(solution)/shard_map/column_forward_kernel/pallas_call | solution.py:55
  77.1 1.8 %collective-permute-done.12.refs_1_ = bf16[2,4,32,256]{3,2,1,0:T(8,128)(2,1)S(1)} collective-permute-done((bf16[2,4,32,256]{3,2,1,0:T(8,128)(2,1)S(1)}, bf16[2,4,32,256]{3,2,1,0:T(8,128)(2,1)S(1)}, u32[]{:S(2)}, u32[]{:S(2)}) %collective-permute-start.12) | collective-permute-done | bytes 131104 | tf_op jit(solution)/shard_map/ppermute | solution.py:34
  78.9 2.4 %collective-permute-done.15.refs_4_ = bf16[2,4,32,256]{3,2,1,0:T(8,128)(2,1)S(1)} collective-permute-done((bf16[2,4,32,256]{3,2,1,0:T(8,128)(2,1)S(1)}, bf16[2,4,32,256]{3,2,1,0:T(8,128)(2,1)S(1)}, u32[]{:S(2)}, u32[]{:S(2)}) %collective-permute-start.15) | collective-permute-done | bytes 131104 | tf_op jit(solution)/shard_map/ppermute | solution.py:34
  81.3 3.4 %collective-permute-done.16.refs_5_ = bf16[2,4,32,256]{3,2,1,0:T(8,128)(2,1)S(1)} collective-permute-done((bf16[2,4,32,256]{3,2,1,0:T(8,128)(2,1)S(1)}, bf16[2,4,32,256]{3,2,1,0:T(8,128)(2,1)S(1)}, u32[]{:S(2)}, u32[]{:S(2)}) %collective-permute-start.16) | collective-permute-done | bytes 131104 | tf_op jit(solution)/shard_map/ppermute | solution.py:34
  84.8 1.5 %collective-permute-start.26 = (bf16[16,4,32,256]{3,2,1,0:T(8,128)(2,1)S(1)}, bf16[16,4,32,256]{3,2,1,0:T(8,128)(2,1)S(1)}, u32[]{:S(2)}, u32[]{:S(2)}) collective-permute-start(bf16[16,4,32,256]{3,2,1,0:T(8,128)(2,1)S(1)} %gather_kernel.2.first_ref), channel_id=1, source_target_pairs={{0,16},{16,0},{1,17},{17,1},{2,18},{18,2},{3,19},{19,3},{4,20},{20... | collective-permute-start | bytes 3145736 | tf_op jit(solution)/shard_map/ppermute | solution.py:17
  86.3 1.8 %collective-permute-start.25 = (bf16[2,4,32,256]{3,2,1,0:T(8,128)(2,1)S(1)}, bf16[2,4,32,256]{3,2,1,0:T(8,128)(2,1)S(1)}, u32[]{:S(2)}, u32[]{:S(2)}) collective-permute-start(bf16[2,4,32,256]{3,2,1,0:T(8,128)(2,1)S(1)} %get-tuple-element.92), channel_id=1, source_target_pairs={{0,14},{1,15},{2,12},{3,13},{4,10},{5,11},{6,8},{7,9},{8,6},{9,7},... | collective-permute-start | bytes 393224 | tf_op jit(solution)/shard_map/ppermute | solution.py:34
  88.4 2.3 %collective-permute-start.19 = (bf16[2,4,32,256]{3,2,1,0:T(8,128)(2,1)S(1)}, bf16[2,4,32,256]{3,2,1,0:T(8,128)(2,1)S(1)}, u32[]{:S(2)}, u32[]{:S(2)}) collective-permute-start(bf16[2,4,32,256]{3,2,1,0:T(8,128)(2,1)S(1)} %get-tuple-element.83), channel_id=1, source_target_pairs={{0,12},{1,13},{2,14},{3,15},{4,8},{5,9},{6,10},{7,11},{8,4},{9,5},... | collective-permute-start | bytes 393224 | tf_op jit(solution)/shard_map/ppermute | solution.py:34
  90.7 2.5 %collective-permute-start.24 = (bf16[2,4,32,256]{3,2,1,0:T(8,128)(2,1)S(1)}, bf16[2,4,32,256]{3,2,1,0:T(8,128)(2,1)S(1)}, u32[]{:S(2)}, u32[]{:S(2)}) collective-permute-start(bf16[2,4,32,256]{3,2,1,0:T(8,128)(2,1)S(1)} %get-tuple-element.91), channel_id=1, source_target_pairs={{0,10},{1,11},{2,8},{3,9},{4,14},{5,15},{6,12},{7,13},{8,2},{9,3},... | collective-permute-start | bytes 393224 | tf_op jit(solution)/shard_map/ppermute | solution.py:34
  93.2 2.2 %collective-permute-done.25.refs_1_ = bf16[2,4,32,256]{3,2,1,0:T(8,128)(2,1)S(1)} collective-permute-done((bf16[2,4,32,256]{3,2,1,0:T(8,128)(2,1)S(1)}, bf16[2,4,32,256]{3,2,1,0:T(8,128)(2,1)S(1)}, u32[]{:S(2)}, u32[]{:S(2)}) %collective-permute-start.25) | collective-permute-done | bytes 131104 | tf_op jit(solution)/shard_map/ppermute | solution.py:34
  95.4 9.8 %collective-permute-done.18.refs_1_ = bf16[2,4,32,256]{3,2,1,0:T(8,128)(2,1)S(1)} collective-permute-done((bf16[2,4,32,256]{3,2,1,0:T(8,128)(2,1)S(1)}, bf16[2,4,32,256]{3,2,1,0:T(8,128)(2,1)S(1)}, u32[]{:S(2)}, u32[]{:S(2)}) %collective-permute-start.18) | collective-permute-done | bytes 131104 | tf_op jit(solution)/shard_map/ppermute | solution.py:34
  105.2 7.0 %collective-permute-done.24.refs_0_ = bf16[2,4,32,256]{3,2,1,0:T(8,128)(2,1)S(1)} collective-permute-done((bf16[2,4,32,256]{3,2,1,0:T(8,128)(2,1)S(1)}, bf16[2,4,32,256]{3,2,1,0:T(8,128)(2,1)S(1)}, u32[]{:S(2)}, u32[]{:S(2)}) %collective-permute-start.24) | collective-permute-done | bytes 131104 | tf_op jit(solution)/shard_map/ppermute | solution.py:34
  112.2 0.6 collective-permute-start.27
  112.8 1.5 %collective-permute-start.21 = (bf16[2,4,32,256]{3,2,1,0:T(8,128)(2,1)S(1)}, bf16[2,4,32,256]{3,2,1,0:T(8,128)(2,1)S(1)}, u32[]{:S(2)}, u32[]{:S(2)}) collective-permute-start(bf16[2,4,32,256]{3,2,1,0:T(8,128)(2,1)S(1)} %get-tuple-element.85), channel_id=1, source_target_pairs={{0,14},{1,15},{2,12},{3,13},{4,10},{5,11},{6,8},{7,9},{8,6},{9,7},... | collective-permute-start | bytes 393224 | tf_op jit(solution)/shard_map/ppermute | solution.py:34
  114.2 0.7 collective-permute-start.22
  114.9 2.3 %row_backward_kernel.1 = (bf16[4,512,256]{2,1,0:T(8,128)(2,1)}, bf16[4,512,512]{2,1,0:T(8,128)(2,1)S(1)}) custom-call(s32[1]{0:T(128)} %bitcast.me_ref, bf16[4,512,512]{2,1,0:T(8,128)(2,1)S(1)} %copy-done, bf16[4,512,256]{2,1,0:T(8,128)(2,1)S(1)} %bitcast.9, bf16[16,4,32,256]{3,2,1,0:T(8,128)(2,1)S(1)} %gather_kernel.2.first_ref, ...), custom_call_target="tpu_custom_call" | custom-call | flops 1073741824 | bytes 7602176 | tf_op jit(solution)/shard_map/row_backward_kernel/pallas_call | solution.py:55
  117.2 3.0 %collective-permute-done.27.second_ref = bf16[4,4,32,256]{3,2,1,0:T(8,128)(2,1)S(1)} collective-permute-done((bf16[4,4,32,256]{3,2,1,0:T(8,128)(2,1)S(1)}, bf16[4,4,32,256]{3,2,1,0:T(8,128)(2,1)S(1)}, u32[]{:S(2)}, u32[]{:S(2)}) %collective-permute-start.27) | collective-permute-done | bytes 262176 | tf_op jit(solution)/shard_map/ppermute | solution.py:17
  120.2 2.4 %factor_sum_kernel.1 = (bf16[4,512,512]{2,1,0:T(8,128)(2,1)}, bf16[32,64,64]{2,1,0:T(8,128)(2,1)}) custom-call(s32[1]{0:T(128)} %bitcast.me_ref, bf16[4,512,512]{2,1,0:T(8,128)(2,1)S(1)} %get-tuple-element.94.term_ref, bf16[4,512,256]{2,1,0:T(8,128)(2,1)S(1)} %collective-permute-done.9.after_ref.values_ref, ...), custom_call_target="tpu_custom_call" | custom-call | flops 536870912 | bytes 7077888 | tf_op jit(solution)/shard_map/factor_sum_kernel/pallas_call | solution.py:55
  122.6 1.9 %collective-permute-start.28 = (bf16[2,4,32,256]{3,2,1,0:T(8,128)(2,1)S(1)}, bf16[2,4,32,256]{3,2,1,0:T(8,128)(2,1)S(1)}, u32[]{:S(2)}, u32[]{:S(2)}) collective-permute-start(bf16[2,4,32,256]{3,2,1,0:T(8,128)(2,1)S(1)} %get-tuple-element.96), channel_id=1, source_target_pairs={{0,6},{1,7},{2,4},{3,5},{4,2},{5,3},{6,0},{7,1},{8,14},{9,15},{10,... | collective-permute-start | bytes 393224 | tf_op jit(solution)/shard_map/ppermute | solution.py:34
  124.5 0.2 collective-permute-done.22.refs_5_
  124.7 1.6 %collective-permute-done.23.refs_6_ = bf16[2,4,32,256]{3,2,1,0:T(8,128)(2,1)S(1)} collective-permute-done((bf16[2,4,32,256]{3,2,1,0:T(8,128)(2,1)S(1)}, bf16[2,4,32,256]{3,2,1,0:T(8,128)(2,1)S(1)}, u32[]{:S(2)}, u32[]{:S(2)}) %collective-permute-start.23) | collective-permute-done | bytes 131104 | tf_op jit(solution)/shard_map/ppermute | solution.py:34
  126.3 2.6 %collective-permute-done.28.refs_7_ = bf16[2,4,32,256]{3,2,1,0:T(8,128)(2,1)S(1)} collective-permute-done((bf16[2,4,32,256]{3,2,1,0:T(8,128)(2,1)S(1)}, bf16[2,4,32,256]{3,2,1,0:T(8,128)(2,1)S(1)}, u32[]{:S(2)}, u32[]{:S(2)}) %collective-permute-start.28) | collective-permute-done | bytes 131104 | tf_op jit(solution)/shard_map/ppermute | solution.py:34
  128.9 1.8 %output_kernel.1 = (bf16[4,16,32,256]{3,2,1,0:T(8,128)(2,1)}, bf16[4,16,32,256]{3,2,1,0:T(8,128)(2,1)}) custom-call(s32[1]{0:T(128)} %bitcast.me_ref, bf16[4,16,32,256]{3,2,1,0:T(8,128)(2,1)S(1)} %bitcast.11, bf16[4,16,32,256]{3,2,1,0:T(8,128)(2,1)S(1)} %bitcast.13, bf16[2,4,32,256]{3,2,1,0:T(8,128)(2,1)S(1)} %get-tuple-element.81.refs_0_, ...), custom_call_target="tpu_custom_call" | custom-call | bytes 5242880 | tf_op jit(solution)/shard_map/output_kernel/pallas_call | solution.py:55
  (36 shorter events, 0.7 us)
Async XLA Ops:
  0.6 3.3 %copy-start = (bf16[4,512,512]{2,1,0:T(8,128)(2,1)S(1)}, bf16[4,512,512]{2,1,0:T(8,128)(2,1)}, u32[]{:S(2)}) copy-start(bf16[4,512,512]{2,1,0:T(8,128)(2,1)} %left_ref.3) | copy-start | bytes 6291460
  3.4 2.7 %collective-permute-start = (bf16[8,4,32,256]{3,2,1,0:T(8,128)(2,1)}, bf16[8,4,32,256]{3,2,1,0:T(8,128)(2,1)S(1)}, u32[]{:S(2)}, u32[]{:S(2)}) collective-permute-start(bf16[8,4,32,256]{3,2,1,0:T(8,128)(2,1)} %get-tuple-element.54), channel_id=1, source_target_pairs={{0,1},{1,0},{2,3},{3,2},{4,5},{5,4},{6,7},{7,6},{8,9},{9,8},{10,11... | collective-permute-start | bytes 1572872 | tf_op jit(solution)/shard_map/ppermute | solution.py:34
  3.9 1.2 copy-start.1
  5.1 2.8 %copy-start.6 = (bf16[8,4,32,256]{3,2,1,0:T(8,128)(2,1)S(1)}, bf16[8,4,32,256]{3,2,1,0:T(8,128)(2,1)}, u32[]{:S(2)}) copy-start(bf16[8,4,32,256]{3,2,1,0:T(8,128)(2,1)} %get-tuple-element.53.refs_0_) | copy-start | bytes 1572868
  5.1 9.5 %copy-start.2 = (bf16[1,2048,256]{2,1,0:T(8,128)(2,1)S(1)}, bf16[1,2048,256]{2,1,0:T(8,128)(2,1)}, u32[]{:S(2)}) copy-start(bf16[1,2048,256]{2,1,0:T(8,128)(2,1)} %param.5) | copy-start | bytes 3145732
  5.1 54.1 %copy-start.5 = (bf16[32,64,64]{2,1,0:T(8,128)(2,1)S(1)}, bf16[32,64,64]{2,1,0:T(8,128)(2,1)}, u32[]{:S(2)}) copy-start(bf16[32,64,64]{2,1,0:T(8,128)(2,1)} %right_ref.3) | copy-start | bytes 786436
  5.9 2.0 %collective-permute-start.1 = (bf16[8,4,32,256]{3,2,1,0:T(8,128)(2,1)S(1)}, bf16[8,4,32,256]{3,2,1,0:T(8,128)(2,1)S(1)}, u32[]{:S(2)}, u32[]{:S(2)}) collective-permute-start(bf16[8,4,32,256]{3,2,1,0:T(8,128)(2,1)S(1)} %get-tuple-element.57), channel_id=1, source_target_pairs={{0,1},{1,0},{2,3},{3,2},{4,5},{5,4},{6,7},{7,6},{8,9},{9,8},{10,11... | collective-permute-start | bytes 1572872 | tf_op jit(solution)/shard_map/ppermute | solution.py:34
  8.0 29.6 %collective-permute-start.2 = (bf16[2,2,4,32,256]{4,3,2,1,0:T(8,128)(2,1)S(1)}, bf16[2,2,4,32,256]{4,3,2,1,0:T(8,128)(2,1)S(1)}, u32[]{:S(2)}, u32[]{:S(2)}) collective-permute-start(bf16[2,2,4,32,256]{4,3,2,1,0:T(8,128)(2,1)S(1)} %get-tuple-element.59), channel_id=1, source_target_pairs={{0,8},{1,9},{2,10},{3,11},{4,12},{5,13},{6,14},{7,15},{8,0},{9,1},... | collective-permute-start | bytes 786440 | tf_op jit(solution)/shard_map/ppermute | solution.py:34
  11.8 27.3 %collective-permute-start.3 = (bf16[2,2,4,32,256]{4,3,2,1,0:T(8,128)(2,1)S(1)}, bf16[2,2,4,32,256]{4,3,2,1,0:T(8,128)(2,1)S(1)}, u32[]{:S(2)}, u32[]{:S(2)}) collective-permute-start(bf16[2,2,4,32,256]{4,3,2,1,0:T(8,128)(2,1)S(1)} %get-tuple-element.60), channel_id=1, source_target_pairs={{0,2},{1,3},{2,0},{3,1},{4,6},{5,7},{6,4},{7,5},{8,10},{9,11},{10,... | collective-permute-start | bytes 786440 | tf_op jit(solution)/shard_map/ppermute | solution.py:34
  13.3 10.8 %collective-permute-start.8 = (bf16[2,4,32,256]{3,2,1,0:T(8,128)(2,1)S(1)}, bf16[2,4,32,256]{3,2,1,0:T(8,128)(2,1)S(1)}, u32[]{:S(2)}, u32[]{:S(2)}) collective-permute-start(bf16[2,4,32,256]{3,2,1,0:T(8,128)(2,1)S(1)} %get-tuple-element.65), channel_id=1, source_target_pairs={{0,14},{1,15},{2,12},{3,13},{4,10},{5,11},{6,8},{7,9},{8,6},{9,7},... | collective-permute-start | bytes 393224 | tf_op jit(solution)/shard_map/ppermute | solution.py:34
  14.6 57.2 %collective-permute-start.9 = (bf16[4,512,256]{2,1,0:T(8,128)(2,1)S(1)}, bf16[4,512,256]{2,1,0:T(8,128)(2,1)S(1)}, u32[]{:S(2)}, u32[]{:S(2)}) collective-permute-start(bf16[4,512,256]{2,1,0:T(8,128)(2,1)S(1)} %bitcast.8), channel_id=1, source_target_pairs={{0,16},{16,0},{1,17},{17,1},{2,18},{18,2},{3,19},{19,3},{4,20},{20... | collective-permute-start | bytes 3145736 | tf_op jit(solution)/shard_map/ppermute | solution.py:17
  16.1 26.0 %collective-permute-start.4 = (bf16[2,2,4,32,256]{4,3,2,1,0:T(8,128)(2,1)S(1)}, bf16[2,2,4,32,256]{4,3,2,1,0:T(8,128)(2,1)S(1)}, u32[]{:S(2)}, u32[]{:S(2)}) collective-permute-start(bf16[2,2,4,32,256]{4,3,2,1,0:T(8,128)(2,1)S(1)} %get-tuple-element.61), channel_id=1, source_target_pairs={{0,12},{1,13},{2,14},{3,15},{4,8},{5,9},{6,10},{7,11},{8,4},{9,5},... | collective-permute-start | bytes 786440 | tf_op jit(solution)/shard_map/ppermute | solution.py:34
  24.1 26.3 %collective-permute-start.5 = (bf16[2,2,4,32,256]{4,3,2,1,0:T(8,128)(2,1)S(1)}, bf16[2,2,4,32,256]{4,3,2,1,0:T(8,128)(2,1)S(1)}, u32[]{:S(2)}, u32[]{:S(2)}) collective-permute-start(bf16[2,2,4,32,256]{4,3,2,1,0:T(8,128)(2,1)S(1)} %get-tuple-element.62), channel_id=1, source_target_pairs={{0,4},{1,5},{2,6},{3,7},{4,0},{5,1},{6,2},{7,3},{8,12},{9,13},{10,... | collective-permute-start | bytes 786440 | tf_op jit(solution)/shard_map/ppermute | solution.py:34
  37.6 15.6 %collective-permute-start.6 = (bf16[2,2,4,32,256]{4,3,2,1,0:T(8,128)(2,1)S(1)}, bf16[2,2,4,32,256]{4,3,2,1,0:T(8,128)(2,1)S(1)}, u32[]{:S(2)}, u32[]{:S(2)}) collective-permute-start(bf16[2,2,4,32,256]{4,3,2,1,0:T(8,128)(2,1)S(1)} %get-tuple-element.63), channel_id=1, source_target_pairs={{0,10},{1,11},{2,8},{3,9},{4,14},{5,15},{6,12},{7,13},{8,2},{9,3},... | collective-permute-start | bytes 786440 | tf_op jit(solution)/shard_map/ppermute | solution.py:34
  39.1 17.0 %collective-permute-start.7 = (bf16[2,2,4,32,256]{4,3,2,1,0:T(8,128)(2,1)S(1)}, bf16[2,2,4,32,256]{4,3,2,1,0:T(8,128)(2,1)S(1)}, u32[]{:S(2)}, u32[]{:S(2)}) collective-permute-start(bf16[2,2,4,32,256]{4,3,2,1,0:T(8,128)(2,1)S(1)} %get-tuple-element.64), channel_id=1, source_target_pairs={{0,6},{1,7},{2,4},{3,5},{4,2},{5,3},{6,0},{7,1},{8,14},{9,15},{10,... | collective-permute-start | bytes 786440 | tf_op jit(solution)/shard_map/ppermute | solution.py:34
  56.1 7.8 %collective-permute-start.10 = (bf16[2,4,32,256]{3,2,1,0:T(8,128)(2,1)S(1)}, bf16[2,4,32,256]{3,2,1,0:T(8,128)(2,1)S(1)}, u32[]{:S(2)}, u32[]{:S(2)}) collective-permute-start(bf16[2,4,32,256]{3,2,1,0:T(8,128)(2,1)S(1)} %get-tuple-element.69), channel_id=1, source_target_pairs={{0,14},{1,15},{2,12},{3,13},{4,10},{5,11},{6,8},{7,9},{8,6},{9,7},... | collective-permute-start | bytes 393224 | tf_op jit(solution)/shard_map/ppermute | solution.py:34
  63.8 1.9 %collective-permute-start.11 = (bf16[8,4,32,256]{3,2,1,0:T(8,128)(2,1)S(1)}, bf16[8,4,32,256]{3,2,1,0:T(8,128)(2,1)S(1)}, u32[]{:S(2)}, u32[]{:S(2)}) collective-permute-start(bf16[8,4,32,256]{3,2,1,0:T(8,128)(2,1)S(1)} %get-tuple-element.74), channel_id=1, source_target_pairs={{0,1},{1,0},{2,3},{3,2},{4,5},{5,4},{6,7},{7,6},{8,9},{9,8},{10,11... | collective-permute-start | bytes 1572872 | tf_op jit(solution)/shard_map/ppermute | solution.py:34
  65.8 13.0 %collective-permute-start.12 = (bf16[2,4,32,256]{3,2,1,0:T(8,128)(2,1)S(1)}, bf16[2,4,32,256]{3,2,1,0:T(8,128)(2,1)S(1)}, u32[]{:S(2)}, u32[]{:S(2)}) collective-permute-start(bf16[2,4,32,256]{3,2,1,0:T(8,128)(2,1)S(1)} %get-tuple-element.75), channel_id=1, source_target_pairs={{0,8},{1,9},{2,10},{3,11},{4,12},{5,13},{6,14},{7,15},{8,0},{9,1},... | collective-permute-start | bytes 393224 | tf_op jit(solution)/shard_map/ppermute | solution.py:34
  68.9 9.9 %collective-permute-start.13 = (bf16[2,4,32,256]{3,2,1,0:T(8,128)(2,1)S(1)}, bf16[2,4,32,256]{3,2,1,0:T(8,128)(2,1)S(1)}, u32[]{:S(2)}, u32[]{:S(2)}) collective-permute-start(bf16[2,4,32,256]{3,2,1,0:T(8,128)(2,1)S(1)} %get-tuple-element.76), channel_id=1, source_target_pairs={{0,12},{1,13},{2,14},{3,15},{4,8},{5,9},{6,10},{7,11},{8,4},{9,5},... | collective-permute-start | bytes 393224 | tf_op jit(solution)/shard_map/ppermute | solution.py:34
  70.2 8.6 %collective-permute-start.14 = (bf16[2,4,32,256]{3,2,1,0:T(8,128)(2,1)S(1)}, bf16[2,4,32,256]{3,2,1,0:T(8,128)(2,1)S(1)}, u32[]{:S(2)}, u32[]{:S(2)}) collective-permute-start(bf16[2,4,32,256]{3,2,1,0:T(8,128)(2,1)S(1)} %get-tuple-element.77), channel_id=1, source_target_pairs={{0,2},{1,3},{2,0},{3,1},{4,6},{5,7},{6,4},{7,5},{8,10},{9,11},{10,... | collective-permute-start | bytes 393224 | tf_op jit(solution)/shard_map/ppermute | solution.py:34
  71.4 9.9 %collective-permute-start.15 = (bf16[2,4,32,256]{3,2,1,0:T(8,128)(2,1)S(1)}, bf16[2,4,32,256]{3,2,1,0:T(8,128)(2,1)S(1)}, u32[]{:S(2)}, u32[]{:S(2)}) collective-permute-start(bf16[2,4,32,256]{3,2,1,0:T(8,128)(2,1)S(1)} %get-tuple-element.78), channel_id=1, source_target_pairs={{0,4},{1,5},{2,6},{3,7},{4,0},{5,1},{6,2},{7,3},{8,12},{9,13},{10,... | collective-permute-start | bytes 393224 | tf_op jit(solution)/shard_map/ppermute | solution.py:34
  71.8 12.9 %collective-permute-start.16 = (bf16[2,4,32,256]{3,2,1,0:T(8,128)(2,1)S(1)}, bf16[2,4,32,256]{3,2,1,0:T(8,128)(2,1)S(1)}, u32[]{:S(2)}, u32[]{:S(2)}) collective-permute-start(bf16[2,4,32,256]{3,2,1,0:T(8,128)(2,1)S(1)} %get-tuple-element.79), channel_id=1, source_target_pairs={{0,6},{1,7},{2,4},{3,5},{4,2},{5,3},{6,0},{7,1},{8,14},{9,15},{10,... | collective-permute-start | bytes 393224 | tf_op jit(solution)/shard_map/ppermute | solution.py:34
  84.8 35.4 %collective-permute-start.26 = (bf16[16,4,32,256]{3,2,1,0:T(8,128)(2,1)S(1)}, bf16[16,4,32,256]{3,2,1,0:T(8,128)(2,1)S(1)}, u32[]{:S(2)}, u32[]{:S(2)}) collective-permute-start(bf16[16,4,32,256]{3,2,1,0:T(8,128)(2,1)S(1)} %gather_kernel.2.first_ref), channel_id=1, source_target_pairs={{0,16},{16,0},{1,17},{17,1},{2,18},{18,2},{3,19},{19,3},{4,20},{20... | collective-permute-start | bytes 3145736 | tf_op jit(solution)/shard_map/ppermute | solution.py:17
  86.3 1.9 %collective-permute-start.17 = (bf16[8,4,32,256]{3,2,1,0:T(8,128)(2,1)S(1)}, bf16[8,4,32,256]{3,2,1,0:T(8,128)(2,1)S(1)}, u32[]{:S(2)}, u32[]{:S(2)}) collective-permute-start(bf16[8,4,32,256]{3,2,1,0:T(8,128)(2,1)S(1)} %get-tuple-element.80), channel_id=1, source_target_pairs={{0,1},{1,0},{2,3},{3,2},{4,5},{5,4},{6,7},{7,6},{8,9},{9,8},{10,11... | collective-permute-start | bytes 1572872 | tf_op jit(solution)/shard_map/ppermute | solution.py:34
  86.3 9.1 %collective-permute-start.25 = (bf16[2,4,32,256]{3,2,1,0:T(8,128)(2,1)S(1)}, bf16[2,4,32,256]{3,2,1,0:T(8,128)(2,1)S(1)}, u32[]{:S(2)}, u32[]{:S(2)}) collective-permute-start(bf16[2,4,32,256]{3,2,1,0:T(8,128)(2,1)S(1)} %get-tuple-element.92), channel_id=1, source_target_pairs={{0,14},{1,15},{2,12},{3,13},{4,10},{5,11},{6,8},{7,9},{8,6},{9,7},... | collective-permute-start | bytes 393224 | tf_op jit(solution)/shard_map/ppermute | solution.py:34
  88.3 16.9 %collective-permute-start.18 = (bf16[2,4,32,256]{3,2,1,0:T(8,128)(2,1)S(1)}, bf16[2,4,32,256]{3,2,1,0:T(8,128)(2,1)S(1)}, u32[]{:S(2)}, u32[]{:S(2)}) collective-permute-start(bf16[2,4,32,256]{3,2,1,0:T(8,128)(2,1)S(1)} %get-tuple-element.82), channel_id=1, source_target_pairs={{0,8},{1,9},{2,10},{3,11},{4,12},{5,13},{6,14},{7,15},{8,0},{9,1},... | collective-permute-start | bytes 393224 | tf_op jit(solution)/shard_map/ppermute | solution.py:34
  88.4 16.8 %collective-permute-start.19 = (bf16[2,4,32,256]{3,2,1,0:T(8,128)(2,1)S(1)}, bf16[2,4,32,256]{3,2,1,0:T(8,128)(2,1)S(1)}, u32[]{:S(2)}, u32[]{:S(2)}) collective-permute-start(bf16[2,4,32,256]{3,2,1,0:T(8,128)(2,1)S(1)} %get-tuple-element.83), channel_id=1, source_target_pairs={{0,12},{1,13},{2,14},{3,15},{4,8},{5,9},{6,10},{7,11},{8,4},{9,5},... | collective-permute-start | bytes 393224 | tf_op jit(solution)/shard_map/ppermute | solution.py:34
  90.7 21.5 %collective-permute-start.24 = (bf16[2,4,32,256]{3,2,1,0:T(8,128)(2,1)S(1)}, bf16[2,4,32,256]{3,2,1,0:T(8,128)(2,1)S(1)}, u32[]{:S(2)}, u32[]{:S(2)}) collective-permute-start(bf16[2,4,32,256]{3,2,1,0:T(8,128)(2,1)S(1)} %get-tuple-element.91), channel_id=1, source_target_pairs={{0,10},{1,11},{2,8},{3,9},{4,14},{5,15},{6,12},{7,13},{8,2},{9,3},... | collective-permute-start | bytes 393224 | tf_op jit(solution)/shard_map/ppermute | solution.py:34
  112.2 8.0 %collective-permute-start.27 = (bf16[4,4,32,256]{3,2,1,0:T(8,128)(2,1)S(1)}, bf16[4,4,32,256]{3,2,1,0:T(8,128)(2,1)S(1)}, u32[]{:S(2)}, u32[]{:S(2)}) collective-permute-start(bf16[4,4,32,256]{3,2,1,0:T(8,128)(2,1)S(1)} %gather_kernel.3.second_ref), channel_id=1, source_target_pairs={{0,16},{16,0},{1,17},{17,1},{2,18},{18,2},{3,19},{19,3},{4,20},{20... | collective-permute-start | bytes 786440 | tf_op jit(solution)/shard_map/ppermute | solution.py:17
  112.8 11.8 %collective-permute-start.20 = (bf16[2,4,32,256]{3,2,1,0:T(8,128)(2,1)S(1)}, bf16[2,4,32,256]{3,2,1,0:T(8,128)(2,1)S(1)}, u32[]{:S(2)}, u32[]{:S(2)}) collective-permute-start(bf16[2,4,32,256]{3,2,1,0:T(8,128)(2,1)S(1)} %get-tuple-element.84), channel_id=1, source_target_pairs={{0,10},{1,11},{2,8},{3,9},{4,14},{5,15},{6,12},{7,13},{8,2},{9,3},... | collective-permute-start | bytes 393224 | tf_op jit(solution)/shard_map/ppermute | solution.py:34
  112.8 11.8 %collective-permute-start.21 = (bf16[2,4,32,256]{3,2,1,0:T(8,128)(2,1)S(1)}, bf16[2,4,32,256]{3,2,1,0:T(8,128)(2,1)S(1)}, u32[]{:S(2)}, u32[]{:S(2)}) collective-permute-start(bf16[2,4,32,256]{3,2,1,0:T(8,128)(2,1)S(1)} %get-tuple-element.85), channel_id=1, source_target_pairs={{0,14},{1,15},{2,12},{3,13},{4,10},{5,11},{6,8},{7,9},{8,6},{9,7},... | collective-permute-start | bytes 393224 | tf_op jit(solution)/shard_map/ppermute | solution.py:34
  114.2 10.5 %collective-permute-start.22 = (bf16[2,4,32,256]{3,2,1,0:T(8,128)(2,1)S(1)}, bf16[2,4,32,256]{3,2,1,0:T(8,128)(2,1)S(1)}, u32[]{:S(2)}, u32[]{:S(2)}) collective-permute-start(bf16[2,4,32,256]{3,2,1,0:T(8,128)(2,1)S(1)} %get-tuple-element.86), channel_id=1, source_target_pairs={{0,2},{1,3},{2,0},{3,1},{4,6},{5,7},{6,4},{7,5},{8,10},{9,11},{10,... | collective-permute-start | bytes 393224 | tf_op jit(solution)/shard_map/ppermute | solution.py:34
  120.2 6.1 %collective-permute-start.23 = (bf16[2,4,32,256]{3,2,1,0:T(8,128)(2,1)S(1)}, bf16[2,4,32,256]{3,2,1,0:T(8,128)(2,1)S(1)}, u32[]{:S(2)}, u32[]{:S(2)}) collective-permute-start(bf16[2,4,32,256]{3,2,1,0:T(8,128)(2,1)S(1)} %get-tuple-element.87), channel_id=1, source_target_pairs={{0,4},{1,5},{2,6},{3,7},{4,0},{5,1},{6,2},{7,3},{8,12},{9,13},{10,... | collective-permute-start | bytes 393224 | tf_op jit(solution)/shard_map/ppermute | solution.py:34
  120.2 8.7 %copy-start.3 = (bf16[1,2048,256]{2,1,0:T(8,128)(2,1)S(1)}, bf16[1,2048,256]{2,1,0:T(8,128)(2,1)}, u32[]{:S(2)}) copy-start(bf16[1,2048,256]{2,1,0:T(8,128)(2,1)} %param.6) | copy-start | bytes 3145732
  120.2 8.7 %copy-start.4 = (bf16[1,2048,256]{2,1,0:T(8,128)(2,1)S(1)}, bf16[1,2048,256]{2,1,0:T(8,128)(2,1)}, u32[]{:S(2)}) copy-start(bf16[1,2048,256]{2,1,0:T(8,128)(2,1)} %param.7) | copy-start | bytes 3145732
  122.6 6.3 %collective-permute-start.28 = (bf16[2,4,32,256]{3,2,1,0:T(8,128)(2,1)S(1)}, bf16[2,4,32,256]{3,2,1,0:T(8,128)(2,1)S(1)}, u32[]{:S(2)}, u32[]{:S(2)}) collective-permute-start(bf16[2,4,32,256]{3,2,1,0:T(8,128)(2,1)S(1)} %get-tuple-element.96), channel_id=1, source_target_pairs={{0,6},{1,7},{2,4},{3,5},{4,2},{5,3},{6,0},{7,1},{8,14},{9,15},{10,... | collective-permute-start | bytes 393224 | tf_op jit(solution)/shard_map/ppermute | solution.py:34

commit v13 on v12

--- a/solution.py
+++ b/solution.py
@@ -25,8 +25,8 @@
     half = chips // 2
     near = list(range(1, half))
     far = list(range(half, chips, 2)) + list(range(half + 1, chips, 2))
-    in_turns = [t for pair in zip(far, near) for t in pair]
-    return [0] + in_turns + far[half - 1 :], [0] + far[:2] + near + far[2:], [0] + far + near
+    mixed = far[:2] + near[:-1] + far[2:-1] + near[-1:] + far[-1:]
+    return [0] + far[:1] + near + far[1:], [0] + mixed, [0] + far + near
 
 
 def permute(array, offset):
@@ -281,7 +281,7 @@
     def shape(*dims):
         return jax.ShapeDtypeStruct(dims, BF16)
 
-    in_turns, two_far, all_far = orders(chips)
+    one_ahead, two_ahead, all_far = orders(chips)
 
     def ordered(kernel, order):
         return functools.partial(kernel, order)
@@ -300,7 +300,7 @@
 
     hold = pltpu.VMEM(whole.shape, BF16)
     halves = [shape(chips, *block)] * 2
-    last = in_turns[-1]
+    last = one_ahead[-1]
     own, other = call(
         product_kernel,
         me,
@@ -320,10 +320,10 @@
         [shape(2, 2, *block)] * last + [shape(2, *block)] * 2,
     )
     other_values = swap_sequences(after(values, messages[0]))
-    columns = listed(exchange(messages), in_turns)
-    mixed_last = permute(after(mixed_last, columns[1:]), 2 * last)
+    columns = listed(exchange(messages), one_ahead)
+    mixed_last = permute(after(mixed_last, columns[1:-2] + columns[-1:]), 2 * last)
     own, other, grad_column = call(
-        ordered(column_backward_kernel, in_turns),
+        ordered(column_backward_kernel, one_ahead),
         me,
         [right_factor, *columns],
         [shape(chips, *block)] * 2 + [shape(cols, count, channels)],
@@ -334,7 +334,7 @@
     columns[-1] = mixed_last
     packed_right = shape(cols * count * count // channels, channels)
     own, other, right_part = call(
-        ordered(column_forward_kernel, in_turns),
+        ordered(column_forward_kernel, one_ahead),
         me,
         [right_factor, grad_column, other_values, *columns],
         [shape(chips, *block)] * 2 + [packed_right],
@@ -342,19 +342,22 @@
         2 * column_flops,
         unblocked=[2],
     )
-    back = listed(back, two_far)
-    messages = pack(own, permute(after(other, back[1 : chips - 2]), 1))
-    done = [(t, permute(messages[t], 2 * t)) for t in all_far[1:3]]
+    back = listed(back, two_ahead)
+    ahead = chips // 2 + 1
+    messages = pack(own, permute(after(other, back[1:ahead]), 1))
+    done = [(t, permute(messages[t], 2 * t)) for t in all_far[1:2]]
     back[-1] = after(back[-1], [block for _, block in done])
     extra = packed_right.size // math.prod(block)
     (first_part,) = call(
-        gather_kernel, me, [*back[:-2], right_part], [shape(2 * chips - 4 + extra, *block)]
-    )
-    (second_part,) = call(gather_kernel, me, back[-2:], [shape(4, *block)])
+        gather_kernel, me, [*back[:ahead], right_part], [shape(2 * ahead + extra, *block)]
+    )
+    (second_part,) = call(
+        gather_kernel, me, back[ahead:], [shape(2 * (chips - ahead), *block)]
+    )
     other_first = swap_sequences(first_part)
     other_second = swap_sequences(second_part)
     grad_signal, left_term = call(
-        ordered(row_backward_kernel, two_far),
+        ordered(row_backward_kernel, two_ahead),
         me,
         [left_factor, values, first_part, second_part],
         [by_row, left],
@@ -362,7 +365,7 @@
         2 * row_flops,
     )
     grad_left, grad_right = call(
-        ordered(factor_sum_kernel, two_far),
+        ordered(factor_sum_kernel, two_ahead),
         me,
         [left_term, other_values, other_first, other_second, right_part],
         [left, right],

time: 131 us -> 127 us (0.969)
  starting transfers between devices: 53.1 us -> 44.5 us
  waiting for transfers between devices: 59 us -> 63.9 us
    ppermute x26, starting transfers between devices: 49.6 us -> 40.9 us  [permute(): return lax.ppermute(array, 'seq', [(i, i ^ offset) for i in range(seq)])]
    ppermute x26, waiting for transfers between devices: 56 us -> 61.8 us  [permute(): return lax.ppermute(array, 'seq', [(i, i ^ offset) for i in range(seq)])]
  transfers between devices with their start and end apart: 29 -> 29, of which waited for: 18 -> 16; matrix products, arithmetic and copies ran while one was open for 0% -> 0% of each run, Pallas kernels for 9% -> 9%
where the time goes in v13:
time: 127 us
  waiting for transfers between devices  63.9 us (50%)
  starting transfers between devices  44.5 us (35%)
  Pallas kernels  16.6 us (13%)
    ppermute x26, waiting for transfers between devices, permute(): return lax.ppermute(array, 'seq', [(i, i ^ offset) for i in range(seq)])  61.8 us
    ppermute x26, starting transfers between devices, permute(): return lax.ppermute(array, 'seq', [(i, i ^ offset) for i in range(seq)])  40.9 us
    pallas_call x12, Pallas kernels, call(): pl.pallas_call(kernel, out_shape=out_shapes, in_specs=[pl.BlockSpec(memor...  16.6 us
    ppermute x3, starting transfers between devices, swap_sequences(): return lax.ppermute(array, 'dp', [(0, 1), (1, 0)])  3.64 us
  transfers between devices with their start and end apart: 29, of which 16 were waited for; matrix products, arithmetic and copies ran while one was open for 0% of the time, Pallas kernels for 9%

profile of v13, /device:TPU:0, one launch (start us, length us, event | category | flops | bytes accessed | tf_op | source)
XLA Modules:
  0.0 127.1 jit_solution(11189094918927917417)
XLA Ops:
  0.6 2.7 %product_kernel.1 = (bf16[8,4,32,256]{3,2,1,0:T(8,128)(2,1)}, bf16[8,4,32,256]{3,2,1,0:T(8,128)(2,1)}) custom-call(s32[1]{0:T(128)} %bitcast.me_ref, bf16[4,16,32,256]{3,2,1,0:T(8,128)(2,1)} %bitcast.10, bf16[4,16,32,256]{3,2,1,0:T(8,128)(2,1)} %bitcast.12), custom_call_target="tpu_custom_call" | custom-call | bytes 3145728 | tf_op jit(solution)/shard_map/product_kernel/pallas_call | solution.py:55
  3.4 0.5 collective-permute-start
  3.9 1.2 copy-done.1
  5.1 0.8 mix_kernel.1
  6.0 1.9 %collective-permute-done.1.refs_3_ = bf16[8,4,32,256]{3,2,1,0:T(8,128)(2,1)S(1)} collective-permute-done((bf16[8,4,32,256]{3,2,1,0:T(8,128)(2,1)S(1)}, bf16[8,4,32,256]{3,2,1,0:T(8,128)(2,1)S(1)}, u32[]{:S(2)}, u32[]{:S(2)}) %collective-permute-start.1) | collective-permute-done | bytes 524320 | tf_op jit(solution)/shard_map/ppermute | solution.py:34
  7.9 0.1 pack_pairs_kernel.1
  8.0 3.8 %collective-permute-start.2 = (bf16[2,2,4,32,256]{4,3,2,1,0:T(8,128)(2,1)S(1)}, bf16[2,2,4,32,256]{4,3,2,1,0:T(8,128)(2,1)S(1)}, u32[]{:S(2)}, u32[]{:S(2)}) collective-permute-start(bf16[2,2,4,32,256]{4,3,2,1,0:T(8,128)(2,1)S(1)} %get-tuple-element.59), channel_id=1, source_target_pairs={{0,8},{1,9},{2,10},{3,11},{4,12},{5,13},{6,14},{7,15},{8,0},{9,1},... | collective-permute-start | bytes 786440 | tf_op jit(solution)/shard_map/ppermute | solution.py:34
  11.8 1.5 %collective-permute-start.3 = (bf16[2,2,4,32,256]{4,3,2,1,0:T(8,128)(2,1)S(1)}, bf16[2,2,4,32,256]{4,3,2,1,0:T(8,128)(2,1)S(1)}, u32[]{:S(2)}, u32[]{:S(2)}) collective-permute-start(bf16[2,2,4,32,256]{4,3,2,1,0:T(8,128)(2,1)S(1)} %get-tuple-element.60), channel_id=1, source_target_pairs={{0,2},{1,3},{2,0},{3,1},{4,6},{5,7},{6,4},{7,5},{8,10},{9,11},{10,... | collective-permute-start | bytes 786440 | tf_op jit(solution)/shard_map/ppermute | solution.py:34
  13.3 1.3 %collective-permute-start.8 = (bf16[2,4,32,256]{3,2,1,0:T(8,128)(2,1)S(1)}, bf16[2,4,32,256]{3,2,1,0:T(8,128)(2,1)S(1)}, u32[]{:S(2)}, u32[]{:S(2)}) collective-permute-start(bf16[2,4,32,256]{3,2,1,0:T(8,128)(2,1)S(1)} %get-tuple-element.65), channel_id=1, source_target_pairs={{0,14},{1,15},{2,12},{3,13},{4,10},{5,11},{6,8},{7,9},{8,6},{9,7},... | collective-permute-start | bytes 393224 | tf_op jit(solution)/shard_map/ppermute | solution.py:34
  14.6 1.5 %collective-permute-start.9 = (bf16[4,512,256]{2,1,0:T(8,128)(2,1)S(1)}, bf16[4,512,256]{2,1,0:T(8,128)(2,1)S(1)}, u32[]{:S(2)}, u32[]{:S(2)}) collective-permute-start(bf16[4,512,256]{2,1,0:T(8,128)(2,1)S(1)} %bitcast.8), channel_id=1, source_target_pairs={{0,16},{16,0},{1,17},{17,1},{2,18},{18,2},{3,19},{19,3},{4,20},{20... | collective-permute-start | bytes 3145736 | tf_op jit(solution)/shard_map/ppermute | solution.py:17
  16.1 0.3 collective-permute-start.4
  16.4 7.7 %collective-permute-done.8.refs_7_ = bf16[2,4,32,256]{3,2,1,0:T(8,128)(2,1)S(1)} collective-permute-done((bf16[2,4,32,256]{3,2,1,0:T(8,128)(2,1)S(1)}, bf16[2,4,32,256]{3,2,1,0:T(8,128)(2,1)S(1)}, u32[]{:S(2)}, u32[]{:S(2)}) %collective-permute-start.8) | collective-permute-done | bytes 131104 | tf_op jit(solution)/shard_map/ppermute | solution.py:34
  24.1 7.5 %collective-permute-start.5 = (bf16[2,2,4,32,256]{4,3,2,1,0:T(8,128)(2,1)S(1)}, bf16[2,2,4,32,256]{4,3,2,1,0:T(8,128)(2,1)S(1)}, u32[]{:S(2)}, u32[]{:S(2)}) collective-permute-start(bf16[2,2,4,32,256]{4,3,2,1,0:T(8,128)(2,1)S(1)} %get-tuple-element.62), channel_id=1, source_target_pairs={{0,6},{1,7},{2,4},{3,5},{4,2},{5,3},{6,0},{7,1},{8,14},{9,15},{10,... | collective-permute-start | bytes 786440 | tf_op jit(solution)/shard_map/ppermute | solution.py:34
  31.6 3.3 %collective-permute-start.6 = (bf16[2,2,4,32,256]{4,3,2,1,0:T(8,128)(2,1)S(1)}, bf16[2,2,4,32,256]{4,3,2,1,0:T(8,128)(2,1)S(1)}, u32[]{:S(2)}, u32[]{:S(2)}) collective-permute-start(bf16[2,2,4,32,256]{4,3,2,1,0:T(8,128)(2,1)S(1)} %get-tuple-element.63), channel_id=1, source_target_pairs={{0,12},{1,13},{2,14},{3,15},{4,8},{5,9},{6,10},{7,11},{8,4},{9,5},... | collective-permute-start | bytes 786440 | tf_op jit(solution)/shard_map/ppermute | solution.py:34
  35.0 3.4 %collective-permute-done.5.refs_4_ = bf16[2,2,4,32,256]{4,3,2,1,0:T(8,128)(2,1)S(1)} collective-permute-done((bf16[2,2,4,32,256]{4,3,2,1,0:T(8,128)(2,1)S(1)}, bf16[2,2,4,32,256]{4,3,2,1,0:T(8,128)(2,1)S(1)}, u32[]{:S(2)}, u32[]{:S(2)}) %collective-permute-start.5) | collective-permute-done | bytes 262176 | tf_op jit(solution)/shard_map/ppermute | solution.py:34
  38.3 9.5 %collective-permute-done.6.refs_5_ = bf16[2,2,4,32,256]{4,3,2,1,0:T(8,128)(2,1)S(1)} collective-permute-done((bf16[2,2,4,32,256]{4,3,2,1,0:T(8,128)(2,1)S(1)}, bf16[2,2,4,32,256]{4,3,2,1,0:T(8,128)(2,1)S(1)}, u32[]{:S(2)}, u32[]{:S(2)}) %collective-permute-start.6) | collective-permute-done | bytes 262176 | tf_op jit(solution)/shard_map/ppermute | solution.py:34
  47.8 1.4 %collective-permute-start.10 = (bf16[2,4,32,256]{3,2,1,0:T(8,128)(2,1)S(1)}, bf16[2,4,32,256]{3,2,1,0:T(8,128)(2,1)S(1)}, u32[]{:S(2)}, u32[]{:S(2)}) collective-permute-start(bf16[2,4,32,256]{3,2,1,0:T(8,128)(2,1)S(1)} %get-tuple-element.69), channel_id=1, source_target_pairs={{0,14},{1,15},{2,12},{3,13},{4,10},{5,11},{6,8},{7,9},{8,6},{9,7},... | collective-permute-start | bytes 393224 | tf_op jit(solution)/shard_map/ppermute | solution.py:34
  49.2 11.1 %collective-permute-done.7.refs_6_ = bf16[2,2,4,32,256]{4,3,2,1,0:T(8,128)(2,1)S(1)} collective-permute-done((bf16[2,2,4,32,256]{4,3,2,1,0:T(8,128)(2,1)S(1)}, bf16[2,2,4,32,256]{4,3,2,1,0:T(8,128)(2,1)S(1)}, u32[]{:S(2)}, u32[]{:S(2)}) %collective-permute-start.7) | collective-permute-done | bytes 262176 | tf_op jit(solution)/shard_map/ppermute | solution.py:34
  60.2 3.0 %column_backward_kernel.1 = (bf16[8,4,32,256]{3,2,1,0:T(8,128)(2,1)S(1)}, bf16[8,4,32,256]{3,2,1,0:T(8,128)(2,1)S(1)}, bf16[32,64,256]{2,1,0:T(8,128)(2,1)S(1)}) custom-call(s32[1]{0:T(128)} %bitcast.me_ref, bf16[32,64,64]{2,1,0:T(8,128)(2,1)S(1)} %copy-done.5, bf16[2,2,4,32,256]{4,3,2,1,0:T(8,128)(2,1)S(1)} %get-tuple-element.58.refs_0_, ...), custom_call_target="tpu_custom_call" | custom-call | flops 67108864 | bytes 4325376 | tf_op jit(solution)/shard_map/column_backward_kernel/pallas_call | solution.py:55
  63.3 1.9 %collective-permute-done.11.other_ref = bf16[8,4,32,256]{3,2,1,0:T(8,128)(2,1)S(1)} collective-permute-done((bf16[8,4,32,256]{3,2,1,0:T(8,128)(2,1)S(1)}, bf16[8,4,32,256]{3,2,1,0:T(8,128)(2,1)S(1)}, u32[]{:S(2)}, u32[]{:S(2)}) %collective-permute-start.11) | collective-permute-done | bytes 524320 | tf_op jit(solution)/shard_map/ppermute | solution.py:34
  65.3 1.0 collective-permute-start.12
  66.3 2.1 %collective-permute-start.13 = (bf16[2,4,32,256]{3,2,1,0:T(8,128)(2,1)S(1)}, bf16[2,4,32,256]{3,2,1,0:T(8,128)(2,1)S(1)}, u32[]{:S(2)}, u32[]{:S(2)}) collective-permute-start(bf16[2,4,32,256]{3,2,1,0:T(8,128)(2,1)S(1)} %get-tuple-element.76), channel_id=1, source_target_pairs={{0,12},{1,13},{2,14},{3,15},{4,8},{5,9},{6,10},{7,11},{8,4},{9,5},... | collective-permute-start | bytes 393224 | tf_op jit(solution)/shard_map/ppermute | solution.py:34
  68.4 1.5 %collective-permute-start.14 = (bf16[2,4,32,256]{3,2,1,0:T(8,128)(2,1)S(1)}, bf16[2,4,32,256]{3,2,1,0:T(8,128)(2,1)S(1)}, u32[]{:S(2)}, u32[]{:S(2)}) collective-permute-start(bf16[2,4,32,256]{3,2,1,0:T(8,128)(2,1)S(1)} %get-tuple-element.77), channel_id=1, source_target_pairs={{0,2},{1,3},{2,0},{3,1},{4,6},{5,7},{6,4},{7,5},{8,10},{9,11},{10,... | collective-permute-start | bytes 393224 | tf_op jit(solution)/shard_map/ppermute | solution.py:34
  69.9 0.5 collective-permute-start.15
  70.4 3.3 %column_forward_kernel.1 = (bf16[8,4,32,256]{3,2,1,0:T(8,128)(2,1)S(1)}, bf16[8,4,32,256]{3,2,1,0:T(8,128)(2,1)S(1)}, bf16[512,256]{1,0:T(8,128)(2,1)S(1)}) custom-call(s32[1]{0:T(128)} %bitcast.me_ref, bf16[32,64,64]{2,1,0:T(8,128)(2,1)S(1)} %copy-done.5, bf16[32,64,256]{2,1,0:T(8,128)(2,1)S(1)} %get-tuple-element.66.grad_ref, ...), custom_call_target="tpu_custom_call" | custom-call | flops 134217728 | bytes 5636096 | tf_op jit(solution)/shard_map/column_forward_kernel/pallas_call | solution.py:55
  73.7 4.1 %collective-permute-done.12.refs_1_ = bf16[2,4,32,256]{3,2,1,0:T(8,128)(2,1)S(1)} collective-permute-done((bf16[2,4,32,256]{3,2,1,0:T(8,128)(2,1)S(1)}, bf16[2,4,32,256]{3,2,1,0:T(8,128)(2,1)S(1)}, u32[]{:S(2)}, u32[]{:S(2)}) %collective-permute-start.12) | collective-permute-done | bytes 131104 | tf_op jit(solution)/shard_map/ppermute | solution.py:34
  77.8 2.1 %collective-permute-done.15.refs_4_ = bf16[2,4,32,256]{3,2,1,0:T(8,128)(2,1)S(1)} collective-permute-done((bf16[2,4,32,256]{3,2,1,0:T(8,128)(2,1)S(1)}, bf16[2,4,32,256]{3,2,1,0:T(8,128)(2,1)S(1)}, u32[]{:S(2)}, u32[]{:S(2)}) %collective-permute-start.15) | collective-permute-done | bytes 131104 | tf_op jit(solution)/shard_map/ppermute | solution.py:34
  80.0 1.6 %collective-permute-start.26 = (bf16[14,4,32,256]{3,2,1,0:T(8,128)(2,1)S(1)}, bf16[14,4,32,256]{3,2,1,0:T(8,128)(2,1)S(1)}, u32[]{:S(2)}, u32[]{:S(2)}) collective-permute-start(bf16[14,4,32,256]{3,2,1,0:T(8,128)(2,1)S(1)} %gather_kernel.2.first_ref), channel_id=1, source_target_pairs={{0,16},{16,0},{1,17},{17,1},{2,18},{18,2},{3,19},{19,3},{4,20},{20... | collective-permute-start | bytes 2752520 | tf_op jit(solution)/shard_map/ppermute | solution.py:17
  81.5 1.9 %collective-permute-start.25 = (bf16[2,4,32,256]{3,2,1,0:T(8,128)(2,1)S(1)}, bf16[2,4,32,256]{3,2,1,0:T(8,128)(2,1)S(1)}, u32[]{:S(2)}, u32[]{:S(2)}) collective-permute-start(bf16[2,4,32,256]{3,2,1,0:T(8,128)(2,1)S(1)} %get-tuple-element.92), channel_id=1, source_target_pairs={{0,14},{1,15},{2,12},{3,13},{4,10},{5,11},{6,8},{7,9},{8,6},{9,7},... | collective-permute-start | bytes 393224 | tf_op jit(solution)/shard_map/ppermute | solution.py:34
  83.5 1.5 %collective-permute-start.17 = (bf16[2,4,32,256]{3,2,1,0:T(8,128)(2,1)S(1)}, bf16[2,4,32,256]{3,2,1,0:T(8,128)(2,1)S(1)}, u32[]{:S(2)}, u32[]{:S(2)}) collective-permute-start(bf16[2,4,32,256]{3,2,1,0:T(8,128)(2,1)S(1)} %get-tuple-element.81), channel_id=1, source_target_pairs={{0,8},{1,9},{2,10},{3,11},{4,12},{5,13},{6,14},{7,15},{8,0},{9,1},... | collective-permute-start | bytes 393224 | tf_op jit(solution)/shard_map/ppermute | solution.py:34
  85.0 2.2 %collective-permute-start.23 = (bf16[2,4,32,256]{3,2,1,0:T(8,128)(2,1)S(1)}, bf16[2,4,32,256]{3,2,1,0:T(8,128)(2,1)S(1)}, u32[]{:S(2)}, u32[]{:S(2)}) collective-permute-start(bf16[2,4,32,256]{3,2,1,0:T(8,128)(2,1)S(1)} %get-tuple-element.90), channel_id=1, source_target_pairs={{0,10},{1,11},{2,8},{3,9},{4,14},{5,15},{6,12},{7,13},{8,2},{9,3},... | collective-permute-start | bytes 393224 | tf_op jit(solution)/shard_map/ppermute | solution.py:34
  87.2 1.1 collective-permute-start.24
  88.3 2.3 %collective-permute-done.25.refs_2_ = bf16[2,4,32,256]{3,2,1,0:T(8,128)(2,1)S(1)} collective-permute-done((bf16[2,4,32,256]{3,2,1,0:T(8,128)(2,1)S(1)}, bf16[2,4,32,256]{3,2,1,0:T(8,128)(2,1)S(1)}, u32[]{:S(2)}, u32[]{:S(2)}) %collective-permute-start.25) | collective-permute-done | bytes 131104 | tf_op jit(solution)/shard_map/ppermute | solution.py:34
  90.6 11.0 %collective-permute-done.17.refs_1_ = bf16[2,4,32,256]{3,2,1,0:T(8,128)(2,1)S(1)} collective-permute-done((bf16[2,4,32,256]{3,2,1,0:T(8,128)(2,1)S(1)}, bf16[2,4,32,256]{3,2,1,0:T(8,128)(2,1)S(1)}, u32[]{:S(2)}, u32[]{:S(2)}) %collective-permute-start.17) | collective-permute-done | bytes 131104 | tf_op jit(solution)/shard_map/ppermute | solution.py:34
  101.7 1.4 %collective-permute-done.23.refs_0_ = bf16[2,4,32,256]{3,2,1,0:T(8,128)(2,1)S(1)} collective-permute-done((bf16[2,4,32,256]{3,2,1,0:T(8,128)(2,1)S(1)}, bf16[2,4,32,256]{3,2,1,0:T(8,128)(2,1)S(1)}, u32[]{:S(2)}, u32[]{:S(2)}) %collective-permute-start.23) | collective-permute-done | bytes 131104 | tf_op jit(solution)/shard_map/ppermute | solution.py:34
  103.1 0.6 collective-permute-start.27
  103.7 1.6 %collective-permute-start.18 = (bf16[2,4,32,256]{3,2,1,0:T(8,128)(2,1)S(1)}, bf16[2,4,32,256]{3,2,1,0:T(8,128)(2,1)S(1)}, u32[]{:S(2)}, u32[]{:S(2)}) collective-permute-start(bf16[2,4,32,256]{3,2,1,0:T(8,128)(2,1)S(1)} %get-tuple-element.82), channel_id=1, source_target_pairs={{0,12},{1,13},{2,14},{3,15},{4,8},{5,9},{6,10},{7,11},{8,4},{9,5},... | collective-permute-start | bytes 393224 | tf_op jit(solution)/shard_map/ppermute | solution.py:34
  105.2 4.0 %collective-permute-start.20 = (bf16[2,4,32,256]{3,2,1,0:T(8,128)(2,1)S(1)}, bf16[2,4,32,256]{3,2,1,0:T(8,128)(2,1)S(1)}, u32[]{:S(2)}, u32[]{:S(2)}) collective-permute-start(bf16[2,4,32,256]{3,2,1,0:T(8,128)(2,1)S(1)} %get-tuple-element.84), channel_id=1, source_target_pairs={{0,14},{1,15},{2,12},{3,13},{4,10},{5,11},{6,8},{7,9},{8,6},{9,7},... | collective-permute-start | bytes 393224 | tf_op jit(solution)/shard_map/ppermute | solution.py:34
  109.2 2.3 %row_backward_kernel.1 = (bf16[4,512,256]{2,1,0:T(8,128)(2,1)}, bf16[4,512,512]{2,1,0:T(8,128)(2,1)S(1)}) custom-call(s32[1]{0:T(128)} %bitcast.me_ref, bf16[4,512,512]{2,1,0:T(8,128)(2,1)S(1)} %copy-done, bf16[4,512,256]{2,1,0:T(8,128)(2,1)S(1)} %bitcast.9, bf16[14,4,32,256]{3,2,1,0:T(8,128)(2,1)S(1)} %gather_kernel.2.first_ref, ...), custom_call_target="tpu_custom_call" | custom-call | flops 1073741824 | bytes 7602176 | tf_op jit(solution)/shard_map/row_backward_kernel/pallas_call | solution.py:55
  111.5 2.0 %collective-permute-done.27.second_ref = bf16[6,4,32,256]{3,2,1,0:T(8,128)(2,1)S(1)} collective-permute-done((bf16[6,4,32,256]{3,2,1,0:T(8,128)(2,1)S(1)}, bf16[6,4,32,256]{3,2,1,0:T(8,128)(2,1)S(1)}, u32[]{:S(2)}, u32[]{:S(2)}) %collective-permute-start.27) | collective-permute-done | bytes 393248 | tf_op jit(solution)/shard_map/ppermute | solution.py:17
  113.5 0.8 collective-permute-start.22
  114.4 2.4 %factor_sum_kernel.1 = (bf16[4,512,512]{2,1,0:T(8,128)(2,1)}, bf16[32,64,64]{2,1,0:T(8,128)(2,1)}) custom-call(s32[1]{0:T(128)} %bitcast.me_ref, bf16[4,512,512]{2,1,0:T(8,128)(2,1)S(1)} %get-tuple-element.94.term_ref, bf16[4,512,256]{2,1,0:T(8,128)(2,1)S(1)} %collective-permute-done.9.after_ref.values_ref, ...), custom_call_target="tpu_custom_call" | custom-call | flops 536870912 | bytes 7077888 | tf_op jit(solution)/shard_map/factor_sum_kernel/pallas_call | solution.py:55
  116.8 2.9 %collective-permute-start.28 = (bf16[2,4,32,256]{3,2,1,0:T(8,128)(2,1)S(1)}, bf16[2,4,32,256]{3,2,1,0:T(8,128)(2,1)S(1)}, u32[]{:S(2)}, u32[]{:S(2)}) collective-permute-start(bf16[2,4,32,256]{3,2,1,0:T(8,128)(2,1)S(1)} %get-tuple-element.96), channel_id=1, source_target_pairs={{0,6},{1,7},{2,4},{3,5},{4,2},{5,3},{6,0},{7,1},{8,14},{9,15},{10,... | collective-permute-start | bytes 393224 | tf_op jit(solution)/shard_map/ppermute | solution.py:34
  119.7 0.7 collective-permute-done.19.refs_3_
  120.4 0.2 collective-permute-done.21.refs_5_
  120.5 1.4 %collective-permute-done.22.refs_6_ = bf16[2,4,32,256]{3,2,1,0:T(8,128)(2,1)S(1)} collective-permute-done((bf16[2,4,32,256]{3,2,1,0:T(8,128)(2,1)S(1)}, bf16[2,4,32,256]{3,2,1,0:T(8,128)(2,1)S(1)}, u32[]{:S(2)}, u32[]{:S(2)}) %collective-permute-start.22) | collective-permute-done | bytes 131104 | tf_op jit(solution)/shard_map/ppermute | solution.py:34
  121.9 3.4 %collective-permute-done.28.refs_7_ = bf16[2,4,32,256]{3,2,1,0:T(8,128)(2,1)S(1)} collective-permute-done((bf16[2,4,32,256]{3,2,1,0:T(8,128)(2,1)S(1)}, bf16[2,4,32,256]{3,2,1,0:T(8,128)(2,1)S(1)}, u32[]{:S(2)}, u32[]{:S(2)}) %collective-permute-start.28) | collective-permute-done | bytes 131104 | tf_op jit(solution)/shard_map/ppermute | solution.py:34
  125.3 1.8 %output_kernel.1 = (bf16[4,16,32,256]{3,2,1,0:T(8,128)(2,1)}, bf16[4,16,32,256]{3,2,1,0:T(8,128)(2,1)}) custom-call(s32[1]{0:T(128)} %bitcast.me_ref, bf16[4,16,32,256]{3,2,1,0:T(8,128)(2,1)S(1)} %bitcast.11, bf16[4,16,32,256]{3,2,1,0:T(8,128)(2,1)S(1)} %bitcast.13, bf16[2,4,32,256]{3,2,1,0:T(8,128)(2,1)S(1)} %get-tuple-element.80.refs_0_, ...), custom_call_target="tpu_custom_call" | custom-call | bytes 5242880 | tf_op jit(solution)/shard_map/output_kernel/pallas_call | solution.py:55
  (36 shorter events, 0.5 us)
Async XLA Ops:
  0.6 3.3 %copy-start = (bf16[4,512,512]{2,1,0:T(8,128)(2,1)S(1)}, bf16[4,512,512]{2,1,0:T(8,128)(2,1)}, u32[]{:S(2)}) copy-start(bf16[4,512,512]{2,1,0:T(8,128)(2,1)} %left_ref.3) | copy-start | bytes 6291460
  3.4 2.7 %collective-permute-start = (bf16[8,4,32,256]{3,2,1,0:T(8,128)(2,1)}, bf16[8,4,32,256]{3,2,1,0:T(8,128)(2,1)S(1)}, u32[]{:S(2)}, u32[]{:S(2)}) collective-permute-start(bf16[8,4,32,256]{3,2,1,0:T(8,128)(2,1)} %get-tuple-element.54), channel_id=1, source_target_pairs={{0,1},{1,0},{2,3},{3,2},{4,5},{5,4},{6,7},{7,6},{8,9},{9,8},{10,11... | collective-permute-start | bytes 1572872 | tf_op jit(solution)/shard_map/ppermute | solution.py:34
  3.9 1.2 copy-start.1
  5.1 2.8 %copy-start.6 = (bf16[8,4,32,256]{3,2,1,0:T(8,128)(2,1)S(1)}, bf16[8,4,32,256]{3,2,1,0:T(8,128)(2,1)}, u32[]{:S(2)}) copy-start(bf16[8,4,32,256]{3,2,1,0:T(8,128)(2,1)} %get-tuple-element.53.refs_0_) | copy-start | bytes 1572868
  5.1 9.5 %copy-start.2 = (bf16[1,2048,256]{2,1,0:T(8,128)(2,1)S(1)}, bf16[1,2048,256]{2,1,0:T(8,128)(2,1)}, u32[]{:S(2)}) copy-start(bf16[1,2048,256]{2,1,0:T(8,128)(2,1)} %param.5) | copy-start | bytes 3145732
  5.1 55.1 %copy-start.5 = (bf16[32,64,64]{2,1,0:T(8,128)(2,1)S(1)}, bf16[32,64,64]{2,1,0:T(8,128)(2,1)}, u32[]{:S(2)}) copy-start(bf16[32,64,64]{2,1,0:T(8,128)(2,1)} %right_ref.3) | copy-start | bytes 786436
  5.9 2.0 %collective-permute-start.1 = (bf16[8,4,32,256]{3,2,1,0:T(8,128)(2,1)S(1)}, bf16[8,4,32,256]{3,2,1,0:T(8,128)(2,1)S(1)}, u32[]{:S(2)}, u32[]{:S(2)}) collective-permute-start(bf16[8,4,32,256]{3,2,1,0:T(8,128)(2,1)S(1)} %get-tuple-element.57), channel_id=1, source_target_pairs={{0,1},{1,0},{2,3},{3,2},{4,5},{5,4},{6,7},{7,6},{8,9},{9,8},{10,11... | collective-permute-start | bytes 1572872 | tf_op jit(solution)/shard_map/ppermute | solution.py:34
  8.0 23.6 %collective-permute-start.2 = (bf16[2,2,4,32,256]{4,3,2,1,0:T(8,128)(2,1)S(1)}, bf16[2,2,4,32,256]{4,3,2,1,0:T(8,128)(2,1)S(1)}, u32[]{:S(2)}, u32[]{:S(2)}) collective-permute-start(bf16[2,2,4,32,256]{4,3,2,1,0:T(8,128)(2,1)S(1)} %get-tuple-element.59), channel_id=1, source_target_pairs={{0,8},{1,9},{2,10},{3,11},{4,12},{5,13},{6,14},{7,15},{8,0},{9,1},... | collective-permute-start | bytes 786440 | tf_op jit(solution)/shard_map/ppermute | solution.py:34
  11.8 23.1 %collective-permute-start.3 = (bf16[2,2,4,32,256]{4,3,2,1,0:T(8,128)(2,1)S(1)}, bf16[2,2,4,32,256]{4,3,2,1,0:T(8,128)(2,1)S(1)}, u32[]{:S(2)}, u32[]{:S(2)}) collective-permute-start(bf16[2,2,4,32,256]{4,3,2,1,0:T(8,128)(2,1)S(1)} %get-tuple-element.60), channel_id=1, source_target_pairs={{0,2},{1,3},{2,0},{3,1},{4,6},{5,7},{6,4},{7,5},{8,10},{9,11},{10,... | collective-permute-start | bytes 786440 | tf_op jit(solution)/shard_map/ppermute | solution.py:34
  13.3 10.8 %collective-permute-start.8 = (bf16[2,4,32,256]{3,2,1,0:T(8,128)(2,1)S(1)}, bf16[2,4,32,256]{3,2,1,0:T(8,128)(2,1)S(1)}, u32[]{:S(2)}, u32[]{:S(2)}) collective-permute-start(bf16[2,4,32,256]{3,2,1,0:T(8,128)(2,1)S(1)} %get-tuple-element.65), channel_id=1, source_target_pairs={{0,14},{1,15},{2,12},{3,13},{4,10},{5,11},{6,8},{7,9},{8,6},{9,7},... | collective-permute-start | bytes 393224 | tf_op jit(solution)/shard_map/ppermute | solution.py:34
  14.6 55.7 %collective-permute-start.9 = (bf16[4,512,256]{2,1,0:T(8,128)(2,1)S(1)}, bf16[4,512,256]{2,1,0:T(8,128)(2,1)S(1)}, u32[]{:S(2)}, u32[]{:S(2)}) collective-permute-start(bf16[4,512,256]{2,1,0:T(8,128)(2,1)S(1)} %bitcast.8), channel_id=1, source_target_pairs={{0,16},{16,0},{1,17},{17,1},{2,18},{18,2},{3,19},{19,3},{4,20},{20... | collective-permute-start | bytes 3145736 | tf_op jit(solution)/shard_map/ppermute | solution.py:17
  16.1 18.8 %collective-permute-start.4 = (bf16[2,2,4,32,256]{4,3,2,1,0:T(8,128)(2,1)S(1)}, bf16[2,2,4,32,256]{4,3,2,1,0:T(8,128)(2,1)S(1)}, u32[]{:S(2)}, u32[]{:S(2)}) collective-permute-start(bf16[2,2,4,32,256]{4,3,2,1,0:T(8,128)(2,1)S(1)} %get-tuple-element.61), channel_id=1, source_target_pairs={{0,4},{1,5},{2,6},{3,7},{4,0},{5,1},{6,2},{7,3},{8,12},{9,13},{10,... | collective-permute-start | bytes 786440 | tf_op jit(solution)/shard_map/ppermute | solution.py:34
  24.1 14.2 %collective-permute-start.5 = (bf16[2,2,4,32,256]{4,3,2,1,0:T(8,128)(2,1)S(1)}, bf16[2,2,4,32,256]{4,3,2,1,0:T(8,128)(2,1)S(1)}, u32[]{:S(2)}, u32[]{:S(2)}) collective-permute-start(bf16[2,2,4,32,256]{4,3,2,1,0:T(8,128)(2,1)S(1)} %get-tuple-element.62), channel_id=1, source_target_pairs={{0,6},{1,7},{2,4},{3,5},{4,2},{5,3},{6,0},{7,1},{8,14},{9,15},{10,... | collective-permute-start | bytes 786440 | tf_op jit(solution)/shard_map/ppermute | solution.py:34
  31.6 16.2 %collective-permute-start.6 = (bf16[2,2,4,32,256]{4,3,2,1,0:T(8,128)(2,1)S(1)}, bf16[2,2,4,32,256]{4,3,2,1,0:T(8,128)(2,1)S(1)}, u32[]{:S(2)}, u32[]{:S(2)}) collective-permute-start(bf16[2,2,4,32,256]{4,3,2,1,0:T(8,128)(2,1)S(1)} %get-tuple-element.63), channel_id=1, source_target_pairs={{0,12},{1,13},{2,14},{3,15},{4,8},{5,9},{6,10},{7,11},{8,4},{9,5},... | collective-permute-start | bytes 786440 | tf_op jit(solution)/shard_map/ppermute | solution.py:34
  34.9 25.3 %collective-permute-start.7 = (bf16[2,2,4,32,256]{4,3,2,1,0:T(8,128)(2,1)S(1)}, bf16[2,2,4,32,256]{4,3,2,1,0:T(8,128)(2,1)S(1)}, u32[]{:S(2)}, u32[]{:S(2)}) collective-permute-start(bf16[2,2,4,32,256]{4,3,2,1,0:T(8,128)(2,1)S(1)} %get-tuple-element.64), channel_id=1, source_target_pairs={{0,10},{1,11},{2,8},{3,9},{4,14},{5,15},{6,12},{7,13},{8,2},{9,3},... | collective-permute-start | bytes 786440 | tf_op jit(solution)/shard_map/ppermute | solution.py:34
  47.8 15.4 %collective-permute-start.10 = (bf16[2,4,32,256]{3,2,1,0:T(8,128)(2,1)S(1)}, bf16[2,4,32,256]{3,2,1,0:T(8,128)(2,1)S(1)}, u32[]{:S(2)}, u32[]{:S(2)}) collective-permute-start(bf16[2,4,32,256]{3,2,1,0:T(8,128)(2,1)S(1)} %get-tuple-element.69), channel_id=1, source_target_pairs={{0,14},{1,15},{2,12},{3,13},{4,10},{5,11},{6,8},{7,9},{8,6},{9,7},... | collective-permute-start | bytes 393224 | tf_op jit(solution)/shard_map/ppermute | solution.py:34
  63.2 2.0 %collective-permute-start.11 = (bf16[8,4,32,256]{3,2,1,0:T(8,128)(2,1)S(1)}, bf16[8,4,32,256]{3,2,1,0:T(8,128)(2,1)S(1)}, u32[]{:S(2)}, u32[]{:S(2)}) collective-permute-start(bf16[8,4,32,256]{3,2,1,0:T(8,128)(2,1)S(1)} %get-tuple-element.74), channel_id=1, source_target_pairs={{0,1},{1,0},{2,3},{3,2},{4,5},{5,4},{6,7},{7,6},{8,9},{9,8},{10,11... | collective-permute-start | bytes 1572872 | tf_op jit(solution)/shard_map/ppermute | solution.py:34
  65.3 12.6 %collective-permute-start.12 = (bf16[2,4,32,256]{3,2,1,0:T(8,128)(2,1)S(1)}, bf16[2,4,32,256]{3,2,1,0:T(8,128)(2,1)S(1)}, u32[]{:S(2)}, u32[]{:S(2)}) collective-permute-start(bf16[2,4,32,256]{3,2,1,0:T(8,128)(2,1)S(1)} %get-tuple-element.75), channel_id=1, source_target_pairs={{0,8},{1,9},{2,10},{3,11},{4,12},{5,13},{6,14},{7,15},{8,0},{9,1},... | collective-permute-start | bytes 393224 | tf_op jit(solution)/shard_map/ppermute | solution.py:34
  66.3 11.6 %collective-permute-start.13 = (bf16[2,4,32,256]{3,2,1,0:T(8,128)(2,1)S(1)}, bf16[2,4,32,256]{3,2,1,0:T(8,128)(2,1)S(1)}, u32[]{:S(2)}, u32[]{:S(2)}) collective-permute-start(bf16[2,4,32,256]{3,2,1,0:T(8,128)(2,1)S(1)} %get-tuple-element.76), channel_id=1, source_target_pairs={{0,12},{1,13},{2,14},{3,15},{4,8},{5,9},{6,10},{7,11},{8,4},{9,5},... | collective-permute-start | bytes 393224 | tf_op jit(solution)/shard_map/ppermute | solution.py:34
  68.4 9.5 %collective-permute-start.14 = (bf16[2,4,32,256]{3,2,1,0:T(8,128)(2,1)S(1)}, bf16[2,4,32,256]{3,2,1,0:T(8,128)(2,1)S(1)}, u32[]{:S(2)}, u32[]{:S(2)}) collective-permute-start(bf16[2,4,32,256]{3,2,1,0:T(8,128)(2,1)S(1)} %get-tuple-element.77), channel_id=1, source_target_pairs={{0,2},{1,3},{2,0},{3,1},{4,6},{5,7},{6,4},{7,5},{8,10},{9,11},{10,... | collective-permute-start | bytes 393224 | tf_op jit(solution)/shard_map/ppermute | solution.py:34
  69.9 10.0 %collective-permute-start.15 = (bf16[2,4,32,256]{3,2,1,0:T(8,128)(2,1)S(1)}, bf16[2,4,32,256]{3,2,1,0:T(8,128)(2,1)S(1)}, u32[]{:S(2)}, u32[]{:S(2)}) collective-permute-start(bf16[2,4,32,256]{3,2,1,0:T(8,128)(2,1)S(1)} %get-tuple-element.78), channel_id=1, source_target_pairs={{0,4},{1,5},{2,6},{3,7},{4,0},{5,1},{6,2},{7,3},{8,12},{9,13},{10,... | collective-permute-start | bytes 393224 | tf_op jit(solution)/shard_map/ppermute | solution.py:34
  79.9 3.6 %collective-permute-start.16 = (bf16[8,4,32,256]{3,2,1,0:T(8,128)(2,1)S(1)}, bf16[8,4,32,256]{3,2,1,0:T(8,128)(2,1)S(1)}, u32[]{:S(2)}, u32[]{:S(2)}) collective-permute-start(bf16[8,4,32,256]{3,2,1,0:T(8,128)(2,1)S(1)} %get-tuple-element.79), channel_id=1, source_target_pairs={{0,1},{1,0},{2,3},{3,2},{4,5},{5,4},{6,7},{7,6},{8,9},{9,8},{10,11... | collective-permute-start | bytes 1572872 | tf_op jit(solution)/shard_map/ppermute | solution.py:34
  80.0 31.5 %collective-permute-start.26 = (bf16[14,4,32,256]{3,2,1,0:T(8,128)(2,1)S(1)}, bf16[14,4,32,256]{3,2,1,0:T(8,128)(2,1)S(1)}, u32[]{:S(2)}, u32[]{:S(2)}) collective-permute-start(bf16[14,4,32,256]{3,2,1,0:T(8,128)(2,1)S(1)} %gather_kernel.2.first_ref), channel_id=1, source_target_pairs={{0,16},{16,0},{1,17},{17,1},{2,18},{18,2},{3,19},{19,3},{4,20},{20... | collective-permute-start | bytes 2752520 | tf_op jit(solution)/shard_map/ppermute | solution.py:17
  81.5 9.1 %collective-permute-start.25 = (bf16[2,4,32,256]{3,2,1,0:T(8,128)(2,1)S(1)}, bf16[2,4,32,256]{3,2,1,0:T(8,128)(2,1)S(1)}, u32[]{:S(2)}, u32[]{:S(2)}) collective-permute-start(bf16[2,4,32,256]{3,2,1,0:T(8,128)(2,1)S(1)} %get-tuple-element.92), channel_id=1, source_target_pairs={{0,14},{1,15},{2,12},{3,13},{4,10},{5,11},{6,8},{7,9},{8,6},{9,7},... | collective-permute-start | bytes 393224 | tf_op jit(solution)/shard_map/ppermute | solution.py:34
  83.5 18.1 %collective-permute-start.17 = (bf16[2,4,32,256]{3,2,1,0:T(8,128)(2,1)S(1)}, bf16[2,4,32,256]{3,2,1,0:T(8,128)(2,1)S(1)}, u32[]{:S(2)}, u32[]{:S(2)}) collective-permute-start(bf16[2,4,32,256]{3,2,1,0:T(8,128)(2,1)S(1)} %get-tuple-element.81), channel_id=1, source_target_pairs={{0,8},{1,9},{2,10},{3,11},{4,12},{5,13},{6,14},{7,15},{8,0},{9,1},... | collective-permute-start | bytes 393224 | tf_op jit(solution)/shard_map/ppermute | solution.py:34
  85.0 18.0 %collective-permute-start.23 = (bf16[2,4,32,256]{3,2,1,0:T(8,128)(2,1)S(1)}, bf16[2,4,32,256]{3,2,1,0:T(8,128)(2,1)S(1)}, u32[]{:S(2)}, u32[]{:S(2)}) collective-permute-start(bf16[2,4,32,256]{3,2,1,0:T(8,128)(2,1)S(1)} %get-tuple-element.90), channel_id=1, source_target_pairs={{0,10},{1,11},{2,8},{3,9},{4,14},{5,15},{6,12},{7,13},{8,2},{9,3},... | collective-permute-start | bytes 393224 | tf_op jit(solution)/shard_map/ppermute | solution.py:34
  87.2 15.8 %collective-permute-start.24 = (bf16[2,4,32,256]{3,2,1,0:T(8,128)(2,1)S(1)}, bf16[2,4,32,256]{3,2,1,0:T(8,128)(2,1)S(1)}, u32[]{:S(2)}, u32[]{:S(2)}) collective-permute-start(bf16[2,4,32,256]{3,2,1,0:T(8,128)(2,1)S(1)} %get-tuple-element.91), channel_id=1, source_target_pairs={{0,6},{1,7},{2,4},{3,5},{4,2},{5,3},{6,0},{7,1},{8,14},{9,15},{10,... | collective-permute-start | bytes 393224 | tf_op jit(solution)/shard_map/ppermute | solution.py:34
  103.1 10.5 %collective-permute-start.27 = (bf16[6,4,32,256]{3,2,1,0:T(8,128)(2,1)S(1)}, bf16[6,4,32,256]{3,2,1,0:T(8,128)(2,1)S(1)}, u32[]{:S(2)}, u32[]{:S(2)}) collective-permute-start(bf16[6,4,32,256]{3,2,1,0:T(8,128)(2,1)S(1)} %gather_kernel.3.second_ref), channel_id=1, source_target_pairs={{0,16},{16,0},{1,17},{17,1},{2,18},{18,2},{3,19},{19,3},{4,20},{20... | collective-permute-start | bytes 1179656 | tf_op jit(solution)/shard_map/ppermute | solution.py:17
  103.7 13.1 %collective-permute-start.18 = (bf16[2,4,32,256]{3,2,1,0:T(8,128)(2,1)S(1)}, bf16[2,4,32,256]{3,2,1,0:T(8,128)(2,1)S(1)}, u32[]{:S(2)}, u32[]{:S(2)}) collective-permute-start(bf16[2,4,32,256]{3,2,1,0:T(8,128)(2,1)S(1)} %get-tuple-element.82), channel_id=1, source_target_pairs={{0,12},{1,13},{2,14},{3,15},{4,8},{5,9},{6,10},{7,11},{8,4},{9,5},... | collective-permute-start | bytes 393224 | tf_op jit(solution)/shard_map/ppermute | solution.py:34
  105.2 15.1 %collective-permute-start.19 = (bf16[2,4,32,256]{3,2,1,0:T(8,128)(2,1)S(1)}, bf16[2,4,32,256]{3,2,1,0:T(8,128)(2,1)S(1)}, u32[]{:S(2)}, u32[]{:S(2)}) collective-permute-start(bf16[2,4,32,256]{3,2,1,0:T(8,128)(2,1)S(1)} %get-tuple-element.83), channel_id=1, source_target_pairs={{0,10},{1,11},{2,8},{3,9},{4,14},{5,15},{6,12},{7,13},{8,2},{9,3},... | collective-permute-start | bytes 393224 | tf_op jit(solution)/shard_map/ppermute | solution.py:34
  105.2 15.1 %collective-permute-start.20 = (bf16[2,4,32,256]{3,2,1,0:T(8,128)(2,1)S(1)}, bf16[2,4,32,256]{3,2,1,0:T(8,128)(2,1)S(1)}, u32[]{:S(2)}, u32[]{:S(2)}) collective-permute-start(bf16[2,4,32,256]{3,2,1,0:T(8,128)(2,1)S(1)} %get-tuple-element.84), channel_id=1, source_target_pairs={{0,14},{1,15},{2,12},{3,13},{4,10},{5,11},{6,8},{7,9},{8,6},{9,7},... | collective-permute-start | bytes 393224 | tf_op jit(solution)/shard_map/ppermute | solution.py:34
  111.5 9.0 %collective-permute-start.21 = (bf16[2,4,32,256]{3,2,1,0:T(8,128)(2,1)S(1)}, bf16[2,4,32,256]{3,2,1,0:T(8,128)(2,1)S(1)}, u32[]{:S(2)}, u32[]{:S(2)}) collective-permute-start(bf16[2,4,32,256]{3,2,1,0:T(8,128)(2,1)S(1)} %get-tuple-element.85), channel_id=1, source_target_pairs={{0,2},{1,3},{2,0},{3,1},{4,6},{5,7},{6,4},{7,5},{8,10},{9,11},{10,... | collective-permute-start | bytes 393224 | tf_op jit(solution)/shard_map/ppermute | solution.py:34
  113.5 8.4 %collective-permute-start.22 = (bf16[2,4,32,256]{3,2,1,0:T(8,128)(2,1)S(1)}, bf16[2,4,32,256]{3,2,1,0:T(8,128)(2,1)S(1)}, u32[]{:S(2)}, u32[]{:S(2)}) collective-permute-start(bf16[2,4,32,256]{3,2,1,0:T(8,128)(2,1)S(1)} %get-tuple-element.86), channel_id=1, source_target_pairs={{0,4},{1,5},{2,6},{3,7},{4,0},{5,1},{6,2},{7,3},{8,12},{9,13},{10,... | collective-permute-start | bytes 393224 | tf_op jit(solution)/shard_map/ppermute | solution.py:34
  114.4 10.9 %copy-start.3 = (bf16[1,2048,256]{2,1,0:T(8,128)(2,1)S(1)}, bf16[1,2048,256]{2,1,0:T(8,128)(2,1)}, u32[]{:S(2)}) copy-start(bf16[1,2048,256]{2,1,0:T(8,128)(2,1)} %param.6) | copy-start | bytes 3145732
  114.4 10.9 %copy-start.4 = (bf16[1,2048,256]{2,1,0:T(8,128)(2,1)S(1)}, bf16[1,2048,256]{2,1,0:T(8,128)(2,1)}, u32[]{:S(2)}) copy-start(bf16[1,2048,256]{2,1,0:T(8,128)(2,1)} %param.7) | copy-start | bytes 3145732
  116.8 8.5 %collective-permute-start.28 = (bf16[2,4,32,256]{3,2,1,0:T(8,128)(2,1)S(1)}, bf16[2,4,32,256]{3,2,1,0:T(8,128)(2,1)S(1)}, u32[]{:S(2)}, u32[]{:S(2)}) collective-permute-start(bf16[2,4,32,256]{3,2,1,0:T(8,128)(2,1)S(1)} %get-tuple-element.96), channel_id=1, source_target_pairs={{0,6},{1,7},{2,4},{3,5},{4,2},{5,3},{6,0},{7,1},{8,14},{9,15},{10,... | collective-permute-start | bytes 393224 | tf_op jit(solution)/shard_map/ppermute | solution.py:34

commit v14 on v13

--- a/solution.py
+++ b/solution.py
@@ -25,8 +25,7 @@
     half = chips // 2
     near = list(range(1, half))
     far = list(range(half, chips, 2)) + list(range(half + 1, chips, 2))
-    mixed = far[:2] + near[:-1] + far[2:-1] + near[-1:] + far[-1:]
-    return [0] + far[:1] + near + far[1:], [0] + mixed, [0] + far + near
+    return [0] + far[:1] + near + far[1:], [0] + near + far, [0] + far + near
 
 
 def permute(array, offset):
@@ -171,7 +170,7 @@
     send_columns(wide_out, block_views(me, out_refs))
 
 
-def column_forward_kernel(order, me_ref, right_ref, grad_ref, after_ref, *refs):
+def column_forward_kernel(order, me_ref, right_ref, grad_ref, *refs):
     chips = len(order)
     in_refs, out_refs = refs[:chips], refs[chips : chips + 2]
     packed_ref, wide, wide_out = refs[chips + 2 :]
@@ -281,7 +280,7 @@
     def shape(*dims):
         return jax.ShapeDtypeStruct(dims, BF16)
 
-    one_ahead, two_ahead, all_far = orders(chips)
+    one_ahead, near_ahead, all_far = orders(chips)
 
     def ordered(kernel, order):
         return functools.partial(kernel, order)
@@ -319,9 +318,13 @@
         [own, permute(other, 1), own_mixed, permute(other_mixed, 1)],
         [shape(2, 2, *block)] * last + [shape(2, *block)] * 2,
     )
-    other_values = swap_sequences(after(values, messages[0]))
-    columns = listed(exchange(messages), one_ahead)
-    mixed_last = permute(after(mixed_last, columns[1:-2] + columns[-1:]), 2 * last)
+    done = [(t, permute(messages[t], 2 * t)) for t in (one_ahead[2], one_ahead[3])]
+    messages[one_ahead[-2]] = after(messages[one_ahead[-2]], done[0][1])
+    messages[last] = after(messages[last], done[1][1])
+    columns = listed(exchange(messages, done), one_ahead)
+    other_values = swap_sequences(after(values, columns[-3]))
+    in_before = [*columns[1:-2], columns[-1]]
+    mixed_last = permute(after(mixed_last, in_before), 2 * last)
     own, other, grad_column = call(
         ordered(column_backward_kernel, one_ahead),
         me,
@@ -336,15 +339,14 @@
     own, other, right_part = call(
         ordered(column_forward_kernel, one_ahead),
         me,
-        [right_factor, grad_column, other_values, *columns],
+        [right_factor, grad_column, *columns],
         [shape(chips, *block)] * 2 + [packed_right],
         [wide, wide],
         2 * column_flops,
-        unblocked=[2],
-    )
-    back = listed(back, two_ahead)
-    ahead = chips // 2 + 1
-    messages = pack(own, permute(after(other, back[1:ahead]), 1))
+    )
+    back = listed(back, near_ahead)
+    ahead = chips // 2
+    messages = pack(own, permute(after(other, [other_values, *back[1 : ahead + 2]]), 1))
     done = [(t, permute(messages[t], 2 * t)) for t in all_far[1:2]]
     back[-1] = after(back[-1], [block for _, block in done])
     extra = packed_right.size // math.prod(block)
@@ -357,7 +359,7 @@
     other_first = swap_sequences(first_part)
     other_second = swap_sequences(second_part)
     grad_signal, left_term = call(
-        ordered(row_backward_kernel, two_ahead),
+        ordered(row_backward_kernel, near_ahead),
         me,
         [left_factor, values, first_part, second_part],
         [by_row, left],
@@ -365,7 +367,7 @@
         2 * row_flops,
     )
     grad_left, grad_right = call(
-        ordered(factor_sum_kernel, two_ahead),
+        ordered(factor_sum_kernel, near_ahead),
         me,
         [left_term, other_values, other_first, other_second, right_part],
         [left, right],

time: 127 us -> 128 us (level)
  starting transfers between devices: 44.5 us -> 52 us
  waiting for transfers between devices: 63.9 us -> 57.7 us
    ppermute x26, waiting for transfers between devices: 61.8 us -> 52.6 us  [permute(): return lax.ppermute(array, 'seq', [(i, i ^ offset) for i in range(seq)])]
    ppermute x26, starting transfers between devices: 40.9 us -> 48.4 us  [permute(): return lax.ppermute(array, 'seq', [(i, i ^ offset) for i in range(seq)])]
    ppermute x3, waiting for transfers between devices: 2.04 us -> 5.1 us  [swap_sequences(): return lax.ppermute(array, 'dp', [(0, 1), (1, 0)])]
  transfers between devices with their start and end apart: 29 -> 29, of which waited for: 16 -> 14; matrix products, arithmetic and copies ran while one was open for 0% -> 0% of each run, Pallas kernels for 9% -> 9%
where the time goes in v14:
time: 128 us
  waiting for transfers between devices  57.7 us (45%)
  starting transfers between devices  52 us (41%)
  Pallas kernels  16.6 us (13%)
    ppermute x26, waiting for transfers between devices, permute(): return lax.ppermute(array, 'seq', [(i, i ^ offset) for i in range(seq)])  52.6 us
    ppermute x26, starting transfers between devices, permute(): return lax.ppermute(array, 'seq', [(i, i ^ offset) for i in range(seq)])  48.4 us
    pallas_call x12, Pallas kernels, call(): pl.pallas_call(kernel, out_shape=out_shapes, in_specs=[pl.BlockSpec(memor...  16.6 us
    ppermute x3, waiting for transfers between devices, swap_sequences(): return lax.ppermute(array, 'dp', [(0, 1), (1, 0)])  5.1 us
    ppermute x3, starting transfers between devices, swap_sequences(): return lax.ppermute(array, 'dp', [(0, 1), (1, 0)])  3.65 us
  transfers between devices with their start and end apart: 29, of which 14 were waited for; matrix products, arithmetic and copies ran while one was open for 0% of the time, Pallas kernels for 9%

profile of v14, /device:TPU:0, one launch (start us, length us, event | category | flops | bytes accessed | tf_op | source)
XLA Modules:
  0.0 128.3 jit_solution(15955046756044990585)
XLA Ops:
  0.6 2.7 %product_kernel.1 = (bf16[8,4,32,256]{3,2,1,0:T(8,128)(2,1)}, bf16[8,4,32,256]{3,2,1,0:T(8,128)(2,1)}) custom-call(s32[1]{0:T(128)} %bitcast.me_ref, bf16[4,16,32,256]{3,2,1,0:T(8,128)(2,1)} %bitcast.10, bf16[4,16,32,256]{3,2,1,0:T(8,128)(2,1)} %bitcast.12), custom_call_target="tpu_custom_call" | custom-call | bytes 3145728 | tf_op jit(solution)/shard_map/product_kernel/pallas_call | solution.py:54
  3.4 0.5 collective-permute-start
  3.9 1.2 copy-done.1
  5.1 0.8 mix_kernel.1
  5.9 0.1 collective-permute-start.1
  6.0 1.9 %collective-permute-done.1.refs_3_ = bf16[8,4,32,256]{3,2,1,0:T(8,128)(2,1)S(1)} collective-permute-done((bf16[8,4,32,256]{3,2,1,0:T(8,128)(2,1)S(1)}, bf16[8,4,32,256]{3,2,1,0:T(8,128)(2,1)S(1)}, u32[]{:S(2)}, u32[]{:S(2)}) %collective-permute-start.1) | collective-permute-done | bytes 524320 | tf_op jit(solution)/shard_map/ppermute | solution.py:33
  7.9 0.1 pack_pairs_kernel.1
  8.0 2.7 %collective-permute-start.3 = (bf16[2,2,4,32,256]{4,3,2,1,0:T(8,128)(2,1)S(1)}, bf16[2,2,4,32,256]{4,3,2,1,0:T(8,128)(2,1)S(1)}, u32[]{:S(2)}, u32[]{:S(2)}) collective-permute-start(bf16[2,2,4,32,256]{4,3,2,1,0:T(8,128)(2,1)S(1)} %get-tuple-element.62), channel_id=1, source_target_pairs={{0,2},{1,3},{2,0},{3,1},{4,6},{5,7},{6,4},{7,5},{8,10},{9,11},{10,... | collective-permute-start | bytes 786440 | tf_op jit(solution)/shard_map/ppermute | solution.py:33
  10.8 1.6 %collective-permute-start.4 = (bf16[2,2,4,32,256]{4,3,2,1,0:T(8,128)(2,1)S(1)}, bf16[2,2,4,32,256]{4,3,2,1,0:T(8,128)(2,1)S(1)}, u32[]{:S(2)}, u32[]{:S(2)}) collective-permute-start(bf16[2,2,4,32,256]{4,3,2,1,0:T(8,128)(2,1)S(1)} %get-tuple-element.63), channel_id=1, source_target_pairs={{0,4},{1,5},{2,6},{3,7},{4,0},{5,1},{6,2},{7,3},{8,12},{9,13},{10,... | collective-permute-start | bytes 786440 | tf_op jit(solution)/shard_map/ppermute | solution.py:33
  12.3 2.5 %collective-permute-start.6 = (bf16[2,2,4,32,256]{4,3,2,1,0:T(8,128)(2,1)S(1)}, bf16[2,2,4,32,256]{4,3,2,1,0:T(8,128)(2,1)S(1)}, u32[]{:S(2)}, u32[]{:S(2)}) collective-permute-start(bf16[2,2,4,32,256]{4,3,2,1,0:T(8,128)(2,1)S(1)} %get-tuple-element.65), channel_id=1, source_target_pairs={{0,12},{1,13},{2,14},{3,15},{4,8},{5,9},{6,10},{7,11},{8,4},{9,5},... | collective-permute-start | bytes 786440 | tf_op jit(solution)/shard_map/ppermute | solution.py:33
  14.8 0.1 collective-permute-start.2
  14.9 1.7 %collective-permute-start.5 = (bf16[2,2,4,32,256]{4,3,2,1,0:T(8,128)(2,1)S(1)}, bf16[2,2,4,32,256]{4,3,2,1,0:T(8,128)(2,1)S(1)}, u32[]{:S(2)}, u32[]{:S(2)}) collective-permute-start(bf16[2,2,4,32,256]{4,3,2,1,0:T(8,128)(2,1)S(1)} %get-tuple-element.64), channel_id=1, source_target_pairs={{0,6},{1,7},{2,4},{3,5},{4,2},{5,3},{6,0},{7,1},{8,14},{9,15},{10,... | collective-permute-start | bytes 786440 | tf_op jit(solution)/shard_map/ppermute | solution.py:33
  16.7 0.9 collective-permute-done.3.refs_2_
  17.6 3.8 %collective-permute-start.7 = (bf16[2,2,4,32,256]{4,3,2,1,0:T(8,128)(2,1)S(1)}, bf16[2,2,4,32,256]{4,3,2,1,0:T(8,128)(2,1)S(1)}, u32[]{:S(2)}, u32[]{:S(2)}) collective-permute-start(bf16[2,2,4,32,256]{4,3,2,1,0:T(8,128)(2,1)S(1)} %get-tuple-element.67), channel_id=1, source_target_pairs={{0,10},{1,11},{2,8},{3,9},{4,14},{5,15},{6,12},{7,13},{8,2},{9,3},... | collective-permute-start | bytes 786440 | tf_op jit(solution)/shard_map/ppermute | solution.py:33
  21.4 7.7 %collective-permute-start.8 = (bf16[2,4,32,256]{3,2,1,0:T(8,128)(2,1)S(1)}, bf16[2,4,32,256]{3,2,1,0:T(8,128)(2,1)S(1)}, u32[]{:S(2)}, u32[]{:S(2)}) collective-permute-start(bf16[2,4,32,256]{3,2,1,0:T(8,128)(2,1)S(1)} %get-tuple-element.69), channel_id=1, source_target_pairs={{0,14},{1,15},{2,12},{3,13},{4,10},{5,11},{6,8},{7,9},{8,6},{9,7},... | collective-permute-start | bytes 393224 | tf_op jit(solution)/shard_map/ppermute | solution.py:33
  29.1 1.5 %collective-permute-start.10 = (bf16[4,512,256]{2,1,0:T(8,128)(2,1)S(1)}, bf16[4,512,256]{2,1,0:T(8,128)(2,1)S(1)}, u32[]{:S(2)}, u32[]{:S(2)}) collective-permute-start(bf16[4,512,256]{2,1,0:T(8,128)(2,1)S(1)} %bitcast.8), channel_id=1, source_target_pairs={{0,16},{16,0},{1,17},{17,1},{2,18},{18,2},{3,19},{19,3},{4,20},{20... | collective-permute-start | bytes 3145736 | tf_op jit(solution)/shard_map/ppermute | solution.py:17
  30.6 16.8 %collective-permute-done.2.refs_1_ = bf16[2,2,4,32,256]{4,3,2,1,0:T(8,128)(2,1)S(1)} collective-permute-done((bf16[2,2,4,32,256]{4,3,2,1,0:T(8,128)(2,1)S(1)}, bf16[2,2,4,32,256]{4,3,2,1,0:T(8,128)(2,1)S(1)}, u32[]{:S(2)}, u32[]{:S(2)}) %collective-permute-start.2) | collective-permute-done | bytes 262176 | tf_op jit(solution)/shard_map/ppermute | solution.py:33
  47.4 2.9 %collective-permute-start.9 = (bf16[2,4,32,256]{3,2,1,0:T(8,128)(2,1)S(1)}, bf16[2,4,32,256]{3,2,1,0:T(8,128)(2,1)S(1)}, u32[]{:S(2)}, u32[]{:S(2)}) collective-permute-start(bf16[2,4,32,256]{3,2,1,0:T(8,128)(2,1)S(1)} %get-tuple-element.72), channel_id=1, source_target_pairs={{0,14},{1,15},{2,12},{3,13},{4,10},{5,11},{6,8},{7,9},{8,6},{9,7},... | collective-permute-start | bytes 393224 | tf_op jit(solution)/shard_map/ppermute | solution.py:33
  50.3 5.5 %collective-permute-done.7.refs_6_ = bf16[2,2,4,32,256]{4,3,2,1,0:T(8,128)(2,1)S(1)} collective-permute-done((bf16[2,2,4,32,256]{4,3,2,1,0:T(8,128)(2,1)S(1)}, bf16[2,2,4,32,256]{4,3,2,1,0:T(8,128)(2,1)S(1)}, u32[]{:S(2)}, u32[]{:S(2)}) %collective-permute-start.7) | collective-permute-done | bytes 262176 | tf_op jit(solution)/shard_map/ppermute | solution.py:33
  55.7 3.0 %column_backward_kernel.1 = (bf16[8,4,32,256]{3,2,1,0:T(8,128)(2,1)S(1)}, bf16[8,4,32,256]{3,2,1,0:T(8,128)(2,1)S(1)}, bf16[32,64,256]{2,1,0:T(8,128)(2,1)S(1)}) custom-call(s32[1]{0:T(128)} %bitcast.me_ref, bf16[32,64,64]{2,1,0:T(8,128)(2,1)S(1)} %copy-done.5, bf16[2,2,4,32,256]{4,3,2,1,0:T(8,128)(2,1)S(1)} %get-tuple-element.60.refs_0_, ...), custom_call_target="tpu_custom_call" | custom-call | flops 67108864 | bytes 4325376 | tf_op jit(solution)/shard_map/column_backward_kernel/pallas_call | solution.py:54
  58.7 0.1 collective-permute-start.11
  58.8 1.9 %collective-permute-done.11.other_ref = bf16[8,4,32,256]{3,2,1,0:T(8,128)(2,1)S(1)} collective-permute-done((bf16[8,4,32,256]{3,2,1,0:T(8,128)(2,1)S(1)}, bf16[8,4,32,256]{3,2,1,0:T(8,128)(2,1)S(1)}, u32[]{:S(2)}, u32[]{:S(2)}) %collective-permute-start.11) | collective-permute-done | bytes 524320 | tf_op jit(solution)/shard_map/ppermute | solution.py:33
  60.7 1.6 %collective-permute-start.12 = (bf16[2,4,32,256]{3,2,1,0:T(8,128)(2,1)S(1)}, bf16[2,4,32,256]{3,2,1,0:T(8,128)(2,1)S(1)}, u32[]{:S(2)}, u32[]{:S(2)}) collective-permute-start(bf16[2,4,32,256]{3,2,1,0:T(8,128)(2,1)S(1)} %get-tuple-element.79), channel_id=1, source_target_pairs={{0,2},{1,3},{2,0},{3,1},{4,6},{5,7},{6,4},{7,5},{8,10},{9,11},{10,... | collective-permute-start | bytes 393224 | tf_op jit(solution)/shard_map/ppermute | solution.py:33
  62.3 5.3 %collective-permute-start.13 = (bf16[2,4,32,256]{3,2,1,0:T(8,128)(2,1)S(1)}, bf16[2,4,32,256]{3,2,1,0:T(8,128)(2,1)S(1)}, u32[]{:S(2)}, u32[]{:S(2)}) collective-permute-start(bf16[2,4,32,256]{3,2,1,0:T(8,128)(2,1)S(1)} %get-tuple-element.80), channel_id=1, source_target_pairs={{0,4},{1,5},{2,6},{3,7},{4,0},{5,1},{6,2},{7,3},{8,12},{9,13},{10,... | collective-permute-start | bytes 393224 | tf_op jit(solution)/shard_map/ppermute | solution.py:33
  67.7 3.1 %collective-permute-start.15 = (bf16[2,4,32,256]{3,2,1,0:T(8,128)(2,1)S(1)}, bf16[2,4,32,256]{3,2,1,0:T(8,128)(2,1)S(1)}, u32[]{:S(2)}, u32[]{:S(2)}) collective-permute-start(bf16[2,4,32,256]{3,2,1,0:T(8,128)(2,1)S(1)} %get-tuple-element.82), channel_id=1, source_target_pairs={{0,8},{1,9},{2,10},{3,11},{4,12},{5,13},{6,14},{7,15},{8,0},{9,1},... | collective-permute-start | bytes 393224 | tf_op jit(solution)/shard_map/ppermute | solution.py:33
  70.8 1.2 collective-permute-start.16
  72.0 3.3 %column_forward_kernel.1 = (bf16[8,4,32,256]{3,2,1,0:T(8,128)(2,1)S(1)}, bf16[8,4,32,256]{3,2,1,0:T(8,128)(2,1)S(1)}, bf16[512,256]{1,0:T(8,128)(2,1)S(1)}) custom-call(s32[1]{0:T(128)} %bitcast.me_ref, bf16[32,64,64]{2,1,0:T(8,128)(2,1)S(1)} %copy-done.5, bf16[32,64,256]{2,1,0:T(8,128)(2,1)S(1)} %get-tuple-element.70.grad_ref, ...), custom_call_target="tpu_custom_call" | custom-call | flops 134217728 | bytes 4587520 | tf_op jit(solution)/shard_map/column_forward_kernel/pallas_call | solution.py:54
  75.3 1.4 %collective-permute-done.14.refs_3_ = bf16[2,4,32,256]{3,2,1,0:T(8,128)(2,1)S(1)} collective-permute-done((bf16[2,4,32,256]{3,2,1,0:T(8,128)(2,1)S(1)}, bf16[2,4,32,256]{3,2,1,0:T(8,128)(2,1)S(1)}, u32[]{:S(2)}, u32[]{:S(2)}) %collective-permute-start.14) | collective-permute-done | bytes 131104 | tf_op jit(solution)/shard_map/ppermute | solution.py:33
  76.7 0.5 collective-permute-done.15.refs_0_
  77.2 4.8 %collective-permute-done.16.refs_1_ = bf16[2,4,32,256]{3,2,1,0:T(8,128)(2,1)S(1)} collective-permute-done((bf16[2,4,32,256]{3,2,1,0:T(8,128)(2,1)S(1)}, bf16[2,4,32,256]{3,2,1,0:T(8,128)(2,1)S(1)}, u32[]{:S(2)}, u32[]{:S(2)}) %collective-permute-start.16) | collective-permute-done | bytes 131104 | tf_op jit(solution)/shard_map/ppermute | solution.py:33
  82.1 1.6 %collective-permute-start.26 = (bf16[12,4,32,256]{3,2,1,0:T(8,128)(2,1)S(1)}, bf16[12,4,32,256]{3,2,1,0:T(8,128)(2,1)S(1)}, u32[]{:S(2)}, u32[]{:S(2)}) collective-permute-start(bf16[12,4,32,256]{3,2,1,0:T(8,128)(2,1)S(1)} %gather_kernel.2.first_ref), channel_id=1, source_target_pairs={{0,16},{16,0},{1,17},{17,1},{2,18},{18,2},{3,19},{19,3},{4,20},{20... | collective-permute-start | bytes 2359304 | tf_op jit(solution)/shard_map/ppermute | solution.py:17
  83.7 1.4 %collective-permute-start.25 = (bf16[2,4,32,256]{3,2,1,0:T(8,128)(2,1)S(1)}, bf16[2,4,32,256]{3,2,1,0:T(8,128)(2,1)S(1)}, u32[]{:S(2)}, u32[]{:S(2)}) collective-permute-start(bf16[2,4,32,256]{3,2,1,0:T(8,128)(2,1)S(1)} %get-tuple-element.96), channel_id=1, source_target_pairs={{0,14},{1,15},{2,12},{3,13},{4,10},{5,11},{6,8},{7,9},{8,6},{9,7},... | collective-permute-start | bytes 393224 | tf_op jit(solution)/shard_map/ppermute | solution.py:33
  85.1 1.9 %collective-permute-start.18 = (bf16[2,4,32,256]{3,2,1,0:T(8,128)(2,1)S(1)}, bf16[2,4,32,256]{3,2,1,0:T(8,128)(2,1)S(1)}, u32[]{:S(2)}, u32[]{:S(2)}) collective-permute-start(bf16[2,4,32,256]{3,2,1,0:T(8,128)(2,1)S(1)} %get-tuple-element.86), channel_id=1, source_target_pairs={{0,8},{1,9},{2,10},{3,11},{4,12},{5,13},{6,14},{7,15},{8,0},{9,1},... | collective-permute-start | bytes 393224 | tf_op jit(solution)/shard_map/ppermute | solution.py:33
  87.0 1.9 %collective-permute-start.24 = (bf16[2,4,32,256]{3,2,1,0:T(8,128)(2,1)S(1)}, bf16[2,4,32,256]{3,2,1,0:T(8,128)(2,1)S(1)}, u32[]{:S(2)}, u32[]{:S(2)}) collective-permute-start(bf16[2,4,32,256]{3,2,1,0:T(8,128)(2,1)S(1)} %get-tuple-element.95), channel_id=1, source_target_pairs={{0,10},{1,11},{2,8},{3,9},{4,14},{5,15},{6,12},{7,13},{8,2},{9,3},... | collective-permute-start | bytes 393224 | tf_op jit(solution)/shard_map/ppermute | solution.py:33
  88.8 4.0 %collective-permute-done.25.refs_3_ = bf16[2,4,32,256]{3,2,1,0:T(8,128)(2,1)S(1)} collective-permute-done((bf16[2,4,32,256]{3,2,1,0:T(8,128)(2,1)S(1)}, bf16[2,4,32,256]{3,2,1,0:T(8,128)(2,1)S(1)}, u32[]{:S(2)}, u32[]{:S(2)}) %collective-permute-start.25) | collective-permute-done | bytes 131104 | tf_op jit(solution)/shard_map/ppermute | solution.py:33
  92.8 9.5 %collective-permute-done.18.refs_1_ = bf16[2,4,32,256]{3,2,1,0:T(8,128)(2,1)S(1)} collective-permute-done((bf16[2,4,32,256]{3,2,1,0:T(8,128)(2,1)S(1)}, bf16[2,4,32,256]{3,2,1,0:T(8,128)(2,1)S(1)}, u32[]{:S(2)}, u32[]{:S(2)}) %collective-permute-start.18) | collective-permute-done | bytes 131104 | tf_op jit(solution)/shard_map/ppermute | solution.py:33
  102.3 2.1 %collective-permute-done.24.refs_2_ = bf16[2,4,32,256]{3,2,1,0:T(8,128)(2,1)S(1)} collective-permute-done((bf16[2,4,32,256]{3,2,1,0:T(8,128)(2,1)S(1)}, bf16[2,4,32,256]{3,2,1,0:T(8,128)(2,1)S(1)}, u32[]{:S(2)}, u32[]{:S(2)}) %collective-permute-start.24) | collective-permute-done | bytes 131104 | tf_op jit(solution)/shard_map/ppermute | solution.py:33
  104.5 0.6 collective-permute-start.27
  105.1 2.4 %collective-permute-start.19 = (bf16[2,4,32,256]{3,2,1,0:T(8,128)(2,1)S(1)}, bf16[2,4,32,256]{3,2,1,0:T(8,128)(2,1)S(1)}, u32[]{:S(2)}, u32[]{:S(2)}) collective-permute-start(bf16[2,4,32,256]{3,2,1,0:T(8,128)(2,1)S(1)} %get-tuple-element.87), channel_id=1, source_target_pairs={{0,12},{1,13},{2,14},{3,15},{4,8},{5,9},{6,10},{7,11},{8,4},{9,5},... | collective-permute-start | bytes 393224 | tf_op jit(solution)/shard_map/ppermute | solution.py:33
  107.5 2.4 %collective-permute-start.21 = (bf16[2,4,32,256]{3,2,1,0:T(8,128)(2,1)S(1)}, bf16[2,4,32,256]{3,2,1,0:T(8,128)(2,1)S(1)}, u32[]{:S(2)}, u32[]{:S(2)}) collective-permute-start(bf16[2,4,32,256]{3,2,1,0:T(8,128)(2,1)S(1)} %get-tuple-element.89), channel_id=1, source_target_pairs={{0,14},{1,15},{2,12},{3,13},{4,10},{5,11},{6,8},{7,9},{8,6},{9,7},... | collective-permute-start | bytes 393224 | tf_op jit(solution)/shard_map/ppermute | solution.py:33
  109.8 2.3 %row_backward_kernel.1 = (bf16[4,512,256]{2,1,0:T(8,128)(2,1)}, bf16[4,512,512]{2,1,0:T(8,128)(2,1)S(1)}) custom-call(s32[1]{0:T(128)} %bitcast.me_ref, bf16[4,512,512]{2,1,0:T(8,128)(2,1)S(1)} %copy-done, bf16[4,512,256]{2,1,0:T(8,128)(2,1)S(1)} %bitcast.9, bf16[12,4,32,256]{3,2,1,0:T(8,128)(2,1)S(1)} %gather_kernel.2.first_ref, ...), custom_call_target="tpu_custom_call" | custom-call | flops 1073741824 | bytes 7602176 | tf_op jit(solution)/shard_map/row_backward_kernel/pallas_call | solution.py:54
  112.2 0.5 collective-permute-start.22
  112.7 5.1 %collective-permute-done.27.second_ref = bf16[8,4,32,256]{3,2,1,0:T(8,128)(2,1)S(1)} collective-permute-done((bf16[8,4,32,256]{3,2,1,0:T(8,128)(2,1)S(1)}, bf16[8,4,32,256]{3,2,1,0:T(8,128)(2,1)S(1)}, u32[]{:S(2)}, u32[]{:S(2)}) %collective-permute-start.27) | collective-permute-done | bytes 524320 | tf_op jit(solution)/shard_map/ppermute | solution.py:17
  117.8 2.4 %factor_sum_kernel.1 = (bf16[4,512,512]{2,1,0:T(8,128)(2,1)}, bf16[32,64,64]{2,1,0:T(8,128)(2,1)}) custom-call(s32[1]{0:T(128)} %bitcast.me_ref, bf16[4,512,512]{2,1,0:T(8,128)(2,1)S(1)} %get-tuple-element.98.term_ref, bf16[4,512,256]{2,1,0:T(8,128)(2,1)S(1)} %collective-permute-done.10.values_ref, ...), custom_call_target="tpu_custom_call" | custom-call | flops 536870912 | bytes 7077888 | tf_op jit(solution)/shard_map/factor_sum_kernel/pallas_call | solution.py:54
  120.2 3.0 %collective-permute-start.28 = (bf16[2,4,32,256]{3,2,1,0:T(8,128)(2,1)S(1)}, bf16[2,4,32,256]{3,2,1,0:T(8,128)(2,1)S(1)}, u32[]{:S(2)}, u32[]{:S(2)}) collective-permute-start(bf16[2,4,32,256]{3,2,1,0:T(8,128)(2,1)S(1)} %get-tuple-element.100), channel_id=1, source_target_pairs={{0,6},{1,7},{2,4},{3,5},{4,2},{5,3},{6,0},{7,1},{8,14},{9,15},{10,... | collective-permute-start | bytes 393224 | tf_op jit(solution)/shard_map/ppermute | solution.py:33
  123.2 0.5 collective-permute-done.23.refs_6_
  123.7 2.9 %collective-permute-done.28.refs_7_ = bf16[2,4,32,256]{3,2,1,0:T(8,128)(2,1)S(1)} collective-permute-done((bf16[2,4,32,256]{3,2,1,0:T(8,128)(2,1)S(1)}, bf16[2,4,32,256]{3,2,1,0:T(8,128)(2,1)S(1)}, u32[]{:S(2)}, u32[]{:S(2)}) %collective-permute-start.28) | collective-permute-done | bytes 131104 | tf_op jit(solution)/shard_map/ppermute | solution.py:33
  126.5 1.8 %output_kernel.1 = (bf16[4,16,32,256]{3,2,1,0:T(8,128)(2,1)}, bf16[4,16,32,256]{3,2,1,0:T(8,128)(2,1)}) custom-call(s32[1]{0:T(128)} %bitcast.me_ref, bf16[4,16,32,256]{3,2,1,0:T(8,128)(2,1)S(1)} %bitcast.11, bf16[4,16,32,256]{3,2,1,0:T(8,128)(2,1)S(1)} %bitcast.13, bf16[2,4,32,256]{3,2,1,0:T(8,128)(2,1)S(1)} %get-tuple-element.85.refs_0_, ...), custom_call_target="tpu_custom_call" | custom-call | bytes 5242880 | tf_op jit(solution)/shard_map/output_kernel/pallas_call | solution.py:54
  (36 shorter events, 0.3 us)
Async XLA Ops:
  0.6 3.3 %copy-start = (bf16[4,512,512]{2,1,0:T(8,128)(2,1)S(1)}, bf16[4,512,512]{2,1,0:T(8,128)(2,1)}, u32[]{:S(2)}) copy-start(bf16[4,512,512]{2,1,0:T(8,128)(2,1)} %left_ref.3) | copy-start | bytes 6291460
  3.4 2.7 %collective-permute-start = (bf16[8,4,32,256]{3,2,1,0:T(8,128)(2,1)}, bf16[8,4,32,256]{3,2,1,0:T(8,128)(2,1)S(1)}, u32[]{:S(2)}, u32[]{:S(2)}) collective-permute-start(bf16[8,4,32,256]{3,2,1,0:T(8,128)(2,1)} %get-tuple-element.56), channel_id=1, source_target_pairs={{0,1},{1,0},{2,3},{3,2},{4,5},{5,4},{6,7},{7,6},{8,9},{9,8},{10,11... | collective-permute-start | bytes 1572872 | tf_op jit(solution)/shard_map/ppermute | solution.py:33
  3.9 1.2 copy-start.1
  5.1 2.8 %copy-start.6 = (bf16[8,4,32,256]{3,2,1,0:T(8,128)(2,1)S(1)}, bf16[8,4,32,256]{3,2,1,0:T(8,128)(2,1)}, u32[]{:S(2)}) copy-start(bf16[8,4,32,256]{3,2,1,0:T(8,128)(2,1)} %get-tuple-element.55.refs_0_) | copy-start | bytes 1572868
  5.1 24.0 %copy-start.2 = (bf16[1,2048,256]{2,1,0:T(8,128)(2,1)S(1)}, bf16[1,2048,256]{2,1,0:T(8,128)(2,1)}, u32[]{:S(2)}) copy-start(bf16[1,2048,256]{2,1,0:T(8,128)(2,1)} %param.5) | copy-start | bytes 3145732
  5.1 50.6 %copy-start.5 = (bf16[32,64,64]{2,1,0:T(8,128)(2,1)S(1)}, bf16[32,64,64]{2,1,0:T(8,128)(2,1)}, u32[]{:S(2)}) copy-start(bf16[32,64,64]{2,1,0:T(8,128)(2,1)} %right_ref.3) | copy-start | bytes 786436
  5.9 2.0 %collective-permute-start.1 = (bf16[8,4,32,256]{3,2,1,0:T(8,128)(2,1)S(1)}, bf16[8,4,32,256]{3,2,1,0:T(8,128)(2,1)S(1)}, u32[]{:S(2)}, u32[]{:S(2)}) collective-permute-start(bf16[8,4,32,256]{3,2,1,0:T(8,128)(2,1)S(1)} %get-tuple-element.59), channel_id=1, source_target_pairs={{0,1},{1,0},{2,3},{3,2},{4,5},{5,4},{6,7},{7,6},{8,9},{9,8},{10,11... | collective-permute-start | bytes 1572872 | tf_op jit(solution)/shard_map/ppermute | solution.py:33
  8.0 9.6 %collective-permute-start.3 = (bf16[2,2,4,32,256]{4,3,2,1,0:T(8,128)(2,1)S(1)}, bf16[2,2,4,32,256]{4,3,2,1,0:T(8,128)(2,1)S(1)}, u32[]{:S(2)}, u32[]{:S(2)}) collective-permute-start(bf16[2,2,4,32,256]{4,3,2,1,0:T(8,128)(2,1)S(1)} %get-tuple-element.62), channel_id=1, source_target_pairs={{0,2},{1,3},{2,0},{3,1},{4,6},{5,7},{6,4},{7,5},{8,10},{9,11},{10,... | collective-permute-start | bytes 786440 | tf_op jit(solution)/shard_map/ppermute | solution.py:33
  10.8 10.6 %collective-permute-start.4 = (bf16[2,2,4,32,256]{4,3,2,1,0:T(8,128)(2,1)S(1)}, bf16[2,2,4,32,256]{4,3,2,1,0:T(8,128)(2,1)S(1)}, u32[]{:S(2)}, u32[]{:S(2)}) collective-permute-start(bf16[2,2,4,32,256]{4,3,2,1,0:T(8,128)(2,1)S(1)} %get-tuple-element.63), channel_id=1, source_target_pairs={{0,4},{1,5},{2,6},{3,7},{4,0},{5,1},{6,2},{7,3},{8,12},{9,13},{10,... | collective-permute-start | bytes 786440 | tf_op jit(solution)/shard_map/ppermute | solution.py:33
  12.3 16.8 %collective-permute-start.6 = (bf16[2,2,4,32,256]{4,3,2,1,0:T(8,128)(2,1)S(1)}, bf16[2,2,4,32,256]{4,3,2,1,0:T(8,128)(2,1)S(1)}, u32[]{:S(2)}, u32[]{:S(2)}) collective-permute-start(bf16[2,2,4,32,256]{4,3,2,1,0:T(8,128)(2,1)S(1)} %get-tuple-element.65), channel_id=1, source_target_pairs={{0,12},{1,13},{2,14},{3,15},{4,8},{5,9},{6,10},{7,11},{8,4},{9,5},... | collective-permute-start | bytes 786440 | tf_op jit(solution)/shard_map/ppermute | solution.py:33
  14.8 32.5 %collective-permute-start.2 = (bf16[2,2,4,32,256]{4,3,2,1,0:T(8,128)(2,1)S(1)}, bf16[2,2,4,32,256]{4,3,2,1,0:T(8,128)(2,1)S(1)}, u32[]{:S(2)}, u32[]{:S(2)}) collective-permute-start(bf16[2,2,4,32,256]{4,3,2,1,0:T(8,128)(2,1)S(1)} %get-tuple-element.61), channel_id=1, source_target_pairs={{0,8},{1,9},{2,10},{3,11},{4,12},{5,13},{6,14},{7,15},{8,0},{9,1},... | collective-permute-start | bytes 786440 | tf_op jit(solution)/shard_map/ppermute | solution.py:33
  14.9 32.4 %collective-permute-start.5 = (bf16[2,2,4,32,256]{4,3,2,1,0:T(8,128)(2,1)S(1)}, bf16[2,2,4,32,256]{4,3,2,1,0:T(8,128)(2,1)S(1)}, u32[]{:S(2)}, u32[]{:S(2)}) collective-permute-start(bf16[2,2,4,32,256]{4,3,2,1,0:T(8,128)(2,1)S(1)} %get-tuple-element.64), channel_id=1, source_target_pairs={{0,6},{1,7},{2,4},{3,5},{4,2},{5,3},{6,0},{7,1},{8,14},{9,15},{10,... | collective-permute-start | bytes 786440 | tf_op jit(solution)/shard_map/ppermute | solution.py:33
  17.6 38.1 %collective-permute-start.7 = (bf16[2,2,4,32,256]{4,3,2,1,0:T(8,128)(2,1)S(1)}, bf16[2,2,4,32,256]{4,3,2,1,0:T(8,128)(2,1)S(1)}, u32[]{:S(2)}, u32[]{:S(2)}) collective-permute-start(bf16[2,2,4,32,256]{4,3,2,1,0:T(8,128)(2,1)S(1)} %get-tuple-element.67), channel_id=1, source_target_pairs={{0,10},{1,11},{2,8},{3,9},{4,14},{5,15},{6,12},{7,13},{8,2},{9,3},... | collective-permute-start | bytes 786440 | tf_op jit(solution)/shard_map/ppermute | solution.py:33
  21.4 26.0 %collective-permute-start.8 = (bf16[2,4,32,256]{3,2,1,0:T(8,128)(2,1)S(1)}, bf16[2,4,32,256]{3,2,1,0:T(8,128)(2,1)S(1)}, u32[]{:S(2)}, u32[]{:S(2)}) collective-permute-start(bf16[2,4,32,256]{3,2,1,0:T(8,128)(2,1)S(1)} %get-tuple-element.69), channel_id=1, source_target_pairs={{0,14},{1,15},{2,12},{3,13},{4,10},{5,11},{6,8},{7,9},{8,6},{9,7},... | collective-permute-start | bytes 393224 | tf_op jit(solution)/shard_map/ppermute | solution.py:33
  29.1 53.0 %collective-permute-start.10 = (bf16[4,512,256]{2,1,0:T(8,128)(2,1)S(1)}, bf16[4,512,256]{2,1,0:T(8,128)(2,1)S(1)}, u32[]{:S(2)}, u32[]{:S(2)}) collective-permute-start(bf16[4,512,256]{2,1,0:T(8,128)(2,1)S(1)} %bitcast.8), channel_id=1, source_target_pairs={{0,16},{16,0},{1,17},{17,1},{2,18},{18,2},{3,19},{19,3},{4,20},{20... | collective-permute-start | bytes 3145736 | tf_op jit(solution)/shard_map/ppermute | solution.py:17
  47.4 11.3 %collective-permute-start.9 = (bf16[2,4,32,256]{3,2,1,0:T(8,128)(2,1)S(1)}, bf16[2,4,32,256]{3,2,1,0:T(8,128)(2,1)S(1)}, u32[]{:S(2)}, u32[]{:S(2)}) collective-permute-start(bf16[2,4,32,256]{3,2,1,0:T(8,128)(2,1)S(1)} %get-tuple-element.72), channel_id=1, source_target_pairs={{0,14},{1,15},{2,12},{3,13},{4,10},{5,11},{6,8},{7,9},{8,6},{9,7},... | collective-permute-start | bytes 393224 | tf_op jit(solution)/shard_map/ppermute | solution.py:33
  58.7 2.0 %collective-permute-start.11 = (bf16[8,4,32,256]{3,2,1,0:T(8,128)(2,1)S(1)}, bf16[8,4,32,256]{3,2,1,0:T(8,128)(2,1)S(1)}, u32[]{:S(2)}, u32[]{:S(2)}) collective-permute-start(bf16[8,4,32,256]{3,2,1,0:T(8,128)(2,1)S(1)} %get-tuple-element.78), channel_id=1, source_target_pairs={{0,1},{1,0},{2,3},{3,2},{4,5},{5,4},{6,7},{7,6},{8,9},{9,8},{10,11... | collective-permute-start | bytes 1572872 | tf_op jit(solution)/shard_map/ppermute | solution.py:33
  60.7 10.1 %collective-permute-start.12 = (bf16[2,4,32,256]{3,2,1,0:T(8,128)(2,1)S(1)}, bf16[2,4,32,256]{3,2,1,0:T(8,128)(2,1)S(1)}, u32[]{:S(2)}, u32[]{:S(2)}) collective-permute-start(bf16[2,4,32,256]{3,2,1,0:T(8,128)(2,1)S(1)} %get-tuple-element.79), channel_id=1, source_target_pairs={{0,2},{1,3},{2,0},{3,1},{4,6},{5,7},{6,4},{7,5},{8,10},{9,11},{10,... | collective-permute-start | bytes 393224 | tf_op jit(solution)/shard_map/ppermute | solution.py:33
  62.3 13.0 %collective-permute-start.13 = (bf16[2,4,32,256]{3,2,1,0:T(8,128)(2,1)S(1)}, bf16[2,4,32,256]{3,2,1,0:T(8,128)(2,1)S(1)}, u32[]{:S(2)}, u32[]{:S(2)}) collective-permute-start(bf16[2,4,32,256]{3,2,1,0:T(8,128)(2,1)S(1)} %get-tuple-element.80), channel_id=1, source_target_pairs={{0,4},{1,5},{2,6},{3,7},{4,0},{5,1},{6,2},{7,3},{8,12},{9,13},{10,... | collective-permute-start | bytes 393224 | tf_op jit(solution)/shard_map/ppermute | solution.py:33
  67.7 9.1 %collective-permute-start.14 = (bf16[2,4,32,256]{3,2,1,0:T(8,128)(2,1)S(1)}, bf16[2,4,32,256]{3,2,1,0:T(8,128)(2,1)S(1)}, u32[]{:S(2)}, u32[]{:S(2)}) collective-permute-start(bf16[2,4,32,256]{3,2,1,0:T(8,128)(2,1)S(1)} %get-tuple-element.81), channel_id=1, source_target_pairs={{0,6},{1,7},{2,4},{3,5},{4,2},{5,3},{6,0},{7,1},{8,14},{9,15},{10,... | collective-permute-start | bytes 393224 | tf_op jit(solution)/shard_map/ppermute | solution.py:33
  67.7 9.6 %collective-permute-start.15 = (bf16[2,4,32,256]{3,2,1,0:T(8,128)(2,1)S(1)}, bf16[2,4,32,256]{3,2,1,0:T(8,128)(2,1)S(1)}, u32[]{:S(2)}, u32[]{:S(2)}) collective-permute-start(bf16[2,4,32,256]{3,2,1,0:T(8,128)(2,1)S(1)} %get-tuple-element.82), channel_id=1, source_target_pairs={{0,8},{1,9},{2,10},{3,11},{4,12},{5,13},{6,14},{7,15},{8,0},{9,1},... | collective-permute-start | bytes 393224 | tf_op jit(solution)/shard_map/ppermute | solution.py:33
  70.8 11.3 %collective-permute-start.16 = (bf16[2,4,32,256]{3,2,1,0:T(8,128)(2,1)S(1)}, bf16[2,4,32,256]{3,2,1,0:T(8,128)(2,1)S(1)}, u32[]{:S(2)}, u32[]{:S(2)}) collective-permute-start(bf16[2,4,32,256]{3,2,1,0:T(8,128)(2,1)S(1)} %get-tuple-element.83), channel_id=1, source_target_pairs={{0,12},{1,13},{2,14},{3,15},{4,8},{5,9},{6,10},{7,11},{8,4},{9,5},... | collective-permute-start | bytes 393224 | tf_op jit(solution)/shard_map/ppermute | solution.py:33
  82.1 3.0 %collective-permute-start.17 = (bf16[8,4,32,256]{3,2,1,0:T(8,128)(2,1)S(1)}, bf16[8,4,32,256]{3,2,1,0:T(8,128)(2,1)S(1)}, u32[]{:S(2)}, u32[]{:S(2)}) collective-permute-start(bf16[8,4,32,256]{3,2,1,0:T(8,128)(2,1)S(1)} %get-tuple-element.84), channel_id=1, source_target_pairs={{0,1},{1,0},{2,3},{3,2},{4,5},{5,4},{6,7},{7,6},{8,9},{9,8},{10,11... | collective-permute-start | bytes 1572872 | tf_op jit(solution)/shard_map/ppermute | solution.py:33
  82.1 30.0 %collective-permute-start.26 = (bf16[12,4,32,256]{3,2,1,0:T(8,128)(2,1)S(1)}, bf16[12,4,32,256]{3,2,1,0:T(8,128)(2,1)S(1)}, u32[]{:S(2)}, u32[]{:S(2)}) collective-permute-start(bf16[12,4,32,256]{3,2,1,0:T(8,128)(2,1)S(1)} %gather_kernel.2.first_ref), channel_id=1, source_target_pairs={{0,16},{16,0},{1,17},{17,1},{2,18},{18,2},{3,19},{19,3},{4,20},{20... | collective-permute-start | bytes 2359304 | tf_op jit(solution)/shard_map/ppermute | solution.py:17
  83.7 9.1 %collective-permute-start.25 = (bf16[2,4,32,256]{3,2,1,0:T(8,128)(2,1)S(1)}, bf16[2,4,32,256]{3,2,1,0:T(8,128)(2,1)S(1)}, u32[]{:S(2)}, u32[]{:S(2)}) collective-permute-start(bf16[2,4,32,256]{3,2,1,0:T(8,128)(2,1)S(1)} %get-tuple-element.96), channel_id=1, source_target_pairs={{0,14},{1,15},{2,12},{3,13},{4,10},{5,11},{6,8},{7,9},{8,6},{9,7},... | collective-permute-start | bytes 393224 | tf_op jit(solution)/shard_map/ppermute | solution.py:33
  85.1 17.2 %collective-permute-start.18 = (bf16[2,4,32,256]{3,2,1,0:T(8,128)(2,1)S(1)}, bf16[2,4,32,256]{3,2,1,0:T(8,128)(2,1)S(1)}, u32[]{:S(2)}, u32[]{:S(2)}) collective-permute-start(bf16[2,4,32,256]{3,2,1,0:T(8,128)(2,1)S(1)} %get-tuple-element.86), channel_id=1, source_target_pairs={{0,8},{1,9},{2,10},{3,11},{4,12},{5,13},{6,14},{7,15},{8,0},{9,1},... | collective-permute-start | bytes 393224 | tf_op jit(solution)/shard_map/ppermute | solution.py:33
  87.0 17.4 %collective-permute-start.24 = (bf16[2,4,32,256]{3,2,1,0:T(8,128)(2,1)S(1)}, bf16[2,4,32,256]{3,2,1,0:T(8,128)(2,1)S(1)}, u32[]{:S(2)}, u32[]{:S(2)}) collective-permute-start(bf16[2,4,32,256]{3,2,1,0:T(8,128)(2,1)S(1)} %get-tuple-element.95), channel_id=1, source_target_pairs={{0,10},{1,11},{2,8},{3,9},{4,14},{5,15},{6,12},{7,13},{8,2},{9,3},... | collective-permute-start | bytes 393224 | tf_op jit(solution)/shard_map/ppermute | solution.py:33
  104.5 13.3 %collective-permute-start.27 = (bf16[8,4,32,256]{3,2,1,0:T(8,128)(2,1)S(1)}, bf16[8,4,32,256]{3,2,1,0:T(8,128)(2,1)S(1)}, u32[]{:S(2)}, u32[]{:S(2)}) collective-permute-start(bf16[8,4,32,256]{3,2,1,0:T(8,128)(2,1)S(1)} %gather_kernel.3.second_ref), channel_id=1, source_target_pairs={{0,16},{16,0},{1,17},{17,1},{2,18},{18,2},{3,19},{19,3},{4,20},{20... | collective-permute-start | bytes 1572872 | tf_op jit(solution)/shard_map/ppermute | solution.py:17
  105.1 15.1 %collective-permute-start.19 = (bf16[2,4,32,256]{3,2,1,0:T(8,128)(2,1)S(1)}, bf16[2,4,32,256]{3,2,1,0:T(8,128)(2,1)S(1)}, u32[]{:S(2)}, u32[]{:S(2)}) collective-permute-start(bf16[2,4,32,256]{3,2,1,0:T(8,128)(2,1)S(1)} %get-tuple-element.87), channel_id=1, source_target_pairs={{0,12},{1,13},{2,14},{3,15},{4,8},{5,9},{6,10},{7,11},{8,4},{9,5},... | collective-permute-start | bytes 393224 | tf_op jit(solution)/shard_map/ppermute | solution.py:33
  107.5 15.7 %collective-permute-start.20 = (bf16[2,4,32,256]{3,2,1,0:T(8,128)(2,1)S(1)}, bf16[2,4,32,256]{3,2,1,0:T(8,128)(2,1)S(1)}, u32[]{:S(2)}, u32[]{:S(2)}) collective-permute-start(bf16[2,4,32,256]{3,2,1,0:T(8,128)(2,1)S(1)} %get-tuple-element.88), channel_id=1, source_target_pairs={{0,10},{1,11},{2,8},{3,9},{4,14},{5,15},{6,12},{7,13},{8,2},{9,3},... | collective-permute-start | bytes 393224 | tf_op jit(solution)/shard_map/ppermute | solution.py:33
  107.5 15.7 %collective-permute-start.21 = (bf16[2,4,32,256]{3,2,1,0:T(8,128)(2,1)S(1)}, bf16[2,4,32,256]{3,2,1,0:T(8,128)(2,1)S(1)}, u32[]{:S(2)}, u32[]{:S(2)}) collective-permute-start(bf16[2,4,32,256]{3,2,1,0:T(8,128)(2,1)S(1)} %get-tuple-element.89), channel_id=1, source_target_pairs={{0,14},{1,15},{2,12},{3,13},{4,10},{5,11},{6,8},{7,9},{8,6},{9,7},... | collective-permute-start | bytes 393224 | tf_op jit(solution)/shard_map/ppermute | solution.py:33
  112.2 11.0 %collective-permute-start.22 = (bf16[2,4,32,256]{3,2,1,0:T(8,128)(2,1)S(1)}, bf16[2,4,32,256]{3,2,1,0:T(8,128)(2,1)S(1)}, u32[]{:S(2)}, u32[]{:S(2)}) collective-permute-start(bf16[2,4,32,256]{3,2,1,0:T(8,128)(2,1)S(1)} %get-tuple-element.90), channel_id=1, source_target_pairs={{0,2},{1,3},{2,0},{3,1},{4,6},{5,7},{6,4},{7,5},{8,10},{9,11},{10,... | collective-permute-start | bytes 393224 | tf_op jit(solution)/shard_map/ppermute | solution.py:33
  117.8 5.9 %collective-permute-start.23 = (bf16[2,4,32,256]{3,2,1,0:T(8,128)(2,1)S(1)}, bf16[2,4,32,256]{3,2,1,0:T(8,128)(2,1)S(1)}, u32[]{:S(2)}, u32[]{:S(2)}) collective-permute-start(bf16[2,4,32,256]{3,2,1,0:T(8,128)(2,1)S(1)} %get-tuple-element.91), channel_id=1, source_target_pairs={{0,4},{1,5},{2,6},{3,7},{4,0},{5,1},{6,2},{7,3},{8,12},{9,13},{10,... | collective-permute-start | bytes 393224 | tf_op jit(solution)/shard_map/ppermute | solution.py:33
  117.8 8.8 %copy-start.3 = (bf16[1,2048,256]{2,1,0:T(8,128)(2,1)S(1)}, bf16[1,2048,256]{2,1,0:T(8,128)(2,1)}, u32[]{:S(2)}) copy-start(bf16[1,2048,256]{2,1,0:T(8,128)(2,1)} %param.6) | copy-start | bytes 3145732
  117.8 8.8 %copy-start.4 = (bf16[1,2048,256]{2,1,0:T(8,128)(2,1)S(1)}, bf16[1,2048,256]{2,1,0:T(8,128)(2,1)}, u32[]{:S(2)}) copy-start(bf16[1,2048,256]{2,1,0:T(8,128)(2,1)} %param.7) | copy-start | bytes 3145732
  120.2 6.4 %collective-permute-start.28 = (bf16[2,4,32,256]{3,2,1,0:T(8,128)(2,1)S(1)}, bf16[2,4,32,256]{3,2,1,0:T(8,128)(2,1)S(1)}, u32[]{:S(2)}, u32[]{:S(2)}) collective-permute-start(bf16[2,4,32,256]{3,2,1,0:T(8,128)(2,1)S(1)} %get-tuple-element.100), channel_id=1, source_target_pairs={{0,6},{1,7},{2,4},{3,5},{4,2},{5,3},{6,0},{7,1},{8,14},{9,15},{10,... | collective-permute-start | bytes 393224 | tf_op jit(solution)/shard_map/ppermute | solution.py:33

commit v15 on v13

--- a/solution.py
+++ b/solution.py
@@ -25,8 +25,7 @@
     half = chips // 2
     near = list(range(1, half))
     far = list(range(half, chips, 2)) + list(range(half + 1, chips, 2))
-    mixed = far[:2] + near[:-1] + far[2:-1] + near[-1:] + far[-1:]
-    return [0] + far[:1] + near + far[1:], [0] + mixed, [0] + far + near
+    return [0] + far[:1] + near + far[1:], [0] + far + near
 
 
 def permute(array, offset):
@@ -157,10 +156,10 @@
         ref[...] = block.reshape(rows, cols, channels)
 
 
-def column_backward_kernel(order, me_ref, right_ref, *refs):
+def column_backward_kernel(order, direct, me_ref, right_ref, *refs):
     chips = len(order)
-    in_refs, out_refs = refs[:chips], refs[chips : chips + 2]
-    by_column_ref, wide, wide_out = refs[chips + 2 :]
+    in_refs, own_ref, other_ref = refs[:chips], refs[chips], refs[chips + 1]
+    direct_refs, (by_column_ref, wide, wide_out) = refs[chips + 2 : -3], refs[-3:]
     cols, count, _ = right_ref.shape
     me = me_ref[0]
     load_columns(of_pair(received_views(me, in_refs, order), 0), wide)
@@ -168,7 +167,11 @@
         grad = column(wide, k, count, cols)
         by_column_ref[k] = grad
         store_column(wide_out, k, count, cols, dot(right_ref[k], grad, ((0,), (0,))))
-    send_columns(wide_out, block_views(me, out_refs))
+    views = [(me ^ (2 * t + e), direct_refs[2 * n + e]) for n, t in enumerate(direct) for e in range(2)]
+    others = [t for t in range(chips) if t not in direct]
+    for e, ref in enumerate((own_ref, other_ref)):
+        views += [(me ^ (2 * t + e), ref.at[n]) for n, t in enumerate(others)]
+    send_columns(wide_out, views)
 
 
 def column_forward_kernel(order, me_ref, right_ref, grad_ref, after_ref, *refs):
@@ -196,12 +199,16 @@
     _, rows, cols, channels = out_ref.shape
     size = rows * cols
     for ref in refs[:-1]:
+        if ref.ndim == 3:
+            out_ref[n] = ref[...]
+            n += 1
+            continue
         if ref.ndim == 2:
             for start in range(0, ref.shape[0], size):
                 out_ref[n] = ref[start : start + size].reshape(rows, cols, channels)
                 n += 1
             continue
-        for e in range(ref.shape[0]):
+        for e in range(2):
             out_ref[n] = ref[e]
             n += 1
 
@@ -281,7 +288,7 @@
     def shape(*dims):
         return jax.ShapeDtypeStruct(dims, BF16)
 
-    one_ahead, two_ahead, all_far = orders(chips)
+    one_ahead, all_far = orders(chips)
 
     def ordered(kernel, order):
         return functools.partial(kernel, order)
@@ -296,7 +303,7 @@
     column_flops = 2 * cols * count * count * channels
 
     def pack(own, swapped):
-        return list(call(pack_kernel, me, [own, swapped], [shape(2, *own.shape[1:])] * chips))
+        return list(call(pack_kernel, me, [own, swapped], [shape(2, *own.shape[1:])] * own.shape[0]))
 
     hold = pltpu.VMEM(whole.shape, BF16)
     halves = [shape(chips, *block)] * 2
@@ -322,15 +329,20 @@
     other_values = swap_sequences(after(values, messages[0]))
     columns = listed(exchange(messages), one_ahead)
     mixed_last = permute(after(mixed_last, columns[1:-2] + columns[-1:]), 2 * last)
-    own, other, grad_column = call(
-        ordered(column_backward_kernel, one_ahead),
+    direct = all_far[1:3]
+    others = [t for t in range(chips) if t not in direct]
+    own, other, *blocks, grad_column = call(
+        functools.partial(column_backward_kernel, one_ahead, direct),
         me,
         [right_factor, *columns],
-        [shape(chips, *block)] * 2 + [shape(cols, count, channels)],
+        [shape(len(others), *block)] * 2
+        + [shape(*block)] * 2 * len(direct)
+        + [shape(cols, count, channels)],
         [wide, wide],
         column_flops,
     )
-    back = exchange(pack(own, permute(after(other, mixed_last), 1)))
+    blocks = [permute(x, 2 * direct[n // 2] + n % 2) for n, x in enumerate(blocks)]
+    own_back, other_back = own, other
     columns[-1] = mixed_last
     packed_right = shape(cols * count * count // channels, channels)
     own, other, right_part = call(
@@ -342,22 +354,30 @@
         2 * column_flops,
         unblocked=[2],
     )
-    back = listed(back, two_ahead)
-    ahead = chips // 2 + 1
-    messages = pack(own, permute(after(other, back[1:ahead]), 1))
-    done = [(t, permute(messages[t], 2 * t)) for t in all_far[1:2]]
-    back[-1] = after(back[-1], [block for _, block in done])
+    other_back = after(other_back, [mixed_last, *blocks, right_part])
+    back = pack(own_back, permute(other_back, 1))
+    back = dict(zip(others, back))
+    third = all_far[3]
+    back[third] = permute(back[third], 2 * third)
+    for t in all_far[4:]:
+        message = after(back[t], back[third]) if t in all_far[-1:] else back[t]
+        back[t] = permute(message, 2 * t)
+    back = [back[t] for t in all_far if t in others]
+    messages = pack(own, permute(after(other, blocks), 1))
+    done = []
     extra = packed_right.size // math.prod(block)
+    sent_first = [back[0], *blocks]
+    ahead = 1 + len(direct)
     (first_part,) = call(
-        gather_kernel, me, [*back[:ahead], right_part], [shape(2 * ahead + extra, *block)]
+        gather_kernel, me, [*sent_first, right_part], [shape(2 * ahead + extra, *block)]
     )
     (second_part,) = call(
-        gather_kernel, me, back[ahead:], [shape(2 * (chips - ahead), *block)]
+        gather_kernel, me, back[1:], [shape(2 * (chips - ahead), *block)]
     )
     other_first = swap_sequences(first_part)
     other_second = swap_sequences(second_part)
     grad_signal, left_term = call(
-        ordered(row_backward_kernel, two_ahead),
+        ordered(row_backward_kernel, all_far),
         me,
         [left_factor, values, first_part, second_part],
         [by_row, left],
@@ -365,7 +385,7 @@
         2 * row_flops,
     )
     grad_left, grad_right = call(
-        ordered(factor_sum_kernel, two_ahead),
+        ordered(factor_sum_kernel, all_far),
         me,
         [left_term, other_values, other_first, other_second, right_part],
         [left, right],
@@ -373,7 +393,7 @@
         row_flops,
     )
     last = all_far[-1]
-    messages[last] = after(messages[last], grad_left)
+    messages[last] = after(messages[last], left_term)
     second = listed(exchange(messages, done), all_far)
     output, grad_gate = call(
         ordered(output_kernel, all_far), me, [gate, cotangent, *second], [whole, whole]

time: 127 us -> 132 us (1.039)
  starting transfers between devices: 44.5 us -> 48 us
  waiting for transfers between devices: 63.9 us -> 65.4 us
    ppermute x26 -> x28, waiting for transfers between devices: 61.8 us -> 65.4 us  [permute(): return lax.ppermute(array, 'seq', [(i, i ^ offset) for i in range(seq)])]
    ppermute x26 -> x28, starting transfers between devices: 40.9 us -> 44.1 us  [permute(): return lax.ppermute(array, 'seq', [(i, i ^ offset) for i in range(seq)])]
    ppermute x3, waiting for transfers between devices: 2.04 us -> 0.01 us  [swap_sequences(): return lax.ppermute(array, 'dp', [(0, 1), (1, 0)])]
  transfers between devices with their start and end apart: 29 -> 31, of which waited for: 16 -> 15; matrix products, arithmetic and copies ran while one was open for 0% -> 0% of each run, Pallas kernels for 9% -> 9%
where the time goes in v15:
time: 132 us
  waiting for transfers between devices  65.4 us (50%)
  starting transfers between devices  48 us (36%)
  Pallas kernels  16.6 us (13%)
    ppermute x28, waiting for transfers between devices, permute(): return lax.ppermute(array, 'seq', [(i, i ^ offset) for i in range(seq)])  65.4 us
    ppermute x28, starting transfers between devices, permute(): return lax.ppermute(array, 'seq', [(i, i ^ offset) for i in range(seq)])  44.1 us
    pallas_call x12, Pallas kernels, call(): pl.pallas_call(kernel, out_shape=out_shapes, in_specs=[pl.BlockSpec(memor...  16.6 us
    ppermute x3, starting transfers between devices, swap_sequences(): return lax.ppermute(array, 'dp', [(0, 1), (1, 0)])  3.9 us
  transfers between devices with their start and end apart: 31, of which 15 were waited for; matrix products, arithmetic and copies ran while one was open for 0% of the time, Pallas kernels for 9%

profile of v15, /device:TPU:0, one launch (start us, length us, event | category | flops | bytes accessed | tf_op | source)
XLA Modules:
  0.0 132.0 jit_solution(3239689380499872958)
XLA Ops:
  0.6 2.7 %product_kernel.1 = (bf16[8,4,32,256]{3,2,1,0:T(8,128)(2,1)}, bf16[8,4,32,256]{3,2,1,0:T(8,128)(2,1)}) custom-call(s32[1]{0:T(128)} %bitcast.me_ref, bf16[4,16,32,256]{3,2,1,0:T(8,128)(2,1)} %bitcast.10, bf16[4,16,32,256]{3,2,1,0:T(8,128)(2,1)} %bitcast.12), custom_call_target="tpu_custom_call" | custom-call | bytes 3145728 | tf_op jit(solution)/shard_map/product_kernel/pallas_call | solution.py:54
  3.4 0.5 collective-permute-start
  3.9 1.2 copy-done.1
  5.1 0.8 mix_kernel.1
  6.0 1.9 %collective-permute-done.1.refs_3_ = bf16[8,4,32,256]{3,2,1,0:T(8,128)(2,1)S(1)} collective-permute-done((bf16[8,4,32,256]{3,2,1,0:T(8,128)(2,1)S(1)}, bf16[8,4,32,256]{3,2,1,0:T(8,128)(2,1)S(1)}, u32[]{:S(2)}, u32[]{:S(2)}) %collective-permute-start.1) | collective-permute-done | bytes 524320 | tf_op jit(solution)/shard_map/ppermute | solution.py:33
  7.9 0.1 pack_pairs_kernel.1
  8.0 2.7 %collective-permute-start.9 = (bf16[4,512,256]{2,1,0:T(8,128)(2,1)S(1)}, bf16[4,512,256]{2,1,0:T(8,128)(2,1)S(1)}, u32[]{:S(2)}, u32[]{:S(2)}) collective-permute-start(bf16[4,512,256]{2,1,0:T(8,128)(2,1)S(1)} %bitcast.8), channel_id=1, source_target_pairs={{0,16},{16,0},{1,17},{17,1},{2,18},{18,2},{3,19},{19,3},{4,20},{20... | collective-permute-start | bytes 3145736 | tf_op jit(solution)/shard_map/ppermute | solution.py:17
  10.7 2.6 %collective-permute-start.2 = (bf16[2,2,4,32,256]{4,3,2,1,0:T(8,128)(2,1)S(1)}, bf16[2,2,4,32,256]{4,3,2,1,0:T(8,128)(2,1)S(1)}, u32[]{:S(2)}, u32[]{:S(2)}) collective-permute-start(bf16[2,2,4,32,256]{4,3,2,1,0:T(8,128)(2,1)S(1)} %get-tuple-element.61), channel_id=1, source_target_pairs={{0,8},{1,9},{2,10},{3,11},{4,12},{5,13},{6,14},{7,15},{8,0},{9,1},... | collective-permute-start | bytes 786440 | tf_op jit(solution)/shard_map/ppermute | solution.py:33
  13.3 1.5 %collective-permute-start.3 = (bf16[2,2,4,32,256]{4,3,2,1,0:T(8,128)(2,1)S(1)}, bf16[2,2,4,32,256]{4,3,2,1,0:T(8,128)(2,1)S(1)}, u32[]{:S(2)}, u32[]{:S(2)}) collective-permute-start(bf16[2,2,4,32,256]{4,3,2,1,0:T(8,128)(2,1)S(1)} %get-tuple-element.62), channel_id=1, source_target_pairs={{0,2},{1,3},{2,0},{3,1},{4,6},{5,7},{6,4},{7,5},{8,10},{9,11},{10,... | collective-permute-start | bytes 786440 | tf_op jit(solution)/shard_map/ppermute | solution.py:33
  14.8 1.3 collective-permute-start.8
  16.1 0.3 collective-permute-start.4
  16.4 9.3 %collective-permute-done.8.refs_7_ = bf16[2,4,32,256]{3,2,1,0:T(8,128)(2,1)S(1)} collective-permute-done((bf16[2,4,32,256]{3,2,1,0:T(8,128)(2,1)S(1)}, bf16[2,4,32,256]{3,2,1,0:T(8,128)(2,1)S(1)}, u32[]{:S(2)}, u32[]{:S(2)}) %collective-permute-start.8) | collective-permute-done | bytes 131104 | tf_op jit(solution)/shard_map/ppermute | solution.py:33
  25.7 7.2 %collective-permute-start.5 = (bf16[2,2,4,32,256]{4,3,2,1,0:T(8,128)(2,1)S(1)}, bf16[2,2,4,32,256]{4,3,2,1,0:T(8,128)(2,1)S(1)}, u32[]{:S(2)}, u32[]{:S(2)}) collective-permute-start(bf16[2,2,4,32,256]{4,3,2,1,0:T(8,128)(2,1)S(1)} %get-tuple-element.64), channel_id=1, source_target_pairs={{0,6},{1,7},{2,4},{3,5},{4,2},{5,3},{6,0},{7,1},{8,14},{9,15},{10,... | collective-permute-start | bytes 786440 | tf_op jit(solution)/shard_map/ppermute | solution.py:33
  32.8 3.3 %collective-permute-start.6 = (bf16[2,2,4,32,256]{4,3,2,1,0:T(8,128)(2,1)S(1)}, bf16[2,2,4,32,256]{4,3,2,1,0:T(8,128)(2,1)S(1)}, u32[]{:S(2)}, u32[]{:S(2)}) collective-permute-start(bf16[2,2,4,32,256]{4,3,2,1,0:T(8,128)(2,1)S(1)} %get-tuple-element.65), channel_id=1, source_target_pairs={{0,12},{1,13},{2,14},{3,15},{4,8},{5,9},{6,10},{7,11},{8,4},{9,5},... | collective-permute-start | bytes 786440 | tf_op jit(solution)/shard_map/ppermute | solution.py:33
  36.2 3.3 %collective-permute-done.5.refs_4_ = bf16[2,2,4,32,256]{4,3,2,1,0:T(8,128)(2,1)S(1)} collective-permute-done((bf16[2,2,4,32,256]{4,3,2,1,0:T(8,128)(2,1)S(1)}, bf16[2,2,4,32,256]{4,3,2,1,0:T(8,128)(2,1)S(1)}, u32[]{:S(2)}, u32[]{:S(2)}) %collective-permute-start.5) | collective-permute-done | bytes 262176 | tf_op jit(solution)/shard_map/ppermute | solution.py:33
  39.5 9.5 %collective-permute-done.6.refs_5_ = bf16[2,2,4,32,256]{4,3,2,1,0:T(8,128)(2,1)S(1)} collective-permute-done((bf16[2,2,4,32,256]{4,3,2,1,0:T(8,128)(2,1)S(1)}, bf16[2,2,4,32,256]{4,3,2,1,0:T(8,128)(2,1)S(1)}, u32[]{:S(2)}, u32[]{:S(2)}) %collective-permute-start.6) | collective-permute-done | bytes 262176 | tf_op jit(solution)/shard_map/ppermute | solution.py:33
  49.0 1.1 collective-permute-start.10
  50.2 11.3 %collective-permute-done.7.refs_6_ = bf16[2,2,4,32,256]{4,3,2,1,0:T(8,128)(2,1)S(1)} collective-permute-done((bf16[2,2,4,32,256]{4,3,2,1,0:T(8,128)(2,1)S(1)}, bf16[2,2,4,32,256]{4,3,2,1,0:T(8,128)(2,1)S(1)}, u32[]{:S(2)}, u32[]{:S(2)}) %collective-permute-start.7) | collective-permute-done | bytes 262176 | tf_op jit(solution)/shard_map/ppermute | solution.py:33
  61.5 3.0 %column_backward_kernel.1 = (bf16[6,4,32,256]{3,2,1,0:T(8,128)(2,1)S(1)}, bf16[6,4,32,256]{3,2,1,0:T(8,128)(2,1)S(1)}, bf16[4,32,256]{2,1,0:T(8,128)(2,1)S(1)}, ...) custom-call(s32[1]{0:T(128)} %bitcast.me_ref, ...), custom_call_target="tpu_custom_call" | custom-call | flops 67108864 | bytes 4325376 | tf_op jit(solution)/shard_map/column_backward_kernel/pallas_call | solution.py:54
  64.5 1.1 collective-permute-start.12
  65.6 2.3 %collective-permute-start.13 = (bf16[4,32,256]{2,1,0:T(8,128)(2,1)S(1)}, bf16[4,32,256]{2,1,0:T(8,128)(2,1)S(1)}, u32[]{:S(2)}, u32[]{:S(2)}) collective-permute-start(bf16[4,32,256]{2,1,0:T(8,128)(2,1)S(1)} %get-tuple-element.76), channel_id=1, source_target_pairs={{0,12},{1,13},{2,14},{3,15},{4,8},{5,9},{6,10},{7,11},{8,4},{9,5},... | collective-permute-start | bytes 196616 | tf_op jit(solution)/shard_map/ppermute | solution.py:33
  68.0 2.7 %collective-permute-start.14 = (bf16[4,32,256]{2,1,0:T(8,128)(2,1)S(1)}, bf16[4,32,256]{2,1,0:T(8,128)(2,1)S(1)}, u32[]{:S(2)}, u32[]{:S(2)}) collective-permute-start(bf16[4,32,256]{2,1,0:T(8,128)(2,1)S(1)} %get-tuple-element.77), channel_id=1, source_target_pairs={{0,13},{1,12},{2,15},{3,14},{4,9},{5,8},{6,11},{7,10},{8,5},{9,4},... | collective-permute-start | bytes 196616 | tf_op jit(solution)/shard_map/ppermute | solution.py:33
  70.7 3.3 %column_forward_kernel.1 = (bf16[8,4,32,256]{3,2,1,0:T(8,128)(2,1)S(1)}, bf16[8,4,32,256]{3,2,1,0:T(8,128)(2,1)S(1)}, bf16[512,256]{1,0:T(8,128)(2,1)S(1)}) custom-call(s32[1]{0:T(128)} %bitcast.me_ref, bf16[32,64,64]{2,1,0:T(8,128)(2,1)S(1)} %copy-done.5, bf16[32,64,256]{2,1,0:T(8,128)(2,1)S(1)} %get-tuple-element.68.grad_ref, ...), custom_call_target="tpu_custom_call" | custom-call | flops 134217728 | bytes 5636096 | tf_op jit(solution)/shard_map/column_forward_kernel/pallas_call | solution.py:54
  74.1 0.5 collective-permute-done.11.refs_1_
  74.5 1.9 %collective-permute-start.22 = (bf16[6,4,32,256]{3,2,1,0:T(8,128)(2,1)S(1)}, bf16[6,4,32,256]{3,2,1,0:T(8,128)(2,1)S(1)}, u32[]{:S(2)}, u32[]{:S(2)}) collective-permute-start(bf16[6,4,32,256]{3,2,1,0:T(8,128)(2,1)S(1)} %get-tuple-element.90), channel_id=1, source_target_pairs={{0,1},{1,0},{2,3},{3,2},{4,5},{5,4},{6,7},{7,6},{8,9},{9,8},{10,11... | collective-permute-start | bytes 1179656 | tf_op jit(solution)/shard_map/ppermute | solution.py:33
  76.5 1.3 collective-permute-done.22.other_ref
  77.9 3.6 %collective-permute-start.23 = (bf16[2,4,32,256]{3,2,1,0:T(8,128)(2,1)S(1)}, bf16[2,4,32,256]{3,2,1,0:T(8,128)(2,1)S(1)}, u32[]{:S(2)}, u32[]{:S(2)}) collective-permute-start(bf16[2,4,32,256]{3,2,1,0:T(8,128)(2,1)S(1)} %get-tuple-element.92), channel_id=1, source_target_pairs={{0,10},{1,11},{2,8},{3,9},{4,14},{5,15},{6,12},{7,13},{8,2},{9,3},... | collective-permute-start | bytes 393224 | tf_op jit(solution)/shard_map/ppermute | solution.py:33
  81.5 1.9 %collective-permute-start.24 = (bf16[2,4,32,256]{3,2,1,0:T(8,128)(2,1)S(1)}, bf16[2,4,32,256]{3,2,1,0:T(8,128)(2,1)S(1)}, u32[]{:S(2)}, u32[]{:S(2)}) collective-permute-start(bf16[2,4,32,256]{3,2,1,0:T(8,128)(2,1)S(1)} %get-tuple-element.93), channel_id=1, source_target_pairs={{0,14},{1,15},{2,12},{3,13},{4,10},{5,11},{6,8},{7,9},{8,6},{9,7},... | collective-permute-start | bytes 393224 | tf_op jit(solution)/shard_map/ppermute | solution.py:33
  83.4 1.5 %collective-permute-start.25 = (bf16[2,4,32,256]{3,2,1,0:T(8,128)(2,1)S(1)}, bf16[2,4,32,256]{3,2,1,0:T(8,128)(2,1)S(1)}, u32[]{:S(2)}, u32[]{:S(2)}) collective-permute-start(bf16[2,4,32,256]{3,2,1,0:T(8,128)(2,1)S(1)} %get-tuple-element.94), channel_id=1, source_target_pairs={{0,2},{1,3},{2,0},{3,1},{4,6},{5,7},{6,4},{7,5},{8,10},{9,11},{10,... | collective-permute-start | bytes 393224 | tf_op jit(solution)/shard_map/ppermute | solution.py:33
  85.0 6.8 %collective-permute-done.23.refs_0_ = bf16[2,4,32,256]{3,2,1,0:T(8,128)(2,1)S(1)} collective-permute-done((bf16[2,4,32,256]{3,2,1,0:T(8,128)(2,1)S(1)}, bf16[2,4,32,256]{3,2,1,0:T(8,128)(2,1)S(1)}, u32[]{:S(2)}, u32[]{:S(2)}) %collective-permute-start.23) | collective-permute-done | bytes 131104 | tf_op jit(solution)/shard_map/ppermute | solution.py:33
  91.8 0.6 collective-permute-start.29
  92.4 0.1 collective-permute-done.25.refs_2_
  92.5 1.1 collective-permute-done.26.refs_3_
  93.6 4.0 %collective-permute-done.27.refs_4_ = bf16[2,4,32,256]{3,2,1,0:T(8,128)(2,1)S(1)} collective-permute-done((bf16[2,4,32,256]{3,2,1,0:T(8,128)(2,1)S(1)}, bf16[2,4,32,256]{3,2,1,0:T(8,128)(2,1)S(1)}, u32[]{:S(2)}, u32[]{:S(2)}) %collective-permute-start.27) | collective-permute-done | bytes 131104 | tf_op jit(solution)/shard_map/ppermute | solution.py:33
  97.6 0.6 collective-permute-start.30
  98.3 0.4 collective-permute-start.16
  98.7 2.1 %collective-permute-start.17 = (bf16[2,4,32,256]{3,2,1,0:T(8,128)(2,1)S(1)}, bf16[2,4,32,256]{3,2,1,0:T(8,128)(2,1)S(1)}, u32[]{:S(2)}, u32[]{:S(2)}) collective-permute-start(bf16[2,4,32,256]{3,2,1,0:T(8,128)(2,1)S(1)} %get-tuple-element.81), channel_id=1, source_target_pairs={{0,12},{1,13},{2,14},{3,15},{4,8},{5,9},{6,10},{7,11},{8,4},{9,5},... | collective-permute-start | bytes 393224 | tf_op jit(solution)/shard_map/ppermute | solution.py:33
  100.8 2.2 %collective-permute-start.18 = (bf16[2,4,32,256]{3,2,1,0:T(8,128)(2,1)S(1)}, bf16[2,4,32,256]{3,2,1,0:T(8,128)(2,1)S(1)}, u32[]{:S(2)}, u32[]{:S(2)}) collective-permute-start(bf16[2,4,32,256]{3,2,1,0:T(8,128)(2,1)S(1)} %get-tuple-element.82), channel_id=1, source_target_pairs={{0,10},{1,11},{2,8},{3,9},{4,14},{5,15},{6,12},{7,13},{8,2},{9,3},... | collective-permute-start | bytes 393224 | tf_op jit(solution)/shard_map/ppermute | solution.py:33
  103.0 7.8 %collective-permute-done.16.refs_1_ = bf16[2,4,32,256]{3,2,1,0:T(8,128)(2,1)S(1)} collective-permute-done((bf16[2,4,32,256]{3,2,1,0:T(8,128)(2,1)S(1)}, bf16[2,4,32,256]{3,2,1,0:T(8,128)(2,1)S(1)}, u32[]{:S(2)}, u32[]{:S(2)}) %collective-permute-start.16) | collective-permute-done | bytes 131104 | tf_op jit(solution)/shard_map/ppermute | solution.py:33
  110.8 2.9 %collective-permute-start.19 = (bf16[2,4,32,256]{3,2,1,0:T(8,128)(2,1)S(1)}, bf16[2,4,32,256]{3,2,1,0:T(8,128)(2,1)S(1)}, u32[]{:S(2)}, u32[]{:S(2)}) collective-permute-start(bf16[2,4,32,256]{3,2,1,0:T(8,128)(2,1)S(1)} %get-tuple-element.83), channel_id=1, source_target_pairs={{0,14},{1,15},{2,12},{3,13},{4,10},{5,11},{6,8},{7,9},{8,6},{9,7},... | collective-permute-start | bytes 393224 | tf_op jit(solution)/shard_map/ppermute | solution.py:33
  113.7 2.3 %row_backward_kernel.1 = (bf16[4,512,256]{2,1,0:T(8,128)(2,1)}, bf16[4,512,512]{2,1,0:T(8,128)(2,1)S(1)}) custom-call(s32[1]{0:T(128)} %bitcast.me_ref, bf16[4,512,512]{2,1,0:T(8,128)(2,1)S(1)} %copy-done, bf16[4,512,256]{2,1,0:T(8,128)(2,1)S(1)} %bitcast.9, bf16[10,4,32,256]{3,2,1,0:T(8,128)(2,1)S(1)} %gather_kernel.2.first_ref, ...), custom_call_target="tpu_custom_call" | custom-call | flops 1073741824 | bytes 7602176 | tf_op jit(solution)/shard_map/row_backward_kernel/pallas_call | solution.py:54
  116.0 0.4 collective-permute-start.20
  116.4 3.9 %collective-permute-done.18.refs_3_ = bf16[2,4,32,256]{3,2,1,0:T(8,128)(2,1)S(1)} collective-permute-done((bf16[2,4,32,256]{3,2,1,0:T(8,128)(2,1)S(1)}, bf16[2,4,32,256]{3,2,1,0:T(8,128)(2,1)S(1)}, u32[]{:S(2)}, u32[]{:S(2)}) %collective-permute-start.18) | collective-permute-done | bytes 131104 | tf_op jit(solution)/shard_map/ppermute | solution.py:33
  120.3 2.8 %collective-permute-start.28 = (bf16[2,4,32,256]{3,2,1,0:T(8,128)(2,1)S(1)}, bf16[2,4,32,256]{3,2,1,0:T(8,128)(2,1)S(1)}, u32[]{:S(2)}, u32[]{:S(2)}) collective-permute-start(bf16[2,4,32,256]{3,2,1,0:T(8,128)(2,1)S(1)} %get-tuple-element.99), channel_id=1, source_target_pairs={{0,6},{1,7},{2,4},{3,5},{4,2},{5,3},{6,0},{7,1},{8,14},{9,15},{10,... | collective-permute-start | bytes 393224 | tf_op jit(solution)/shard_map/ppermute | solution.py:33
  123.1 3.4 %collective-permute-done.21.refs_6_ = bf16[2,4,32,256]{3,2,1,0:T(8,128)(2,1)S(1)} collective-permute-done((bf16[2,4,32,256]{3,2,1,0:T(8,128)(2,1)S(1)}, bf16[2,4,32,256]{3,2,1,0:T(8,128)(2,1)S(1)}, u32[]{:S(2)}, u32[]{:S(2)}) %collective-permute-start.21) | collective-permute-done | bytes 131104 | tf_op jit(solution)/shard_map/ppermute | solution.py:33
  126.5 1.4 %collective-permute-done.28.refs_7_ = bf16[2,4,32,256]{3,2,1,0:T(8,128)(2,1)S(1)} collective-permute-done((bf16[2,4,32,256]{3,2,1,0:T(8,128)(2,1)S(1)}, bf16[2,4,32,256]{3,2,1,0:T(8,128)(2,1)S(1)}, u32[]{:S(2)}, u32[]{:S(2)}) %collective-permute-start.28) | collective-permute-done | bytes 131104 | tf_op jit(solution)/shard_map/ppermute | solution.py:33
  127.9 1.8 %output_kernel.1 = (bf16[4,16,32,256]{3,2,1,0:T(8,128)(2,1)}, bf16[4,16,32,256]{3,2,1,0:T(8,128)(2,1)}) custom-call(s32[1]{0:T(128)} %bitcast.me_ref, bf16[4,16,32,256]{3,2,1,0:T(8,128)(2,1)S(1)} %bitcast.11, bf16[4,16,32,256]{3,2,1,0:T(8,128)(2,1)S(1)} %bitcast.13, bf16[2,4,32,256]{3,2,1,0:T(8,128)(2,1)S(1)} %get-tuple-element.79.refs_0_, ...), custom_call_target="tpu_custom_call" | custom-call | bytes 5242880 | tf_op jit(solution)/shard_map/output_kernel/pallas_call | solution.py:54
  129.6 2.4 %factor_sum_kernel.1 = (bf16[4,512,512]{2,1,0:T(8,128)(2,1)}, bf16[32,64,64]{2,1,0:T(8,128)(2,1)}) custom-call(s32[1]{0:T(128)} %bitcast.me_ref, bf16[4,512,512]{2,1,0:T(8,128)(2,1)S(1)} %get-tuple-element.98.term_ref, bf16[4,512,256]{2,1,0:T(8,128)(2,1)S(1)} %collective-permute-done.9.after_ref.values_ref, ...), custom_call_target="tpu_custom_call" | custom-call | flops 536870912 | bytes 7077888 | tf_op jit(solution)/shard_map/factor_sum_kernel/pallas_call | solution.py:54
  (40 shorter events, 0.5 us)
Async XLA Ops:
  0.6 3.3 %copy-start = (bf16[4,512,512]{2,1,0:T(8,128)(2,1)S(1)}, bf16[4,512,512]{2,1,0:T(8,128)(2,1)}, u32[]{:S(2)}) copy-start(bf16[4,512,512]{2,1,0:T(8,128)(2,1)} %left_ref.3) | copy-start | bytes 6291460
  3.4 2.7 %collective-permute-start = (bf16[8,4,32,256]{3,2,1,0:T(8,128)(2,1)}, bf16[8,4,32,256]{3,2,1,0:T(8,128)(2,1)S(1)}, u32[]{:S(2)}, u32[]{:S(2)}) collective-permute-start(bf16[8,4,32,256]{3,2,1,0:T(8,128)(2,1)} %get-tuple-element.56), channel_id=1, source_target_pairs={{0,1},{1,0},{2,3},{3,2},{4,5},{5,4},{6,7},{7,6},{8,9},{9,8},{10,11... | collective-permute-start | bytes 1572872 | tf_op jit(solution)/shard_map/ppermute | solution.py:33
  3.9 1.2 copy-start.1
  5.1 2.8 %copy-start.6 = (bf16[8,4,32,256]{3,2,1,0:T(8,128)(2,1)S(1)}, bf16[8,4,32,256]{3,2,1,0:T(8,128)(2,1)}, u32[]{:S(2)}) copy-start(bf16[8,4,32,256]{3,2,1,0:T(8,128)(2,1)} %get-tuple-element.55.refs_0_) | copy-start | bytes 1572868
  5.1 2.9 %copy-start.2 = (bf16[1,2048,256]{2,1,0:T(8,128)(2,1)S(1)}, bf16[1,2048,256]{2,1,0:T(8,128)(2,1)}, u32[]{:S(2)}) copy-start(bf16[1,2048,256]{2,1,0:T(8,128)(2,1)} %param.5) | copy-start | bytes 3145732
  5.1 56.4 %copy-start.5 = (bf16[32,64,64]{2,1,0:T(8,128)(2,1)S(1)}, bf16[32,64,64]{2,1,0:T(8,128)(2,1)}, u32[]{:S(2)}) copy-start(bf16[32,64,64]{2,1,0:T(8,128)(2,1)} %right_ref.3) | copy-start | bytes 786436
  5.9 2.0 %collective-permute-start.1 = (bf16[8,4,32,256]{3,2,1,0:T(8,128)(2,1)S(1)}, bf16[8,4,32,256]{3,2,1,0:T(8,128)(2,1)S(1)}, u32[]{:S(2)}, u32[]{:S(2)}) collective-permute-start(bf16[8,4,32,256]{3,2,1,0:T(8,128)(2,1)S(1)} %get-tuple-element.59), channel_id=1, source_target_pairs={{0,1},{1,0},{2,3},{3,2},{4,5},{5,4},{6,7},{7,6},{8,9},{9,8},{10,11... | collective-permute-start | bytes 1572872 | tf_op jit(solution)/shard_map/ppermute | solution.py:33
  8.0 62.7 %collective-permute-start.9 = (bf16[4,512,256]{2,1,0:T(8,128)(2,1)S(1)}, bf16[4,512,256]{2,1,0:T(8,128)(2,1)S(1)}, u32[]{:S(2)}, u32[]{:S(2)}) collective-permute-start(bf16[4,512,256]{2,1,0:T(8,128)(2,1)S(1)} %bitcast.8), channel_id=1, source_target_pairs={{0,16},{16,0},{1,17},{17,1},{2,18},{18,2},{3,19},{19,3},{4,20},{20... | collective-permute-start | bytes 3145736 | tf_op jit(solution)/shard_map/ppermute | solution.py:17
  10.7 22.1 %collective-permute-start.2 = (bf16[2,2,4,32,256]{4,3,2,1,0:T(8,128)(2,1)S(1)}, bf16[2,2,4,32,256]{4,3,2,1,0:T(8,128)(2,1)S(1)}, u32[]{:S(2)}, u32[]{:S(2)}) collective-permute-start(bf16[2,2,4,32,256]{4,3,2,1,0:T(8,128)(2,1)S(1)} %get-tuple-element.61), channel_id=1, source_target_pairs={{0,8},{1,9},{2,10},{3,11},{4,12},{5,13},{6,14},{7,15},{8,0},{9,1},... | collective-permute-start | bytes 786440 | tf_op jit(solution)/shard_map/ppermute | solution.py:33
  13.3 22.8 %collective-permute-start.3 = (bf16[2,2,4,32,256]{4,3,2,1,0:T(8,128)(2,1)S(1)}, bf16[2,2,4,32,256]{4,3,2,1,0:T(8,128)(2,1)S(1)}, u32[]{:S(2)}, u32[]{:S(2)}) collective-permute-start(bf16[2,2,4,32,256]{4,3,2,1,0:T(8,128)(2,1)S(1)} %get-tuple-element.62), channel_id=1, source_target_pairs={{0,2},{1,3},{2,0},{3,1},{4,6},{5,7},{6,4},{7,5},{8,10},{9,11},{10,... | collective-permute-start | bytes 786440 | tf_op jit(solution)/shard_map/ppermute | solution.py:33
  14.8 10.8 %collective-permute-start.8 = (bf16[2,4,32,256]{3,2,1,0:T(8,128)(2,1)S(1)}, bf16[2,4,32,256]{3,2,1,0:T(8,128)(2,1)S(1)}, u32[]{:S(2)}, u32[]{:S(2)}) collective-permute-start(bf16[2,4,32,256]{3,2,1,0:T(8,128)(2,1)S(1)} %get-tuple-element.67), channel_id=1, source_target_pairs={{0,14},{1,15},{2,12},{3,13},{4,10},{5,11},{6,8},{7,9},{8,6},{9,7},... | collective-permute-start | bytes 393224 | tf_op jit(solution)/shard_map/ppermute | solution.py:33
  16.1 20.0 %collective-permute-start.4 = (bf16[2,2,4,32,256]{4,3,2,1,0:T(8,128)(2,1)S(1)}, bf16[2,2,4,32,256]{4,3,2,1,0:T(8,128)(2,1)S(1)}, u32[]{:S(2)}, u32[]{:S(2)}) collective-permute-start(bf16[2,2,4,32,256]{4,3,2,1,0:T(8,128)(2,1)S(1)} %get-tuple-element.63), channel_id=1, source_target_pairs={{0,4},{1,5},{2,6},{3,7},{4,0},{5,1},{6,2},{7,3},{8,12},{9,13},{10,... | collective-permute-start | bytes 786440 | tf_op jit(solution)/shard_map/ppermute | solution.py:33
  25.7 13.8 %collective-permute-start.5 = (bf16[2,2,4,32,256]{4,3,2,1,0:T(8,128)(2,1)S(1)}, bf16[2,2,4,32,256]{4,3,2,1,0:T(8,128)(2,1)S(1)}, u32[]{:S(2)}, u32[]{:S(2)}) collective-permute-start(bf16[2,2,4,32,256]{4,3,2,1,0:T(8,128)(2,1)S(1)} %get-tuple-element.64), channel_id=1, source_target_pairs={{0,6},{1,7},{2,4},{3,5},{4,2},{5,3},{6,0},{7,1},{8,14},{9,15},{10,... | collective-permute-start | bytes 786440 | tf_op jit(solution)/shard_map/ppermute | solution.py:33
  32.8 16.2 %collective-permute-start.6 = (bf16[2,2,4,32,256]{4,3,2,1,0:T(8,128)(2,1)S(1)}, bf16[2,2,4,32,256]{4,3,2,1,0:T(8,128)(2,1)S(1)}, u32[]{:S(2)}, u32[]{:S(2)}) collective-permute-start(bf16[2,2,4,32,256]{4,3,2,1,0:T(8,128)(2,1)S(1)} %get-tuple-element.65), channel_id=1, source_target_pairs={{0,12},{1,13},{2,14},{3,15},{4,8},{5,9},{6,10},{7,11},{8,4},{9,5},... | collective-permute-start | bytes 786440 | tf_op jit(solution)/shard_map/ppermute | solution.py:33
  36.2 25.3 %collective-permute-start.7 = (bf16[2,2,4,32,256]{4,3,2,1,0:T(8,128)(2,1)S(1)}, bf16[2,2,4,32,256]{4,3,2,1,0:T(8,128)(2,1)S(1)}, u32[]{:S(2)}, u32[]{:S(2)}) collective-permute-start(bf16[2,2,4,32,256]{4,3,2,1,0:T(8,128)(2,1)S(1)} %get-tuple-element.66), channel_id=1, source_target_pairs={{0,10},{1,11},{2,8},{3,9},{4,14},{5,15},{6,12},{7,13},{8,2},{9,3},... | collective-permute-start | bytes 786440 | tf_op jit(solution)/shard_map/ppermute | solution.py:33
  49.0 18.9 %collective-permute-start.10 = (bf16[2,4,32,256]{3,2,1,0:T(8,128)(2,1)S(1)}, bf16[2,4,32,256]{3,2,1,0:T(8,128)(2,1)S(1)}, u32[]{:S(2)}, u32[]{:S(2)}) collective-permute-start(bf16[2,4,32,256]{3,2,1,0:T(8,128)(2,1)S(1)} %get-tuple-element.71), channel_id=1, source_target_pairs={{0,14},{1,15},{2,12},{3,13},{4,10},{5,11},{6,8},{7,9},{8,6},{9,7},... | collective-permute-start | bytes 393224 | tf_op jit(solution)/shard_map/ppermute | solution.py:33
  64.4 10.1 %collective-permute-start.11 = (bf16[4,32,256]{2,1,0:T(8,128)(2,1)S(1)}, bf16[4,32,256]{2,1,0:T(8,128)(2,1)S(1)}, u32[]{:S(2)}, u32[]{:S(2)}) collective-permute-start(bf16[4,32,256]{2,1,0:T(8,128)(2,1)S(1)} %get-tuple-element.74), channel_id=1, source_target_pairs={{0,8},{1,9},{2,10},{3,11},{4,12},{5,13},{6,14},{7,15},{8,0},{9,1},... | collective-permute-start | bytes 196616 | tf_op jit(solution)/shard_map/ppermute | solution.py:33
  64.5 10.0 %collective-permute-start.12 = (bf16[4,32,256]{2,1,0:T(8,128)(2,1)S(1)}, bf16[4,32,256]{2,1,0:T(8,128)(2,1)S(1)}, u32[]{:S(2)}, u32[]{:S(2)}) collective-permute-start(bf16[4,32,256]{2,1,0:T(8,128)(2,1)S(1)} %get-tuple-element.75), channel_id=1, source_target_pairs={{0,9},{1,8},{2,11},{3,10},{4,13},{5,12},{6,15},{7,14},{8,1},{9,0},... | collective-permute-start | bytes 196616 | tf_op jit(solution)/shard_map/ppermute | solution.py:33
  65.6 8.9 %collective-permute-start.13 = (bf16[4,32,256]{2,1,0:T(8,128)(2,1)S(1)}, bf16[4,32,256]{2,1,0:T(8,128)(2,1)S(1)}, u32[]{:S(2)}, u32[]{:S(2)}) collective-permute-start(bf16[4,32,256]{2,1,0:T(8,128)(2,1)S(1)} %get-tuple-element.76), channel_id=1, source_target_pairs={{0,12},{1,13},{2,14},{3,15},{4,8},{5,9},{6,10},{7,11},{8,4},{9,5},... | collective-permute-start | bytes 196616 | tf_op jit(solution)/shard_map/ppermute | solution.py:33
  68.0 6.5 %collective-permute-start.14 = (bf16[4,32,256]{2,1,0:T(8,128)(2,1)S(1)}, bf16[4,32,256]{2,1,0:T(8,128)(2,1)S(1)}, u32[]{:S(2)}, u32[]{:S(2)}) collective-permute-start(bf16[4,32,256]{2,1,0:T(8,128)(2,1)S(1)} %get-tuple-element.77), channel_id=1, source_target_pairs={{0,13},{1,12},{2,15},{3,14},{4,9},{5,8},{6,11},{7,10},{8,5},{9,4},... | collective-permute-start | bytes 196616 | tf_op jit(solution)/shard_map/ppermute | solution.py:33
  74.5 3.3 %collective-permute-start.22 = (bf16[6,4,32,256]{3,2,1,0:T(8,128)(2,1)S(1)}, bf16[6,4,32,256]{3,2,1,0:T(8,128)(2,1)S(1)}, u32[]{:S(2)}, u32[]{:S(2)}) collective-permute-start(bf16[6,4,32,256]{3,2,1,0:T(8,128)(2,1)S(1)} %get-tuple-element.90), channel_id=1, source_target_pairs={{0,1},{1,0},{2,3},{3,2},{4,5},{5,4},{6,7},{7,6},{8,9},{9,8},{10,11... | collective-permute-start | bytes 1179656 | tf_op jit(solution)/shard_map/ppermute | solution.py:33
  76.4 21.8 %collective-permute-start.15 = (bf16[8,4,32,256]{3,2,1,0:T(8,128)(2,1)S(1)}, bf16[8,4,32,256]{3,2,1,0:T(8,128)(2,1)S(1)}, u32[]{:S(2)}, u32[]{:S(2)}) collective-permute-start(bf16[8,4,32,256]{3,2,1,0:T(8,128)(2,1)S(1)} %get-tuple-element.78), channel_id=1, source_target_pairs={{0,1},{1,0},{2,3},{3,2},{4,5},{5,4},{6,7},{7,6},{8,9},{9,8},{10,11... | collective-permute-start | bytes 1572872 | tf_op jit(solution)/shard_map/ppermute | solution.py:33
  77.9 13.8 %collective-permute-start.23 = (bf16[2,4,32,256]{3,2,1,0:T(8,128)(2,1)S(1)}, bf16[2,4,32,256]{3,2,1,0:T(8,128)(2,1)S(1)}, u32[]{:S(2)}, u32[]{:S(2)}) collective-permute-start(bf16[2,4,32,256]{3,2,1,0:T(8,128)(2,1)S(1)} %get-tuple-element.92), channel_id=1, source_target_pairs={{0,10},{1,11},{2,8},{3,9},{4,14},{5,15},{6,12},{7,13},{8,2},{9,3},... | collective-permute-start | bytes 393224 | tf_op jit(solution)/shard_map/ppermute | solution.py:33
  81.5 10.3 %collective-permute-start.24 = (bf16[2,4,32,256]{3,2,1,0:T(8,128)(2,1)S(1)}, bf16[2,4,32,256]{3,2,1,0:T(8,128)(2,1)S(1)}, u32[]{:S(2)}, u32[]{:S(2)}) collective-permute-start(bf16[2,4,32,256]{3,2,1,0:T(8,128)(2,1)S(1)} %get-tuple-element.93), channel_id=1, source_target_pairs={{0,14},{1,15},{2,12},{3,13},{4,10},{5,11},{6,8},{7,9},{8,6},{9,7},... | collective-permute-start | bytes 393224 | tf_op jit(solution)/shard_map/ppermute | solution.py:33
  83.4 9.1 %collective-permute-start.25 = (bf16[2,4,32,256]{3,2,1,0:T(8,128)(2,1)S(1)}, bf16[2,4,32,256]{3,2,1,0:T(8,128)(2,1)S(1)}, u32[]{:S(2)}, u32[]{:S(2)}) collective-permute-start(bf16[2,4,32,256]{3,2,1,0:T(8,128)(2,1)S(1)} %get-tuple-element.94), channel_id=1, source_target_pairs={{0,2},{1,3},{2,0},{3,1},{4,6},{5,7},{6,4},{7,5},{8,10},{9,11},{10,... | collective-permute-start | bytes 393224 | tf_op jit(solution)/shard_map/ppermute | solution.py:33
  84.9 8.6 %collective-permute-start.26 = (bf16[2,4,32,256]{3,2,1,0:T(8,128)(2,1)S(1)}, bf16[2,4,32,256]{3,2,1,0:T(8,128)(2,1)S(1)}, u32[]{:S(2)}, u32[]{:S(2)}) collective-permute-start(bf16[2,4,32,256]{3,2,1,0:T(8,128)(2,1)S(1)} %get-tuple-element.95), channel_id=1, source_target_pairs={{0,4},{1,5},{2,6},{3,7},{4,0},{5,1},{6,2},{7,3},{8,12},{9,13},{10,... | collective-permute-start | bytes 393224 | tf_op jit(solution)/shard_map/ppermute | solution.py:33
  91.7 5.9 %collective-permute-start.27 = (bf16[2,4,32,256]{3,2,1,0:T(8,128)(2,1)S(1)}, bf16[2,4,32,256]{3,2,1,0:T(8,128)(2,1)S(1)}, u32[]{:S(2)}, u32[]{:S(2)}) collective-permute-start(bf16[2,4,32,256]{3,2,1,0:T(8,128)(2,1)S(1)} %get-tuple-element.97), channel_id=1, source_target_pairs={{0,6},{1,7},{2,4},{3,5},{4,2},{5,3},{6,0},{7,1},{8,14},{9,15},{10,... | collective-permute-start | bytes 393224 | tf_op jit(solution)/shard_map/ppermute | solution.py:33
  91.8 37.9 %collective-permute-start.29 = (bf16[10,4,32,256]{3,2,1,0:T(8,128)(2,1)S(1)}, bf16[10,4,32,256]{3,2,1,0:T(8,128)(2,1)S(1)}, u32[]{:S(2)}, u32[]{:S(2)}) collective-permute-start(bf16[10,4,32,256]{3,2,1,0:T(8,128)(2,1)S(1)} %gather_kernel.2.first_ref), channel_id=1, source_target_pairs={{0,16},{16,0},{1,17},{17,1},{2,18},{18,2},{3,19},{19,3},{4,20},{20... | collective-permute-start | bytes 1966088 | tf_op jit(solution)/shard_map/ppermute | solution.py:17
  97.6 32.0 %collective-permute-start.30 = (bf16[10,4,32,256]{3,2,1,0:T(8,128)(2,1)S(1)}, bf16[10,4,32,256]{3,2,1,0:T(8,128)(2,1)S(1)}, u32[]{:S(2)}, u32[]{:S(2)}) collective-permute-start(bf16[10,4,32,256]{3,2,1,0:T(8,128)(2,1)S(1)} %gather_kernel.3.second_ref), channel_id=1, source_target_pairs={{0,16},{16,0},{1,17},{17,1},{2,18},{18,2},{3,19},{19,3},{4,20},{20... | collective-permute-start | bytes 1966088 | tf_op jit(solution)/shard_map/ppermute | solution.py:17
  98.3 12.5 %collective-permute-start.16 = (bf16[2,4,32,256]{3,2,1,0:T(8,128)(2,1)S(1)}, bf16[2,4,32,256]{3,2,1,0:T(8,128)(2,1)S(1)}, u32[]{:S(2)}, u32[]{:S(2)}) collective-permute-start(bf16[2,4,32,256]{3,2,1,0:T(8,128)(2,1)S(1)} %get-tuple-element.80), channel_id=1, source_target_pairs={{0,8},{1,9},{2,10},{3,11},{4,12},{5,13},{6,14},{7,15},{8,0},{9,1},... | collective-permute-start | bytes 393224 | tf_op jit(solution)/shard_map/ppermute | solution.py:33
  98.7 17.3 %collective-permute-start.17 = (bf16[2,4,32,256]{3,2,1,0:T(8,128)(2,1)S(1)}, bf16[2,4,32,256]{3,2,1,0:T(8,128)(2,1)S(1)}, u32[]{:S(2)}, u32[]{:S(2)}) collective-permute-start(bf16[2,4,32,256]{3,2,1,0:T(8,128)(2,1)S(1)} %get-tuple-element.81), channel_id=1, source_target_pairs={{0,12},{1,13},{2,14},{3,15},{4,8},{5,9},{6,10},{7,11},{8,4},{9,5},... | collective-permute-start | bytes 393224 | tf_op jit(solution)/shard_map/ppermute | solution.py:33
  100.8 19.5 %collective-permute-start.18 = (bf16[2,4,32,256]{3,2,1,0:T(8,128)(2,1)S(1)}, bf16[2,4,32,256]{3,2,1,0:T(8,128)(2,1)S(1)}, u32[]{:S(2)}, u32[]{:S(2)}) collective-permute-start(bf16[2,4,32,256]{3,2,1,0:T(8,128)(2,1)S(1)} %get-tuple-element.82), channel_id=1, source_target_pairs={{0,10},{1,11},{2,8},{3,9},{4,14},{5,15},{6,12},{7,13},{8,2},{9,3},... | collective-permute-start | bytes 393224 | tf_op jit(solution)/shard_map/ppermute | solution.py:33
  110.8 17.1 %copy-start.3 = (bf16[1,2048,256]{2,1,0:T(8,128)(2,1)S(1)}, bf16[1,2048,256]{2,1,0:T(8,128)(2,1)}, u32[]{:S(2)}) copy-start(bf16[1,2048,256]{2,1,0:T(8,128)(2,1)} %param.6) | copy-start | bytes 3145732
  110.8 17.1 %copy-start.4 = (bf16[1,2048,256]{2,1,0:T(8,128)(2,1)S(1)}, bf16[1,2048,256]{2,1,0:T(8,128)(2,1)}, u32[]{:S(2)}) copy-start(bf16[1,2048,256]{2,1,0:T(8,128)(2,1)} %param.7) | copy-start | bytes 3145732
  110.8 9.6 %collective-permute-start.19 = (bf16[2,4,32,256]{3,2,1,0:T(8,128)(2,1)S(1)}, bf16[2,4,32,256]{3,2,1,0:T(8,128)(2,1)S(1)}, u32[]{:S(2)}, u32[]{:S(2)}) collective-permute-start(bf16[2,4,32,256]{3,2,1,0:T(8,128)(2,1)S(1)} %get-tuple-element.83), channel_id=1, source_target_pairs={{0,14},{1,15},{2,12},{3,13},{4,10},{5,11},{6,8},{7,9},{8,6},{9,7},... | collective-permute-start | bytes 393224 | tf_op jit(solution)/shard_map/ppermute | solution.py:33
  116.0 7.2 %collective-permute-start.20 = (bf16[2,4,32,256]{3,2,1,0:T(8,128)(2,1)S(1)}, bf16[2,4,32,256]{3,2,1,0:T(8,128)(2,1)S(1)}, u32[]{:S(2)}, u32[]{:S(2)}) collective-permute-start(bf16[2,4,32,256]{3,2,1,0:T(8,128)(2,1)S(1)} %get-tuple-element.84), channel_id=1, source_target_pairs={{0,2},{1,3},{2,0},{3,1},{4,6},{5,7},{6,4},{7,5},{8,10},{9,11},{10,... | collective-permute-start | bytes 393224 | tf_op jit(solution)/shard_map/ppermute | solution.py:33
  120.3 6.2 %collective-permute-start.21 = (bf16[2,4,32,256]{3,2,1,0:T(8,128)(2,1)S(1)}, bf16[2,4,32,256]{3,2,1,0:T(8,128)(2,1)S(1)}, u32[]{:S(2)}, u32[]{:S(2)}) collective-permute-start(bf16[2,4,32,256]{3,2,1,0:T(8,128)(2,1)S(1)} %get-tuple-element.85), channel_id=1, source_target_pairs={{0,4},{1,5},{2,6},{3,7},{4,0},{5,1},{6,2},{7,3},{8,12},{9,13},{10,... | collective-permute-start | bytes 393224 | tf_op jit(solution)/shard_map/ppermute | solution.py:33
  120.3 7.5 %collective-permute-start.28 = (bf16[2,4,32,256]{3,2,1,0:T(8,128)(2,1)S(1)}, bf16[2,4,32,256]{3,2,1,0:T(8,128)(2,1)S(1)}, u32[]{:S(2)}, u32[]{:S(2)}) collective-permute-start(bf16[2,4,32,256]{3,2,1,0:T(8,128)(2,1)S(1)} %get-tuple-element.99), channel_id=1, source_target_pairs={{0,6},{1,7},{2,4},{3,5},{4,2},{5,3},{6,0},{7,1},{8,14},{9,15},{10,... | collective-permute-start | bytes 393224 | tf_op jit(solution)/shard_map/ppermute | solution.py:33

commit v16 on v13

--- a/solution.py
+++ b/solution.py
@@ -25,7 +25,7 @@
     half = chips // 2
     near = list(range(1, half))
     far = list(range(half, chips, 2)) + list(range(half + 1, chips, 2))
-    mixed = far[:2] + near[:-1] + far[2:-1] + near[-1:] + far[-1:]
+    mixed = far[:1] + near[:-1] + far[1:-1] + near[-1:] + far[-1:]
     return [0] + far[:1] + near + far[1:], [0] + mixed, [0] + far + near
 
 
@@ -281,7 +281,7 @@
     def shape(*dims):
         return jax.ShapeDtypeStruct(dims, BF16)
 
-    one_ahead, two_ahead, all_far = orders(chips)
+    one_ahead, few_ahead, all_far = orders(chips)
 
     def ordered(kernel, order):
         return functools.partial(kernel, order)
@@ -342,8 +342,8 @@
         2 * column_flops,
         unblocked=[2],
     )
-    back = listed(back, two_ahead)
-    ahead = chips // 2 + 1
+    back = listed(back, few_ahead)
+    ahead = chips // 2
     messages = pack(own, permute(after(other, back[1:ahead]), 1))
     done = [(t, permute(messages[t], 2 * t)) for t in all_far[1:2]]
     back[-1] = after(back[-1], [block for _, block in done])
@@ -357,7 +357,7 @@
     other_first = swap_sequences(first_part)
     other_second = swap_sequences(second_part)
     grad_signal, left_term = call(
-        ordered(row_backward_kernel, two_ahead),
+        ordered(row_backward_kernel, few_ahead),
         me,
         [left_factor, values, first_part, second_part],
         [by_row, left],
@@ -365,7 +365,7 @@
         2 * row_flops,
     )
     grad_left, grad_right = call(
-        ordered(factor_sum_kernel, two_ahead),
+        ordered(factor_sum_kernel, few_ahead),
         me,
         [left_term, other_values, other_first, other_second, right_part],
         [left, right],

time: 127 us -> 126 us (level)
  waiting for transfers between devices: 63.9 us -> 53.7 us
  starting transfers between devices: 44.5 us -> 53.5 us
    ppermute x26, waiting for transfers between devices: 61.8 us -> 50.6 us  [permute(): return lax.ppermute(array, 'seq', [(i, i ^ offset) for i in range(seq)])]
    ppermute x26, starting transfers between devices: 40.9 us -> 47.9 us  [permute(): return lax.ppermute(array, 'seq', [(i, i ^ offset) for i in range(seq)])]
    ppermute x3, starting transfers between devices: 3.64 us -> 5.64 us  [swap_sequences(): return lax.ppermute(array, 'dp', [(0, 1), (1, 0)])]
  transfers between devices with their start and end apart: 29 -> 29, of which waited for: 16 -> 15; matrix products, arithmetic and copies ran while one was open for 0% -> 0% of each run, Pallas kernels for 9% -> 10%
where the time goes in v16:
time: 126 us
  waiting for transfers between devices  53.7 us (43%)
  starting transfers between devices  53.5 us (42%)
  Pallas kernels  16.6 us (13%)
    ppermute x26, waiting for transfers between devices, permute(): return lax.ppermute(array, 'seq', [(i, i ^ offset) for i in range(seq)])  50.6 us
    ppermute x26, starting transfers between devices, permute(): return lax.ppermute(array, 'seq', [(i, i ^ offset) for i in range(seq)])  47.9 us
    pallas_call x12, Pallas kernels, call(): pl.pallas_call(kernel, out_shape=out_shapes, in_specs=[pl.BlockSpec(memor...  16.6 us
    ppermute x3, starting transfers between devices, swap_sequences(): return lax.ppermute(array, 'dp', [(0, 1), (1, 0)])  5.64 us
    ppermute x3, waiting for transfers between devices, swap_sequences(): return lax.ppermute(array, 'dp', [(0, 1), (1, 0)])  3.13 us
  transfers between devices with their start and end apart: 29, of which 15 were waited for; matrix products, arithmetic and copies ran while one was open for 0% of the time, Pallas kernels for 10%

profile of v16, /device:TPU:0, one launch (start us, length us, event | category | flops | bytes accessed | tf_op | source)
XLA Modules:
  0.0 125.9 jit_solution(15869798490527880022)
XLA Ops:
  0.6 2.7 %product_kernel.1 = (bf16[8,4,32,256]{3,2,1,0:T(8,128)(2,1)}, bf16[8,4,32,256]{3,2,1,0:T(8,128)(2,1)}) custom-call(s32[1]{0:T(128)} %bitcast.me_ref, bf16[4,16,32,256]{3,2,1,0:T(8,128)(2,1)} %bitcast.10, bf16[4,16,32,256]{3,2,1,0:T(8,128)(2,1)} %bitcast.12), custom_call_target="tpu_custom_call" | custom-call | bytes 3145728 | tf_op jit(solution)/shard_map/product_kernel/pallas_call | solution.py:55
  3.4 0.5 collective-permute-start
  3.9 1.2 copy-done.1
  5.1 0.8 mix_kernel.1
  5.9 0.1 collective-permute-start.1
  6.0 1.9 %collective-permute-done.1.refs_3_ = bf16[8,4,32,256]{3,2,1,0:T(8,128)(2,1)S(1)} collective-permute-done((bf16[8,4,32,256]{3,2,1,0:T(8,128)(2,1)S(1)}, bf16[8,4,32,256]{3,2,1,0:T(8,128)(2,1)S(1)}, u32[]{:S(2)}, u32[]{:S(2)}) %collective-permute-start.1) | collective-permute-done | bytes 524320 | tf_op jit(solution)/shard_map/ppermute | solution.py:34
  7.9 0.1 pack_pairs_kernel.1
  8.0 3.8 %collective-permute-start.2 = (bf16[2,2,4,32,256]{4,3,2,1,0:T(8,128)(2,1)S(1)}, bf16[2,2,4,32,256]{4,3,2,1,0:T(8,128)(2,1)S(1)}, u32[]{:S(2)}, u32[]{:S(2)}) collective-permute-start(bf16[2,2,4,32,256]{4,3,2,1,0:T(8,128)(2,1)S(1)} %get-tuple-element.59), channel_id=1, source_target_pairs={{0,8},{1,9},{2,10},{3,11},{4,12},{5,13},{6,14},{7,15},{8,0},{9,1},... | collective-permute-start | bytes 786440 | tf_op jit(solution)/shard_map/ppermute | solution.py:34
  11.8 1.5 %collective-permute-start.3 = (bf16[2,2,4,32,256]{4,3,2,1,0:T(8,128)(2,1)S(1)}, bf16[2,2,4,32,256]{4,3,2,1,0:T(8,128)(2,1)S(1)}, u32[]{:S(2)}, u32[]{:S(2)}) collective-permute-start(bf16[2,2,4,32,256]{4,3,2,1,0:T(8,128)(2,1)S(1)} %get-tuple-element.60), channel_id=1, source_target_pairs={{0,2},{1,3},{2,0},{3,1},{4,6},{5,7},{6,4},{7,5},{8,10},{9,11},{10,... | collective-permute-start | bytes 786440 | tf_op jit(solution)/shard_map/ppermute | solution.py:34
  13.3 1.3 %collective-permute-start.8 = (bf16[2,4,32,256]{3,2,1,0:T(8,128)(2,1)S(1)}, bf16[2,4,32,256]{3,2,1,0:T(8,128)(2,1)S(1)}, u32[]{:S(2)}, u32[]{:S(2)}) collective-permute-start(bf16[2,4,32,256]{3,2,1,0:T(8,128)(2,1)S(1)} %get-tuple-element.65), channel_id=1, source_target_pairs={{0,14},{1,15},{2,12},{3,13},{4,10},{5,11},{6,8},{7,9},{8,6},{9,7},... | collective-permute-start | bytes 393224 | tf_op jit(solution)/shard_map/ppermute | solution.py:34
  14.6 1.5 %collective-permute-start.9 = (bf16[4,512,256]{2,1,0:T(8,128)(2,1)S(1)}, bf16[4,512,256]{2,1,0:T(8,128)(2,1)S(1)}, u32[]{:S(2)}, u32[]{:S(2)}) collective-permute-start(bf16[4,512,256]{2,1,0:T(8,128)(2,1)S(1)} %bitcast.8), channel_id=1, source_target_pairs={{0,16},{16,0},{1,17},{17,1},{2,18},{18,2},{3,19},{19,3},{4,20},{20... | collective-permute-start | bytes 3145736 | tf_op jit(solution)/shard_map/ppermute | solution.py:17
  16.1 0.3 collective-permute-start.4
  16.4 7.7 %collective-permute-done.8.refs_7_ = bf16[2,4,32,256]{3,2,1,0:T(8,128)(2,1)S(1)} collective-permute-done((bf16[2,4,32,256]{3,2,1,0:T(8,128)(2,1)S(1)}, bf16[2,4,32,256]{3,2,1,0:T(8,128)(2,1)S(1)}, u32[]{:S(2)}, u32[]{:S(2)}) %collective-permute-start.8) | collective-permute-done | bytes 131104 | tf_op jit(solution)/shard_map/ppermute | solution.py:34
  24.1 7.5 %collective-permute-start.5 = (bf16[2,2,4,32,256]{4,3,2,1,0:T(8,128)(2,1)S(1)}, bf16[2,2,4,32,256]{4,3,2,1,0:T(8,128)(2,1)S(1)}, u32[]{:S(2)}, u32[]{:S(2)}) collective-permute-start(bf16[2,2,4,32,256]{4,3,2,1,0:T(8,128)(2,1)S(1)} %get-tuple-element.62), channel_id=1, source_target_pairs={{0,6},{1,7},{2,4},{3,5},{4,2},{5,3},{6,0},{7,1},{8,14},{9,15},{10,... | collective-permute-start | bytes 786440 | tf_op jit(solution)/shard_map/ppermute | solution.py:34
  31.6 3.3 %collective-permute-start.6 = (bf16[2,2,4,32,256]{4,3,2,1,0:T(8,128)(2,1)S(1)}, bf16[2,2,4,32,256]{4,3,2,1,0:T(8,128)(2,1)S(1)}, u32[]{:S(2)}, u32[]{:S(2)}) collective-permute-start(bf16[2,2,4,32,256]{4,3,2,1,0:T(8,128)(2,1)S(1)} %get-tuple-element.63), channel_id=1, source_target_pairs={{0,12},{1,13},{2,14},{3,15},{4,8},{5,9},{6,10},{7,11},{8,4},{9,5},... | collective-permute-start | bytes 786440 | tf_op jit(solution)/shard_map/ppermute | solution.py:34
  35.0 3.4 %collective-permute-done.5.refs_4_ = bf16[2,2,4,32,256]{4,3,2,1,0:T(8,128)(2,1)S(1)} collective-permute-done((bf16[2,2,4,32,256]{4,3,2,1,0:T(8,128)(2,1)S(1)}, bf16[2,2,4,32,256]{4,3,2,1,0:T(8,128)(2,1)S(1)}, u32[]{:S(2)}, u32[]{:S(2)}) %collective-permute-start.5) | collective-permute-done | bytes 262176 | tf_op jit(solution)/shard_map/ppermute | solution.py:34
  38.3 9.5 %collective-permute-done.6.refs_5_ = bf16[2,2,4,32,256]{4,3,2,1,0:T(8,128)(2,1)S(1)} collective-permute-done((bf16[2,2,4,32,256]{4,3,2,1,0:T(8,128)(2,1)S(1)}, bf16[2,2,4,32,256]{4,3,2,1,0:T(8,128)(2,1)S(1)}, u32[]{:S(2)}, u32[]{:S(2)}) %collective-permute-start.6) | collective-permute-done | bytes 262176 | tf_op jit(solution)/shard_map/ppermute | solution.py:34
  47.8 1.4 %collective-permute-start.10 = (bf16[2,4,32,256]{3,2,1,0:T(8,128)(2,1)S(1)}, bf16[2,4,32,256]{3,2,1,0:T(8,128)(2,1)S(1)}, u32[]{:S(2)}, u32[]{:S(2)}) collective-permute-start(bf16[2,4,32,256]{3,2,1,0:T(8,128)(2,1)S(1)} %get-tuple-element.69), channel_id=1, source_target_pairs={{0,14},{1,15},{2,12},{3,13},{4,10},{5,11},{6,8},{7,9},{8,6},{9,7},... | collective-permute-start | bytes 393224 | tf_op jit(solution)/shard_map/ppermute | solution.py:34
  49.2 11.1 %collective-permute-done.7.refs_6_ = bf16[2,2,4,32,256]{4,3,2,1,0:T(8,128)(2,1)S(1)} collective-permute-done((bf16[2,2,4,32,256]{4,3,2,1,0:T(8,128)(2,1)S(1)}, bf16[2,2,4,32,256]{4,3,2,1,0:T(8,128)(2,1)S(1)}, u32[]{:S(2)}, u32[]{:S(2)}) %collective-permute-start.7) | collective-permute-done | bytes 262176 | tf_op jit(solution)/shard_map/ppermute | solution.py:34
  60.2 3.0 %column_backward_kernel.1 = (bf16[8,4,32,256]{3,2,1,0:T(8,128)(2,1)S(1)}, bf16[8,4,32,256]{3,2,1,0:T(8,128)(2,1)S(1)}, bf16[32,64,256]{2,1,0:T(8,128)(2,1)S(1)}) custom-call(s32[1]{0:T(128)} %bitcast.me_ref, bf16[32,64,64]{2,1,0:T(8,128)(2,1)S(1)} %copy-done.5, bf16[2,2,4,32,256]{4,3,2,1,0:T(8,128)(2,1)S(1)} %get-tuple-element.58.refs_0_, ...), custom_call_target="tpu_custom_call" | custom-call | flops 67108864 | bytes 4325376 | tf_op jit(solution)/shard_map/column_backward_kernel/pallas_call | solution.py:55
  63.2 0.1 collective-permute-start.11
  63.3 1.9 %collective-permute-done.11.other_ref = bf16[8,4,32,256]{3,2,1,0:T(8,128)(2,1)S(1)} collective-permute-done((bf16[8,4,32,256]{3,2,1,0:T(8,128)(2,1)S(1)}, bf16[8,4,32,256]{3,2,1,0:T(8,128)(2,1)S(1)}, u32[]{:S(2)}, u32[]{:S(2)}) %collective-permute-start.11) | collective-permute-done | bytes 524320 | tf_op jit(solution)/shard_map/ppermute | solution.py:34
  65.3 1.0 collective-permute-start.12
  66.3 1.5 %collective-permute-start.13 = (bf16[2,4,32,256]{3,2,1,0:T(8,128)(2,1)S(1)}, bf16[2,4,32,256]{3,2,1,0:T(8,128)(2,1)S(1)}, u32[]{:S(2)}, u32[]{:S(2)}) collective-permute-start(bf16[2,4,32,256]{3,2,1,0:T(8,128)(2,1)S(1)} %get-tuple-element.76), channel_id=1, source_target_pairs={{0,2},{1,3},{2,0},{3,1},{4,6},{5,7},{6,4},{7,5},{8,10},{9,11},{10,... | collective-permute-start | bytes 393224 | tf_op jit(solution)/shard_map/ppermute | solution.py:34
  67.8 2.6 %collective-permute-start.14 = (bf16[2,4,32,256]{3,2,1,0:T(8,128)(2,1)S(1)}, bf16[2,4,32,256]{3,2,1,0:T(8,128)(2,1)S(1)}, u32[]{:S(2)}, u32[]{:S(2)}) collective-permute-start(bf16[2,4,32,256]{3,2,1,0:T(8,128)(2,1)S(1)} %get-tuple-element.77), channel_id=1, source_target_pairs={{0,4},{1,5},{2,6},{3,7},{4,0},{5,1},{6,2},{7,3},{8,12},{9,13},{10,... | collective-permute-start | bytes 393224 | tf_op jit(solution)/shard_map/ppermute | solution.py:34
  70.4 3.3 %column_forward_kernel.1 = (bf16[8,4,32,256]{3,2,1,0:T(8,128)(2,1)S(1)}, bf16[8,4,32,256]{3,2,1,0:T(8,128)(2,1)S(1)}, bf16[512,256]{1,0:T(8,128)(2,1)S(1)}) custom-call(s32[1]{0:T(128)} %bitcast.me_ref, bf16[32,64,64]{2,1,0:T(8,128)(2,1)S(1)} %copy-done.5, bf16[32,64,256]{2,1,0:T(8,128)(2,1)S(1)} %get-tuple-element.66.grad_ref, ...), custom_call_target="tpu_custom_call" | custom-call | flops 134217728 | bytes 5636096 | tf_op jit(solution)/shard_map/column_forward_kernel/pallas_call | solution.py:55
  73.7 1.0 collective-permute-done.12.refs_1_
  74.7 1.3 %collective-permute-done.14.refs_3_ = bf16[2,4,32,256]{3,2,1,0:T(8,128)(2,1)S(1)} collective-permute-done((bf16[2,4,32,256]{3,2,1,0:T(8,128)(2,1)S(1)}, bf16[2,4,32,256]{3,2,1,0:T(8,128)(2,1)S(1)}, u32[]{:S(2)}, u32[]{:S(2)}) %collective-permute-start.14) | collective-permute-done | bytes 131104 | tf_op jit(solution)/shard_map/ppermute | solution.py:34
  76.0 1.9 %collective-permute-start.25 = (bf16[2,4,32,256]{3,2,1,0:T(8,128)(2,1)S(1)}, bf16[2,4,32,256]{3,2,1,0:T(8,128)(2,1)S(1)}, u32[]{:S(2)}, u32[]{:S(2)}) collective-permute-start(bf16[2,4,32,256]{3,2,1,0:T(8,128)(2,1)S(1)} %get-tuple-element.92), channel_id=1, source_target_pairs={{0,14},{1,15},{2,12},{3,13},{4,10},{5,11},{6,8},{7,9},{8,6},{9,7},... | collective-permute-start | bytes 393224 | tf_op jit(solution)/shard_map/ppermute | solution.py:34
  78.0 1.6 %collective-permute-start.26 = (bf16[12,4,32,256]{3,2,1,0:T(8,128)(2,1)S(1)}, bf16[12,4,32,256]{3,2,1,0:T(8,128)(2,1)S(1)}, u32[]{:S(2)}, u32[]{:S(2)}) collective-permute-start(bf16[12,4,32,256]{3,2,1,0:T(8,128)(2,1)S(1)} %gather_kernel.2.first_ref), channel_id=1, source_target_pairs={{0,16},{16,0},{1,17},{17,1},{2,18},{18,2},{3,19},{19,3},{4,20},{20... | collective-permute-start | bytes 2359304 | tf_op jit(solution)/shard_map/ppermute | solution.py:17
  79.5 1.9 %collective-permute-start.22 = (bf16[2,4,32,256]{3,2,1,0:T(8,128)(2,1)S(1)}, bf16[2,4,32,256]{3,2,1,0:T(8,128)(2,1)S(1)}, u32[]{:S(2)}, u32[]{:S(2)}) collective-permute-start(bf16[2,4,32,256]{3,2,1,0:T(8,128)(2,1)S(1)} %get-tuple-element.89), channel_id=1, source_target_pairs={{0,12},{1,13},{2,14},{3,15},{4,8},{5,9},{6,10},{7,11},{8,4},{9,5},... | collective-permute-start | bytes 393224 | tf_op jit(solution)/shard_map/ppermute | solution.py:34
  81.5 3.9 %collective-permute-start.23 = (bf16[2,4,32,256]{3,2,1,0:T(8,128)(2,1)S(1)}, bf16[2,4,32,256]{3,2,1,0:T(8,128)(2,1)S(1)}, u32[]{:S(2)}, u32[]{:S(2)}) collective-permute-start(bf16[2,4,32,256]{3,2,1,0:T(8,128)(2,1)S(1)} %get-tuple-element.90), channel_id=1, source_target_pairs={{0,10},{1,11},{2,8},{3,9},{4,14},{5,15},{6,12},{7,13},{8,2},{9,3},... | collective-permute-start | bytes 393224 | tf_op jit(solution)/shard_map/ppermute | solution.py:34
  85.4 7.8 %collective-permute-start.24 = (bf16[2,4,32,256]{3,2,1,0:T(8,128)(2,1)S(1)}, bf16[2,4,32,256]{3,2,1,0:T(8,128)(2,1)S(1)}, u32[]{:S(2)}, u32[]{:S(2)}) collective-permute-start(bf16[2,4,32,256]{3,2,1,0:T(8,128)(2,1)S(1)} %get-tuple-element.91), channel_id=1, source_target_pairs={{0,6},{1,7},{2,4},{3,5},{4,2},{5,3},{6,0},{7,1},{8,14},{9,15},{10,... | collective-permute-start | bytes 393224 | tf_op jit(solution)/shard_map/ppermute | solution.py:34
  93.2 4.9 %collective-permute-done.16.refs_1_ = bf16[2,4,32,256]{3,2,1,0:T(8,128)(2,1)S(1)} collective-permute-done((bf16[2,4,32,256]{3,2,1,0:T(8,128)(2,1)S(1)}, bf16[2,4,32,256]{3,2,1,0:T(8,128)(2,1)S(1)}, u32[]{:S(2)}, u32[]{:S(2)}) %collective-permute-start.16) | collective-permute-done | bytes 131104 | tf_op jit(solution)/shard_map/ppermute | solution.py:34
  98.1 3.4 %collective-permute-done.23.refs_1_ = bf16[2,4,32,256]{3,2,1,0:T(8,128)(2,1)S(1)} collective-permute-done((bf16[2,4,32,256]{3,2,1,0:T(8,128)(2,1)S(1)}, bf16[2,4,32,256]{3,2,1,0:T(8,128)(2,1)S(1)}, u32[]{:S(2)}, u32[]{:S(2)}) %collective-permute-start.23) | collective-permute-done | bytes 131104 | tf_op jit(solution)/shard_map/ppermute | solution.py:34
  101.6 0.2 collective-permute-done.24.refs_2_
  101.8 2.6 %collective-permute-start.27 = (bf16[8,4,32,256]{3,2,1,0:T(8,128)(2,1)S(1)}, bf16[8,4,32,256]{3,2,1,0:T(8,128)(2,1)S(1)}, u32[]{:S(2)}, u32[]{:S(2)}) collective-permute-start(bf16[8,4,32,256]{3,2,1,0:T(8,128)(2,1)S(1)} %gather_kernel.3.second_ref), channel_id=1, source_target_pairs={{0,16},{16,0},{1,17},{17,1},{2,18},{18,2},{3,19},{19,3},{4,20},{20... | collective-permute-start | bytes 1572872 | tf_op jit(solution)/shard_map/ppermute | solution.py:17
  104.4 1.9 %collective-permute-start.17 = (bf16[2,4,32,256]{3,2,1,0:T(8,128)(2,1)S(1)}, bf16[2,4,32,256]{3,2,1,0:T(8,128)(2,1)S(1)}, u32[]{:S(2)}, u32[]{:S(2)}) collective-permute-start(bf16[2,4,32,256]{3,2,1,0:T(8,128)(2,1)S(1)} %get-tuple-element.81), channel_id=1, source_target_pairs={{0,12},{1,13},{2,14},{3,15},{4,8},{5,9},{6,10},{7,11},{8,4},{9,5},... | collective-permute-start | bytes 393224 | tf_op jit(solution)/shard_map/ppermute | solution.py:34
  106.4 1.9 %collective-permute-start.19 = (bf16[2,4,32,256]{3,2,1,0:T(8,128)(2,1)S(1)}, bf16[2,4,32,256]{3,2,1,0:T(8,128)(2,1)S(1)}, u32[]{:S(2)}, u32[]{:S(2)}) collective-permute-start(bf16[2,4,32,256]{3,2,1,0:T(8,128)(2,1)S(1)} %get-tuple-element.83), channel_id=1, source_target_pairs={{0,14},{1,15},{2,12},{3,13},{4,10},{5,11},{6,8},{7,9},{8,6},{9,7},... | collective-permute-start | bytes 393224 | tf_op jit(solution)/shard_map/ppermute | solution.py:34
  108.3 2.3 %row_backward_kernel.1 = (bf16[4,512,256]{2,1,0:T(8,128)(2,1)}, bf16[4,512,512]{2,1,0:T(8,128)(2,1)S(1)}) custom-call(s32[1]{0:T(128)} %bitcast.me_ref, bf16[4,512,512]{2,1,0:T(8,128)(2,1)S(1)} %copy-done, bf16[4,512,256]{2,1,0:T(8,128)(2,1)S(1)} %bitcast.9, bf16[12,4,32,256]{3,2,1,0:T(8,128)(2,1)S(1)} %gather_kernel.2.first_ref, ...), custom_call_target="tpu_custom_call" | custom-call | flops 1073741824 | bytes 7602176 | tf_op jit(solution)/shard_map/row_backward_kernel/pallas_call | solution.py:55
  110.6 1.4 %collective-permute-start.20 = (bf16[2,4,32,256]{3,2,1,0:T(8,128)(2,1)S(1)}, bf16[2,4,32,256]{3,2,1,0:T(8,128)(2,1)S(1)}, u32[]{:S(2)}, u32[]{:S(2)}) collective-permute-start(bf16[2,4,32,256]{3,2,1,0:T(8,128)(2,1)S(1)} %get-tuple-element.84), channel_id=1, source_target_pairs={{0,2},{1,3},{2,0},{3,1},{4,6},{5,7},{6,4},{7,5},{8,10},{9,11},{10,... | collective-permute-start | bytes 393224 | tf_op jit(solution)/shard_map/ppermute | solution.py:34
  112.0 3.1 %collective-permute-done.27.second_ref = bf16[8,4,32,256]{3,2,1,0:T(8,128)(2,1)S(1)} collective-permute-done((bf16[8,4,32,256]{3,2,1,0:T(8,128)(2,1)S(1)}, bf16[8,4,32,256]{3,2,1,0:T(8,128)(2,1)S(1)}, u32[]{:S(2)}, u32[]{:S(2)}) %collective-permute-start.27) | collective-permute-done | bytes 524320 | tf_op jit(solution)/shard_map/ppermute | solution.py:17
  115.2 2.4 %factor_sum_kernel.1 = (bf16[4,512,512]{2,1,0:T(8,128)(2,1)}, bf16[32,64,64]{2,1,0:T(8,128)(2,1)}) custom-call(s32[1]{0:T(128)} %bitcast.me_ref, bf16[4,512,512]{2,1,0:T(8,128)(2,1)S(1)} %get-tuple-element.94.term_ref, bf16[4,512,256]{2,1,0:T(8,128)(2,1)S(1)} %collective-permute-done.9.after_ref.values_ref, ...), custom_call_target="tpu_custom_call" | custom-call | flops 536870912 | bytes 7077888 | tf_op jit(solution)/shard_map/factor_sum_kernel/pallas_call | solution.py:55
  117.6 2.2 %collective-permute-start.28 = (bf16[2,4,32,256]{3,2,1,0:T(8,128)(2,1)S(1)}, bf16[2,4,32,256]{3,2,1,0:T(8,128)(2,1)S(1)}, u32[]{:S(2)}, u32[]{:S(2)}) collective-permute-start(bf16[2,4,32,256]{3,2,1,0:T(8,128)(2,1)S(1)} %get-tuple-element.96), channel_id=1, source_target_pairs={{0,6},{1,7},{2,4},{3,5},{4,2},{5,3},{6,0},{7,1},{8,14},{9,15},{10,... | collective-permute-start | bytes 393224 | tf_op jit(solution)/shard_map/ppermute | solution.py:34
  119.8 1.2 collective-permute-done.18.refs_3_
  120.9 0.9 collective-permute-done.21.refs_6_
  121.9 2.3 %collective-permute-done.28.refs_7_ = bf16[2,4,32,256]{3,2,1,0:T(8,128)(2,1)S(1)} collective-permute-done((bf16[2,4,32,256]{3,2,1,0:T(8,128)(2,1)S(1)}, bf16[2,4,32,256]{3,2,1,0:T(8,128)(2,1)S(1)}, u32[]{:S(2)}, u32[]{:S(2)}) %collective-permute-start.28) | collective-permute-done | bytes 131104 | tf_op jit(solution)/shard_map/ppermute | solution.py:34
  124.1 1.8 %output_kernel.1 = (bf16[4,16,32,256]{3,2,1,0:T(8,128)(2,1)}, bf16[4,16,32,256]{3,2,1,0:T(8,128)(2,1)}) custom-call(s32[1]{0:T(128)} %bitcast.me_ref, bf16[4,16,32,256]{3,2,1,0:T(8,128)(2,1)S(1)} %bitcast.11, bf16[4,16,32,256]{3,2,1,0:T(8,128)(2,1)S(1)} %bitcast.13, bf16[2,4,32,256]{3,2,1,0:T(8,128)(2,1)S(1)} %get-tuple-element.79.refs_0_, ...), custom_call_target="tpu_custom_call" | custom-call | bytes 5242880 | tf_op jit(solution)/shard_map/output_kernel/pallas_call | solution.py:55
  (36 shorter events, 0.4 us)
Async XLA Ops:
  0.6 3.3 %copy-start = (bf16[4,512,512]{2,1,0:T(8,128)(2,1)S(1)}, bf16[4,512,512]{2,1,0:T(8,128)(2,1)}, u32[]{:S(2)}) copy-start(bf16[4,512,512]{2,1,0:T(8,128)(2,1)} %left_ref.3) | copy-start | bytes 6291460
  3.4 2.7 %collective-permute-start = (bf16[8,4,32,256]{3,2,1,0:T(8,128)(2,1)}, bf16[8,4,32,256]{3,2,1,0:T(8,128)(2,1)S(1)}, u32[]{:S(2)}, u32[]{:S(2)}) collective-permute-start(bf16[8,4,32,256]{3,2,1,0:T(8,128)(2,1)} %get-tuple-element.54), channel_id=1, source_target_pairs={{0,1},{1,0},{2,3},{3,2},{4,5},{5,4},{6,7},{7,6},{8,9},{9,8},{10,11... | collective-permute-start | bytes 1572872 | tf_op jit(solution)/shard_map/ppermute | solution.py:34
  3.9 1.2 copy-start.1
  5.1 2.8 %copy-start.6 = (bf16[8,4,32,256]{3,2,1,0:T(8,128)(2,1)S(1)}, bf16[8,4,32,256]{3,2,1,0:T(8,128)(2,1)}, u32[]{:S(2)}) copy-start(bf16[8,4,32,256]{3,2,1,0:T(8,128)(2,1)} %get-tuple-element.53.refs_0_) | copy-start | bytes 1572868
  5.1 9.5 %copy-start.2 = (bf16[1,2048,256]{2,1,0:T(8,128)(2,1)S(1)}, bf16[1,2048,256]{2,1,0:T(8,128)(2,1)}, u32[]{:S(2)}) copy-start(bf16[1,2048,256]{2,1,0:T(8,128)(2,1)} %param.5) | copy-start | bytes 3145732
  5.1 55.1 %copy-start.5 = (bf16[32,64,64]{2,1,0:T(8,128)(2,1)S(1)}, bf16[32,64,64]{2,1,0:T(8,128)(2,1)}, u32[]{:S(2)}) copy-start(bf16[32,64,64]{2,1,0:T(8,128)(2,1)} %right_ref.3) | copy-start | bytes 786436
  5.9 2.0 %collective-permute-start.1 = (bf16[8,4,32,256]{3,2,1,0:T(8,128)(2,1)S(1)}, bf16[8,4,32,256]{3,2,1,0:T(8,128)(2,1)S(1)}, u32[]{:S(2)}, u32[]{:S(2)}) collective-permute-start(bf16[8,4,32,256]{3,2,1,0:T(8,128)(2,1)S(1)} %get-tuple-element.57), channel_id=1, source_target_pairs={{0,1},{1,0},{2,3},{3,2},{4,5},{5,4},{6,7},{7,6},{8,9},{9,8},{10,11... | collective-permute-start | bytes 1572872 | tf_op jit(solution)/shard_map/ppermute | solution.py:34
  8.0 23.6 %collective-permute-start.2 = (bf16[2,2,4,32,256]{4,3,2,1,0:T(8,128)(2,1)S(1)}, bf16[2,2,4,32,256]{4,3,2,1,0:T(8,128)(2,1)S(1)}, u32[]{:S(2)}, u32[]{:S(2)}) collective-permute-start(bf16[2,2,4,32,256]{4,3,2,1,0:T(8,128)(2,1)S(1)} %get-tuple-element.59), channel_id=1, source_target_pairs={{0,8},{1,9},{2,10},{3,11},{4,12},{5,13},{6,14},{7,15},{8,0},{9,1},... | collective-permute-start | bytes 786440 | tf_op jit(solution)/shard_map/ppermute | solution.py:34
  11.8 23.1 %collective-permute-start.3 = (bf16[2,2,4,32,256]{4,3,2,1,0:T(8,128)(2,1)S(1)}, bf16[2,2,4,32,256]{4,3,2,1,0:T(8,128)(2,1)S(1)}, u32[]{:S(2)}, u32[]{:S(2)}) collective-permute-start(bf16[2,2,4,32,256]{4,3,2,1,0:T(8,128)(2,1)S(1)} %get-tuple-element.60), channel_id=1, source_target_pairs={{0,2},{1,3},{2,0},{3,1},{4,6},{5,7},{6,4},{7,5},{8,10},{9,11},{10,... | collective-permute-start | bytes 786440 | tf_op jit(solution)/shard_map/ppermute | solution.py:34
  13.3 10.8 %collective-permute-start.8 = (bf16[2,4,32,256]{3,2,1,0:T(8,128)(2,1)S(1)}, bf16[2,4,32,256]{3,2,1,0:T(8,128)(2,1)S(1)}, u32[]{:S(2)}, u32[]{:S(2)}) collective-permute-start(bf16[2,4,32,256]{3,2,1,0:T(8,128)(2,1)S(1)} %get-tuple-element.65), channel_id=1, source_target_pairs={{0,14},{1,15},{2,12},{3,13},{4,10},{5,11},{6,8},{7,9},{8,6},{9,7},... | collective-permute-start | bytes 393224 | tf_op jit(solution)/shard_map/ppermute | solution.py:34
  14.6 55.7 %collective-permute-start.9 = (bf16[4,512,256]{2,1,0:T(8,128)(2,1)S(1)}, bf16[4,512,256]{2,1,0:T(8,128)(2,1)S(1)}, u32[]{:S(2)}, u32[]{:S(2)}) collective-permute-start(bf16[4,512,256]{2,1,0:T(8,128)(2,1)S(1)} %bitcast.8), channel_id=1, source_target_pairs={{0,16},{16,0},{1,17},{17,1},{2,18},{18,2},{3,19},{19,3},{4,20},{20... | collective-permute-start | bytes 3145736 | tf_op jit(solution)/shard_map/ppermute | solution.py:17
  16.1 18.8 %collective-permute-start.4 = (bf16[2,2,4,32,256]{4,3,2,1,0:T(8,128)(2,1)S(1)}, bf16[2,2,4,32,256]{4,3,2,1,0:T(8,128)(2,1)S(1)}, u32[]{:S(2)}, u32[]{:S(2)}) collective-permute-start(bf16[2,2,4,32,256]{4,3,2,1,0:T(8,128)(2,1)S(1)} %get-tuple-element.61), channel_id=1, source_target_pairs={{0,4},{1,5},{2,6},{3,7},{4,0},{5,1},{6,2},{7,3},{8,12},{9,13},{10,... | collective-permute-start | bytes 786440 | tf_op jit(solution)/shard_map/ppermute | solution.py:34
  24.1 14.2 %collective-permute-start.5 = (bf16[2,2,4,32,256]{4,3,2,1,0:T(8,128)(2,1)S(1)}, bf16[2,2,4,32,256]{4,3,2,1,0:T(8,128)(2,1)S(1)}, u32[]{:S(2)}, u32[]{:S(2)}) collective-permute-start(bf16[2,2,4,32,256]{4,3,2,1,0:T(8,128)(2,1)S(1)} %get-tuple-element.62), channel_id=1, source_target_pairs={{0,6},{1,7},{2,4},{3,5},{4,2},{5,3},{6,0},{7,1},{8,14},{9,15},{10,... | collective-permute-start | bytes 786440 | tf_op jit(solution)/shard_map/ppermute | solution.py:34
  31.6 16.2 %collective-permute-start.6 = (bf16[2,2,4,32,256]{4,3,2,1,0:T(8,128)(2,1)S(1)}, bf16[2,2,4,32,256]{4,3,2,1,0:T(8,128)(2,1)S(1)}, u32[]{:S(2)}, u32[]{:S(2)}) collective-permute-start(bf16[2,2,4,32,256]{4,3,2,1,0:T(8,128)(2,1)S(1)} %get-tuple-element.63), channel_id=1, source_target_pairs={{0,12},{1,13},{2,14},{3,15},{4,8},{5,9},{6,10},{7,11},{8,4},{9,5},... | collective-permute-start | bytes 786440 | tf_op jit(solution)/shard_map/ppermute | solution.py:34
  34.9 25.3 %collective-permute-start.7 = (bf16[2,2,4,32,256]{4,3,2,1,0:T(8,128)(2,1)S(1)}, bf16[2,2,4,32,256]{4,3,2,1,0:T(8,128)(2,1)S(1)}, u32[]{:S(2)}, u32[]{:S(2)}) collective-permute-start(bf16[2,2,4,32,256]{4,3,2,1,0:T(8,128)(2,1)S(1)} %get-tuple-element.64), channel_id=1, source_target_pairs={{0,10},{1,11},{2,8},{3,9},{4,14},{5,15},{6,12},{7,13},{8,2},{9,3},... | collective-permute-start | bytes 786440 | tf_op jit(solution)/shard_map/ppermute | solution.py:34
  47.8 15.4 %collective-permute-start.10 = (bf16[2,4,32,256]{3,2,1,0:T(8,128)(2,1)S(1)}, bf16[2,4,32,256]{3,2,1,0:T(8,128)(2,1)S(1)}, u32[]{:S(2)}, u32[]{:S(2)}) collective-permute-start(bf16[2,4,32,256]{3,2,1,0:T(8,128)(2,1)S(1)} %get-tuple-element.69), channel_id=1, source_target_pairs={{0,14},{1,15},{2,12},{3,13},{4,10},{5,11},{6,8},{7,9},{8,6},{9,7},... | collective-permute-start | bytes 393224 | tf_op jit(solution)/shard_map/ppermute | solution.py:34
  63.2 2.0 %collective-permute-start.11 = (bf16[8,4,32,256]{3,2,1,0:T(8,128)(2,1)S(1)}, bf16[8,4,32,256]{3,2,1,0:T(8,128)(2,1)S(1)}, u32[]{:S(2)}, u32[]{:S(2)}) collective-permute-start(bf16[8,4,32,256]{3,2,1,0:T(8,128)(2,1)S(1)} %get-tuple-element.74), channel_id=1, source_target_pairs={{0,1},{1,0},{2,3},{3,2},{4,5},{5,4},{6,7},{7,6},{8,9},{9,8},{10,11... | collective-permute-start | bytes 1572872 | tf_op jit(solution)/shard_map/ppermute | solution.py:34
  65.3 9.4 %collective-permute-start.12 = (bf16[2,4,32,256]{3,2,1,0:T(8,128)(2,1)S(1)}, bf16[2,4,32,256]{3,2,1,0:T(8,128)(2,1)S(1)}, u32[]{:S(2)}, u32[]{:S(2)}) collective-permute-start(bf16[2,4,32,256]{3,2,1,0:T(8,128)(2,1)S(1)} %get-tuple-element.75), channel_id=1, source_target_pairs={{0,8},{1,9},{2,10},{3,11},{4,12},{5,13},{6,14},{7,15},{8,0},{9,1},... | collective-permute-start | bytes 393224 | tf_op jit(solution)/shard_map/ppermute | solution.py:34
  66.3 8.4 %collective-permute-start.13 = (bf16[2,4,32,256]{3,2,1,0:T(8,128)(2,1)S(1)}, bf16[2,4,32,256]{3,2,1,0:T(8,128)(2,1)S(1)}, u32[]{:S(2)}, u32[]{:S(2)}) collective-permute-start(bf16[2,4,32,256]{3,2,1,0:T(8,128)(2,1)S(1)} %get-tuple-element.76), channel_id=1, source_target_pairs={{0,2},{1,3},{2,0},{3,1},{4,6},{5,7},{6,4},{7,5},{8,10},{9,11},{10,... | collective-permute-start | bytes 393224 | tf_op jit(solution)/shard_map/ppermute | solution.py:34
  67.8 8.2 %collective-permute-start.14 = (bf16[2,4,32,256]{3,2,1,0:T(8,128)(2,1)S(1)}, bf16[2,4,32,256]{3,2,1,0:T(8,128)(2,1)S(1)}, u32[]{:S(2)}, u32[]{:S(2)}) collective-permute-start(bf16[2,4,32,256]{3,2,1,0:T(8,128)(2,1)S(1)} %get-tuple-element.77), channel_id=1, source_target_pairs={{0,4},{1,5},{2,6},{3,7},{4,0},{5,1},{6,2},{7,3},{8,12},{9,13},{10,... | collective-permute-start | bytes 393224 | tf_op jit(solution)/shard_map/ppermute | solution.py:34
  76.0 5.4 %collective-permute-start.15 = (bf16[8,4,32,256]{3,2,1,0:T(8,128)(2,1)S(1)}, bf16[8,4,32,256]{3,2,1,0:T(8,128)(2,1)S(1)}, u32[]{:S(2)}, u32[]{:S(2)}) collective-permute-start(bf16[8,4,32,256]{3,2,1,0:T(8,128)(2,1)S(1)} %get-tuple-element.78), channel_id=1, source_target_pairs={{0,1},{1,0},{2,3},{3,2},{4,5},{5,4},{6,7},{7,6},{8,9},{9,8},{10,11... | collective-permute-start | bytes 1572872 | tf_op jit(solution)/shard_map/ppermute | solution.py:34
  76.0 9.4 %collective-permute-start.25 = (bf16[2,4,32,256]{3,2,1,0:T(8,128)(2,1)S(1)}, bf16[2,4,32,256]{3,2,1,0:T(8,128)(2,1)S(1)}, u32[]{:S(2)}, u32[]{:S(2)}) collective-permute-start(bf16[2,4,32,256]{3,2,1,0:T(8,128)(2,1)S(1)} %get-tuple-element.92), channel_id=1, source_target_pairs={{0,14},{1,15},{2,12},{3,13},{4,10},{5,11},{6,8},{7,9},{8,6},{9,7},... | collective-permute-start | bytes 393224 | tf_op jit(solution)/shard_map/ppermute | solution.py:34
  78.0 32.7 %collective-permute-start.26 = (bf16[12,4,32,256]{3,2,1,0:T(8,128)(2,1)S(1)}, bf16[12,4,32,256]{3,2,1,0:T(8,128)(2,1)S(1)}, u32[]{:S(2)}, u32[]{:S(2)}) collective-permute-start(bf16[12,4,32,256]{3,2,1,0:T(8,128)(2,1)S(1)} %gather_kernel.2.first_ref), channel_id=1, source_target_pairs={{0,16},{16,0},{1,17},{17,1},{2,18},{18,2},{3,19},{19,3},{4,20},{20... | collective-permute-start | bytes 2359304 | tf_op jit(solution)/shard_map/ppermute | solution.py:17
  79.5 18.6 %collective-permute-start.22 = (bf16[2,4,32,256]{3,2,1,0:T(8,128)(2,1)S(1)}, bf16[2,4,32,256]{3,2,1,0:T(8,128)(2,1)S(1)}, u32[]{:S(2)}, u32[]{:S(2)}) collective-permute-start(bf16[2,4,32,256]{3,2,1,0:T(8,128)(2,1)S(1)} %get-tuple-element.89), channel_id=1, source_target_pairs={{0,12},{1,13},{2,14},{3,15},{4,8},{5,9},{6,10},{7,11},{8,4},{9,5},... | collective-permute-start | bytes 393224 | tf_op jit(solution)/shard_map/ppermute | solution.py:34
  81.5 16.6 %collective-permute-start.16 = (bf16[2,4,32,256]{3,2,1,0:T(8,128)(2,1)S(1)}, bf16[2,4,32,256]{3,2,1,0:T(8,128)(2,1)S(1)}, u32[]{:S(2)}, u32[]{:S(2)}) collective-permute-start(bf16[2,4,32,256]{3,2,1,0:T(8,128)(2,1)S(1)} %get-tuple-element.80), channel_id=1, source_target_pairs={{0,8},{1,9},{2,10},{3,11},{4,12},{5,13},{6,14},{7,15},{8,0},{9,1},... | collective-permute-start | bytes 393224 | tf_op jit(solution)/shard_map/ppermute | solution.py:34
  81.5 20.0 %collective-permute-start.23 = (bf16[2,4,32,256]{3,2,1,0:T(8,128)(2,1)S(1)}, bf16[2,4,32,256]{3,2,1,0:T(8,128)(2,1)S(1)}, u32[]{:S(2)}, u32[]{:S(2)}) collective-permute-start(bf16[2,4,32,256]{3,2,1,0:T(8,128)(2,1)S(1)} %get-tuple-element.90), channel_id=1, source_target_pairs={{0,10},{1,11},{2,8},{3,9},{4,14},{5,15},{6,12},{7,13},{8,2},{9,3},... | collective-permute-start | bytes 393224 | tf_op jit(solution)/shard_map/ppermute | solution.py:34
  85.4 16.4 %collective-permute-start.24 = (bf16[2,4,32,256]{3,2,1,0:T(8,128)(2,1)S(1)}, bf16[2,4,32,256]{3,2,1,0:T(8,128)(2,1)S(1)}, u32[]{:S(2)}, u32[]{:S(2)}) collective-permute-start(bf16[2,4,32,256]{3,2,1,0:T(8,128)(2,1)S(1)} %get-tuple-element.91), channel_id=1, source_target_pairs={{0,6},{1,7},{2,4},{3,5},{4,2},{5,3},{6,0},{7,1},{8,14},{9,15},{10,... | collective-permute-start | bytes 393224 | tf_op jit(solution)/shard_map/ppermute | solution.py:34
  101.8 13.3 %collective-permute-start.27 = (bf16[8,4,32,256]{3,2,1,0:T(8,128)(2,1)S(1)}, bf16[8,4,32,256]{3,2,1,0:T(8,128)(2,1)S(1)}, u32[]{:S(2)}, u32[]{:S(2)}) collective-permute-start(bf16[8,4,32,256]{3,2,1,0:T(8,128)(2,1)S(1)} %gather_kernel.3.second_ref), channel_id=1, source_target_pairs={{0,16},{16,0},{1,17},{17,1},{2,18},{18,2},{3,19},{19,3},{4,20},{20... | collective-permute-start | bytes 1572872 | tf_op jit(solution)/shard_map/ppermute | solution.py:17
  104.4 13.1 %collective-permute-start.17 = (bf16[2,4,32,256]{3,2,1,0:T(8,128)(2,1)S(1)}, bf16[2,4,32,256]{3,2,1,0:T(8,128)(2,1)S(1)}, u32[]{:S(2)}, u32[]{:S(2)}) collective-permute-start(bf16[2,4,32,256]{3,2,1,0:T(8,128)(2,1)S(1)} %get-tuple-element.81), channel_id=1, source_target_pairs={{0,12},{1,13},{2,14},{3,15},{4,8},{5,9},{6,10},{7,11},{8,4},{9,5},... | collective-permute-start | bytes 393224 | tf_op jit(solution)/shard_map/ppermute | solution.py:34
  106.4 14.5 %collective-permute-start.18 = (bf16[2,4,32,256]{3,2,1,0:T(8,128)(2,1)S(1)}, bf16[2,4,32,256]{3,2,1,0:T(8,128)(2,1)S(1)}, u32[]{:S(2)}, u32[]{:S(2)}) collective-permute-start(bf16[2,4,32,256]{3,2,1,0:T(8,128)(2,1)S(1)} %get-tuple-element.82), channel_id=1, source_target_pairs={{0,10},{1,11},{2,8},{3,9},{4,14},{5,15},{6,12},{7,13},{8,2},{9,3},... | collective-permute-start | bytes 393224 | tf_op jit(solution)/shard_map/ppermute | solution.py:34
  106.4 14.5 %collective-permute-start.19 = (bf16[2,4,32,256]{3,2,1,0:T(8,128)(2,1)S(1)}, bf16[2,4,32,256]{3,2,1,0:T(8,128)(2,1)S(1)}, u32[]{:S(2)}, u32[]{:S(2)}) collective-permute-start(bf16[2,4,32,256]{3,2,1,0:T(8,128)(2,1)S(1)} %get-tuple-element.83), channel_id=1, source_target_pairs={{0,14},{1,15},{2,12},{3,13},{4,10},{5,11},{6,8},{7,9},{8,6},{9,7},... | collective-permute-start | bytes 393224 | tf_op jit(solution)/shard_map/ppermute | solution.py:34
  110.6 10.3 %collective-permute-start.20 = (bf16[2,4,32,256]{3,2,1,0:T(8,128)(2,1)S(1)}, bf16[2,4,32,256]{3,2,1,0:T(8,128)(2,1)S(1)}, u32[]{:S(2)}, u32[]{:S(2)}) collective-permute-start(bf16[2,4,32,256]{3,2,1,0:T(8,128)(2,1)S(1)} %get-tuple-element.84), channel_id=1, source_target_pairs={{0,2},{1,3},{2,0},{3,1},{4,6},{5,7},{6,4},{7,5},{8,10},{9,11},{10,... | collective-permute-start | bytes 393224 | tf_op jit(solution)/shard_map/ppermute | solution.py:34
  115.2 6.7 %collective-permute-start.21 = (bf16[2,4,32,256]{3,2,1,0:T(8,128)(2,1)S(1)}, bf16[2,4,32,256]{3,2,1,0:T(8,128)(2,1)S(1)}, u32[]{:S(2)}, u32[]{:S(2)}) collective-permute-start(bf16[2,4,32,256]{3,2,1,0:T(8,128)(2,1)S(1)} %get-tuple-element.85), channel_id=1, source_target_pairs={{0,4},{1,5},{2,6},{3,7},{4,0},{5,1},{6,2},{7,3},{8,12},{9,13},{10,... | collective-permute-start | bytes 393224 | tf_op jit(solution)/shard_map/ppermute | solution.py:34
  115.2 9.0 %copy-start.3 = (bf16[1,2048,256]{2,1,0:T(8,128)(2,1)S(1)}, bf16[1,2048,256]{2,1,0:T(8,128)(2,1)}, u32[]{:S(2)}) copy-start(bf16[1,2048,256]{2,1,0:T(8,128)(2,1)} %param.6) | copy-start | bytes 3145732
  115.2 9.0 %copy-start.4 = (bf16[1,2048,256]{2,1,0:T(8,128)(2,1)S(1)}, bf16[1,2048,256]{2,1,0:T(8,128)(2,1)}, u32[]{:S(2)}) copy-start(bf16[1,2048,256]{2,1,0:T(8,128)(2,1)} %param.7) | copy-start | bytes 3145732
  117.6 6.6 %collective-permute-start.28 = (bf16[2,4,32,256]{3,2,1,0:T(8,128)(2,1)S(1)}, bf16[2,4,32,256]{3,2,1,0:T(8,128)(2,1)S(1)}, u32[]{:S(2)}, u32[]{:S(2)}) collective-permute-start(bf16[2,4,32,256]{3,2,1,0:T(8,128)(2,1)S(1)} %get-tuple-element.96), channel_id=1, source_target_pairs={{0,6},{1,7},{2,4},{3,5},{4,2},{5,3},{6,0},{7,1},{8,14},{9,15},{10,... | collective-permute-start | bytes 393224 | tf_op jit(solution)/shard_map/ppermute | solution.py:34

commit v17 on v16

--- a/solution.py
+++ b/solution.py
@@ -345,7 +345,7 @@
     back = listed(back, few_ahead)
     ahead = chips // 2
     messages = pack(own, permute(after(other, back[1:ahead]), 1))
-    done = [(t, permute(messages[t], 2 * t)) for t in all_far[1:2]]
+    done = [(t, permute(messages[t], 2 * t)) for t in all_far[1:3]]
     back[-1] = after(back[-1], [block for _, block in done])
     extra = packed_right.size // math.prod(block)
     (first_part,) = call(

time: 126 us -> 131 us (1.040)
  waiting for transfers between devices: 53.7 us -> 61 us
  starting transfers between devices: 53.5 us -> 51.4 us
    ppermute x26, waiting for transfers between devices: 50.6 us -> 55.9 us  [permute(): return lax.ppermute(array, 'seq', [(i, i ^ offset) for i in range(seq)])]
    ppermute x3, waiting for transfers between devices: 3.13 us -> 5.1 us  [swap_sequences(): return lax.ppermute(array, 'dp', [(0, 1), (1, 0)])]
  transfers between devices with their start and end apart: 29 -> 29, of which waited for: 15 -> 13; matrix products, arithmetic and copies ran while one was open for 0% -> 0% of each run, Pallas kernels for 10% -> 9%
where the time goes in v17:
time: 131 us
  waiting for transfers between devices  61 us (47%)
  starting transfers between devices  51.4 us (39%)
  Pallas kernels  16.6 us (13%)
    ppermute x26, waiting for transfers between devices, permute(): return lax.ppermute(array, 'seq', [(i, i ^ offset) for i in range(seq)])  55.9 us
    ppermute x26, starting transfers between devices, permute(): return lax.ppermute(array, 'seq', [(i, i ^ offset) for i in range(seq)])  46.8 us
    pallas_call x12, Pallas kernels, call(): pl.pallas_call(kernel, out_shape=out_shapes, in_specs=[pl.BlockSpec(memor...  16.6 us
    ppermute x3, waiting for transfers between devices, swap_sequences(): return lax.ppermute(array, 'dp', [(0, 1), (1, 0)])  5.1 us
    ppermute x3, starting transfers between devices, swap_sequences(): return lax.ppermute(array, 'dp', [(0, 1), (1, 0)])  4.61 us
  transfers between devices with their start and end apart: 29, of which 13 were waited for; matrix products, arithmetic and copies ran while one was open for 0% of the time, Pallas kernels for 9%

profile of v17, /device:TPU:0, one launch (start us, length us, event | category | flops | bytes accessed | tf_op | source)
XLA Modules:
  0.0 131.1 jit_solution(12290719797499650517)
XLA Ops:
  0.6 2.7 %product_kernel.1 = (bf16[8,4,32,256]{3,2,1,0:T(8,128)(2,1)}, bf16[8,4,32,256]{3,2,1,0:T(8,128)(2,1)}) custom-call(s32[1]{0:T(128)} %bitcast.me_ref, bf16[4,16,32,256]{3,2,1,0:T(8,128)(2,1)} %bitcast.10, bf16[4,16,32,256]{3,2,1,0:T(8,128)(2,1)} %bitcast.12), custom_call_target="tpu_custom_call" | custom-call | bytes 3145728 | tf_op jit(solution)/shard_map/product_kernel/pallas_call | solution.py:55
  3.4 0.5 collective-permute-start
  3.9 1.2 copy-done.1
  5.1 0.8 mix_kernel.1
  5.9 0.1 collective-permute-start.1
  6.0 1.9 %collective-permute-done.1.refs_3_ = bf16[8,4,32,256]{3,2,1,0:T(8,128)(2,1)S(1)} collective-permute-done((bf16[8,4,32,256]{3,2,1,0:T(8,128)(2,1)S(1)}, bf16[8,4,32,256]{3,2,1,0:T(8,128)(2,1)S(1)}, u32[]{:S(2)}, u32[]{:S(2)}) %collective-permute-start.1) | collective-permute-done | bytes 524320 | tf_op jit(solution)/shard_map/ppermute | solution.py:34
  7.9 0.1 pack_pairs_kernel.1
  8.0 3.8 %collective-permute-start.2 = (bf16[2,2,4,32,256]{4,3,2,1,0:T(8,128)(2,1)S(1)}, bf16[2,2,4,32,256]{4,3,2,1,0:T(8,128)(2,1)S(1)}, u32[]{:S(2)}, u32[]{:S(2)}) collective-permute-start(bf16[2,2,4,32,256]{4,3,2,1,0:T(8,128)(2,1)S(1)} %get-tuple-element.59), channel_id=1, source_target_pairs={{0,8},{1,9},{2,10},{3,11},{4,12},{5,13},{6,14},{7,15},{8,0},{9,1},... | collective-permute-start | bytes 786440 | tf_op jit(solution)/shard_map/ppermute | solution.py:34
  11.8 1.5 %collective-permute-start.3 = (bf16[2,2,4,32,256]{4,3,2,1,0:T(8,128)(2,1)S(1)}, bf16[2,2,4,32,256]{4,3,2,1,0:T(8,128)(2,1)S(1)}, u32[]{:S(2)}, u32[]{:S(2)}) collective-permute-start(bf16[2,2,4,32,256]{4,3,2,1,0:T(8,128)(2,1)S(1)} %get-tuple-element.60), channel_id=1, source_target_pairs={{0,2},{1,3},{2,0},{3,1},{4,6},{5,7},{6,4},{7,5},{8,10},{9,11},{10,... | collective-permute-start | bytes 786440 | tf_op jit(solution)/shard_map/ppermute | solution.py:34
  13.3 1.3 collective-permute-start.8
  14.6 1.5 %collective-permute-start.9 = (bf16[4,512,256]{2,1,0:T(8,128)(2,1)S(1)}, bf16[4,512,256]{2,1,0:T(8,128)(2,1)S(1)}, u32[]{:S(2)}, u32[]{:S(2)}) collective-permute-start(bf16[4,512,256]{2,1,0:T(8,128)(2,1)S(1)} %bitcast.8), channel_id=1, source_target_pairs={{0,16},{16,0},{1,17},{17,1},{2,18},{18,2},{3,19},{19,3},{4,20},{20... | collective-permute-start | bytes 3145736 | tf_op jit(solution)/shard_map/ppermute | solution.py:17
  16.1 0.3 collective-permute-start.4
  16.4 7.7 %collective-permute-done.8.refs_7_ = bf16[2,4,32,256]{3,2,1,0:T(8,128)(2,1)S(1)} collective-permute-done((bf16[2,4,32,256]{3,2,1,0:T(8,128)(2,1)S(1)}, bf16[2,4,32,256]{3,2,1,0:T(8,128)(2,1)S(1)}, u32[]{:S(2)}, u32[]{:S(2)}) %collective-permute-start.8) | collective-permute-done | bytes 131104 | tf_op jit(solution)/shard_map/ppermute | solution.py:34
  24.1 7.5 %collective-permute-start.5 = (bf16[2,2,4,32,256]{4,3,2,1,0:T(8,128)(2,1)S(1)}, bf16[2,2,4,32,256]{4,3,2,1,0:T(8,128)(2,1)S(1)}, u32[]{:S(2)}, u32[]{:S(2)}) collective-permute-start(bf16[2,2,4,32,256]{4,3,2,1,0:T(8,128)(2,1)S(1)} %get-tuple-element.62), channel_id=1, source_target_pairs={{0,6},{1,7},{2,4},{3,5},{4,2},{5,3},{6,0},{7,1},{8,14},{9,15},{10,... | collective-permute-start | bytes 786440 | tf_op jit(solution)/shard_map/ppermute | solution.py:34
  31.6 3.3 %collective-permute-start.6 = (bf16[2,2,4,32,256]{4,3,2,1,0:T(8,128)(2,1)S(1)}, bf16[2,2,4,32,256]{4,3,2,1,0:T(8,128)(2,1)S(1)}, u32[]{:S(2)}, u32[]{:S(2)}) collective-permute-start(bf16[2,2,4,32,256]{4,3,2,1,0:T(8,128)(2,1)S(1)} %get-tuple-element.63), channel_id=1, source_target_pairs={{0,12},{1,13},{2,14},{3,15},{4,8},{5,9},{6,10},{7,11},{8,4},{9,5},... | collective-permute-start | bytes 786440 | tf_op jit(solution)/shard_map/ppermute | solution.py:34
  35.0 3.4 %collective-permute-done.5.refs_4_ = bf16[2,2,4,32,256]{4,3,2,1,0:T(8,128)(2,1)S(1)} collective-permute-done((bf16[2,2,4,32,256]{4,3,2,1,0:T(8,128)(2,1)S(1)}, bf16[2,2,4,32,256]{4,3,2,1,0:T(8,128)(2,1)S(1)}, u32[]{:S(2)}, u32[]{:S(2)}) %collective-permute-start.5) | collective-permute-done | bytes 262176 | tf_op jit(solution)/shard_map/ppermute | solution.py:34
  38.3 9.5 %collective-permute-done.6.refs_5_ = bf16[2,2,4,32,256]{4,3,2,1,0:T(8,128)(2,1)S(1)} collective-permute-done((bf16[2,2,4,32,256]{4,3,2,1,0:T(8,128)(2,1)S(1)}, bf16[2,2,4,32,256]{4,3,2,1,0:T(8,128)(2,1)S(1)}, u32[]{:S(2)}, u32[]{:S(2)}) %collective-permute-start.6) | collective-permute-done | bytes 262176 | tf_op jit(solution)/shard_map/ppermute | solution.py:34
  47.8 1.4 %collective-permute-start.10 = (bf16[2,4,32,256]{3,2,1,0:T(8,128)(2,1)S(1)}, bf16[2,4,32,256]{3,2,1,0:T(8,128)(2,1)S(1)}, u32[]{:S(2)}, u32[]{:S(2)}) collective-permute-start(bf16[2,4,32,256]{3,2,1,0:T(8,128)(2,1)S(1)} %get-tuple-element.69), channel_id=1, source_target_pairs={{0,14},{1,15},{2,12},{3,13},{4,10},{5,11},{6,8},{7,9},{8,6},{9,7},... | collective-permute-start | bytes 393224 | tf_op jit(solution)/shard_map/ppermute | solution.py:34
  49.2 11.1 %collective-permute-done.7.refs_6_ = bf16[2,2,4,32,256]{4,3,2,1,0:T(8,128)(2,1)S(1)} collective-permute-done((bf16[2,2,4,32,256]{4,3,2,1,0:T(8,128)(2,1)S(1)}, bf16[2,2,4,32,256]{4,3,2,1,0:T(8,128)(2,1)S(1)}, u32[]{:S(2)}, u32[]{:S(2)}) %collective-permute-start.7) | collective-permute-done | bytes 262176 | tf_op jit(solution)/shard_map/ppermute | solution.py:34
  60.2 3.0 %column_backward_kernel.1 = (bf16[8,4,32,256]{3,2,1,0:T(8,128)(2,1)S(1)}, bf16[8,4,32,256]{3,2,1,0:T(8,128)(2,1)S(1)}, bf16[32,64,256]{2,1,0:T(8,128)(2,1)S(1)}) custom-call(s32[1]{0:T(128)} %bitcast.me_ref, bf16[32,64,64]{2,1,0:T(8,128)(2,1)S(1)} %copy-done.5, bf16[2,2,4,32,256]{4,3,2,1,0:T(8,128)(2,1)S(1)} %get-tuple-element.58.refs_0_, ...), custom_call_target="tpu_custom_call" | custom-call | flops 67108864 | bytes 4325376 | tf_op jit(solution)/shard_map/column_backward_kernel/pallas_call | solution.py:55
  63.2 0.1 collective-permute-start.11
  63.3 1.9 %collective-permute-done.11.other_ref = bf16[8,4,32,256]{3,2,1,0:T(8,128)(2,1)S(1)} collective-permute-done((bf16[8,4,32,256]{3,2,1,0:T(8,128)(2,1)S(1)}, bf16[8,4,32,256]{3,2,1,0:T(8,128)(2,1)S(1)}, u32[]{:S(2)}, u32[]{:S(2)}) %collective-permute-start.11) | collective-permute-done | bytes 524320 | tf_op jit(solution)/shard_map/ppermute | solution.py:34
  65.2 0.1 pack_kernel.2
  65.3 1.0 collective-permute-start.12
  66.3 1.5 %collective-permute-start.13 = (bf16[2,4,32,256]{3,2,1,0:T(8,128)(2,1)S(1)}, bf16[2,4,32,256]{3,2,1,0:T(8,128)(2,1)S(1)}, u32[]{:S(2)}, u32[]{:S(2)}) collective-permute-start(bf16[2,4,32,256]{3,2,1,0:T(8,128)(2,1)S(1)} %get-tuple-element.76), channel_id=1, source_target_pairs={{0,2},{1,3},{2,0},{3,1},{4,6},{5,7},{6,4},{7,5},{8,10},{9,11},{10,... | collective-permute-start | bytes 393224 | tf_op jit(solution)/shard_map/ppermute | solution.py:34
  67.8 2.6 %collective-permute-start.14 = (bf16[2,4,32,256]{3,2,1,0:T(8,128)(2,1)S(1)}, bf16[2,4,32,256]{3,2,1,0:T(8,128)(2,1)S(1)}, u32[]{:S(2)}, u32[]{:S(2)}) collective-permute-start(bf16[2,4,32,256]{3,2,1,0:T(8,128)(2,1)S(1)} %get-tuple-element.77), channel_id=1, source_target_pairs={{0,4},{1,5},{2,6},{3,7},{4,0},{5,1},{6,2},{7,3},{8,12},{9,13},{10,... | collective-permute-start | bytes 393224 | tf_op jit(solution)/shard_map/ppermute | solution.py:34
  70.4 3.3 %column_forward_kernel.1 = (bf16[8,4,32,256]{3,2,1,0:T(8,128)(2,1)S(1)}, bf16[8,4,32,256]{3,2,1,0:T(8,128)(2,1)S(1)}, bf16[512,256]{1,0:T(8,128)(2,1)S(1)}) custom-call(s32[1]{0:T(128)} %bitcast.me_ref, bf16[32,64,64]{2,1,0:T(8,128)(2,1)S(1)} %copy-done.5, bf16[32,64,256]{2,1,0:T(8,128)(2,1)S(1)} %get-tuple-element.66.grad_ref, ...), custom_call_target="tpu_custom_call" | custom-call | flops 134217728 | bytes 5636096 | tf_op jit(solution)/shard_map/column_forward_kernel/pallas_call | solution.py:55
  73.7 1.0 collective-permute-done.12.refs_1_
  74.7 1.3 collective-permute-done.14.refs_3_
  76.0 1.9 %collective-permute-start.25 = (bf16[2,4,32,256]{3,2,1,0:T(8,128)(2,1)S(1)}, bf16[2,4,32,256]{3,2,1,0:T(8,128)(2,1)S(1)}, u32[]{:S(2)}, u32[]{:S(2)}) collective-permute-start(bf16[2,4,32,256]{3,2,1,0:T(8,128)(2,1)S(1)} %get-tuple-element.92), channel_id=1, source_target_pairs={{0,14},{1,15},{2,12},{3,13},{4,10},{5,11},{6,8},{7,9},{8,6},{9,7},... | collective-permute-start | bytes 393224 | tf_op jit(solution)/shard_map/ppermute | solution.py:34
  77.9 0.1 pack_kernel.3
  78.0 0.1 collective-permute-start.16
  78.1 1.6 %collective-permute-start.26 = (bf16[12,4,32,256]{3,2,1,0:T(8,128)(2,1)S(1)}, bf16[12,4,32,256]{3,2,1,0:T(8,128)(2,1)S(1)}, u32[]{:S(2)}, u32[]{:S(2)}) collective-permute-start(bf16[12,4,32,256]{3,2,1,0:T(8,128)(2,1)S(1)} %gather_kernel.2.first_ref), channel_id=1, source_target_pairs={{0,16},{16,0},{1,17},{17,1},{2,18},{18,2},{3,19},{19,3},{4,20},{20... | collective-permute-start | bytes 2359304 | tf_op jit(solution)/shard_map/ppermute | solution.py:17
  79.7 1.9 %collective-permute-start.22 = (bf16[2,4,32,256]{3,2,1,0:T(8,128)(2,1)S(1)}, bf16[2,4,32,256]{3,2,1,0:T(8,128)(2,1)S(1)}, u32[]{:S(2)}, u32[]{:S(2)}) collective-permute-start(bf16[2,4,32,256]{3,2,1,0:T(8,128)(2,1)S(1)} %get-tuple-element.89), channel_id=1, source_target_pairs={{0,12},{1,13},{2,14},{3,15},{4,8},{5,9},{6,10},{7,11},{8,4},{9,5},... | collective-permute-start | bytes 393224 | tf_op jit(solution)/shard_map/ppermute | solution.py:34
  81.6 1.9 %collective-permute-start.17 = (bf16[2,4,32,256]{3,2,1,0:T(8,128)(2,1)S(1)}, bf16[2,4,32,256]{3,2,1,0:T(8,128)(2,1)S(1)}, u32[]{:S(2)}, u32[]{:S(2)}) collective-permute-start(bf16[2,4,32,256]{3,2,1,0:T(8,128)(2,1)S(1)} %get-tuple-element.81), channel_id=1, source_target_pairs={{0,12},{1,13},{2,14},{3,15},{4,8},{5,9},{6,10},{7,11},{8,4},{9,5},... | collective-permute-start | bytes 393224 | tf_op jit(solution)/shard_map/ppermute | solution.py:34
  83.5 1.6 %collective-permute-done.25.refs_3_ = bf16[2,4,32,256]{3,2,1,0:T(8,128)(2,1)S(1)} collective-permute-done((bf16[2,4,32,256]{3,2,1,0:T(8,128)(2,1)S(1)}, bf16[2,4,32,256]{3,2,1,0:T(8,128)(2,1)S(1)}, u32[]{:S(2)}, u32[]{:S(2)}) %collective-permute-start.25) | collective-permute-done | bytes 131104 | tf_op jit(solution)/shard_map/ppermute | solution.py:34
  85.1 11.1 %collective-permute-start.23 = (bf16[2,4,32,256]{3,2,1,0:T(8,128)(2,1)S(1)}, bf16[2,4,32,256]{3,2,1,0:T(8,128)(2,1)S(1)}, u32[]{:S(2)}, u32[]{:S(2)}) collective-permute-start(bf16[2,4,32,256]{3,2,1,0:T(8,128)(2,1)S(1)} %get-tuple-element.90), channel_id=1, source_target_pairs={{0,10},{1,11},{2,8},{3,9},{4,14},{5,15},{6,12},{7,13},{8,2},{9,3},... | collective-permute-start | bytes 393224 | tf_op jit(solution)/shard_map/ppermute | solution.py:34
  96.2 1.6 %collective-permute-done.16.refs_1_ = bf16[2,4,32,256]{3,2,1,0:T(8,128)(2,1)S(1)} collective-permute-done((bf16[2,4,32,256]{3,2,1,0:T(8,128)(2,1)S(1)}, bf16[2,4,32,256]{3,2,1,0:T(8,128)(2,1)S(1)}, u32[]{:S(2)}, u32[]{:S(2)}) %collective-permute-start.16) | collective-permute-done | bytes 131104 | tf_op jit(solution)/shard_map/ppermute | solution.py:34
  97.8 9.2 %collective-permute-done.23.refs_1_ = bf16[2,4,32,256]{3,2,1,0:T(8,128)(2,1)S(1)} collective-permute-done((bf16[2,4,32,256]{3,2,1,0:T(8,128)(2,1)S(1)}, bf16[2,4,32,256]{3,2,1,0:T(8,128)(2,1)S(1)}, u32[]{:S(2)}, u32[]{:S(2)}) %collective-permute-start.23) | collective-permute-done | bytes 131104 | tf_op jit(solution)/shard_map/ppermute | solution.py:34
  107.1 1.6 %collective-permute-start.27 = (bf16[8,4,32,256]{3,2,1,0:T(8,128)(2,1)S(1)}, bf16[8,4,32,256]{3,2,1,0:T(8,128)(2,1)S(1)}, u32[]{:S(2)}, u32[]{:S(2)}) collective-permute-start(bf16[8,4,32,256]{3,2,1,0:T(8,128)(2,1)S(1)} %gather_kernel.3.second_ref), channel_id=1, source_target_pairs={{0,16},{16,0},{1,17},{17,1},{2,18},{18,2},{3,19},{19,3},{4,20},{20... | collective-permute-start | bytes 1572872 | tf_op jit(solution)/shard_map/ppermute | solution.py:17
  108.7 2.6 %collective-permute-start.19 = (bf16[2,4,32,256]{3,2,1,0:T(8,128)(2,1)S(1)}, bf16[2,4,32,256]{3,2,1,0:T(8,128)(2,1)S(1)}, u32[]{:S(2)}, u32[]{:S(2)}) collective-permute-start(bf16[2,4,32,256]{3,2,1,0:T(8,128)(2,1)S(1)} %get-tuple-element.83), channel_id=1, source_target_pairs={{0,14},{1,15},{2,12},{3,13},{4,10},{5,11},{6,8},{7,9},{8,6},{9,7},... | collective-permute-start | bytes 393224 | tf_op jit(solution)/shard_map/ppermute | solution.py:34
  111.3 0.7 collective-permute-start.20
  112.1 2.3 %row_backward_kernel.1 = (bf16[4,512,256]{2,1,0:T(8,128)(2,1)}, bf16[4,512,512]{2,1,0:T(8,128)(2,1)S(1)}) custom-call(s32[1]{0:T(128)} %bitcast.me_ref, bf16[4,512,512]{2,1,0:T(8,128)(2,1)S(1)} %copy-done, bf16[4,512,256]{2,1,0:T(8,128)(2,1)S(1)} %bitcast.9, bf16[12,4,32,256]{3,2,1,0:T(8,128)(2,1)S(1)} %gather_kernel.2.first_ref, ...), custom_call_target="tpu_custom_call" | custom-call | flops 1073741824 | bytes 7602176 | tf_op jit(solution)/shard_map/row_backward_kernel/pallas_call | solution.py:55
  114.4 1.6 %collective-permute-start.21 = (bf16[2,4,32,256]{3,2,1,0:T(8,128)(2,1)S(1)}, bf16[2,4,32,256]{3,2,1,0:T(8,128)(2,1)S(1)}, u32[]{:S(2)}, u32[]{:S(2)}) collective-permute-start(bf16[2,4,32,256]{3,2,1,0:T(8,128)(2,1)S(1)} %get-tuple-element.85), channel_id=1, source_target_pairs={{0,4},{1,5},{2,6},{3,7},{4,0},{5,1},{6,2},{7,3},{8,12},{9,13},{10,... | collective-permute-start | bytes 393224 | tf_op jit(solution)/shard_map/ppermute | solution.py:34
  116.0 5.1 %collective-permute-done.27.second_ref = bf16[8,4,32,256]{3,2,1,0:T(8,128)(2,1)S(1)} collective-permute-done((bf16[8,4,32,256]{3,2,1,0:T(8,128)(2,1)S(1)}, bf16[8,4,32,256]{3,2,1,0:T(8,128)(2,1)S(1)}, u32[]{:S(2)}, u32[]{:S(2)}) %collective-permute-start.27) | collective-permute-done | bytes 524320 | tf_op jit(solution)/shard_map/ppermute | solution.py:17
  121.1 2.4 %factor_sum_kernel.1 = (bf16[4,512,512]{2,1,0:T(8,128)(2,1)}, bf16[32,64,64]{2,1,0:T(8,128)(2,1)}) custom-call(s32[1]{0:T(128)} %bitcast.me_ref, bf16[4,512,512]{2,1,0:T(8,128)(2,1)S(1)} %get-tuple-element.94.term_ref, bf16[4,512,256]{2,1,0:T(8,128)(2,1)S(1)} %collective-permute-done.9.after_ref.values_ref, ...), custom_call_target="tpu_custom_call" | custom-call | flops 536870912 | bytes 7077888 | tf_op jit(solution)/shard_map/factor_sum_kernel/pallas_call | solution.py:55
  123.5 5.8 %collective-permute-done.28.refs_7_ = bf16[2,4,32,256]{3,2,1,0:T(8,128)(2,1)S(1)} collective-permute-done((bf16[2,4,32,256]{3,2,1,0:T(8,128)(2,1)S(1)}, bf16[2,4,32,256]{3,2,1,0:T(8,128)(2,1)S(1)}, u32[]{:S(2)}, u32[]{:S(2)}) %collective-permute-start.28) | collective-permute-done | bytes 131104 | tf_op jit(solution)/shard_map/ppermute | solution.py:34
  129.3 1.8 %output_kernel.1 = (bf16[4,16,32,256]{3,2,1,0:T(8,128)(2,1)}, bf16[4,16,32,256]{3,2,1,0:T(8,128)(2,1)}) custom-call(s32[1]{0:T(128)} %bitcast.me_ref, bf16[4,16,32,256]{3,2,1,0:T(8,128)(2,1)S(1)} %bitcast.11, bf16[4,16,32,256]{3,2,1,0:T(8,128)(2,1)S(1)} %bitcast.13, bf16[2,4,32,256]{3,2,1,0:T(8,128)(2,1)S(1)} %get-tuple-element.79.refs_0_, ...), custom_call_target="tpu_custom_call" | custom-call | bytes 5242880 | tf_op jit(solution)/shard_map/output_kernel/pallas_call | solution.py:55
  (36 shorter events, 0.2 us)
Async XLA Ops:
  0.6 3.3 %copy-start = (bf16[4,512,512]{2,1,0:T(8,128)(2,1)S(1)}, bf16[4,512,512]{2,1,0:T(8,128)(2,1)}, u32[]{:S(2)}) copy-start(bf16[4,512,512]{2,1,0:T(8,128)(2,1)} %left_ref.3) | copy-start | bytes 6291460
  3.4 2.7 %collective-permute-start = (bf16[8,4,32,256]{3,2,1,0:T(8,128)(2,1)}, bf16[8,4,32,256]{3,2,1,0:T(8,128)(2,1)S(1)}, u32[]{:S(2)}, u32[]{:S(2)}) collective-permute-start(bf16[8,4,32,256]{3,2,1,0:T(8,128)(2,1)} %get-tuple-element.54), channel_id=1, source_target_pairs={{0,1},{1,0},{2,3},{3,2},{4,5},{5,4},{6,7},{7,6},{8,9},{9,8},{10,11... | collective-permute-start | bytes 1572872 | tf_op jit(solution)/shard_map/ppermute | solution.py:34
  3.9 1.2 copy-start.1
  5.1 2.8 %copy-start.6 = (bf16[8,4,32,256]{3,2,1,0:T(8,128)(2,1)S(1)}, bf16[8,4,32,256]{3,2,1,0:T(8,128)(2,1)}, u32[]{:S(2)}) copy-start(bf16[8,4,32,256]{3,2,1,0:T(8,128)(2,1)} %get-tuple-element.53.refs_0_) | copy-start | bytes 1572868
  5.1 9.5 %copy-start.2 = (bf16[1,2048,256]{2,1,0:T(8,128)(2,1)S(1)}, bf16[1,2048,256]{2,1,0:T(8,128)(2,1)}, u32[]{:S(2)}) copy-start(bf16[1,2048,256]{2,1,0:T(8,128)(2,1)} %param.5) | copy-start | bytes 3145732
  5.1 55.1 %copy-start.5 = (bf16[32,64,64]{2,1,0:T(8,128)(2,1)S(1)}, bf16[32,64,64]{2,1,0:T(8,128)(2,1)}, u32[]{:S(2)}) copy-start(bf16[32,64,64]{2,1,0:T(8,128)(2,1)} %right_ref.3) | copy-start | bytes 786436
  5.9 2.0 %collective-permute-start.1 = (bf16[8,4,32,256]{3,2,1,0:T(8,128)(2,1)S(1)}, bf16[8,4,32,256]{3,2,1,0:T(8,128)(2,1)S(1)}, u32[]{:S(2)}, u32[]{:S(2)}) collective-permute-start(bf16[8,4,32,256]{3,2,1,0:T(8,128)(2,1)S(1)} %get-tuple-element.57), channel_id=1, source_target_pairs={{0,1},{1,0},{2,3},{3,2},{4,5},{5,4},{6,7},{7,6},{8,9},{9,8},{10,11... | collective-permute-start | bytes 1572872 | tf_op jit(solution)/shard_map/ppermute | solution.py:34
  8.0 23.6 %collective-permute-start.2 = (bf16[2,2,4,32,256]{4,3,2,1,0:T(8,128)(2,1)S(1)}, bf16[2,2,4,32,256]{4,3,2,1,0:T(8,128)(2,1)S(1)}, u32[]{:S(2)}, u32[]{:S(2)}) collective-permute-start(bf16[2,2,4,32,256]{4,3,2,1,0:T(8,128)(2,1)S(1)} %get-tuple-element.59), channel_id=1, source_target_pairs={{0,8},{1,9},{2,10},{3,11},{4,12},{5,13},{6,14},{7,15},{8,0},{9,1},... | collective-permute-start | bytes 786440 | tf_op jit(solution)/shard_map/ppermute | solution.py:34
  11.8 23.1 %collective-permute-start.3 = (bf16[2,2,4,32,256]{4,3,2,1,0:T(8,128)(2,1)S(1)}, bf16[2,2,4,32,256]{4,3,2,1,0:T(8,128)(2,1)S(1)}, u32[]{:S(2)}, u32[]{:S(2)}) collective-permute-start(bf16[2,2,4,32,256]{4,3,2,1,0:T(8,128)(2,1)S(1)} %get-tuple-element.60), channel_id=1, source_target_pairs={{0,2},{1,3},{2,0},{3,1},{4,6},{5,7},{6,4},{7,5},{8,10},{9,11},{10,... | collective-permute-start | bytes 786440 | tf_op jit(solution)/shard_map/ppermute | solution.py:34
  13.3 10.8 %collective-permute-start.8 = (bf16[2,4,32,256]{3,2,1,0:T(8,128)(2,1)S(1)}, bf16[2,4,32,256]{3,2,1,0:T(8,128)(2,1)S(1)}, u32[]{:S(2)}, u32[]{:S(2)}) collective-permute-start(bf16[2,4,32,256]{3,2,1,0:T(8,128)(2,1)S(1)} %get-tuple-element.65), channel_id=1, source_target_pairs={{0,14},{1,15},{2,12},{3,13},{4,10},{5,11},{6,8},{7,9},{8,6},{9,7},... | collective-permute-start | bytes 393224 | tf_op jit(solution)/shard_map/ppermute | solution.py:34
  14.6 55.7 %collective-permute-start.9 = (bf16[4,512,256]{2,1,0:T(8,128)(2,1)S(1)}, bf16[4,512,256]{2,1,0:T(8,128)(2,1)S(1)}, u32[]{:S(2)}, u32[]{:S(2)}) collective-permute-start(bf16[4,512,256]{2,1,0:T(8,128)(2,1)S(1)} %bitcast.8), channel_id=1, source_target_pairs={{0,16},{16,0},{1,17},{17,1},{2,18},{18,2},{3,19},{19,3},{4,20},{20... | collective-permute-start | bytes 3145736 | tf_op jit(solution)/shard_map/ppermute | solution.py:17
  16.1 18.8 %collective-permute-start.4 = (bf16[2,2,4,32,256]{4,3,2,1,0:T(8,128)(2,1)S(1)}, bf16[2,2,4,32,256]{4,3,2,1,0:T(8,128)(2,1)S(1)}, u32[]{:S(2)}, u32[]{:S(2)}) collective-permute-start(bf16[2,2,4,32,256]{4,3,2,1,0:T(8,128)(2,1)S(1)} %get-tuple-element.61), channel_id=1, source_target_pairs={{0,4},{1,5},{2,6},{3,7},{4,0},{5,1},{6,2},{7,3},{8,12},{9,13},{10,... | collective-permute-start | bytes 786440 | tf_op jit(solution)/shard_map/ppermute | solution.py:34
  24.1 14.2 %collective-permute-start.5 = (bf16[2,2,4,32,256]{4,3,2,1,0:T(8,128)(2,1)S(1)}, bf16[2,2,4,32,256]{4,3,2,1,0:T(8,128)(2,1)S(1)}, u32[]{:S(2)}, u32[]{:S(2)}) collective-permute-start(bf16[2,2,4,32,256]{4,3,2,1,0:T(8,128)(2,1)S(1)} %get-tuple-element.62), channel_id=1, source_target_pairs={{0,6},{1,7},{2,4},{3,5},{4,2},{5,3},{6,0},{7,1},{8,14},{9,15},{10,... | collective-permute-start | bytes 786440 | tf_op jit(solution)/shard_map/ppermute | solution.py:34
  31.6 16.2 %collective-permute-start.6 = (bf16[2,2,4,32,256]{4,3,2,1,0:T(8,128)(2,1)S(1)}, bf16[2,2,4,32,256]{4,3,2,1,0:T(8,128)(2,1)S(1)}, u32[]{:S(2)}, u32[]{:S(2)}) collective-permute-start(bf16[2,2,4,32,256]{4,3,2,1,0:T(8,128)(2,1)S(1)} %get-tuple-element.63), channel_id=1, source_target_pairs={{0,12},{1,13},{2,14},{3,15},{4,8},{5,9},{6,10},{7,11},{8,4},{9,5},... | collective-permute-start | bytes 786440 | tf_op jit(solution)/shard_map/ppermute | solution.py:34
  34.9 25.3 %collective-permute-start.7 = (bf16[2,2,4,32,256]{4,3,2,1,0:T(8,128)(2,1)S(1)}, bf16[2,2,4,32,256]{4,3,2,1,0:T(8,128)(2,1)S(1)}, u32[]{:S(2)}, u32[]{:S(2)}) collective-permute-start(bf16[2,2,4,32,256]{4,3,2,1,0:T(8,128)(2,1)S(1)} %get-tuple-element.64), channel_id=1, source_target_pairs={{0,10},{1,11},{2,8},{3,9},{4,14},{5,15},{6,12},{7,13},{8,2},{9,3},... | collective-permute-start | bytes 786440 | tf_op jit(solution)/shard_map/ppermute | solution.py:34
  47.8 15.4 %collective-permute-start.10 = (bf16[2,4,32,256]{3,2,1,0:T(8,128)(2,1)S(1)}, bf16[2,4,32,256]{3,2,1,0:T(8,128)(2,1)S(1)}, u32[]{:S(2)}, u32[]{:S(2)}) collective-permute-start(bf16[2,4,32,256]{3,2,1,0:T(8,128)(2,1)S(1)} %get-tuple-element.69), channel_id=1, source_target_pairs={{0,14},{1,15},{2,12},{3,13},{4,10},{5,11},{6,8},{7,9},{8,6},{9,7},... | collective-permute-start | bytes 393224 | tf_op jit(solution)/shard_map/ppermute | solution.py:34
  63.2 2.0 %collective-permute-start.11 = (bf16[8,4,32,256]{3,2,1,0:T(8,128)(2,1)S(1)}, bf16[8,4,32,256]{3,2,1,0:T(8,128)(2,1)S(1)}, u32[]{:S(2)}, u32[]{:S(2)}) collective-permute-start(bf16[8,4,32,256]{3,2,1,0:T(8,128)(2,1)S(1)} %get-tuple-element.74), channel_id=1, source_target_pairs={{0,1},{1,0},{2,3},{3,2},{4,5},{5,4},{6,7},{7,6},{8,9},{9,8},{10,11... | collective-permute-start | bytes 1572872 | tf_op jit(solution)/shard_map/ppermute | solution.py:34
  65.3 9.4 %collective-permute-start.12 = (bf16[2,4,32,256]{3,2,1,0:T(8,128)(2,1)S(1)}, bf16[2,4,32,256]{3,2,1,0:T(8,128)(2,1)S(1)}, u32[]{:S(2)}, u32[]{:S(2)}) collective-permute-start(bf16[2,4,32,256]{3,2,1,0:T(8,128)(2,1)S(1)} %get-tuple-element.75), channel_id=1, source_target_pairs={{0,8},{1,9},{2,10},{3,11},{4,12},{5,13},{6,14},{7,15},{8,0},{9,1},... | collective-permute-start | bytes 393224 | tf_op jit(solution)/shard_map/ppermute | solution.py:34
  66.3 8.4 %collective-permute-start.13 = (bf16[2,4,32,256]{3,2,1,0:T(8,128)(2,1)S(1)}, bf16[2,4,32,256]{3,2,1,0:T(8,128)(2,1)S(1)}, u32[]{:S(2)}, u32[]{:S(2)}) collective-permute-start(bf16[2,4,32,256]{3,2,1,0:T(8,128)(2,1)S(1)} %get-tuple-element.76), channel_id=1, source_target_pairs={{0,2},{1,3},{2,0},{3,1},{4,6},{5,7},{6,4},{7,5},{8,10},{9,11},{10,... | collective-permute-start | bytes 393224 | tf_op jit(solution)/shard_map/ppermute | solution.py:34
  67.8 8.2 %collective-permute-start.14 = (bf16[2,4,32,256]{3,2,1,0:T(8,128)(2,1)S(1)}, bf16[2,4,32,256]{3,2,1,0:T(8,128)(2,1)S(1)}, u32[]{:S(2)}, u32[]{:S(2)}) collective-permute-start(bf16[2,4,32,256]{3,2,1,0:T(8,128)(2,1)S(1)} %get-tuple-element.77), channel_id=1, source_target_pairs={{0,4},{1,5},{2,6},{3,7},{4,0},{5,1},{6,2},{7,3},{8,12},{9,13},{10,... | collective-permute-start | bytes 393224 | tf_op jit(solution)/shard_map/ppermute | solution.py:34
  76.0 1.9 %collective-permute-start.15 = (bf16[8,4,32,256]{3,2,1,0:T(8,128)(2,1)S(1)}, bf16[8,4,32,256]{3,2,1,0:T(8,128)(2,1)S(1)}, u32[]{:S(2)}, u32[]{:S(2)}) collective-permute-start(bf16[8,4,32,256]{3,2,1,0:T(8,128)(2,1)S(1)} %get-tuple-element.78), channel_id=1, source_target_pairs={{0,1},{1,0},{2,3},{3,2},{4,5},{5,4},{6,7},{7,6},{8,9},{9,8},{10,11... | collective-permute-start | bytes 1572872 | tf_op jit(solution)/shard_map/ppermute | solution.py:34
  76.0 9.1 %collective-permute-start.25 = (bf16[2,4,32,256]{3,2,1,0:T(8,128)(2,1)S(1)}, bf16[2,4,32,256]{3,2,1,0:T(8,128)(2,1)S(1)}, u32[]{:S(2)}, u32[]{:S(2)}) collective-permute-start(bf16[2,4,32,256]{3,2,1,0:T(8,128)(2,1)S(1)} %get-tuple-element.92), channel_id=1, source_target_pairs={{0,14},{1,15},{2,12},{3,13},{4,10},{5,11},{6,8},{7,9},{8,6},{9,7},... | collective-permute-start | bytes 393224 | tf_op jit(solution)/shard_map/ppermute | solution.py:34
  78.0 19.8 %collective-permute-start.16 = (bf16[2,4,32,256]{3,2,1,0:T(8,128)(2,1)S(1)}, bf16[2,4,32,256]{3,2,1,0:T(8,128)(2,1)S(1)}, u32[]{:S(2)}, u32[]{:S(2)}) collective-permute-start(bf16[2,4,32,256]{3,2,1,0:T(8,128)(2,1)S(1)} %get-tuple-element.80), channel_id=1, source_target_pairs={{0,8},{1,9},{2,10},{3,11},{4,12},{5,13},{6,14},{7,15},{8,0},{9,1},... | collective-permute-start | bytes 393224 | tf_op jit(solution)/shard_map/ppermute | solution.py:34
  78.1 36.3 %collective-permute-start.26 = (bf16[12,4,32,256]{3,2,1,0:T(8,128)(2,1)S(1)}, bf16[12,4,32,256]{3,2,1,0:T(8,128)(2,1)S(1)}, u32[]{:S(2)}, u32[]{:S(2)}) collective-permute-start(bf16[12,4,32,256]{3,2,1,0:T(8,128)(2,1)S(1)} %gather_kernel.2.first_ref), channel_id=1, source_target_pairs={{0,16},{16,0},{1,17},{17,1},{2,18},{18,2},{3,19},{19,3},{4,20},{20... | collective-permute-start | bytes 2359304 | tf_op jit(solution)/shard_map/ppermute | solution.py:17
  79.7 18.1 %collective-permute-start.22 = (bf16[2,4,32,256]{3,2,1,0:T(8,128)(2,1)S(1)}, bf16[2,4,32,256]{3,2,1,0:T(8,128)(2,1)S(1)}, u32[]{:S(2)}, u32[]{:S(2)}) collective-permute-start(bf16[2,4,32,256]{3,2,1,0:T(8,128)(2,1)S(1)} %get-tuple-element.89), channel_id=1, source_target_pairs={{0,12},{1,13},{2,14},{3,15},{4,8},{5,9},{6,10},{7,11},{8,4},{9,5},... | collective-permute-start | bytes 393224 | tf_op jit(solution)/shard_map/ppermute | solution.py:34
  81.6 16.2 %collective-permute-start.17 = (bf16[2,4,32,256]{3,2,1,0:T(8,128)(2,1)S(1)}, bf16[2,4,32,256]{3,2,1,0:T(8,128)(2,1)S(1)}, u32[]{:S(2)}, u32[]{:S(2)}) collective-permute-start(bf16[2,4,32,256]{3,2,1,0:T(8,128)(2,1)S(1)} %get-tuple-element.81), channel_id=1, source_target_pairs={{0,12},{1,13},{2,14},{3,15},{4,8},{5,9},{6,10},{7,11},{8,4},{9,5},... | collective-permute-start | bytes 393224 | tf_op jit(solution)/shard_map/ppermute | solution.py:34
  85.1 22.0 %collective-permute-start.23 = (bf16[2,4,32,256]{3,2,1,0:T(8,128)(2,1)S(1)}, bf16[2,4,32,256]{3,2,1,0:T(8,128)(2,1)S(1)}, u32[]{:S(2)}, u32[]{:S(2)}) collective-permute-start(bf16[2,4,32,256]{3,2,1,0:T(8,128)(2,1)S(1)} %get-tuple-element.90), channel_id=1, source_target_pairs={{0,10},{1,11},{2,8},{3,9},{4,14},{5,15},{6,12},{7,13},{8,2},{9,3},... | collective-permute-start | bytes 393224 | tf_op jit(solution)/shard_map/ppermute | solution.py:34
  97.8 9.3 %collective-permute-start.24 = (bf16[2,4,32,256]{3,2,1,0:T(8,128)(2,1)S(1)}, bf16[2,4,32,256]{3,2,1,0:T(8,128)(2,1)S(1)}, u32[]{:S(2)}, u32[]{:S(2)}) collective-permute-start(bf16[2,4,32,256]{3,2,1,0:T(8,128)(2,1)S(1)} %get-tuple-element.91), channel_id=1, source_target_pairs={{0,6},{1,7},{2,4},{3,5},{4,2},{5,3},{6,0},{7,1},{8,14},{9,15},{10,... | collective-permute-start | bytes 393224 | tf_op jit(solution)/shard_map/ppermute | solution.py:34
  107.1 13.9 %collective-permute-start.27 = (bf16[8,4,32,256]{3,2,1,0:T(8,128)(2,1)S(1)}, bf16[8,4,32,256]{3,2,1,0:T(8,128)(2,1)S(1)}, u32[]{:S(2)}, u32[]{:S(2)}) collective-permute-start(bf16[8,4,32,256]{3,2,1,0:T(8,128)(2,1)S(1)} %gather_kernel.3.second_ref), channel_id=1, source_target_pairs={{0,16},{16,0},{1,17},{17,1},{2,18},{18,2},{3,19},{19,3},{4,20},{20... | collective-permute-start | bytes 1572872 | tf_op jit(solution)/shard_map/ppermute | solution.py:17
  108.7 14.8 %collective-permute-start.18 = (bf16[2,4,32,256]{3,2,1,0:T(8,128)(2,1)S(1)}, bf16[2,4,32,256]{3,2,1,0:T(8,128)(2,1)S(1)}, u32[]{:S(2)}, u32[]{:S(2)}) collective-permute-start(bf16[2,4,32,256]{3,2,1,0:T(8,128)(2,1)S(1)} %get-tuple-element.82), channel_id=1, source_target_pairs={{0,10},{1,11},{2,8},{3,9},{4,14},{5,15},{6,12},{7,13},{8,2},{9,3},... | collective-permute-start | bytes 393224 | tf_op jit(solution)/shard_map/ppermute | solution.py:34
  108.7 14.8 %collective-permute-start.19 = (bf16[2,4,32,256]{3,2,1,0:T(8,128)(2,1)S(1)}, bf16[2,4,32,256]{3,2,1,0:T(8,128)(2,1)S(1)}, u32[]{:S(2)}, u32[]{:S(2)}) collective-permute-start(bf16[2,4,32,256]{3,2,1,0:T(8,128)(2,1)S(1)} %get-tuple-element.83), channel_id=1, source_target_pairs={{0,14},{1,15},{2,12},{3,13},{4,10},{5,11},{6,8},{7,9},{8,6},{9,7},... | collective-permute-start | bytes 393224 | tf_op jit(solution)/shard_map/ppermute | solution.py:34
  111.3 12.1 %collective-permute-start.20 = (bf16[2,4,32,256]{3,2,1,0:T(8,128)(2,1)S(1)}, bf16[2,4,32,256]{3,2,1,0:T(8,128)(2,1)S(1)}, u32[]{:S(2)}, u32[]{:S(2)}) collective-permute-start(bf16[2,4,32,256]{3,2,1,0:T(8,128)(2,1)S(1)} %get-tuple-element.84), channel_id=1, source_target_pairs={{0,2},{1,3},{2,0},{3,1},{4,6},{5,7},{6,4},{7,5},{8,10},{9,11},{10,... | collective-permute-start | bytes 393224 | tf_op jit(solution)/shard_map/ppermute | solution.py:34
  114.4 9.1 %collective-permute-start.21 = (bf16[2,4,32,256]{3,2,1,0:T(8,128)(2,1)S(1)}, bf16[2,4,32,256]{3,2,1,0:T(8,128)(2,1)S(1)}, u32[]{:S(2)}, u32[]{:S(2)}) collective-permute-start(bf16[2,4,32,256]{3,2,1,0:T(8,128)(2,1)S(1)} %get-tuple-element.85), channel_id=1, source_target_pairs={{0,4},{1,5},{2,6},{3,7},{4,0},{5,1},{6,2},{7,3},{8,12},{9,13},{10,... | collective-permute-start | bytes 393224 | tf_op jit(solution)/shard_map/ppermute | solution.py:34
  121.1 8.3 %copy-start.3 = (bf16[1,2048,256]{2,1,0:T(8,128)(2,1)S(1)}, bf16[1,2048,256]{2,1,0:T(8,128)(2,1)}, u32[]{:S(2)}) copy-start(bf16[1,2048,256]{2,1,0:T(8,128)(2,1)} %param.6) | copy-start | bytes 3145732
  121.1 8.3 %copy-start.4 = (bf16[1,2048,256]{2,1,0:T(8,128)(2,1)S(1)}, bf16[1,2048,256]{2,1,0:T(8,128)(2,1)}, u32[]{:S(2)}) copy-start(bf16[1,2048,256]{2,1,0:T(8,128)(2,1)} %param.7) | copy-start | bytes 3145732
  123.4 5.9 %collective-permute-start.28 = (bf16[2,4,32,256]{3,2,1,0:T(8,128)(2,1)S(1)}, bf16[2,4,32,256]{3,2,1,0:T(8,128)(2,1)S(1)}, u32[]{:S(2)}, u32[]{:S(2)}) collective-permute-start(bf16[2,4,32,256]{3,2,1,0:T(8,128)(2,1)S(1)} %get-tuple-element.96), channel_id=1, source_target_pairs={{0,6},{1,7},{2,4},{3,5},{4,2},{5,3},{6,0},{7,1},{8,14},{9,15},{10,... | collective-permute-start | bytes 393224 | tf_op jit(solution)/shard_map/ppermute | solution.py:34

commit v18 on v16

--- a/solution.py
+++ b/solution.py
@@ -46,7 +46,7 @@
     return [messages[t] for t in order]
 
 
-def call(kernel, me, inputs, out_shapes, scratch=(), flops=0, unblocked=(), vmem=32):
+def call(kernel, me, inputs, out_shapes, scratch=(), flops=0, unblocked=(), vmem=32, stored=True):
     whole = pl.BlockSpec(memory_space=pltpu.VMEM)
     moved = sum(x.size * x.dtype.itemsize for x in (*inputs, *out_shapes))
     in_specs = [
@@ -56,7 +56,7 @@
         kernel,
         out_shape=out_shapes,
         in_specs=[pl.BlockSpec(memory_space=pltpu.SMEM)] + in_specs,
-        out_specs=[whole] * len(out_shapes),
+        out_specs=[whole if stored else pl.BlockSpec(memory_space=pl.ANY)] * len(out_shapes),
         scratch_shapes=scratch,
         compiler_params=pltpu.CompilerParams(vmem_limit_bytes=vmem * MIB),
         name=getattr(kernel, "func", kernel).__name__,
@@ -260,11 +260,19 @@
 
 def output_kernel(order, me_ref, gate_ref, cotangent_ref, *refs):
     chips = len(order)
-    out_ref, grad_ref = refs[chips:]
-    for c, ref in received_views(me_ref[0], refs[:chips], order):
-        second = ref[...].astype(F32)
-        out_ref[:, c] = (gate_ref[:, c].astype(F32) * second).astype(BF16)
-        grad_ref[:, c] = (cotangent_ref[:, c].astype(F32) * second).astype(BF16)
+    out_hbm, grad_hbm, out, grad, sems = refs[chips:]
+    blocks = received_views(me_ref[0], refs[:chips], order)
+    stores = []
+    for i in range(out.shape[0]):
+        for c, ref in blocks:
+            second = ref[i].astype(F32)
+            out[i, c] = (gate_ref[i, c].astype(F32) * second).astype(BF16)
+            grad[i, c] = (cotangent_ref[i, c].astype(F32) * second).astype(BF16)
+        for n, (source, target) in enumerate(((out, out_hbm), (grad, grad_hbm))):
+            stores.append(pltpu.make_async_copy(source.at[i], target.at[i], sems.at[n, i]))
+            stores[-1].start()
+    for store in stores:
+        store.wait()
 
 
 def direct_shards(signal, gating, upstream, left_factor, right_factor):
@@ -376,7 +384,12 @@
     messages[last] = after(messages[last], grad_left)
     second = listed(exchange(messages, done), all_far)
     output, grad_gate = call(
-        ordered(output_kernel, all_far), me, [gate, cotangent, *second], [whole, whole]
+        ordered(output_kernel, all_far),
+        me,
+        [gate, cotangent, *second],
+        [whole, whole],
+        [hold, hold, pltpu.SemaphoreType.DMA((2, rows))],
+        stored=False,
     )
     return (
         output.reshape(signal.shape),

time: 126 us -> 126 us (level)
  no operation moved by 1% of the time
where the time goes in v18:
time: 126 us
  waiting for transfers between devices  53.7 us (43%)
  starting transfers between devices  53.5 us (42%)
  Pallas kernels  16.6 us (13%)
    ppermute x26, waiting for transfers between devices, permute(): return lax.ppermute(array, 'seq', [(i, i ^ offset) for i in range(seq)])  50.6 us
    ppermute x26, starting transfers between devices, permute(): return lax.ppermute(array, 'seq', [(i, i ^ offset) for i in range(seq)])  47.9 us
    pallas_call x12, Pallas kernels, call(): pl.pallas_call(kernel, out_shape=out_shapes, in_specs=[pl.BlockSpec(memor...  16.6 us
    ppermute x3, starting transfers between devices, swap_sequences(): return lax.ppermute(array, 'dp', [(0, 1), (1, 0)])  5.64 us
    ppermute x3, waiting for transfers between devices, swap_sequences(): return lax.ppermute(array, 'dp', [(0, 1), (1, 0)])  3.13 us
  transfers between devices with their start and end apart: 29, of which 15 were waited for; matrix products, arithmetic and copies ran while one was open for 0% of the time, Pallas kernels for 10%

profile of v18, /device:TPU:0, one launch (start us, length us, event | category | flops | bytes accessed | tf_op | source)
XLA Modules:
  0.0 125.9 jit_solution(11971913821456747561)
XLA Ops:
  0.6 2.7 %product_kernel.1 = (bf16[8,4,32,256]{3,2,1,0:T(8,128)(2,1)}, bf16[8,4,32,256]{3,2,1,0:T(8,128)(2,1)}) custom-call(s32[1]{0:T(128)} %bitcast.me_ref, bf16[4,16,32,256]{3,2,1,0:T(8,128)(2,1)} %bitcast.10, bf16[4,16,32,256]{3,2,1,0:T(8,128)(2,1)} %bitcast.12), custom_call_target="tpu_custom_call" | custom-call | bytes 3145728 | tf_op jit(solution)/shard_map/product_kernel/pallas_call | solution.py:55
  3.4 0.5 collective-permute-start
  3.9 1.2 copy-done.1
  5.1 0.8 mix_kernel.1
  5.9 0.1 collective-permute-start.1
  6.0 1.9 %collective-permute-done.1.refs_3_ = bf16[8,4,32,256]{3,2,1,0:T(8,128)(2,1)S(1)} collective-permute-done((bf16[8,4,32,256]{3,2,1,0:T(8,128)(2,1)S(1)}, bf16[8,4,32,256]{3,2,1,0:T(8,128)(2,1)S(1)}, u32[]{:S(2)}, u32[]{:S(2)}) %collective-permute-start.1) | collective-permute-done | bytes 524320 | tf_op jit(solution)/shard_map/ppermute | solution.py:34
  7.9 0.1 pack_pairs_kernel.1
  8.0 3.8 %collective-permute-start.2 = (bf16[2,2,4,32,256]{4,3,2,1,0:T(8,128)(2,1)S(1)}, bf16[2,2,4,32,256]{4,3,2,1,0:T(8,128)(2,1)S(1)}, u32[]{:S(2)}, u32[]{:S(2)}) collective-permute-start(bf16[2,2,4,32,256]{4,3,2,1,0:T(8,128)(2,1)S(1)} %get-tuple-element.59), channel_id=1, source_target_pairs={{0,8},{1,9},{2,10},{3,11},{4,12},{5,13},{6,14},{7,15},{8,0},{9,1},... | collective-permute-start | bytes 786440 | tf_op jit(solution)/shard_map/ppermute | solution.py:34
  11.8 1.5 %collective-permute-start.3 = (bf16[2,2,4,32,256]{4,3,2,1,0:T(8,128)(2,1)S(1)}, bf16[2,2,4,32,256]{4,3,2,1,0:T(8,128)(2,1)S(1)}, u32[]{:S(2)}, u32[]{:S(2)}) collective-permute-start(bf16[2,2,4,32,256]{4,3,2,1,0:T(8,128)(2,1)S(1)} %get-tuple-element.60), channel_id=1, source_target_pairs={{0,2},{1,3},{2,0},{3,1},{4,6},{5,7},{6,4},{7,5},{8,10},{9,11},{10,... | collective-permute-start | bytes 786440 | tf_op jit(solution)/shard_map/ppermute | solution.py:34
  13.3 1.3 %collective-permute-start.8 = (bf16[2,4,32,256]{3,2,1,0:T(8,128)(2,1)S(1)}, bf16[2,4,32,256]{3,2,1,0:T(8,128)(2,1)S(1)}, u32[]{:S(2)}, u32[]{:S(2)}) collective-permute-start(bf16[2,4,32,256]{3,2,1,0:T(8,128)(2,1)S(1)} %get-tuple-element.65), channel_id=1, source_target_pairs={{0,14},{1,15},{2,12},{3,13},{4,10},{5,11},{6,8},{7,9},{8,6},{9,7},... | collective-permute-start | bytes 393224 | tf_op jit(solution)/shard_map/ppermute | solution.py:34
  14.6 1.5 %collective-permute-start.9 = (bf16[4,512,256]{2,1,0:T(8,128)(2,1)S(1)}, bf16[4,512,256]{2,1,0:T(8,128)(2,1)S(1)}, u32[]{:S(2)}, u32[]{:S(2)}) collective-permute-start(bf16[4,512,256]{2,1,0:T(8,128)(2,1)S(1)} %bitcast.8), channel_id=1, source_target_pairs={{0,16},{16,0},{1,17},{17,1},{2,18},{18,2},{3,19},{19,3},{4,20},{20... | collective-permute-start | bytes 3145736 | tf_op jit(solution)/shard_map/ppermute | solution.py:17
  16.1 0.3 collective-permute-start.4
  16.4 7.7 %collective-permute-done.8.refs_7_ = bf16[2,4,32,256]{3,2,1,0:T(8,128)(2,1)S(1)} collective-permute-done((bf16[2,4,32,256]{3,2,1,0:T(8,128)(2,1)S(1)}, bf16[2,4,32,256]{3,2,1,0:T(8,128)(2,1)S(1)}, u32[]{:S(2)}, u32[]{:S(2)}) %collective-permute-start.8) | collective-permute-done | bytes 131104 | tf_op jit(solution)/shard_map/ppermute | solution.py:34
  24.1 7.5 %collective-permute-start.5 = (bf16[2,2,4,32,256]{4,3,2,1,0:T(8,128)(2,1)S(1)}, bf16[2,2,4,32,256]{4,3,2,1,0:T(8,128)(2,1)S(1)}, u32[]{:S(2)}, u32[]{:S(2)}) collective-permute-start(bf16[2,2,4,32,256]{4,3,2,1,0:T(8,128)(2,1)S(1)} %get-tuple-element.62), channel_id=1, source_target_pairs={{0,6},{1,7},{2,4},{3,5},{4,2},{5,3},{6,0},{7,1},{8,14},{9,15},{10,... | collective-permute-start | bytes 786440 | tf_op jit(solution)/shard_map/ppermute | solution.py:34
  31.6 3.3 %collective-permute-start.6 = (bf16[2,2,4,32,256]{4,3,2,1,0:T(8,128)(2,1)S(1)}, bf16[2,2,4,32,256]{4,3,2,1,0:T(8,128)(2,1)S(1)}, u32[]{:S(2)}, u32[]{:S(2)}) collective-permute-start(bf16[2,2,4,32,256]{4,3,2,1,0:T(8,128)(2,1)S(1)} %get-tuple-element.63), channel_id=1, source_target_pairs={{0,12},{1,13},{2,14},{3,15},{4,8},{5,9},{6,10},{7,11},{8,4},{9,5},... | collective-permute-start | bytes 786440 | tf_op jit(solution)/shard_map/ppermute | solution.py:34
  35.0 3.4 %collective-permute-done.5.refs_4_ = bf16[2,2,4,32,256]{4,3,2,1,0:T(8,128)(2,1)S(1)} collective-permute-done((bf16[2,2,4,32,256]{4,3,2,1,0:T(8,128)(2,1)S(1)}, bf16[2,2,4,32,256]{4,3,2,1,0:T(8,128)(2,1)S(1)}, u32[]{:S(2)}, u32[]{:S(2)}) %collective-permute-start.5) | collective-permute-done | bytes 262176 | tf_op jit(solution)/shard_map/ppermute | solution.py:34
  38.3 9.5 %collective-permute-done.6.refs_5_ = bf16[2,2,4,32,256]{4,3,2,1,0:T(8,128)(2,1)S(1)} collective-permute-done((bf16[2,2,4,32,256]{4,3,2,1,0:T(8,128)(2,1)S(1)}, bf16[2,2,4,32,256]{4,3,2,1,0:T(8,128)(2,1)S(1)}, u32[]{:S(2)}, u32[]{:S(2)}) %collective-permute-start.6) | collective-permute-done | bytes 262176 | tf_op jit(solution)/shard_map/ppermute | solution.py:34
  47.8 1.4 %collective-permute-start.10 = (bf16[2,4,32,256]{3,2,1,0:T(8,128)(2,1)S(1)}, bf16[2,4,32,256]{3,2,1,0:T(8,128)(2,1)S(1)}, u32[]{:S(2)}, u32[]{:S(2)}) collective-permute-start(bf16[2,4,32,256]{3,2,1,0:T(8,128)(2,1)S(1)} %get-tuple-element.69), channel_id=1, source_target_pairs={{0,14},{1,15},{2,12},{3,13},{4,10},{5,11},{6,8},{7,9},{8,6},{9,7},... | collective-permute-start | bytes 393224 | tf_op jit(solution)/shard_map/ppermute | solution.py:34
  49.2 11.1 %collective-permute-done.7.refs_6_ = bf16[2,2,4,32,256]{4,3,2,1,0:T(8,128)(2,1)S(1)} collective-permute-done((bf16[2,2,4,32,256]{4,3,2,1,0:T(8,128)(2,1)S(1)}, bf16[2,2,4,32,256]{4,3,2,1,0:T(8,128)(2,1)S(1)}, u32[]{:S(2)}, u32[]{:S(2)}) %collective-permute-start.7) | collective-permute-done | bytes 262176 | tf_op jit(solution)/shard_map/ppermute | solution.py:34
  60.2 3.0 %column_backward_kernel.1 = (bf16[8,4,32,256]{3,2,1,0:T(8,128)(2,1)S(1)}, bf16[8,4,32,256]{3,2,1,0:T(8,128)(2,1)S(1)}, bf16[32,64,256]{2,1,0:T(8,128)(2,1)S(1)}) custom-call(s32[1]{0:T(128)} %bitcast.me_ref, bf16[32,64,64]{2,1,0:T(8,128)(2,1)S(1)} %copy-done.5, bf16[2,2,4,32,256]{4,3,2,1,0:T(8,128)(2,1)S(1)} %get-tuple-element.58.refs_0_, ...), custom_call_target="tpu_custom_call" | custom-call | flops 67108864 | bytes 4325376 | tf_op jit(solution)/shard_map/column_backward_kernel/pallas_call | solution.py:55
  63.3 1.9 %collective-permute-done.11.other_ref = bf16[8,4,32,256]{3,2,1,0:T(8,128)(2,1)S(1)} collective-permute-done((bf16[8,4,32,256]{3,2,1,0:T(8,128)(2,1)S(1)}, bf16[8,4,32,256]{3,2,1,0:T(8,128)(2,1)S(1)}, u32[]{:S(2)}, u32[]{:S(2)}) %collective-permute-start.11) | collective-permute-done | bytes 524320 | tf_op jit(solution)/shard_map/ppermute | solution.py:34
  65.3 1.0 collective-permute-start.12
  66.3 1.5 %collective-permute-start.13 = (bf16[2,4,32,256]{3,2,1,0:T(8,128)(2,1)S(1)}, bf16[2,4,32,256]{3,2,1,0:T(8,128)(2,1)S(1)}, u32[]{:S(2)}, u32[]{:S(2)}) collective-permute-start(bf16[2,4,32,256]{3,2,1,0:T(8,128)(2,1)S(1)} %get-tuple-element.76), channel_id=1, source_target_pairs={{0,2},{1,3},{2,0},{3,1},{4,6},{5,7},{6,4},{7,5},{8,10},{9,11},{10,... | collective-permute-start | bytes 393224 | tf_op jit(solution)/shard_map/ppermute | solution.py:34
  67.8 2.6 %collective-permute-start.14 = (bf16[2,4,32,256]{3,2,1,0:T(8,128)(2,1)S(1)}, bf16[2,4,32,256]{3,2,1,0:T(8,128)(2,1)S(1)}, u32[]{:S(2)}, u32[]{:S(2)}) collective-permute-start(bf16[2,4,32,256]{3,2,1,0:T(8,128)(2,1)S(1)} %get-tuple-element.77), channel_id=1, source_target_pairs={{0,4},{1,5},{2,6},{3,7},{4,0},{5,1},{6,2},{7,3},{8,12},{9,13},{10,... | collective-permute-start | bytes 393224 | tf_op jit(solution)/shard_map/ppermute | solution.py:34
  70.4 3.3 %column_forward_kernel.1 = (bf16[8,4,32,256]{3,2,1,0:T(8,128)(2,1)S(1)}, bf16[8,4,32,256]{3,2,1,0:T(8,128)(2,1)S(1)}, bf16[512,256]{1,0:T(8,128)(2,1)S(1)}) custom-call(s32[1]{0:T(128)} %bitcast.me_ref, bf16[32,64,64]{2,1,0:T(8,128)(2,1)S(1)} %copy-done.5, bf16[32,64,256]{2,1,0:T(8,128)(2,1)S(1)} %get-tuple-element.66.grad_ref, ...), custom_call_target="tpu_custom_call" | custom-call | flops 134217728 | bytes 5636096 | tf_op jit(solution)/shard_map/column_forward_kernel/pallas_call | solution.py:55
  73.7 1.0 collective-permute-done.12.refs_1_
  74.7 1.3 %collective-permute-done.14.refs_3_ = bf16[2,4,32,256]{3,2,1,0:T(8,128)(2,1)S(1)} collective-permute-done((bf16[2,4,32,256]{3,2,1,0:T(8,128)(2,1)S(1)}, bf16[2,4,32,256]{3,2,1,0:T(8,128)(2,1)S(1)}, u32[]{:S(2)}, u32[]{:S(2)}) %collective-permute-start.14) | collective-permute-done | bytes 131104 | tf_op jit(solution)/shard_map/ppermute | solution.py:34
  76.0 1.9 %collective-permute-start.25 = (bf16[2,4,32,256]{3,2,1,0:T(8,128)(2,1)S(1)}, bf16[2,4,32,256]{3,2,1,0:T(8,128)(2,1)S(1)}, u32[]{:S(2)}, u32[]{:S(2)}) collective-permute-start(bf16[2,4,32,256]{3,2,1,0:T(8,128)(2,1)S(1)} %get-tuple-element.92), channel_id=1, source_target_pairs={{0,14},{1,15},{2,12},{3,13},{4,10},{5,11},{6,8},{7,9},{8,6},{9,7},... | collective-permute-start | bytes 393224 | tf_op jit(solution)/shard_map/ppermute | solution.py:34
  78.0 1.6 %collective-permute-start.26 = (bf16[12,4,32,256]{3,2,1,0:T(8,128)(2,1)S(1)}, bf16[12,4,32,256]{3,2,1,0:T(8,128)(2,1)S(1)}, u32[]{:S(2)}, u32[]{:S(2)}) collective-permute-start(bf16[12,4,32,256]{3,2,1,0:T(8,128)(2,1)S(1)} %gather_kernel.2.first_ref), channel_id=1, source_target_pairs={{0,16},{16,0},{1,17},{17,1},{2,18},{18,2},{3,19},{19,3},{4,20},{20... | collective-permute-start | bytes 2359304 | tf_op jit(solution)/shard_map/ppermute | solution.py:17
  79.5 1.9 %collective-permute-start.22 = (bf16[2,4,32,256]{3,2,1,0:T(8,128)(2,1)S(1)}, bf16[2,4,32,256]{3,2,1,0:T(8,128)(2,1)S(1)}, u32[]{:S(2)}, u32[]{:S(2)}) collective-permute-start(bf16[2,4,32,256]{3,2,1,0:T(8,128)(2,1)S(1)} %get-tuple-element.89), channel_id=1, source_target_pairs={{0,12},{1,13},{2,14},{3,15},{4,8},{5,9},{6,10},{7,11},{8,4},{9,5},... | collective-permute-start | bytes 393224 | tf_op jit(solution)/shard_map/ppermute | solution.py:34
  81.5 0.1 collective-permute-start.16
  81.5 3.9 %collective-permute-start.23 = (bf16[2,4,32,256]{3,2,1,0:T(8,128)(2,1)S(1)}, bf16[2,4,32,256]{3,2,1,0:T(8,128)(2,1)S(1)}, u32[]{:S(2)}, u32[]{:S(2)}) collective-permute-start(bf16[2,4,32,256]{3,2,1,0:T(8,128)(2,1)S(1)} %get-tuple-element.90), channel_id=1, source_target_pairs={{0,10},{1,11},{2,8},{3,9},{4,14},{5,15},{6,12},{7,13},{8,2},{9,3},... | collective-permute-start | bytes 393224 | tf_op jit(solution)/shard_map/ppermute | solution.py:34
  85.4 7.8 %collective-permute-start.24 = (bf16[2,4,32,256]{3,2,1,0:T(8,128)(2,1)S(1)}, bf16[2,4,32,256]{3,2,1,0:T(8,128)(2,1)S(1)}, u32[]{:S(2)}, u32[]{:S(2)}) collective-permute-start(bf16[2,4,32,256]{3,2,1,0:T(8,128)(2,1)S(1)} %get-tuple-element.91), channel_id=1, source_target_pairs={{0,6},{1,7},{2,4},{3,5},{4,2},{5,3},{6,0},{7,1},{8,14},{9,15},{10,... | collective-permute-start | bytes 393224 | tf_op jit(solution)/shard_map/ppermute | solution.py:34
  93.2 4.9 %collective-permute-done.16.refs_1_ = bf16[2,4,32,256]{3,2,1,0:T(8,128)(2,1)S(1)} collective-permute-done((bf16[2,4,32,256]{3,2,1,0:T(8,128)(2,1)S(1)}, bf16[2,4,32,256]{3,2,1,0:T(8,128)(2,1)S(1)}, u32[]{:S(2)}, u32[]{:S(2)}) %collective-permute-start.16) | collective-permute-done | bytes 131104 | tf_op jit(solution)/shard_map/ppermute | solution.py:34
  98.1 3.4 %collective-permute-done.23.refs_1_ = bf16[2,4,32,256]{3,2,1,0:T(8,128)(2,1)S(1)} collective-permute-done((bf16[2,4,32,256]{3,2,1,0:T(8,128)(2,1)S(1)}, bf16[2,4,32,256]{3,2,1,0:T(8,128)(2,1)S(1)}, u32[]{:S(2)}, u32[]{:S(2)}) %collective-permute-start.23) | collective-permute-done | bytes 131104 | tf_op jit(solution)/shard_map/ppermute | solution.py:34
  101.6 0.2 collective-permute-done.24.refs_2_
  101.8 2.6 %collective-permute-start.27 = (bf16[8,4,32,256]{3,2,1,0:T(8,128)(2,1)S(1)}, bf16[8,4,32,256]{3,2,1,0:T(8,128)(2,1)S(1)}, u32[]{:S(2)}, u32[]{:S(2)}) collective-permute-start(bf16[8,4,32,256]{3,2,1,0:T(8,128)(2,1)S(1)} %gather_kernel.3.second_ref), channel_id=1, source_target_pairs={{0,16},{16,0},{1,17},{17,1},{2,18},{18,2},{3,19},{19,3},{4,20},{20... | collective-permute-start | bytes 1572872 | tf_op jit(solution)/shard_map/ppermute | solution.py:17
  104.4 1.9 %collective-permute-start.17 = (bf16[2,4,32,256]{3,2,1,0:T(8,128)(2,1)S(1)}, bf16[2,4,32,256]{3,2,1,0:T(8,128)(2,1)S(1)}, u32[]{:S(2)}, u32[]{:S(2)}) collective-permute-start(bf16[2,4,32,256]{3,2,1,0:T(8,128)(2,1)S(1)} %get-tuple-element.81), channel_id=1, source_target_pairs={{0,12},{1,13},{2,14},{3,15},{4,8},{5,9},{6,10},{7,11},{8,4},{9,5},... | collective-permute-start | bytes 393224 | tf_op jit(solution)/shard_map/ppermute | solution.py:34
  106.4 1.9 %collective-permute-start.19 = (bf16[2,4,32,256]{3,2,1,0:T(8,128)(2,1)S(1)}, bf16[2,4,32,256]{3,2,1,0:T(8,128)(2,1)S(1)}, u32[]{:S(2)}, u32[]{:S(2)}) collective-permute-start(bf16[2,4,32,256]{3,2,1,0:T(8,128)(2,1)S(1)} %get-tuple-element.83), channel_id=1, source_target_pairs={{0,14},{1,15},{2,12},{3,13},{4,10},{5,11},{6,8},{7,9},{8,6},{9,7},... | collective-permute-start | bytes 393224 | tf_op jit(solution)/shard_map/ppermute | solution.py:34
  108.3 2.3 %row_backward_kernel.1 = (bf16[4,512,256]{2,1,0:T(8,128)(2,1)}, bf16[4,512,512]{2,1,0:T(8,128)(2,1)S(1)}) custom-call(s32[1]{0:T(128)} %bitcast.me_ref, bf16[4,512,512]{2,1,0:T(8,128)(2,1)S(1)} %copy-done, bf16[4,512,256]{2,1,0:T(8,128)(2,1)S(1)} %bitcast.9, bf16[12,4,32,256]{3,2,1,0:T(8,128)(2,1)S(1)} %gather_kernel.2.first_ref, ...), custom_call_target="tpu_custom_call" | custom-call | flops 1073741824 | bytes 7602176 | tf_op jit(solution)/shard_map/row_backward_kernel/pallas_call | solution.py:55
  110.6 1.4 %collective-permute-start.20 = (bf16[2,4,32,256]{3,2,1,0:T(8,128)(2,1)S(1)}, bf16[2,4,32,256]{3,2,1,0:T(8,128)(2,1)S(1)}, u32[]{:S(2)}, u32[]{:S(2)}) collective-permute-start(bf16[2,4,32,256]{3,2,1,0:T(8,128)(2,1)S(1)} %get-tuple-element.84), channel_id=1, source_target_pairs={{0,2},{1,3},{2,0},{3,1},{4,6},{5,7},{6,4},{7,5},{8,10},{9,11},{10,... | collective-permute-start | bytes 393224 | tf_op jit(solution)/shard_map/ppermute | solution.py:34
  112.0 3.1 %collective-permute-done.27.second_ref = bf16[8,4,32,256]{3,2,1,0:T(8,128)(2,1)S(1)} collective-permute-done((bf16[8,4,32,256]{3,2,1,0:T(8,128)(2,1)S(1)}, bf16[8,4,32,256]{3,2,1,0:T(8,128)(2,1)S(1)}, u32[]{:S(2)}, u32[]{:S(2)}) %collective-permute-start.27) | collective-permute-done | bytes 524320 | tf_op jit(solution)/shard_map/ppermute | solution.py:17
  115.2 2.4 %factor_sum_kernel.1 = (bf16[4,512,512]{2,1,0:T(8,128)(2,1)}, bf16[32,64,64]{2,1,0:T(8,128)(2,1)}) custom-call(s32[1]{0:T(128)} %bitcast.me_ref, bf16[4,512,512]{2,1,0:T(8,128)(2,1)S(1)} %get-tuple-element.94.term_ref, bf16[4,512,256]{2,1,0:T(8,128)(2,1)S(1)} %collective-permute-done.9.after_ref.values_ref, ...), custom_call_target="tpu_custom_call" | custom-call | flops 536870912 | bytes 7077888 | tf_op jit(solution)/shard_map/factor_sum_kernel/pallas_call | solution.py:55
  117.6 2.2 %collective-permute-start.28 = (bf16[2,4,32,256]{3,2,1,0:T(8,128)(2,1)S(1)}, bf16[2,4,32,256]{3,2,1,0:T(8,128)(2,1)S(1)}, u32[]{:S(2)}, u32[]{:S(2)}) collective-permute-start(bf16[2,4,32,256]{3,2,1,0:T(8,128)(2,1)S(1)} %get-tuple-element.96), channel_id=1, source_target_pairs={{0,6},{1,7},{2,4},{3,5},{4,2},{5,3},{6,0},{7,1},{8,14},{9,15},{10,... | collective-permute-start | bytes 393224 | tf_op jit(solution)/shard_map/ppermute | solution.py:34
  119.8 1.2 collective-permute-done.18.refs_3_
  120.9 0.9 collective-permute-done.21.refs_6_
  121.9 2.3 %collective-permute-done.28.refs_7_ = bf16[2,4,32,256]{3,2,1,0:T(8,128)(2,1)S(1)} collective-permute-done((bf16[2,4,32,256]{3,2,1,0:T(8,128)(2,1)S(1)}, bf16[2,4,32,256]{3,2,1,0:T(8,128)(2,1)S(1)}, u32[]{:S(2)}, u32[]{:S(2)}) %collective-permute-start.28) | collective-permute-done | bytes 131104 | tf_op jit(solution)/shard_map/ppermute | solution.py:34
  124.1 1.8 %output_kernel.1 = (bf16[4,16,32,256]{3,2,1,0:T(8,128)(2,1)}, bf16[4,16,32,256]{3,2,1,0:T(8,128)(2,1)}) custom-call(s32[1]{0:T(128)} %bitcast.me_ref, bf16[4,16,32,256]{3,2,1,0:T(8,128)(2,1)S(1)} %bitcast.11, bf16[4,16,32,256]{3,2,1,0:T(8,128)(2,1)S(1)} %bitcast.13, bf16[2,4,32,256]{3,2,1,0:T(8,128)(2,1)S(1)} %get-tuple-element.79.refs_0_, ...), custom_call_target="tpu_custom_call" | custom-call | bytes 5242880 | tf_op jit(solution)/shard_map/output_kernel/pallas_call | solution.py:55
  (36 shorter events, 0.4 us)
Async XLA Ops:
  0.6 3.3 %copy-start = (bf16[4,512,512]{2,1,0:T(8,128)(2,1)S(1)}, bf16[4,512,512]{2,1,0:T(8,128)(2,1)}, u32[]{:S(2)}) copy-start(bf16[4,512,512]{2,1,0:T(8,128)(2,1)} %left_ref.3) | copy-start | bytes 6291460
  3.4 2.7 %collective-permute-start = (bf16[8,4,32,256]{3,2,1,0:T(8,128)(2,1)}, bf16[8,4,32,256]{3,2,1,0:T(8,128)(2,1)S(1)}, u32[]{:S(2)}, u32[]{:S(2)}) collective-permute-start(bf16[8,4,32,256]{3,2,1,0:T(8,128)(2,1)} %get-tuple-element.54), channel_id=1, source_target_pairs={{0,1},{1,0},{2,3},{3,2},{4,5},{5,4},{6,7},{7,6},{8,9},{9,8},{10,11... | collective-permute-start | bytes 1572872 | tf_op jit(solution)/shard_map/ppermute | solution.py:34
  3.9 1.2 copy-start.1
  5.1 2.8 %copy-start.6 = (bf16[8,4,32,256]{3,2,1,0:T(8,128)(2,1)S(1)}, bf16[8,4,32,256]{3,2,1,0:T(8,128)(2,1)}, u32[]{:S(2)}) copy-start(bf16[8,4,32,256]{3,2,1,0:T(8,128)(2,1)} %get-tuple-element.53.refs_0_) | copy-start | bytes 1572868
  5.1 9.5 %copy-start.2 = (bf16[1,2048,256]{2,1,0:T(8,128)(2,1)S(1)}, bf16[1,2048,256]{2,1,0:T(8,128)(2,1)}, u32[]{:S(2)}) copy-start(bf16[1,2048,256]{2,1,0:T(8,128)(2,1)} %param.5) | copy-start | bytes 3145732
  5.1 55.1 %copy-start.5 = (bf16[32,64,64]{2,1,0:T(8,128)(2,1)S(1)}, bf16[32,64,64]{2,1,0:T(8,128)(2,1)}, u32[]{:S(2)}) copy-start(bf16[32,64,64]{2,1,0:T(8,128)(2,1)} %right_ref.3) | copy-start | bytes 786436
  5.9 2.0 %collective-permute-start.1 = (bf16[8,4,32,256]{3,2,1,0:T(8,128)(2,1)S(1)}, bf16[8,4,32,256]{3,2,1,0:T(8,128)(2,1)S(1)}, u32[]{:S(2)}, u32[]{:S(2)}) collective-permute-start(bf16[8,4,32,256]{3,2,1,0:T(8,128)(2,1)S(1)} %get-tuple-element.57), channel_id=1, source_target_pairs={{0,1},{1,0},{2,3},{3,2},{4,5},{5,4},{6,7},{7,6},{8,9},{9,8},{10,11... | collective-permute-start | bytes 1572872 | tf_op jit(solution)/shard_map/ppermute | solution.py:34
  8.0 23.6 %collective-permute-start.2 = (bf16[2,2,4,32,256]{4,3,2,1,0:T(8,128)(2,1)S(1)}, bf16[2,2,4,32,256]{4,3,2,1,0:T(8,128)(2,1)S(1)}, u32[]{:S(2)}, u32[]{:S(2)}) collective-permute-start(bf16[2,2,4,32,256]{4,3,2,1,0:T(8,128)(2,1)S(1)} %get-tuple-element.59), channel_id=1, source_target_pairs={{0,8},{1,9},{2,10},{3,11},{4,12},{5,13},{6,14},{7,15},{8,0},{9,1},... | collective-permute-start | bytes 786440 | tf_op jit(solution)/shard_map/ppermute | solution.py:34
  11.8 23.1 %collective-permute-start.3 = (bf16[2,2,4,32,256]{4,3,2,1,0:T(8,128)(2,1)S(1)}, bf16[2,2,4,32,256]{4,3,2,1,0:T(8,128)(2,1)S(1)}, u32[]{:S(2)}, u32[]{:S(2)}) collective-permute-start(bf16[2,2,4,32,256]{4,3,2,1,0:T(8,128)(2,1)S(1)} %get-tuple-element.60), channel_id=1, source_target_pairs={{0,2},{1,3},{2,0},{3,1},{4,6},{5,7},{6,4},{7,5},{8,10},{9,11},{10,... | collective-permute-start | bytes 786440 | tf_op jit(solution)/shard_map/ppermute | solution.py:34
  13.3 10.8 %collective-permute-start.8 = (bf16[2,4,32,256]{3,2,1,0:T(8,128)(2,1)S(1)}, bf16[2,4,32,256]{3,2,1,0:T(8,128)(2,1)S(1)}, u32[]{:S(2)}, u32[]{:S(2)}) collective-permute-start(bf16[2,4,32,256]{3,2,1,0:T(8,128)(2,1)S(1)} %get-tuple-element.65), channel_id=1, source_target_pairs={{0,14},{1,15},{2,12},{3,13},{4,10},{5,11},{6,8},{7,9},{8,6},{9,7},... | collective-permute-start | bytes 393224 | tf_op jit(solution)/shard_map/ppermute | solution.py:34
  14.6 55.7 %collective-permute-start.9 = (bf16[4,512,256]{2,1,0:T(8,128)(2,1)S(1)}, bf16[4,512,256]{2,1,0:T(8,128)(2,1)S(1)}, u32[]{:S(2)}, u32[]{:S(2)}) collective-permute-start(bf16[4,512,256]{2,1,0:T(8,128)(2,1)S(1)} %bitcast.8), channel_id=1, source_target_pairs={{0,16},{16,0},{1,17},{17,1},{2,18},{18,2},{3,19},{19,3},{4,20},{20... | collective-permute-start | bytes 3145736 | tf_op jit(solution)/shard_map/ppermute | solution.py:17
  16.1 18.8 %collective-permute-start.4 = (bf16[2,2,4,32,256]{4,3,2,1,0:T(8,128)(2,1)S(1)}, bf16[2,2,4,32,256]{4,3,2,1,0:T(8,128)(2,1)S(1)}, u32[]{:S(2)}, u32[]{:S(2)}) collective-permute-start(bf16[2,2,4,32,256]{4,3,2,1,0:T(8,128)(2,1)S(1)} %get-tuple-element.61), channel_id=1, source_target_pairs={{0,4},{1,5},{2,6},{3,7},{4,0},{5,1},{6,2},{7,3},{8,12},{9,13},{10,... | collective-permute-start | bytes 786440 | tf_op jit(solution)/shard_map/ppermute | solution.py:34
  24.1 14.2 %collective-permute-start.5 = (bf16[2,2,4,32,256]{4,3,2,1,0:T(8,128)(2,1)S(1)}, bf16[2,2,4,32,256]{4,3,2,1,0:T(8,128)(2,1)S(1)}, u32[]{:S(2)}, u32[]{:S(2)}) collective-permute-start(bf16[2,2,4,32,256]{4,3,2,1,0:T(8,128)(2,1)S(1)} %get-tuple-element.62), channel_id=1, source_target_pairs={{0,6},{1,7},{2,4},{3,5},{4,2},{5,3},{6,0},{7,1},{8,14},{9,15},{10,... | collective-permute-start | bytes 786440 | tf_op jit(solution)/shard_map/ppermute | solution.py:34
  31.6 16.2 %collective-permute-start.6 = (bf16[2,2,4,32,256]{4,3,2,1,0:T(8,128)(2,1)S(1)}, bf16[2,2,4,32,256]{4,3,2,1,0:T(8,128)(2,1)S(1)}, u32[]{:S(2)}, u32[]{:S(2)}) collective-permute-start(bf16[2,2,4,32,256]{4,3,2,1,0:T(8,128)(2,1)S(1)} %get-tuple-element.63), channel_id=1, source_target_pairs={{0,12},{1,13},{2,14},{3,15},{4,8},{5,9},{6,10},{7,11},{8,4},{9,5},... | collective-permute-start | bytes 786440 | tf_op jit(solution)/shard_map/ppermute | solution.py:34
  34.9 25.3 %collective-permute-start.7 = (bf16[2,2,4,32,256]{4,3,2,1,0:T(8,128)(2,1)S(1)}, bf16[2,2,4,32,256]{4,3,2,1,0:T(8,128)(2,1)S(1)}, u32[]{:S(2)}, u32[]{:S(2)}) collective-permute-start(bf16[2,2,4,32,256]{4,3,2,1,0:T(8,128)(2,1)S(1)} %get-tuple-element.64), channel_id=1, source_target_pairs={{0,10},{1,11},{2,8},{3,9},{4,14},{5,15},{6,12},{7,13},{8,2},{9,3},... | collective-permute-start | bytes 786440 | tf_op jit(solution)/shard_map/ppermute | solution.py:34
  47.8 15.4 %collective-permute-start.10 = (bf16[2,4,32,256]{3,2,1,0:T(8,128)(2,1)S(1)}, bf16[2,4,32,256]{3,2,1,0:T(8,128)(2,1)S(1)}, u32[]{:S(2)}, u32[]{:S(2)}) collective-permute-start(bf16[2,4,32,256]{3,2,1,0:T(8,128)(2,1)S(1)} %get-tuple-element.69), channel_id=1, source_target_pairs={{0,14},{1,15},{2,12},{3,13},{4,10},{5,11},{6,8},{7,9},{8,6},{9,7},... | collective-permute-start | bytes 393224 | tf_op jit(solution)/shard_map/ppermute | solution.py:34
  63.2 2.0 %collective-permute-start.11 = (bf16[8,4,32,256]{3,2,1,0:T(8,128)(2,1)S(1)}, bf16[8,4,32,256]{3,2,1,0:T(8,128)(2,1)S(1)}, u32[]{:S(2)}, u32[]{:S(2)}) collective-permute-start(bf16[8,4,32,256]{3,2,1,0:T(8,128)(2,1)S(1)} %get-tuple-element.74), channel_id=1, source_target_pairs={{0,1},{1,0},{2,3},{3,2},{4,5},{5,4},{6,7},{7,6},{8,9},{9,8},{10,11... | collective-permute-start | bytes 1572872 | tf_op jit(solution)/shard_map/ppermute | solution.py:34
  65.3 9.4 %collective-permute-start.12 = (bf16[2,4,32,256]{3,2,1,0:T(8,128)(2,1)S(1)}, bf16[2,4,32,256]{3,2,1,0:T(8,128)(2,1)S(1)}, u32[]{:S(2)}, u32[]{:S(2)}) collective-permute-start(bf16[2,4,32,256]{3,2,1,0:T(8,128)(2,1)S(1)} %get-tuple-element.75), channel_id=1, source_target_pairs={{0,8},{1,9},{2,10},{3,11},{4,12},{5,13},{6,14},{7,15},{8,0},{9,1},... | collective-permute-start | bytes 393224 | tf_op jit(solution)/shard_map/ppermute | solution.py:34
  66.3 8.4 %collective-permute-start.13 = (bf16[2,4,32,256]{3,2,1,0:T(8,128)(2,1)S(1)}, bf16[2,4,32,256]{3,2,1,0:T(8,128)(2,1)S(1)}, u32[]{:S(2)}, u32[]{:S(2)}) collective-permute-start(bf16[2,4,32,256]{3,2,1,0:T(8,128)(2,1)S(1)} %get-tuple-element.76), channel_id=1, source_target_pairs={{0,2},{1,3},{2,0},{3,1},{4,6},{5,7},{6,4},{7,5},{8,10},{9,11},{10,... | collective-permute-start | bytes 393224 | tf_op jit(solution)/shard_map/ppermute | solution.py:34
  67.8 8.2 %collective-permute-start.14 = (bf16[2,4,32,256]{3,2,1,0:T(8,128)(2,1)S(1)}, bf16[2,4,32,256]{3,2,1,0:T(8,128)(2,1)S(1)}, u32[]{:S(2)}, u32[]{:S(2)}) collective-permute-start(bf16[2,4,32,256]{3,2,1,0:T(8,128)(2,1)S(1)} %get-tuple-element.77), channel_id=1, source_target_pairs={{0,4},{1,5},{2,6},{3,7},{4,0},{5,1},{6,2},{7,3},{8,12},{9,13},{10,... | collective-permute-start | bytes 393224 | tf_op jit(solution)/shard_map/ppermute | solution.py:34
  76.0 5.4 %collective-permute-start.15 = (bf16[8,4,32,256]{3,2,1,0:T(8,128)(2,1)S(1)}, bf16[8,4,32,256]{3,2,1,0:T(8,128)(2,1)S(1)}, u32[]{:S(2)}, u32[]{:S(2)}) collective-permute-start(bf16[8,4,32,256]{3,2,1,0:T(8,128)(2,1)S(1)} %get-tuple-element.78), channel_id=1, source_target_pairs={{0,1},{1,0},{2,3},{3,2},{4,5},{5,4},{6,7},{7,6},{8,9},{9,8},{10,11... | collective-permute-start | bytes 1572872 | tf_op jit(solution)/shard_map/ppermute | solution.py:34
  76.0 9.4 %collective-permute-start.25 = (bf16[2,4,32,256]{3,2,1,0:T(8,128)(2,1)S(1)}, bf16[2,4,32,256]{3,2,1,0:T(8,128)(2,1)S(1)}, u32[]{:S(2)}, u32[]{:S(2)}) collective-permute-start(bf16[2,4,32,256]{3,2,1,0:T(8,128)(2,1)S(1)} %get-tuple-element.92), channel_id=1, source_target_pairs={{0,14},{1,15},{2,12},{3,13},{4,10},{5,11},{6,8},{7,9},{8,6},{9,7},... | collective-permute-start | bytes 393224 | tf_op jit(solution)/shard_map/ppermute | solution.py:34
  78.0 32.7 %collective-permute-start.26 = (bf16[12,4,32,256]{3,2,1,0:T(8,128)(2,1)S(1)}, bf16[12,4,32,256]{3,2,1,0:T(8,128)(2,1)S(1)}, u32[]{:S(2)}, u32[]{:S(2)}) collective-permute-start(bf16[12,4,32,256]{3,2,1,0:T(8,128)(2,1)S(1)} %gather_kernel.2.first_ref), channel_id=1, source_target_pairs={{0,16},{16,0},{1,17},{17,1},{2,18},{18,2},{3,19},{19,3},{4,20},{20... | collective-permute-start | bytes 2359304 | tf_op jit(solution)/shard_map/ppermute | solution.py:17
  79.5 18.6 %collective-permute-start.22 = (bf16[2,4,32,256]{3,2,1,0:T(8,128)(2,1)S(1)}, bf16[2,4,32,256]{3,2,1,0:T(8,128)(2,1)S(1)}, u32[]{:S(2)}, u32[]{:S(2)}) collective-permute-start(bf16[2,4,32,256]{3,2,1,0:T(8,128)(2,1)S(1)} %get-tuple-element.89), channel_id=1, source_target_pairs={{0,12},{1,13},{2,14},{3,15},{4,8},{5,9},{6,10},{7,11},{8,4},{9,5},... | collective-permute-start | bytes 393224 | tf_op jit(solution)/shard_map/ppermute | solution.py:34
  81.5 16.6 %collective-permute-start.16 = (bf16[2,4,32,256]{3,2,1,0:T(8,128)(2,1)S(1)}, bf16[2,4,32,256]{3,2,1,0:T(8,128)(2,1)S(1)}, u32[]{:S(2)}, u32[]{:S(2)}) collective-permute-start(bf16[2,4,32,256]{3,2,1,0:T(8,128)(2,1)S(1)} %get-tuple-element.80), channel_id=1, source_target_pairs={{0,8},{1,9},{2,10},{3,11},{4,12},{5,13},{6,14},{7,15},{8,0},{9,1},... | collective-permute-start | bytes 393224 | tf_op jit(solution)/shard_map/ppermute | solution.py:34
  81.5 20.0 %collective-permute-start.23 = (bf16[2,4,32,256]{3,2,1,0:T(8,128)(2,1)S(1)}, bf16[2,4,32,256]{3,2,1,0:T(8,128)(2,1)S(1)}, u32[]{:S(2)}, u32[]{:S(2)}) collective-permute-start(bf16[2,4,32,256]{3,2,1,0:T(8,128)(2,1)S(1)} %get-tuple-element.90), channel_id=1, source_target_pairs={{0,10},{1,11},{2,8},{3,9},{4,14},{5,15},{6,12},{7,13},{8,2},{9,3},... | collective-permute-start | bytes 393224 | tf_op jit(solution)/shard_map/ppermute | solution.py:34
  85.4 16.4 %collective-permute-start.24 = (bf16[2,4,32,256]{3,2,1,0:T(8,128)(2,1)S(1)}, bf16[2,4,32,256]{3,2,1,0:T(8,128)(2,1)S(1)}, u32[]{:S(2)}, u32[]{:S(2)}) collective-permute-start(bf16[2,4,32,256]{3,2,1,0:T(8,128)(2,1)S(1)} %get-tuple-element.91), channel_id=1, source_target_pairs={{0,6},{1,7},{2,4},{3,5},{4,2},{5,3},{6,0},{7,1},{8,14},{9,15},{10,... | collective-permute-start | bytes 393224 | tf_op jit(solution)/shard_map/ppermute | solution.py:34
  101.8 13.3 %collective-permute-start.27 = (bf16[8,4,32,256]{3,2,1,0:T(8,128)(2,1)S(1)}, bf16[8,4,32,256]{3,2,1,0:T(8,128)(2,1)S(1)}, u32[]{:S(2)}, u32[]{:S(2)}) collective-permute-start(bf16[8,4,32,256]{3,2,1,0:T(8,128)(2,1)S(1)} %gather_kernel.3.second_ref), channel_id=1, source_target_pairs={{0,16},{16,0},{1,17},{17,1},{2,18},{18,2},{3,19},{19,3},{4,20},{20... | collective-permute-start | bytes 1572872 | tf_op jit(solution)/shard_map/ppermute | solution.py:17
  104.4 13.1 %collective-permute-start.17 = (bf16[2,4,32,256]{3,2,1,0:T(8,128)(2,1)S(1)}, bf16[2,4,32,256]{3,2,1,0:T(8,128)(2,1)S(1)}, u32[]{:S(2)}, u32[]{:S(2)}) collective-permute-start(bf16[2,4,32,256]{3,2,1,0:T(8,128)(2,1)S(1)} %get-tuple-element.81), channel_id=1, source_target_pairs={{0,12},{1,13},{2,14},{3,15},{4,8},{5,9},{6,10},{7,11},{8,4},{9,5},... | collective-permute-start | bytes 393224 | tf_op jit(solution)/shard_map/ppermute | solution.py:34
  106.4 14.5 %collective-permute-start.18 = (bf16[2,4,32,256]{3,2,1,0:T(8,128)(2,1)S(1)}, bf16[2,4,32,256]{3,2,1,0:T(8,128)(2,1)S(1)}, u32[]{:S(2)}, u32[]{:S(2)}) collective-permute-start(bf16[2,4,32,256]{3,2,1,0:T(8,128)(2,1)S(1)} %get-tuple-element.82), channel_id=1, source_target_pairs={{0,10},{1,11},{2,8},{3,9},{4,14},{5,15},{6,12},{7,13},{8,2},{9,3},... | collective-permute-start | bytes 393224 | tf_op jit(solution)/shard_map/ppermute | solution.py:34
  106.4 14.5 %collective-permute-start.19 = (bf16[2,4,32,256]{3,2,1,0:T(8,128)(2,1)S(1)}, bf16[2,4,32,256]{3,2,1,0:T(8,128)(2,1)S(1)}, u32[]{:S(2)}, u32[]{:S(2)}) collective-permute-start(bf16[2,4,32,256]{3,2,1,0:T(8,128)(2,1)S(1)} %get-tuple-element.83), channel_id=1, source_target_pairs={{0,14},{1,15},{2,12},{3,13},{4,10},{5,11},{6,8},{7,9},{8,6},{9,7},... | collective-permute-start | bytes 393224 | tf_op jit(solution)/shard_map/ppermute | solution.py:34
  110.6 10.3 %collective-permute-start.20 = (bf16[2,4,32,256]{3,2,1,0:T(8,128)(2,1)S(1)}, bf16[2,4,32,256]{3,2,1,0:T(8,128)(2,1)S(1)}, u32[]{:S(2)}, u32[]{:S(2)}) collective-permute-start(bf16[2,4,32,256]{3,2,1,0:T(8,128)(2,1)S(1)} %get-tuple-element.84), channel_id=1, source_target_pairs={{0,2},{1,3},{2,0},{3,1},{4,6},{5,7},{6,4},{7,5},{8,10},{9,11},{10,... | collective-permute-start | bytes 393224 | tf_op jit(solution)/shard_map/ppermute | solution.py:34
  115.2 6.7 %collective-permute-start.21 = (bf16[2,4,32,256]{3,2,1,0:T(8,128)(2,1)S(1)}, bf16[2,4,32,256]{3,2,1,0:T(8,128)(2,1)S(1)}, u32[]{:S(2)}, u32[]{:S(2)}) collective-permute-start(bf16[2,4,32,256]{3,2,1,0:T(8,128)(2,1)S(1)} %get-tuple-element.85), channel_id=1, source_target_pairs={{0,4},{1,5},{2,6},{3,7},{4,0},{5,1},{6,2},{7,3},{8,12},{9,13},{10,... | collective-permute-start | bytes 393224 | tf_op jit(solution)/shard_map/ppermute | solution.py:34
  115.2 9.0 %copy-start.3 = (bf16[1,2048,256]{2,1,0:T(8,128)(2,1)S(1)}, bf16[1,2048,256]{2,1,0:T(8,128)(2,1)}, u32[]{:S(2)}) copy-start(bf16[1,2048,256]{2,1,0:T(8,128)(2,1)} %param.6) | copy-start | bytes 3145732
  115.2 9.0 %copy-start.4 = (bf16[1,2048,256]{2,1,0:T(8,128)(2,1)S(1)}, bf16[1,2048,256]{2,1,0:T(8,128)(2,1)}, u32[]{:S(2)}) copy-start(bf16[1,2048,256]{2,1,0:T(8,128)(2,1)} %param.7) | copy-start | bytes 3145732
  117.6 6.6 %collective-permute-start.28 = (bf16[2,4,32,256]{3,2,1,0:T(8,128)(2,1)S(1)}, bf16[2,4,32,256]{3,2,1,0:T(8,128)(2,1)S(1)}, u32[]{:S(2)}, u32[]{:S(2)}) collective-permute-start(bf16[2,4,32,256]{3,2,1,0:T(8,128)(2,1)S(1)} %get-tuple-element.96), channel_id=1, source_target_pairs={{0,6},{1,7},{2,4},{3,5},{4,2},{5,3},{6,0},{7,1},{8,14},{9,15},{10,... | collective-permute-start | bytes 393224 | tf_op jit(solution)/shard_map/ppermute | solution.py:34

commit v19 on v16

--- a/solution.py
+++ b/solution.py
@@ -26,7 +26,7 @@
     near = list(range(1, half))
     far = list(range(half, chips, 2)) + list(range(half + 1, chips, 2))
     mixed = far[:1] + near[:-1] + far[1:-1] + near[-1:] + far[-1:]
-    return [0] + far[:1] + near + far[1:], [0] + mixed, [0] + far + near
+    return [0] + far[:1] + near + far[1:], [0] + mixed, [0] + far[:2] + far[:1:-1] + near
 
 
 def permute(array, offset):

time: 126 us -> 127 us (level)
  transfers between devices with their start and end apart: 29 -> 29, of which waited for: 15 -> 15; matrix products, arithmetic and copies ran while one was open for 0% -> 0% of each run, Pallas kernels for 10% -> 9%
where the time goes in v19:
time: 127 us
  waiting for transfers between devices  54.4 us (43%)
  starting transfers between devices  53.5 us (42%)
  Pallas kernels  16.6 us (13%)
    ppermute x26, waiting for transfers between devices, permute(): return lax.ppermute(array, 'seq', [(i, i ^ offset) for i in range(seq)])  51.3 us
    ppermute x26, starting transfers between devices, permute(): return lax.ppermute(array, 'seq', [(i, i ^ offset) for i in range(seq)])  47.9 us
    pallas_call x12, Pallas kernels, call(): pl.pallas_call(kernel, out_shape=out_shapes, in_specs=[pl.BlockSpec(memor...  16.6 us
    ppermute x3, starting transfers between devices, swap_sequences(): return lax.ppermute(array, 'dp', [(0, 1), (1, 0)])  5.64 us
    ppermute x3, waiting for transfers between devices, swap_sequences(): return lax.ppermute(array, 'dp', [(0, 1), (1, 0)])  3.13 us
  transfers between devices with their start and end apart: 29, of which 15 were waited for; matrix products, arithmetic and copies ran while one was open for 0% of the time, Pallas kernels for 9%

profile of v19, /device:TPU:0, one launch (start us, length us, event | category | flops | bytes accessed | tf_op | source)
XLA Modules:
  0.0 126.6 jit_solution(1923006137925342534)
XLA Ops:
  0.6 2.7 %product_kernel.1 = (bf16[8,4,32,256]{3,2,1,0:T(8,128)(2,1)}, bf16[8,4,32,256]{3,2,1,0:T(8,128)(2,1)}) custom-call(s32[1]{0:T(128)} %bitcast.me_ref, bf16[4,16,32,256]{3,2,1,0:T(8,128)(2,1)} %bitcast.10, bf16[4,16,32,256]{3,2,1,0:T(8,128)(2,1)} %bitcast.12), custom_call_target="tpu_custom_call" | custom-call | bytes 3145728 | tf_op jit(solution)/shard_map/product_kernel/pallas_call | solution.py:55
  3.4 0.5 collective-permute-start
  3.9 1.2 copy-done.1
  5.1 0.8 mix_kernel.1
  5.9 0.1 collective-permute-start.1
  6.0 1.9 %collective-permute-done.1.refs_3_ = bf16[8,4,32,256]{3,2,1,0:T(8,128)(2,1)S(1)} collective-permute-done((bf16[8,4,32,256]{3,2,1,0:T(8,128)(2,1)S(1)}, bf16[8,4,32,256]{3,2,1,0:T(8,128)(2,1)S(1)}, u32[]{:S(2)}, u32[]{:S(2)}) %collective-permute-start.1) | collective-permute-done | bytes 524320 | tf_op jit(solution)/shard_map/ppermute | solution.py:34
  7.9 0.1 pack_pairs_kernel.1
  8.0 3.8 %collective-permute-start.2 = (bf16[2,2,4,32,256]{4,3,2,1,0:T(8,128)(2,1)S(1)}, bf16[2,2,4,32,256]{4,3,2,1,0:T(8,128)(2,1)S(1)}, u32[]{:S(2)}, u32[]{:S(2)}) collective-permute-start(bf16[2,2,4,32,256]{4,3,2,1,0:T(8,128)(2,1)S(1)} %get-tuple-element.59), channel_id=1, source_target_pairs={{0,8},{1,9},{2,10},{3,11},{4,12},{5,13},{6,14},{7,15},{8,0},{9,1},... | collective-permute-start | bytes 786440 | tf_op jit(solution)/shard_map/ppermute | solution.py:34
  11.8 1.5 %collective-permute-start.3 = (bf16[2,2,4,32,256]{4,3,2,1,0:T(8,128)(2,1)S(1)}, bf16[2,2,4,32,256]{4,3,2,1,0:T(8,128)(2,1)S(1)}, u32[]{:S(2)}, u32[]{:S(2)}) collective-permute-start(bf16[2,2,4,32,256]{4,3,2,1,0:T(8,128)(2,1)S(1)} %get-tuple-element.60), channel_id=1, source_target_pairs={{0,2},{1,3},{2,0},{3,1},{4,6},{5,7},{6,4},{7,5},{8,10},{9,11},{10,... | collective-permute-start | bytes 786440 | tf_op jit(solution)/shard_map/ppermute | solution.py:34
  13.3 1.3 %collective-permute-start.8 = (bf16[2,4,32,256]{3,2,1,0:T(8,128)(2,1)S(1)}, bf16[2,4,32,256]{3,2,1,0:T(8,128)(2,1)S(1)}, u32[]{:S(2)}, u32[]{:S(2)}) collective-permute-start(bf16[2,4,32,256]{3,2,1,0:T(8,128)(2,1)S(1)} %get-tuple-element.65), channel_id=1, source_target_pairs={{0,14},{1,15},{2,12},{3,13},{4,10},{5,11},{6,8},{7,9},{8,6},{9,7},... | collective-permute-start | bytes 393224 | tf_op jit(solution)/shard_map/ppermute | solution.py:34
  14.6 1.5 %collective-permute-start.9 = (bf16[4,512,256]{2,1,0:T(8,128)(2,1)S(1)}, bf16[4,512,256]{2,1,0:T(8,128)(2,1)S(1)}, u32[]{:S(2)}, u32[]{:S(2)}) collective-permute-start(bf16[4,512,256]{2,1,0:T(8,128)(2,1)S(1)} %bitcast.8), channel_id=1, source_target_pairs={{0,16},{16,0},{1,17},{17,1},{2,18},{18,2},{3,19},{19,3},{4,20},{20... | collective-permute-start | bytes 3145736 | tf_op jit(solution)/shard_map/ppermute | solution.py:17
  16.1 0.3 collective-permute-start.4
  16.4 7.7 %collective-permute-done.8.refs_7_ = bf16[2,4,32,256]{3,2,1,0:T(8,128)(2,1)S(1)} collective-permute-done((bf16[2,4,32,256]{3,2,1,0:T(8,128)(2,1)S(1)}, bf16[2,4,32,256]{3,2,1,0:T(8,128)(2,1)S(1)}, u32[]{:S(2)}, u32[]{:S(2)}) %collective-permute-start.8) | collective-permute-done | bytes 131104 | tf_op jit(solution)/shard_map/ppermute | solution.py:34
  24.1 7.5 %collective-permute-start.5 = (bf16[2,2,4,32,256]{4,3,2,1,0:T(8,128)(2,1)S(1)}, bf16[2,2,4,32,256]{4,3,2,1,0:T(8,128)(2,1)S(1)}, u32[]{:S(2)}, u32[]{:S(2)}) collective-permute-start(bf16[2,2,4,32,256]{4,3,2,1,0:T(8,128)(2,1)S(1)} %get-tuple-element.62), channel_id=1, source_target_pairs={{0,6},{1,7},{2,4},{3,5},{4,2},{5,3},{6,0},{7,1},{8,14},{9,15},{10,... | collective-permute-start | bytes 786440 | tf_op jit(solution)/shard_map/ppermute | solution.py:34
  31.6 3.3 %collective-permute-start.6 = (bf16[2,2,4,32,256]{4,3,2,1,0:T(8,128)(2,1)S(1)}, bf16[2,2,4,32,256]{4,3,2,1,0:T(8,128)(2,1)S(1)}, u32[]{:S(2)}, u32[]{:S(2)}) collective-permute-start(bf16[2,2,4,32,256]{4,3,2,1,0:T(8,128)(2,1)S(1)} %get-tuple-element.63), channel_id=1, source_target_pairs={{0,12},{1,13},{2,14},{3,15},{4,8},{5,9},{6,10},{7,11},{8,4},{9,5},... | collective-permute-start | bytes 786440 | tf_op jit(solution)/shard_map/ppermute | solution.py:34
  35.0 3.4 %collective-permute-done.5.refs_4_ = bf16[2,2,4,32,256]{4,3,2,1,0:T(8,128)(2,1)S(1)} collective-permute-done((bf16[2,2,4,32,256]{4,3,2,1,0:T(8,128)(2,1)S(1)}, bf16[2,2,4,32,256]{4,3,2,1,0:T(8,128)(2,1)S(1)}, u32[]{:S(2)}, u32[]{:S(2)}) %collective-permute-start.5) | collective-permute-done | bytes 262176 | tf_op jit(solution)/shard_map/ppermute | solution.py:34
  38.3 9.5 %collective-permute-done.6.refs_5_ = bf16[2,2,4,32,256]{4,3,2,1,0:T(8,128)(2,1)S(1)} collective-permute-done((bf16[2,2,4,32,256]{4,3,2,1,0:T(8,128)(2,1)S(1)}, bf16[2,2,4,32,256]{4,3,2,1,0:T(8,128)(2,1)S(1)}, u32[]{:S(2)}, u32[]{:S(2)}) %collective-permute-start.6) | collective-permute-done | bytes 262176 | tf_op jit(solution)/shard_map/ppermute | solution.py:34
  47.8 1.4 %collective-permute-start.10 = (bf16[2,4,32,256]{3,2,1,0:T(8,128)(2,1)S(1)}, bf16[2,4,32,256]{3,2,1,0:T(8,128)(2,1)S(1)}, u32[]{:S(2)}, u32[]{:S(2)}) collective-permute-start(bf16[2,4,32,256]{3,2,1,0:T(8,128)(2,1)S(1)} %get-tuple-element.69), channel_id=1, source_target_pairs={{0,14},{1,15},{2,12},{3,13},{4,10},{5,11},{6,8},{7,9},{8,6},{9,7},... | collective-permute-start | bytes 393224 | tf_op jit(solution)/shard_map/ppermute | solution.py:34
  49.2 11.1 %collective-permute-done.7.refs_6_ = bf16[2,2,4,32,256]{4,3,2,1,0:T(8,128)(2,1)S(1)} collective-permute-done((bf16[2,2,4,32,256]{4,3,2,1,0:T(8,128)(2,1)S(1)}, bf16[2,2,4,32,256]{4,3,2,1,0:T(8,128)(2,1)S(1)}, u32[]{:S(2)}, u32[]{:S(2)}) %collective-permute-start.7) | collective-permute-done | bytes 262176 | tf_op jit(solution)/shard_map/ppermute | solution.py:34
  60.2 3.0 %column_backward_kernel.1 = (bf16[8,4,32,256]{3,2,1,0:T(8,128)(2,1)S(1)}, bf16[8,4,32,256]{3,2,1,0:T(8,128)(2,1)S(1)}, bf16[32,64,256]{2,1,0:T(8,128)(2,1)S(1)}) custom-call(s32[1]{0:T(128)} %bitcast.me_ref, bf16[32,64,64]{2,1,0:T(8,128)(2,1)S(1)} %copy-done.5, bf16[2,2,4,32,256]{4,3,2,1,0:T(8,128)(2,1)S(1)} %get-tuple-element.58.refs_0_, ...), custom_call_target="tpu_custom_call" | custom-call | flops 67108864 | bytes 4325376 | tf_op jit(solution)/shard_map/column_backward_kernel/pallas_call | solution.py:55
  63.3 1.9 %collective-permute-done.11.other_ref = bf16[8,4,32,256]{3,2,1,0:T(8,128)(2,1)S(1)} collective-permute-done((bf16[8,4,32,256]{3,2,1,0:T(8,128)(2,1)S(1)}, bf16[8,4,32,256]{3,2,1,0:T(8,128)(2,1)S(1)}, u32[]{:S(2)}, u32[]{:S(2)}) %collective-permute-start.11) | collective-permute-done | bytes 524320 | tf_op jit(solution)/shard_map/ppermute | solution.py:34
  65.3 1.0 collective-permute-start.12
  66.3 1.5 %collective-permute-start.13 = (bf16[2,4,32,256]{3,2,1,0:T(8,128)(2,1)S(1)}, bf16[2,4,32,256]{3,2,1,0:T(8,128)(2,1)S(1)}, u32[]{:S(2)}, u32[]{:S(2)}) collective-permute-start(bf16[2,4,32,256]{3,2,1,0:T(8,128)(2,1)S(1)} %get-tuple-element.76), channel_id=1, source_target_pairs={{0,2},{1,3},{2,0},{3,1},{4,6},{5,7},{6,4},{7,5},{8,10},{9,11},{10,... | collective-permute-start | bytes 393224 | tf_op jit(solution)/shard_map/ppermute | solution.py:34
  67.8 2.6 %collective-permute-start.14 = (bf16[2,4,32,256]{3,2,1,0:T(8,128)(2,1)S(1)}, bf16[2,4,32,256]{3,2,1,0:T(8,128)(2,1)S(1)}, u32[]{:S(2)}, u32[]{:S(2)}) collective-permute-start(bf16[2,4,32,256]{3,2,1,0:T(8,128)(2,1)S(1)} %get-tuple-element.77), channel_id=1, source_target_pairs={{0,4},{1,5},{2,6},{3,7},{4,0},{5,1},{6,2},{7,3},{8,12},{9,13},{10,... | collective-permute-start | bytes 393224 | tf_op jit(solution)/shard_map/ppermute | solution.py:34
  70.4 3.3 %column_forward_kernel.1 = (bf16[8,4,32,256]{3,2,1,0:T(8,128)(2,1)S(1)}, bf16[8,4,32,256]{3,2,1,0:T(8,128)(2,1)S(1)}, bf16[512,256]{1,0:T(8,128)(2,1)S(1)}) custom-call(s32[1]{0:T(128)} %bitcast.me_ref, bf16[32,64,64]{2,1,0:T(8,128)(2,1)S(1)} %copy-done.5, bf16[32,64,256]{2,1,0:T(8,128)(2,1)S(1)} %get-tuple-element.66.grad_ref, ...), custom_call_target="tpu_custom_call" | custom-call | flops 134217728 | bytes 5636096 | tf_op jit(solution)/shard_map/column_forward_kernel/pallas_call | solution.py:55
  73.7 1.0 collective-permute-done.12.refs_1_
  74.7 1.3 %collective-permute-done.14.refs_3_ = bf16[2,4,32,256]{3,2,1,0:T(8,128)(2,1)S(1)} collective-permute-done((bf16[2,4,32,256]{3,2,1,0:T(8,128)(2,1)S(1)}, bf16[2,4,32,256]{3,2,1,0:T(8,128)(2,1)S(1)}, u32[]{:S(2)}, u32[]{:S(2)}) %collective-permute-start.14) | collective-permute-done | bytes 131104 | tf_op jit(solution)/shard_map/ppermute | solution.py:34
  76.0 1.9 %collective-permute-start.25 = (bf16[2,4,32,256]{3,2,1,0:T(8,128)(2,1)S(1)}, bf16[2,4,32,256]{3,2,1,0:T(8,128)(2,1)S(1)}, u32[]{:S(2)}, u32[]{:S(2)}) collective-permute-start(bf16[2,4,32,256]{3,2,1,0:T(8,128)(2,1)S(1)} %get-tuple-element.92), channel_id=1, source_target_pairs={{0,14},{1,15},{2,12},{3,13},{4,10},{5,11},{6,8},{7,9},{8,6},{9,7},... | collective-permute-start | bytes 393224 | tf_op jit(solution)/shard_map/ppermute | solution.py:34
  78.0 1.6 %collective-permute-start.26 = (bf16[12,4,32,256]{3,2,1,0:T(8,128)(2,1)S(1)}, bf16[12,4,32,256]{3,2,1,0:T(8,128)(2,1)S(1)}, u32[]{:S(2)}, u32[]{:S(2)}) collective-permute-start(bf16[12,4,32,256]{3,2,1,0:T(8,128)(2,1)S(1)} %gather_kernel.2.first_ref), channel_id=1, source_target_pairs={{0,16},{16,0},{1,17},{17,1},{2,18},{18,2},{3,19},{19,3},{4,20},{20... | collective-permute-start | bytes 2359304 | tf_op jit(solution)/shard_map/ppermute | solution.py:17
  79.5 1.9 %collective-permute-start.22 = (bf16[2,4,32,256]{3,2,1,0:T(8,128)(2,1)S(1)}, bf16[2,4,32,256]{3,2,1,0:T(8,128)(2,1)S(1)}, u32[]{:S(2)}, u32[]{:S(2)}) collective-permute-start(bf16[2,4,32,256]{3,2,1,0:T(8,128)(2,1)S(1)} %get-tuple-element.89), channel_id=1, source_target_pairs={{0,12},{1,13},{2,14},{3,15},{4,8},{5,9},{6,10},{7,11},{8,4},{9,5},... | collective-permute-start | bytes 393224 | tf_op jit(solution)/shard_map/ppermute | solution.py:34
  81.5 0.1 collective-permute-start.16
  81.5 3.9 %collective-permute-start.23 = (bf16[2,4,32,256]{3,2,1,0:T(8,128)(2,1)S(1)}, bf16[2,4,32,256]{3,2,1,0:T(8,128)(2,1)S(1)}, u32[]{:S(2)}, u32[]{:S(2)}) collective-permute-start(bf16[2,4,32,256]{3,2,1,0:T(8,128)(2,1)S(1)} %get-tuple-element.90), channel_id=1, source_target_pairs={{0,10},{1,11},{2,8},{3,9},{4,14},{5,15},{6,12},{7,13},{8,2},{9,3},... | collective-permute-start | bytes 393224 | tf_op jit(solution)/shard_map/ppermute | solution.py:34
  85.4 7.8 %collective-permute-start.24 = (bf16[2,4,32,256]{3,2,1,0:T(8,128)(2,1)S(1)}, bf16[2,4,32,256]{3,2,1,0:T(8,128)(2,1)S(1)}, u32[]{:S(2)}, u32[]{:S(2)}) collective-permute-start(bf16[2,4,32,256]{3,2,1,0:T(8,128)(2,1)S(1)} %get-tuple-element.91), channel_id=1, source_target_pairs={{0,6},{1,7},{2,4},{3,5},{4,2},{5,3},{6,0},{7,1},{8,14},{9,15},{10,... | collective-permute-start | bytes 393224 | tf_op jit(solution)/shard_map/ppermute | solution.py:34
  93.2 4.9 %collective-permute-done.16.refs_1_ = bf16[2,4,32,256]{3,2,1,0:T(8,128)(2,1)S(1)} collective-permute-done((bf16[2,4,32,256]{3,2,1,0:T(8,128)(2,1)S(1)}, bf16[2,4,32,256]{3,2,1,0:T(8,128)(2,1)S(1)}, u32[]{:S(2)}, u32[]{:S(2)}) %collective-permute-start.16) | collective-permute-done | bytes 131104 | tf_op jit(solution)/shard_map/ppermute | solution.py:34
  98.1 3.4 %collective-permute-done.23.refs_1_ = bf16[2,4,32,256]{3,2,1,0:T(8,128)(2,1)S(1)} collective-permute-done((bf16[2,4,32,256]{3,2,1,0:T(8,128)(2,1)S(1)}, bf16[2,4,32,256]{3,2,1,0:T(8,128)(2,1)S(1)}, u32[]{:S(2)}, u32[]{:S(2)}) %collective-permute-start.23) | collective-permute-done | bytes 131104 | tf_op jit(solution)/shard_map/ppermute | solution.py:34
  101.6 0.2 collective-permute-done.24.refs_2_
  101.8 2.6 %collective-permute-start.27 = (bf16[8,4,32,256]{3,2,1,0:T(8,128)(2,1)S(1)}, bf16[8,4,32,256]{3,2,1,0:T(8,128)(2,1)S(1)}, u32[]{:S(2)}, u32[]{:S(2)}) collective-permute-start(bf16[8,4,32,256]{3,2,1,0:T(8,128)(2,1)S(1)} %gather_kernel.3.second_ref), channel_id=1, source_target_pairs={{0,16},{16,0},{1,17},{17,1},{2,18},{18,2},{3,19},{19,3},{4,20},{20... | collective-permute-start | bytes 1572872 | tf_op jit(solution)/shard_map/ppermute | solution.py:17
  104.4 1.9 %collective-permute-start.17 = (bf16[2,4,32,256]{3,2,1,0:T(8,128)(2,1)S(1)}, bf16[2,4,32,256]{3,2,1,0:T(8,128)(2,1)S(1)}, u32[]{:S(2)}, u32[]{:S(2)}) collective-permute-start(bf16[2,4,32,256]{3,2,1,0:T(8,128)(2,1)S(1)} %get-tuple-element.81), channel_id=1, source_target_pairs={{0,12},{1,13},{2,14},{3,15},{4,8},{5,9},{6,10},{7,11},{8,4},{9,5},... | collective-permute-start | bytes 393224 | tf_op jit(solution)/shard_map/ppermute | solution.py:34
  106.4 1.9 %collective-permute-start.18 = (bf16[2,4,32,256]{3,2,1,0:T(8,128)(2,1)S(1)}, bf16[2,4,32,256]{3,2,1,0:T(8,128)(2,1)S(1)}, u32[]{:S(2)}, u32[]{:S(2)}) collective-permute-start(bf16[2,4,32,256]{3,2,1,0:T(8,128)(2,1)S(1)} %get-tuple-element.82), channel_id=1, source_target_pairs={{0,14},{1,15},{2,12},{3,13},{4,10},{5,11},{6,8},{7,9},{8,6},{9,7},... | collective-permute-start | bytes 393224 | tf_op jit(solution)/shard_map/ppermute | solution.py:34
  108.3 2.3 %row_backward_kernel.1 = (bf16[4,512,256]{2,1,0:T(8,128)(2,1)}, bf16[4,512,512]{2,1,0:T(8,128)(2,1)S(1)}) custom-call(s32[1]{0:T(128)} %bitcast.me_ref, bf16[4,512,512]{2,1,0:T(8,128)(2,1)S(1)} %copy-done, bf16[4,512,256]{2,1,0:T(8,128)(2,1)S(1)} %bitcast.9, bf16[12,4,32,256]{3,2,1,0:T(8,128)(2,1)S(1)} %gather_kernel.2.first_ref, ...), custom_call_target="tpu_custom_call" | custom-call | flops 1073741824 | bytes 7602176 | tf_op jit(solution)/shard_map/row_backward_kernel/pallas_call | solution.py:55
  110.6 1.4 %collective-permute-start.20 = (bf16[2,4,32,256]{3,2,1,0:T(8,128)(2,1)S(1)}, bf16[2,4,32,256]{3,2,1,0:T(8,128)(2,1)S(1)}, u32[]{:S(2)}, u32[]{:S(2)}) collective-permute-start(bf16[2,4,32,256]{3,2,1,0:T(8,128)(2,1)S(1)} %get-tuple-element.84), channel_id=1, source_target_pairs={{0,2},{1,3},{2,0},{3,1},{4,6},{5,7},{6,4},{7,5},{8,10},{9,11},{10,... | collective-permute-start | bytes 393224 | tf_op jit(solution)/shard_map/ppermute | solution.py:34
  112.0 3.1 %collective-permute-done.27.second_ref = bf16[8,4,32,256]{3,2,1,0:T(8,128)(2,1)S(1)} collective-permute-done((bf16[8,4,32,256]{3,2,1,0:T(8,128)(2,1)S(1)}, bf16[8,4,32,256]{3,2,1,0:T(8,128)(2,1)S(1)}, u32[]{:S(2)}, u32[]{:S(2)}) %collective-permute-start.27) | collective-permute-done | bytes 524320 | tf_op jit(solution)/shard_map/ppermute | solution.py:17
  115.2 2.4 %factor_sum_kernel.1 = (bf16[4,512,512]{2,1,0:T(8,128)(2,1)}, bf16[32,64,64]{2,1,0:T(8,128)(2,1)}) custom-call(s32[1]{0:T(128)} %bitcast.me_ref, bf16[4,512,512]{2,1,0:T(8,128)(2,1)S(1)} %get-tuple-element.94.term_ref, bf16[4,512,256]{2,1,0:T(8,128)(2,1)S(1)} %collective-permute-done.9.after_ref.values_ref, ...), custom_call_target="tpu_custom_call" | custom-call | flops 536870912 | bytes 7077888 | tf_op jit(solution)/shard_map/factor_sum_kernel/pallas_call | solution.py:55
  117.6 2.2 %collective-permute-start.28 = (bf16[2,4,32,256]{3,2,1,0:T(8,128)(2,1)S(1)}, bf16[2,4,32,256]{3,2,1,0:T(8,128)(2,1)S(1)}, u32[]{:S(2)}, u32[]{:S(2)}) collective-permute-start(bf16[2,4,32,256]{3,2,1,0:T(8,128)(2,1)S(1)} %get-tuple-element.96), channel_id=1, source_target_pairs={{0,6},{1,7},{2,4},{3,5},{4,2},{5,3},{6,0},{7,1},{8,14},{9,15},{10,... | collective-permute-start | bytes 393224 | tf_op jit(solution)/shard_map/ppermute | solution.py:34
  119.8 1.3 %collective-permute-done.19.refs_4_ = bf16[2,4,32,256]{3,2,1,0:T(8,128)(2,1)S(1)} collective-permute-done((bf16[2,4,32,256]{3,2,1,0:T(8,128)(2,1)S(1)}, bf16[2,4,32,256]{3,2,1,0:T(8,128)(2,1)S(1)}, u32[]{:S(2)}, u32[]{:S(2)}) %collective-permute-start.19) | collective-permute-done | bytes 131104 | tf_op jit(solution)/shard_map/ppermute | solution.py:34
  121.1 1.7 %collective-permute-done.21.refs_6_ = bf16[2,4,32,256]{3,2,1,0:T(8,128)(2,1)S(1)} collective-permute-done((bf16[2,4,32,256]{3,2,1,0:T(8,128)(2,1)S(1)}, bf16[2,4,32,256]{3,2,1,0:T(8,128)(2,1)S(1)}, u32[]{:S(2)}, u32[]{:S(2)}) %collective-permute-start.21) | collective-permute-done | bytes 131104 | tf_op jit(solution)/shard_map/ppermute | solution.py:34
  122.8 2.0 %collective-permute-done.28.refs_7_ = bf16[2,4,32,256]{3,2,1,0:T(8,128)(2,1)S(1)} collective-permute-done((bf16[2,4,32,256]{3,2,1,0:T(8,128)(2,1)S(1)}, bf16[2,4,32,256]{3,2,1,0:T(8,128)(2,1)S(1)}, u32[]{:S(2)}, u32[]{:S(2)}) %collective-permute-start.28) | collective-permute-done | bytes 131104 | tf_op jit(solution)/shard_map/ppermute | solution.py:34
  124.8 1.8 %output_kernel.1 = (bf16[4,16,32,256]{3,2,1,0:T(8,128)(2,1)}, bf16[4,16,32,256]{3,2,1,0:T(8,128)(2,1)}) custom-call(s32[1]{0:T(128)} %bitcast.me_ref, bf16[4,16,32,256]{3,2,1,0:T(8,128)(2,1)S(1)} %bitcast.11, bf16[4,16,32,256]{3,2,1,0:T(8,128)(2,1)S(1)} %bitcast.13, bf16[2,4,32,256]{3,2,1,0:T(8,128)(2,1)S(1)} %get-tuple-element.79.refs_0_, ...), custom_call_target="tpu_custom_call" | custom-call | bytes 5242880 | tf_op jit(solution)/shard_map/output_kernel/pallas_call | solution.py:55
  (36 shorter events, 0.4 us)
Async XLA Ops:
  0.6 3.3 %copy-start = (bf16[4,512,512]{2,1,0:T(8,128)(2,1)S(1)}, bf16[4,512,512]{2,1,0:T(8,128)(2,1)}, u32[]{:S(2)}) copy-start(bf16[4,512,512]{2,1,0:T(8,128)(2,1)} %left_ref.3) | copy-start | bytes 6291460
  3.4 2.7 %collective-permute-start = (bf16[8,4,32,256]{3,2,1,0:T(8,128)(2,1)}, bf16[8,4,32,256]{3,2,1,0:T(8,128)(2,1)S(1)}, u32[]{:S(2)}, u32[]{:S(2)}) collective-permute-start(bf16[8,4,32,256]{3,2,1,0:T(8,128)(2,1)} %get-tuple-element.54), channel_id=1, source_target_pairs={{0,1},{1,0},{2,3},{3,2},{4,5},{5,4},{6,7},{7,6},{8,9},{9,8},{10,11... | collective-permute-start | bytes 1572872 | tf_op jit(solution)/shard_map/ppermute | solution.py:34
  3.9 1.2 copy-start.1
  5.1 2.8 %copy-start.6 = (bf16[8,4,32,256]{3,2,1,0:T(8,128)(2,1)S(1)}, bf16[8,4,32,256]{3,2,1,0:T(8,128)(2,1)}, u32[]{:S(2)}) copy-start(bf16[8,4,32,256]{3,2,1,0:T(8,128)(2,1)} %get-tuple-element.53.refs_0_) | copy-start | bytes 1572868
  5.1 9.5 %copy-start.2 = (bf16[1,2048,256]{2,1,0:T(8,128)(2,1)S(1)}, bf16[1,2048,256]{2,1,0:T(8,128)(2,1)}, u32[]{:S(2)}) copy-start(bf16[1,2048,256]{2,1,0:T(8,128)(2,1)} %param.5) | copy-start | bytes 3145732
  5.1 55.1 %copy-start.5 = (bf16[32,64,64]{2,1,0:T(8,128)(2,1)S(1)}, bf16[32,64,64]{2,1,0:T(8,128)(2,1)}, u32[]{:S(2)}) copy-start(bf16[32,64,64]{2,1,0:T(8,128)(2,1)} %right_ref.3) | copy-start | bytes 786436
  5.9 2.0 %collective-permute-start.1 = (bf16[8,4,32,256]{3,2,1,0:T(8,128)(2,1)S(1)}, bf16[8,4,32,256]{3,2,1,0:T(8,128)(2,1)S(1)}, u32[]{:S(2)}, u32[]{:S(2)}) collective-permute-start(bf16[8,4,32,256]{3,2,1,0:T(8,128)(2,1)S(1)} %get-tuple-element.57), channel_id=1, source_target_pairs={{0,1},{1,0},{2,3},{3,2},{4,5},{5,4},{6,7},{7,6},{8,9},{9,8},{10,11... | collective-permute-start | bytes 1572872 | tf_op jit(solution)/shard_map/ppermute | solution.py:34
  8.0 23.6 %collective-permute-start.2 = (bf16[2,2,4,32,256]{4,3,2,1,0:T(8,128)(2,1)S(1)}, bf16[2,2,4,32,256]{4,3,2,1,0:T(8,128)(2,1)S(1)}, u32[]{:S(2)}, u32[]{:S(2)}) collective-permute-start(bf16[2,2,4,32,256]{4,3,2,1,0:T(8,128)(2,1)S(1)} %get-tuple-element.59), channel_id=1, source_target_pairs={{0,8},{1,9},{2,10},{3,11},{4,12},{5,13},{6,14},{7,15},{8,0},{9,1},... | collective-permute-start | bytes 786440 | tf_op jit(solution)/shard_map/ppermute | solution.py:34
  11.8 23.1 %collective-permute-start.3 = (bf16[2,2,4,32,256]{4,3,2,1,0:T(8,128)(2,1)S(1)}, bf16[2,2,4,32,256]{4,3,2,1,0:T(8,128)(2,1)S(1)}, u32[]{:S(2)}, u32[]{:S(2)}) collective-permute-start(bf16[2,2,4,32,256]{4,3,2,1,0:T(8,128)(2,1)S(1)} %get-tuple-element.60), channel_id=1, source_target_pairs={{0,2},{1,3},{2,0},{3,1},{4,6},{5,7},{6,4},{7,5},{8,10},{9,11},{10,... | collective-permute-start | bytes 786440 | tf_op jit(solution)/shard_map/ppermute | solution.py:34
  13.3 10.8 %collective-permute-start.8 = (bf16[2,4,32,256]{3,2,1,0:T(8,128)(2,1)S(1)}, bf16[2,4,32,256]{3,2,1,0:T(8,128)(2,1)S(1)}, u32[]{:S(2)}, u32[]{:S(2)}) collective-permute-start(bf16[2,4,32,256]{3,2,1,0:T(8,128)(2,1)S(1)} %get-tuple-element.65), channel_id=1, source_target_pairs={{0,14},{1,15},{2,12},{3,13},{4,10},{5,11},{6,8},{7,9},{8,6},{9,7},... | collective-permute-start | bytes 393224 | tf_op jit(solution)/shard_map/ppermute | solution.py:34
  14.6 55.7 %collective-permute-start.9 = (bf16[4,512,256]{2,1,0:T(8,128)(2,1)S(1)}, bf16[4,512,256]{2,1,0:T(8,128)(2,1)S(1)}, u32[]{:S(2)}, u32[]{:S(2)}) collective-permute-start(bf16[4,512,256]{2,1,0:T(8,128)(2,1)S(1)} %bitcast.8), channel_id=1, source_target_pairs={{0,16},{16,0},{1,17},{17,1},{2,18},{18,2},{3,19},{19,3},{4,20},{20... | collective-permute-start | bytes 3145736 | tf_op jit(solution)/shard_map/ppermute | solution.py:17
  16.1 18.8 %collective-permute-start.4 = (bf16[2,2,4,32,256]{4,3,2,1,0:T(8,128)(2,1)S(1)}, bf16[2,2,4,32,256]{4,3,2,1,0:T(8,128)(2,1)S(1)}, u32[]{:S(2)}, u32[]{:S(2)}) collective-permute-start(bf16[2,2,4,32,256]{4,3,2,1,0:T(8,128)(2,1)S(1)} %get-tuple-element.61), channel_id=1, source_target_pairs={{0,4},{1,5},{2,6},{3,7},{4,0},{5,1},{6,2},{7,3},{8,12},{9,13},{10,... | collective-permute-start | bytes 786440 | tf_op jit(solution)/shard_map/ppermute | solution.py:34
  24.1 14.2 %collective-permute-start.5 = (bf16[2,2,4,32,256]{4,3,2,1,0:T(8,128)(2,1)S(1)}, bf16[2,2,4,32,256]{4,3,2,1,0:T(8,128)(2,1)S(1)}, u32[]{:S(2)}, u32[]{:S(2)}) collective-permute-start(bf16[2,2,4,32,256]{4,3,2,1,0:T(8,128)(2,1)S(1)} %get-tuple-element.62), channel_id=1, source_target_pairs={{0,6},{1,7},{2,4},{3,5},{4,2},{5,3},{6,0},{7,1},{8,14},{9,15},{10,... | collective-permute-start | bytes 786440 | tf_op jit(solution)/shard_map/ppermute | solution.py:34
  31.6 16.2 %collective-permute-start.6 = (bf16[2,2,4,32,256]{4,3,2,1,0:T(8,128)(2,1)S(1)}, bf16[2,2,4,32,256]{4,3,2,1,0:T(8,128)(2,1)S(1)}, u32[]{:S(2)}, u32[]{:S(2)}) collective-permute-start(bf16[2,2,4,32,256]{4,3,2,1,0:T(8,128)(2,1)S(1)} %get-tuple-element.63), channel_id=1, source_target_pairs={{0,12},{1,13},{2,14},{3,15},{4,8},{5,9},{6,10},{7,11},{8,4},{9,5},... | collective-permute-start | bytes 786440 | tf_op jit(solution)/shard_map/ppermute | solution.py:34
  34.9 25.3 %collective-permute-start.7 = (bf16[2,2,4,32,256]{4,3,2,1,0:T(8,128)(2,1)S(1)}, bf16[2,2,4,32,256]{4,3,2,1,0:T(8,128)(2,1)S(1)}, u32[]{:S(2)}, u32[]{:S(2)}) collective-permute-start(bf16[2,2,4,32,256]{4,3,2,1,0:T(8,128)(2,1)S(1)} %get-tuple-element.64), channel_id=1, source_target_pairs={{0,10},{1,11},{2,8},{3,9},{4,14},{5,15},{6,12},{7,13},{8,2},{9,3},... | collective-permute-start | bytes 786440 | tf_op jit(solution)/shard_map/ppermute | solution.py:34
  47.8 15.4 %collective-permute-start.10 = (bf16[2,4,32,256]{3,2,1,0:T(8,128)(2,1)S(1)}, bf16[2,4,32,256]{3,2,1,0:T(8,128)(2,1)S(1)}, u32[]{:S(2)}, u32[]{:S(2)}) collective-permute-start(bf16[2,4,32,256]{3,2,1,0:T(8,128)(2,1)S(1)} %get-tuple-element.69), channel_id=1, source_target_pairs={{0,14},{1,15},{2,12},{3,13},{4,10},{5,11},{6,8},{7,9},{8,6},{9,7},... | collective-permute-start | bytes 393224 | tf_op jit(solution)/shard_map/ppermute | solution.py:34
  63.2 2.0 %collective-permute-start.11 = (bf16[8,4,32,256]{3,2,1,0:T(8,128)(2,1)S(1)}, bf16[8,4,32,256]{3,2,1,0:T(8,128)(2,1)S(1)}, u32[]{:S(2)}, u32[]{:S(2)}) collective-permute-start(bf16[8,4,32,256]{3,2,1,0:T(8,128)(2,1)S(1)} %get-tuple-element.74), channel_id=1, source_target_pairs={{0,1},{1,0},{2,3},{3,2},{4,5},{5,4},{6,7},{7,6},{8,9},{9,8},{10,11... | collective-permute-start | bytes 1572872 | tf_op jit(solution)/shard_map/ppermute | solution.py:34
  65.3 9.4 %collective-permute-start.12 = (bf16[2,4,32,256]{3,2,1,0:T(8,128)(2,1)S(1)}, bf16[2,4,32,256]{3,2,1,0:T(8,128)(2,1)S(1)}, u32[]{:S(2)}, u32[]{:S(2)}) collective-permute-start(bf16[2,4,32,256]{3,2,1,0:T(8,128)(2,1)S(1)} %get-tuple-element.75), channel_id=1, source_target_pairs={{0,8},{1,9},{2,10},{3,11},{4,12},{5,13},{6,14},{7,15},{8,0},{9,1},... | collective-permute-start | bytes 393224 | tf_op jit(solution)/shard_map/ppermute | solution.py:34
  66.3 8.4 %collective-permute-start.13 = (bf16[2,4,32,256]{3,2,1,0:T(8,128)(2,1)S(1)}, bf16[2,4,32,256]{3,2,1,0:T(8,128)(2,1)S(1)}, u32[]{:S(2)}, u32[]{:S(2)}) collective-permute-start(bf16[2,4,32,256]{3,2,1,0:T(8,128)(2,1)S(1)} %get-tuple-element.76), channel_id=1, source_target_pairs={{0,2},{1,3},{2,0},{3,1},{4,6},{5,7},{6,4},{7,5},{8,10},{9,11},{10,... | collective-permute-start | bytes 393224 | tf_op jit(solution)/shard_map/ppermute | solution.py:34
  67.8 8.2 %collective-permute-start.14 = (bf16[2,4,32,256]{3,2,1,0:T(8,128)(2,1)S(1)}, bf16[2,4,32,256]{3,2,1,0:T(8,128)(2,1)S(1)}, u32[]{:S(2)}, u32[]{:S(2)}) collective-permute-start(bf16[2,4,32,256]{3,2,1,0:T(8,128)(2,1)S(1)} %get-tuple-element.77), channel_id=1, source_target_pairs={{0,4},{1,5},{2,6},{3,7},{4,0},{5,1},{6,2},{7,3},{8,12},{9,13},{10,... | collective-permute-start | bytes 393224 | tf_op jit(solution)/shard_map/ppermute | solution.py:34
  76.0 5.4 %collective-permute-start.15 = (bf16[8,4,32,256]{3,2,1,0:T(8,128)(2,1)S(1)}, bf16[8,4,32,256]{3,2,1,0:T(8,128)(2,1)S(1)}, u32[]{:S(2)}, u32[]{:S(2)}) collective-permute-start(bf16[8,4,32,256]{3,2,1,0:T(8,128)(2,1)S(1)} %get-tuple-element.78), channel_id=1, source_target_pairs={{0,1},{1,0},{2,3},{3,2},{4,5},{5,4},{6,7},{7,6},{8,9},{9,8},{10,11... | collective-permute-start | bytes 1572872 | tf_op jit(solution)/shard_map/ppermute | solution.py:34
  76.0 9.4 %collective-permute-start.25 = (bf16[2,4,32,256]{3,2,1,0:T(8,128)(2,1)S(1)}, bf16[2,4,32,256]{3,2,1,0:T(8,128)(2,1)S(1)}, u32[]{:S(2)}, u32[]{:S(2)}) collective-permute-start(bf16[2,4,32,256]{3,2,1,0:T(8,128)(2,1)S(1)} %get-tuple-element.92), channel_id=1, source_target_pairs={{0,14},{1,15},{2,12},{3,13},{4,10},{5,11},{6,8},{7,9},{8,6},{9,7},... | collective-permute-start | bytes 393224 | tf_op jit(solution)/shard_map/ppermute | solution.py:34
  78.0 32.7 %collective-permute-start.26 = (bf16[12,4,32,256]{3,2,1,0:T(8,128)(2,1)S(1)}, bf16[12,4,32,256]{3,2,1,0:T(8,128)(2,1)S(1)}, u32[]{:S(2)}, u32[]{:S(2)}) collective-permute-start(bf16[12,4,32,256]{3,2,1,0:T(8,128)(2,1)S(1)} %gather_kernel.2.first_ref), channel_id=1, source_target_pairs={{0,16},{16,0},{1,17},{17,1},{2,18},{18,2},{3,19},{19,3},{4,20},{20... | collective-permute-start | bytes 2359304 | tf_op jit(solution)/shard_map/ppermute | solution.py:17
  79.5 18.6 %collective-permute-start.22 = (bf16[2,4,32,256]{3,2,1,0:T(8,128)(2,1)S(1)}, bf16[2,4,32,256]{3,2,1,0:T(8,128)(2,1)S(1)}, u32[]{:S(2)}, u32[]{:S(2)}) collective-permute-start(bf16[2,4,32,256]{3,2,1,0:T(8,128)(2,1)S(1)} %get-tuple-element.89), channel_id=1, source_target_pairs={{0,12},{1,13},{2,14},{3,15},{4,8},{5,9},{6,10},{7,11},{8,4},{9,5},... | collective-permute-start | bytes 393224 | tf_op jit(solution)/shard_map/ppermute | solution.py:34
  81.5 16.6 %collective-permute-start.16 = (bf16[2,4,32,256]{3,2,1,0:T(8,128)(2,1)S(1)}, bf16[2,4,32,256]{3,2,1,0:T(8,128)(2,1)S(1)}, u32[]{:S(2)}, u32[]{:S(2)}) collective-permute-start(bf16[2,4,32,256]{3,2,1,0:T(8,128)(2,1)S(1)} %get-tuple-element.80), channel_id=1, source_target_pairs={{0,8},{1,9},{2,10},{3,11},{4,12},{5,13},{6,14},{7,15},{8,0},{9,1},... | collective-permute-start | bytes 393224 | tf_op jit(solution)/shard_map/ppermute | solution.py:34
  81.5 20.0 %collective-permute-start.23 = (bf16[2,4,32,256]{3,2,1,0:T(8,128)(2,1)S(1)}, bf16[2,4,32,256]{3,2,1,0:T(8,128)(2,1)S(1)}, u32[]{:S(2)}, u32[]{:S(2)}) collective-permute-start(bf16[2,4,32,256]{3,2,1,0:T(8,128)(2,1)S(1)} %get-tuple-element.90), channel_id=1, source_target_pairs={{0,10},{1,11},{2,8},{3,9},{4,14},{5,15},{6,12},{7,13},{8,2},{9,3},... | collective-permute-start | bytes 393224 | tf_op jit(solution)/shard_map/ppermute | solution.py:34
  85.4 16.4 %collective-permute-start.24 = (bf16[2,4,32,256]{3,2,1,0:T(8,128)(2,1)S(1)}, bf16[2,4,32,256]{3,2,1,0:T(8,128)(2,1)S(1)}, u32[]{:S(2)}, u32[]{:S(2)}) collective-permute-start(bf16[2,4,32,256]{3,2,1,0:T(8,128)(2,1)S(1)} %get-tuple-element.91), channel_id=1, source_target_pairs={{0,6},{1,7},{2,4},{3,5},{4,2},{5,3},{6,0},{7,1},{8,14},{9,15},{10,... | collective-permute-start | bytes 393224 | tf_op jit(solution)/shard_map/ppermute | solution.py:34
  101.8 13.3 %collective-permute-start.27 = (bf16[8,4,32,256]{3,2,1,0:T(8,128)(2,1)S(1)}, bf16[8,4,32,256]{3,2,1,0:T(8,128)(2,1)S(1)}, u32[]{:S(2)}, u32[]{:S(2)}) collective-permute-start(bf16[8,4,32,256]{3,2,1,0:T(8,128)(2,1)S(1)} %gather_kernel.3.second_ref), channel_id=1, source_target_pairs={{0,16},{16,0},{1,17},{17,1},{2,18},{18,2},{3,19},{19,3},{4,20},{20... | collective-permute-start | bytes 1572872 | tf_op jit(solution)/shard_map/ppermute | solution.py:17
  104.4 13.1 %collective-permute-start.17 = (bf16[2,4,32,256]{3,2,1,0:T(8,128)(2,1)S(1)}, bf16[2,4,32,256]{3,2,1,0:T(8,128)(2,1)S(1)}, u32[]{:S(2)}, u32[]{:S(2)}) collective-permute-start(bf16[2,4,32,256]{3,2,1,0:T(8,128)(2,1)S(1)} %get-tuple-element.81), channel_id=1, source_target_pairs={{0,12},{1,13},{2,14},{3,15},{4,8},{5,9},{6,10},{7,11},{8,4},{9,5},... | collective-permute-start | bytes 393224 | tf_op jit(solution)/shard_map/ppermute | solution.py:34
  106.4 13.4 %collective-permute-start.18 = (bf16[2,4,32,256]{3,2,1,0:T(8,128)(2,1)S(1)}, bf16[2,4,32,256]{3,2,1,0:T(8,128)(2,1)S(1)}, u32[]{:S(2)}, u32[]{:S(2)}) collective-permute-start(bf16[2,4,32,256]{3,2,1,0:T(8,128)(2,1)S(1)} %get-tuple-element.82), channel_id=1, source_target_pairs={{0,14},{1,15},{2,12},{3,13},{4,10},{5,11},{6,8},{7,9},{8,6},{9,7},... | collective-permute-start | bytes 393224 | tf_op jit(solution)/shard_map/ppermute | solution.py:34
  108.3 12.8 %collective-permute-start.19 = (bf16[2,4,32,256]{3,2,1,0:T(8,128)(2,1)S(1)}, bf16[2,4,32,256]{3,2,1,0:T(8,128)(2,1)S(1)}, u32[]{:S(2)}, u32[]{:S(2)}) collective-permute-start(bf16[2,4,32,256]{3,2,1,0:T(8,128)(2,1)S(1)} %get-tuple-element.83), channel_id=1, source_target_pairs={{0,10},{1,11},{2,8},{3,9},{4,14},{5,15},{6,12},{7,13},{8,2},{9,3},... | collective-permute-start | bytes 393224 | tf_op jit(solution)/shard_map/ppermute | solution.py:34
  110.6 10.5 %collective-permute-start.20 = (bf16[2,4,32,256]{3,2,1,0:T(8,128)(2,1)S(1)}, bf16[2,4,32,256]{3,2,1,0:T(8,128)(2,1)S(1)}, u32[]{:S(2)}, u32[]{:S(2)}) collective-permute-start(bf16[2,4,32,256]{3,2,1,0:T(8,128)(2,1)S(1)} %get-tuple-element.84), channel_id=1, source_target_pairs={{0,2},{1,3},{2,0},{3,1},{4,6},{5,7},{6,4},{7,5},{8,10},{9,11},{10,... | collective-permute-start | bytes 393224 | tf_op jit(solution)/shard_map/ppermute | solution.py:34
  115.2 7.6 %collective-permute-start.21 = (bf16[2,4,32,256]{3,2,1,0:T(8,128)(2,1)S(1)}, bf16[2,4,32,256]{3,2,1,0:T(8,128)(2,1)S(1)}, u32[]{:S(2)}, u32[]{:S(2)}) collective-permute-start(bf16[2,4,32,256]{3,2,1,0:T(8,128)(2,1)S(1)} %get-tuple-element.85), channel_id=1, source_target_pairs={{0,4},{1,5},{2,6},{3,7},{4,0},{5,1},{6,2},{7,3},{8,12},{9,13},{10,... | collective-permute-start | bytes 393224 | tf_op jit(solution)/shard_map/ppermute | solution.py:34
  115.2 9.6 %copy-start.3 = (bf16[1,2048,256]{2,1,0:T(8,128)(2,1)S(1)}, bf16[1,2048,256]{2,1,0:T(8,128)(2,1)}, u32[]{:S(2)}) copy-start(bf16[1,2048,256]{2,1,0:T(8,128)(2,1)} %param.6) | copy-start | bytes 3145732
  115.2 9.6 %copy-start.4 = (bf16[1,2048,256]{2,1,0:T(8,128)(2,1)S(1)}, bf16[1,2048,256]{2,1,0:T(8,128)(2,1)}, u32[]{:S(2)}) copy-start(bf16[1,2048,256]{2,1,0:T(8,128)(2,1)} %param.7) | copy-start | bytes 3145732
  117.6 7.2 %collective-permute-start.28 = (bf16[2,4,32,256]{3,2,1,0:T(8,128)(2,1)S(1)}, bf16[2,4,32,256]{3,2,1,0:T(8,128)(2,1)S(1)}, u32[]{:S(2)}, u32[]{:S(2)}) collective-permute-start(bf16[2,4,32,256]{3,2,1,0:T(8,128)(2,1)S(1)} %get-tuple-element.96), channel_id=1, source_target_pairs={{0,6},{1,7},{2,4},{3,5},{4,2},{5,3},{6,0},{7,1},{8,14},{9,15},{10,... | collective-permute-start | bytes 393224 | tf_op jit(solution)/shard_map/ppermute | solution.py:34
